TPU v7x, 32 devices: a whole 2x2x4 slice. The times are simulated.
32 devices in a mesh: dp: 4 (over x, core), fsdp: 8 (over z, y).
Axes of the slice: x: 2, y: 2, z: 4, core: 2. Of those that a mesh axis runs over, the one named last changes fastest.
Arguments:
- tokens: bfloat16 [32768, 768], P(('dp', 'fsdp')), may hold values from -6 to 6
- lengths: int32 [64], P(('dp', 'fsdp')), may hold values from 65 to 512, as said below
- w_qkv: bfloat16 [768, 2304], P(('dp', 'fsdp')), may hold values from -0.21875 to 0.21875
- bias_q: bfloat16 [768], P(('dp', 'fsdp')), may hold values from -3 to 3
- bias_v: bfloat16 [768], P(('dp', 'fsdp')), may hold values from -3 to 3
- w_out: bfloat16 [768, 768], P(('dp', 'fsdp')), may hold values from -0.625 to 0.625
- bias_out: bfloat16 [768], P(('dp', 'fsdp')), may hold values from -3 to 3
- gain_one: bfloat16 [768], P(('dp', 'fsdp')), may hold values from 0.5 to 1.5
- shift_one: bfloat16 [768], P(('dp', 'fsdp')), may hold values from -2 to 2
- w_in: bfloat16 [768, 3072], P(('dp', 'fsdp')), may hold values from -0.21875 to 0.21875
- bias_in: bfloat16 [3072], P(('dp', 'fsdp')), may hold values from -3 to 3
- w_back: bfloat16 [3072, 768], P(('dp', 'fsdp')), may hold values from -0.109375 to 0.109375
- bias_back: bfloat16 [768], P(('dp', 'fsdp')), may hold values from -3 to 3
- gain_two: bfloat16 [768], P(('dp', 'fsdp')), may hold values from 0.5 to 1.5
- shift_two: bfloat16 [768], P(('dp', 'fsdp')), may hold values from -2 to 2
- cotangent: bfloat16 [32768, 768], P(('dp', 'fsdp')), may hold values from -6 to 6
Outputs:
- activations: bfloat16 [32768, 768], P(('dp', 'fsdp'))
- input_grad: bfloat16 [32768, 768], P(('dp', 'fsdp'))
- w_qkv_grad: float32 [768, 2304], P(('dp', 'fsdp'))
- bias_q_grad: float32 [768], P(('dp', 'fsdp'))
- bias_v_grad: float32 [768], P(('dp', 'fsdp'))
- w_out_grad: float32 [768, 768], P(('dp', 'fsdp'))
- bias_out_grad: float32 [768], P(('dp', 'fsdp'))
- gain_one_grad: float32 [768], P(('dp', 'fsdp'))
- shift_one_grad: float32 [768], P(('dp', 'fsdp'))
- w_in_grad: float32 [768, 3072], P(('dp', 'fsdp'))
- bias_in_grad: float32 [3072], P(('dp', 'fsdp'))
- w_back_grad: float32 [3072, 768], P(('dp', 'fsdp'))
- bias_back_grad: float32 [768], P(('dp', 'fsdp'))
- gain_two_grad: float32 [768], P(('dp', 'fsdp'))
- shift_two_grad: float32 [768], P(('dp', 'fsdp'))
Inputs may be any that keep to these rules, and one draw needn't show every extreme that they name: Tokens at positions 512 * s + t with t < lengths[s] are real, the rest padding; some sequence has exactly 512.
All inputs are finite; a program needn't handle non-finite values.
Results may differ from a plain program's by a relative error of at most 0.019.
Values may be sent and summed in bfloat16 or wider, within the bound.
No kernel may reach another device: no remote copies, remote signals or barrier semaphores. Data moves between devices by JAX's collectives and lax.ppermute only.
A program may use at most 192 MiB of HBM per device.

v0:
```python
from functools import partial

import jax
import jax.numpy as jnp
from jax import lax
from jax.sharding import PartitionSpec as P

D = 768
HEADS = 12
HEAD_DIM = 64
APPS = 2


def normalize(value, gain, shift):
    centered = value - jnp.mean(value, axis=-1, keepdims=True)
    variance = jnp.mean(centered * centered, axis=-1, keepdims=True)
    return centered * lax.rsqrt(variance + 1e-12) * gain + shift


def product(left, right):
    return jnp.dot(left, right, preferred_element_type=jnp.float32)


def dot_rows(left, right):
    return lax.dot_general(
        left, right, (((0,), (0,)), ((), ())), preferred_element_type=jnp.float32
    )


def dot_back(left, right):
    return lax.dot_general(
        left, right, (((1,), (1,)), ((), ())), preferred_element_type=jnp.float32
    )


def column_sums(value):
    return jnp.sum(value.astype(jnp.float32), axis=0)


def score_block(queries, key_rows, valid_keys):
    scores = (
        jnp.einsum("qhd,khd->hqk", queries, key_rows, preferred_element_type=jnp.float32) * 0.125
    )
    return jnp.where(valid_keys[None, None, :], scores, -1e30)


def attend_forward(pieces):
    queries, key_rows, value_rows, valid_keys = pieces
    scores = score_block(queries, key_rows, valid_keys)
    largest = jnp.max(scores, axis=-1, keepdims=True)
    raised = jnp.exp(scores - largest)
    totals = jnp.sum(raised, axis=-1, keepdims=True)
    probs = (raised / totals).astype(jnp.bfloat16)
    context = jnp.einsum("hqk,khd->qhd", probs, value_rows, preferred_element_type=jnp.float32)
    return (context.astype(jnp.bfloat16), (largest + jnp.log(totals))[..., 0])


def attend_backward(pieces):
    queries, key_rows, value_rows, valid_keys, log_total, context_grad = pieces
    scores = score_block(queries, key_rows, valid_keys)
    probs = jnp.exp(scores - log_total[..., None])
    value_grad = jnp.einsum(
        "hqk,qhd->khd", probs.astype(jnp.bfloat16), context_grad, preferred_element_type=jnp.float32
    )
    prob_grad = jnp.einsum(
        "qhd,khd->hqk", context_grad, value_rows, preferred_element_type=jnp.float32
    )
    inner = jnp.sum(probs * prob_grad, axis=-1, keepdims=True)
    score_grad = (probs * (prob_grad - inner)).astype(jnp.bfloat16)
    query_grad = (
        jnp.einsum("hqk,khd->qhd", score_grad, key_rows, preferred_element_type=jnp.float32) * 0.125
    )
    key_grad = (
        jnp.einsum("hqk,qhd->khd", score_grad, queries, preferred_element_type=jnp.float32) * 0.125
    )
    return (query_grad, key_grad, value_grad)


def layer_forward(inputs, whole, valid_keys):
    (
        w_qkv,
        bias_q,
        bias_v,
        w_out,
        bias_out,
        gain_one,
        shift_one,
        w_in,
        bias_in,
        w_back,
        bias_back,
        gain_two,
        shift_two,
    ) = whole
    count = valid_keys.shape[0]
    seq_len = valid_keys.shape[1]
    input_low = inputs.astype(jnp.bfloat16)
    projected = product(input_low, w_qkv)
    queries = (projected[:, :D] + bias_q.astype(jnp.float32)).astype(jnp.bfloat16)
    key_rows = projected[:, D : 2 * D].astype(jnp.bfloat16)
    value_rows = (projected[:, 2 * D :] + bias_v.astype(jnp.float32)).astype(jnp.bfloat16)
    shape_four = (count, seq_len, HEADS, HEAD_DIM)
    queries = queries.reshape(shape_four)
    key_rows = key_rows.reshape(shape_four)
    value_rows = value_rows.reshape(shape_four)
    context, log_total = lax.map(attend_forward, (queries, key_rows, value_rows, valid_keys))
    context = context.reshape(count * seq_len, D)
    first_sum = inputs + product(context, w_out) + bias_out.astype(jnp.float32)
    middle = normalize(first_sum, gain_one.astype(jnp.float32), shift_one.astype(jnp.float32))
    before = product(middle.astype(jnp.bfloat16), w_in) + bias_in.astype(jnp.float32)
    hidden = jax.nn.gelu(before, approximate=True).astype(jnp.bfloat16)
    second_sum = middle + product(hidden, w_back) + bias_back.astype(jnp.float32)
    outputs = normalize(second_sum, gain_two.astype(jnp.float32), shift_two.astype(jnp.float32))
    stored = (
        input_low,
        queries,
        key_rows,
        value_rows,
        log_total,
        context,
        first_sum,
        before,
        second_sum,
    )
    return (outputs, stored)


def layer_backward(out_grad, stored, whole, valid_keys):
    (
        w_qkv,
        bias_q,
        bias_v,
        w_out,
        bias_out,
        gain_one,
        shift_one,
        w_in,
        bias_in,
        w_back,
        bias_back,
        gain_two,
        shift_two,
    ) = whole
    input_low, queries, key_rows, value_rows, log_total, context, first_sum, before, second_sum = (
        stored
    )
    rows = input_low.shape[0]
    gain_first = gain_one.astype(jnp.float32)
    shift_first = shift_one.astype(jnp.float32)
    middle = normalize(first_sum, gain_first, shift_first)
    _, norm_two_pull = jax.vjp(
        normalize, second_sum, gain_two.astype(jnp.float32), shift_two.astype(jnp.float32)
    )
    sum_two_grad, gain_two_grad, shift_two_grad = norm_two_pull(out_grad)
    branch_low = sum_two_grad.astype(jnp.bfloat16)
    bias_back_grad = column_sums(branch_low)
    hidden = jax.nn.gelu(before, approximate=True).astype(jnp.bfloat16)
    w_back_grad = dot_rows(hidden, branch_low)
    hidden_grad = dot_back(branch_low, w_back)
    _, gelu_pull = jax.vjp(partial(jax.nn.gelu, approximate=True), before)
    (before_grad,) = gelu_pull(hidden_grad)
    before_low = before_grad.astype(jnp.bfloat16)
    bias_in_grad = column_sums(before_low)
    w_in_grad = dot_rows(middle.astype(jnp.bfloat16), before_low)
    middle_grad = sum_two_grad + dot_back(before_low, w_in)
    _, norm_one_pull = jax.vjp(normalize, first_sum, gain_first, shift_first)
    sum_one_grad, gain_one_grad, shift_one_grad = norm_one_pull(middle_grad)
    attend_low = sum_one_grad.astype(jnp.bfloat16)
    bias_out_grad = column_sums(attend_low)
    w_out_grad = dot_rows(context, attend_low)
    context_grad = dot_back(attend_low, w_out).astype(jnp.bfloat16).reshape(queries.shape)
    query_grad, key_grad, value_grad = lax.map(
        attend_backward, (queries, key_rows, value_rows, valid_keys, log_total, context_grad)
    )
    projected_grad = jnp.concatenate(
        [query_grad.reshape(rows, D), key_grad.reshape(rows, D), value_grad.reshape(rows, D)],
        axis=1,
    ).astype(jnp.bfloat16)
    bias_q_grad = column_sums(projected_grad[:, :D])
    bias_v_grad = column_sums(projected_grad[:, 2 * D :])
    w_qkv_grad = dot_rows(input_low, projected_grad)
    input_grad = sum_one_grad + dot_back(projected_grad, w_qkv)
    grads = (
        w_qkv_grad,
        bias_q_grad,
        bias_v_grad,
        w_out_grad,
        bias_out_grad,
        gain_one_grad,
        shift_one_grad,
        w_in_grad,
        bias_in_grad,
        w_back_grad,
        bias_back_grad,
        gain_two_grad,
        shift_two_grad,
    )
    return (input_grad, grads)


def local(
    tokens,
    lengths,
    w_qkv,
    bias_q,
    bias_v,
    w_out,
    bias_out,
    gain_one,
    shift_one,
    w_in,
    bias_in,
    w_back,
    bias_back,
    gain_two,
    shift_two,
    cotangent,
):
    count = lengths.shape[0]
    seq_len = tokens.shape[0] // count
    positions = jnp.arange(seq_len, dtype=jnp.int32)
    valid_keys = positions[None, :] < lengths[:, None]
    whole = None
    activations = tokens.astype(jnp.float32)
    saved = []
    for step in range(APPS):
        whole = (
            lax.all_gather(w_qkv, ("dp", "fsdp"), axis=0, tiled=True),
            lax.all_gather(bias_q, ("dp", "fsdp"), axis=0, tiled=True),
            lax.all_gather(bias_v, ("dp", "fsdp"), axis=0, tiled=True),
            lax.all_gather(w_out, ("dp", "fsdp"), axis=0, tiled=True),
            lax.all_gather(bias_out, ("dp", "fsdp"), axis=0, tiled=True),
            lax.all_gather(gain_one, ("dp", "fsdp"), axis=0, tiled=True),
            lax.all_gather(shift_one, ("dp", "fsdp"), axis=0, tiled=True),
            lax.all_gather(w_in, ("dp", "fsdp"), axis=0, tiled=True),
            lax.all_gather(bias_in, ("dp", "fsdp"), axis=0, tiled=True),
            lax.all_gather(w_back, ("dp", "fsdp"), axis=0, tiled=True),
            lax.all_gather(bias_back, ("dp", "fsdp"), axis=0, tiled=True),
            lax.all_gather(gain_two, ("dp", "fsdp"), axis=0, tiled=True),
            lax.all_gather(shift_two, ("dp", "fsdp"), axis=0, tiled=True),
        )
        activations, stored = layer_forward(activations, whole, valid_keys)
        saved.append(stored)
    running_grad = cotangent.astype(jnp.float32)
    totals = None
    for step in reversed(range(APPS)):
        whole = (
            lax.all_gather(w_qkv, ("dp", "fsdp"), axis=0, tiled=True),
            lax.all_gather(bias_q, ("dp", "fsdp"), axis=0, tiled=True),
            lax.all_gather(bias_v, ("dp", "fsdp"), axis=0, tiled=True),
            lax.all_gather(w_out, ("dp", "fsdp"), axis=0, tiled=True),
            lax.all_gather(bias_out, ("dp", "fsdp"), axis=0, tiled=True),
            lax.all_gather(gain_one, ("dp", "fsdp"), axis=0, tiled=True),
            lax.all_gather(shift_one, ("dp", "fsdp"), axis=0, tiled=True),
            lax.all_gather(w_in, ("dp", "fsdp"), axis=0, tiled=True),
            lax.all_gather(bias_in, ("dp", "fsdp"), axis=0, tiled=True),
            lax.all_gather(w_back, ("dp", "fsdp"), axis=0, tiled=True),
            lax.all_gather(bias_back, ("dp", "fsdp"), axis=0, tiled=True),
            lax.all_gather(gain_two, ("dp", "fsdp"), axis=0, tiled=True),
            lax.all_gather(shift_two, ("dp", "fsdp"), axis=0, tiled=True),
        )
        running_grad, grads = layer_backward(running_grad, saved[step], whole, valid_keys)
        if totals is None:
            totals = grads
        else:
            totals = tuple((held + added for held, added in zip(totals, grads)))
    owned = (
        lax.psum_scatter(totals[0], ("dp", "fsdp"), scatter_dimension=0, tiled=True),
        lax.psum_scatter(totals[1], ("dp", "fsdp"), scatter_dimension=0, tiled=True),
        lax.psum_scatter(totals[2], ("dp", "fsdp"), scatter_dimension=0, tiled=True),
        lax.psum_scatter(totals[3], ("dp", "fsdp"), scatter_dimension=0, tiled=True),
        lax.psum_scatter(totals[4], ("dp", "fsdp"), scatter_dimension=0, tiled=True),
        lax.psum_scatter(totals[5], ("dp", "fsdp"), scatter_dimension=0, tiled=True),
        lax.psum_scatter(totals[6], ("dp", "fsdp"), scatter_dimension=0, tiled=True),
        lax.psum_scatter(totals[7], ("dp", "fsdp"), scatter_dimension=0, tiled=True),
        lax.psum_scatter(totals[8], ("dp", "fsdp"), scatter_dimension=0, tiled=True),
        lax.psum_scatter(totals[9], ("dp", "fsdp"), scatter_dimension=0, tiled=True),
        lax.psum_scatter(totals[10], ("dp", "fsdp"), scatter_dimension=0, tiled=True),
        lax.psum_scatter(totals[11], ("dp", "fsdp"), scatter_dimension=0, tiled=True),
        lax.psum_scatter(totals[12], ("dp", "fsdp"), scatter_dimension=0, tiled=True),
    )
    return (
        activations.astype(jnp.bfloat16),
        running_grad.astype(jnp.bfloat16),
        owned[0],
        owned[1],
        owned[2],
        owned[3],
        owned[4],
        owned[5],
        owned[6],
        owned[7],
        owned[8],
        owned[9],
        owned[10],
        owned[11],
        owned[12],
    )


def solution(mesh):
    placed = (
        P(("dp", "fsdp"), None),
        P(("dp", "fsdp")),
        P(("dp", "fsdp"), None),
        P(("dp", "fsdp")),
        P(("dp", "fsdp")),
        P(("dp", "fsdp"), None),
        P(("dp", "fsdp")),
        P(("dp", "fsdp")),
        P(("dp", "fsdp")),
        P(("dp", "fsdp"), None),
        P(("dp", "fsdp")),
        P(("dp", "fsdp"), None),
        P(("dp", "fsdp")),
        P(("dp", "fsdp")),
        P(("dp", "fsdp")),
        P(("dp", "fsdp"), None),
    )
    return jax.shard_map(
        local,
        mesh=mesh,
        in_specs=placed,
        out_specs=(
            P(("dp", "fsdp"), None),
            P(("dp", "fsdp"), None),
            P(("dp", "fsdp"), None),
            P(("dp", "fsdp")),
            P(("dp", "fsdp")),
            P(("dp", "fsdp"), None),
            P(("dp", "fsdp")),
            P(("dp", "fsdp")),
            P(("dp", "fsdp")),
            P(("dp", "fsdp"), None),
            P(("dp", "fsdp")),
            P(("dp", "fsdp"), None),
            P(("dp", "fsdp")),
            P(("dp", "fsdp")),
            P(("dp", "fsdp")),
        ),
        check_vma=False,
    )
```

profile of v0, /device:TPU:0, one launch (start us, length us, event | category | flops | bytes accessed | tf_op | source)
XLA Modules:
  0.0 1025.6 jit_solution(1250772004812278440)
XLA Ops:
  17.6 42.4 %all-reduce.19 = (bf16[768]{0:T(1024)(128)(2,1)S(1)}, bf16[768]{0:T(1024)(128)(2,1)S(1)}, bf16[768]{0:T(1024)(128)(2,1)S(1)}, bf16[768]{0:T(1024)(128)(2,1)S(1)}...) all-reduce(bf16[768]{0:T(1024)(128)(2,1)S(1)} %dynamic-update-slice, ...), channel_id=1, replica_groups=mesh['dp'=4,'fsdp'=8] {'dp','fsdp'}, use_global_device_ids=true, to_apply=%add | all-reduce | flops 9216 | bytes 36864
  67.5 6.6 all-gather.5.cloned.1.call-done
  74.1 5.8 fusion.141
  86.6 2.9 copy.123
  96.9 3.9 reshape.276
  103.9 20.5 %while.52 = (s32[]{:T(128)}, bf16[2,512,12,64]{1,3,2,0:T(8,128)(2,1)}, f32[2,12,512]{2,1,0:T(8,128)S(1)}, bf16[2,512,12,64]{1,3,2,0:T(8,128)(2,1)}, pred[2,512]{...) while((s32[]{:T(128)}, ...), condition=%wide.region_3.4_spmd, body=%wide.region_0.3_spmd.sunk | while | flops 843442176 | bytes 47428216 | solution.py:106
  104.3 3.1 fusion.212
  110.1 4.2 fusion.214
  114.3 3.1 fusion.212
  120.0 4.2 fusion.214
  124.4 4.2 copy.126
  130.2 3.8 fusion.137
  135.6 60.1 %all-gather.9.cloned.1.call-done = bf16[768,3072]{1,0:T(8,128)(2,1)} async-done(((bf16[24,3072]{1,0:T(8,128)(2,1)}), bf16[768,3072]{1,0:T(8,128)(2,1)}) %all-gather.9.cloned.1.call-update) | async-done | bytes 4718608 | tf_op jit(solution)/shard_map/all_gather | solution.py:235
  195.7 10.6 %fusion.130 = f32[1024,3072]{1,0:T(8,128)} fusion(bf16[768,3072]{1,0:T(8,128)(2,1)} %all-gather.9.cloned.1.call-done, f32[1024,768]{0,1:T(8,128)S(1)} %get-tuple-element.486, f32[768]{0:T(1024)S(1)} %convert_element_type.181, f32[768]{0:T(1024)S(1)} %convert_element_type.180, f32[1024]{0:T(1024)S(1)} %fusion.117, f32[1024]{0:T(1024)S(1)} %broadcast_multiply_fusion.3), kind=kOutput, calls=%fused_computation.229 | convolution fusion | flops 4835770368 | bytes 20461568 | tf_op jit(solution)/shard_map/dot_general | solution.py:21
  206.3 54.7 %all-gather.11.cloned.1.call-done = bf16[3072,768]{1,0:T(8,128)(2,1)} async-done(((bf16[96,768]{1,0:T(8,128)(2,1)}), bf16[3072,768]{1,0:T(8,128)(2,1)}) %all-gather.11.cloned.1.call-update) | async-done | bytes 4718608 | tf_op jit(solution)/shard_map/all_gather | solution.py:237
  261.0 11.7 %fusion.138 = (f32[1024]{0:T(1024)S(1)}, f32[1024,768]{0,1:T(8,128)S(1)}) fusion(f32[768]{0:T(1024)S(1)} %copy-done.112, bf16[3072,768]{1,0:T(8,128)(2,1)} %all-gather.11.cloned.1.call-done, f32[1024,3072]{1,0:T(8,128)} %fusion.130, f32[3072]{0:T(1024)S(1)} %copy-done.100, f32[768]{0:T(1024)S(1)} %convert_element_type.181, ...), kind=kOutput, calls=%fused_computation.236 | convolution fusion | flops 4868799488 | bytes 23626752 | tf_op jit(solution)/shard_map/dot_general | solution.py:21
  274.4 4.4 fusion.127
  285.5 2.9 copy.130
  295.9 3.8 reshape.280
  302.8 20.4 %while.53 = (s32[]{:T(128)}, bf16[2,512,12,64]{1,3,2,0:T(8,128)(2,1)}, f32[2,12,512]{2,1,0:T(8,128)S(1)}, bf16[2,512,12,64]{1,3,2,0:T(8,128)(2,1)}, pred[2,512]{...) while((s32[]{:T(128)}, ...), condition=%wide.region_11.12_spmd, body=%wide.region_8.11_spmd.sunk | while | flops 843442176 | bytes 47428216 | solution.py:106
  303.2 3.1 fusion.216
  308.9 4.2 fusion.218
  313.1 3.1 fusion.216
  318.9 4.2 fusion.218
  323.2 3.2 copy.133
  329.7 8.6 fusion.123
  338.4 11.8 %fusion.140 = (f32[1024]{0:T(1024)S(1)}, f32[1024,768]{0,1:T(8,128)S(1)}) fusion(f32[768]{0:T(1024)S(1)} %copy-done.113, bf16[3072,768]{1,0:T(8,128)(2,1)} %all-gather.11.cloned.1.call-done, f32[1024,3072]{1,0:T(8,128)} %fusion.123, f32[3072]{0:T(1024)S(1)} %copy-done.101, f32[768]{0:T(1024)S(1)} %convert_element_type.181, ...), kind=kOutput, calls=%fused_computation.238 | convolution fusion | flops 4868799488 | bytes 23626752 | tf_op jit(solution)/shard_map/dot_general | solution.py:21
  354.0 3.3 convert_reduce_fusion.4
  357.3 18.1 %convert_reduce_fusion.1 = (f32[3072]{0:T(1024)}, bf16[1024,3072]{1,0:T(8,128)(2,1)}) fusion(f32[1024,3072]{1,0:T(8,128)} %fusion.123, f32[3072]{0:T(1024)S(1)} %copy-done.101, bf16[1024,768]{0,1:T(8,128)(2,1)S(1)} %get-tuple-element.459, bf16[3072,768]{1,0:T(8,128)(2,1)} %all-gather.11.cloned.1.call-done), kind=kOutput, calls=%fused_computation.131 | convolution fusion | flops 4904186880 | bytes 25190400 | tf_op jit(solution)/shard_map/dot_general | solution.py:31
  375.4 9.8 multiply_reduce_fusion.4
  388.6 2.9 fusion.142
  396.7 3.8 reshape.282
  400.5 2.9 copy.140
  407.4 49.5 %while.54 = (s32[]{:T(128)}, bf16[2,512,12,64]{1,3,2,0:T(8,128)(2,1)}, bf16[2,512,12,64]{1,3,2,0:T(8,128)(2,1)}, bf16[2,512,12,64]{1,3,2,0:T(8,128)(2,1)}, bf16[...) while((s32[]{:T(128)}, ...), condition=%wide.region_22.23_spmd, body=%wide.region_20.22_spmd.sunk | while | flops 2061232128 | bytes 142540592 | solution.py:172
  409.3 7.4 multiply_reduce_fusion.14
  416.7 7.2 multiply_convert_fusion.10
  428.3 3.8 bitcast_dynamic-update-slice_fusion.20
  434.0 7.4 multiply_reduce_fusion.14
  441.4 7.2 multiply_convert_fusion.10
  453.0 3.8 bitcast_dynamic-update-slice_fusion.20
  456.9 3.0 copy.142
  469.4 5.3 multiply_reduce_fusion.2
  477.1 18.0 %convert_reduce_fusion = (f32[3072]{0:T(1024)}, bf16[1024,3072]{1,0:T(8,128)(2,1)}) fusion(f32[1024,3072]{1,0:T(8,128)} %fusion.130, f32[3072]{0:T(1024)S(1)} %copy-done.102, bf16[1024,768]{0,1:T(8,128)(2,1)S(1)} %get-tuple-element.457, bf16[3072,768]{1,0:T(8,128)(2,1)S(1)} %bitcast.315), kind=kOutput, calls=%fused_computation.130 | convolution fusion | flops 4904186880 | bytes 25190400 | tf_op jit(solution)/shard_map/dot_general | solution.py:31
  495.1 8.9 multiply_reduce_fusion.3
  508.1 2.9 convolution_add_fusion.2
  521.6 49.8 %while.55 = (s32[]{:T(128)}, bf16[2,512,12,64]{1,3,2,0:T(8,128)(2,1)}, bf16[2,512,12,64]{1,3,2,0:T(8,128)(2,1)}, bf16[2,512,12,64]{1,3,2,0:T(8,128)(2,1)}, bf16[...) while((s32[]{:T(128)}, ...), condition=%wide.region_29.30_spmd, body=%wide.region_27.29_spmd.sunk | while | flops 2061232128 | bytes 142540592 | solution.py:172
  523.6 7.4 multiply_reduce_fusion.15
  531.0 7.4 multiply_convert_fusion.11
  542.7 3.8 bitcast_dynamic-update-slice_fusion.23
  548.4 7.4 multiply_reduce_fusion.15
  555.8 7.3 multiply_convert_fusion.11
  567.5 3.8 bitcast_dynamic-update-slice_fusion.23
  571.4 3.2 copy.154
  581.3 4.1 fusion.125
  585.4 6.6 bitcast_add_fusion
  593.4 11.7 %fusion.133 = f32[3072,768]{1,0:T(8,128)S(1)} fusion(bf16[1024,768]{0,1:T(8,128)(2,1)S(1)} %copy-done.49, f32[1024,3072]{1,0:T(8,128)} %fusion.123, f32[3072]{0:T(1024)S(1)} %copy-done.103), kind=kOutput, calls=%fused_computation.231 | convolution fusion | flops 4863295488 | bytes 23605248 | tf_op jit(solution)/shard_map/dot_general | solution.py:25
  605.1 14.1 %convolution_add_fusion = f32[3072,768]{1,0:T(8,128)} fusion(f32[3072,768]{1,0:T(8,128)S(1)} %fusion.133, bf16[1024,768]{0,1:T(8,128)(2,1)S(1)} %copy-done.51, f32[1024,3072]{1,0:T(8,128)} %fusion.130, f32[3072]{0:T(1024)S(1)} %copy-done.103), kind=kOutput, calls=%fused_computation.135 | convolution fusion | flops 4865654784 | bytes 33042432 | tf_op jit(solution)/shard_map/dot_general | solution.py:25
  619.9 9.0 fusion.121
  628.9 10.8 %convolution_add_fusion.1 = f32[768,3072]{1,0:T(8,128)} fusion(f32[768,3072]{1,0:T(8,128)S(1)} %fusion.121, bf16[1024,3072]{1,0:T(8,128)(2,1)} %get-tuple-element.499, f32[1024,768]{0,1:T(8,128)S(1)} %copy-done.6, f32[768]{0:T(1024)S(1)} %copy-done.56, f32[768]{0:T(1024)S(1)} %copy-done.54, f32[1024]{0:T(1024)S(1)} %copy-done.68, f32[1024]{0:T(1024)S(1)} %copy-done.63), kind=kOutput, calls=%fused_computation.136 | convolution fusion | flops 4838129664 | bytes 28325888 | tf_op jit(solution)/shard_map/dot_general | solution.py:25
  643.6 40.9 %all-reduce.18 = (f32[768]{0:T(1024)S(1)}, f32[768]{0:T(1024)S(1)}, f32[768]{0:T(1024)S(1)}, f32[768]{0:T(1024)S(1)}, f32[768]{0:T(1024)S(1)}, /*index=5*/f32[30...) all-reduce(f32[768]{0:T(1024)S(1)} %add.343, ...), channel_id=3, replica_groups=mesh['dp'=4,'fsdp'=8] {'dp','fsdp'}, use_global_device_ids=true, to_apply=%region_33.34.clone | all-reduce | flops 9216 | bytes 73728
  689.2 8.2 add_convert_fusion
  701.2 33.7 %reduce-scatter.5.cloned.1.call-done = f32[24,2304]{1,0:T(8,128)} async-done(((f32[768,2304]{1,0:T(8,128)}), f32[24,2304]{1,0:T(8,128)}) %reduce-scatter.5.cloned.1.call-update) | async-done | bytes 221200 | tf_op jit(solution)/shard_map/reduce_scatter | solution.py:268
  734.9 141.3 %reduce-scatter.11.cloned.1.call-done = f32[96,768]{1,0:T(8,128)} async-done(((f32[3072,768]{1,0:T(8,128)}), f32[96,768]{1,0:T(8,128)}) %reduce-scatter.11.cloned.1.call-update) | async-done | bytes 294928 | tf_op jit(solution)/shard_map/reduce_scatter | solution.py:277
  876.2 142.1 %reduce-scatter.9.cloned.1.call-done = f32[24,3072]{1,0:T(8,128)} async-done(((f32[768,3072]{1,0:T(8,128)}), f32[24,3072]{1,0:T(8,128)}) %reduce-scatter.9.cloned.1.call-update) | async-done | bytes 294928 | tf_op jit(solution)/shard_map/reduce_scatter | solution.py:275
  (472 shorter events, 158.3 us)
Async XLA Ops:
  7.2 58.8 %copy-start.42 = (bf16[1024,768]{1,0:T(8,128)(2,1)S(1)}, bf16[1024,768]{1,0:T(8,128)(2,1)}, u32[]{:S(2)}) copy-start(bf16[1024,768]{1,0:T(8,128)(2,1)} %param.39) | copy-start | bytes 4718596
  7.2 66.9 %all-gather.5.cloned.1.call-start = ((), (), s32[]{:S(2)}) async-start(), calls=%async_computation.4 | async-start | bytes 3649536 | tf_op jit(solution)/shard_map/all_gather | solution.py:228
  7.9 122.2 %all-gather.7.cloned.1.call-start = ((), (), s32[]{:S(2)}) async-start(), calls=%async_computation.5 | async-start | bytes 1216512 | tf_op jit(solution)/shard_map/all_gather | solution.py:231
  8.7 187.0 %all-gather.9.cloned.1.call-start = ((), (), s32[]{:S(2)}) async-start(), calls=%async_computation.6 | async-start | bytes 4866048 | tf_op jit(solution)/shard_map/all_gather | solution.py:235
  9.4 251.6 %all-gather.11.cloned.1.call-start = ((), (), s32[]{:S(2)}) async-start(), calls=%async_computation.7 | async-start | bytes 4866048 | tf_op jit(solution)/shard_map/all_gather | solution.py:237
  10.0 691.2 %reduce-scatter.7.cloned.1.call-start = ((), (), s32[]{:S(2)}) async-start(), calls=%async_computation.9 | async-start | bytes 2433024 | tf_op jit(solution)/shard_map/reduce_scatter | solution.py:271
  60.0 20.1 %copy-start.77 = (f32[768]{0:T(1024)}, f32[768]{0:T(1024)S(1)}, u32[]{:S(2)}) copy-start(f32[768]{0:T(1024)S(1)} %convert_element_type.175) | copy-start | bytes 9220
  60.0 20.1 %copy-start.79 = (f32[768]{0:T(1024)}, f32[768]{0:T(1024)S(1)}, u32[]{:S(2)}) copy-start(f32[768]{0:T(1024)S(1)} %convert_element_type.177) | copy-start | bytes 9220
  60.8 69.4 %copy-start.114 = (f32[768]{0:T(1024)}, f32[768]{0:T(1024)S(1)}, u32[]{:S(2)}) copy-start(f32[768]{0:T(1024)S(1)} %convert_element_type.179) | copy-start | bytes 9220
  60.8 13.3 %copy-start.43 = (bf16[1024,768]{1,0:T(8,128)(2,1)S(1)}, bf16[1024,768]{1,0:T(8,128)(2,1)}, u32[]{:S(2)}) copy-start(bf16[1024,768]{1,0:T(8,128)(2,1)} %param.24) | copy-start | bytes 4718596
  63.5 321.7 %copy-start.52 = (f32[768]{0:T(1024)}, f32[768]{0:T(1024)S(1)}, u32[]{:S(2)}) copy-start(f32[768]{0:T(1024)S(1)} %convert_element_type.180) | copy-start | bytes 9220
  63.5 274.8 %copy-start.55 = (f32[768]{0:T(1024)}, f32[768]{0:T(1024)S(1)}, u32[]{:S(2)}) copy-start(f32[768]{0:T(1024)S(1)} %convert_element_type.181) | copy-start | bytes 9220
  124.3 5.8 copy-start
  124.3 5.8 copy-start.2
  124.3 5.8 copy-start.57
  134.0 127.0 %copy-start.4 = (f32[1024,768]{0,1:T(8,128)}, f32[1024,768]{0,1:T(8,128)S(1)}, u32[]{:S(2)}) copy-start(f32[1024,768]{0,1:T(8,128)S(1)} %get-tuple-element.486) | copy-start | bytes 9437188
  134.0 127.0 %copy-start.61 = (f32[1024]{0:T(1024)}, f32[1024]{0:T(1024)S(1)}, u32[]{:S(2)}) copy-start(f32[1024]{0:T(1024)S(1)} %broadcast_multiply_fusion.3) | copy-start | bytes 12292
  135.6 125.4 %copy-start.66 = (f32[1024]{0:T(1024)}, f32[1024]{0:T(1024)S(1)}, u32[]{:S(2)}) copy-start(f32[1024]{0:T(1024)S(1)} %fusion.117) | copy-start | bytes 12292
  135.6 125.4 %copy-start.100 = (f32[3072]{0:T(1024)S(1)}, f32[3072]{0:T(1024)}, u32[]{:S(2)}) copy-start(f32[3072]{0:T(1024)} %convert_element_type.183) | copy-start | bytes 36868
  135.6 125.4 %copy-start.112 = (f32[768]{0:T(1024)S(1)}, f32[768]{0:T(1024)}, u32[]{:S(2)}) copy-start(f32[768]{0:T(1024)} %convert_element_type.185) | copy-start | bytes 9220
  261.0 13.3 %copy-start.116 = (bf16[768,2304]{1,0:T(8,128)(2,1)S(1)}, bf16[768,2304]{1,0:T(8,128)(2,1)}, u32[]{:S(2)}) copy-start(bf16[768,2304]{1,0:T(8,128)(2,1)} %all-gather.5.cloned.1.call-done) | copy-start | bytes 10616836
  272.8 6.0 copy-start.22
  272.8 54.0 %copy-start.74 = (f32[1024]{0:T(1024)}, f32[1024]{0:T(1024)S(1)}, u32[]{:S(2)}) copy-start(f32[1024]{0:T(1024)S(1)} %broadcast_multiply_fusion.2) | copy-start | bytes 12292
  274.4 52.5 %copy-start.92 = (f32[1024]{0:T(1024)}, f32[1024]{0:T(1024)S(1)}, u32[]{:S(2)}) copy-start(f32[1024]{0:T(1024)S(1)} %fusion.118) | copy-start | bytes 12292
  274.4 4.4 copy-start.78
  274.4 4.4 copy-start.80
  328.9 56.3 %copy-start.7 = (f32[1024,768]{0,1:T(8,128)}, f32[1024,768]{0,1:T(8,128)S(1)}, u32[]{:S(2)}) copy-start(f32[1024,768]{0,1:T(8,128)S(1)} %get-tuple-element.490) | copy-start | bytes 9437188
  329.0 56.3 %copy-start.64 = (f32[1024]{0:T(1024)}, f32[1024]{0:T(1024)S(1)}, u32[]{:S(2)}) copy-start(f32[1024]{0:T(1024)S(1)} %broadcast_multiply_fusion.1) | copy-start | bytes 12292
  329.7 55.6 %copy-start.69 = (f32[1024]{0:T(1024)}, f32[1024]{0:T(1024)S(1)}, u32[]{:S(2)}) copy-start(f32[1024]{0:T(1024)S(1)} %fusion.119) | copy-start | bytes 12292
  329.7 8.7 copy-start.101
  329.7 8.7 copy-start.113
  338.3 11.8 %copy-start.8 = (bf16[1024,768]{0,1:T(8,128)(2,1)S(1)}, bf16[1024,768]{0,1:T(8,128)(2,1)}, u32[]{:S(2)}) copy-start(bf16[1024,768]{0,1:T(8,128)(2,1)} %copy.135) | copy-start | bytes 4718596
  357.3 18.1 %copy-start.48 = (bf16[1024,768]{0,1:T(8,128)(2,1)}, bf16[1024,768]{0,1:T(8,128)(2,1)S(1)}, u32[]{:S(2)}) copy-start(bf16[1024,768]{0,1:T(8,128)(2,1)S(1)} %get-tuple-element.459) | copy-start | bytes 4718596
  386.0 5.4 copy-start.27
  386.1 5.4 copy-start.97
  416.7 7.2 copy-start.37
  441.4 7.2 copy-start.37
  469.3 5.4 copy-start.59
  469.4 5.4 copy-start.84
  475.5 19.5 %slice-start.2 = ((s8[4718592]{0:T(1024)(128)(4,1)}), s8[4194304]{0:T(1024)(128)(4,1)S(1)}, s32[]{:S(2)}) async-start(s8[4718592]{0:T(1024)(128)(4,1)} %bitcast.288), calls=%async_computation.14 | async-start | bytes 8388608
  476.5 18.5 %copy-start.50 = (bf16[1024,768]{0,1:T(8,128)(2,1)}, bf16[1024,768]{0,1:T(8,128)(2,1)S(1)}, u32[]{:S(2)}) copy-start(bf16[1024,768]{0,1:T(8,128)(2,1)S(1)} %get-tuple-element.457) | copy-start | bytes 4718596
  477.0 18.0 %copy-start.5 = (f32[1024,768]{0,1:T(8,128)S(1)}, f32[1024,768]{0,1:T(8,128)}, u32[]{:S(2)}) copy-start(f32[1024,768]{0,1:T(8,128)} %copy-done.4) | copy-start | bytes 9437188
  477.0 18.0 %slice-start.3 = ((s8[4718592]{0:T(1024)(128)(4,1)}), s8[524288]{0:T(1024)(128)(4,1)S(1)}, s32[]{:S(2)}) async-start(s8[4718592]{0:T(1024)(128)(4,1)} %bitcast.288), calls=%async_computation.15 | async-start | bytes 1048576
  477.0 18.0 %copy-start.53 = (f32[768]{0:T(1024)S(1)}, f32[768]{0:T(1024)}, u32[]{:S(2)}) copy-start(f32[768]{0:T(1024)} %copy-done.52) | copy-start | bytes 9220
  477.0 18.0 %copy-start.62 = (f32[1024]{0:T(1024)S(1)}, f32[1024]{0:T(1024)}, u32[]{:S(2)}) copy-start(f32[1024]{0:T(1024)} %copy-done.61) | copy-start | bytes 12292
  477.1 18.0 %copy-start.67 = (f32[1024]{0:T(1024)S(1)}, f32[1024]{0:T(1024)}, u32[]{:S(2)}) copy-start(f32[1024]{0:T(1024)} %copy-done.66) | copy-start | bytes 12292
  495.1 8.9 copy-start.82
  504.9 6.1 copy-start.95
  511.0 223.8 %reduce-scatter.5.cloned.1.call-start = ((), (), s32[]{:S(2)}) async-start(), calls=%async_computation.8 | async-start | bytes 7299072 | tf_op jit(solution)/shard_map/reduce_scatter | solution.py:268
  517.6 4.0 copy-start.3
  517.6 4.0 copy-start.58
  531.0 7.4 copy-start.32
  555.8 7.3 copy-start.32
  575.0 4.5 copy-start.21
  575.0 4.6 slice-start.4
  581.2 4.1 copy-start.60
  581.3 4.1 copy-start.44
  592.0 13.0 %copy-start.51 = (bf16[1024,768]{0,1:T(8,128)(2,1)S(1)}, bf16[1024,768]{0,1:T(8,128)(2,1)}, u32[]{:S(2)}) copy-start(bf16[1024,768]{0,1:T(8,128)(2,1)} %copy-done.50) | copy-start | bytes 4718596
  592.0 284.1 %reduce-scatter.11.cloned.1.call-start = ((), (), s32[]{:S(2)}) async-start(), calls=%async_computation.11 | async-start | bytes 9732096 | tf_op jit(solution)/shard_map/reduce_scatter | solution.py:277
  619.3 9.6 copy-start.6
  619.3 9.6 copy-start.63
  619.3 9.6 copy-start.68
  619.3 399.0 %reduce-scatter.9.cloned.1.call-start = ((), (), s32[]{:S(2)}) async-start(), calls=%async_computation.10 | async-start | bytes 9732096 | tf_op jit(solution)/shard_map/reduce_scatter | solution.py:275
  640.6 48.7 %copy-start.96 = (f32[1024]{0:T(1024)S(1)}, f32[1024]{0:T(1024)}, u32[]{:S(2)}) copy-start(f32[1024]{0:T(1024)} %copy-done.95) | copy-start | bytes 12292
  (87 other events, 158.0 us)
Sparse Core Ops, SparseCore 0:
  10.9 63.1 all-gather.4
  77.0 53.0 all-gather.6
  133.0 62.6 all-gather.8
  198.5 62.4 all-gather.10
  511.1 97.8 reduce-scatter.6
  616.1 118.7 reduce-scatter.4
  741.3 134.7 reduce-scatter.10
  883.7 134.5 reduce-scatter.8
where the time goes:
time: 1030 us
  waiting for transfers between devices  441 us (43%)
  matrix products  288 us (28%)
  local copies, waits for them, and re-layouts  130 us (13%)
  blocking collectives  83.4 us (8%)
  other arithmetic  64 us (6%)
  between operations  16.3 us (2%)
    reduce_scatter x1, waiting for transfers between devices, local(): lax.psum_scatter(totals[7], ('dp', 'fsdp'), scatter_dimension=0, tiled=True)  142 us
    reduce_scatter x1, waiting for transfers between devices, local(): lax.psum_scatter(totals[9], ('dp', 'fsdp'), scatter_dimension=0, tiled=True)  141 us
    unnamed x2, blocking collectives  83.4 us
    dot_general x8, matrix products, dot_back(): lax.dot_general(left, right, (((1,), (1,)), ((), ())), preferred_element_...  73.7 us
    dot_general x8, matrix products, dot_rows(): lax.dot_general(left, right, (((0,), (0,)), ((), ())), preferred_element_...  61.9 us
    all_gather x1, waiting for transfers between devices, local(): lax.all_gather(w_in, ('dp', 'fsdp'), axis=0, tiled=True)  60.1 us
    dot_general x8, matrix products, product(): return jnp.dot(left, right, preferred_element_type=jnp.float32)  58.8 us
    all_gather x1, waiting for transfers between devices, local(): lax.all_gather(w_back, ('dp', 'fsdp'), axis=0, tiled=True)  54.7 us
  transfers between devices with their start and end apart: 8, of which 6 were waited for; matrix products, arithmetic and copies ran while one was open for 22% of the time, Pallas kernels for 0%

commit v1 on v0

v1 whole, which is shorter than its diff:
```python
import jax
import jax.numpy as jnp
from jax import lax
from jax.experimental import pallas as pl
from jax.experimental.pallas import tpu as pltpu
from jax.sharding import PartitionSpec as P

D = 768
HEADS = 12
HEAD_DIM = 64
APPS = 2
PAIR = 2 * HEAD_DIM
AXES = ("dp", "fsdp")
BF = jnp.bfloat16
F32 = jnp.float32
NN = (((1,), (0,)), ((), ()))
NT = (((1,), (1,)), ((), ()))
TN = (((0,), (0,)), ((), ()))
VMEM = 56 * 2**20
BQ, BV, BO, G1, S1, BB, G2, S2 = range(8)


def mm(left, right, dims):
    return lax.dot_general(left, right, dims, preferred_element_type=F32)


def params(limit=VMEM):
    return pltpu.CompilerParams(vmem_limit_bytes=limit)


def cost(flops, nbytes, trans=0):
    return pl.CostEstimate(flops=int(flops), bytes_accessed=int(nbytes), transcendentals=int(trans))


def once(shape, index):
    return pl.BlockSpec(shape, index, pipeline_mode=pl.Buffered(1))


def normed(z):
    centered = z - jnp.mean(z, axis=-1, keepdims=True)
    root = lax.rsqrt(jnp.mean(centered * centered, axis=-1, keepdims=True) + 1e-12)
    return centered * root, root


def normed_back(n, root, e):
    return root * (e - jnp.mean(e, axis=-1, keepdims=True) - n * jnp.mean(e * n, axis=-1, keepdims=True))


def colsum(v):
    return jnp.sum(v, axis=0, keepdims=True)


def qkv_body(x_ref, w_ref, vec_ref, o_ref, xt_ref):
    part = pl.program_id(0)

    @pl.when(part == 0)
    def _():
        xt_ref[...] = x_ref[...].T

    acc = mm(x_ref[...], w_ref[...], NN)
    bias = jnp.where(part == 0, vec_ref[BQ : BQ + 1, :], jnp.where(part == 2, vec_ref[BV : BV + 1, :], 0.0))
    o_ref[...] = (acc + bias).astype(BF)


def qkv_call(x, w, vec):
    rows = x.shape[0]
    return pl.pallas_call(
        qkv_body,
        grid=(3,),
        in_specs=[
            once((rows, D), lambda i: (0, 0)),
            pl.BlockSpec((D, D), lambda i: (0, i)),
            once((8, D), lambda i: (0, 0)),
        ],
        out_specs=[pl.BlockSpec((rows, D), lambda i: (0, i)), pl.BlockSpec((D, rows), lambda i: (0, 0))],
        out_shape=[jax.ShapeDtypeStruct((rows, 3 * D), BF), jax.ShapeDtypeStruct((D, rows), BF)],
        compiler_params=params(),
        cost_estimate=cost(6 * rows * D * D, 2 * (rows * D * 5 + 3 * D * D)),
        name="qkv",
    )(x, w, vec)


def attend_body(seq, pairs, len_ref, q_ref, k_ref, v_ref, o_ref, l_ref):
    count = len_ref[pl.program_id(0)]
    lane = lax.broadcasted_iota(jnp.int32, (seq, PAIR), 1)
    ok = lax.broadcasted_iota(jnp.int32, (1, seq), 1) < count
    units = [(pr, h) for pr in range(pairs) for h in range(2)]

    def score(unit):
        pr, h = unit
        cols = slice(pr * PAIR, (pr + 1) * PAIR)
        mine = (lane >= HEAD_DIM) == (h == 1)
        q = jnp.where(mine, q_ref[:, cols] * BF(0.125), BF(0))
        return jnp.where(ok, mm(q, k_ref[:, cols], NT), -1e30)

    ahead = score(units[0])
    held = {}
    for i, (pr, h) in enumerate(units):
        s = ahead
        if i + 1 < len(units):
            ahead = score(units[i + 1])
        cols = slice(pr * PAIR, (pr + 1) * PAIR)
        top = jnp.max(s, axis=1, keepdims=True)
        p = jnp.exp(s - top)
        total = jnp.sum(p, axis=1, keepdims=True)
        held[h] = mm(p.astype(BF), v_ref[:, cols], NN) / total
        l_ref[0, pr, h : h + 1, :] = (top + jnp.log(total)).reshape(1, seq)
        if h == 1:
            o_ref[:, cols] = jnp.where(lane < HEAD_DIM, held[0], held[1]).astype(BF)


def attend_call(qkv, lengths, pairs=3):
    rows = qkv.shape[0]
    count = lengths.shape[0]
    seq = rows // count
    groups = D // PAIR // pairs
    wide = PAIR * pairs

    def part(o):
        return pl.BlockSpec((seq, wide), lambda s, p, n: (s, o * groups + p))

    def body(*refs):
        attend_body(seq, pairs, *refs)

    flops = 4 * count * HEADS * seq * seq * HEAD_DIM
    return pl.pallas_call(
        body,
        grid_spec=pltpu.PrefetchScalarGridSpec(
            num_scalar_prefetch=1,
            grid=(count, groups),
            in_specs=[part(0), part(1), part(2)],
            out_specs=[part(0), pl.BlockSpec((1, pairs, 2, seq), lambda s, p, n: (s, p, 0, 0))],
        ),
        out_shape=[
            jax.ShapeDtypeStruct((rows, D), BF),
            jax.ShapeDtypeStruct((count, D // PAIR, 2, seq), F32),
        ],
        compiler_params=params(),
        cost_estimate=cost(4 * flops, 8 * rows * D, count * HEADS * seq * seq),
        name="attend",
    )(lengths, qkv, qkv, qkv)


def gelu_both(u):
    a = 0.7978845608028654
    sq = u * u
    t = jnp.tanh(u * (a + (a * 0.044715) * sq))
    half = 0.5 + 0.5 * t
    slope = half + (u * (0.5 - 0.5 * t * t)) * (a + (3 * a * 0.044715) * sq)
    return u * half, slope


def ffn_body(
    steps, x_ref, ctx_ref, wo_ref, vec_ref, wi_ref, bi_ref, wb_ref,
    z1_ref, h1t_ref, ctxt_ref, g_ref, gp_ref, z2_ref, y_ref, yb_ref,
    h1_s, h1b_s, acc_s,
):
    step = pl.program_id(0)

    @pl.when(step == 0)
    def _():
        ctx = ctx_ref[...]
        z1 = x_ref[...].astype(F32) + mm(ctx, wo_ref[...], NN) + vec_ref[BO : BO + 1, :]
        z1_ref[...] = z1
        n, _ = normed(z1)
        h1 = n * vec_ref[G1 : G1 + 1, :] + vec_ref[S1 : S1 + 1, :]
        h1_s[...] = h1
        low = h1.astype(BF)
        h1b_s[...] = low
        h1t_ref[...] = low.T
        ctxt_ref[...] = ctx.T

    f = mm(h1b_s[...], wi_ref[...], NN) + bi_ref[...]
    g, slope = gelu_both(f)
    g = g.astype(BF)
    g_ref[...] = g
    gp_ref[...] = slope.astype(BF)
    more = mm(g, wb_ref[...], NN)

    @pl.when(step == 0)
    def _():
        acc_s[...] = more

    @pl.when(step > 0)
    def _():
        acc_s[...] += more

    @pl.when(step == steps - 1)
    def _():
        z2 = h1_s[...] + acc_s[...] + vec_ref[BB : BB + 1, :]
        z2_ref[...] = z2
        n, _ = normed(z2)
        y = n * vec_ref[G2 : G2 + 1, :] + vec_ref[S2 : S2 + 1, :]
        y_ref[...] = y
        yb_ref[...] = y.astype(BF)


def ffn_call(x, ctx, wo, vec, wi, bi, wb, chunk=512):
    rows = x.shape[0]
    ff = wi.shape[1]
    steps = ff // chunk
    full = once((rows, D), lambda i: (0, 0))
    keep = once((rows, D), lambda i: (0, 0))
    cols = pl.BlockSpec((rows, chunk), lambda i: (0, i))
    flip = once((D, rows), lambda i: (0, 0))

    def body(*refs):
        ffn_body(steps, *refs)

    return pl.pallas_call(
        body,
        grid=(steps,),
        in_specs=[
            full,
            full,
            once((D, D), lambda i: (0, 0)),
            once((8, D), lambda i: (0, 0)),
            pl.BlockSpec((D, chunk), lambda i: (0, i)),
            pl.BlockSpec((1, chunk), lambda i: (0, i)),
            pl.BlockSpec((chunk, D), lambda i: (i, 0)),
        ],
        out_specs=[keep, flip, flip, cols, cols, keep, keep, keep],
        out_shape=[
            jax.ShapeDtypeStruct((rows, D), F32),
            jax.ShapeDtypeStruct((D, rows), BF),
            jax.ShapeDtypeStruct((D, rows), BF),
            jax.ShapeDtypeStruct((rows, ff), BF),
            jax.ShapeDtypeStruct((rows, ff), BF),
            jax.ShapeDtypeStruct((rows, D), F32),
            jax.ShapeDtypeStruct((rows, D), F32),
            jax.ShapeDtypeStruct((rows, D), BF),
        ],
        scratch_shapes=[pltpu.VMEM((rows, D), F32), pltpu.VMEM((rows, D), BF), pltpu.VMEM((rows, D), F32)],
        compiler_params=params(),
        cost_estimate=cost(2 * rows * D * (D + 2 * ff), 20 * rows * D + 4 * rows * ff + 4 * D * ff, rows * ff),
        name="ffn",
    )(x, ctx, wo, vec, wi, bi, wb)


def ffn_back_body(
    steps, dy_ref, z2_ref, z1_ref, gp_ref, wb_ref, wi_ref, wo_ref, vec_ref,
    e2_ref, e1_ref, dz1_ref, ea_ref, dctx_ref, sums_ref, bi_ref,
    dz2_s, acc_s,
):
    step = pl.program_id(0)

    @pl.when(step == 0)
    def _():
        dy = dy_ref[...].astype(F32)
        n, root = normed(z2_ref[...])
        sums_ref[G2 : G2 + 1, :] = colsum(dy * n)
        sums_ref[S2 : S2 + 1, :] = colsum(dy)
        dz2 = normed_back(n, root, dy * vec_ref[G2 : G2 + 1, :])
        dz2_s[...] = dz2
        low = dz2.astype(BF)
        e2_ref[...] = low
        sums_ref[BB : BB + 1, :] = colsum(low.astype(F32))

    df = mm(e2_ref[...], wb_ref[...], NT) * gp_ref[...].astype(F32)
    e1 = df.astype(BF)
    e1_ref[...] = e1
    bi_ref[...] = colsum(e1.astype(F32))
    more = mm(e1, wi_ref[...], NT)

    @pl.when(step == 0)
    def _():
        acc_s[...] = more

    @pl.when(step > 0)
    def _():
        acc_s[...] += more

    @pl.when(step == steps - 1)
    def _():
        dh1 = dz2_s[...] + acc_s[...]
        n, root = normed(z1_ref[...])
        sums_ref[G1 : G1 + 1, :] = colsum(dh1 * n)
        sums_ref[S1 : S1 + 1, :] = colsum(dh1)
        dz1 = normed_back(n, root, dh1 * vec_ref[G1 : G1 + 1, :])
        dz1_ref[...] = dz1
        low = dz1.astype(BF)
        ea_ref[...] = low
        sums_ref[BO : BO + 1, :] = colsum(low.astype(F32))
        sums_ref[BQ : BQ + 1, :] = jnp.zeros((1, D), F32)
        sums_ref[BV : BV + 1, :] = jnp.zeros((1, D), F32)
        dctx_ref[...] = mm(low, wo_ref[...], NT).astype(BF)


def ffn_back_call(dy, z2, z1, gp, wb, wi, wo, vec, chunk=512):
    rows = dy.shape[0]
    ff = wi.shape[1]
    steps = ff // chunk
    keep = once((rows, D), lambda i: (0, 0))
    cols = pl.BlockSpec((rows, chunk), lambda i: (0, i))

    def body(*refs):
        ffn_back_body(steps, *refs)

    return pl.pallas_call(
        body,
        grid=(steps,),
        in_specs=[
            keep,
            keep,
            keep,
            cols,
            pl.BlockSpec((chunk, D), lambda i: (i, 0)),
            pl.BlockSpec((D, chunk), lambda i: (0, i)),
            once((D, D), lambda i: (0, 0)),
            once((8, D), lambda i: (0, 0)),
        ],
        out_specs=[
            keep,
            cols,
            keep,
            keep,
            keep,
            once((8, D), lambda i: (0, 0)),
            pl.BlockSpec((1, chunk), lambda i: (0, i)),
        ],
        out_shape=[
            jax.ShapeDtypeStruct((rows, D), BF),
            jax.ShapeDtypeStruct((rows, ff), BF),
            jax.ShapeDtypeStruct((rows, D), F32),
            jax.ShapeDtypeStruct((rows, D), BF),
            jax.ShapeDtypeStruct((rows, D), BF),
            jax.ShapeDtypeStruct((8, D), F32),
            jax.ShapeDtypeStruct((1, ff), F32),
        ],
        scratch_shapes=[pltpu.VMEM((rows, D), F32), pltpu.VMEM((rows, D), F32)],
        compiler_params=params(),
        cost_estimate=cost(2 * rows * D * (D + 2 * ff), 20 * rows * D + 4 * rows * ff + 4 * D * ff),
        name="ffn_back",
    )(dy, z2, z1, gp, wb, wi, wo, vec)


def attend_back_body(seq, pairs, len_ref, q_ref, k_ref, v_ref, d_ref, l_ref, eq_ref, ek_ref, ev_ref, bq_ref, bv_ref):
    count = len_ref[pl.program_id(0)]
    lane = lax.broadcasted_iota(jnp.int32, (seq, PAIR), 1)
    ok = lax.broadcasted_iota(jnp.int32, (seq, seq), 0) < count
    units = [(pr, h) for pr in range(pairs) for h in range(2)]

    def score(unit):
        pr, h = unit
        cols = slice(pr * PAIR, (pr + 1) * PAIR)
        mine = (lane >= HEAD_DIM) == (h == 1)
        q = jnp.where(mine, q_ref[:, cols] * BF(0.125), BF(0))
        s = jnp.where(ok, mm(k_ref[:, cols], q, NT), -1e30)
        return s, mm(v_ref[:, cols], jnp.where(mine, d_ref[:, cols], BF(0)), NT)

    ahead = score(units[0])
    eq, ek, ev = {}, {}, {}
    for i, (pr, h) in enumerate(units):
        s, dp = ahead
        if i + 1 < len(units):
            ahead = score(units[i + 1])
        cols = slice(pr * PAIR, (pr + 1) * PAIR)
        if h == 0:
            kt = (k_ref[:, cols] * BF(0.125)).T
        p = jnp.exp(s - l_ref[0, pr, h : h + 1, :])
        pd = p * dp
        ds = (pd - p * colsum(pd)).astype(BF)
        ev[h] = mm(p.astype(BF), d_ref[:, cols], NN)
        ek[h] = mm(ds, q_ref[:, cols] * BF(0.125), NN)
        eq[h] = mm(kt[h * HEAD_DIM : (h + 1) * HEAD_DIM], ds, NN)
        if h == 1:
            low = jnp.concatenate([eq[0], eq[1]], axis=0).T.astype(BF)
            eq_ref[:, cols] = low
            bq_ref[0, :, cols] = colsum(low.astype(F32))
            ek_ref[:, cols] = jnp.where(lane < HEAD_DIM, ek[0], ek[1]).astype(BF)
            low = jnp.where(lane < HEAD_DIM, ev[0], ev[1]).astype(BF)
            ev_ref[:, cols] = low
            bv_ref[0, :, cols] = colsum(low.astype(F32))


def attend_back_call(qkv, dctx, lse, lengths, pairs=3):
    rows = qkv.shape[0]
    count = lengths.shape[0]
    seq = rows // count
    groups = D // PAIR // pairs
    wide = PAIR * pairs

    def part(o):
        return pl.BlockSpec((seq, wide), lambda s, p, n: (s, o * groups + p))

    def body(*refs):
        attend_back_body(seq, pairs, *refs)

    flops = 10 * count * HEADS * seq * seq * HEAD_DIM
    line = pl.BlockSpec((1, 1, wide), lambda s, p, n: (s, 0, p))
    return pl.pallas_call(
        body,
        grid_spec=pltpu.PrefetchScalarGridSpec(
            num_scalar_prefetch=1,
            grid=(count, groups),
            in_specs=[
                part(0),
                part(1),
                part(2),
                part(0),
                pl.BlockSpec((1, pairs, 2, seq), lambda s, p, n: (s, p, 0, 0)),
            ],
            out_specs=[part(0), part(0), part(0), line, line],
        ),
        out_shape=[jax.ShapeDtypeStruct((rows, D), BF)] * 3 + [jax.ShapeDtypeStruct((count, 1, D), F32)] * 2,
        compiler_params=params(),
        cost_estimate=cost(4 * flops, 14 * rows * D, count * HEADS * seq * seq),
        name="attend_back",
    )(lengths, qkv, qkv, qkv, dctx, lse)


def dx_body(dz1_ref, eq_ref, ek_ref, ev_ref, w_ref, o_ref):
    acc = mm(eq_ref[...], w_ref[:, :D], NT)
    acc += mm(ek_ref[...], w_ref[:, D : 2 * D], NT)
    acc += mm(ev_ref[...], w_ref[:, 2 * D :], NT)
    o_ref[...] = (dz1_ref[...] + acc).astype(o_ref.dtype)


def dx_call(dz1, eq, ek, ev, w, dtype, block=256):
    rows = dz1.shape[0]
    line = pl.BlockSpec((block, D), lambda i: (i, 0))
    return pl.pallas_call(
        dx_body,
        grid=(rows // block,),
        in_specs=[line, line, line, line, once((D, 3 * D), lambda i: (0, 0))],
        out_specs=line,
        out_shape=jax.ShapeDtypeStruct((rows, D), dtype),
        compiler_params=params(),
        cost_estimate=cost(6 * rows * D * D, 14 * rows * D + 6 * D * D),
        name="dx",
    )(dz1, eq, ek, ev, w)


def wgrad_t_body(a_ref, b_ref, c_ref, d_ref, o_ref):
    o_ref[...] = (mm(a_ref[...], b_ref[...], TN) + mm(c_ref[...], d_ref[...], TN)).astype(BF)


def wgrad_t_call(a, b, c, d, block=768):
    rows, m = a.shape
    n = b.shape[1]
    part = pl.BlockSpec((rows, block), lambda i: (0, i))
    held = once((rows, n), lambda i: (0, 0))
    return pl.pallas_call(
        wgrad_t_body,
        grid=(m // block,),
        in_specs=[part, held, part, held],
        out_specs=pl.BlockSpec((block, n), lambda i: (i, 0)),
        out_shape=jax.ShapeDtypeStruct((m, n), BF),
        compiler_params=params(),
        cost_estimate=cost(4 * rows * m * n, 4 * rows * (m + n) + 2 * m * n),
        name="wgrad_t",
    )(a, b, c, d)


def wgrad_body(a_ref, b_ref, c_ref, d_ref, o_ref):
    o_ref[...] = (mm(a_ref[...], b_ref[...], NN) + mm(c_ref[...], d_ref[...], NN)).astype(BF)


def wgrad_call(a, b, c, d, block=768):
    m, rows = a.shape
    n = b.shape[1]
    block = min(block, n)
    held = once((m, rows), lambda i: (0, 0))
    part = pl.BlockSpec((rows, block), lambda i: (0, i))
    return pl.pallas_call(
        wgrad_body,
        grid=(n // block,),
        in_specs=[held, part, held, part],
        out_specs=pl.BlockSpec((m, block), lambda i: (0, i)),
        out_shape=jax.ShapeDtypeStruct((m, n), BF),
        compiler_params=params(),
        cost_estimate=cost(4 * rows * m * n, 4 * rows * (m + n) + 2 * m * n),
        name="wgrad",
    )(a, b, c, d)


def layer_forward(x, low, weights, lengths):
    w_qkv, w_out, w_in, w_back, vec, bias_in = weights
    qkv, lowt = qkv_call(low, w_qkv, vec)
    ctx, lse = attend_call(qkv, lengths)
    z1, h1t, ctxt, g, slope, z2, y, y_low = ffn_call(x, ctx, w_out, vec, w_in, bias_in, w_back)
    return y, y_low, (lowt, qkv, lse, z1, h1t, ctxt, g, slope, z2)


class Grid:
    def __init__(self, sizes):
        self.dp, self.fsdp = sizes["dp"], sizes["fsdp"]
        self.count = self.dp * self.fsdp
        self.x, self.core = self.dp // 2, 2
        self.y = self.fsdp // 4
        self.z = self.fsdp // self.y if self.y else 0
        self.staged = self.x == 2 and self.y == 2

    def place(self):
        dp, fsdp = lax.axis_index("dp"), lax.axis_index("fsdp")
        return dp // 2, dp % 2, fsdp // self.y, fsdp % self.y

    def shift(self, dim, step):
        sizes = (self.x, self.core, self.z, self.y)
        pairs = []
        for i in range(self.count):
            at = [i // (self.core * self.fsdp), i // self.fsdp % self.core, i % self.fsdp // self.y, i % self.y]
            at[dim] = (at[dim] + step) % sizes[dim]
            pairs.append((i, ((at[0] * self.core + at[1]) * self.z + at[2]) * self.y + at[3]))
        return pairs

    def send(self, value, dim, step=1):
        return lax.ppermute(value, AXES, self.shift(dim, step))


X, CORE, Z, Y = range(4)


def assemble_body(half, at_ref, *refs):
    parts, out_ref, sems = refs[:16], refs[16], refs[17]
    x, core, y = at_ref[0], at_ref[1], at_ref[2]
    copies = []
    for i, part in enumerate(parts):
        side, dx, dc, dy = i >> 3, (i >> 2) & 1, (i >> 1) & 1, i & 1
        target = out_ref.at[
            (x + dx) % 2, (core + dc) % 2, :, (y + dy) % 2, :, pl.ds(side * half, half)
        ]
        copies.append(pltpu.make_async_copy(part, target, sems.at[i]))
    for copy in copies:
        copy.start()
    for copy in copies:
        copy.wait()


def gather_rows(grid, shard):
    rows, cols = shard.shape
    half = cols // 2
    x, core, z, y = grid.place()
    ring = [shard] + [grid.send(shard, Z, k) for k in range(1, grid.z)]
    ring = ring[::-1]
    line = lax.dynamic_slice_in_dim(jnp.stack(ring + ring), grid.z - 1 - z, grid.z, 0)
    left, right = line[:, :, :half], line[:, :, half:]
    left_y = grid.send(left, Y)
    right_x = grid.send(right, X)
    left_x, left_xy = grid.send(left, X), grid.send(left_y, X)
    right_y, right_xy = grid.send(right, Y), grid.send(right_x, Y)
    parts = []
    for near, by_y, by_x, both in ((left, left_y, left_x, left_xy), (right, right_y, right_x, right_xy)):
        for pair in ((near, by_y), (by_x, both)):
            parts += list(pair)
            parts += [grid.send(v, CORE) for v in pair]
    whole = pl.pallas_call(
        lambda *refs: assemble_body(half, *refs),
        grid_spec=pltpu.PrefetchScalarGridSpec(
            num_scalar_prefetch=1,
            grid=(1,),
            in_specs=[pl.BlockSpec(memory_space=pl.ANY)] * 16,
            out_specs=pl.BlockSpec(memory_space=pl.ANY),
            scratch_shapes=[pltpu.SemaphoreType.DMA((16,))],
        ),
        out_shape=jax.ShapeDtypeStruct((2, 2, grid.z, 2, rows, cols), shard.dtype),
        compiler_params=pltpu.CompilerParams(vmem_limit_bytes=2 * 2**20),
        cost_estimate=cost(0, 4 * rows * cols * grid.count),
        name="assemble",
    )(jnp.stack([x, core, y]).astype(jnp.int32), *parts)
    return whole.reshape(grid.count * rows, cols)


def pick(value, index, dim):
    return lax.dynamic_index_in_dim(value, index, dim, keepdims=False)


def scatter_rows(grid, total):
    rows = total.shape[0] // grid.count
    cols = total.shape[1]
    half = cols // 2
    kind = total.dtype
    x, core, z, y = grid.place()
    view = total.reshape(2, 2, grid.z, 2, rows, cols)
    came = grid.send(pick(view, 1 - core, 1), CORE)
    mine = pick(view, core, 1)

    def both(pieces):
        a, b = pieces
        return (a.astype(F32) + b.astype(F32)).astype(kind)

    left, right = (mine[..., :half], came[..., :half]), (mine[..., half:], came[..., half:])
    left_out = both([pick(v, 1 - x, 0) for v in left])
    left_keep = both([pick(v, x, 0) for v in left])
    right_out = both([pick(v, 1 - y, 2) for v in right])
    right_keep = both([pick(v, y, 2) for v in right])
    left_in, right_in = grid.send(left_out, X), grid.send(right_out, Y)
    left, right = (left_keep, left_in), (right_keep, right_in)
    left_out = both([pick(v, 1 - y, 1) for v in left])
    left_keep = both([pick(v, y, 1) for v in left])
    right_out = both([pick(v, 1 - x, 0) for v in right])
    right_keep = both([pick(v, x, 0) for v in right])
    left_in, right_in = grid.send(left_out, Y), grid.send(right_out, X)
    line = jnp.concatenate([both((left_keep, left_in)), both((right_keep, right_in))], axis=-1)
    result = pick(line, z, 0).astype(F32)
    for k in range(1, grid.z):
        result += grid.send(pick(line, (z + k) % grid.z, 0), Z, k).astype(F32)
    return result


def gather(grid, shard):
    if grid.staged:
        return gather_rows(grid, shard)
    return lax.all_gather(shard, AXES, axis=0, tiled=True)


def scatter(grid, total):
    if grid.staged:
        return scatter_rows(grid, total)
    return lax.psum_scatter(total.astype(F32), AXES, scatter_dimension=0, tiled=True)


def pad_to(value, rows, cols):
    return jnp.pad(value, ((0, rows - value.shape[0]), (0, cols - value.shape[1])))


def make_local(grid):
    def local(
        tokens, lengths, w_qkv, bias_q, bias_v, w_out, bias_out, gain_one, shift_one, w_in, bias_in,
        w_back, bias_back, gain_two, shift_two, cotangent,
    ):
        rows = bias_q.shape[0]
        span = bias_in.shape[0]
        small = jnp.concatenate(
            [bias_q, bias_v, bias_out, gain_one, shift_one, bias_back, gain_two, shift_two, bias_in]
        )
        tail = 8
        packed = jnp.concatenate([w_out, pad_to(small[None], tail, D)], axis=0)
        packed = gather(grid, packed).reshape(grid.count, rows + tail, D)
        w_qkv = gather(grid, w_qkv)
        w_in = gather(grid, w_in)
        w_back = gather(grid, w_back)
        w_out = packed[:, :rows].reshape(D, D)
        small = packed[:, rows, : 8 * rows + span].astype(F32)
        vec = small[:, : 8 * rows].reshape(grid.count, 8, rows).swapaxes(0, 1).reshape(8, D)
        bias_in = small[:, 8 * rows :].reshape(1, -1)
        weights = (w_qkv, w_out, w_in, w_back, vec, bias_in)

        x, low = tokens, tokens
        saved = []
        for _ in range(APPS):
            x, low, stored = layer_forward(x, low, weights, lengths)
            saved.append(stored)
        activations = low

        grad = cotangent
        back = [None] * APPS
        for step in reversed(range(APPS)):
            lowt, qkv, lse, z1, h1t, ctxt, g, slope, z2 = saved[step]
            e2, e1, dz1, ea, dctx, sums, sum_in = ffn_back_call(grad, z2, z1, slope, w_back, w_in, w_out, vec)
            eq, ek, ev, sum_q, sum_v = attend_back_call(qkv, dctx, lse, lengths)
            grad = dx_call(dz1, eq, ek, ev, w_qkv, F32 if step else BF)
            back[step] = (e2, e1, ea, eq, ek, ev, sums, sum_in, sum_q, sum_v)
        one, two = back
        w_back_grad = scatter(grid, wgrad_t_call(saved[1][6], two[0], saved[0][6], one[0]))
        w_in_grad = scatter(grid, wgrad_call(saved[1][4], two[1], saved[0][4], one[1]))
        w_out_grad = scatter(grid, wgrad_call(saved[1][5], two[2], saved[0][5], one[2]))
        parts = [scatter(grid, wgrad_call(saved[1][0], two[i], saved[0][0], one[i])) for i in (3, 4, 5)]
        w_qkv_grad = jnp.concatenate(parts, axis=1)

        sums = one[6] + two[6]
        sum_q = jnp.sum(one[8] + two[8], axis=(0, 1))
        sum_v = jnp.sum(one[9] + two[9], axis=(0, 1))
        sums = jnp.concatenate([sum_q[None], sum_v[None], sums[2:]], axis=0)
        sums = sums.reshape(8, grid.count, rows).swapaxes(0, 1).reshape(grid.count, 8 * rows)
        sums = jnp.concatenate([sums, (one[7] + two[7]).reshape(grid.count, span)], axis=1)
        wide = -(-(8 * rows + span) // 256) * 256
        owned = scatter(grid, jnp.pad(sums[:, None, :], ((0, 0), (0, 7), (0, wide - sums.shape[1]))).reshape(-1, wide))[0]
        owned = [owned[i * rows : (i + 1) * rows] for i in range(8)] + [owned[8 * rows : 8 * rows + span]]
        return (
            activations, grad, w_qkv_grad, owned[BQ], owned[BV], w_out_grad, owned[BO], owned[G1], owned[S1],
            w_in_grad, owned[8], w_back_grad, owned[BB], owned[G2], owned[S2],
        )

    return local


def solution(mesh):
    wide, line = P(AXES, None), P(AXES)
    return jax.shard_map(
        make_local(Grid(mesh.shape)),
        mesh=mesh,
        in_specs=(wide, line, wide, line, line, wide, line, line, line, wide, line, wide, line, line, line, wide),
        out_specs=(wide, wide, wide, line, line, wide, line, line, line, wide, line, wide, line, line, line),
        check_vma=False,
    )
```

time: 1030 us -> 596 us (0.58)
  waiting for transfers between devices: 441 us -> 99.8 us
  matrix products: 288 us -> 0 us
  Pallas kernels: 0 us -> 281 us
  starting transfers between devices: 0.31 us -> 116 us
  blocking collectives: 83.4 us -> 0 us
  local copies, waits for them, and re-layouts: 130 us -> 71.4 us
  other arithmetic: 64 us -> 13.9 us
  between operations: 16.3 us -> 2.52 us
    reduce_scatter x4 -> x0, waiting for transfers between devices: 317 us -> none  [the longest x1 142 us: local(): lax.psum_scatter(totals[7], ('dp', 'fsdp'), scatter_dimension=0, tiled=True)]
    dot_general x52 -> x0, matrix products: 288 us -> none  [the longest x8 73.7 us: dot_back(): lax.dot_general(left, right, (((1,), (1,)), ((), ())), preferred_element_...]
    pallas_call x0 -> x22, Pallas kernels: none -> 281 us  [the longest x2 59.1 us: ffn_call(): pl.pallas_call(body, grid=(steps,), in_specs=[full, full, once((D, D), la...]
    all_gather x4 -> x0, waiting for transfers between devices: 121 us -> none  [the longest x1 60.1 us: local(): lax.all_gather(w_in, ('dp', 'fsdp'), axis=0, tiled=True)]
    ppermute x0 -> x124, starting transfers between devices: none -> 116 us  [send(): return lax.ppermute(value, AXES, self.shift(dim, step))]
    ppermute x0 -> x124, waiting for transfers between devices: none -> 99.8 us  [send(): return lax.ppermute(value, AXES, self.shift(dim, step))]
    unnamed x2 -> x0, blocking collectives: 83.4 us -> none
    convert_element_type x15 -> x37, other arithmetic: 36.2 us -> 3.12 us  [the longest x36 3.11 us: both(): return (a.astype(F32) + b.astype(F32)).astype(kind)]
  transfers between devices with their start and end apart: 8 -> 124, of which waited for: 6 -> 47; matrix products, arithmetic and copies ran while one was open for 22% -> 7% of each run, Pallas kernels for 0% -> 17%
where the time goes in v1:
time: 596 us; the launch traced here: 585 us
  Pallas kernels  281 us (47%)
  starting transfers between devices  116 us (19%)
  waiting for transfers between devices  99.8 us (17%)
  local copies, waits for them, and re-layouts  71.4 us (12%)
  other arithmetic  13.9 us (2%)
    ppermute x124, starting transfers between devices, send(): return lax.ppermute(value, AXES, self.shift(dim, step))  116 us
    ppermute x124, waiting for transfers between devices, send(): return lax.ppermute(value, AXES, self.shift(dim, step))  99.8 us
    pallas_call x2, Pallas kernels, ffn_call(): pl.pallas_call(body, grid=(steps,), in_specs=[full, full, once((D, D), la...  59.1 us
    pallas_call x2, Pallas kernels, ffn_back_call(): pl.pallas_call(body, grid=(steps,), in_specs=[keep, keep, keep, cols, pl....  56.7 us
    pallas_call x2, Pallas kernels, attend_back_call(): pl.pallas_call(body, grid_spec=pltpu.PrefetchScalarGridSpec(num_scalar_pr...  43.5 us
    pallas_call x5, Pallas kernels, wgrad_call(): pl.pallas_call(wgrad_body, grid=(n // block,), in_specs=[held, part, held...  40.8 us
    unnamed x168, local copies, waits for them, and re-layouts  32 us
    pallas_call x2, Pallas kernels, attend_call(): pl.pallas_call(body, grid_spec=pltpu.PrefetchScalarGridSpec(num_scalar_pr...  26 us
  transfers between devices with their start and end apart: 124, of which 47 were waited for; matrix products, arithmetic and copies ran while one was open for 7% of the time, Pallas kernels for 17%

profile of v1, /device:TPU:0, one launch (start us, length us, event | category | flops | bytes accessed | tf_op | source)
XLA Modules:
  0.0 585.0 jit_solution(16624034393744832760)
XLA Ops:
  0.7 6.1 %concatenate.43 = bf16[288]{0:T(512)(128)(2,1)S(1)} concatenate(bf16[24]{0:T(256)(128)(2,1)} %param.19, bf16[24]{0:T(256)(128)(2,1)} %param.20, bf16[24]{0:T(256)(128)(2,1)} %param.22, bf16[24]{0:T(256)(128)(2,1)} %param.23, bf16[24]{0:T(256)(128)(2,1)} %param.24, bf16[24]{0:T(256)(128)(2,1)} %param.28, bf16[24]{0:T(256)(128)(2,1)} %param.29, bf16[24]{0:T(256)(128)(2,1)} %param.30, ...), dimensions={0} | concatenate | bytes 1152 | tf_op jit(solution)/shard_map/concatenate | solution.py:624
  7.6 5.0 collective-permute-start.17
  14.7 2.9 collective-permute-start.18
  17.6 11.7 %collective-permute-done.18 = bf16[32,768]{1,0:T(8,128)(2,1)S(1)} collective-permute-done((bf16[32,768]{1,0:T(8,128)(2,1)S(1)}, bf16[32,768]{1,0:T(8,128)(2,1)S(1)}, u32[]{:S(2)}, u32[]{:S(2)}) %collective-permute-start.18) | collective-permute-done | bytes 49184 | tf_op jit(solution)/shard_map/ppermute | solution.py:508
  29.3 3.4 collective-permute-start
  34.5 2.1 collective-permute-done
  36.6 5.6 collective-permute-done.1
  42.2 2.3 collective-permute-start.34
  45.2 3.5 collective-permute-done.34
  61.8 2.0 collective-permute-done.31.refs_14_
  68.0 4.2 collective-permute-done.13.refs_13_
  72.1 3.5 collective-permute-done.3.refs_2_
  82.5 2.4 collective-permute-done.64.refs_13_
  85.4 5.0 collective-permute-done.57.refs_5_
  94.5 3.1 collective-permute-done.37.refs_2_
  97.6 2.8 collective-permute-done.47.refs_13_
  100.8 4.1 collective-permute-done.40.refs_5_
  109.0 2.5 collective-permute-done.7.refs_6_
  114.4 2.9 collective-permute-done.58.refs_6_
  140.3 2.4 assemble.4
  146.4 8.2 %qkv.2 = (bf16[1024,2304]{1,0:T(8,128)(2,1)}, bf16[768,1024]{1,0:T(8,128)(2,1)}) custom-call(bf16[1024,768]{1,0:T(8,128)(2,1)} %refs_0_.7, bf16[768,2304]{1,0:T(8,128)(2,1)} %bitcast.441, f32[8,768]{1,0:T(8,128)} %reshape.406.vec_ref.refs_3_.refs_7_), custom_call_target="tpu_custom_call" | custom-call | flops 3623878656 | bytes 11403264 | tf_op jit(solution)/shard_map/qkv/pallas_call | solution.py:67
  155.8 13.1 %attend.2 = (bf16[1024,768]{1,0:T(8,128)(2,1)}, f32[2,6,2,512]{3,2,1,0:T(2,128)}) custom-call(s32[2]{0:T(128)} %refs_0_.11, bf16[1024,2304]{1,0:T(8,128)(2,1)} %get-tuple-element.62.refs_1_.refs_2_.refs_3_, bf16[1024,2304]{1,0:T(8,128)(2,1)} %get-tuple-element.62.refs_1_.refs_2_.refs_3_, bf16[1024,2304]{1,0:T(8,128)(2,1)} %get-tuple-element.62.refs_1_.refs_2_.refs_3_), custom_call_target="tpu_custom_call" | custom-call | flops 6442450944 | bytes 6291456 | tf_op jit(solution)/shard_map/attend/pallas_call | solution.py:126
  168.9 2.3 assemble.7
  171.2 2.2 copy-done.1
  174.7 2.2 copy-done.2
  176.9 29.5 %ffn.2 = (f32[1024,768]{1,0:T(8,128)}, bf16[768,1024]{1,0:T(8,128)(2,1)}, bf16[768,1024]{1,0:T(8,128)(2,1)}, bf16[1024,3072]{1,0:T(8,128)(2,1)}, bf16[1024,3072]...) custom-call(bf16[1024,768]{1,0:T(8,128)(2,1)} %refs_0_.7, ...), custom_call_target="tpu_custom_call" | custom-call | flops 10871635968 | bytes 37748736 | tf_op jit(solution)/shard_map/ffn/pallas_call | solution.py:210
  206.4 8.2 %qkv.3 = (bf16[1024,2304]{1,0:T(8,128)(2,1)}, bf16[768,1024]{1,0:T(8,128)(2,1)}) custom-call(bf16[1024,768]{1,0:T(8,128)(2,1)} %get-tuple-element.65.x_ref, bf16[768,2304]{1,0:T(8,128)(2,1)} %bitcast.442, f32[8,768]{1,0:T(8,128)} %reshape.406.vec_ref.refs_3_.refs_7_), custom_call_target="tpu_custom_call" | custom-call | flops 3623878656 | bytes 11403264 | tf_op jit(solution)/shard_map/qkv/pallas_call | solution.py:67
  214.6 12.9 %attend.3 = (bf16[1024,768]{1,0:T(8,128)(2,1)}, f32[2,6,2,512]{3,2,1,0:T(2,128)}) custom-call(s32[2]{0:T(128)} %refs_0_.11, bf16[1024,2304]{1,0:T(8,128)(2,1)} %get-tuple-element.66.refs_1_.refs_2_.refs_3_, bf16[1024,2304]{1,0:T(8,128)(2,1)} %get-tuple-element.66.refs_1_.refs_2_.refs_3_, bf16[1024,2304]{1,0:T(8,128)(2,1)} %get-tuple-element.66.refs_1_.refs_2_.refs_3_), custom_call_target="tpu_custom_call" | custom-call | flops 6442450944 | bytes 6291456 | tf_op jit(solution)/shard_map/attend/pallas_call | solution.py:126
  227.5 29.5 %ffn.3 = (f32[1024,768]{1,0:T(8,128)}, bf16[768,1024]{1,0:T(8,128)(2,1)}, bf16[768,1024]{1,0:T(8,128)(2,1)}, bf16[1024,3072]{1,0:T(8,128)(2,1)}, bf16[1024,3072]...) custom-call(f32[1024,768]{1,0:T(8,128)} %get-tuple-element.64.refs_0_, ...), custom_call_target="tpu_custom_call" | custom-call | flops 10871635968 | bytes 37748736 | tf_op jit(solution)/shard_map/ffn/pallas_call | solution.py:210
  257.1 28.1 %ffn_back.2 = (bf16[1024,768]{1,0:T(8,128)(2,1)}, bf16[1024,3072]{1,0:T(8,128)(2,1)}, f32[1024,768]{1,0:T(8,128)}, bf16[1024,768]{1,0:T(8,128)(2,1)}, bf16[1024,...) custom-call(bf16[1024,768]{1,0:T(8,128)(2,1)} %refs_0_.9, f32[1024,768]{1,0:T(8,128)} %get-tuple-element.69.refs_1_, ...), custom_call_target="tpu_custom_call" | custom-call | flops 10871635968 | bytes 37748736 | tf_op jit(solution)/shard_map/ffn_back/pallas_call | solution.py:299
  285.1 21.8 %attend_back.2 = (bf16[1024,768]{1,0:T(8,128)(2,1)}, bf16[1024,768]{1,0:T(8,128)(2,1)}, bf16[1024,768]{1,0:T(8,128)(2,1)}, f32[2,1,768]{2,1,0:T(1,128)}, f32[2,1,768]{2,1,0:T(1,128)}) custom-call(s32[2]{0:T(128)} %refs_0_.11, bf16[1024,2304]{1,0:T(8,128)(2,1)} %get-tuple-element.66.refs_1_.refs_2_.refs_3_, ...), custom_call_target="tpu_custom_call" | custom-call | flops 16106127360 | bytes 11010048 | tf_op jit(solution)/shard_map/attend_back/pallas_call | solution.py:391
  306.9 9.0 %dx.2.refs_0_ = f32[1024,768]{1,0:T(8,128)} custom-call(f32[1024,768]{1,0:T(8,128)} %get-tuple-element.72.dz1_ref, bf16[1024,768]{1,0:T(8,128)(2,1)} %get-tuple-element.75.eq_ref.b_ref, bf16[1024,768]{1,0:T(8,128)(2,1)} %get-tuple-element.76.ek_ref.b_ref, bf16[1024,768]{1,0:T(8,128)(2,1)} %get-tuple-element.77.ev_ref.b_ref, bf16[768,2304]{1,0:T(8,128)(2,1)} %bitcast.443), custom_call_target="tpu_custom_call" | custom-call | flops 3623878656 | bytes 14548992 | tf_op jit(solution)/shard_map/dx/pallas_call | solution.py:422
  315.9 28.6 %ffn_back.3 = (bf16[1024,768]{1,0:T(8,128)(2,1)}, bf16[1024,3072]{1,0:T(8,128)(2,1)}, f32[1024,768]{1,0:T(8,128)}, bf16[1024,768]{1,0:T(8,128)(2,1)}, bf16[1024,...) custom-call(f32[1024,768]{1,0:T(8,128)} %dx.2.refs_0_, f32[1024,768]{1,0:T(8,128)} %get-tuple-element.78.refs_1_, ...), custom_call_target="tpu_custom_call" | custom-call | flops 10871635968 | bytes 37748736 | tf_op jit(solution)/shard_map/ffn_back/pallas_call | solution.py:299
  344.5 14.5 %wgrad_t.1 = bf16[3072,768]{1,0:T(8,128)(2,1)} custom-call(bf16[1024,3072]{1,0:T(8,128)(2,1)} %get-tuple-element.105.a_ref, bf16[1024,768]{1,0:T(8,128)(2,1)} %get-tuple-element.106.b_ref, bf16[1024,3072]{1,0:T(8,128)(2,1)} %get-tuple-element.107.c_ref, bf16[1024,768]{1,0:T(8,128)(2,1)} %get-tuple-element.108.d_ref), custom_call_target="tpu_custom_call" | custom-call | flops 9663676416 | bytes 20447232 | tf_op jit(solution)/shard_map/wgrad_t/pallas_call | solution.py:443
  358.9 2.7 constant_dynamic-slice_fusion
  365.2 14.7 %wgrad.9 = bf16[768,3072]{1,0:T(8,128)(2,1)} custom-call(bf16[768,1024]{1,0:T(8,128)(2,1)} %get-tuple-element.101.a_ref, bf16[1024,3072]{1,0:T(8,128)(2,1)} %get-tuple-element.102.b_ref, bf16[768,1024]{1,0:T(8,128)(2,1)} %get-tuple-element.103.c_ref, bf16[1024,3072]{1,0:T(8,128)(2,1)} %get-tuple-element.104.d_ref), custom_call_target="tpu_custom_call" | custom-call | flops 9663676416 | bytes 20447232 | tf_op jit(solution)/shard_map/wgrad/pallas_call | solution.py:465
  380.0 2.7 constant_dynamic-slice_fusion.2
  384.8 21.8 %attend_back.3 = (bf16[1024,768]{1,0:T(8,128)(2,1)}, bf16[1024,768]{1,0:T(8,128)(2,1)}, bf16[1024,768]{1,0:T(8,128)(2,1)}, f32[2,1,768]{2,1,0:T(1,128)}, f32[2,1,768]{2,1,0:T(1,128)}) custom-call(s32[2]{0:T(128)} %refs_0_.11, bf16[1024,2304]{1,0:T(8,128)(2,1)} %get-tuple-element.62.refs_1_.refs_2_.refs_3_, ...), custom_call_target="tpu_custom_call" | custom-call | flops 16106127360 | bytes 11010048 | tf_op jit(solution)/shard_map/attend_back/pallas_call | solution.py:391
  406.6 6.5 %wgrad.7 = bf16[768,768]{1,0:T(8,128)(2,1)} custom-call(bf16[768,1024]{1,0:T(8,128)(2,1)} %get-tuple-element.87.a_ref, bf16[1024,768]{1,0:T(8,128)(2,1)} %get-tuple-element.77.ev_ref.b_ref, bf16[768,1024]{1,0:T(8,128)(2,1)} %get-tuple-element.88.c_ref, bf16[1024,768]{1,0:T(8,128)(2,1)} %get-tuple-element.86.ev_ref.d_ref), custom_call_target="tpu_custom_call" | custom-call | flops 2415919104 | bytes 7471104 | tf_op jit(solution)/shard_map/wgrad/pallas_call | solution.py:465
  413.0 6.6 %wgrad.8 = bf16[768,768]{1,0:T(8,128)(2,1)} custom-call(bf16[768,1024]{1,0:T(8,128)(2,1)} %get-tuple-element.97.a_ref, bf16[1024,768]{1,0:T(8,128)(2,1)} %get-tuple-element.98.b_ref, bf16[768,1024]{1,0:T(8,128)(2,1)} %get-tuple-element.99.c_ref, bf16[1024,768]{1,0:T(8,128)(2,1)} %get-tuple-element.100.d_ref), custom_call_target="tpu_custom_call" | custom-call | flops 2415919104 | bytes 7471104 | tf_op jit(solution)/shard_map/wgrad/pallas_call | solution.py:465
  419.6 2.5 constant_dynamic-slice_fusion.4
  436.2 6.5 %wgrad.5 = bf16[768,768]{1,0:T(8,128)(2,1)} custom-call(bf16[768,1024]{1,0:T(8,128)(2,1)} %get-tuple-element.87.a_ref, bf16[1024,768]{1,0:T(8,128)(2,1)} %get-tuple-element.75.eq_ref.b_ref, bf16[768,1024]{1,0:T(8,128)(2,1)} %get-tuple-element.88.c_ref, bf16[1024,768]{1,0:T(8,128)(2,1)} %get-tuple-element.84.eq_ref.d_ref), custom_call_target="tpu_custom_call" | custom-call | flops 2415919104 | bytes 7471104 | tf_op jit(solution)/shard_map/wgrad/pallas_call | solution.py:465
  442.7 6.5 %wgrad.6 = bf16[768,768]{1,0:T(8,128)(2,1)} custom-call(bf16[768,1024]{1,0:T(8,128)(2,1)} %get-tuple-element.87.a_ref, bf16[1024,768]{1,0:T(8,128)(2,1)} %get-tuple-element.76.ek_ref.b_ref, bf16[768,1024]{1,0:T(8,128)(2,1)} %get-tuple-element.88.c_ref, bf16[1024,768]{1,0:T(8,128)(2,1)} %get-tuple-element.85.ek_ref.d_ref), custom_call_target="tpu_custom_call" | custom-call | flops 2415919104 | bytes 7471104 | tf_op jit(solution)/shard_map/wgrad/pallas_call | solution.py:465
  450.8 8.6 %dx.3 = bf16[1024,768]{1,0:T(8,128)(2,1)} custom-call(f32[1024,768]{1,0:T(8,128)} %get-tuple-element.81.dz1_ref, bf16[1024,768]{1,0:T(8,128)(2,1)} %get-tuple-element.84.eq_ref.d_ref, bf16[1024,768]{1,0:T(8,128)(2,1)} %get-tuple-element.85.ek_ref.d_ref, bf16[1024,768]{1,0:T(8,128)(2,1)} %get-tuple-element.86.ev_ref.d_ref, bf16[768,2304]{1,0:T(8,128)(2,1)} %bitcast.444), custom_call_target="tpu_custom_call" | custom-call | flops 3623878656 | bytes 14548992 | tf_op jit(solution)/shard_map/dx/pallas_call | solution.py:422
  471.4 3.5 collective-permute-start.98
  474.8 3.1 collective-permute-start.99
  486.1 2.7 collective-permute-done.103
  492.6 2.3 collective-permute-done.69
  511.9 4.1 collective-permute-start.74
  518.3 3.0 collective-permute-start.82
  521.2 2.0 collective-permute-start.83
  524.0 2.4 collective-permute-start.90
  526.4 2.7 collective-permute-start.91
  529.3 2.0 collective-permute-start.106
  531.3 3.7 collective-permute-start.107
  535.7 2.0 fusion.163
  540.9 1.8 fusion.165
  545.8 8.5 %collective-permute-done.119 = bf16[2,4,96,384]{3,2,1,0:T(8,128)(2,1)S(1)} collective-permute-done((bf16[2,4,96,384]{3,2,1,0:T(8,128)(2,1)S(1)}, bf16[2,4,96,384]{3,2,1,0:T(8,128)(2,1)S(1)}, u32[]{:S(2)}, u32[]{:S(2)}) %collective-permute-start.119) | collective-permute-done | bytes 589856 | tf_op jit(solution)/shard_map/ppermute | solution.py:508
  557.1 6.3 %collective-permute-done.111 = bf16[2,4,24,1536]{3,2,1,0:T(8,128)(2,1)S(1)} collective-permute-done((bf16[2,4,24,1536]{3,2,1,0:T(8,128)(2,1)S(1)}, bf16[2,4,24,1536]{3,2,1,0:T(8,128)(2,1)S(1)}, u32[]{:S(2)}, u32[]{:S(2)}) %collective-permute-start.111) | collective-permute-done | bytes 589856 | tf_op jit(solution)/shard_map/ppermute | solution.py:508
  565.7 2.1 collective-permute-done.120
  569.0 3.0 collective-permute-start.123
  575.3 2.0 collective-permute-start.115
  578.2 1.9 collective-permute-done.113
  580.1 3.7 collective-permute-done.114
  (501 shorter events, 153.4 us)
Async XLA Ops:
  7.6 10.0 %collective-permute-start.17 = (bf16[32,768]{1,0:T(8,128)(2,1)S(1)}, bf16[32,768]{1,0:T(8,128)(2,1)S(1)}, u32[]{:S(2)}, u32[]{:S(2)}) collective-permute-start(bf16[32,768]{1,0:T(8,128)(2,1)S(1)} %fusion.103), channel_id=1, source_target_pairs={{0,6},{1,7},{2,0},{3,1},{4,2},{5,3},{6,4},{7,5},{8,14},{9,15},{10,... | collective-permute-start | bytes 147464 | tf_op jit(solution)/shard_map/ppermute | solution.py:508
  12.6 36.1 %collective-permute-start.51 = (bf16[96,768]{1,0:T(8,128)(2,1)}, bf16[96,768]{1,0:T(8,128)(2,1)S(1)}, u32[]{:S(2)}, u32[]{:S(2)}) collective-permute-start(bf16[96,768]{1,0:T(8,128)(2,1)} %param.27), channel_id=1, source_target_pairs={{0,6},{1,7},{2,0},{3,1},{4,2},{5,3},{6,4},{7,5},{8,14},{9,15},{10,... | collective-permute-start | bytes 442376 | tf_op jit(solution)/shard_map/ppermute | solution.py:508
  13.1 37.3 %collective-permute-start.52 = (bf16[96,768]{1,0:T(8,128)(2,1)}, bf16[96,768]{1,0:T(8,128)(2,1)S(1)}, u32[]{:S(2)}, u32[]{:S(2)}) collective-permute-start(bf16[96,768]{1,0:T(8,128)(2,1)} %param.27), channel_id=1, source_target_pairs={{0,4},{1,5},{2,6},{3,7},{4,0},{5,1},{6,2},{7,3},{8,12},{9,13},{10,... | collective-permute-start | bytes 442376 | tf_op jit(solution)/shard_map/ppermute | solution.py:508
  13.1 38.9 %collective-permute-start.53 = (bf16[96,768]{1,0:T(8,128)(2,1)}, bf16[96,768]{1,0:T(8,128)(2,1)S(1)}, u32[]{:S(2)}, u32[]{:S(2)}) collective-permute-start(bf16[96,768]{1,0:T(8,128)(2,1)} %param.27), channel_id=1, source_target_pairs={{0,2},{1,3},{2,4},{3,5},{4,6},{5,7},{6,0},{7,1},{8,10},{9,11},{10,... | collective-permute-start | bytes 442376 | tf_op jit(solution)/shard_map/ppermute | solution.py:508
  14.7 14.7 %collective-permute-start.18 = (bf16[32,768]{1,0:T(8,128)(2,1)S(1)}, bf16[32,768]{1,0:T(8,128)(2,1)S(1)}, u32[]{:S(2)}, u32[]{:S(2)}) collective-permute-start(bf16[32,768]{1,0:T(8,128)(2,1)S(1)} %fusion.103), channel_id=1, source_target_pairs={{0,4},{1,5},{2,6},{3,7},{4,0},{5,1},{6,2},{7,3},{8,12},{9,13},{10,... | collective-permute-start | bytes 147464 | tf_op jit(solution)/shard_map/ppermute | solution.py:508
  17.6 15.2 %collective-permute-start.19 = (bf16[32,768]{1,0:T(8,128)(2,1)S(1)}, bf16[32,768]{1,0:T(8,128)(2,1)S(1)}, u32[]{:S(2)}, u32[]{:S(2)}) collective-permute-start(bf16[32,768]{1,0:T(8,128)(2,1)S(1)} %fusion.103), channel_id=1, source_target_pairs={{0,2},{1,3},{2,4},{3,5},{4,6},{5,7},{6,0},{7,1},{8,10},{9,11},{10,... | collective-permute-start | bytes 147464 | tf_op jit(solution)/shard_map/ppermute | solution.py:508
  32.8 9.4 %collective-permute-start.1 = (bf16[24,2304]{1,0:T(8,128)(2,1)}, bf16[24,2304]{1,0:T(8,128)(2,1)S(1)}, u32[]{:S(2)}, u32[]{:S(2)}) collective-permute-start(bf16[24,2304]{1,0:T(8,128)(2,1)} %param.18), channel_id=1, source_target_pairs={{0,4},{1,5},{2,6},{3,7},{4,0},{5,1},{6,2},{7,3},{8,12},{9,13},{10,... | collective-permute-start | bytes 331784 | tf_op jit(solution)/shard_map/ppermute | solution.py:508
  36.5 8.0 %collective-permute-start.2 = (bf16[24,2304]{1,0:T(8,128)(2,1)S(1)}, bf16[24,2304]{1,0:T(8,128)(2,1)S(1)}, u32[]{:S(2)}, u32[]{:S(2)}) collective-permute-start(bf16[24,2304]{1,0:T(8,128)(2,1)S(1)} %copy-done.65), channel_id=1, source_target_pairs={{0,2},{1,3},{2,4},{3,5},{4,6},{5,7},{6,0},{7,1},{8,10},{9,11},{10,... | collective-permute-start | bytes 331784 | tf_op jit(solution)/shard_map/ppermute | solution.py:508
  44.5 9.7 %collective-permute-start.35 = (bf16[24,3072]{1,0:T(8,128)(2,1)S(1)}, bf16[24,3072]{1,0:T(8,128)(2,1)S(1)}, u32[]{:S(2)}, u32[]{:S(2)}) collective-permute-start(bf16[24,3072]{1,0:T(8,128)(2,1)S(1)} %copy-done.64), channel_id=1, source_target_pairs={{0,4},{1,5},{2,6},{3,7},{4,0},{5,1},{6,2},{7,3},{8,12},{9,13},{10,... | collective-permute-start | bytes 442376 | tf_op jit(solution)/shard_map/ppermute | solution.py:508
  50.4 8.0 %collective-permute-start.23 = (bf16[4,32,384]{2,1,0:T(8,128)(2,1)S(1)}, bf16[4,32,384]{2,1,0:T(8,128)(2,1)S(1)}, u32[]{:S(2)}, u32[]{:S(2)}) collective-permute-start(bf16[4,32,384]{2,1,0:T(8,128)(2,1)S(1)} %get-tuple-element.184.refs_1_), channel_id=1, source_target_pairs={{0,16},{1,17},{2,18},{3,19},{4,20},{5,21},{6,22},{7,23},{8,24},{9,... | collective-permute-start | bytes 294920 | tf_op jit(solution)/shard_map/ppermute | solution.py:508
  63.8 8.4 %collective-permute-start.13 = (bf16[4,24,1152]{2,1,0:T(8,128)(2,1)S(1)}, bf16[4,24,1152]{2,1,0:T(8,128)(2,1)S(1)}, u32[]{:S(2)}, u32[]{:S(2)}) collective-permute-start(bf16[4,24,1152]{2,1,0:T(8,128)(2,1)S(1)} %get-tuple-element.141.refs_9_), channel_id=1, source_target_pairs={{0,16},{1,17},{2,18},{3,19},{4,20},{5,21},{6,22},{7,23},{8,24},{9,... | collective-permute-start | bytes 663560 | tf_op jit(solution)/shard_map/ppermute | solution.py:508
  65.0 12.2 %collective-permute-start.10 = (bf16[4,24,1152]{2,1,0:T(8,128)(2,1)S(1)}, bf16[4,24,1152]{2,1,0:T(8,128)(2,1)}, u32[]{:S(2)}, u32[]{:S(2)}) collective-permute-start(bf16[4,24,1152]{2,1,0:T(8,128)(2,1)S(1)} %get-tuple-element.141.refs_9_), channel_id=1, source_target_pairs={{0,1},{1,0},{2,3},{3,2},{4,5},{5,4},{6,7},{7,6},{8,9},{9,8},{10,11... | collective-permute-start | bytes 663560 | tf_op jit(solution)/shard_map/ppermute | solution.py:508
  66.5 9.1 %collective-permute-start.3 = (bf16[4,24,1152]{2,1,0:T(8,128)(2,1)S(1)}, bf16[4,24,1152]{2,1,0:T(8,128)(2,1)S(1)}, u32[]{:S(2)}, u32[]{:S(2)}) collective-permute-start(bf16[4,24,1152]{2,1,0:T(8,128)(2,1)S(1)} %get-tuple-element.142.refs_1_), channel_id=1, source_target_pairs={{0,1},{1,0},{2,3},{3,2},{4,5},{5,4},{6,7},{7,6},{8,9},{9,8},{10,11... | collective-permute-start | bytes 663560 | tf_op jit(solution)/shard_map/ppermute | solution.py:508
  67.0 11.6 %collective-permute-start.6 = (bf16[4,24,1152]{2,1,0:T(8,128)(2,1)S(1)}, bf16[4,24,1152]{2,1,0:T(8,128)(2,1)}, u32[]{:S(2)}, u32[]{:S(2)}) collective-permute-start(bf16[4,24,1152]{2,1,0:T(8,128)(2,1)S(1)} %get-tuple-element.142.refs_1_), channel_id=1, source_target_pairs={{0,16},{1,17},{2,18},{3,19},{4,20},{5,21},{6,22},{7,23},{8,24},{9,... | collective-permute-start | bytes 663560 | tf_op jit(solution)/shard_map/ppermute | solution.py:508
  67.8 10.8 %collective-permute-start.11 = (bf16[4,24,1152]{2,1,0:T(8,128)(2,1)S(1)}, bf16[4,24,1152]{2,1,0:T(8,128)(2,1)S(1)}, u32[]{:S(2)}, u32[]{:S(2)}) collective-permute-start(bf16[4,24,1152]{2,1,0:T(8,128)(2,1)S(1)} %get-tuple-element.141.refs_9_), channel_id=1, source_target_pairs={{0,8},{1,9},{2,10},{3,11},{4,12},{5,13},{6,14},{7,15},{8,0},{9,1},... | collective-permute-start | bytes 663560 | tf_op jit(solution)/shard_map/ppermute | solution.py:508
  72.1 7.7 %collective-permute-start.4 = (bf16[4,24,1152]{2,1,0:T(8,128)(2,1)S(1)}, bf16[4,24,1152]{2,1,0:T(8,128)(2,1)S(1)}, u32[]{:S(2)}, u32[]{:S(2)}) collective-permute-start(bf16[4,24,1152]{2,1,0:T(8,128)(2,1)S(1)} %get-tuple-element.142.refs_1_), channel_id=1, source_target_pairs={{0,8},{1,9},{2,10},{3,11},{4,12},{5,13},{6,14},{7,15},{8,0},{9,1},... | collective-permute-start | bytes 663560 | tf_op jit(solution)/shard_map/ppermute | solution.py:508
  77.3 7.6 %collective-permute-start.64 = (bf16[4,96,384]{2,1,0:T(8,128)(2,1)S(1)}, bf16[4,96,384]{2,1,0:T(8,128)(2,1)S(1)}, u32[]{:S(2)}, u32[]{:S(2)}) collective-permute-start(bf16[4,96,384]{2,1,0:T(8,128)(2,1)S(1)} %get-tuple-element.137.refs_9_), channel_id=1, source_target_pairs={{0,16},{1,17},{2,18},{3,19},{4,20},{5,21},{6,22},{7,23},{8,24},{9,... | collective-permute-start | bytes 884744 | tf_op jit(solution)/shard_map/ppermute | solution.py:508
  80.6 9.8 %collective-permute-start.57 = (bf16[4,96,384]{2,1,0:T(8,128)(2,1)S(1)}, bf16[4,96,384]{2,1,0:T(8,128)(2,1)S(1)}, u32[]{:S(2)}, u32[]{:S(2)}) collective-permute-start(bf16[4,96,384]{2,1,0:T(8,128)(2,1)S(1)} %get-tuple-element.138.refs_1_), channel_id=1, source_target_pairs={{0,16},{1,17},{2,18},{3,19},{4,20},{5,21},{6,22},{7,23},{8,24},{9,... | collective-permute-start | bytes 884744 | tf_op jit(solution)/shard_map/ppermute | solution.py:508
  81.3 10.5 %collective-permute-start.61 = (bf16[4,96,384]{2,1,0:T(8,128)(2,1)S(1)}, bf16[4,96,384]{2,1,0:T(8,128)(2,1)S(1)}, u32[]{:S(2)}, u32[]{:S(2)}) collective-permute-start(bf16[4,96,384]{2,1,0:T(8,128)(2,1)S(1)} %get-tuple-element.137.refs_9_), channel_id=1, source_target_pairs={{0,1},{1,0},{2,3},{3,2},{4,5},{5,4},{6,7},{7,6},{8,9},{9,8},{10,11... | collective-permute-start | bytes 884744 | tf_op jit(solution)/shard_map/ppermute | solution.py:508
  81.8 10.7 %collective-permute-start.55 = (bf16[4,96,384]{2,1,0:T(8,128)(2,1)S(1)}, bf16[4,96,384]{2,1,0:T(8,128)(2,1)S(1)}, u32[]{:S(2)}, u32[]{:S(2)}) collective-permute-start(bf16[4,96,384]{2,1,0:T(8,128)(2,1)S(1)} %get-tuple-element.138.refs_1_), channel_id=1, source_target_pairs={{0,8},{1,9},{2,10},{3,11},{4,12},{5,13},{6,14},{7,15},{8,0},{9,1},... | collective-permute-start | bytes 884744 | tf_op jit(solution)/shard_map/ppermute | solution.py:508
  82.5 11.3 %collective-permute-start.62 = (bf16[4,96,384]{2,1,0:T(8,128)(2,1)S(1)}, bf16[4,96,384]{2,1,0:T(8,128)(2,1)S(1)}, u32[]{:S(2)}, u32[]{:S(2)}) collective-permute-start(bf16[4,96,384]{2,1,0:T(8,128)(2,1)S(1)} %get-tuple-element.137.refs_9_), channel_id=1, source_target_pairs={{0,8},{1,9},{2,10},{3,11},{4,12},{5,13},{6,14},{7,15},{8,0},{9,1},... | collective-permute-start | bytes 884744 | tf_op jit(solution)/shard_map/ppermute | solution.py:508
  84.9 12.7 %collective-permute-start.37 = (bf16[4,24,1536]{2,1,0:T(8,128)(2,1)S(1)}, bf16[4,24,1536]{2,1,0:T(8,128)(2,1)S(1)}, u32[]{:S(2)}, u32[]{:S(2)}) collective-permute-start(bf16[4,24,1536]{2,1,0:T(8,128)(2,1)S(1)} %get-tuple-element.140.refs_1_), channel_id=1, source_target_pairs={{0,1},{1,0},{2,3},{3,2},{4,5},{5,4},{6,7},{7,6},{8,9},{9,8},{10,11... | collective-permute-start | bytes 884744 | tf_op jit(solution)/shard_map/ppermute | solution.py:508
  90.4 9.9 %collective-permute-start.47 = (bf16[4,24,1536]{2,1,0:T(8,128)(2,1)S(1)}, bf16[4,24,1536]{2,1,0:T(8,128)(2,1)S(1)}, u32[]{:S(2)}, u32[]{:S(2)}) collective-permute-start(bf16[4,24,1536]{2,1,0:T(8,128)(2,1)S(1)} %get-tuple-element.139.refs_9_), channel_id=1, source_target_pairs={{0,16},{1,17},{2,18},{3,19},{4,20},{5,21},{6,22},{7,23},{8,24},{9,... | collective-permute-start | bytes 884744 | tf_op jit(solution)/shard_map/ppermute | solution.py:508
  91.8 13.1 %collective-permute-start.40 = (bf16[4,24,1536]{2,1,0:T(8,128)(2,1)S(1)}, bf16[4,24,1536]{2,1,0:T(8,128)(2,1)S(1)}, u32[]{:S(2)}, u32[]{:S(2)}) collective-permute-start(bf16[4,24,1536]{2,1,0:T(8,128)(2,1)S(1)} %get-tuple-element.140.refs_1_), channel_id=1, source_target_pairs={{0,16},{1,17},{2,18},{3,19},{4,20},{5,21},{6,22},{7,23},{8,24},{9,... | collective-permute-start | bytes 884744 | tf_op jit(solution)/shard_map/ppermute | solution.py:508
  93.3 12.4 %collective-permute-start.44 = (bf16[4,24,1536]{2,1,0:T(8,128)(2,1)S(1)}, bf16[4,24,1536]{2,1,0:T(8,128)(2,1)S(1)}, u32[]{:S(2)}, u32[]{:S(2)}) collective-permute-start(bf16[4,24,1536]{2,1,0:T(8,128)(2,1)S(1)} %get-tuple-element.139.refs_9_), channel_id=1, source_target_pairs={{0,1},{1,0},{2,3},{3,2},{4,5},{5,4},{6,7},{7,6},{8,9},{9,8},{10,11... | collective-permute-start | bytes 884744 | tf_op jit(solution)/shard_map/ppermute | solution.py:508
  94.5 11.2 %collective-permute-start.38 = (bf16[4,24,1536]{2,1,0:T(8,128)(2,1)S(1)}, bf16[4,24,1536]{2,1,0:T(8,128)(2,1)S(1)}, u32[]{:S(2)}, u32[]{:S(2)}) collective-permute-start(bf16[4,24,1536]{2,1,0:T(8,128)(2,1)S(1)} %get-tuple-element.140.refs_1_), channel_id=1, source_target_pairs={{0,8},{1,9},{2,10},{3,11},{4,12},{5,13},{6,14},{7,15},{8,0},{9,1},... | collective-permute-start | bytes 884744 | tf_op jit(solution)/shard_map/ppermute | solution.py:508
  97.6 9.3 %collective-permute-start.45 = (bf16[4,24,1536]{2,1,0:T(8,128)(2,1)S(1)}, bf16[4,24,1536]{2,1,0:T(8,128)(2,1)S(1)}, u32[]{:S(2)}, u32[]{:S(2)}) collective-permute-start(bf16[4,24,1536]{2,1,0:T(8,128)(2,1)S(1)} %get-tuple-element.139.refs_9_), channel_id=1, source_target_pairs={{0,8},{1,9},{2,10},{3,11},{4,12},{5,13},{6,14},{7,15},{8,0},{9,1},... | collective-permute-start | bytes 884744 | tf_op jit(solution)/shard_map/ppermute | solution.py:508
  100.3 8.6 %collective-permute-start.14 = (bf16[4,24,1152]{2,1,0:T(8,128)(2,1)S(1)}, bf16[4,24,1152]{2,1,0:T(8,128)(2,1)}, u32[]{:S(2)}, u32[]{:S(2)}) collective-permute-start(bf16[4,24,1152]{2,1,0:T(8,128)(2,1)S(1)} %collective-permute-done.13.refs_13_), channel_id=1, source_target_pairs={{0,1},{1,0},{2,3},{3,2},{4,5},{5,4},{6,7},{7,6},{8,9},{9,8},{10,11... | collective-permute-start | bytes 663560 | tf_op jit(solution)/shard_map/ppermute | solution.py:508
  107.6 9.6 %collective-permute-start.58 = (bf16[4,96,384]{2,1,0:T(8,128)(2,1)S(1)}, bf16[4,96,384]{2,1,0:T(8,128)(2,1)}, u32[]{:S(2)}, u32[]{:S(2)}) collective-permute-start(bf16[4,96,384]{2,1,0:T(8,128)(2,1)S(1)} %collective-permute-done.54.refs_2_), channel_id=1, source_target_pairs={{0,16},{1,17},{2,18},{3,19},{4,20},{5,21},{6,22},{7,23},{8,24},{9,... | collective-permute-start | bytes 884744 | tf_op jit(solution)/shard_map/ppermute | solution.py:508
  113.3 31.9 %collective-permute-start.56 = (bf16[4,96,384]{2,1,0:T(8,128)(2,1)S(1)}, bf16[4,96,384]{2,1,0:T(8,128)(2,1)}, u32[]{:S(2)}, u32[]{:S(2)}) collective-permute-start(bf16[4,96,384]{2,1,0:T(8,128)(2,1)S(1)} %collective-permute-done.54.refs_2_), channel_id=1, source_target_pairs={{0,8},{1,9},{2,10},{3,11},{4,12},{5,13},{6,14},{7,15},{8,0},{9,1},... | collective-permute-start | bytes 884744 | tf_op jit(solution)/shard_map/ppermute | solution.py:508
  113.8 30.6 %collective-permute-start.65 = (bf16[4,96,384]{2,1,0:T(8,128)(2,1)S(1)}, bf16[4,96,384]{2,1,0:T(8,128)(2,1)}, u32[]{:S(2)}, u32[]{:S(2)}) collective-permute-start(bf16[4,96,384]{2,1,0:T(8,128)(2,1)S(1)} %collective-permute-done.64.refs_13_), channel_id=1, source_target_pairs={{0,1},{1,0},{2,3},{3,2},{4,5},{5,4},{6,7},{7,6},{8,9},{9,8},{10,11... | collective-permute-start | bytes 884744 | tf_op jit(solution)/shard_map/ppermute | solution.py:508
  117.3 28.2 %collective-permute-start.66 = (bf16[4,96,384]{2,1,0:T(8,128)(2,1)S(1)}, bf16[4,96,384]{2,1,0:T(8,128)(2,1)}, u32[]{:S(2)}, u32[]{:S(2)}) collective-permute-start(bf16[4,96,384]{2,1,0:T(8,128)(2,1)S(1)} %collective-permute-done.64.refs_13_), channel_id=1, source_target_pairs={{0,8},{1,9},{2,10},{3,11},{4,12},{5,13},{6,14},{7,15},{8,0},{9,1},... | collective-permute-start | bytes 884744 | tf_op jit(solution)/shard_map/ppermute | solution.py:508
  117.3 28.7 %collective-permute-start.59 = (bf16[4,96,384]{2,1,0:T(8,128)(2,1)S(1)}, bf16[4,96,384]{2,1,0:T(8,128)(2,1)}, u32[]{:S(2)}, u32[]{:S(2)}) collective-permute-start(bf16[4,96,384]{2,1,0:T(8,128)(2,1)S(1)} %collective-permute-done.57.refs_5_), channel_id=1, source_target_pairs={{0,8},{1,9},{2,10},{3,11},{4,12},{5,13},{6,14},{7,15},{8,0},{9,1},... | collective-permute-start | bytes 884744 | tf_op jit(solution)/shard_map/ppermute | solution.py:508
  117.8 28.2 %collective-permute-start.63 = (bf16[4,96,384]{2,1,0:T(8,128)(2,1)S(1)}, bf16[4,96,384]{2,1,0:T(8,128)(2,1)}, u32[]{:S(2)}, u32[]{:S(2)}) collective-permute-start(bf16[4,96,384]{2,1,0:T(8,128)(2,1)S(1)} %collective-permute-done.61.refs_10_), channel_id=1, source_target_pairs={{0,8},{1,9},{2,10},{3,11},{4,12},{5,13},{6,14},{7,15},{8,0},{9,1},... | collective-permute-start | bytes 884744 | tf_op jit(solution)/shard_map/ppermute | solution.py:508
  144.5 10.2 %collective-permute-start.41 = (bf16[4,24,1536]{2,1,0:T(8,128)(2,1)S(1)}, bf16[4,24,1536]{2,1,0:T(8,128)(2,1)S(1)}, u32[]{:S(2)}, u32[]{:S(2)}) collective-permute-start(bf16[4,24,1536]{2,1,0:T(8,128)(2,1)S(1)} %collective-permute-done.37.refs_2_), channel_id=1, source_target_pairs={{0,16},{1,17},{2,18},{3,19},{4,20},{5,21},{6,22},{7,23},{8,24},{9,... | collective-permute-start | bytes 884744 | tf_op jit(solution)/shard_map/ppermute | solution.py:508
  145.3 9.9 %collective-permute-start.39 = (bf16[4,24,1536]{2,1,0:T(8,128)(2,1)S(1)}, bf16[4,24,1536]{2,1,0:T(8,128)(2,1)S(1)}, u32[]{:S(2)}, u32[]{:S(2)}) collective-permute-start(bf16[4,24,1536]{2,1,0:T(8,128)(2,1)S(1)} %collective-permute-done.37.refs_2_), channel_id=1, source_target_pairs={{0,8},{1,9},{2,10},{3,11},{4,12},{5,13},{6,14},{7,15},{8,0},{9,1},... | collective-permute-start | bytes 884744 | tf_op jit(solution)/shard_map/ppermute | solution.py:508
  145.4 9.3 %collective-permute-start.48 = (bf16[4,24,1536]{2,1,0:T(8,128)(2,1)S(1)}, bf16[4,24,1536]{2,1,0:T(8,128)(2,1)S(1)}, u32[]{:S(2)}, u32[]{:S(2)}) collective-permute-start(bf16[4,24,1536]{2,1,0:T(8,128)(2,1)S(1)} %copy-done.4), channel_id=1, source_target_pairs={{0,1},{1,0},{2,3},{3,2},{4,5},{5,4},{6,7},{7,6},{8,9},{9,8},{10,11... | collective-permute-start | bytes 884744 | tf_op jit(solution)/shard_map/ppermute | solution.py:508
  145.9 9.4 %collective-permute-start.60 = (bf16[4,96,384]{2,1,0:T(8,128)(2,1)}, bf16[4,96,384]{2,1,0:T(8,128)(2,1)S(1)}, u32[]{:S(2)}, u32[]{:S(2)}) collective-permute-start(bf16[4,96,384]{2,1,0:T(8,128)(2,1)} %collective-permute-done.58.refs_6_), channel_id=1, source_target_pairs={{0,8},{1,9},{2,10},{3,11},{4,12},{5,13},{6,14},{7,15},{8,0},{9,1},... | collective-permute-start | bytes 884744 | tf_op jit(solution)/shard_map/ppermute | solution.py:508
  146.0 9.7 %collective-permute-start.67 = (bf16[4,96,384]{2,1,0:T(8,128)(2,1)}, bf16[4,96,384]{2,1,0:T(8,128)(2,1)S(1)}, u32[]{:S(2)}, u32[]{:S(2)}) collective-permute-start(bf16[4,96,384]{2,1,0:T(8,128)(2,1)} %collective-permute-done.65.refs_14_), channel_id=1, source_target_pairs={{0,8},{1,9},{2,10},{3,11},{4,12},{5,13},{6,14},{7,15},{8,0},{9,1},... | collective-permute-start | bytes 884744 | tf_op jit(solution)/shard_map/ppermute | solution.py:508
  154.7 18.7 %collective-permute-start.49 = (bf16[4,24,1536]{2,1,0:T(8,128)(2,1)S(1)}, bf16[4,24,1536]{2,1,0:T(8,128)(2,1)S(1)}, u32[]{:S(2)}, u32[]{:S(2)}) collective-permute-start(bf16[4,24,1536]{2,1,0:T(8,128)(2,1)S(1)} %copy-done.4), channel_id=1, source_target_pairs={{0,8},{1,9},{2,10},{3,11},{4,12},{5,13},{6,14},{7,15},{8,0},{9,1},... | collective-permute-start | bytes 884744 | tf_op jit(solution)/shard_map/ppermute | solution.py:508
  154.7 18.6 %collective-permute-start.42 = (bf16[4,24,1536]{2,1,0:T(8,128)(2,1)S(1)}, bf16[4,24,1536]{2,1,0:T(8,128)(2,1)S(1)}, u32[]{:S(2)}, u32[]{:S(2)}) collective-permute-start(bf16[4,24,1536]{2,1,0:T(8,128)(2,1)S(1)} %copy-done.8), channel_id=1, source_target_pairs={{0,8},{1,9},{2,10},{3,11},{4,12},{5,13},{6,14},{7,15},{8,0},{9,1},... | collective-permute-start | bytes 884744 | tf_op jit(solution)/shard_map/ppermute | solution.py:508
  155.2 18.2 %collective-permute-start.46 = (bf16[4,24,1536]{2,1,0:T(8,128)(2,1)S(1)}, bf16[4,24,1536]{2,1,0:T(8,128)(2,1)S(1)}, u32[]{:S(2)}, u32[]{:S(2)}) collective-permute-start(bf16[4,24,1536]{2,1,0:T(8,128)(2,1)S(1)} %copy-done.12), channel_id=1, source_target_pairs={{0,8},{1,9},{2,10},{3,11},{4,12},{5,13},{6,14},{7,15},{8,0},{9,1},... | collective-permute-start | bytes 884744 | tf_op jit(solution)/shard_map/ppermute | solution.py:508
  155.3 18.1 %collective-permute-start.43 = (bf16[4,24,1536]{2,1,0:T(8,128)(2,1)S(1)}, bf16[4,24,1536]{2,1,0:T(8,128)(2,1)S(1)}, u32[]{:S(2)}, u32[]{:S(2)}) collective-permute-start(bf16[4,24,1536]{2,1,0:T(8,128)(2,1)S(1)} %collective-permute-done.41.refs_6_), channel_id=1, source_target_pairs={{0,8},{1,9},{2,10},{3,11},{4,12},{5,13},{6,14},{7,15},{8,0},{9,1},... | collective-permute-start | bytes 884744 | tf_op jit(solution)/shard_map/ppermute | solution.py:508
  155.7 17.7 %collective-permute-start.50 = (bf16[4,24,1536]{2,1,0:T(8,128)(2,1)S(1)}, bf16[4,24,1536]{2,1,0:T(8,128)(2,1)S(1)}, u32[]{:S(2)}, u32[]{:S(2)}) collective-permute-start(bf16[4,24,1536]{2,1,0:T(8,128)(2,1)S(1)} %collective-permute-done.48.refs_14_), channel_id=1, source_target_pairs={{0,8},{1,9},{2,10},{3,11},{4,12},{5,13},{6,14},{7,15},{8,0},{9,1},... | collective-permute-start | bytes 884744 | tf_op jit(solution)/shard_map/ppermute | solution.py:508
  363.2 172.4 %collective-permute-start.116 = (bf16[2,4,2,96,768]{4,3,1,2,0:T(8,128)(2,1)}, bf16[2,4,2,96,768]{4,3,1,2,0:T(8,128)(2,1)}, u32[]{:S(2)}, u32[]{:S(2)}) collective-permute-start(bf16[2,4,2,96,768]{4,3,1,2,0:T(8,128)(2,1)} %bitcast.429), channel_id=1, source_target_pairs={{0,8},{1,9},{2,10},{3,11},{4,12},{5,13},{6,14},{7,15},{8,0},{9,1},... | collective-permute-start | bytes 7077896 | tf_op jit(solution)/shard_map/ppermute | solution.py:508
  384.3 155.8 %collective-permute-start.108 = (bf16[2,4,2,24,3072]{4,3,1,2,0:T(8,128)(2,1)}, bf16[2,4,2,24,3072]{4,3,1,2,0:T(8,128)(2,1)}, u32[]{:S(2)}, u32[]{:S(2)}) collective-permute-start(bf16[2,4,2,24,3072]{4,3,1,2,0:T(8,128)(2,1)} %bitcast.431), channel_id=1, source_target_pairs={{0,8},{1,9},{2,10},{3,11},{4,12},{5,13},{6,14},{7,15},{8,0},{9,1},... | collective-permute-start | bytes 7077896 | tf_op jit(solution)/shard_map/ppermute | solution.py:508
  435.8 24.8 %collective-permute-start.92 = (f32[2,4,2,8,512]{4,3,1,2,0:T(8,128)}, f32[2,4,2,8,512]{4,3,1,2,0:T(8,128)S(1)}, u32[]{:S(2)}, u32[]{:S(2)}) collective-permute-start(f32[2,4,2,8,512]{4,3,1,2,0:T(8,128)} %copy.72), channel_id=1, source_target_pairs={{0,8},{1,9},{2,10},{3,11},{4,12},{5,13},{6,14},{7,15},{8,0},{9,1},... | collective-permute-start | bytes 786440 | tf_op jit(solution)/shard_map/ppermute | solution.py:508
  470.7 8.5 %collective-permute-start.97 = (f32[8,512]{1,0:T(8,128)S(1)}, f32[8,512]{1,0:T(8,128)S(1)}, u32[]{:S(2)}, u32[]{:S(2)}) collective-permute-start(f32[8,512]{1,0:T(8,128)S(1)} %get-tuple-element.205), channel_id=1, source_target_pairs={{0,2},{1,3},{2,4},{3,5},{4,6},{5,7},{6,0},{7,1},{8,10},{9,11},{10,... | collective-permute-start | bytes 49160 | tf_op jit(solution)/shard_map/ppermute | solution.py:508
  471.4 7.9 %collective-permute-start.98 = (f32[8,512]{1,0:T(8,128)S(1)}, f32[8,512]{1,0:T(8,128)S(1)}, u32[]{:S(2)}, u32[]{:S(2)}) collective-permute-start(f32[8,512]{1,0:T(8,128)S(1)} %get-tuple-element.206), channel_id=1, source_target_pairs={{0,4},{1,5},{2,6},{3,7},{4,0},{5,1},{6,2},{7,3},{8,12},{9,13},{10,... | collective-permute-start | bytes 49160 | tf_op jit(solution)/shard_map/ppermute | solution.py:508
  529.3 13.8 %collective-permute-start.105 = (bf16[24,768]{1,0:T(8,128)(2,1)S(1)}, bf16[24,768]{1,0:T(8,128)(2,1)S(1)}, u32[]{:S(2)}, u32[]{:S(2)}) collective-permute-start(bf16[24,768]{1,0:T(8,128)(2,1)S(1)} %get-tuple-element.189), channel_id=1, source_target_pairs={{0,2},{1,3},{2,4},{3,5},{4,6},{5,7},{6,0},{7,1},{8,10},{9,11},{10,... | collective-permute-start | bytes 110600 | tf_op jit(solution)/shard_map/ppermute | solution.py:508
  529.3 14.8 %collective-permute-start.106 = (bf16[24,768]{1,0:T(8,128)(2,1)S(1)}, bf16[24,768]{1,0:T(8,128)(2,1)S(1)}, u32[]{:S(2)}, u32[]{:S(2)}) collective-permute-start(bf16[24,768]{1,0:T(8,128)(2,1)S(1)} %get-tuple-element.190), channel_id=1, source_target_pairs={{0,4},{1,5},{2,6},{3,7},{4,0},{5,1},{6,2},{7,3},{8,12},{9,13},{10,... | collective-permute-start | bytes 110600 | tf_op jit(solution)/shard_map/ppermute | solution.py:508
  531.3 13.9 %collective-permute-start.107 = (bf16[24,768]{1,0:T(8,128)(2,1)S(1)}, bf16[24,768]{1,0:T(8,128)(2,1)S(1)}, u32[]{:S(2)}, u32[]{:S(2)}) collective-permute-start(bf16[24,768]{1,0:T(8,128)(2,1)S(1)} %get-tuple-element.191), channel_id=1, source_target_pairs={{0,6},{1,7},{2,0},{3,1},{4,2},{5,3},{6,4},{7,5},{8,14},{9,15},{10,... | collective-permute-start | bytes 110600 | tf_op jit(solution)/shard_map/ppermute | solution.py:508
  538.0 16.3 %collective-permute-start.119 = (bf16[2,4,96,384]{3,2,1,0:T(8,128)(2,1)S(1)}, bf16[2,4,96,384]{3,2,1,0:T(8,128)(2,1)S(1)}, u32[]{:S(2)}, u32[]{:S(2)}) collective-permute-start(bf16[2,4,96,384]{3,2,1,0:T(8,128)(2,1)S(1)} %get-tuple-element.114), channel_id=1, source_target_pairs={{0,1},{1,0},{2,3},{3,2},{4,5},{5,4},{6,7},{7,6},{8,9},{9,8},{10,11... | collective-permute-start | bytes 1769480 | tf_op jit(solution)/shard_map/ppermute | solution.py:508
  540.2 16.3 %collective-permute-start.117 = (bf16[4,2,96,384]{3,2,0,1:T(8,128)(2,1)S(1)}, bf16[4,2,96,384]{3,2,0,1:T(8,128)(2,1)S(1)}, u32[]{:S(2)}, u32[]{:S(2)}) collective-permute-start(bf16[4,2,96,384]{3,2,0,1:T(8,128)(2,1)S(1)} %get-tuple-element.120), channel_id=1, source_target_pairs={{0,16},{1,17},{2,18},{3,19},{4,20},{5,21},{6,22},{7,23},{8,24},{9,... | collective-permute-start | bytes 1769480 | tf_op jit(solution)/shard_map/ppermute | solution.py:508
  543.1 20.3 %collective-permute-start.111 = (bf16[2,4,24,1536]{3,2,1,0:T(8,128)(2,1)S(1)}, bf16[2,4,24,1536]{3,2,1,0:T(8,128)(2,1)S(1)}, u32[]{:S(2)}, u32[]{:S(2)}) collective-permute-start(bf16[2,4,24,1536]{3,2,1,0:T(8,128)(2,1)S(1)} %get-tuple-element.122), channel_id=1, source_target_pairs={{0,1},{1,0},{2,3},{3,2},{4,5},{5,4},{6,7},{7,6},{8,9},{9,8},{10,11... | collective-permute-start | bytes 1769480 | tf_op jit(solution)/shard_map/ppermute | solution.py:508
  544.1 20.6 %collective-permute-start.109 = (bf16[4,2,24,1536]{3,2,0,1:T(8,128)(2,1)S(1)}, bf16[4,2,24,1536]{3,2,0,1:T(8,128)(2,1)S(1)}, u32[]{:S(2)}, u32[]{:S(2)}) collective-permute-start(bf16[4,2,24,1536]{3,2,0,1:T(8,128)(2,1)S(1)} %get-tuple-element.128), channel_id=1, source_target_pairs={{0,16},{1,17},{2,18},{3,19},{4,20},{5,21},{6,22},{7,23},{8,24},{9,... | collective-permute-start | bytes 1769480 | tf_op jit(solution)/shard_map/ppermute | solution.py:508
  554.4 13.3 %collective-permute-start.120 = (bf16[4,96,384]{2,1,0:T(8,128)(2,1)S(1)}, bf16[4,96,384]{2,1,0:T(8,128)(2,1)S(1)}, u32[]{:S(2)}, u32[]{:S(2)}) collective-permute-start(bf16[4,96,384]{2,1,0:T(8,128)(2,1)S(1)} %fusion.23), channel_id=1, source_target_pairs={{0,16},{1,17},{2,18},{3,19},{4,20},{5,21},{6,22},{7,23},{8,24},{9,... | collective-permute-start | bytes 884744 | tf_op jit(solution)/shard_map/ppermute | solution.py:508
  556.6 11.3 %collective-permute-start.118 = (bf16[4,96,384]{2,1,0:T(8,128)(2,1)S(1)}, bf16[4,96,384]{2,1,0:T(8,128)(2,1)S(1)}, u32[]{:S(2)}, u32[]{:S(2)}) collective-permute-start(bf16[4,96,384]{2,1,0:T(8,128)(2,1)S(1)} %fusion.21), channel_id=1, source_target_pairs={{0,1},{1,0},{2,3},{3,2},{4,5},{5,4},{6,7},{7,6},{8,9},{9,8},{10,11... | collective-permute-start | bytes 884744 | tf_op jit(solution)/shard_map/ppermute | solution.py:508
  563.5 8.5 %collective-permute-start.112 = (bf16[4,24,1536]{2,1,0:T(8,128)(2,1)S(1)}, bf16[4,24,1536]{2,1,0:T(8,128)(2,1)S(1)}, u32[]{:S(2)}, u32[]{:S(2)}) collective-permute-start(bf16[4,24,1536]{2,1,0:T(8,128)(2,1)S(1)} %fusion.19), channel_id=1, source_target_pairs={{0,16},{1,17},{2,18},{3,19},{4,20},{5,21},{6,22},{7,23},{8,24},{9,... | collective-permute-start | bytes 884744 | tf_op jit(solution)/shard_map/ppermute | solution.py:508
  568.1 9.3 %collective-permute-start.122 = (bf16[96,768]{1,0:T(8,128)(2,1)S(1)}, bf16[96,768]{1,0:T(8,128)(2,1)S(1)}, u32[]{:S(2)}, u32[]{:S(2)}) collective-permute-start(bf16[96,768]{1,0:T(8,128)(2,1)S(1)} %get-tuple-element.144), channel_id=1, source_target_pairs={{0,4},{1,5},{2,6},{3,7},{4,0},{5,1},{6,2},{7,3},{8,12},{9,13},{10,... | collective-permute-start | bytes 442376 | tf_op jit(solution)/shard_map/ppermute | solution.py:508
  569.0 8.4 %collective-permute-start.123 = (bf16[96,768]{1,0:T(8,128)(2,1)S(1)}, bf16[96,768]{1,0:T(8,128)(2,1)S(1)}, u32[]{:S(2)}, u32[]{:S(2)}) collective-permute-start(bf16[96,768]{1,0:T(8,128)(2,1)S(1)} %get-tuple-element.145), channel_id=1, source_target_pairs={{0,6},{1,7},{2,0},{3,1},{4,2},{5,3},{6,4},{7,5},{8,14},{9,15},{10,... | collective-permute-start | bytes 442376 | tf_op jit(solution)/shard_map/ppermute | solution.py:508
  572.3 7.8 %collective-permute-start.113 = (bf16[24,3072]{1,0:T(8,128)(2,1)S(1)}, bf16[24,3072]{1,0:T(8,128)(2,1)S(1)}, u32[]{:S(2)}, u32[]{:S(2)}) collective-permute-start(bf16[24,3072]{1,0:T(8,128)(2,1)S(1)} %get-tuple-element.146), channel_id=1, source_target_pairs={{0,2},{1,3},{2,4},{3,5},{4,6},{5,7},{6,0},{7,1},{8,10},{9,11},{10,... | collective-permute-start | bytes 442376 | tf_op jit(solution)/shard_map/ppermute | solution.py:508
  572.9 10.8 %collective-permute-start.114 = (bf16[24,3072]{1,0:T(8,128)(2,1)S(1)}, bf16[24,3072]{1,0:T(8,128)(2,1)S(1)}, u32[]{:S(2)}, u32[]{:S(2)}) collective-permute-start(bf16[24,3072]{1,0:T(8,128)(2,1)S(1)} %get-tuple-element.147), channel_id=1, source_target_pairs={{0,4},{1,5},{2,6},{3,7},{4,0},{5,1},{6,2},{7,3},{8,12},{9,13},{10,... | collective-permute-start | bytes 442376 | tf_op jit(solution)/shard_map/ppermute | solution.py:508
  575.3 8.5 %collective-permute-start.115 = (bf16[24,3072]{1,0:T(8,128)(2,1)S(1)}, bf16[24,3072]{1,0:T(8,128)(2,1)S(1)}, u32[]{:S(2)}, u32[]{:S(2)}) collective-permute-start(bf16[24,3072]{1,0:T(8,128)(2,1)S(1)} %get-tuple-element.148), channel_id=1, source_target_pairs={{0,6},{1,7},{2,0},{3,1},{4,2},{5,3},{6,4},{7,5},{8,14},{9,15},{10,... | collective-permute-start | bytes 442376 | tf_op jit(solution)/shard_map/ppermute | solution.py:508
  (130 other events, 756.2 us)

commit v2 on v1

v2 whole, which is shorter than its diff:
```python
import jax
import jax.numpy as jnp
from jax import lax
from jax.experimental import pallas as pl
from jax.experimental.pallas import tpu as pltpu
from jax.sharding import PartitionSpec as P

D = 768
HEADS = 12
HEAD_DIM = 64
APPS = 2
PAIR = 2 * HEAD_DIM
AXES = ("dp", "fsdp")
BF = jnp.bfloat16
F32 = jnp.float32
NN = (((1,), (0,)), ((), ()))
NT = (((1,), (1,)), ((), ()))
TN = (((0,), (0,)), ((), ()))
VMEM = 56 * 2**20
BQ, BV, BO, G1, S1, BB, G2, S2 = range(8)


def mm(left, right, dims):
    return lax.dot_general(left, right, dims, preferred_element_type=F32)


def params(limit=VMEM):
    return pltpu.CompilerParams(vmem_limit_bytes=limit)


def cost(flops, nbytes, trans=0):
    return pl.CostEstimate(flops=int(flops), bytes_accessed=int(nbytes), transcendentals=int(trans))


def once(shape, index):
    return pl.BlockSpec(shape, index, pipeline_mode=pl.Buffered(1))


def normed(z):
    centered = z - jnp.mean(z, axis=-1, keepdims=True)
    root = lax.rsqrt(jnp.mean(centered * centered, axis=-1, keepdims=True) + 1e-12)
    return centered * root, root


def normed_back(n, root, e):
    return root * (e - jnp.mean(e, axis=-1, keepdims=True) - n * jnp.mean(e * n, axis=-1, keepdims=True))


def colsum(v):
    return jnp.sum(v, axis=0, keepdims=True)


def qkv_body(x_ref, w_ref, vec_ref, o_ref, xt_ref):
    part = pl.program_id(0)

    @pl.when(part == 0)
    def _():
        xt_ref[...] = x_ref[...].T

    acc = mm(x_ref[...], w_ref[0], NN)
    bias = jnp.where(part == 0, vec_ref[BQ : BQ + 1, :], jnp.where(part == 2, vec_ref[BV : BV + 1, :], 0.0))
    o_ref[...] = (acc + bias).astype(BF)


def qkv_call(x, w, vec):
    rows = x.shape[0]
    return pl.pallas_call(
        qkv_body,
        grid=(3,),
        in_specs=[
            once((rows, D), lambda i: (0, 0)),
            pl.BlockSpec((1, D, D), lambda i: (i, 0, 0)),
            once(vec.shape, lambda i: (0, 0)),
        ],
        out_specs=[pl.BlockSpec((rows, D), lambda i: (0, i)), pl.BlockSpec((D, rows), lambda i: (0, 0))],
        out_shape=[jax.ShapeDtypeStruct((rows, 3 * D), BF), jax.ShapeDtypeStruct((D, rows), BF)],
        compiler_params=params(),
        cost_estimate=cost(6 * rows * D * D, 2 * (rows * D * 5 + 3 * D * D)),
        name="qkv",
    )(x, w, vec)


def attend_body(seq, pairs, len_ref, q_ref, k_ref, v_ref, o_ref, l_ref):
    count = len_ref[pl.program_id(0)]
    lane = lax.broadcasted_iota(jnp.int32, (seq, PAIR), 1)
    ok = lax.broadcasted_iota(jnp.int32, (1, seq), 1) < count
    units = [(pr, h) for pr in range(pairs) for h in range(2)]

    def score(unit):
        pr, h = unit
        cols = slice(pr * PAIR, (pr + 1) * PAIR)
        mine = (lane >= HEAD_DIM) == (h == 1)
        q = jnp.where(mine, q_ref[:, cols] * BF(0.125), BF(0))
        return jnp.where(ok, mm(q, k_ref[:, cols], NT), -1e30)

    ahead = score(units[0])
    held = {}
    for i, (pr, h) in enumerate(units):
        s = ahead
        if i + 1 < len(units):
            ahead = score(units[i + 1])
        cols = slice(pr * PAIR, (pr + 1) * PAIR)
        top = jnp.max(s, axis=1, keepdims=True)
        p = jnp.exp(s - top)
        total = jnp.sum(p, axis=1, keepdims=True)
        held[h] = mm(p.astype(BF), v_ref[:, cols], NN) / total
        l_ref[0, pr, h : h + 1, :] = (top + jnp.log(total)).reshape(1, seq)
        if h == 1:
            o_ref[:, cols] = jnp.where(lane < HEAD_DIM, held[0], held[1]).astype(BF)


def attend_call(qkv, lengths, pairs=3):
    rows = qkv.shape[0]
    count = lengths.shape[0]
    seq = rows // count
    groups = D // PAIR // pairs
    wide = PAIR * pairs

    def part(o):
        return pl.BlockSpec((seq, wide), lambda s, p, n: (s, o * groups + p))

    def body(*refs):
        attend_body(seq, pairs, *refs)

    flops = 4 * count * HEADS * seq * seq * HEAD_DIM
    return pl.pallas_call(
        body,
        grid_spec=pltpu.PrefetchScalarGridSpec(
            num_scalar_prefetch=1,
            grid=(count, groups),
            in_specs=[part(0), part(1), part(2)],
            out_specs=[part(0), pl.BlockSpec((1, pairs, 2, seq), lambda s, p, n: (s, p, 0, 0))],
        ),
        out_shape=[
            jax.ShapeDtypeStruct((rows, D), BF),
            jax.ShapeDtypeStruct((count, D // PAIR, 2, seq), F32),
        ],
        compiler_params=params(),
        cost_estimate=cost(4 * flops, 8 * rows * D, count * HEADS * seq * seq),
        name="attend",
    )(lengths, qkv, qkv, qkv)


def gelu_both(u):
    a = 0.7978845608028654
    sq = u * u
    t = jnp.tanh(u * (a + (a * 0.044715) * sq))
    half = 0.5 + 0.5 * t
    slope = half + (u * (0.5 - 0.5 * t * t)) * (a + (3 * a * 0.044715) * sq)
    return u * half, slope


def ffn_body(
    steps, x_ref, ctx_ref, wo_ref, vec_ref, wi_ref, wb_ref,
    z1_ref, h1t_ref, ctxt_ref, g_ref, gp_ref, z2_ref, y_ref, yb_ref,
    h1_s, h1b_s, acc_s,
):
    step = pl.program_id(0)

    @pl.when(step == 0)
    def _():
        ctx = ctx_ref[...]
        z1 = x_ref[...].astype(F32) + mm(ctx, wo_ref[0], NN) + vec_ref[BO : BO + 1, :]
        z1_ref[...] = z1
        n, _ = normed(z1)
        h1 = n * vec_ref[G1 : G1 + 1, :] + vec_ref[S1 : S1 + 1, :]
        h1_s[...] = h1
        low = h1.astype(BF)
        h1b_s[...] = low
        h1t_ref[...] = low.T
        ctxt_ref[...] = ctx.T

    f = mm(h1b_s[...], wi_ref[0], NN) + vec_ref[pl.ds(8 + step, 1), :]
    g, slope = gelu_both(f)
    g = g.astype(BF)
    g_ref[...] = g
    gp_ref[...] = slope.astype(BF)
    more = mm(g, wb_ref[...], NN)

    @pl.when(step == 0)
    def _():
        acc_s[...] = more

    @pl.when(step > 0)
    def _():
        acc_s[...] += more

    @pl.when(step == steps - 1)
    def _():
        z2 = h1_s[...] + acc_s[...] + vec_ref[BB : BB + 1, :]
        z2_ref[...] = z2
        n, _ = normed(z2)
        y = n * vec_ref[G2 : G2 + 1, :] + vec_ref[S2 : S2 + 1, :]
        y_ref[...] = y
        yb_ref[...] = y.astype(BF)


def ffn_call(x, ctx, wo, vec, wi, wb):
    rows = x.shape[0]
    ff = wb.shape[0]
    chunk = D
    steps = ff // chunk
    full = once((rows, D), lambda i: (0, 0))
    keep = once((rows, D), lambda i: (0, 0))
    cols = pl.BlockSpec((rows, chunk), lambda i: (0, i))
    flip = once((D, rows), lambda i: (0, 0))

    def body(*refs):
        ffn_body(steps, *refs)

    return pl.pallas_call(
        body,
        grid=(steps,),
        in_specs=[
            full,
            full,
            once((1, D, D), lambda i: (3, 0, 0)),
            once(vec.shape, lambda i: (0, 0)),
            pl.BlockSpec((1, D, chunk), lambda i: (i, 0, 0)),
            pl.BlockSpec((chunk, D), lambda i: (i, 0)),
        ],
        out_specs=[keep, flip, flip, cols, cols, keep, keep, keep],
        out_shape=[
            jax.ShapeDtypeStruct((rows, D), F32),
            jax.ShapeDtypeStruct((D, rows), BF),
            jax.ShapeDtypeStruct((D, rows), BF),
            jax.ShapeDtypeStruct((rows, ff), BF),
            jax.ShapeDtypeStruct((rows, ff), BF),
            jax.ShapeDtypeStruct((rows, D), F32),
            jax.ShapeDtypeStruct((rows, D), F32),
            jax.ShapeDtypeStruct((rows, D), BF),
        ],
        scratch_shapes=[pltpu.VMEM((rows, D), F32), pltpu.VMEM((rows, D), BF), pltpu.VMEM((rows, D), F32)],
        compiler_params=params(),
        cost_estimate=cost(2 * rows * D * (D + 2 * ff), 20 * rows * D + 4 * rows * ff + 4 * D * ff, rows * ff),
        name="ffn",
    )(x, ctx, wo, vec, wi, wb)


def ffn_back_body(
    steps, dy_ref, z2_ref, z1_ref, gp_ref, wb_ref, wi_ref, wo_ref, vec_ref,
    e2_ref, e1_ref, dz1_ref, ea_ref, dctx_ref, sums_ref,
    dz2_s, acc_s,
):
    step = pl.program_id(0)

    @pl.when(step == 0)
    def _():
        sums_ref[...] = jnp.zeros_like(sums_ref)
        dy = dy_ref[...].astype(F32)
        n, root = normed(z2_ref[...])
        sums_ref[G2 : G2 + 1, :] = colsum(dy * n)
        sums_ref[S2 : S2 + 1, :] = colsum(dy)
        dz2 = normed_back(n, root, dy * vec_ref[G2 : G2 + 1, :])
        dz2_s[...] = dz2
        low = dz2.astype(BF)
        e2_ref[...] = low
        sums_ref[BB : BB + 1, :] = colsum(low.astype(F32))

    df = mm(e2_ref[...], wb_ref[...], NT) * gp_ref[...].astype(F32)
    e1 = df.astype(BF)
    e1_ref[...] = e1
    sums_ref[pl.ds(8 + step, 1), :] = colsum(e1.astype(F32))
    more = mm(e1, wi_ref[0], NT)

    @pl.when(step == 0)
    def _():
        acc_s[...] = more

    @pl.when(step > 0)
    def _():
        acc_s[...] += more

    @pl.when(step == steps - 1)
    def _():
        dh1 = dz2_s[...] + acc_s[...]
        n, root = normed(z1_ref[...])
        sums_ref[G1 : G1 + 1, :] = colsum(dh1 * n)
        sums_ref[S1 : S1 + 1, :] = colsum(dh1)
        dz1 = normed_back(n, root, dh1 * vec_ref[G1 : G1 + 1, :])
        dz1_ref[...] = dz1
        low = dz1.astype(BF)
        ea_ref[...] = low
        sums_ref[BO : BO + 1, :] = colsum(low.astype(F32))
        dctx_ref[...] = mm(low, wo_ref[0], NT).astype(BF)


def ffn_back_call(dy, z2, z1, gp, wb, wi, wo, vec):
    rows = dy.shape[0]
    ff = wb.shape[0]
    chunk = D
    steps = ff // chunk
    keep = once((rows, D), lambda i: (0, 0))
    cols = pl.BlockSpec((rows, chunk), lambda i: (0, i))

    def body(*refs):
        ffn_back_body(steps, *refs)

    return pl.pallas_call(
        body,
        grid=(steps,),
        in_specs=[
            keep,
            keep,
            keep,
            cols,
            pl.BlockSpec((chunk, D), lambda i: (i, 0)),
            pl.BlockSpec((1, D, chunk), lambda i: (i, 0, 0)),
            once((1, D, D), lambda i: (3, 0, 0)),
            once(vec.shape, lambda i: (0, 0)),
        ],
        out_specs=[
            keep,
            cols,
            keep,
            keep,
            keep,
            once(vec.shape, lambda i: (0, 0)),
        ],
        out_shape=[
            jax.ShapeDtypeStruct((rows, D), BF),
            jax.ShapeDtypeStruct((rows, ff), BF),
            jax.ShapeDtypeStruct((rows, D), F32),
            jax.ShapeDtypeStruct((rows, D), BF),
            jax.ShapeDtypeStruct((rows, D), BF),
            jax.ShapeDtypeStruct(vec.shape, F32),
        ],
        scratch_shapes=[pltpu.VMEM((rows, D), F32), pltpu.VMEM((rows, D), F32)],
        compiler_params=params(),
        cost_estimate=cost(2 * rows * D * (D + 2 * ff), 20 * rows * D + 4 * rows * ff + 4 * D * ff),
        name="ffn_back",
    )(dy, z2, z1, gp, wb, wi, wo, vec)


def attend_back_body(seq, pairs, len_ref, q_ref, k_ref, v_ref, d_ref, l_ref, *rest):
    e_ref, bq_ref, bv_ref = rest[-3:]
    count = len_ref[pl.program_id(0)]
    lane = lax.broadcasted_iota(jnp.int32, (seq, PAIR), 1)
    ok = lax.broadcasted_iota(jnp.int32, (seq, seq), 0) < count
    units = [(pr, h) for pr in range(pairs) for h in range(2)]

    def score(unit):
        pr, h = unit
        cols = slice(pr * PAIR, (pr + 1) * PAIR)
        mine = (lane >= HEAD_DIM) == (h == 1)
        q = jnp.where(mine, q_ref[:, cols] * BF(0.125), BF(0))
        s = jnp.where(ok, mm(k_ref[:, cols], q, NT), -1e30)
        return s, mm(v_ref[:, cols], jnp.where(mine, d_ref[:, cols], BF(0)), NT)

    ahead = score(units[0])
    eq, ek, ev = {}, {}, {}
    for i, (pr, h) in enumerate(units):
        s, dp = ahead
        if i + 1 < len(units):
            ahead = score(units[i + 1])
        cols = slice(pr * PAIR, (pr + 1) * PAIR)
        if h == 0:
            kt = (k_ref[:, cols] * BF(0.125)).T
        p = jnp.exp(s - l_ref[0, pr, h : h + 1, :])
        pd = p * dp
        ds = (pd - p * colsum(pd)).astype(BF)
        ev[h] = mm(p.astype(BF), d_ref[:, cols], NN)
        ek[h] = mm(ds, q_ref[:, cols] * BF(0.125), NN)
        eq[h] = mm(kt[h * HEAD_DIM : (h + 1) * HEAD_DIM], ds, NN)
        if h == 1:
            low = jnp.concatenate([eq[0], eq[1]], axis=0).T.astype(BF)
            e_ref[0, :, cols] = low
            bq_ref[0, :, cols] = colsum(low.astype(F32))
            e_ref[1, :, cols] = jnp.where(lane < HEAD_DIM, ek[0], ek[1]).astype(BF)
            low = jnp.where(lane < HEAD_DIM, ev[0], ev[1]).astype(BF)
            e_ref[2, :, cols] = low
            bv_ref[0, :, cols] = colsum(low.astype(F32))


GROUPS = 2
WIDE = D // GROUPS


def attend_back_call(qkv, dctx, lse, lengths, group, after=()):
    rows = qkv.shape[0]
    count = lengths.shape[0]
    seq = rows // count
    pairs = WIDE // PAIR

    def part(o):
        return pl.BlockSpec((seq, WIDE), lambda s, n: (s, o * GROUPS + group))

    def body(*refs):
        attend_back_body(seq, pairs, *refs)

    flops = 10 * count * 2 * pairs * seq * seq * HEAD_DIM
    line = pl.BlockSpec((1, 1, WIDE), lambda s, n: (s, 0, 0))
    return pl.pallas_call(
        body,
        grid_spec=pltpu.PrefetchScalarGridSpec(
            num_scalar_prefetch=1,
            grid=(count,),
            in_specs=[
                part(0),
                part(1),
                part(2),
                part(0),
                pl.BlockSpec((1, pairs, 2, seq), lambda s, n: (s, group, 0, 0)),
            ]
            + [pl.BlockSpec(memory_space=pl.ANY)] * len(after),
            out_specs=[pl.BlockSpec((3, seq, WIDE), lambda s, n: (0, s, 0)), line, line],
        ),
        out_shape=[jax.ShapeDtypeStruct((3, rows, WIDE), BF)] + [jax.ShapeDtypeStruct((count, 1, WIDE), F32)] * 2,
        compiler_params=params(),
        cost_estimate=cost(4 * flops, 14 * rows * WIDE, count * 2 * pairs * seq * seq),
        name="attend_back",
    )(lengths, qkv, qkv, qkv, dctx, lse, *after)


def dx_body(dz1_ref, e0_ref, e1_ref, w_ref, *rest):
    o_ref = rest[-1]
    acc = dz1_ref[...]
    for i in range(3):
        acc += mm(e0_ref[i], w_ref[i, :, :WIDE], NT)
        acc += mm(e1_ref[i], w_ref[i, :, WIDE:], NT)
    o_ref[...] = acc.astype(o_ref.dtype)


def dx_call(dz1, e0, e1, w, dtype, after=(), block=256):
    rows = dz1.shape[0]
    line = pl.BlockSpec((block, D), lambda i: (i, 0))
    part = pl.BlockSpec((3, block, WIDE), lambda i: (0, i, 0))
    return pl.pallas_call(
        dx_body,
        grid=(rows // block,),
        in_specs=[line, part, part, once((3, D, D), lambda i: (0, 0, 0))]
        + [pl.BlockSpec(memory_space=pl.ANY)] * len(after),
        out_specs=line,
        out_shape=jax.ShapeDtypeStruct((rows, D), dtype),
        compiler_params=params(),
        cost_estimate=cost(6 * rows * D * D, 14 * rows * D + 6 * D * D),
        name="dx",
    )(dz1, e0, e1, w, *after)


def wgrad_body(rows, core_ref, a_ref, c_ref, b_ref, d_ref, *rest):
    keep_ref, send_ref, acc_s = rest[-3:]
    b = b_ref[...].reshape(b_ref.shape[-2:])
    d = d_ref[...].reshape(d_ref.shape[-2:])
    acc_s[...] = mm(a_ref[...], b, NN) + mm(c_ref[...], d, NN)
    part = 8 * rows
    for out, core in ((keep_ref, core_ref[0]), (send_ref, 1 - core_ref[0])):
        for xi in range(2):
            for s in range(8):
                start = pl.multiple_of(core * part + (2 * xi * part + s * rows), 8)
                out[xi, s // 2, s % 2, 0] = acc_s[pl.ds(start, rows), :].astype(BF)


def wgrad_call(core, a, c, b, d, rows, spec, units, width, after=()):
    m, k = a.shape
    held = once((m, k), lambda i, n: (0, 0))
    out = pl.BlockSpec((2, 4, 2, 1, rows, width), lambda i, n: (0, 0, 0, i, 0, 0))
    return pl.pallas_call(
        lambda *refs: wgrad_body(rows, *refs),
        grid_spec=pltpu.PrefetchScalarGridSpec(
            num_scalar_prefetch=1,
            grid=(units,),
            in_specs=[held, held, spec, spec] + [pl.BlockSpec(memory_space=pl.ANY)] * len(after),
            out_specs=[out, out],
            scratch_shapes=[pltpu.VMEM((m, width), F32)],
        ),
        out_shape=[jax.ShapeDtypeStruct((2, 4, 2, units, rows, width), BF)] * 2,
        compiler_params=params(),
        cost_estimate=cost(4 * k * m * width * units, 4 * k * (m + units * width) + 2 * m * width * units),
        name="wgrad",
    )(core, a, c, b, d, *after)


def wgrad_back_call(core, two, one, e_two, e_one, rows):
    k, ff = two.shape
    block = ff // 8

    def cols(other):
        def index(x, s, n):
            c = 1 - n[0] if other else n[0]
            return (0, (x * 2 + c) * 2 + s)

        return pl.BlockSpec((k, block), index)

    held = once((k, D), lambda x, s, n: (0, 0))
    out = pl.BlockSpec((1, 2, 2, 4, rows, D), lambda x, s, n: (x, s, 0, 0, 0, 0))

    def body(core_ref, g2k, g1k, g2s, g1s, e2_ref, e1_ref, keep_ref, send_ref):
        for a, c, o in ((g2k, g1k, keep_ref), (g2s, g1s, send_ref)):
            acc = mm(a[...], e2_ref[...], TN) + mm(c[...], e1_ref[...], TN)
            for s in range(16):
                o[0, s // 8, s // 4 % 2, s % 4] = acc[s * rows : (s + 1) * rows].astype(BF)

    return pl.pallas_call(
        body,
        grid_spec=pltpu.PrefetchScalarGridSpec(
            num_scalar_prefetch=1,
            grid=(2, 2),
            in_specs=[cols(False), cols(False), cols(True), cols(True), held, held],
            out_specs=[out, out],
        ),
        out_shape=[jax.ShapeDtypeStruct((2, 4, 2, 4, rows, D), BF)] * 2,
        compiler_params=params(),
        cost_estimate=cost(4 * k * ff * D, 4 * k * (ff + D) + 2 * ff * D),
        name="wgrad_back",
    )(core, two, one, two, one, e_two, e_one)


def layer_forward(x, low, weights, lengths):
    first, w_in, w_back, vec = weights
    qkv, lowt = qkv_call(low, first, vec)
    ctx, lse = attend_call(qkv, lengths)
    z1, h1t, ctxt, g, slope, z2, y, y_low = ffn_call(x, ctx, first, vec, w_in, w_back)
    return y, y_low, (lowt, qkv, lse, z1, h1t, ctxt, g, slope, z2)


class Grid:
    def __init__(self, sizes):
        self.dp, self.fsdp = sizes["dp"], sizes["fsdp"]
        self.count = self.dp * self.fsdp
        self.x, self.core = self.dp // 2, 2
        self.y = self.fsdp // 4
        self.z = self.fsdp // self.y if self.y else 0
        self.staged = self.x == 2 and self.y == 2

    def place(self):
        dp, fsdp = lax.axis_index("dp"), lax.axis_index("fsdp")
        return dp // 2, dp % 2, fsdp // self.y, fsdp % self.y

    def shift(self, dim, step):
        sizes = (self.x, self.core, self.z, self.y)
        pairs = []
        for i in range(self.count):
            at = [i // (self.core * self.fsdp), i // self.fsdp % self.core, i % self.fsdp // self.y, i % self.y]
            at[dim] = (at[dim] + step) % sizes[dim]
            pairs.append((i, ((at[0] * self.core + at[1]) * self.z + at[2]) * self.y + at[3]))
        return pairs

    def send(self, value, dim, step=1):
        return lax.ppermute(value, AXES, self.shift(dim, step))


X, CORE, Z, Y = range(4)


def pack_body(at_ref, wq_ref, wo_ref, wi_ref, wb_ref, *rest):
    vectors, span_ref, one_ref, two_ref, line_s = rest[:8], rest[8], rest[9], rest[10], rest[11]
    rows = wq_ref.shape[0]
    for i in range(3):
        one_ref[i] = wq_ref[:, i * D : (i + 1) * D]
    one_ref[3] = wo_ref[...]
    for i in range(4):
        two_ref[i] = wi_ref[:, i * D : (i + 1) * D]
        two_ref[4 + i] = wb_ref[i * rows : (i + 1) * rows]
    line_s[...] = jnp.zeros_like(line_s)
    for i, ref in enumerate(vectors):
        line_s[i : i + 1, :rows] = ref[...].astype(F32)
    span = span_ref.shape[1]
    line_s[8:9, :span] = span_ref[...].astype(F32)
    device = at_ref[0]
    per = D // span
    top = pltpu.roll(line_s[:8], device * rows, 1)
    low = pltpu.roll(line_s[8:16], lax.rem(device, per) * span, 1)
    here = lax.broadcasted_iota(jnp.int32, (8, D), 0) == lax.div(device, per)
    low = jnp.where(here, jnp.broadcast_to(low[:1], (8, D)), 0.0)
    one_ref[4] = jnp.concatenate([top, low, jnp.zeros((rows - 16, D), F32)], axis=0).astype(BF)


def pack(device, w_qkv, w_out, w_in, w_back, vectors, span):
    rows = w_qkv.shape[0]
    return pl.pallas_call(
        pack_body,
        grid_spec=pltpu.PrefetchScalarGridSpec(
            num_scalar_prefetch=1,
            grid=(1,),
            in_specs=[pl.BlockSpec(memory_space=pltpu.VMEM)] * 13,
            out_specs=[pl.BlockSpec(memory_space=pltpu.VMEM)] * 2,
            scratch_shapes=[pltpu.VMEM((16, D), F32)],
        ),
        out_shape=[jax.ShapeDtypeStruct((5, rows, D), BF), jax.ShapeDtypeStruct((8, rows, D), BF)],
        compiler_params=params(8 * 2**20),
        name="pack",
    )(device, w_qkv, w_out, w_in, w_back, *[v[None] for v in vectors], span[None])


def place_body(split, at_ref, *refs):
    parts, outs, sems = refs[:8], refs[8:-1], refs[-1]
    x, core, z, y = at_ref[0], at_ref[1], at_ref[2], at_ref[3]
    copies = []
    for i, part in enumerate(parts):
        side, far, other = i >> 2, (i >> 1) & 1, i & 1
        count = part.shape[2]
        for near in range(2):
            px = (x + (far if side == 0 else near)) % 2
            py = (y + (near if side == 0 else far)) % 2
            pc = (core + other) % 2
            for dz in range(4):
                pz = (z + 4 - dz) % 4
                if split:
                    target = outs[side].at[:, px, pc, pz, py] if side == 0 else outs[side].at[px, pc, pz, py]
                else:
                    target = outs[0].at[pl.ds(0 if side == 0 else 5 - count, count), px, pc, pz, py]
                copies.append(pltpu.make_async_copy(part.at[near, dz], target, sems.at[len(copies)]))
    for copy in copies:
        copy.start()
    for copy in copies:
        copy.wait()


def place(at, parts, split):
    rows = parts[0].shape[3]
    if split:
        shapes = [(4, 2, 2, 4, 2, rows, D), (2, 2, 4, 2, 4, rows, D)]
    else:
        shapes = [(5, 2, 2, 4, 2, rows, D)]
    return pl.pallas_call(
        lambda *refs: place_body(split, *refs),
        grid_spec=pltpu.PrefetchScalarGridSpec(
            num_scalar_prefetch=1,
            grid=(1,),
            in_specs=[pl.BlockSpec(memory_space=pl.ANY)] * 8,
            out_specs=[pl.BlockSpec(memory_space=pl.ANY)] * len(shapes),
            scratch_shapes=[pltpu.SemaphoreType.DMA((64,))],
        ),
        out_shape=[jax.ShapeDtypeStruct(shape, BF) for shape in shapes],
        compiler_params=params(2 * 2**20),
        name="place",
    )(at, *parts)


def gather_packet(grid, at, packet, first, split):
    ring = [packet] + [grid.send(packet, Z, k) for k in range(1, 4)]
    parts = []
    for units, order in ((slice(0, first), (Y, X)), (slice(first, None), (X, Y))):
        line = jnp.stack([r[units] for r in ring])
        near = jnp.stack([line, grid.send(line, order[0])])
        far = grid.send(near, order[1])
        parts += [near, grid.send(near, CORE), far, grid.send(far, CORE)]
    return place(at, parts, split)


def pick(value, index, dim):
    return lax.dynamic_index_in_dim(value, index, dim, keepdims=False)


def added(a, b, *picks):
    for index, dim in picks:
        a, b = pick(a, index, dim), pick(b, index, dim)
    return (a.astype(F32) + b.astype(F32)).astype(BF)


class Sum:
    def __init__(self, grid, place, left, right):
        self.grid, self.place = grid, place
        self.left = (left[0], grid.send(left[1], CORE))
        self.right = (right[0], grid.send(right[1], CORE))

    def one(self):
        x, _, _, y = self.place
        out_l, out_r = added(*self.left, (1 - x, 0)), added(*self.right, (1 - y, 2))
        keep_l, keep_r = added(*self.left, (x, 0)), added(*self.right, (y, 2))
        self.left = (keep_l, self.grid.send(out_l, X))
        self.right = (keep_r, self.grid.send(out_r, Y))
        return [out_l, out_r]

    def two(self):
        x, _, _, y = self.place
        out_l, out_r = added(*self.left, (1 - y, 1)), added(*self.right, (1 - x, 0))
        keep_l, keep_r = added(*self.left, (y, 1)), added(*self.right, (x, 0))
        self.left = (keep_l, self.grid.send(out_l, Y))
        self.right = (keep_r, self.grid.send(out_r, X))
        return [out_l, out_r]

    def three(self):
        z = self.place[2]
        line = jnp.concatenate([added(*self.left), added(*self.right)], axis=1)
        self.own = pick(line, z, 0)
        self.came = [self.grid.send(pick(line, (z + k) % 4, 0), Z, k) for k in range(1, 4)]
        return [line]

    def result(self):
        total = self.own.astype(F32)
        for piece in self.came:
            total += piece.astype(F32)
        return total


def staged(grid, lengths, tokens, cotangent, shards):
    w_qkv, bias_q, bias_v, w_out, bias_out, gain_one, shift_one, w_in, bias_in, w_back, bias_back, gain_two, shift_two = shards
    rows, span = bias_q.shape[0], bias_in.shape[0]
    where = grid.place()
    x, core, z, y = where
    device = lax.axis_index(AXES)
    at = jnp.stack([x, core, z, y]).astype(jnp.int32)
    core = core.astype(jnp.int32)[None]
    vectors = [bias_q, bias_v, bias_out, gain_one, shift_one, bias_back, gain_two, shift_two]
    one, two = pack(device.astype(jnp.int32)[None], w_qkv, w_out, w_in, w_back, vectors, bias_in)
    (first,) = gather_packet(grid, at, one, 2, False)
    w_in, w_back = gather_packet(grid, at, two, 4, True)
    first = first.reshape(5, grid.count * rows, D)
    w_in = w_in.reshape(4, grid.count * rows, D)
    w_back = w_back.reshape(grid.count * span, D)
    vec = jnp.sum(first[4].reshape(grid.count, rows, D).astype(F32), axis=0)
    weights = (first, w_in, w_back, vec)

    value, low = tokens, tokens
    saved = []
    for _ in range(APPS):
        value, low, stored = layer_forward(value, low, weights, lengths)
        saved.append(stored)
    activations = low

    lowt2, qkv, lse, z1, h1t2, ctxt2, g2, slope, z2 = saved[1]
    e2_2, e1_2, dz1, ea_2, dctx, sums_2 = ffn_back_call(cotangent, z2, z1, slope, w_back, w_in, first, vec)
    heads_2 = [attend_back_call(qkv, dctx, lse, lengths, i) for i in range(GROUPS)]
    grad = dx_call(dz1, heads_2[0][0], heads_2[1][0], first, F32)

    lowt1, qkv, lse, z1, h1t1, ctxt1, g1, slope, z2 = saved[0]
    e2_1, e1_1, dz1, ea_1, dctx, sums_1 = ffn_back_call(grad, z2, z1, slope, w_back, w_in, first, vec)
    right = wgrad_back_call(core, g2, g1, e2_2, e2_1, rows)
    left = wgrad_call(
        core, h1t2, h1t1, e1_2, e1_1, rows, pl.BlockSpec((tokens.shape[0], D), lambda i, n: (0, i)), 4, D
    )
    wide = Sum(grid, where, left, right)

    def by_heads(i, after):
        spec = pl.BlockSpec((1, tokens.shape[0], WIDE), lambda i, n: (i, 0, 0))
        return wgrad_call(core, lowt2, lowt1, heads_2[i][0], heads_1[i][0], rows, spec, 3, WIDE, after)

    heads_1 = [attend_back_call(qkv, dctx, lse, lengths, 0)]
    left = by_heads(0, ())
    right = wgrad_call(
        core, ctxt2, ctxt1, ea_2, ea_1, rows, pl.BlockSpec((tokens.shape[0], WIDE), lambda i, n: (0, i)), 2, WIDE
    )
    group_0 = Sum(grid, where, left, right)
    heads_1.append(attend_back_call(qkv, dctx, lse, lengths, 1, wide.one()))
    after = group_0.one() + wide.two()
    left = by_heads(1, after)
    sums = sums_1 + sums_2
    by_group = [[a + b for a, b in zip(heads_1[i][1:], heads_2[i][1:])] for i in range(GROUPS)]
    line_q, line_v = [jnp.concatenate([jnp.sum(by_group[i][j], axis=0) for i in range(GROUPS)], axis=1) for j in range(2)]
    small = jnp.concatenate([line_q, line_v, sums[2:12]], axis=0).astype(BF)
    small = jnp.concatenate([small[:, :WIDE], small[:, WIDE:]], axis=0)
    small = jnp.broadcast_to(small, (2, 4, 2, 1) + small.shape)
    group_1 = Sum(grid, where, left, (small, small))
    after = group_1.one() + group_0.two()
    grad = dx_call(dz1, heads_1[0][0], heads_1[1][0], first, BF, after)
    wide.three()
    group_0.three()
    group_1.two()
    group_1.three()
    total, half_0, half_1 = wide.result(), group_0.result(), group_1.result()

    w_in_grad = total[:4].swapaxes(0, 1).reshape(rows, 4 * D)
    w_back_grad = total[4:].reshape(4 * rows, D)
    w_qkv_grad = jnp.stack([half_0[:3], half_1[:3]], axis=1).transpose(2, 0, 1, 3).reshape(rows, 3 * D)
    w_out_grad = half_0[3:].swapaxes(0, 1).reshape(rows, D)
    small = half_1[3]
    small = jnp.concatenate([small[:12], small[12:]], axis=1)
    mine = lax.dynamic_slice(small, (0, device * rows), (8, rows))
    per = D // span
    last = lax.dynamic_slice(small, (8 + device // per, device % per * span), (1, span))[0]
    return activations, grad, w_qkv_grad, w_out_grad, w_in_grad, w_back_grad, [mine[i] for i in range(8)] + [last]


def plain(grid, lengths, tokens, cotangent, shards):
    w_qkv, bias_q, bias_v, w_out, bias_out, gain_one, shift_one, w_in, bias_in, w_back, bias_back, gain_two, shift_two = shards
    vectors = [bias_q, bias_v, bias_out, gain_one, shift_one, bias_back, gain_two, shift_two]

    def whole(v):
        return lax.all_gather(v, AXES, axis=0, tiled=True)

    lines = jnp.stack([whole(v) for v in vectors])
    vec = jnp.concatenate([lines, whole(bias_in).reshape(4, D), jnp.zeros((4, D), BF)], axis=0).astype(F32)

    def blocks(w):
        return w.reshape(D, -1, D).swapaxes(0, 1)

    first = jnp.concatenate([blocks(whole(w_qkv)), whole(w_out)[None], jnp.zeros((1, D, D), BF)], axis=0)
    w_in, w_back = blocks(whole(w_in)), whole(w_back)
    weights = (first, w_in, w_back, vec)
    value, low = tokens, tokens
    saved = []
    for _ in range(APPS):
        value, low, stored = layer_forward(value, low, weights, lengths)
        saved.append(stored)
    activations, grad, totals = low, cotangent, None
    for step in reversed(range(APPS)):
        lowt, qkv, lse, z1, h1t, ctxt, g, slope, z2 = saved[step]
        e2, e1, dz1, ea, dctx, sums = ffn_back_call(grad, z2, z1, slope, w_back, w_in, first, vec)
        heads = [attend_back_call(qkv, dctx, lse, lengths, i) for i in range(GROUPS)]
        grad = dx_call(dz1, heads[0][0], heads[1][0], first, F32 if step else BF)
        e = jnp.concatenate([heads[i][0] for i in range(GROUPS)], axis=2).swapaxes(0, 1).reshape(-1, 3 * D)
        lines = [jnp.concatenate([jnp.sum(heads[i][j], axis=0) for i in range(GROUPS)], axis=1) for j in (1, 2)]
        grads = [mm(lowt, e, NN), mm(ctxt, ea, NN), mm(h1t, e1, NN), mm(g, e2, TN)]
        grads += [jnp.concatenate(lines + [sums[2:]], axis=0)]
        totals = grads if totals is None else [a + b for a, b in zip(totals, grads)]
    lines = list(totals.pop())
    totals += lines[:8] + [jnp.concatenate(lines[8:12])]
    owned = [lax.psum_scatter(v, AXES, scatter_dimension=0, tiled=True) for v in totals]
    return activations, grad, *owned[:4], owned[4:]


def make_local(grid):
    def local(tokens, lengths, *rest):
        run = staged if grid.staged else plain
        activations, grad, w_qkv, w_out, w_in, w_back, lines = run(grid, lengths, tokens, rest[-1], rest[:-1])
        return (
            activations, grad, w_qkv, lines[BQ], lines[BV], w_out, lines[BO], lines[G1], lines[S1],
            w_in, lines[8], w_back, lines[BB], lines[G2], lines[S2],
        )

    return local


def solution(mesh):
    wide, line = P(AXES, None), P(AXES)
    return jax.shard_map(
        make_local(Grid(mesh.shape)),
        mesh=mesh,
        in_specs=(wide, line, wide, line, line, wide, line, line, line, wide, line, wide, line, line, line, wide),
        out_specs=(wide, wide, wide, line, line, wide, line, line, line, wide, line, wide, line, line, line),
        check_vma=False,
    )
```

time: 596 us -> 531 us (0.89)
  starting transfers between devices: 116 us -> 64.1 us
  local copies, waits for them, and re-layouts: 71.4 us -> 38.3 us
  waiting for transfers between devices: 99.8 us -> 116 us
  Pallas kernels: 281 us -> 288 us
    ppermute x124 -> x49, starting transfers between devices: 116 us -> 64.1 us  [send(): return lax.ppermute(value, AXES, self.shift(dim, step))]
    ppermute x124 -> x49, waiting for transfers between devices: 99.8 us -> 116 us  [send(): return lax.ppermute(value, AXES, self.shift(dim, step))]
    dynamic_slice x17 -> x0, local copies, waits for them, and re-layouts: 13.2 us -> none  [pick(): return lax.dynamic_index_in_dim(value, index, dim, keepdims=False)]
    unnamed x168 -> x85, local copies, waits for them, and re-layouts: 32 us -> 21.2 us
    pallas_call x0 -> x5, local copies, waits for them, and re-layouts: none -> 10.5 us  [the longest x4 7.23 us: wgrad_call(): pl.pallas_call(lambda *refs: wgrad_body(rows, *refs), grid_spec=pltpu.Pre...]
    concatenate x4 -> x0, local copies, waits for them, and re-layouts: 9.76 us -> none  [the longest x1 6.14 us: local(): jnp.concatenate([bias_q, bias_v, bias_out, gain_one, shift_one, bias_back...]
    slice x24 -> x3, local copies, waits for them, and re-layouts: 9.39 us -> 0.76 us  [the longest x1 0.75 us: staged(): w_back_grad = total[4:].reshape(4 * rows, D)]
    convert_element_type x37 -> x20, other arithmetic: 3.12 us -> 10.5 us  [added(): return (a.astype(F32) + b.astype(F32)).astype(BF)]
  transfers between devices with their start and end apart: 124 -> 49, of which waited for: 47 -> 19; matrix products, arithmetic and copies ran while one was open for 7% -> 5% of each run, Pallas kernels for 17% -> 19%
where the time goes in v2:
time: 531 us; the launch traced here: 523 us
  Pallas kernels  288 us (54%)
  waiting for transfers between devices  116 us (22%)
  starting transfers between devices  64.1 us (12%)
  local copies, waits for them, and re-layouts  38.3 us (7%)
  other arithmetic  14.8 us (3%)
    ppermute x49, waiting for transfers between devices, send(): return lax.ppermute(value, AXES, self.shift(dim, step))  116 us
    ppermute x49, starting transfers between devices, send(): return lax.ppermute(value, AXES, self.shift(dim, step))  64.1 us
    pallas_call x2, Pallas kernels, ffn_call(): pl.pallas_call(body, grid=(steps,), in_specs=[full, full, once((1, D, D),...  57.4 us
    pallas_call x2, Pallas kernels, ffn_back_call(): pl.pallas_call(body, grid=(steps,), in_specs=[keep, keep, keep, cols, pl....  55.3 us
    pallas_call x4, Pallas kernels, attend_back_call(): pl.pallas_call(body, grid_spec=pltpu.PrefetchScalarGridSpec(num_scalar_pr...  50 us
    pallas_call x4, Pallas kernels, wgrad_call(): pl.pallas_call(lambda *refs: wgrad_body(rows, *refs), grid_spec=pltpu.Pre...  39.6 us
    pallas_call x2, Pallas kernels, attend_call(): pl.pallas_call(body, grid_spec=pltpu.PrefetchScalarGridSpec(num_scalar_pr...  25.9 us
    unnamed x85, local copies, waits for them, and re-layouts  21.2 us
  transfers between devices with their start and end apart: 49, of which 19 were waited for; matrix products, arithmetic and copies ran while one was open for 5% of the time, Pallas kernels for 19%

profile of v2, /device:TPU:0, one launch (start us, length us, event | category | flops | bytes accessed | tf_op | source)
XLA Modules:
  0.0 523.1 jit_solution(6203483888860276780)
XLA Ops:
  10.2 3.1 collective-permute-start.11
  13.2 2.6 collective-permute-start.12
  17.6 1.7 collective-permute-start.1
  19.4 19.5 %collective-permute-done.2 = bf16[5,24,768]{2,1,0:T(8,128)(2,1)S(1)} collective-permute-done((bf16[5,24,768]{2,1,0:T(8,128)(2,1)S(1)}, bf16[5,24,768]{2,1,0:T(8,128)(2,1)S(1)}, u32[]{:S(2)}, u32[]{:S(2)}) %collective-permute-start.2) | collective-permute-done | bytes 184352 | tf_op jit(solution)/shard_map/ppermute | solution.py:540
  38.9 15.0 %collective-permute-start = (bf16[5,24,768]{2,1,0:T(8,128)(2,1)S(1)}, bf16[5,24,768]{2,1,0:T(8,128)(2,1)S(1)}, u32[]{:S(2)}, u32[]{:S(2)}) collective-permute-start(bf16[5,24,768]{2,1,0:T(8,128)(2,1)S(1)} %get-tuple-element.76), channel_id=1, source_target_pairs={{0,2},{1,3},{2,4},{3,5},{4,6},{5,7},{6,0},{7,1},{8,10},{9,11},{10,... | collective-permute-start | bytes 552968 | tf_op jit(solution)/shard_map/ppermute | solution.py:540
  53.8 3.3 collective-permute-done.1
  57.9 1.6 collective-permute-start.7
  59.7 1.6 collective-permute-start.14
  62.6 8.4 %collective-permute-done.7 = bf16[4,3,24,768]{3,2,1,0:T(8,128)(2,1)S(1)} collective-permute-done((bf16[4,3,24,768]{3,2,1,0:T(8,128)(2,1)S(1)}, bf16[4,3,24,768]{3,2,1,0:T(8,128)(2,1)S(1)}, u32[]{:S(2)}, u32[]{:S(2)}) %collective-permute-start.7) | collective-permute-done | bytes 442400 | tf_op jit(solution)/shard_map/ppermute | solution.py:540
  71.2 1.6 collective-permute-start.9
  72.8 9.6 %collective-permute-done.3 = bf16[4,2,24,768]{3,2,1,0:T(8,128)(2,1)S(1)} collective-permute-done((bf16[4,2,24,768]{3,2,1,0:T(8,128)(2,1)S(1)}, bf16[4,2,24,768]{3,2,1,0:T(8,128)(2,1)S(1)}, u32[]{:S(2)}, u32[]{:S(2)}) %collective-permute-start.3) | collective-permute-done | bytes 294944 | tf_op jit(solution)/shard_map/ppermute | solution.py:540
  83.2 1.6 collective-permute-start.16
  84.8 1.6 collective-permute-start.20
  86.4 12.4 %collective-permute-done.5.refs_3_ = bf16[2,4,2,24,768]{4,3,2,1,0:T(8,128)(2,1)} collective-permute-done((bf16[2,4,2,24,768]{4,3,2,1,0:T(8,128)(2,1)S(1)}, bf16[2,4,2,24,768]{4,3,2,1,0:T(8,128)(2,1)}, u32[]{:S(2)}, u32[]{:S(2)}) %collective-permute-start.5) | collective-permute-done | bytes 589856 | tf_op jit(solution)/shard_map/ppermute | solution.py:540
  98.9 2.5 collective-permute-done.9.refs_7_
  102.8 2.7 collective-permute-done.6.refs_4_
  105.9 14.1 %collective-permute-done.16.refs_3_ = bf16[2,4,4,24,768]{4,3,2,1,0:T(8,128)(2,1)} collective-permute-done((bf16[2,4,4,24,768]{4,3,2,1,0:T(8,128)(2,1)S(1)}, bf16[2,4,4,24,768]{4,3,2,1,0:T(8,128)(2,1)}, u32[]{:S(2)}, u32[]{:S(2)}) %collective-permute-start.16) | collective-permute-done | bytes 1179680 | tf_op jit(solution)/shard_map/ppermute | solution.py:540
  120.1 4.7 collective-permute-done.20.refs_7_
  128.1 4.2 place.2
  133.4 1.6 copy-done
  134.9 8.2 %qkv.2 = (bf16[1024,2304]{1,0:T(8,128)(2,1)}, bf16[768,1024]{1,0:T(8,128)(2,1)}) custom-call(bf16[1024,768]{1,0:T(8,128)(2,1)} %refs_0_.9, bf16[5,768,768]{2,1,0:T(8,128)(2,1)} %bitcast.232, f32[24,768]{1,0:T(8,128)} %convert_reduce_fusion.vec_ref.refs_3_.refs_7_), custom_call_target="tpu_custom_call" | custom-call | flops 3623878656 | bytes 11403264 | tf_op jit(solution)/shard_map/qkv/pallas_call | solution.py:67
  143.1 12.9 %attend.2 = (bf16[1024,768]{1,0:T(8,128)(2,1)}, f32[2,6,2,512]{3,2,1,0:T(2,128)}) custom-call(s32[2]{0:T(128)} %refs_0_.15, bf16[1024,2304]{1,0:T(8,128)(2,1)} %get-tuple-element.77.refs_1_.refs_2_.refs_3_, bf16[1024,2304]{1,0:T(8,128)(2,1)} %get-tuple-element.77.refs_1_.refs_2_.refs_3_, bf16[1024,2304]{1,0:T(8,128)(2,1)} %get-tuple-element.77.refs_1_.refs_2_.refs_3_), custom_call_target="tpu_custom_call" | custom-call | flops 6442450944 | bytes 6291456 | tf_op jit(solution)/shard_map/attend/pallas_call | solution.py:126
  156.1 5.4 %place.3 = (bf16[4,2,2,4,2,24,768]{6,5,4,3,2,1,0:T(8,128)(2,1)S(1)}, bf16[2,2,4,2,4,24,768]{6,5,4,3,2,1,0:T(8,128)(2,1)S(1)}) custom-call(s32[4]{0:T(128)S(1)} %pad_add_fusion.refs_0_, bf16[2,4,4,24,768]{4,3,2,1,0:T(8,128)(2,1)S(1)} %pad_maximum_fusion.refs_1_, bf16[2,4,4,24,768]{4,3,2,1,0:T(8,128)(2,1)} %collective-permute-done.15.refs_2_, ...), custom_call_target="tpu_custom_call" | custom-call | tf_op jit(solution)/shard_map/place/pallas_call | solution.py:616
  161.5 2.2 copy-done.20
  163.7 2.1 copy-done.21
  165.8 28.5 %ffn.2 = (f32[1024,768]{1,0:T(8,128)}, bf16[768,1024]{1,0:T(8,128)(2,1)}, bf16[768,1024]{1,0:T(8,128)(2,1)}, bf16[1024,3072]{1,0:T(8,128)(2,1)}, bf16[1024,3072]...) custom-call(bf16[1024,768]{1,0:T(8,128)(2,1)} %refs_0_.9, ...), custom_call_target="tpu_custom_call" | custom-call | flops 10871635968 | bytes 37748736 | tf_op jit(solution)/shard_map/ffn/pallas_call | solution.py:211
  194.4 8.1 %qkv.3 = (bf16[1024,2304]{1,0:T(8,128)(2,1)}, bf16[768,1024]{1,0:T(8,128)(2,1)}) custom-call(bf16[1024,768]{1,0:T(8,128)(2,1)} %get-tuple-element.83.x_ref, bf16[5,768,768]{2,1,0:T(8,128)(2,1)} %bitcast.234, f32[24,768]{1,0:T(8,128)} %convert_reduce_fusion.vec_ref.refs_3_.refs_7_), custom_call_target="tpu_custom_call" | custom-call | flops 3623878656 | bytes 11403264 | tf_op jit(solution)/shard_map/qkv/pallas_call | solution.py:67
  202.5 13.0 %attend.3 = (bf16[1024,768]{1,0:T(8,128)(2,1)}, f32[2,6,2,512]{3,2,1,0:T(2,128)}) custom-call(s32[2]{0:T(128)} %refs_0_.15, bf16[1024,2304]{1,0:T(8,128)(2,1)} %get-tuple-element.84.refs_1_.refs_2_.refs_3_, bf16[1024,2304]{1,0:T(8,128)(2,1)} %get-tuple-element.84.refs_1_.refs_2_.refs_3_, bf16[1024,2304]{1,0:T(8,128)(2,1)} %get-tuple-element.84.refs_1_.refs_2_.refs_3_), custom_call_target="tpu_custom_call" | custom-call | flops 6442450944 | bytes 6291456 | tf_op jit(solution)/shard_map/attend/pallas_call | solution.py:126
  215.5 28.9 %ffn.3 = (f32[1024,768]{1,0:T(8,128)}, bf16[768,1024]{1,0:T(8,128)(2,1)}, bf16[768,1024]{1,0:T(8,128)(2,1)}, bf16[1024,3072]{1,0:T(8,128)(2,1)}, bf16[1024,3072]...) custom-call(f32[1024,768]{1,0:T(8,128)} %get-tuple-element.82.refs_0_, ...), custom_call_target="tpu_custom_call" | custom-call | flops 10871635968 | bytes 37748736 | tf_op jit(solution)/shard_map/ffn/pallas_call | solution.py:211
  244.4 27.7 %ffn_back.2 = (bf16[1024,768]{1,0:T(8,128)(2,1)}, bf16[1024,3072]{1,0:T(8,128)(2,1)}, f32[1024,768]{1,0:T(8,128)}, bf16[1024,768]{1,0:T(8,128)(2,1)}, bf16[1024,768]{1,0:T(8,128)(2,1)}, /*index=5*/f32[24,768]{1,0:T(8,128)}) custom-call(bf16[1024,768]{1,0:T(8,128)(2,1)} %refs_0_.11, f32[1024,768]{1,0:T(8,128)} %get-tuple-element.87.refs_1_, ...), custom_call_target="tpu_custom_call" | custom-call | flops 10871635968 | bytes 37748736 | tf_op jit(solution)/shard_map/ffn_back/pallas_call | solution.py:299
  272.1 12.5 %attend_back.5 = (bf16[3,1024,384]{2,1,0:T(8,128)(2,1)}, f32[2,1,384]{2,1,0:T(1,128)}, f32[2,1,384]{2,1,0:T(1,128)}) custom-call(s32[2]{0:T(128)} %refs_0_.15, bf16[1024,2304]{1,0:T(8,128)(2,1)} %get-tuple-element.84.refs_1_.refs_2_.refs_3_, bf16[1024,2304]{1,0:T(8,128)(2,1)} %get-tuple-element.84.refs_1_.refs_2_.refs_3_, ...), custom_call_target="tpu_custom_call" | custom-call | flops 8053063680 | bytes 5505024 | tf_op jit(solution)/shard_map/attend_back/pallas_call | solution.py:393
  284.6 12.3 %attend_back.4 = (bf16[3,1024,384]{2,1,0:T(8,128)(2,1)}, f32[2,1,384]{2,1,0:T(1,128)}, f32[2,1,384]{2,1,0:T(1,128)}) custom-call(s32[2]{0:T(128)} %refs_0_.15, bf16[1024,2304]{1,0:T(8,128)(2,1)} %get-tuple-element.84.refs_1_.refs_2_.refs_3_, bf16[1024,2304]{1,0:T(8,128)(2,1)} %get-tuple-element.84.refs_1_.refs_2_.refs_3_, ...), custom_call_target="tpu_custom_call" | custom-call | flops 8053063680 | bytes 5505024 | tf_op jit(solution)/shard_map/attend_back/pallas_call | solution.py:393
  296.9 9.6 %dx.2.refs_0_ = f32[1024,768]{1,0:T(8,128)} custom-call(f32[1024,768]{1,0:T(8,128)} %get-tuple-element.90.dz1_ref, bf16[3,1024,384]{2,1,0:T(8,128)(2,1)} %get-tuple-element.93.e0_ref.refs_3_, bf16[3,1024,384]{2,1,0:T(8,128)(2,1)} %get-tuple-element.94.e1_ref.refs_3_, bf16[5,768,768]{2,1,0:T(8,128)(2,1)} %bitcast.237), custom_call_target="tpu_custom_call" | custom-call | flops 3623878656 | bytes 14548992 | tf_op jit(solution)/shard_map/dx/pallas_call | solution.py:428
  306.5 27.6 %ffn_back.3 = (bf16[1024,768]{1,0:T(8,128)(2,1)}, bf16[1024,3072]{1,0:T(8,128)(2,1)}, f32[1024,768]{1,0:T(8,128)}, bf16[1024,768]{1,0:T(8,128)(2,1)}, bf16[1024,768]{1,0:T(8,128)(2,1)}, /*index=5*/f32[24,768]{1,0:T(8,128)}) custom-call(f32[1024,768]{1,0:T(8,128)} %dx.2.refs_0_, f32[1024,768]{1,0:T(8,128)} %get-tuple-element.95.refs_1_, ...), custom_call_target="tpu_custom_call" | custom-call | flops 10871635968 | bytes 37748736 | tf_op jit(solution)/shard_map/ffn_back/pallas_call | solution.py:299
  334.1 15.0 %wgrad.4 = (bf16[2,4,2,4,24,768]{5,4,3,2,1,0:T(8,128)(2,1)}, bf16[2,4,2,4,24,768]{5,4,3,2,1,0:T(8,128)(2,1)}) custom-call(s32[1]{0:T(128)} %bitcast.1.refs_0_.core_ref, bf16[768,1024]{1,0:T(8,128)(2,1)} %get-tuple-element.102.refs_1_, bf16[768,1024]{1,0:T(8,128)(2,1)} %get-tuple-element.103.refs_2_, bf16[1024,3072]{1,0:T(8,128)(2,1)} %get-tuple-element.104.refs_3_, ...), custom_call_target="tpu_custom_call" | custom-call | flops 9663676416 | bytes 20447232 | tf_op jit(solution)/shard_map/wgrad/pallas_call | solution.py:458
  349.1 1.8 copy.54
  351.5 7.0 %wgrad.6 = (bf16[2,4,2,2,24,384]{5,4,3,2,1,0:T(8,128)(2,1)}, bf16[2,4,2,2,24,384]{5,4,3,2,1,0:T(8,128)(2,1)}) custom-call(s32[1]{0:T(128)} %bitcast.1.refs_0_.core_ref, bf16[768,1024]{1,0:T(8,128)(2,1)} %get-tuple-element.119.refs_1_, bf16[768,1024]{1,0:T(8,128)(2,1)} %get-tuple-element.120.refs_2_, bf16[1024,768]{1,0:T(8,128)(2,1)} %get-tuple-element.121.refs_3_, ...), custom_call_target="tpu_custom_call" | custom-call | flops 2415919104 | bytes 7471104 | tf_op jit(solution)/shard_map/wgrad/pallas_call | solution.py:458
  358.5 1.9 copy.61
  360.5 12.7 %attend_back.6 = (bf16[3,1024,384]{2,1,0:T(8,128)(2,1)}, f32[2,1,384]{2,1,0:T(1,128)}, f32[2,1,384]{2,1,0:T(1,128)}) custom-call(s32[2]{0:T(128)} %refs_0_.15, bf16[1024,2304]{1,0:T(8,128)(2,1)} %get-tuple-element.77.refs_1_.refs_2_.refs_3_, bf16[1024,2304]{1,0:T(8,128)(2,1)} %get-tuple-element.77.refs_1_.refs_2_.refs_3_, ...), custom_call_target="tpu_custom_call" | custom-call | flops 8053063680 | bytes 5505024 | tf_op jit(solution)/shard_map/attend_back/pallas_call | solution.py:393
  373.2 8.8 %wgrad.5 = (bf16[2,4,2,3,24,384]{5,4,3,2,1,0:T(8,128)(2,1)}, bf16[2,4,2,3,24,384]{5,4,3,2,1,0:T(8,128)(2,1)}) custom-call(s32[1]{0:T(128)} %bitcast.1.refs_0_.core_ref, bf16[768,1024]{1,0:T(8,128)(2,1)} %get-tuple-element.115.refs_1_, bf16[768,1024]{1,0:T(8,128)(2,1)} %get-tuple-element.116.refs_2_, bf16[3,1024,384]{2,1,0:T(8,128)(2,1)} %get-tuple-element.93.e0_ref.refs_3_, ...), custom_call_target="tpu_custom_call" | custom-call | flops 3623878656 | bytes 9633792 | tf_op jit(solution)/shard_map/wgrad/pallas_call | solution.py:458
  382.0 2.2 copy.59
  384.7 14.7 %wgrad_back.1 = (bf16[2,4,2,4,24,768]{5,4,3,2,1,0:T(8,128)(2,1)}, bf16[2,4,2,4,24,768]{5,4,3,2,1,0:T(8,128)(2,1)}) custom-call(s32[1]{0:T(128)} %bitcast.1.refs_0_.core_ref, bf16[1024,3072]{1,0:T(8,128)(2,1)} %get-tuple-element.108.g2k.g2s, bf16[1024,3072]{1,0:T(8,128)(2,1)} %get-tuple-element.109.g1k.g1s, bf16[1024,3072]{1,0:T(8,128)(2,1)} %get-tuple-element.108.g2k.g2s, ...), custom_call_target="tpu_custom_call" | custom-call | flops 9663676416 | bytes 20447232 | tf_op jit(solution)/shard_map/wgrad_back/pallas_call | solution.py:494
  399.4 3.2 copy.56
  402.7 1.4 add_convert_fusion.8
  404.1 1.6 collective-permute-start.31
  407.8 5.7 %collective-permute-done.31 = bf16[2,4,2,24,384]{4,3,2,1,0:T(8,128)(2,1)S(1)} collective-permute-done((bf16[2,4,2,24,384]{4,3,2,1,0:T(8,128)(2,1)S(1)}, bf16[2,4,2,24,384]{4,3,2,1,0:T(8,128)(2,1)S(1)}, u32[]{:S(2)}, u32[]{:S(2)}) %collective-permute-start.31) | collective-permute-done | bytes 294944 | tf_op jit(solution)/shard_map/ppermute | solution.py:540
  415.1 5.2 collective-permute-done.30
  420.9 1.6 collective-permute-done.33
  422.6 3.7 collective-permute-done.32
  427.1 2.2 collective-permute-start.34
  429.3 2.9 collective-permute-start.36
  432.3 2.3 add_convert_fusion.1
  436.7 2.3 add_convert_fusion
  440.1 12.5 %attend_back.7 = (bf16[3,1024,384]{2,1,0:T(8,128)(2,1)}, f32[2,1,384]{2,1,0:T(1,128)}, f32[2,1,384]{2,1,0:T(1,128)}) custom-call(s32[2]{0:T(128)} %refs_0_.15, bf16[1024,2304]{1,0:T(8,128)(2,1)} %get-tuple-element.77.refs_1_.refs_2_.refs_3_, bf16[1024,2304]{1,0:T(8,128)(2,1)} %get-tuple-element.77.refs_1_.refs_2_.refs_3_, ...), custom_call_target="tpu_custom_call" | custom-call | flops 8053063680 | bytes 5505024 | tf_op jit(solution)/shard_map/attend_back/pallas_call | solution.py:393
  453.6 1.5 collective-permute-done.29
  456.9 9.7 %collective-permute-done.39 = bf16[2,4,1,24,384]{4,3,1,2,0:T(8,128)(2,1)S(1)} collective-permute-done((bf16[2,4,1,24,384]{4,3,1,2,0:T(8,128)(2,1)S(1)}, bf16[2,4,1,24,384]{4,3,1,2,0:T(8,128)(2,1)S(1)}, u32[]{:S(2)}, u32[]{:S(2)}) %collective-permute-start.39) | collective-permute-done | bytes 147488 | tf_op jit(solution)/shard_map/ppermute | solution.py:540
  469.9 8.8 %wgrad.7 = (bf16[2,4,2,3,24,384]{5,4,3,2,1,0:T(8,128)(2,1)}, bf16[2,4,2,3,24,384]{5,4,3,2,1,0:T(8,128)(2,1)}) custom-call(s32[1]{0:T(128)} %bitcast.1.refs_0_.core_ref, bf16[768,1024]{1,0:T(8,128)(2,1)} %get-tuple-element.115.refs_1_, bf16[768,1024]{1,0:T(8,128)(2,1)} %get-tuple-element.116.refs_2_, bf16[3,1024,384]{2,1,0:T(8,128)(2,1)} %get-tuple-element.94.e1_ref.refs_3_, ...), custom_call_target="tpu_custom_call" | custom-call | flops 3623878656 | bytes 9633792 | tf_op jit(solution)/shard_map/wgrad/pallas_call | solution.py:458
  484.3 2.0 collective-permute-start.47
  486.3 1.8 collective-permute-start.48
  488.9 9.2 %dx.3 = bf16[1024,768]{1,0:T(8,128)(2,1)} custom-call(f32[1024,768]{1,0:T(8,128)} %get-tuple-element.98.dz1_ref, bf16[3,1024,384]{2,1,0:T(8,128)(2,1)} %get-tuple-element.101.refs_4_.e0_ref, bf16[3,1024,384]{2,1,0:T(8,128)(2,1)} %get-tuple-element.114.refs_4_.e1_ref, bf16[5,768,768]{2,1,0:T(8,128)(2,1)} %bitcast.239, ...), custom_call_target="tpu_custom_call" | custom-call | flops 3623878656 | bytes 14548992 | tf_op jit(solution)/shard_map/dx/pallas_call | solution.py:428
  499.6 8.2 %collective-permute-done.47 = bf16[8,24,768]{2,1,0:T(8,128)(2,1)S(1)} collective-permute-done((bf16[8,24,768]{2,1,0:T(8,128)(2,1)S(1)}, bf16[8,24,768]{2,1,0:T(8,128)(2,1)S(1)}, u32[]{:S(2)}, u32[]{:S(2)}) %collective-permute-start.47) | collective-permute-done | bytes 294944 | tf_op jit(solution)/shard_map/ppermute | solution.py:540
  508.1 6.2 %collective-permute-start.41 = (bf16[4,24,384]{2,1,0:T(8,128)(2,1)S(1)}, bf16[4,24,384]{2,1,0:T(8,128)(2,1)S(1)}, u32[]{:S(2)}, u32[]{:S(2)}) collective-permute-start(bf16[4,24,384]{2,1,0:T(8,128)(2,1)S(1)} %get-tuple-element.165), channel_id=1, source_target_pairs={{0,2},{1,3},{2,4},{3,5},{4,6},{5,7},{6,0},{7,1},{8,10},{9,11},{10,... | collective-permute-start | bytes 221192 | tf_op jit(solution)/shard_map/ppermute | solution.py:540
  514.9 1.9 collective-permute-start.43
  518.2 2.4 collective-permute-done.42
  (219 shorter events, 48.4 us)
Async XLA Ops:
  10.2 49.3 %collective-permute-start.11 = (bf16[8,24,768]{2,1,0:T(8,128)(2,1)S(1)}, bf16[8,24,768]{2,1,0:T(8,128)(2,1)S(1)}, u32[]{:S(2)}, u32[]{:S(2)}) collective-permute-start(bf16[8,24,768]{2,1,0:T(8,128)(2,1)S(1)} %get-tuple-element.79), channel_id=1, source_target_pairs={{0,2},{1,3},{2,4},{3,5},{4,6},{5,7},{6,0},{7,1},{8,10},{9,11},{10,... | collective-permute-start | bytes 884744 | tf_op jit(solution)/shard_map/ppermute | solution.py:540
  13.2 46.3 %collective-permute-start.12 = (bf16[8,24,768]{2,1,0:T(8,128)(2,1)S(1)}, bf16[8,24,768]{2,1,0:T(8,128)(2,1)S(1)}, u32[]{:S(2)}, u32[]{:S(2)}) collective-permute-start(bf16[8,24,768]{2,1,0:T(8,128)(2,1)S(1)} %get-tuple-element.79), channel_id=1, source_target_pairs={{0,4},{1,5},{2,6},{3,7},{4,0},{5,1},{6,2},{7,3},{8,12},{9,13},{10,... | collective-permute-start | bytes 884744 | tf_op jit(solution)/shard_map/ppermute | solution.py:540
  15.8 43.7 %collective-permute-start.13 = (bf16[8,24,768]{2,1,0:T(8,128)(2,1)S(1)}, bf16[8,24,768]{2,1,0:T(8,128)(2,1)S(1)}, u32[]{:S(2)}, u32[]{:S(2)}) collective-permute-start(bf16[8,24,768]{2,1,0:T(8,128)(2,1)S(1)} %get-tuple-element.79), channel_id=1, source_target_pairs={{0,6},{1,7},{2,0},{3,1},{4,2},{5,3},{6,4},{7,5},{8,14},{9,15},{10,... | collective-permute-start | bytes 884744 | tf_op jit(solution)/shard_map/ppermute | solution.py:540
  17.2 21.7 %collective-permute-start.2 = (bf16[5,24,768]{2,1,0:T(8,128)(2,1)S(1)}, bf16[5,24,768]{2,1,0:T(8,128)(2,1)S(1)}, u32[]{:S(2)}, u32[]{:S(2)}) collective-permute-start(bf16[5,24,768]{2,1,0:T(8,128)(2,1)S(1)} %get-tuple-element.76), channel_id=1, source_target_pairs={{0,6},{1,7},{2,0},{3,1},{4,2},{5,3},{6,4},{7,5},{8,14},{9,15},{10,... | collective-permute-start | bytes 552968 | tf_op jit(solution)/shard_map/ppermute | solution.py:540
  17.6 39.5 %collective-permute-start.1 = (bf16[5,24,768]{2,1,0:T(8,128)(2,1)S(1)}, bf16[5,24,768]{2,1,0:T(8,128)(2,1)S(1)}, u32[]{:S(2)}, u32[]{:S(2)}) collective-permute-start(bf16[5,24,768]{2,1,0:T(8,128)(2,1)S(1)} %get-tuple-element.76), channel_id=1, source_target_pairs={{0,4},{1,5},{2,6},{3,7},{4,0},{5,1},{6,2},{7,3},{8,12},{9,13},{10,... | collective-permute-start | bytes 552968 | tf_op jit(solution)/shard_map/ppermute | solution.py:540
  38.9 18.9 %collective-permute-start = (bf16[5,24,768]{2,1,0:T(8,128)(2,1)S(1)}, bf16[5,24,768]{2,1,0:T(8,128)(2,1)S(1)}, u32[]{:S(2)}, u32[]{:S(2)}) collective-permute-start(bf16[5,24,768]{2,1,0:T(8,128)(2,1)S(1)} %get-tuple-element.76), channel_id=1, source_target_pairs={{0,2},{1,3},{2,4},{3,5},{4,6},{5,7},{6,0},{7,1},{8,10},{9,11},{10,... | collective-permute-start | bytes 552968 | tf_op jit(solution)/shard_map/ppermute | solution.py:540
  57.9 13.2 %collective-permute-start.7 = (bf16[4,3,24,768]{3,2,1,0:T(8,128)(2,1)S(1)}, bf16[4,3,24,768]{3,2,1,0:T(8,128)(2,1)S(1)}, u32[]{:S(2)}, u32[]{:S(2)}) collective-permute-start(bf16[4,3,24,768]{3,2,1,0:T(8,128)(2,1)S(1)} %get-tuple-element.159), channel_id=1, source_target_pairs={{0,16},{1,17},{2,18},{3,19},{4,20},{5,21},{6,22},{7,23},{8,24},{9,... | collective-permute-start | bytes 1327112 | tf_op jit(solution)/shard_map/ppermute | solution.py:540
  59.7 23.3 %collective-permute-start.14 = (bf16[4,4,24,768]{3,2,1,0:T(8,128)(2,1)S(1)}, bf16[4,4,24,768]{3,2,1,0:T(8,128)(2,1)S(1)}, u32[]{:S(2)}, u32[]{:S(2)}) collective-permute-start(bf16[4,4,24,768]{3,2,1,0:T(8,128)(2,1)S(1)} %get-tuple-element.157), channel_id=1, source_target_pairs={{0,1},{1,0},{2,3},{3,2},{4,5},{5,4},{6,7},{7,6},{8,9},{9,8},{10,11... | collective-permute-start | bytes 1769480 | tf_op jit(solution)/shard_map/ppermute | solution.py:540
  61.4 23.3 %collective-permute-start.18 = (bf16[4,4,24,768]{3,2,1,0:T(8,128)(2,1)S(1)}, bf16[4,4,24,768]{3,2,1,0:T(8,128)(2,1)S(1)}, u32[]{:S(2)}, u32[]{:S(2)}) collective-permute-start(bf16[4,4,24,768]{3,2,1,0:T(8,128)(2,1)S(1)} %get-tuple-element.155), channel_id=1, source_target_pairs={{0,16},{1,17},{2,18},{3,19},{4,20},{5,21},{6,22},{7,23},{8,24},{9,... | collective-permute-start | bytes 1769480 | tf_op jit(solution)/shard_map/ppermute | solution.py:540
  62.1 20.3 %collective-permute-start.3 = (bf16[4,2,24,768]{3,2,1,0:T(8,128)(2,1)S(1)}, bf16[4,2,24,768]{3,2,1,0:T(8,128)(2,1)S(1)}, u32[]{:S(2)}, u32[]{:S(2)}) collective-permute-start(bf16[4,2,24,768]{3,2,1,0:T(8,128)(2,1)S(1)} %get-tuple-element.177), channel_id=1, source_target_pairs={{0,1},{1,0},{2,3},{3,2},{4,5},{5,4},{6,7},{7,6},{8,9},{9,8},{10,11... | collective-permute-start | bytes 884744 | tf_op jit(solution)/shard_map/ppermute | solution.py:540
  71.2 27.7 %copy-start.1 = (bf16[2,4,3,24,768]{4,3,2,1,0:T(8,128)(2,1)}, bf16[2,4,3,24,768]{4,3,2,1,0:T(8,128)(2,1)S(1)}, u32[]{:S(2)}) copy-start(bf16[2,4,3,24,768]{4,3,2,1,0:T(8,128)(2,1)S(1)} %pad_maximum_fusion.2.refs_5_) | copy-start | bytes 2654212
  71.2 30.3 %collective-permute-start.9 = (bf16[2,4,3,24,768]{4,3,2,1,0:T(8,128)(2,1)S(1)}, bf16[2,4,3,24,768]{4,3,2,1,0:T(8,128)(2,1)}, u32[]{:S(2)}, u32[]{:S(2)}) collective-permute-start(bf16[2,4,3,24,768]{4,3,2,1,0:T(8,128)(2,1)S(1)} %pad_maximum_fusion.2.refs_5_), channel_id=1, source_target_pairs={{0,1},{1,0},{2,3},{3,2},{4,5},{5,4},{6,7},{7,6},{8,9},{9,8},{10,11... | collective-permute-start | bytes 2654216 | tf_op jit(solution)/shard_map/ppermute | solution.py:540
  82.4 16.4 %collective-permute-start.5 = (bf16[2,4,2,24,768]{4,3,2,1,0:T(8,128)(2,1)S(1)}, bf16[2,4,2,24,768]{4,3,2,1,0:T(8,128)(2,1)}, u32[]{:S(2)}, u32[]{:S(2)}) collective-permute-start(bf16[2,4,2,24,768]{4,3,2,1,0:T(8,128)(2,1)S(1)} %pad_maximum_fusion.3.refs_1_), channel_id=1, source_target_pairs={{0,16},{1,17},{2,18},{3,19},{4,20},{5,21},{6,22},{7,23},{8,24},{9,... | collective-permute-start | bytes 1769480 | tf_op jit(solution)/shard_map/ppermute | solution.py:540
  83.0 18.4 %collective-permute-start.4 = (bf16[2,4,2,24,768]{4,3,2,1,0:T(8,128)(2,1)S(1)}, bf16[2,4,2,24,768]{4,3,2,1,0:T(8,128)(2,1)S(1)}, u32[]{:S(2)}, u32[]{:S(2)}) collective-permute-start(bf16[2,4,2,24,768]{4,3,2,1,0:T(8,128)(2,1)S(1)} %pad_maximum_fusion.3.refs_1_), channel_id=1, source_target_pairs={{0,8},{1,9},{2,10},{3,11},{4,12},{5,13},{6,14},{7,15},{8,0},{9,1},... | collective-permute-start | bytes 1769480 | tf_op jit(solution)/shard_map/ppermute | solution.py:540
  83.2 36.9 %collective-permute-start.16 = (bf16[2,4,4,24,768]{4,3,2,1,0:T(8,128)(2,1)S(1)}, bf16[2,4,4,24,768]{4,3,2,1,0:T(8,128)(2,1)}, u32[]{:S(2)}, u32[]{:S(2)}) collective-permute-start(bf16[2,4,4,24,768]{4,3,2,1,0:T(8,128)(2,1)S(1)} %pad_maximum_fusion.refs_1_), channel_id=1, source_target_pairs={{0,16},{1,17},{2,18},{3,19},{4,20},{5,21},{6,22},{7,23},{8,24},{9,... | collective-permute-start | bytes 3538952 | tf_op jit(solution)/shard_map/ppermute | solution.py:540
  84.8 39.9 %collective-permute-start.20 = (bf16[2,4,4,24,768]{4,3,2,1,0:T(8,128)(2,1)S(1)}, bf16[2,4,4,24,768]{4,3,2,1,0:T(8,128)(2,1)}, u32[]{:S(2)}, u32[]{:S(2)}) collective-permute-start(bf16[2,4,4,24,768]{4,3,2,1,0:T(8,128)(2,1)S(1)} %pad_maximum_fusion.1.refs_5_), channel_id=1, source_target_pairs={{0,1},{1,0},{2,3},{3,2},{4,5},{5,4},{6,7},{7,6},{8,9},{9,8},{10,11... | collective-permute-start | bytes 3538952 | tf_op jit(solution)/shard_map/ppermute | solution.py:540
  98.9 3.9 collective-permute-start.8
  101.4 23.4 %collective-permute-start.10 = (bf16[2,4,3,24,768]{4,3,2,1,0:T(8,128)(2,1)}, bf16[2,4,3,24,768]{4,3,2,1,0:T(8,128)(2,1)}, u32[]{:S(2)}, u32[]{:S(2)}) collective-permute-start(bf16[2,4,3,24,768]{4,3,2,1,0:T(8,128)(2,1)} %collective-permute-done.9.refs_7_), channel_id=1, source_target_pairs={{0,8},{1,9},{2,10},{3,11},{4,12},{5,13},{6,14},{7,15},{8,0},{9,1},... | collective-permute-start | bytes 2654216 | tf_op jit(solution)/shard_map/ppermute | solution.py:540
  102.3 3.2 collective-permute-start.6
  102.8 53.2 %collective-permute-start.15 = (bf16[2,4,4,24,768]{4,3,2,1,0:T(8,128)(2,1)S(1)}, bf16[2,4,4,24,768]{4,3,2,1,0:T(8,128)(2,1)}, u32[]{:S(2)}, u32[]{:S(2)}) collective-permute-start(bf16[2,4,4,24,768]{4,3,2,1,0:T(8,128)(2,1)S(1)} %pad_maximum_fusion.refs_1_), channel_id=1, source_target_pairs={{0,8},{1,9},{2,10},{3,11},{4,12},{5,13},{6,14},{7,15},{8,0},{9,1},... | collective-permute-start | bytes 3538952 | tf_op jit(solution)/shard_map/ppermute | solution.py:540
  105.6 50.5 %collective-permute-start.19 = (bf16[2,4,4,24,768]{4,3,2,1,0:T(8,128)(2,1)S(1)}, bf16[2,4,4,24,768]{4,3,2,1,0:T(8,128)(2,1)}, u32[]{:S(2)}, u32[]{:S(2)}) collective-permute-start(bf16[2,4,4,24,768]{4,3,2,1,0:T(8,128)(2,1)S(1)} %pad_maximum_fusion.1.refs_5_), channel_id=1, source_target_pairs={{0,8},{1,9},{2,10},{3,11},{4,12},{5,13},{6,14},{7,15},{8,0},{9,1},... | collective-permute-start | bytes 3538952 | tf_op jit(solution)/shard_map/ppermute | solution.py:540
  120.1 36.0 %collective-permute-start.17 = (bf16[2,4,4,24,768]{4,3,2,1,0:T(8,128)(2,1)}, bf16[2,4,4,24,768]{4,3,2,1,0:T(8,128)(2,1)}, u32[]{:S(2)}, u32[]{:S(2)}) collective-permute-start(bf16[2,4,4,24,768]{4,3,2,1,0:T(8,128)(2,1)} %collective-permute-done.16.refs_3_), channel_id=1, source_target_pairs={{0,8},{1,9},{2,10},{3,11},{4,12},{5,13},{6,14},{7,15},{8,0},{9,1},... | collective-permute-start | bytes 3538952 | tf_op jit(solution)/shard_map/ppermute | solution.py:540
  124.7 31.3 %collective-permute-start.21 = (bf16[2,4,4,24,768]{4,3,2,1,0:T(8,128)(2,1)}, bf16[2,4,4,24,768]{4,3,2,1,0:T(8,128)(2,1)}, u32[]{:S(2)}, u32[]{:S(2)}) collective-permute-start(bf16[2,4,4,24,768]{4,3,2,1,0:T(8,128)(2,1)} %collective-permute-done.20.refs_7_), channel_id=1, source_target_pairs={{0,8},{1,9},{2,10},{3,11},{4,12},{5,13},{6,14},{7,15},{8,0},{9,1},... | collective-permute-start | bytes 3538952 | tf_op jit(solution)/shard_map/ppermute | solution.py:540
  132.4 2.6 copy-start
  350.9 81.3 %collective-permute-start.22 = (bf16[2,4,2,4,24,768]{5,4,3,1,2,0:T(8,128)(2,1)S(1)}, bf16[2,4,2,4,24,768]{5,4,3,1,2,0:T(8,128)(2,1)}, u32[]{:S(2)}, u32[]{:S(2)}) collective-permute-start(bf16[2,4,2,4,24,768]{5,4,3,1,2,0:T(8,128)(2,1)S(1)} %copy.54), channel_id=1, source_target_pairs={{0,8},{1,9},{2,10},{3,11},{4,12},{5,13},{6,14},{7,15},{8,0},{9,1},... | collective-permute-start | bytes 7077896 | tf_op jit(solution)/shard_map/ppermute | solution.py:540
  360.4 42.2 %collective-permute-start.25 = (bf16[2,4,2,2,24,384]{5,4,3,1,2,0:T(8,128)(2,1)}, bf16[2,4,2,2,24,384]{5,4,3,1,2,0:T(8,128)(2,1)}, u32[]{:S(2)}, u32[]{:S(2)}) collective-permute-start(bf16[2,4,2,2,24,384]{5,4,3,1,2,0:T(8,128)(2,1)} %copy.61), channel_id=1, source_target_pairs={{0,8},{1,9},{2,10},{3,11},{4,12},{5,13},{6,14},{7,15},{8,0},{9,1},... | collective-permute-start | bytes 1769480 | tf_op jit(solution)/shard_map/ppermute | solution.py:540
  384.2 21.6 %collective-permute-start.24 = (bf16[2,4,2,3,24,384]{5,4,3,1,2,0:T(8,128)(2,1)}, bf16[2,4,2,3,24,384]{5,4,3,1,2,0:T(8,128)(2,1)}, u32[]{:S(2)}, u32[]{:S(2)}) collective-permute-start(bf16[2,4,2,3,24,384]{5,4,3,1,2,0:T(8,128)(2,1)} %copy.59), channel_id=1, source_target_pairs={{0,8},{1,9},{2,10},{3,11},{4,12},{5,13},{6,14},{7,15},{8,0},{9,1},... | collective-permute-start | bytes 2654216 | tf_op jit(solution)/shard_map/ppermute | solution.py:540
  402.6 3.2 copy-start.26
  402.6 33.7 %collective-permute-start.23 = (bf16[2,4,2,4,24,768]{5,4,3,1,2,0:T(8,128)(2,1)}, bf16[2,4,2,4,24,768]{5,4,3,1,2,0:T(8,128)(2,1)}, u32[]{:S(2)}, u32[]{:S(2)}) collective-permute-start(bf16[2,4,2,4,24,768]{5,4,3,1,2,0:T(8,128)(2,1)} %copy.56), channel_id=1, source_target_pairs={{0,8},{1,9},{2,10},{3,11},{4,12},{5,13},{6,14},{7,15},{8,0},{9,1},... | collective-permute-start | bytes 7077896 | tf_op jit(solution)/shard_map/ppermute | solution.py:540
  404.1 9.5 %copy-start.31 = (bf16[2,4,2,24,384]{4,3,2,1,0:T(8,128)(2,1)}, bf16[2,4,2,24,384]{4,3,2,1,0:T(8,128)(2,1)S(1)}, u32[]{:S(2)}) copy-start(bf16[2,4,2,24,384]{4,3,2,1,0:T(8,128)(2,1)S(1)} %get-tuple-element.151.refs_6_) | copy-start | bytes 884740
  404.1 3.7 copy-start.34
  404.1 3.6 copy-start.35
  404.1 9.4 %collective-permute-start.31 = (bf16[2,4,2,24,384]{4,3,2,1,0:T(8,128)(2,1)S(1)}, bf16[2,4,2,24,384]{4,3,2,1,0:T(8,128)(2,1)S(1)}, u32[]{:S(2)}, u32[]{:S(2)}) collective-permute-start(bf16[2,4,2,24,384]{4,3,2,1,0:T(8,128)(2,1)S(1)} %get-tuple-element.151.refs_6_), channel_id=1, source_target_pairs={{0,1},{1,0},{2,3},{3,2},{4,5},{5,4},{6,7},{7,6},{8,9},{9,8},{10,11... | collective-permute-start | bytes 884744 | tf_op jit(solution)/shard_map/ppermute | solution.py:540
  405.8 8.4 %copy-start.38 = (f32[2,1,384]{2,1,0:T(1,128)S(1)}, f32[2,1,384]{2,1,0:T(1,128)}, u32[]{:S(2)}) copy-start(f32[2,1,384]{2,1,0:T(1,128)} %get-tuple-element.128) | copy-start | bytes 9220
  405.8 8.4 %copy-start.39 = (f32[2,1,384]{2,1,0:T(1,128)S(1)}, f32[2,1,384]{2,1,0:T(1,128)}, u32[]{:S(2)}) copy-start(f32[2,1,384]{2,1,0:T(1,128)} %get-tuple-element.132) | copy-start | bytes 9220
  405.8 8.4 %copy-start.40 = (f32[2,1,384]{2,1,0:T(1,128)S(1)}, f32[2,1,384]{2,1,0:T(1,128)}, u32[]{:S(2)}) copy-start(f32[2,1,384]{2,1,0:T(1,128)} %get-tuple-element.127) | copy-start | bytes 9220
  405.8 8.4 %copy-start.41 = (f32[2,1,384]{2,1,0:T(1,128)S(1)}, f32[2,1,384]{2,1,0:T(1,128)}, u32[]{:S(2)}) copy-start(f32[2,1,384]{2,1,0:T(1,128)} %get-tuple-element.131) | copy-start | bytes 9220
  407.2 13.1 %collective-permute-start.30 = (bf16[4,2,3,24,384]{4,3,2,0,1:T(8,128)(2,1)S(1)}, bf16[4,2,3,24,384]{4,3,2,0,1:T(8,128)(2,1)S(1)}, u32[]{:S(2)}, u32[]{:S(2)}) collective-permute-start(bf16[4,2,3,24,384]{4,3,2,0,1:T(8,128)(2,1)S(1)} %get-tuple-element.146), channel_id=1, source_target_pairs={{0,16},{1,17},{2,18},{3,19},{4,20},{5,21},{6,22},{7,23},{8,24},{9,... | collective-permute-start | bytes 1327112 | tf_op jit(solution)/shard_map/ppermute | solution.py:540
  413.6 13.6 %copy-start.28 = (bf16[4,2,24,384]{3,2,1,0:T(8,128)(2,1)}, bf16[4,2,24,384]{3,2,1,0:T(8,128)(2,1)S(1)}, u32[]{:S(2)}) copy-start(bf16[4,2,24,384]{3,2,1,0:T(8,128)(2,1)S(1)} %fusion.42.rest_3_) | copy-start | bytes 442372
  413.6 9.0 %collective-permute-start.33 = (bf16[4,2,24,384]{3,2,1,0:T(8,128)(2,1)S(1)}, bf16[4,2,24,384]{3,2,1,0:T(8,128)(2,1)S(1)}, u32[]{:S(2)}, u32[]{:S(2)}) collective-permute-start(bf16[4,2,24,384]{3,2,1,0:T(8,128)(2,1)S(1)} %fusion.42.rest_3_), channel_id=1, source_target_pairs={{0,16},{1,17},{2,18},{3,19},{4,20},{5,21},{6,22},{7,23},{8,24},{9,... | collective-permute-start | bytes 442376 | tf_op jit(solution)/shard_map/ppermute | solution.py:540
  415.1 17.2 %copy-start.22 = (bf16[2,4,2,4,24,768]{5,4,3,2,1,0:T(8,128)(2,1)S(1)}, bf16[2,4,2,4,24,768]{5,4,3,2,1,0:T(8,128)(2,1)}, u32[]{:S(2)}) copy-start(bf16[2,4,2,4,24,768]{5,4,3,2,1,0:T(8,128)(2,1)} %get-tuple-element.106) | copy-start | bytes 7077892
  420.3 14.3 %copy-start.25 = (bf16[4,3,24,384]{3,2,1,0:T(8,128)(2,1)}, bf16[4,3,24,384]{3,2,1,0:T(8,128)(2,1)S(1)}, u32[]{:S(2)}) copy-start(bf16[4,3,24,384]{3,2,1,0:T(8,128)(2,1)S(1)} %fusion.36.rest_2_) | copy-start | bytes 663556
  420.3 6.0 %collective-permute-start.32 = (bf16[4,3,24,384]{3,2,1,0:T(8,128)(2,1)S(1)}, bf16[4,3,24,384]{3,2,1,0:T(8,128)(2,1)S(1)}, u32[]{:S(2)}, u32[]{:S(2)}) collective-permute-start(bf16[4,3,24,384]{3,2,1,0:T(8,128)(2,1)S(1)} %fusion.36.rest_2_), channel_id=1, source_target_pairs={{0,1},{1,0},{2,3},{3,2},{4,5},{5,4},{6,7},{7,6},{8,9},{9,8},{10,11... | collective-permute-start | bytes 663560 | tf_op jit(solution)/shard_map/ppermute | solution.py:540
  427.1 26.3 %collective-permute-start.34 = (bf16[5,24,384]{2,1,0:T(8,128)(2,1)}, bf16[5,24,384]{2,1,0:T(8,128)(2,1)S(1)}, u32[]{:S(2)}, u32[]{:S(2)}) collective-permute-start(bf16[5,24,384]{2,1,0:T(8,128)(2,1)} %get-tuple-element.160), channel_id=1, source_target_pairs={{0,2},{1,3},{2,4},{3,5},{4,6},{5,7},{6,0},{7,1},{8,10},{9,11},{10,... | collective-permute-start | bytes 276488 | tf_op jit(solution)/shard_map/ppermute | solution.py:540
  429.3 24.2 %collective-permute-start.35 = (bf16[5,24,384]{2,1,0:T(8,128)(2,1)S(1)}, bf16[5,24,384]{2,1,0:T(8,128)(2,1)S(1)}, u32[]{:S(2)}, u32[]{:S(2)}) collective-permute-start(bf16[5,24,384]{2,1,0:T(8,128)(2,1)S(1)} %get-tuple-element.161), channel_id=1, source_target_pairs={{0,4},{1,5},{2,6},{3,7},{4,0},{5,1},{6,2},{7,3},{8,12},{9,13},{10,... | collective-permute-start | bytes 276488 | tf_op jit(solution)/shard_map/ppermute | solution.py:540
  429.3 24.2 %collective-permute-start.36 = (bf16[5,24,384]{2,1,0:T(8,128)(2,1)S(1)}, bf16[5,24,384]{2,1,0:T(8,128)(2,1)S(1)}, u32[]{:S(2)}, u32[]{:S(2)}) collective-permute-start(bf16[5,24,384]{2,1,0:T(8,128)(2,1)S(1)} %get-tuple-element.162), channel_id=1, source_target_pairs={{0,6},{1,7},{2,0},{3,1},{4,2},{5,3},{6,4},{7,5},{8,14},{9,15},{10,... | collective-permute-start | bytes 276488 | tf_op jit(solution)/shard_map/ppermute | solution.py:540
  435.7 33.2 %collective-permute-start.26 = (bf16[4,2,4,24,768]{4,3,2,0,1:T(8,128)(2,1)S(1)}, bf16[4,2,4,24,768]{4,3,2,0,1:T(8,128)(2,1)S(1)}, u32[]{:S(2)}, u32[]{:S(2)}) collective-permute-start(bf16[4,2,4,24,768]{4,3,2,0,1:T(8,128)(2,1)S(1)} %get-tuple-element.142), channel_id=1, source_target_pairs={{0,16},{1,17},{2,18},{3,19},{4,20},{5,21},{6,22},{7,23},{8,24},{9,... | collective-permute-start | bytes 3538952 | tf_op jit(solution)/shard_map/ppermute | solution.py:540
  439.1 13.5 %copy-start.36 = (f32[2,1,384]{2,1,0:T(1,128)S(1)}, f32[2,1,384]{2,1,0:T(1,128)}, u32[]{:S(2)}) copy-start(f32[2,1,384]{2,1,0:T(1,128)} %get-tuple-element.130) | copy-start | bytes 9220
  439.1 13.5 %copy-start.37 = (f32[2,1,384]{2,1,0:T(1,128)S(1)}, f32[2,1,384]{2,1,0:T(1,128)}, u32[]{:S(2)}) copy-start(f32[2,1,384]{2,1,0:T(1,128)} %get-tuple-element.134) | copy-start | bytes 9220
  439.1 28.3 %collective-permute-start.27 = (bf16[2,4,4,24,768]{4,3,2,1,0:T(8,128)(2,1)S(1)}, bf16[2,4,4,24,768]{4,3,2,1,0:T(8,128)(2,1)S(1)}, u32[]{:S(2)}, u32[]{:S(2)}) collective-permute-start(bf16[2,4,4,24,768]{4,3,2,1,0:T(8,128)(2,1)S(1)} %get-tuple-element.140.refs_7_), channel_id=1, source_target_pairs={{0,1},{1,0},{2,3},{3,2},{4,5},{5,4},{6,7},{7,6},{8,9},{9,8},{10,11... | collective-permute-start | bytes 3538952 | tf_op jit(solution)/shard_map/ppermute | solution.py:540
  453.4 1.6 collective-permute-start.29
  455.8 10.8 %collective-permute-start.39 = (bf16[2,4,1,24,384]{4,3,1,2,0:T(8,128)(2,1)S(1)}, bf16[2,4,1,24,384]{4,3,1,2,0:T(8,128)(2,1)S(1)}, u32[]{:S(2)}, u32[]{:S(2)}) collective-permute-start(bf16[2,4,1,24,384]{4,3,1,2,0:T(8,128)(2,1)S(1)} %get-tuple-element.163), channel_id=1, source_target_pairs={{0,1},{1,0},{2,3},{3,2},{4,5},{5,4},{6,7},{7,6},{8,9},{9,8},{10,11... | collective-permute-start | bytes 442376 | tf_op jit(solution)/shard_map/ppermute | solution.py:540
  466.6 14.2 %collective-permute-start.40 = (bf16[4,1,24,384]{3,2,1,0:T(8,128)(2,1)S(1)}, bf16[4,1,24,384]{3,2,1,0:T(8,128)(2,1)}, u32[]{:S(2)}, u32[]{:S(2)}) collective-permute-start(bf16[4,1,24,384]{3,2,1,0:T(8,128)(2,1)S(1)} %fusion.58), channel_id=1, source_target_pairs={{0,16},{1,17},{2,18},{3,19},{4,20},{5,21},{6,22},{7,23},{8,24},{9,... | collective-permute-start | bytes 221192 | tf_op jit(solution)/shard_map/ppermute | solution.py:540
  467.6 14.1 %collective-permute-start.45 = (bf16[4,4,24,768]{3,2,1,0:T(8,128)(2,1)S(1)}, bf16[4,4,24,768]{3,2,1,0:T(8,128)(2,1)S(1)}, u32[]{:S(2)}, u32[]{:S(2)}) collective-permute-start(bf16[4,4,24,768]{3,2,1,0:T(8,128)(2,1)S(1)} %fusion.9.refs_8_), channel_id=1, source_target_pairs={{0,16},{1,17},{2,18},{3,19},{4,20},{5,21},{6,22},{7,23},{8,24},{9,... | collective-permute-start | bytes 1769480 | tf_op jit(solution)/shard_map/ppermute | solution.py:540
  469.1 12.9 %collective-permute-start.44 = (bf16[4,4,24,768]{3,2,1,0:T(8,128)(2,1)S(1)}, bf16[4,4,24,768]{3,2,1,0:T(8,128)(2,1)S(1)}, u32[]{:S(2)}, u32[]{:S(2)}) collective-permute-start(bf16[4,4,24,768]{3,2,1,0:T(8,128)(2,1)S(1)} %fusion.8.refs_7_), channel_id=1, source_target_pairs={{0,1},{1,0},{2,3},{3,2},{4,5},{5,4},{6,7},{7,6},{8,9},{9,8},{10,11... | collective-permute-start | bytes 1769480 | tf_op jit(solution)/shard_map/ppermute | solution.py:540
  480.0 2.5 collective-permute-start.28
  483.3 14.8 %collective-permute-start.37 = (bf16[4,2,3,24,384]{4,3,2,0,1:T(8,128)(2,1)S(1)}, bf16[4,2,3,24,384]{4,3,2,0,1:T(8,128)(2,1)S(1)}, u32[]{:S(2)}, u32[]{:S(2)}) collective-permute-start(bf16[4,2,3,24,384]{4,3,2,0,1:T(8,128)(2,1)S(1)} %get-tuple-element.144), channel_id=1, source_target_pairs={{0,16},{1,17},{2,18},{3,19},{4,20},{5,21},{6,22},{7,23},{8,24},{9,... | collective-permute-start | bytes 1327112 | tf_op jit(solution)/shard_map/ppermute | solution.py:540
  484.2 15.3 %collective-permute-start.46 = (bf16[8,24,768]{2,1,0:T(8,128)(2,1)S(1)}, bf16[8,24,768]{2,1,0:T(8,128)(2,1)S(1)}, u32[]{:S(2)}, u32[]{:S(2)}) collective-permute-start(bf16[8,24,768]{2,1,0:T(8,128)(2,1)S(1)} %get-tuple-element.147), channel_id=1, source_target_pairs={{0,2},{1,3},{2,4},{3,5},{4,6},{5,7},{6,0},{7,1},{8,10},{9,11},{10,... | collective-permute-start | bytes 884744 | tf_op jit(solution)/shard_map/ppermute | solution.py:540
  484.3 23.5 %collective-permute-start.47 = (bf16[8,24,768]{2,1,0:T(8,128)(2,1)S(1)}, bf16[8,24,768]{2,1,0:T(8,128)(2,1)S(1)}, u32[]{:S(2)}, u32[]{:S(2)}) collective-permute-start(bf16[8,24,768]{2,1,0:T(8,128)(2,1)S(1)} %get-tuple-element.148), channel_id=1, source_target_pairs={{0,4},{1,5},{2,6},{3,7},{4,0},{5,1},{6,2},{7,3},{8,12},{9,13},{10,... | collective-permute-start | bytes 884744 | tf_op jit(solution)/shard_map/ppermute | solution.py:540
  486.3 21.5 %collective-permute-start.48 = (bf16[8,24,768]{2,1,0:T(8,128)(2,1)S(1)}, bf16[8,24,768]{2,1,0:T(8,128)(2,1)S(1)}, u32[]{:S(2)}, u32[]{:S(2)}) collective-permute-start(bf16[8,24,768]{2,1,0:T(8,128)(2,1)S(1)} %get-tuple-element.149), channel_id=1, source_target_pairs={{0,6},{1,7},{2,0},{3,1},{4,2},{5,3},{6,4},{7,5},{8,14},{9,15},{10,... | collective-permute-start | bytes 884744 | tf_op jit(solution)/shard_map/ppermute | solution.py:540
  498.2 9.7 %collective-permute-start.38 = (bf16[4,3,24,384]{3,2,1,0:T(8,128)(2,1)S(1)}, bf16[4,3,24,384]{3,2,1,0:T(8,128)(2,1)S(1)}, u32[]{:S(2)}, u32[]{:S(2)}) collective-permute-start(bf16[4,3,24,384]{3,2,1,0:T(8,128)(2,1)S(1)} %fusion.39), channel_id=1, source_target_pairs={{0,1},{1,0},{2,3},{3,2},{4,5},{5,4},{6,7},{7,6},{8,9},{9,8},{10,11... | collective-permute-start | bytes 663560 | tf_op jit(solution)/shard_map/ppermute | solution.py:540
  508.1 10.1 %collective-permute-start.41 = (bf16[4,24,384]{2,1,0:T(8,128)(2,1)S(1)}, bf16[4,24,384]{2,1,0:T(8,128)(2,1)S(1)}, u32[]{:S(2)}, u32[]{:S(2)}) collective-permute-start(bf16[4,24,384]{2,1,0:T(8,128)(2,1)S(1)} %get-tuple-element.165), channel_id=1, source_target_pairs={{0,2},{1,3},{2,4},{3,5},{4,6},{5,7},{6,0},{7,1},{8,10},{9,11},{10,... | collective-permute-start | bytes 221192 | tf_op jit(solution)/shard_map/ppermute | solution.py:540
  514.3 6.3 %collective-permute-start.42 = (bf16[4,24,384]{2,1,0:T(8,128)(2,1)S(1)}, bf16[4,24,384]{2,1,0:T(8,128)(2,1)S(1)}, u32[]{:S(2)}, u32[]{:S(2)}) collective-permute-start(bf16[4,24,384]{2,1,0:T(8,128)(2,1)S(1)} %get-tuple-element.166), channel_id=1, source_target_pairs={{0,4},{1,5},{2,6},{3,7},{4,0},{5,1},{6,2},{7,3},{8,12},{9,13},{10,... | collective-permute-start | bytes 221192 | tf_op jit(solution)/shard_map/ppermute | solution.py:540
  514.9 5.8 %collective-permute-start.43 = (bf16[4,24,384]{2,1,0:T(8,128)(2,1)S(1)}, bf16[4,24,384]{2,1,0:T(8,128)(2,1)S(1)}, u32[]{:S(2)}, u32[]{:S(2)}) collective-permute-start(bf16[4,24,384]{2,1,0:T(8,128)(2,1)S(1)} %get-tuple-element.167), channel_id=1, source_target_pairs={{0,6},{1,7},{2,0},{3,1},{4,2},{5,3},{6,4},{7,5},{8,14},{9,15},{10,... | collective-permute-start | bytes 221192 | tf_op jit(solution)/shard_map/ppermute | solution.py:540
  (27 other events, 30.4 us)

commit v3 on v2

--- a/solution.py
+++ b/solution.py
@@ -50,13 +50,8 @@
     return jnp.sum(v, axis=0, keepdims=True)
 
 
-def qkv_body(x_ref, w_ref, vec_ref, o_ref, xt_ref):
+def qkv_body(x_ref, w_ref, vec_ref, o_ref):
     part = pl.program_id(0)
-
-    @pl.when(part == 0)
-    def _():
-        xt_ref[...] = x_ref[...].T
-
     acc = mm(x_ref[...], w_ref[0], NN)
     bias = jnp.where(part == 0, vec_ref[BQ : BQ + 1, :], jnp.where(part == 2, vec_ref[BV : BV + 1, :], 0.0))
     o_ref[...] = (acc + bias).astype(BF)
@@ -72,10 +67,10 @@
             pl.BlockSpec((1, D, D), lambda i: (i, 0, 0)),
             once(vec.shape, lambda i: (0, 0)),
         ],
-        out_specs=[pl.BlockSpec((rows, D), lambda i: (0, i)), pl.BlockSpec((D, rows), lambda i: (0, 0))],
-        out_shape=[jax.ShapeDtypeStruct((rows, 3 * D), BF), jax.ShapeDtypeStruct((D, rows), BF)],
-        compiler_params=params(),
-        cost_estimate=cost(6 * rows * D * D, 2 * (rows * D * 5 + 3 * D * D)),
+        out_specs=pl.BlockSpec((rows, D), lambda i: (0, i)),
+        out_shape=jax.ShapeDtypeStruct((rows, 3 * D), BF),
+        compiler_params=params(),
+        cost_estimate=cost(6 * rows * D * D, 2 * (rows * D * 4 + 3 * D * D)),
         name="qkv",
     )(x, w, vec)
 
@@ -143,180 +138,173 @@
 
 def gelu_both(u):
     a = 0.7978845608028654
-    sq = u * u
-    t = jnp.tanh(u * (a + (a * 0.044715) * sq))
-    half = 0.5 + 0.5 * t
-    slope = half + (u * (0.5 - 0.5 * t * t)) * (a + (3 * a * 0.044715) * sq)
-    return u * half, slope
+    c = a + (a * 0.044715) * (u * u)
+    s = 0.5 + 0.5 * jnp.tanh(u * c)
+    g = u * s
+    return g, s + (g * (1.0 - s)) * (6.0 * c - 4.0 * a)
+
+
+ANY = pl.BlockSpec(memory_space=pl.ANY)
+
+
+def by_rows(block, width):
+    return pl.BlockSpec((block, width), lambda i: (i, 0))
 
 
 def ffn_body(
-    steps, x_ref, ctx_ref, wo_ref, vec_ref, wi_ref, wb_ref,
-    z1_ref, h1t_ref, ctxt_ref, g_ref, gp_ref, z2_ref, y_ref, yb_ref,
-    h1_s, h1b_s, acc_s,
+    renorm, x_ref, ctx_ref, vec_ref, wo_h, wi_h, wb_h,
+    z1_ref, h1_ref, g_ref, slope_ref, z2_ref, y_ref, wo_s, wi_s, wb_s, sems,
 ):
     step = pl.program_id(0)
+    copies = [
+        pltpu.make_async_copy(wo_h.at[3], wo_s, sems.at[0]),
+        pltpu.make_async_copy(wi_h, wi_s, sems.at[1]),
+        pltpu.make_async_copy(wb_h, wb_s, sems.at[2]),
+    ]
 
     @pl.when(step == 0)
     def _():
-        ctx = ctx_ref[...]
-        z1 = x_ref[...].astype(F32) + mm(ctx, wo_ref[0], NN) + vec_ref[BO : BO + 1, :]
-        z1_ref[...] = z1
-        n, _ = normed(z1)
-        h1 = n * vec_ref[G1 : G1 + 1, :] + vec_ref[S1 : S1 + 1, :]
-        h1_s[...] = h1
-        low = h1.astype(BF)
-        h1b_s[...] = low
-        h1t_ref[...] = low.T
-        ctxt_ref[...] = ctx.T
-
-    f = mm(h1b_s[...], wi_ref[0], NN) + vec_ref[pl.ds(8 + step, 1), :]
-    g, slope = gelu_both(f)
-    g = g.astype(BF)
-    g_ref[...] = g
-    gp_ref[...] = slope.astype(BF)
-    more = mm(g, wb_ref[...], NN)
+        for copy in copies:
+            copy.start()
+        copies[0].wait()
+
+    x = x_ref[...].astype(F32)
+    if renorm:
+        n, _ = normed(x)
+        x = n * vec_ref[G2 : G2 + 1, :] + vec_ref[S2 : S2 + 1, :]
+    z1 = x + mm(ctx_ref[...], wo_s[...], NN) + vec_ref[BO : BO + 1, :]
+    z1_ref[...] = z1
+    n, _ = normed(z1)
+    h1 = n * vec_ref[G1 : G1 + 1, :] + vec_ref[S1 : S1 + 1, :]
+    low = h1.astype(BF)
+    h1_ref[...] = low
 
     @pl.when(step == 0)
     def _():
-        acc_s[...] = more
-
-    @pl.when(step > 0)
-    def _():
-        acc_s[...] += more
-
-    @pl.when(step == steps - 1)
-    def _():
-        z2 = h1_s[...] + acc_s[...] + vec_ref[BB : BB + 1, :]
-        z2_ref[...] = z2
-        n, _ = normed(z2)
-        y = n * vec_ref[G2 : G2 + 1, :] + vec_ref[S2 : S2 + 1, :]
-        y_ref[...] = y
-        yb_ref[...] = y.astype(BF)
-
-
-def ffn_call(x, ctx, wo, vec, wi, wb):
+        copies[1].wait()
+        copies[2].wait()
+
+    units = wi_s.shape[0]
+
+    def up(j):
+        return mm(low, wi_s[j], NN) + vec_ref[8 + j : 9 + j, :]
+
+    acc = h1 + vec_ref[BB : BB + 1, :]
+    f = up(0)
+    for j in range(units):
+        ahead = up(j + 1) if j + 1 < units else None
+        cols = slice(j * D, (j + 1) * D)
+        g, slope = gelu_both(f)
+        g = g.astype(BF)
+        g_ref[:, cols] = g
+        slope_ref[:, cols] = slope.astype(BF)
+        acc += mm(g, wb_s[cols, :], NN)
+        f = ahead
+    z2_ref[...] = acc
+    n, _ = normed(acc)
+    y_ref[...] = (n * vec_ref[G2 : G2 + 1, :] + vec_ref[S2 : S2 + 1, :]).astype(BF)
+
+
+def weight_scratch(ff):
+    return [
+        pltpu.VMEM((D, D), BF),
+        pltpu.VMEM((ff // D, D, D), BF),
+        pltpu.VMEM((ff, D), BF),
+        pltpu.SemaphoreType.DMA((3,)),
+    ]
+
+
+def ffn_call(x, ctx, first, vec, wi, wb, renorm, block=512):
     rows = x.shape[0]
     ff = wb.shape[0]
-    chunk = D
-    steps = ff // chunk
-    full = once((rows, D), lambda i: (0, 0))
-    keep = once((rows, D), lambda i: (0, 0))
-    cols = pl.BlockSpec((rows, chunk), lambda i: (0, i))
-    flip = once((D, rows), lambda i: (0, 0))
-
-    def body(*refs):
-        ffn_body(steps, *refs)
-
-    return pl.pallas_call(
-        body,
-        grid=(steps,),
-        in_specs=[
-            full,
-            full,
-            once((1, D, D), lambda i: (3, 0, 0)),
-            once(vec.shape, lambda i: (0, 0)),
-            pl.BlockSpec((1, D, chunk), lambda i: (i, 0, 0)),
-            pl.BlockSpec((chunk, D), lambda i: (i, 0)),
-        ],
-        out_specs=[keep, flip, flip, cols, cols, keep, keep, keep],
+    line, wide = by_rows(block, D), by_rows(block, ff)
+    return pl.pallas_call(
+        lambda *refs: ffn_body(renorm, *refs),
+        grid=(rows // block,),
+        in_specs=[line, line, once(vec.shape, lambda i: (0, 0)), ANY, ANY, ANY],
+        out_specs=[line, line, wide, wide, line, line],
         out_shape=[
             jax.ShapeDtypeStruct((rows, D), F32),
-            jax.ShapeDtypeStruct((D, rows), BF),
-            jax.ShapeDtypeStruct((D, rows), BF),
+            jax.ShapeDtypeStruct((rows, D), BF),
             jax.ShapeDtypeStruct((rows, ff), BF),
             jax.ShapeDtypeStruct((rows, ff), BF),
             jax.ShapeDtypeStruct((rows, D), F32),
-            jax.ShapeDtypeStruct((rows, D), F32),
             jax.ShapeDtypeStruct((rows, D), BF),
         ],
-        scratch_shapes=[pltpu.VMEM((rows, D), F32), pltpu.VMEM((rows, D), BF), pltpu.VMEM((rows, D), F32)],
+        scratch_shapes=weight_scratch(ff),
         compiler_params=params(),
         cost_estimate=cost(2 * rows * D * (D + 2 * ff), 20 * rows * D + 4 * rows * ff + 4 * D * ff, rows * ff),
         name="ffn",
-    )(x, ctx, wo, vec, wi, wb)
+    )(x, ctx, vec, first, wi, wb)
 
 
 def ffn_back_body(
-    steps, dy_ref, z2_ref, z1_ref, gp_ref, wb_ref, wi_ref, wo_ref, vec_ref,
-    e2_ref, e1_ref, dz1_ref, ea_ref, dctx_ref, sums_ref,
-    dz2_s, acc_s,
+    dy_ref, z2_ref, z1_ref, slope_ref, vec_ref, wb_h, wi_h, wo_h,
+    e2_ref, e1_ref, dz1_ref, ea_ref, dctx_ref, sums_ref, wo_s, wi_s, wb_s, sems,
 ):
     step = pl.program_id(0)
+    copies = [
+        pltpu.make_async_copy(wb_h, wb_s, sems.at[0]),
+        pltpu.make_async_copy(wi_h, wi_s, sems.at[1]),
+        pltpu.make_async_copy(wo_h.at[3], wo_s, sems.at[2]),
+    ]
 
     @pl.when(step == 0)
     def _():
+        for copy in copies:
+            copy.start()
         sums_ref[...] = jnp.zeros_like(sums_ref)
-        dy = dy_ref[...].astype(F32)
-        n, root = normed(z2_ref[...])
-        sums_ref[G2 : G2 + 1, :] = colsum(dy * n)
-        sums_ref[S2 : S2 + 1, :] = colsum(dy)
-        dz2 = normed_back(n, root, dy * vec_ref[G2 : G2 + 1, :])
-        dz2_s[...] = dz2
-        low = dz2.astype(BF)
-        e2_ref[...] = low
-        sums_ref[BB : BB + 1, :] = colsum(low.astype(F32))
-
-    df = mm(e2_ref[...], wb_ref[...], NT) * gp_ref[...].astype(F32)
-    e1 = df.astype(BF)
-    e1_ref[...] = e1
-    sums_ref[pl.ds(8 + step, 1), :] = colsum(e1.astype(F32))
-    more = mm(e1, wi_ref[0], NT)
+
+    dy = dy_ref[...].astype(F32)
+    n, root = normed(z2_ref[...])
+    sums_ref[G2 : G2 + 1, :] += colsum(dy * n)
+    sums_ref[S2 : S2 + 1, :] += colsum(dy)
+    dz2 = normed_back(n, root, dy * vec_ref[G2 : G2 + 1, :])
+    e2 = dz2.astype(BF)
+    e2_ref[...] = e2
+    sums_ref[BB : BB + 1, :] += colsum(e2.astype(F32))
 
     @pl.when(step == 0)
     def _():
-        acc_s[...] = more
-
-    @pl.when(step > 0)
-    def _():
-        acc_s[...] += more
-
-    @pl.when(step == steps - 1)
-    def _():
-        dh1 = dz2_s[...] + acc_s[...]
-        n, root = normed(z1_ref[...])
-        sums_ref[G1 : G1 + 1, :] = colsum(dh1 * n)
-        sums_ref[S1 : S1 + 1, :] = colsum(dh1)
-        dz1 = normed_back(n, root, dh1 * vec_ref[G1 : G1 + 1, :])
-        dz1_ref[...] = dz1
-        low = dz1.astype(BF)
-        ea_ref[...] = low
-        sums_ref[BO : BO + 1, :] = colsum(low.astype(F32))
-        dctx_ref[...] = mm(low, wo_ref[0], NT).astype(BF)
-
-
-def ffn_back_call(dy, z2, z1, gp, wb, wi, wo, vec):
+        for copy in copies:
+            copy.wait()
+
+    units = wi_s.shape[0]
+
+    def up(j):
+        return mm(e2, wb_s[j * D : (j + 1) * D, :], NT)
+
+    acc = dz2
+    f = up(0)
+    for j in range(units):
+        ahead = up(j + 1) if j + 1 < units else None
+        cols = slice(j * D, (j + 1) * D)
+        e1 = (f * slope_ref[:, cols].astype(F32)).astype(BF)
+        e1_ref[:, cols] = e1
+        sums_ref[8 + j : 9 + j, :] += colsum(e1.astype(F32))
+        acc += mm(e1, wi_s[j], NT)
+        f = ahead
+    n, root = normed(z1_ref[...])
+    sums_ref[G1 : G1 + 1, :] += colsum(acc * n)
+    sums_ref[S1 : S1 + 1, :] += colsum(acc)
+    dz1 = normed_back(n, root, acc * vec_ref[G1 : G1 + 1, :])
+    dz1_ref[...] = dz1
+    ea = dz1.astype(BF)
+    ea_ref[...] = ea
+    sums_ref[BO : BO + 1, :] += colsum(ea.astype(F32))
+    dctx_ref[...] = mm(ea, wo_s[...], NT).astype(BF)
+
+
+def ffn_back_call(dy, z2, z1, slope, wb, wi, first, vec, block=256):
     rows = dy.shape[0]
     ff = wb.shape[0]
-    chunk = D
-    steps = ff // chunk
-    keep = once((rows, D), lambda i: (0, 0))
-    cols = pl.BlockSpec((rows, chunk), lambda i: (0, i))
-
-    def body(*refs):
-        ffn_back_body(steps, *refs)
-
-    return pl.pallas_call(
-        body,
-        grid=(steps,),
-        in_specs=[
-            keep,
-            keep,
-            keep,
-            cols,
-            pl.BlockSpec((chunk, D), lambda i: (i, 0)),
-            pl.BlockSpec((1, D, chunk), lambda i: (i, 0, 0)),
-            once((1, D, D), lambda i: (3, 0, 0)),
-            once(vec.shape, lambda i: (0, 0)),
-        ],
-        out_specs=[
-            keep,
-            cols,
-            keep,
-            keep,
-            keep,
-            once(vec.shape, lambda i: (0, 0)),
-        ],
+    line, wide = by_rows(block, D), by_rows(block, ff)
+    held = once(vec.shape, lambda i: (0, 0))
+    return pl.pallas_call(
+        ffn_back_body,
+        grid=(rows // block,),
+        in_specs=[line, line, line, wide, held, ANY, ANY, ANY],
+        out_specs=[line, wide, line, line, line, held],
         out_shape=[
             jax.ShapeDtypeStruct((rows, D), BF),
             jax.ShapeDtypeStruct((rows, ff), BF),
@@ -325,15 +313,14 @@
             jax.ShapeDtypeStruct((rows, D), BF),
             jax.ShapeDtypeStruct(vec.shape, F32),
         ],
-        scratch_shapes=[pltpu.VMEM((rows, D), F32), pltpu.VMEM((rows, D), F32)],
+        scratch_shapes=weight_scratch(ff),
         compiler_params=params(),
         cost_estimate=cost(2 * rows * D * (D + 2 * ff), 20 * rows * D + 4 * rows * ff + 4 * D * ff),
         name="ffn_back",
-    )(dy, z2, z1, gp, wb, wi, wo, vec)
-
-
-def attend_back_body(seq, pairs, len_ref, q_ref, k_ref, v_ref, d_ref, l_ref, *rest):
-    e_ref, bq_ref, bv_ref = rest[-3:]
+    )(dy, z2, z1, slope, vec, wb, wi, first)
+
+
+def attend_back_body(seq, pairs, len_ref, q_ref, k_ref, v_ref, d_ref, l_ref, e_ref, bq_ref, bv_ref):
     count = len_ref[pl.program_id(0)]
     lane = lax.broadcasted_iota(jnp.int32, (seq, PAIR), 1)
     ok = lax.broadcasted_iota(jnp.int32, (seq, seq), 0) < count
@@ -376,7 +363,7 @@
 WIDE = D // GROUPS
 
 
-def attend_back_call(qkv, dctx, lse, lengths, group, after=()):
+def attend_back_call(qkv, dctx, lse, lengths, group):
     rows = qkv.shape[0]
     count = lengths.shape[0]
     seq = rows // count
@@ -401,19 +388,17 @@
                 part(2),
                 part(0),
                 pl.BlockSpec((1, pairs, 2, seq), lambda s, n: (s, group, 0, 0)),
-            ]
-            + [pl.BlockSpec(memory_space=pl.ANY)] * len(after),
+            ],
             out_specs=[pl.BlockSpec((3, seq, WIDE), lambda s, n: (0, s, 0)), line, line],
         ),
         out_shape=[jax.ShapeDtypeStruct((3, rows, WIDE), BF)] + [jax.ShapeDtypeStruct((count, 1, WIDE), F32)] * 2,
         compiler_params=params(),
         cost_estimate=cost(4 * flops, 14 * rows * WIDE, count * 2 * pairs * seq * seq),
         name="attend_back",
-    )(lengths, qkv, qkv, qkv, dctx, lse, *after)
-
-
-def dx_body(dz1_ref, e0_ref, e1_ref, w_ref, *rest):
-    o_ref = rest[-1]
+    )(lengths, qkv, qkv, qkv, dctx, lse)
+
+
+def dx_body(dz1_ref, e0_ref, e1_ref, w_ref, o_ref):
     acc = dz1_ref[...]
     for i in range(3):
         acc += mm(e0_ref[i], w_ref[i, :, :WIDE], NT)
@@ -421,54 +406,57 @@
     o_ref[...] = acc.astype(o_ref.dtype)
 
 
-def dx_call(dz1, e0, e1, w, dtype, after=(), block=256):
+def dx_call(dz1, e0, e1, w, dtype, block=256):
     rows = dz1.shape[0]
     line = pl.BlockSpec((block, D), lambda i: (i, 0))
     part = pl.BlockSpec((3, block, WIDE), lambda i: (0, i, 0))
     return pl.pallas_call(
         dx_body,
         grid=(rows // block,),
-        in_specs=[line, part, part, once((3, D, D), lambda i: (0, 0, 0))]
-        + [pl.BlockSpec(memory_space=pl.ANY)] * len(after),
+        in_specs=[line, part, part, once((3, D, D), lambda i: (0, 0, 0))],
         out_specs=line,
         out_shape=jax.ShapeDtypeStruct((rows, D), dtype),
         compiler_params=params(),
         cost_estimate=cost(6 * rows * D * D, 14 * rows * D + 6 * D * D),
         name="dx",
-    )(dz1, e0, e1, w, *after)
-
-
-def wgrad_body(rows, core_ref, a_ref, c_ref, b_ref, d_ref, *rest):
-    keep_ref, send_ref, acc_s = rest[-3:]
+    )(dz1, e0, e1, w)
+
+
+def wgrad_body(rows, x_first, core_ref, a_ref, c_ref, b_ref, d_ref, keep_ref, send_ref, acc_s):
     b = b_ref[...].reshape(b_ref.shape[-2:])
     d = d_ref[...].reshape(d_ref.shape[-2:])
-    acc_s[...] = mm(a_ref[...], b, NN) + mm(c_ref[...], d, NN)
+    acc_s[...] = mm(a_ref[...], b, TN) + mm(c_ref[...], d, TN)
     part = 8 * rows
     for out, core in ((keep_ref, core_ref[0]), (send_ref, 1 - core_ref[0])):
         for xi in range(2):
             for s in range(8):
+                zi, yi = s // 2, s % 2
                 start = pl.multiple_of(core * part + (2 * xi * part + s * rows), 8)
-                out[xi, s // 2, s % 2, 0] = acc_s[pl.ds(start, rows), :].astype(BF)
-
-
-def wgrad_call(core, a, c, b, d, rows, spec, units, width, after=()):
-    m, k = a.shape
-    held = once((m, k), lambda i, n: (0, 0))
-    out = pl.BlockSpec((2, 4, 2, 1, rows, width), lambda i, n: (0, 0, 0, i, 0, 0))
-    return pl.pallas_call(
-        lambda *refs: wgrad_body(rows, *refs),
+                value = acc_s[pl.ds(start, rows), :].astype(BF)
+                if x_first:
+                    out[xi, yi, zi, 0] = value
+                else:
+                    out[yi, xi, zi, 0] = value
+
+
+def wgrad_call(core, a, c, b, d, rows, spec, units, width, x_first):
+    k, m = a.shape
+    held = once((k, m), lambda i, n: (0, 0))
+    out = pl.BlockSpec((2, 2, 4, 1, rows, width), lambda i, n: (0, 0, 0, i, 0, 0))
+    return pl.pallas_call(
+        lambda *refs: wgrad_body(rows, x_first, *refs),
         grid_spec=pltpu.PrefetchScalarGridSpec(
             num_scalar_prefetch=1,
             grid=(units,),
-            in_specs=[held, held, spec, spec] + [pl.BlockSpec(memory_space=pl.ANY)] * len(after),
+            in_specs=[held, held, spec, spec],
             out_specs=[out, out],
             scratch_shapes=[pltpu.VMEM((m, width), F32)],
         ),
-        out_shape=[jax.ShapeDtypeStruct((2, 4, 2, units, rows, width), BF)] * 2,
+        out_shape=[jax.ShapeDtypeStruct((2, 2, 4, units, rows, width), BF)] * 2,
         compiler_params=params(),
         cost_estimate=cost(4 * k * m * width * units, 4 * k * (m + units * width) + 2 * m * width * units),
         name="wgrad",
-    )(core, a, c, b, d, *after)
+    )(core, a, c, b, d)
 
 
 def wgrad_back_call(core, two, one, e_two, e_one, rows):
@@ -483,13 +471,13 @@
         return pl.BlockSpec((k, block), index)
 
     held = once((k, D), lambda x, s, n: (0, 0))
-    out = pl.BlockSpec((1, 2, 2, 4, rows, D), lambda x, s, n: (x, s, 0, 0, 0, 0))
+    out = pl.BlockSpec((2, 1, 2, 4, rows, D), lambda x, s, n: (0, x, s, 0, 0, 0))
 
     def body(core_ref, g2k, g1k, g2s, g1s, e2_ref, e1_ref, keep_ref, send_ref):
         for a, c, o in ((g2k, g1k, keep_ref), (g2s, g1s, send_ref)):
             acc = mm(a[...], e2_ref[...], TN) + mm(c[...], e1_ref[...], TN)
             for s in range(16):
-                o[0, s // 8, s // 4 % 2, s % 4] = acc[s * rows : (s + 1) * rows].astype(BF)
+                o[s // 4 % 2, 0, s // 8, s % 4] = acc[s * rows : (s + 1) * rows].astype(BF)
 
     return pl.pallas_call(
         body,
@@ -499,19 +487,19 @@
             in_specs=[cols(False), cols(False), cols(True), cols(True), held, held],
             out_specs=[out, out],
         ),
-        out_shape=[jax.ShapeDtypeStruct((2, 4, 2, 4, rows, D), BF)] * 2,
+        out_shape=[jax.ShapeDtypeStruct((2, 2, 4, 4, rows, D), BF)] * 2,
         compiler_params=params(),
         cost_estimate=cost(4 * k * ff * D, 4 * k * (ff + D) + 2 * ff * D),
         name="wgrad_back",
     )(core, two, one, two, one, e_two, e_one)
 
 
-def layer_forward(x, low, weights, lengths):
+def layer_forward(x, low, weights, lengths, renorm):
     first, w_in, w_back, vec = weights
-    qkv, lowt = qkv_call(low, first, vec)
+    qkv = qkv_call(low, first, vec)
     ctx, lse = attend_call(qkv, lengths)
-    z1, h1t, ctxt, g, slope, z2, y, y_low = ffn_call(x, ctx, first, vec, w_in, w_back)
-    return y, y_low, (lowt, qkv, lse, z1, h1t, ctxt, g, slope, z2)
+    z1, h1, g, slope, z2, y = ffn_call(x, ctx, first, vec, w_in, w_back, renorm)
+    return z2, y, (low, qkv, lse, ctx, z1, h1, g, slope, z2)
 
 
 class Grid:
@@ -543,15 +531,12 @@
 X, CORE, Z, Y = range(4)
 
 
-def pack_body(at_ref, wq_ref, wo_ref, wi_ref, wb_ref, *rest):
-    vectors, span_ref, one_ref, two_ref, line_s = rest[:8], rest[8], rest[9], rest[10], rest[11]
+def pack_one_body(at_ref, wq_ref, wo_ref, *rest):
+    vectors, span_ref, one_ref, line_s = rest[:8], rest[8], rest[9], rest[10]
     rows = wq_ref.shape[0]
     for i in range(3):
         one_ref[i] = wq_ref[:, i * D : (i + 1) * D]
     one_ref[3] = wo_ref[...]
-    for i in range(4):
-        two_ref[i] = wi_ref[:, i * D : (i + 1) * D]
-        two_ref[4 + i] = wb_ref[i * rows : (i + 1) * rows]
     line_s[...] = jnp.zeros_like(line_s)
     for i, ref in enumerate(vectors):
         line_s[i : i + 1, :rows] = ref[...].astype(F32)
@@ -566,21 +551,46 @@
     one_ref[4] = jnp.concatenate([top, low, jnp.zeros((rows - 16, D), F32)], axis=0).astype(BF)
 
 
-def pack(device, w_qkv, w_out, w_in, w_back, vectors, span):
+def whole_block(v):
+    return pl.BlockSpec(v.shape, lambda *_: (0,) * v.ndim)
+
+
+def pack_one(device, w_qkv, w_out, vectors, span):
     rows = w_qkv.shape[0]
-    return pl.pallas_call(
-        pack_body,
+    operands = [w_qkv, w_out, *[v[None] for v in vectors], span[None]]
+    return pl.pallas_call(
+        pack_one_body,
         grid_spec=pltpu.PrefetchScalarGridSpec(
             num_scalar_prefetch=1,
             grid=(1,),
-            in_specs=[pl.BlockSpec(memory_space=pltpu.VMEM)] * 13,
-            out_specs=[pl.BlockSpec(memory_space=pltpu.VMEM)] * 2,
+            in_specs=[whole_block(v) for v in operands],
+            out_specs=pl.BlockSpec((5, rows, D), lambda *_: (0, 0, 0)),
             scratch_shapes=[pltpu.VMEM((16, D), F32)],
         ),
-        out_shape=[jax.ShapeDtypeStruct((5, rows, D), BF), jax.ShapeDtypeStruct((8, rows, D), BF)],
-        compiler_params=params(8 * 2**20),
-        name="pack",
-    )(device, w_qkv, w_out, w_in, w_back, *[v[None] for v in vectors], span[None])
+        out_shape=jax.ShapeDtypeStruct((5, rows, D), BF),
+        compiler_params=params(),
+        name="pack_one",
+    )(device, *operands)
+
+
+def pack_two_body(wi_ref, wb_ref, two_ref):
+    rows = wi_ref.shape[0]
+    for i in range(4):
+        two_ref[i] = wi_ref[:, i * D : (i + 1) * D]
+        two_ref[4 + i] = wb_ref[i * rows : (i + 1) * rows]
+
+
+def pack_two(w_in, w_back):
+    rows = w_in.shape[0]
+    return pl.pallas_call(
+        pack_two_body,
+        grid=(1,),
+        in_specs=[whole_block(w_in), whole_block(w_back)],
+        out_specs=pl.BlockSpec((8, rows, D), lambda *_: (0, 0, 0)),
+        out_shape=jax.ShapeDtypeStruct((8, rows, D), BF),
+        compiler_params=params(),
+        name="pack_two",
+    )(w_in, w_back)
 
 
 def place_body(split, at_ref, *refs):
@@ -618,25 +628,39 @@
         grid_spec=pltpu.PrefetchScalarGridSpec(
             num_scalar_prefetch=1,
             grid=(1,),
-            in_specs=[pl.BlockSpec(memory_space=pl.ANY)] * 8,
-            out_specs=[pl.BlockSpec(memory_space=pl.ANY)] * len(shapes),
+            in_specs=[ANY] * 8,
+            out_specs=[ANY] * len(shapes),
             scratch_shapes=[pltpu.SemaphoreType.DMA((64,))],
         ),
         out_shape=[jax.ShapeDtypeStruct(shape, BF) for shape in shapes],
-        compiler_params=params(2 * 2**20),
+        compiler_params=params(),
         name="place",
     )(at, *parts)
 
 
-def gather_packet(grid, at, packet, first, split):
-    ring = [packet] + [grid.send(packet, Z, k) for k in range(1, 4)]
-    parts = []
-    for units, order in ((slice(0, first), (Y, X)), (slice(first, None), (X, Y))):
-        line = jnp.stack([r[units] for r in ring])
-        near = jnp.stack([line, grid.send(line, order[0])])
-        far = grid.send(near, order[1])
-        parts += [near, grid.send(near, CORE), far, grid.send(far, CORE)]
-    return place(at, parts, split)
+def after(value, *others):
+    return lax.optimization_barrier((value, *others))[0]
+
+
+class Gather:
+    def __init__(self, grid, packet, first):
+        self.grid, self.first = grid, first
+        self.ring = [packet] + [grid.send(packet, Z, k) for k in range(1, 4)]
+
+    def one(self, *others):
+        ring = lax.optimization_barrier((*self.ring, *others))[:4]
+        self.line = [jnp.stack([r[: self.first] for r in ring]), jnp.stack([r[self.first :] for r in ring])]
+        self.came = [self.grid.send(v, d) for v, d in zip(self.line, (Y, X))]
+
+    def two(self):
+        self.near = [jnp.stack(pair) for pair in zip(self.line, self.came)]
+        self.far = [self.grid.send(v, d) for v, d in zip(self.near, (X, Y))]
+
+    def parts(self):
+        out = []
+        for near, far in zip(self.near, self.far):
+            out += [near, self.grid.send(near, CORE), far, self.grid.send(far, CORE)]
+        return out
 
 
 def pick(value, index, dim):
@@ -655,24 +679,27 @@
         self.left = (left[0], grid.send(left[1], CORE))
         self.right = (right[0], grid.send(right[1], CORE))
 
-    def one(self):
+    def one(self, *others):
         x, _, _, y = self.place
-        out_l, out_r = added(*self.left, (1 - x, 0)), added(*self.right, (1 - y, 2))
-        keep_l, keep_r = added(*self.left, (x, 0)), added(*self.right, (y, 2))
+        self.left = (after(self.left[0], *others), self.left[1])
+        self.right = (after(self.right[0], *others), self.right[1])
+        out_l, out_r = added(*self.left, (1 - x, 0)), added(*self.right, (1 - y, 0))
+        keep_l, keep_r = added(*self.left, (x, 0)), added(*self.right, (y, 0))
         self.left = (keep_l, self.grid.send(out_l, X))
         self.right = (keep_r, self.grid.send(out_r, Y))
         return [out_l, out_r]
 
     def two(self):
         x, _, _, y = self.place
-        out_l, out_r = added(*self.left, (1 - y, 1)), added(*self.right, (1 - x, 0))
-        keep_l, keep_r = added(*self.left, (y, 1)), added(*self.right, (x, 0))
+        out_l, out_r = added(*self.left, (1 - y, 0)), added(*self.right, (1 - x, 0))
+        keep_l, keep_r = added(*self.left, (y, 0)), added(*self.right, (x, 0))
         self.left = (keep_l, self.grid.send(out_l, Y))
         self.right = (keep_r, self.grid.send(out_r, X))
         return [out_l, out_r]
 
-    def three(self):
+    def three(self, *others):
         z = self.place[2]
+        self.left = (after(self.left[0], *others), self.left[1])
         line = jnp.concatenate([added(*self.left), added(*self.right)], axis=1)
         self.own = pick(line, z, 0)
         self.came = [self.grid.send(pick(line, (z + k) % 4, 0), Z, k) for k in range(1, 4)]
@@ -694,60 +721,67 @@
     at = jnp.stack([x, core, z, y]).astype(jnp.int32)
     core = core.astype(jnp.int32)[None]
     vectors = [bias_q, bias_v, bias_out, gain_one, shift_one, bias_back, gain_two, shift_two]
-    one, two = pack(device.astype(jnp.int32)[None], w_qkv, w_out, w_in, w_back, vectors, bias_in)
-    (first,) = gather_packet(grid, at, one, 2, False)
-    w_in, w_back = gather_packet(grid, at, two, 4, True)
+    one = Gather(grid, pack_one(device.astype(jnp.int32)[None], w_qkv, w_out, vectors, bias_in), 2)
+    two = Gather(grid, after(pack_two(w_in, w_back), *one.ring), 4)
+    one.one()
+    one.two()
+    two.one(*one.far)
+    (first,) = place(at, one.parts(), False)
     first = first.reshape(5, grid.count * rows, D)
+    vec = jnp.sum(first[4].reshape(grid.count, rows, D).astype(F32), axis=0)
+    qkv = qkv_call(tokens, first, vec)
+    two.two()
+    ctx, lse = attend_call(after(qkv, *two.near), lengths)
+    w_in, w_back = place(at, two.parts(), True)
     w_in = w_in.reshape(4, grid.count * rows, D)
     w_back = w_back.reshape(grid.count * span, D)
-    vec = jnp.sum(first[4].reshape(grid.count, rows, D).astype(F32), axis=0)
+    z1, h1, g, slope, z2, low = ffn_call(tokens, ctx, first, vec, w_in, w_back, False)
+    saved = [(tokens, qkv, lse, ctx, z1, h1, g, slope, z2)]
     weights = (first, w_in, w_back, vec)
-
-    value, low = tokens, tokens
-    saved = []
-    for _ in range(APPS):
-        value, low, stored = layer_forward(value, low, weights, lengths)
-        saved.append(stored)
+    _, low, stored = layer_forward(z2, low, weights, lengths, True)
+    saved.append(stored)
     activations = low
 
-    lowt2, qkv, lse, z1, h1t2, ctxt2, g2, slope, z2 = saved[1]
+    low2, qkv, lse, ctx2, z1, h2, g2, slope, z2 = saved[1]
     e2_2, e1_2, dz1, ea_2, dctx, sums_2 = ffn_back_call(cotangent, z2, z1, slope, w_back, w_in, first, vec)
     heads_2 = [attend_back_call(qkv, dctx, lse, lengths, i) for i in range(GROUPS)]
     grad = dx_call(dz1, heads_2[0][0], heads_2[1][0], first, F32)
 
-    lowt1, qkv, lse, z1, h1t1, ctxt1, g1, slope, z2 = saved[0]
+    low1, qkv, lse, ctx1, z1, h1, g1, slope, z2 = saved[0]
     e2_1, e1_1, dz1, ea_1, dctx, sums_1 = ffn_back_call(grad, z2, z1, slope, w_back, w_in, first, vec)
+    count = tokens.shape[0]
+
+    def by_heads(i, low2):
+        spec = pl.BlockSpec((1, count, WIDE), lambda i, n: (i, 0, 0))
+        return wgrad_call(core, low2, low1, heads_2[i][0], heads_1[i][0], rows, spec, 3, WIDE, True)
+
     right = wgrad_back_call(core, g2, g1, e2_2, e2_1, rows)
-    left = wgrad_call(
-        core, h1t2, h1t1, e1_2, e1_1, rows, pl.BlockSpec((tokens.shape[0], D), lambda i, n: (0, i)), 4, D
-    )
+    spec = pl.BlockSpec((count, D), lambda i, n: (0, i))
+    left = wgrad_call(core, after(h2, right[0]), h1, e1_2, e1_1, rows, spec, 4, D, True)
     wide = Sum(grid, where, left, right)
-
-    def by_heads(i, after):
-        spec = pl.BlockSpec((1, tokens.shape[0], WIDE), lambda i, n: (i, 0, 0))
-        return wgrad_call(core, lowt2, lowt1, heads_2[i][0], heads_1[i][0], rows, spec, 3, WIDE, after)
-
-    heads_1 = [attend_back_call(qkv, dctx, lse, lengths, 0)]
-    left = by_heads(0, ())
-    right = wgrad_call(
-        core, ctxt2, ctxt1, ea_2, ea_1, rows, pl.BlockSpec((tokens.shape[0], WIDE), lambda i, n: (0, i)), 2, WIDE
-    )
+    heads_1 = [attend_back_call(qkv, after(dctx, left[0]), lse, lengths, 0)]
+    steps = wide.one()
+    heads_1.append(attend_back_call(qkv, after(dctx, heads_1[0][0], *steps), lse, lengths, 1))
+    spec = pl.BlockSpec((count, WIDE), lambda i, n: (0, i))
+    right = wgrad_call(core, after(ctx2, heads_1[1][0]), ctx1, ea_2, ea_1, rows, spec, 2, WIDE, False)
+    left = by_heads(0, after(low2, right[0]))
     group_0 = Sum(grid, where, left, right)
-    heads_1.append(attend_back_call(qkv, dctx, lse, lengths, 1, wide.one()))
-    after = group_0.one() + wide.two()
-    left = by_heads(1, after)
+    steps = wide.two()
+    left = by_heads(1, after(low2, left[0], *steps))
     sums = sums_1 + sums_2
     by_group = [[a + b for a, b in zip(heads_1[i][1:], heads_2[i][1:])] for i in range(GROUPS)]
     line_q, line_v = [jnp.concatenate([jnp.sum(by_group[i][j], axis=0) for i in range(GROUPS)], axis=1) for j in range(2)]
     small = jnp.concatenate([line_q, line_v, sums[2:12]], axis=0).astype(BF)
     small = jnp.concatenate([small[:, :WIDE], small[:, WIDE:]], axis=0)
-    small = jnp.broadcast_to(small, (2, 4, 2, 1) + small.shape)
+    small = jnp.broadcast_to(small, (2, 2, 4, 1) + small.shape)
+    small = after(small, left[0])
     group_1 = Sum(grid, where, left, (small, small))
-    after = group_1.one() + group_0.two()
-    grad = dx_call(dz1, heads_1[0][0], heads_1[1][0], first, BF, after)
-    wide.three()
+    steps = group_0.one(left[0]) + wide.three(left[0])
+    grad = dx_call(after(dz1, left[0], *steps), heads_1[0][0], heads_1[1][0], first, BF)
+    group_1.one()
+    group_0.two()
+    group_1.two()
     group_0.three()
-    group_1.two()
     group_1.three()
     total, half_0, half_1 = wide.result(), group_0.result(), group_1.result()
 
@@ -781,18 +815,18 @@
     weights = (first, w_in, w_back, vec)
     value, low = tokens, tokens
     saved = []
-    for _ in range(APPS):
-        value, low, stored = layer_forward(value, low, weights, lengths)
+    for step in range(APPS):
+        value, low, stored = layer_forward(value, low, weights, lengths, step > 0)
         saved.append(stored)
     activations, grad, totals = low, cotangent, None
     for step in reversed(range(APPS)):
-        lowt, qkv, lse, z1, h1t, ctxt, g, slope, z2 = saved[step]
+        low, qkv, lse, ctx, z1, h1, g, slope, z2 = saved[step]
         e2, e1, dz1, ea, dctx, sums = ffn_back_call(grad, z2, z1, slope, w_back, w_in, first, vec)
         heads = [attend_back_call(qkv, dctx, lse, lengths, i) for i in range(GROUPS)]
         grad = dx_call(dz1, heads[0][0], heads[1][0], first, F32 if step else BF)
         e = jnp.concatenate([heads[i][0] for i in range(GROUPS)], axis=2).swapaxes(0, 1).reshape(-1, 3 * D)
         lines = [jnp.concatenate([jnp.sum(heads[i][j], axis=0) for i in range(GROUPS)], axis=1) for j in (1, 2)]
-        grads = [mm(lowt, e, NN), mm(ctxt, ea, NN), mm(h1t, e1, NN), mm(g, e2, TN)]
+        grads = [mm(low, e, TN), mm(ctx, ea, TN), mm(h1, e1, TN), mm(g, e2, TN)]
         grads += [jnp.concatenate(lines + [sums[2:]], axis=0)]
         totals = grads if totals is None else [a + b for a, b in zip(totals, grads)]
     lines = list(totals.pop())

time: 531 us -> 936 us (1.76)
  Pallas kernels: 288 us -> 731 us
  local copies, waits for them, and re-layouts: 38.3 us -> 11.3 us
    pallas_call x2, Pallas kernels: 9.65 us -> 469 us  [place(): pl.pallas_call(lambda *refs: place_body(split, *refs), grid_spec=pltpu.Pr...]
    unnamed x85 -> x47, local copies, waits for them, and re-layouts: 21.2 us -> 4.68 us
    pallas_call x9 -> x10, Pallas kernels: 152 us -> 136 us  [the longest x2 47.5 us: ffn_back_call(): pl.pallas_call(ffn_back_body, grid=(rows // block,), in_specs=[line, line...]
    pallas_call x5 -> x0, local copies, waits for them, and re-layouts: 10.5 us -> none  [the longest x4 7.23 us: wgrad_call(): pl.pallas_call(lambda *refs: wgrad_body(rows, *refs), grid_spec=pltpu.Pre...]
  transfers between devices with their start and end apart: 49 -> 49, of which waited for: 19 -> 23; matrix products, arithmetic and copies ran while one was open for 5% -> 2% of each run, Pallas kernels for 19% -> 30%
where the time goes in v3:
time: 936 us; the launch traced here: 932 us
  Pallas kernels  731 us (78%)
  waiting for transfers between devices  113 us (12%)
  starting transfers between devices  55 us (6%)
  other arithmetic  19.5 us (2%)
  local copies, waits for them, and re-layouts  11.3 us (1%)
    pallas_call x2, Pallas kernels, place(): pl.pallas_call(lambda *refs: place_body(split, *refs), grid_spec=pltpu.Pr...  469 us
    ppermute x49, waiting for transfers between devices, send(): return lax.ppermute(value, AXES, self.shift(dim, step))  113 us
    ppermute x49, starting transfers between devices, send(): return lax.ppermute(value, AXES, self.shift(dim, step))  55 us
    pallas_call x4, Pallas kernels, attend_back_call(): pl.pallas_call(body, grid_spec=pltpu.PrefetchScalarGridSpec(num_scalar_pr...  50 us
    pallas_call x2, Pallas kernels, ffn_back_call(): pl.pallas_call(ffn_back_body, grid=(rows // block,), in_specs=[line, line...  47.5 us
    pallas_call x2, Pallas kernels, ffn_call(): pl.pallas_call(lambda *refs: ffn_body(renorm, *refs), grid=(rows // block...  44.7 us
    pallas_call x4, Pallas kernels, wgrad_call(): pl.pallas_call(lambda *refs: wgrad_body(rows, x_first, *refs), grid_spec=...  40.3 us
    pallas_call x2, Pallas kernels, attend_call(): pl.pallas_call(body, grid_spec=pltpu.PrefetchScalarGridSpec(num_scalar_pr...  25.9 us
  transfers between devices with their start and end apart: 49, of which 23 were waited for; matrix products, arithmetic and copies ran while one was open for 2% of the time, Pallas kernels for 30%

profile of v3, /device:TPU:0, one launch (start us, length us, event | category | flops | bytes accessed | tf_op | source)
XLA Modules:
  0.0 931.5 jit_solution(7471543952914784923)
XLA Ops:
  0.7 1.8 pack_one.1
  2.4 3.0 collective-permute-start
  5.4 2.6 collective-permute-start.1
  8.0 1.3 collective-permute-start.2
  9.4 3.9 collective-permute-done
  13.2 7.1 collective-permute-done.1
  21.3 1.6 collective-permute-start.7
  23.9 1.6 collective-permute-start.3
  25.5 7.9 collective-permute-done.7
  33.5 1.6 collective-permute-start.9
  35.2 1.6 collective-permute-start.5
  36.7 1.7 pack_two.1
  38.4 4.5 collective-permute-start.11
  43.5 1.8 collective-permute-start.13
  45.3 5.8 collective-permute-done.11
  51.1 9.4 %collective-permute-done.12 = bf16[8,24,768]{2,1,0:T(8,128)(2,1)S(1)} collective-permute-done((bf16[8,24,768]{2,1,0:T(8,128)(2,1)}, bf16[8,24,768]{2,1,0:T(8,128)(2,1)S(1)}, u32[]{:S(2)}, u32[]{:S(2)}) %collective-permute-start.12) | collective-permute-done | bytes 294944 | tf_op jit(solution)/shard_map/ppermute | solution.py:528
  63.5 13.6 %collective-permute-done.15 = bf16[4,4,24,768]{3,2,1,0:T(8,128)(2,1)S(1)} collective-permute-done((bf16[4,4,24,768]{3,2,1,0:T(8,128)(2,1)S(1)}, bf16[4,4,24,768]{3,2,1,0:T(8,128)(2,1)S(1)}, u32[]{:S(2)}, u32[]{:S(2)}) %collective-permute-start.15) | collective-permute-done | bytes 589856 | tf_op jit(solution)/shard_map/ppermute | solution.py:528
  77.8 1.3 collective-permute-start.17
  80.5 2.4 collective-permute-done.8.refs_6_
  84.1 19.7 %collective-permute-done.20.refs_7_ = bf16[2,4,4,24,768]{4,3,2,1,0:T(8,128)(2,1)} collective-permute-done((bf16[2,4,4,24,768]{4,3,2,1,0:T(8,128)(2,1)S(1)}, bf16[2,4,4,24,768]{4,3,2,1,0:T(8,128)(2,1)}, u32[]{:S(2)}, u32[]{:S(2)}) %collective-permute-start.20) | collective-permute-done | bytes 1179680 | tf_op jit(solution)/shard_map/ppermute | solution.py:528
  104.9 181.0 %place.2 = bf16[5,2,2,4,2,24,768]{6,5,4,3,2,1,0:T(8,128)(2,1)} custom-call(s32[4]{0:T(128)} %pad_add_fusion.refs_0_, bf16[2,4,2,24,768]{4,3,2,1,0:T(8,128)(2,1)} %copy-done.3, bf16[2,4,2,24,768]{4,3,2,1,0:T(8,128)(2,1)} %copy-done.14, bf16[2,4,2,24,768]{4,3,2,1,0:T(8,128)(2,1)} %collective-permute-done.5.refs_3_, ...), custom_call_target="tpu_custom_call" | custom-call | tf_op jit(solution)/shard_map/place/pallas_call | solution.py:626
  286.0 2.1 convert_reduce_fusion.vec_ref.refs_2_
  288.1 7.9 qkv.2.refs_1_.refs_2_.refs_3_
  295.9 12.9 %attend.2 = (bf16[1024,768]{1,0:T(8,128)(2,1)}, f32[2,6,2,512]{3,2,1,0:T(2,128)}) custom-call(s32[2]{0:T(128)} %refs_0_.13, bf16[1024,2304]{1,0:T(8,128)(2,1)} %qkv.2.refs_1_.refs_2_.refs_3_, bf16[1024,2304]{1,0:T(8,128)(2,1)} %qkv.2.refs_1_.refs_2_.refs_3_, bf16[1024,2304]{1,0:T(8,128)(2,1)} %qkv.2.refs_1_.refs_2_.refs_3_), custom_call_target="tpu_custom_call" | custom-call | flops 6442450944 | bytes 6291456 | tf_op jit(solution)/shard_map/attend/pallas_call | solution.py:121
  311.8 288.2 %place.3 = (bf16[4,2,2,4,2,24,768]{6,5,4,3,2,1,0:T(8,128)(2,1)}, bf16[2,2,4,2,4,24,768]{6,5,4,3,2,1,0:T(8,128)(2,1)}) custom-call(s32[4]{0:T(128)} %pad_add_fusion.refs_0_, bf16[2,4,4,24,768]{4,3,2,1,0:T(8,128)(2,1)} %copy-done.1, bf16[2,4,4,24,768]{4,3,2,1,0:T(8,128)(2,1)} %copy-done.7, bf16[2,4,4,24,768]{4,3,2,1,0:T(8,128)(2,1)} %collective-permute-done.17.refs_3_, ...), custom_call_target="tpu_custom_call" | custom-call | tf_op jit(solution)/shard_map/place/pallas_call | solution.py:626
  600.0 22.2 %ffn.2 = (f32[1024,768]{1,0:T(8,128)}, bf16[1024,768]{1,0:T(8,128)(2,1)}, bf16[1024,3072]{1,0:T(8,128)(2,1)}, bf16[1024,3072]{1,0:T(8,128)(2,1)}, f32[1024,768]{1,0:T(8,128)}, /*index=5*/bf16[1024,768]{1,0:T(8,128)(2,1)}) custom-call(bf16[1024,768]{1,0:T(8,128)(2,1)} %refs_2_.3, bf16[1024,768]{1,0:T(8,128)(2,1)} %get-tuple-element.98.refs_1_.refs_2_, ...), custom_call_target="tpu_custom_call" | custom-call | flops 10871635968 | bytes 37748736 | tf_op jit(solution)/shard_map/ffn/pallas_call | solution.py:221
  622.2 7.9 qkv.3.refs_1_.refs_2_.refs_3_
  630.1 13.0 %attend.3 = (bf16[1024,768]{1,0:T(8,128)(2,1)}, f32[2,6,2,512]{3,2,1,0:T(2,128)}) custom-call(s32[2]{0:T(128)} %refs_0_.13, bf16[1024,2304]{1,0:T(8,128)(2,1)} %qkv.3.refs_1_.refs_2_.refs_3_, bf16[1024,2304]{1,0:T(8,128)(2,1)} %qkv.3.refs_1_.refs_2_.refs_3_, bf16[1024,2304]{1,0:T(8,128)(2,1)} %qkv.3.refs_1_.refs_2_.refs_3_), custom_call_target="tpu_custom_call" | custom-call | flops 6442450944 | bytes 6291456 | tf_op jit(solution)/shard_map/attend/pallas_call | solution.py:121
  643.1 22.5 %ffn.3 = (f32[1024,768]{1,0:T(8,128)}, bf16[1024,768]{1,0:T(8,128)(2,1)}, bf16[1024,3072]{1,0:T(8,128)(2,1)}, bf16[1024,3072]{1,0:T(8,128)(2,1)}, f32[1024,768]{1,0:T(8,128)}, /*index=5*/bf16[1024,768]{1,0:T(8,128)(2,1)}) custom-call(f32[1024,768]{1,0:T(8,128)} %get-tuple-element.101.refs_0_.z2_ref, bf16[1024,768]{1,0:T(8,128)(2,1)} %get-tuple-element.135.refs_1_, ...), custom_call_target="tpu_custom_call" | custom-call | flops 10871635968 | bytes 37748736 | tf_op jit(solution)/shard_map/ffn/pallas_call | solution.py:221
  665.5 23.8 %ffn_back.2 = (bf16[1024,768]{1,0:T(8,128)(2,1)}, bf16[1024,3072]{1,0:T(8,128)(2,1)}, f32[1024,768]{1,0:T(8,128)}, bf16[1024,768]{1,0:T(8,128)(2,1)}, bf16[1024,768]{1,0:T(8,128)(2,1)}, /*index=5*/f32[24,768]{1,0:T(8,128)}) custom-call(bf16[1024,768]{1,0:T(8,128)(2,1)} %dy_ref.1, f32[1024,768]{1,0:T(8,128)} %get-tuple-element.105.z2_ref, ...), custom_call_target="tpu_custom_call" | custom-call | flops 10871635968 | bytes 37748736 | tf_op jit(solution)/shard_map/ffn_back/pallas_call | solution.py:303
  689.4 12.3 %attend_back.5 = (bf16[3,1024,384]{2,1,0:T(8,128)(2,1)}, f32[2,1,384]{2,1,0:T(1,128)}, f32[2,1,384]{2,1,0:T(1,128)}) custom-call(s32[2]{0:T(128)} %refs_0_.13, bf16[1024,2304]{1,0:T(8,128)(2,1)} %qkv.3.refs_1_.refs_2_.refs_3_, bf16[1024,2304]{1,0:T(8,128)(2,1)} %qkv.3.refs_1_.refs_2_.refs_3_, bf16[1024,2304]{1,0:T(8,128)(2,1)} %qkv.3.refs_1_.refs_2_.refs_3_, ...), custom_call_target="tpu_custom_call" | custom-call | flops 8053063680 | bytes 5505024 | tf_op jit(solution)/shard_map/attend_back/pallas_call | solution.py:380
  701.7 12.5 %attend_back.4 = (bf16[3,1024,384]{2,1,0:T(8,128)(2,1)}, f32[2,1,384]{2,1,0:T(1,128)}, f32[2,1,384]{2,1,0:T(1,128)}) custom-call(s32[2]{0:T(128)} %refs_0_.13, bf16[1024,2304]{1,0:T(8,128)(2,1)} %qkv.3.refs_1_.refs_2_.refs_3_, bf16[1024,2304]{1,0:T(8,128)(2,1)} %qkv.3.refs_1_.refs_2_.refs_3_, bf16[1024,2304]{1,0:T(8,128)(2,1)} %qkv.3.refs_1_.refs_2_.refs_3_, ...), custom_call_target="tpu_custom_call" | custom-call | flops 8053063680 | bytes 5505024 | tf_op jit(solution)/shard_map/attend_back/pallas_call | solution.py:380
  714.2 9.6 %dx.2.dy_ref = f32[1024,768]{1,0:T(8,128)} custom-call(f32[1024,768]{1,0:T(8,128)} %get-tuple-element.108.dz1_ref, bf16[3,1024,384]{2,1,0:T(8,128)(2,1)} %get-tuple-element.111.e0_ref.refs_3_, bf16[3,1024,384]{2,1,0:T(8,128)(2,1)} %get-tuple-element.112.e1_ref.refs_3_, bf16[5,768,768]{2,1,0:T(8,128)(2,1)} %bitcast.222), custom_call_target="tpu_custom_call" | custom-call | flops 3623878656 | bytes 14548992 | tf_op jit(solution)/shard_map/dx/pallas_call | solution.py:413
  723.8 23.7 %ffn_back.3 = (bf16[1024,768]{1,0:T(8,128)(2,1)}, bf16[1024,3072]{1,0:T(8,128)(2,1)}, f32[1024,768]{1,0:T(8,128)}, bf16[1024,768]{1,0:T(8,128)(2,1)}, bf16[1024,768]{1,0:T(8,128)(2,1)}, /*index=5*/f32[24,768]{1,0:T(8,128)}) custom-call(f32[1024,768]{1,0:T(8,128)} %dx.2.dy_ref, f32[1024,768]{1,0:T(8,128)} %get-tuple-element.101.refs_0_.z2_ref, ...), custom_call_target="tpu_custom_call" | custom-call | flops 10871635968 | bytes 37748736 | tf_op jit(solution)/shard_map/ffn_back/pallas_call | solution.py:303
  747.5 14.9 %wgrad_back.1 = (bf16[2,2,4,4,24,768]{5,4,3,2,1,0:T(8,128)(2,1)}, bf16[2,2,4,4,24,768]{5,4,3,2,1,0:T(8,128)(2,1)}) custom-call(s32[1]{0:T(128)} %bitcast.1.core_ref.refs_0_, bf16[1024,3072]{1,0:T(8,128)(2,1)} %get-tuple-element.118.g2k.g2s, bf16[1024,3072]{1,0:T(8,128)(2,1)} %get-tuple-element.119.g1k.g1s, bf16[1024,3072]{1,0:T(8,128)(2,1)} %get-tuple-element.118.g2k.g2s, ...), custom_call_target="tpu_custom_call" | custom-call | flops 9663676416 | bytes 20447232 | tf_op jit(solution)/shard_map/wgrad_back/pallas_call | solution.py:482
  762.8 15.3 %wgrad.4 = (bf16[2,2,4,4,24,768]{5,4,3,2,1,0:T(8,128)(2,1)}, bf16[2,2,4,4,24,768]{5,4,3,2,1,0:T(8,128)(2,1)}) custom-call(s32[1]{0:T(128)} %bitcast.1.core_ref.refs_0_, bf16[1024,768]{1,0:T(8,128)(2,1)} %get-tuple-element.123.refs_1_, bf16[1024,768]{1,0:T(8,128)(2,1)} %get-tuple-element.124.refs_2_, bf16[1024,3072]{1,0:T(8,128)(2,1)} %get-tuple-element.125.refs_3_, ...), custom_call_target="tpu_custom_call" | custom-call | flops 9663676416 | bytes 20447232 | tf_op jit(solution)/shard_map/wgrad/pallas_call | solution.py:446
  778.2 12.5 %attend_back.6 = (bf16[3,1024,384]{2,1,0:T(8,128)(2,1)}, f32[2,1,384]{2,1,0:T(1,128)}, f32[2,1,384]{2,1,0:T(1,128)}) custom-call(s32[2]{0:T(128)} %refs_0_.13, bf16[1024,2304]{1,0:T(8,128)(2,1)} %qkv.2.refs_1_.refs_2_.refs_3_, bf16[1024,2304]{1,0:T(8,128)(2,1)} %qkv.2.refs_1_.refs_2_.refs_3_, bf16[1024,2304]{1,0:T(8,128)(2,1)} %qkv.2.refs_1_.refs_2_.refs_3_, ...), custom_call_target="tpu_custom_call" | custom-call | flops 8053063680 | bytes 5505024 | tf_op jit(solution)/shard_map/attend_back/pallas_call | solution.py:380
  792.2 3.5 add_convert_fusion
  795.7 1.5 collective-permute-start.25
  797.2 1.7 add_convert_fusion.1
  799.5 12.7 %attend_back.7 = (bf16[3,1024,384]{2,1,0:T(8,128)(2,1)}, f32[2,1,384]{2,1,0:T(1,128)}, f32[2,1,384]{2,1,0:T(1,128)}) custom-call(s32[2]{0:T(128)} %refs_0_.13, bf16[1024,2304]{1,0:T(8,128)(2,1)} %qkv.2.refs_1_.refs_2_.refs_3_, bf16[1024,2304]{1,0:T(8,128)(2,1)} %qkv.2.refs_1_.refs_2_.refs_3_, bf16[1024,2304]{1,0:T(8,128)(2,1)} %qkv.2.refs_1_.refs_2_.refs_3_, ...), custom_call_target="tpu_custom_call" | custom-call | flops 8053063680 | bytes 5505024 | tf_op jit(solution)/shard_map/attend_back/pallas_call | solution.py:380
  813.6 7.1 wgrad.5
  820.7 9.0 wgrad.6
  832.5 9.0 wgrad.7
  841.7 1.6 collective-permute-start.29
  843.8 1.2 add_convert_fusion.9
  845.0 1.5 collective-permute-start.32
  846.6 1.4 add_convert_fusion.7
  849.6 1.2 collective-permute-start.41
  850.9 9.5 %dx.3 = bf16[1024,768]{1,0:T(8,128)(2,1)} custom-call(f32[1024,768]{1,0:T(8,128)} %get-tuple-element.148.dz1_ref, bf16[3,1024,384]{2,1,0:T(8,128)(2,1)} %get-tuple-element.130.refs_4_.e0_ref, bf16[3,1024,384]{2,1,0:T(8,128)(2,1)} %get-tuple-element.134.refs_4_.e1_ref, bf16[5,768,768]{2,1,0:T(8,128)(2,1)} %bitcast.224), custom_call_target="tpu_custom_call" | custom-call | flops 3623878656 | bytes 14548992 | tf_op jit(solution)/shard_map/dx/pallas_call | solution.py:413
  860.4 5.6 collective-permute-done.32
  866.0 2.2 collective-permute-done.41
  868.8 1.6 collective-permute-start.42
  870.5 3.5 collective-permute-done.33
  876.1 3.8 collective-permute-done.31
  880.1 7.3 collective-permute-start.34
  887.3 2.4 collective-permute-start.36
  890.5 2.0 collective-permute-start.47
  892.4 11.2 %collective-permute-done.35 = bf16[5,24,384]{2,1,0:T(8,128)(2,1)S(1)} collective-permute-done((bf16[5,24,384]{2,1,0:T(8,128)(2,1)S(1)}, bf16[5,24,384]{2,1,0:T(8,128)(2,1)S(1)}, u32[]{:S(2)}, u32[]{:S(2)}) %collective-permute-start.35) | collective-permute-done | bytes 92192 | tf_op jit(solution)/shard_map/ppermute | solution.py:528
  905.2 7.2 collective-permute-done.38
  915.4 3.1 collective-permute-done.39
  918.6 4.6 collective-permute-start.43
  923.2 2.4 collective-permute-start.45
  927.1 1.6 collective-permute-done.44
  (171 shorter events, 33.8 us)
Async XLA Ops:
  2.4 10.8 %collective-permute-start = (bf16[5,24,768]{2,1,0:T(8,128)(2,1)}, bf16[5,24,768]{2,1,0:T(8,128)(2,1)S(1)}, u32[]{:S(2)}, u32[]{:S(2)}) collective-permute-start(bf16[5,24,768]{2,1,0:T(8,128)(2,1)} %pack_one.1), channel_id=1, source_target_pairs={{0,2},{1,3},{2,4},{3,5},{4,6},{5,7},{6,0},{7,1},{8,10},{9,11},{10,... | collective-permute-start | bytes 552968 | tf_op jit(solution)/shard_map/ppermute | solution.py:528
  5.4 14.9 %collective-permute-start.1 = (bf16[5,24,768]{2,1,0:T(8,128)(2,1)}, bf16[5,24,768]{2,1,0:T(8,128)(2,1)S(1)}, u32[]{:S(2)}, u32[]{:S(2)}) collective-permute-start(bf16[5,24,768]{2,1,0:T(8,128)(2,1)} %pack_one.1), channel_id=1, source_target_pairs={{0,4},{1,5},{2,6},{3,7},{4,0},{5,1},{6,2},{7,3},{8,12},{9,13},{10,... | collective-permute-start | bytes 552968 | tf_op jit(solution)/shard_map/ppermute | solution.py:528
  8.0 12.3 %collective-permute-start.2 = (bf16[5,24,768]{2,1,0:T(8,128)(2,1)}, bf16[5,24,768]{2,1,0:T(8,128)(2,1)S(1)}, u32[]{:S(2)}, u32[]{:S(2)}) collective-permute-start(bf16[5,24,768]{2,1,0:T(8,128)(2,1)} %pack_one.1), channel_id=1, source_target_pairs={{0,6},{1,7},{2,0},{3,1},{4,2},{5,3},{6,4},{7,5},{8,14},{9,15},{10,... | collective-permute-start | bytes 552968 | tf_op jit(solution)/shard_map/ppermute | solution.py:528
  21.3 12.1 %collective-permute-start.7 = (bf16[4,3,24,768]{3,2,1,0:T(8,128)(2,1)S(1)}, bf16[4,3,24,768]{3,2,1,0:T(8,128)(2,1)S(1)}, u32[]{:S(2)}, u32[]{:S(2)}) collective-permute-start(bf16[4,3,24,768]{3,2,1,0:T(8,128)(2,1)S(1)} %get-tuple-element.189), channel_id=1, source_target_pairs={{0,16},{1,17},{2,18},{3,19},{4,20},{5,21},{6,22},{7,23},{8,24},{9,... | collective-permute-start | bytes 1327112 | tf_op jit(solution)/shard_map/ppermute | solution.py:528
  23.9 11.2 %collective-permute-start.3 = (bf16[4,2,24,768]{3,2,1,0:T(8,128)(2,1)S(1)}, bf16[4,2,24,768]{3,2,1,0:T(8,128)(2,1)S(1)}, u32[]{:S(2)}, u32[]{:S(2)}) collective-permute-start(bf16[4,2,24,768]{3,2,1,0:T(8,128)(2,1)S(1)} %get-tuple-element.205), channel_id=1, source_target_pairs={{0,1},{1,0},{2,3},{3,2},{4,5},{5,4},{6,7},{7,6},{8,9},{9,8},{10,11... | collective-permute-start | bytes 884744 | tf_op jit(solution)/shard_map/ppermute | solution.py:528
  33.5 45.6 %copy-start.2 = (bf16[2,4,3,24,768]{4,3,2,1,0:T(8,128)(2,1)}, bf16[2,4,3,24,768]{4,3,2,1,0:T(8,128)(2,1)S(1)}, u32[]{:S(2)}) copy-start(bf16[2,4,3,24,768]{4,3,2,1,0:T(8,128)(2,1)S(1)} %pad_maximum_fusion.3.refs_5_) | copy-start | bytes 2654212
  33.5 27.5 %collective-permute-start.9 = (bf16[2,4,3,24,768]{4,3,2,1,0:T(8,128)(2,1)S(1)}, bf16[2,4,3,24,768]{4,3,2,1,0:T(8,128)(2,1)}, u32[]{:S(2)}, u32[]{:S(2)}) collective-permute-start(bf16[2,4,3,24,768]{4,3,2,1,0:T(8,128)(2,1)S(1)} %pad_maximum_fusion.3.refs_5_), channel_id=1, source_target_pairs={{0,1},{1,0},{2,3},{3,2},{4,5},{5,4},{6,7},{7,6},{8,9},{9,8},{10,11... | collective-permute-start | bytes 2654216 | tf_op jit(solution)/shard_map/ppermute | solution.py:528
  35.1 28.3 %copy-start.3 = (bf16[2,4,2,24,768]{4,3,2,1,0:T(8,128)(2,1)}, bf16[2,4,2,24,768]{4,3,2,1,0:T(8,128)(2,1)S(1)}, u32[]{:S(2)}) copy-start(bf16[2,4,2,24,768]{4,3,2,1,0:T(8,128)(2,1)S(1)} %pad_maximum_fusion.4.refs_1_) | copy-start | bytes 1769476
  35.2 25.8 %collective-permute-start.5 = (bf16[2,4,2,24,768]{4,3,2,1,0:T(8,128)(2,1)S(1)}, bf16[2,4,2,24,768]{4,3,2,1,0:T(8,128)(2,1)}, u32[]{:S(2)}, u32[]{:S(2)}) collective-permute-start(bf16[2,4,2,24,768]{4,3,2,1,0:T(8,128)(2,1)S(1)} %pad_maximum_fusion.4.refs_1_), channel_id=1, source_target_pairs={{0,16},{1,17},{2,18},{3,19},{4,20},{5,21},{6,22},{7,23},{8,24},{9,... | collective-permute-start | bytes 1769480 | tf_op jit(solution)/shard_map/ppermute | solution.py:528
  38.4 12.7 %collective-permute-start.11 = (bf16[8,24,768]{2,1,0:T(8,128)(2,1)}, bf16[8,24,768]{2,1,0:T(8,128)(2,1)S(1)}, u32[]{:S(2)}, u32[]{:S(2)}) collective-permute-start(bf16[8,24,768]{2,1,0:T(8,128)(2,1)} %pack_two.1), channel_id=1, source_target_pairs={{0,2},{1,3},{2,4},{3,5},{4,6},{5,7},{6,0},{7,1},{8,10},{9,11},{10,... | collective-permute-start | bytes 884744 | tf_op jit(solution)/shard_map/ppermute | solution.py:528
  42.9 17.6 %collective-permute-start.12 = (bf16[8,24,768]{2,1,0:T(8,128)(2,1)}, bf16[8,24,768]{2,1,0:T(8,128)(2,1)S(1)}, u32[]{:S(2)}, u32[]{:S(2)}) collective-permute-start(bf16[8,24,768]{2,1,0:T(8,128)(2,1)} %pack_two.1), channel_id=1, source_target_pairs={{0,4},{1,5},{2,6},{3,7},{4,0},{5,1},{6,2},{7,3},{8,12},{9,13},{10,... | collective-permute-start | bytes 884744 | tf_op jit(solution)/shard_map/ppermute | solution.py:528
  43.5 17.5 %collective-permute-start.13 = (bf16[8,24,768]{2,1,0:T(8,128)(2,1)}, bf16[8,24,768]{2,1,0:T(8,128)(2,1)S(1)}, u32[]{:S(2)}, u32[]{:S(2)}) collective-permute-start(bf16[8,24,768]{2,1,0:T(8,128)(2,1)} %pack_two.1), channel_id=1, source_target_pairs={{0,6},{1,7},{2,0},{3,1},{4,2},{5,3},{6,4},{7,5},{8,14},{9,15},{10,... | collective-permute-start | bytes 884744 | tf_op jit(solution)/shard_map/ppermute | solution.py:528
  62.2 14.8 %collective-permute-start.15 = (bf16[4,4,24,768]{3,2,1,0:T(8,128)(2,1)S(1)}, bf16[4,4,24,768]{3,2,1,0:T(8,128)(2,1)S(1)}, u32[]{:S(2)}, u32[]{:S(2)}) collective-permute-start(bf16[4,4,24,768]{3,2,1,0:T(8,128)(2,1)S(1)} %get-tuple-element.185), channel_id=1, source_target_pairs={{0,16},{1,17},{2,18},{3,19},{4,20},{5,21},{6,22},{7,23},{8,24},{9,... | collective-permute-start | bytes 1769480 | tf_op jit(solution)/shard_map/ppermute | solution.py:528
  62.9 14.8 %collective-permute-start.14 = (bf16[4,4,24,768]{3,2,1,0:T(8,128)(2,1)S(1)}, bf16[4,4,24,768]{3,2,1,0:T(8,128)(2,1)S(1)}, u32[]{:S(2)}, u32[]{:S(2)}) collective-permute-start(bf16[4,4,24,768]{3,2,1,0:T(8,128)(2,1)S(1)} %get-tuple-element.187), channel_id=1, source_target_pairs={{0,1},{1,0},{2,3},{3,2},{4,5},{5,4},{6,7},{7,6},{8,9},{9,8},{10,11... | collective-permute-start | bytes 1769480 | tf_op jit(solution)/shard_map/ppermute | solution.py:528
  63.5 16.2 %collective-permute-start.4 = (bf16[2,4,2,24,768]{4,3,2,1,0:T(8,128)(2,1)S(1)}, bf16[2,4,2,24,768]{4,3,2,1,0:T(8,128)(2,1)S(1)}, u32[]{:S(2)}, u32[]{:S(2)}) collective-permute-start(bf16[2,4,2,24,768]{4,3,2,1,0:T(8,128)(2,1)S(1)} %pad_maximum_fusion.4.refs_1_), channel_id=1, source_target_pairs={{0,8},{1,9},{2,10},{3,11},{4,12},{5,13},{6,14},{7,15},{8,0},{9,1},... | collective-permute-start | bytes 1769480 | tf_op jit(solution)/shard_map/ppermute | solution.py:528
  77.1 5.8 copy-start
  77.1 26.7 %collective-permute-start.20 = (bf16[2,4,4,24,768]{4,3,2,1,0:T(8,128)(2,1)S(1)}, bf16[2,4,4,24,768]{4,3,2,1,0:T(8,128)(2,1)}, u32[]{:S(2)}, u32[]{:S(2)}) collective-permute-start(bf16[2,4,4,24,768]{4,3,2,1,0:T(8,128)(2,1)S(1)} %pad_maximum_fusion.2.refs_5_), channel_id=1, source_target_pairs={{0,1},{1,0},{2,3},{3,2},{4,5},{5,4},{6,7},{7,6},{8,9},{9,8},{10,11... | collective-permute-start | bytes 3538952 | tf_op jit(solution)/shard_map/ppermute | solution.py:528
  77.8 208.1 %copy-start.1 = (bf16[2,4,4,24,768]{4,3,2,1,0:T(8,128)(2,1)}, bf16[2,4,4,24,768]{4,3,2,1,0:T(8,128)(2,1)S(1)}, u32[]{:S(2)}) copy-start(bf16[2,4,4,24,768]{4,3,2,1,0:T(8,128)(2,1)S(1)} %pad_maximum_fusion.1.refs_1_) | copy-start | bytes 3538948
  77.8 26.4 %collective-permute-start.17 = (bf16[2,4,4,24,768]{4,3,2,1,0:T(8,128)(2,1)S(1)}, bf16[2,4,4,24,768]{4,3,2,1,0:T(8,128)(2,1)}, u32[]{:S(2)}, u32[]{:S(2)}) collective-permute-start(bf16[2,4,4,24,768]{4,3,2,1,0:T(8,128)(2,1)S(1)} %pad_maximum_fusion.1.refs_1_), channel_id=1, source_target_pairs={{0,16},{1,17},{2,18},{3,19},{4,20},{5,21},{6,22},{7,23},{8,24},{9,... | collective-permute-start | bytes 3538952 | tf_op jit(solution)/shard_map/ppermute | solution.py:528
  79.1 3.8 collective-permute-start.8
  79.1 25.8 %collective-permute-start.10 = (bf16[2,4,3,24,768]{4,3,2,1,0:T(8,128)(2,1)}, bf16[2,4,3,24,768]{4,3,2,1,0:T(8,128)(2,1)}, u32[]{:S(2)}, u32[]{:S(2)}) collective-permute-start(bf16[2,4,3,24,768]{4,3,2,1,0:T(8,128)(2,1)} %collective-permute-done.9.refs_7_), channel_id=1, source_target_pairs={{0,8},{1,9},{2,10},{3,11},{4,12},{5,13},{6,14},{7,15},{8,0},{9,1},... | collective-permute-start | bytes 2654216 | tf_op jit(solution)/shard_map/ppermute | solution.py:528
  80.5 3.5 collective-permute-start.6
  82.9 226.0 %collective-permute-start.19 = (bf16[2,4,4,24,768]{4,3,2,1,0:T(8,128)(2,1)S(1)}, bf16[2,4,4,24,768]{4,3,2,1,0:T(8,128)(2,1)S(1)}, u32[]{:S(2)}, u32[]{:S(2)}) collective-permute-start(bf16[2,4,4,24,768]{4,3,2,1,0:T(8,128)(2,1)S(1)} %pad_maximum_fusion.2.refs_5_), channel_id=1, source_target_pairs={{0,8},{1,9},{2,10},{3,11},{4,12},{5,13},{6,14},{7,15},{8,0},{9,1},... | collective-permute-start | bytes 3538952 | tf_op jit(solution)/shard_map/ppermute | solution.py:528
  84.0 224.9 %collective-permute-start.16 = (bf16[2,4,4,24,768]{4,3,2,1,0:T(8,128)(2,1)S(1)}, bf16[2,4,4,24,768]{4,3,2,1,0:T(8,128)(2,1)S(1)}, u32[]{:S(2)}, u32[]{:S(2)}) collective-permute-start(bf16[2,4,4,24,768]{4,3,2,1,0:T(8,128)(2,1)S(1)} %pad_maximum_fusion.1.refs_1_), channel_id=1, source_target_pairs={{0,8},{1,9},{2,10},{3,11},{4,12},{5,13},{6,14},{7,15},{8,0},{9,1},... | collective-permute-start | bytes 3538952 | tf_op jit(solution)/shard_map/ppermute | solution.py:528
  103.8 205.1 %collective-permute-start.21 = (bf16[2,4,4,24,768]{4,3,2,1,0:T(8,128)(2,1)}, bf16[2,4,4,24,768]{4,3,2,1,0:T(8,128)(2,1)S(1)}, u32[]{:S(2)}, u32[]{:S(2)}) collective-permute-start(bf16[2,4,4,24,768]{4,3,2,1,0:T(8,128)(2,1)} %collective-permute-done.20.refs_7_), channel_id=1, source_target_pairs={{0,8},{1,9},{2,10},{3,11},{4,12},{5,13},{6,14},{7,15},{8,0},{9,1},... | collective-permute-start | bytes 3538952 | tf_op jit(solution)/shard_map/ppermute | solution.py:528
  104.2 204.7 %collective-permute-start.18 = (bf16[2,4,4,24,768]{4,3,2,1,0:T(8,128)(2,1)}, bf16[2,4,4,24,768]{4,3,2,1,0:T(8,128)(2,1)S(1)}, u32[]{:S(2)}, u32[]{:S(2)}) collective-permute-start(bf16[2,4,4,24,768]{4,3,2,1,0:T(8,128)(2,1)} %collective-permute-done.17.refs_3_), channel_id=1, source_target_pairs={{0,8},{1,9},{2,10},{3,11},{4,12},{5,13},{6,14},{7,15},{8,0},{9,1},... | collective-permute-start | bytes 3538952 | tf_op jit(solution)/shard_map/ppermute | solution.py:528
  762.4 29.8 %collective-permute-start.23 = (bf16[2,2,4,4,24,768]{5,4,3,2,1,0:T(8,128)(2,1)}, bf16[2,2,4,4,24,768]{5,4,3,2,1,0:T(8,128)(2,1)}, u32[]{:S(2)}, u32[]{:S(2)}) collective-permute-start(bf16[2,2,4,4,24,768]{5,4,3,2,1,0:T(8,128)(2,1)} %get-tuple-element.132), channel_id=1, source_target_pairs={{0,8},{1,9},{2,10},{3,11},{4,12},{5,13},{6,14},{7,15},{8,0},{9,1},... | collective-permute-start | bytes 7077896 | tf_op jit(solution)/shard_map/ppermute | solution.py:528
  778.1 19.1 %collective-permute-start.22 = (bf16[2,2,4,4,24,768]{5,4,3,2,1,0:T(8,128)(2,1)}, bf16[2,2,4,4,24,768]{5,4,3,2,1,0:T(8,128)(2,1)S(1)}, u32[]{:S(2)}, u32[]{:S(2)}) collective-permute-start(bf16[2,2,4,4,24,768]{5,4,3,2,1,0:T(8,128)(2,1)} %get-tuple-element.131), channel_id=1, source_target_pairs={{0,8},{1,9},{2,10},{3,11},{4,12},{5,13},{6,14},{7,15},{8,0},{9,1},... | collective-permute-start | bytes 7077896 | tf_op jit(solution)/shard_map/ppermute | solution.py:528
  778.2 12.5 %copy-start.21 = (f32[2,1,384]{2,1,0:T(1,128)S(1)}, f32[2,1,384]{2,1,0:T(1,128)}, u32[]{:S(2)}) copy-start(f32[2,1,384]{2,1,0:T(1,128)} %get-tuple-element.151) | copy-start | bytes 9220
  778.2 13.2 %copy-start.20 = (f32[2,1,384]{2,1,0:T(1,128)S(1)}, f32[2,1,384]{2,1,0:T(1,128)}, u32[]{:S(2)}) copy-start(f32[2,1,384]{2,1,0:T(1,128)} %get-tuple-element.155) | copy-start | bytes 9220
  778.2 14.0 %copy-start.16 = (f32[24,768]{1,0:T(8,128)S(1)}, f32[24,768]{1,0:T(8,128)}, u32[]{:S(2)}) copy-start(f32[24,768]{1,0:T(8,128)} %get-tuple-element.159) | copy-start | bytes 221188
  778.2 14.0 %copy-start.17 = (f32[24,768]{1,0:T(8,128)S(1)}, f32[24,768]{1,0:T(8,128)}, u32[]{:S(2)}) copy-start(f32[24,768]{1,0:T(8,128)} %get-tuple-element.158) | copy-start | bytes 221188
  778.2 14.0 %copy-start.4 = (bf16[2,2,4,4,24,768]{5,4,3,2,1,0:T(8,128)(2,1)S(1)}, bf16[2,2,4,4,24,768]{5,4,3,2,1,0:T(8,128)(2,1)}, u32[]{:S(2)}) copy-start(bf16[2,2,4,4,24,768]{5,4,3,2,1,0:T(8,128)(2,1)} %get-tuple-element.122) | copy-start | bytes 7077892
  795.7 34.5 %collective-permute-start.25 = (bf16[2,4,4,24,768]{4,3,2,1,0:T(8,128)(2,1)}, bf16[2,4,4,24,768]{4,3,2,1,0:T(8,128)(2,1)S(1)}, u32[]{:S(2)}, u32[]{:S(2)}) collective-permute-start(bf16[2,4,4,24,768]{4,3,2,1,0:T(8,128)(2,1)} %get-tuple-element.162), channel_id=1, source_target_pairs={{0,1},{1,0},{2,3},{3,2},{4,5},{5,4},{6,7},{7,6},{8,9},{9,8},{10,11... | collective-permute-start | bytes 3538952 | tf_op jit(solution)/shard_map/ppermute | solution.py:528
  798.9 32.4 %collective-permute-start.24 = (bf16[2,4,4,24,768]{4,3,2,1,0:T(8,128)(2,1)}, bf16[2,4,4,24,768]{4,3,2,1,0:T(8,128)(2,1)S(1)}, u32[]{:S(2)}, u32[]{:S(2)}) collective-permute-start(bf16[2,4,4,24,768]{4,3,2,1,0:T(8,128)(2,1)} %get-tuple-element.164), channel_id=1, source_target_pairs={{0,16},{1,17},{2,18},{3,19},{4,20},{5,21},{6,22},{7,23},{8,24},{9,... | collective-permute-start | bytes 3538952 | tf_op jit(solution)/shard_map/ppermute | solution.py:528
  799.5 12.7 %copy-start.19 = (f32[2,1,384]{2,1,0:T(1,128)S(1)}, f32[2,1,384]{2,1,0:T(1,128)}, u32[]{:S(2)}) copy-start(f32[2,1,384]{2,1,0:T(1,128)} %get-tuple-element.153) | copy-start | bytes 9220
  799.5 13.4 %copy-start.18 = (f32[2,1,384]{2,1,0:T(1,128)S(1)}, f32[2,1,384]{2,1,0:T(1,128)}, u32[]{:S(2)}) copy-start(f32[2,1,384]{2,1,0:T(1,128)} %get-tuple-element.157) | copy-start | bytes 9220
  820.7 23.1 %collective-permute-start.27 = (bf16[2,2,4,2,24,384]{5,4,3,2,1,0:T(8,128)(2,1)}, bf16[2,2,4,2,24,384]{5,4,3,2,1,0:T(8,128)(2,1)}, u32[]{:S(2)}, u32[]{:S(2)}) collective-permute-start(bf16[2,2,4,2,24,384]{5,4,3,2,1,0:T(8,128)(2,1)} %get-tuple-element.146), channel_id=1, source_target_pairs={{0,8},{1,9},{2,10},{3,11},{4,12},{5,13},{6,14},{7,15},{8,0},{9,1},... | collective-permute-start | bytes 1769480 | tf_op jit(solution)/shard_map/ppermute | solution.py:528
  829.7 16.9 %collective-permute-start.26 = (bf16[2,2,4,3,24,384]{5,4,3,2,1,0:T(8,128)(2,1)}, bf16[2,2,4,3,24,384]{5,4,3,2,1,0:T(8,128)(2,1)}, u32[]{:S(2)}, u32[]{:S(2)}) collective-permute-start(bf16[2,2,4,3,24,384]{5,4,3,2,1,0:T(8,128)(2,1)} %get-tuple-element.144), channel_id=1, source_target_pairs={{0,8},{1,9},{2,10},{3,11},{4,12},{5,13},{6,14},{7,15},{8,0},{9,1},... | collective-permute-start | bytes 2654216 | tf_op jit(solution)/shard_map/ppermute | solution.py:528
  832.5 11.3 %copy-start.15 = (bf16[2,2,4,2,24,384]{5,4,3,2,1,0:T(8,128)(2,1)S(1)}, bf16[2,2,4,2,24,384]{5,4,3,2,1,0:T(8,128)(2,1)}, u32[]{:S(2)}) copy-start(bf16[2,2,4,2,24,384]{5,4,3,2,1,0:T(8,128)(2,1)} %get-tuple-element.145) | copy-start | bytes 1769476
  841.5 5.1 copy-start.13
  841.5 7.0 collective-permute-start.40
  841.7 33.3 %collective-permute-start.29 = (bf16[4,4,24,768]{3,2,1,0:T(8,128)(2,1)}, bf16[4,4,24,768]{3,2,1,0:T(8,128)(2,1)S(1)}, u32[]{:S(2)}, u32[]{:S(2)}) collective-permute-start(bf16[4,4,24,768]{3,2,1,0:T(8,128)(2,1)} %fusion.8), channel_id=1, source_target_pairs={{0,16},{1,17},{2,18},{3,19},{4,20},{5,21},{6,22},{7,23},{8,24},{9,... | collective-permute-start | bytes 1769480 | tf_op jit(solution)/shard_map/ppermute | solution.py:528
  843.3 31.6 %collective-permute-start.28 = (bf16[4,4,24,768]{3,2,1,0:T(8,128)(2,1)}, bf16[4,4,24,768]{3,2,1,0:T(8,128)(2,1)S(1)}, u32[]{:S(2)}, u32[]{:S(2)}) collective-permute-start(bf16[4,4,24,768]{3,2,1,0:T(8,128)(2,1)} %get-tuple-element.166), channel_id=1, source_target_pairs={{0,1},{1,0},{2,3},{3,2},{4,5},{5,4},{6,7},{7,6},{8,9},{9,8},{10,11... | collective-permute-start | bytes 1769480 | tf_op jit(solution)/shard_map/ppermute | solution.py:528
  845.0 20.9 %collective-permute-start.32 = (bf16[2,4,2,24,384]{4,3,2,1,0:T(8,128)(2,1)S(1)}, bf16[2,4,2,24,384]{4,3,2,1,0:T(8,128)(2,1)S(1)}, u32[]{:S(2)}, u32[]{:S(2)}) collective-permute-start(bf16[2,4,2,24,384]{4,3,2,1,0:T(8,128)(2,1)S(1)} %get-tuple-element.175), channel_id=1, source_target_pairs={{0,1},{1,0},{2,3},{3,2},{4,5},{5,4},{6,7},{7,6},{8,9},{9,8},{10,11... | collective-permute-start | bytes 884744 | tf_op jit(solution)/shard_map/ppermute | solution.py:528
  847.9 20.9 %collective-permute-start.30 = (bf16[2,4,3,24,384]{4,3,2,1,0:T(8,128)(2,1)S(1)}, bf16[2,4,3,24,384]{4,3,2,1,0:T(8,128)(2,1)S(1)}, u32[]{:S(2)}, u32[]{:S(2)}) collective-permute-start(bf16[2,4,3,24,384]{4,3,2,1,0:T(8,128)(2,1)S(1)} %get-tuple-element.168), channel_id=1, source_target_pairs={{0,16},{1,17},{2,18},{3,19},{4,20},{5,21},{6,22},{7,23},{8,24},{9,... | collective-permute-start | bytes 1327112 | tf_op jit(solution)/shard_map/ppermute | solution.py:528
  849.6 16.4 %copy-start.22 = (bf16[2,2,4,3,24,384]{5,4,3,2,1,0:T(8,128)(2,1)S(1)}, bf16[2,2,4,3,24,384]{5,4,3,2,1,0:T(8,128)(2,1)}, u32[]{:S(2)}) copy-start(bf16[2,2,4,3,24,384]{5,4,3,2,1,0:T(8,128)(2,1)} %get-tuple-element.149) | copy-start | bytes 2654212
  849.6 18.6 %collective-permute-start.41 = (bf16[2,4,1,24,384]{4,3,1,2,0:T(8,128)(2,1)S(1)}, bf16[2,4,1,24,384]{4,3,1,2,0:T(8,128)(2,1)S(1)}, u32[]{:S(2)}, u32[]{:S(2)}) collective-permute-start(bf16[2,4,1,24,384]{4,3,1,2,0:T(8,128)(2,1)S(1)} %get-tuple-element.183), channel_id=1, source_target_pairs={{0,1},{1,0},{2,3},{3,2},{4,5},{5,4},{6,7},{7,6},{8,9},{9,8},{10,11... | collective-permute-start | bytes 442376 | tf_op jit(solution)/shard_map/ppermute | solution.py:528
  866.0 37.8 %collective-permute-start.37 = (bf16[2,2,4,3,24,384]{5,4,3,2,1,0:T(8,128)(2,1)S(1)}, bf16[2,2,4,3,24,384]{5,4,3,2,1,0:T(8,128)(2,1)S(1)}, u32[]{:S(2)}, u32[]{:S(2)}) collective-permute-start(bf16[2,2,4,3,24,384]{5,4,3,2,1,0:T(8,128)(2,1)S(1)} %copy-done.22), channel_id=1, source_target_pairs={{0,8},{1,9},{2,10},{3,11},{4,12},{5,13},{6,14},{7,15},{8,0},{9,1},... | collective-permute-start | bytes 2654216 | tf_op jit(solution)/shard_map/ppermute | solution.py:528
  868.3 5.8 collective-permute-start.33
  868.8 6.0 collective-permute-start.42
  874.0 5.9 collective-permute-start.31
  880.1 10.4 %collective-permute-start.34 = (bf16[5,24,384]{2,1,0:T(8,128)(2,1)S(1)}, bf16[5,24,384]{2,1,0:T(8,128)(2,1)S(1)}, u32[]{:S(2)}, u32[]{:S(2)}) collective-permute-start(bf16[5,24,384]{2,1,0:T(8,128)(2,1)S(1)} %get-tuple-element.190), channel_id=1, source_target_pairs={{0,2},{1,3},{2,4},{3,5},{4,6},{5,7},{6,0},{7,1},{8,10},{9,11},{10,... | collective-permute-start | bytes 276488 | tf_op jit(solution)/shard_map/ppermute | solution.py:528
  887.3 16.3 %collective-permute-start.35 = (bf16[5,24,384]{2,1,0:T(8,128)(2,1)S(1)}, bf16[5,24,384]{2,1,0:T(8,128)(2,1)S(1)}, u32[]{:S(2)}, u32[]{:S(2)}) collective-permute-start(bf16[5,24,384]{2,1,0:T(8,128)(2,1)S(1)} %get-tuple-element.191), channel_id=1, source_target_pairs={{0,4},{1,5},{2,6},{3,7},{4,0},{5,1},{6,2},{7,3},{8,12},{9,13},{10,... | collective-permute-start | bytes 276488 | tf_op jit(solution)/shard_map/ppermute | solution.py:528
  887.3 16.4 %copy-start.12 = (bf16[2,2,4,3,24,384]{5,4,3,2,1,0:T(8,128)(2,1)S(1)}, bf16[2,2,4,3,24,384]{5,4,3,2,1,0:T(8,128)(2,1)}, u32[]{:S(2)}) copy-start(bf16[2,2,4,3,24,384]{5,4,3,2,1,0:T(8,128)(2,1)} %get-tuple-element.142) | copy-start | bytes 2654212
  887.3 16.3 %collective-permute-start.36 = (bf16[5,24,384]{2,1,0:T(8,128)(2,1)S(1)}, bf16[5,24,384]{2,1,0:T(8,128)(2,1)S(1)}, u32[]{:S(2)}, u32[]{:S(2)}) collective-permute-start(bf16[5,24,384]{2,1,0:T(8,128)(2,1)S(1)} %get-tuple-element.192), channel_id=1, source_target_pairs={{0,6},{1,7},{2,0},{3,1},{4,2},{5,3},{6,4},{7,5},{8,14},{9,15},{10,... | collective-permute-start | bytes 276488 | tf_op jit(solution)/shard_map/ppermute | solution.py:528
  889.9 23.1 %collective-permute-start.46 = (bf16[8,24,768]{2,1,0:T(8,128)(2,1)S(1)}, bf16[8,24,768]{2,1,0:T(8,128)(2,1)S(1)}, u32[]{:S(2)}, u32[]{:S(2)}) collective-permute-start(bf16[8,24,768]{2,1,0:T(8,128)(2,1)S(1)} %get-tuple-element.171), channel_id=1, source_target_pairs={{0,2},{1,3},{2,4},{3,5},{4,6},{5,7},{6,0},{7,1},{8,10},{9,11},{10,... | collective-permute-start | bytes 884744 | tf_op jit(solution)/shard_map/ppermute | solution.py:528
  890.5 23.6 %collective-permute-start.47 = (bf16[8,24,768]{2,1,0:T(8,128)(2,1)S(1)}, bf16[8,24,768]{2,1,0:T(8,128)(2,1)S(1)}, u32[]{:S(2)}, u32[]{:S(2)}) collective-permute-start(bf16[8,24,768]{2,1,0:T(8,128)(2,1)S(1)} %get-tuple-element.172), channel_id=1, source_target_pairs={{0,4},{1,5},{2,6},{3,7},{4,0},{5,1},{6,2},{7,3},{8,12},{9,13},{10,... | collective-permute-start | bytes 884744 | tf_op jit(solution)/shard_map/ppermute | solution.py:528
  903.7 11.6 %collective-permute-start.48 = (bf16[8,24,768]{2,1,0:T(8,128)(2,1)S(1)}, bf16[8,24,768]{2,1,0:T(8,128)(2,1)S(1)}, u32[]{:S(2)}, u32[]{:S(2)}) collective-permute-start(bf16[8,24,768]{2,1,0:T(8,128)(2,1)S(1)} %get-tuple-element.173), channel_id=1, source_target_pairs={{0,6},{1,7},{2,0},{3,1},{4,2},{5,3},{6,4},{7,5},{8,14},{9,15},{10,... | collective-permute-start | bytes 884744 | tf_op jit(solution)/shard_map/ppermute | solution.py:528
  904.0 8.4 collective-permute-start.38
  912.5 6.0 collective-permute-start.39
  918.6 8.5 collective-permute-start.43
  923.2 5.6 collective-permute-start.44
  923.2 5.6 collective-permute-start.45
  (8 other events, 14.7 us)

commit v4 on v3

--- a/solution.py
+++ b/solution.py
@@ -28,12 +28,16 @@
     return pltpu.CompilerParams(vmem_limit_bytes=limit)
 
 
-def cost(flops, nbytes, trans=0):
-    return pl.CostEstimate(flops=int(flops), bytes_accessed=int(nbytes), transcendentals=int(trans))
+def cost():
+    return pl.CostEstimate(flops=1, bytes_accessed=1, transcendentals=0)
 
 
 def once(shape, index):
     return pl.BlockSpec(shape, index, pipeline_mode=pl.Buffered(1))
+
+
+def whole_block(v):
+    return pl.BlockSpec(v.shape, lambda *_: (0,) * v.ndim)
 
 
 def normed(z):
@@ -70,7 +74,7 @@
         out_specs=pl.BlockSpec((rows, D), lambda i: (0, i)),
         out_shape=jax.ShapeDtypeStruct((rows, 3 * D), BF),
         compiler_params=params(),
-        cost_estimate=cost(6 * rows * D * D, 2 * (rows * D * 4 + 3 * D * D)),
+        cost_estimate=cost(),
         name="qkv",
     )(x, w, vec)
 
@@ -117,7 +121,6 @@
     def body(*refs):
         attend_body(seq, pairs, *refs)
 
-    flops = 4 * count * HEADS * seq * seq * HEAD_DIM
     return pl.pallas_call(
         body,
         grid_spec=pltpu.PrefetchScalarGridSpec(
@@ -131,7 +134,7 @@
             jax.ShapeDtypeStruct((count, D // PAIR, 2, seq), F32),
         ],
         compiler_params=params(),
-        cost_estimate=cost(4 * flops, 8 * rows * D, count * HEADS * seq * seq),
+        cost_estimate=cost(),
         name="attend",
     )(lengths, qkv, qkv, qkv)
 
@@ -233,7 +236,7 @@
         ],
         scratch_shapes=weight_scratch(ff),
         compiler_params=params(),
-        cost_estimate=cost(2 * rows * D * (D + 2 * ff), 20 * rows * D + 4 * rows * ff + 4 * D * ff, rows * ff),
+        cost_estimate=cost(),
         name="ffn",
     )(x, ctx, vec, first, wi, wb)
 
@@ -315,7 +318,7 @@
         ],
         scratch_shapes=weight_scratch(ff),
         compiler_params=params(),
-        cost_estimate=cost(2 * rows * D * (D + 2 * ff), 20 * rows * D + 4 * rows * ff + 4 * D * ff),
+        cost_estimate=cost(),
         name="ffn_back",
     )(dy, z2, z1, slope, vec, wb, wi, first)
 
@@ -375,7 +378,6 @@
     def body(*refs):
         attend_back_body(seq, pairs, *refs)
 
-    flops = 10 * count * 2 * pairs * seq * seq * HEAD_DIM
     line = pl.BlockSpec((1, 1, WIDE), lambda s, n: (s, 0, 0))
     return pl.pallas_call(
         body,
@@ -393,7 +395,7 @@
         ),
         out_shape=[jax.ShapeDtypeStruct((3, rows, WIDE), BF)] + [jax.ShapeDtypeStruct((count, 1, WIDE), F32)] * 2,
         compiler_params=params(),
-        cost_estimate=cost(4 * flops, 14 * rows * WIDE, count * 2 * pairs * seq * seq),
+        cost_estimate=cost(),
         name="attend_back",
     )(lengths, qkv, qkv, qkv, dctx, lse)
 
@@ -417,15 +419,12 @@
         out_specs=line,
         out_shape=jax.ShapeDtypeStruct((rows, D), dtype),
         compiler_params=params(),
-        cost_estimate=cost(6 * rows * D * D, 14 * rows * D + 6 * D * D),
+        cost_estimate=cost(),
         name="dx",
     )(dz1, e0, e1, w)
 
 
-def wgrad_body(rows, x_first, core_ref, a_ref, c_ref, b_ref, d_ref, keep_ref, send_ref, acc_s):
-    b = b_ref[...].reshape(b_ref.shape[-2:])
-    d = d_ref[...].reshape(d_ref.shape[-2:])
-    acc_s[...] = mm(a_ref[...], b, TN) + mm(c_ref[...], d, TN)
+def deal(acc_s, rows, x_first, core_ref, keep_ref, send_ref):
     part = 8 * rows
     for out, core in ((keep_ref, core_ref[0]), (send_ref, 1 - core_ref[0])):
         for xi in range(2):
@@ -439,24 +438,99 @@
                     out[yi, xi, zi, 0] = value
 
 
-def wgrad_call(core, a, c, b, d, rows, spec, units, width, x_first):
-    k, m = a.shape
-    held = once((k, m), lambda i, n: (0, 0))
-    out = pl.BlockSpec((2, 2, 4, 1, rows, width), lambda i, n: (0, 0, 0, i, 0, 0))
-    return pl.pallas_call(
-        lambda *refs: wgrad_body(rows, x_first, *refs),
+def packet(rows, units, width):
+    spec = pl.BlockSpec((2, 2, 4, 1, rows, width), lambda i, n: (0, 0, 0, i, 0, 0))
+    return [spec] * 2, [jax.ShapeDtypeStruct((2, 2, 4, units, rows, width), BF)] * 2
+
+
+def wgrad_in_call(core, a, c, b, d, rows):
+    k, n = b.shape
+    held = once((k, D), lambda i, n: (0, 0))
+    spec = pl.BlockSpec((k, D), lambda i, n: (0, i))
+    out_specs, out_shape = packet(rows, n // D, D)
+
+    def body(core_ref, a_ref, c_ref, b_ref, d_ref, keep_ref, send_ref, acc_s):
+        acc_s[...] = mm(a_ref[...], b_ref[...], TN) + mm(c_ref[...], d_ref[...], TN)
+        deal(acc_s, rows, True, core_ref, keep_ref, send_ref)
+
+    return pl.pallas_call(
+        body,
+        grid_spec=pltpu.PrefetchScalarGridSpec(
+            num_scalar_prefetch=1,
+            grid=(n // D,),
+            in_specs=[held, held, spec, spec],
+            out_specs=out_specs,
+            scratch_shapes=[pltpu.VMEM((D, D), F32)],
+        ),
+        out_shape=out_shape,
+        compiler_params=params(),
+        cost_estimate=cost(),
+        name="wgrad_in",
+    )(core, a, c, b, d)
+
+
+def wgrad_heads_call(core, low2, low1, e2, e1, rows, others, x_first):
+    k = low2.shape[0]
+    last = len(others) == 4
+    held = once((k, D), lambda i, n: (0, 0))
+    spec = pl.BlockSpec((1, k, WIDE), lambda i, n: (jnp.minimum(i, 2), 0, 0))
+    units = 5 if last else 4
+    out_specs, out_shape = packet(rows, units, WIDE)
+    if last:
+        half = pl.BlockSpec((k, WIDE), lambda i, n: (0, jnp.maximum(i - 3, 0)))
+        more = [held, held, half, half]
+    else:
+        more = [whole_block(v) for v in others]
+
+    def body(core_ref, a_ref, c_ref, b_ref, d_ref, *rest):
+        rest, (keep_ref, send_ref, acc_s) = rest[:-3], rest[-3:]
+        step = pl.program_id(0)
+
+        @pl.when(step < 3)
+        def _():
+            acc_s[...] = mm(a_ref[...], b_ref[0], TN) + mm(c_ref[...], d_ref[0], TN)
+
+        if last:
+
+            @pl.when(step >= 3)
+            def _():
+                acc_s[...] = mm(rest[0][...], rest[2][...], TN) + mm(rest[1][...], rest[3][...], TN)
+
+            deal(acc_s, rows, x_first, core_ref, keep_ref, send_ref)
+        else:
+
+            @pl.when(step < 3)
+            def _():
+                deal(acc_s, rows, x_first, core_ref, keep_ref, send_ref)
+
+            @pl.when(step == 3)
+            def _():
+                sums = rest[0][...] + rest[1][...]
+                small = []
+                for g in range(GROUPS):
+                    lines = rest[2 + 4 * g : 6 + 4 * g]
+                    small.append(colsum(lines[0][:, 0, :] + lines[1][:, 0, :]))
+                    small.append(colsum(lines[2][:, 0, :] + lines[3][:, 0, :]))
+                    small.append(sums[2 : rows // 2, g * WIDE : (g + 1) * WIDE])
+                small = jnp.concatenate(small, axis=0).astype(BF)
+                for i in range(16):
+                    keep_ref[i // 8, i // 4 % 2, i % 4, 0] = small
+                    send_ref[i // 8, i // 4 % 2, i % 4, 0] = small
+
+    return pl.pallas_call(
+        body,
         grid_spec=pltpu.PrefetchScalarGridSpec(
             num_scalar_prefetch=1,
             grid=(units,),
-            in_specs=[held, held, spec, spec],
-            out_specs=[out, out],
-            scratch_shapes=[pltpu.VMEM((m, width), F32)],
+            in_specs=[held, held, spec, spec] + more,
+            out_specs=out_specs,
+            scratch_shapes=[pltpu.VMEM((D, WIDE), F32)],
         ),
-        out_shape=[jax.ShapeDtypeStruct((2, 2, 4, units, rows, width), BF)] * 2,
-        compiler_params=params(),
-        cost_estimate=cost(4 * k * m * width * units, 4 * k * (m + units * width) + 2 * m * width * units),
-        name="wgrad",
-    )(core, a, c, b, d)
+        out_shape=out_shape,
+        compiler_params=params(),
+        cost_estimate=cost(),
+        name="wgrad_heads",
+    )(core, low2, low1, e2, e1, *others)
 
 
 def wgrad_back_call(core, two, one, e_two, e_one, rows):
@@ -489,7 +563,7 @@
         ),
         out_shape=[jax.ShapeDtypeStruct((2, 2, 4, 4, rows, D), BF)] * 2,
         compiler_params=params(),
-        cost_estimate=cost(4 * k * ff * D, 4 * k * (ff + D) + 2 * ff * D),
+        cost_estimate=cost(),
         name="wgrad_back",
     )(core, two, one, two, one, e_two, e_one)
 
@@ -551,10 +625,6 @@
     one_ref[4] = jnp.concatenate([top, low, jnp.zeros((rows - 16, D), F32)], axis=0).astype(BF)
 
 
-def whole_block(v):
-    return pl.BlockSpec(v.shape, lambda *_: (0,) * v.ndim)
-
-
 def pack_one(device, w_qkv, w_out, vectors, span):
     rows = w_qkv.shape[0]
     operands = [w_qkv, w_out, *[v[None] for v in vectors], span[None]]
@@ -594,9 +664,10 @@
 
 
 def place_body(split, at_ref, *refs):
-    parts, outs, sems = refs[:8], refs[8:-1], refs[-1]
+    outs = 2 if split else 1
+    parts, outs, held, sems, out_sems = refs[:8], refs[8 : 8 + outs], refs[8 + outs : -2], refs[-2], refs[-1]
     x, core, z, y = at_ref[0], at_ref[1], at_ref[2], at_ref[3]
-    copies = []
+    sides = ([], [])
     for i, part in enumerate(parts):
         side, far, other = i >> 2, (i >> 1) & 1, i & 1
         count = part.shape[2]
@@ -607,13 +678,27 @@
             for dz in range(4):
                 pz = (z + 4 - dz) % 4
                 if split:
-                    target = outs[side].at[:, px, pc, pz, py] if side == 0 else outs[side].at[px, pc, pz, py]
+                    target = held[side].at[:, px, pc, pz, py] if side == 0 else held[side].at[px, pc, pz, py]
                 else:
-                    target = outs[0].at[pl.ds(0 if side == 0 else 5 - count, count), px, pc, pz, py]
-                copies.append(pltpu.make_async_copy(part.at[near, dz], target, sems.at[len(copies)]))
-    for copy in copies:
-        copy.start()
-    for copy in copies:
+                    target = held[0].at[pl.ds(0 if side == 0 else 5 - count, count), px, pc, pz, py]
+                sem = sems.at[i * 8 + near * 4 + dz]
+                sides[side].append(pltpu.make_async_copy(part.at[near, dz], target, sem))
+    for side in sides:
+        for copy in side:
+            copy.start()
+    back = []
+    for side in range(2):
+        for copy in sides[side]:
+            copy.wait()
+        if split:
+            pair = held[side], outs[side]
+        else:
+            count = parts[4 * side].shape[2]
+            span = pl.ds(0 if side == 0 else 5 - count, count)
+            pair = held[0].at[span], outs[0].at[span]
+        back.append(pltpu.make_async_copy(*pair, out_sems.at[side]))
+        back[-1].start()
+    for copy in back:
         copy.wait()
 
 
@@ -630,10 +715,12 @@
             grid=(1,),
             in_specs=[ANY] * 8,
             out_specs=[ANY] * len(shapes),
-            scratch_shapes=[pltpu.SemaphoreType.DMA((64,))],
+            scratch_shapes=[pltpu.VMEM(shape, BF) for shape in shapes]
+            + [pltpu.SemaphoreType.DMA((64,)), pltpu.SemaphoreType.DMA((2,))],
         ),
         out_shape=[jax.ShapeDtypeStruct(shape, BF) for shape in shapes],
         compiler_params=params(),
+        cost_estimate=cost(),
         name="place",
     )(at, *parts)
 
@@ -652,13 +739,15 @@
         self.line = [jnp.stack([r[: self.first] for r in ring]), jnp.stack([r[self.first :] for r in ring])]
         self.came = [self.grid.send(v, d) for v, d in zip(self.line, (Y, X))]
 
-    def two(self):
-        self.near = [jnp.stack(pair) for pair in zip(self.line, self.came)]
+    def two(self, *others):
+        held = lax.optimization_barrier((*self.line, *others))
+        self.near = [jnp.stack(pair) for pair in zip(held, self.came)]
         self.far = [self.grid.send(v, d) for v, d in zip(self.near, (X, Y))]
 
-    def parts(self):
+    def parts(self, *others):
         out = []
-        for near, far in zip(self.near, self.far):
+        held = lax.optimization_barrier((*self.near, *self.far, *others))
+        for near, far in zip(held[:2], held[2:4]):
             out += [near, self.grid.send(near, CORE), far, self.grid.send(far, CORE)]
         return out
 
@@ -674,39 +763,33 @@
 
 
 class Sum:
-    def __init__(self, grid, place, left, right):
-        self.grid, self.place = grid, place
-        self.left = (left[0], grid.send(left[1], CORE))
-        self.right = (right[0], grid.send(right[1], CORE))
+    def __init__(self, grid, place, order, pair):
+        self.grid, self.place, self.order = grid, place, order
+        self.mine, self.came = pair[0], grid.send(pair[1], CORE)
+
+    def cut(self, dim, others):
+        here = self.place[dim]
+        mine = after(self.mine, *others)
+        out = added(mine, self.came, (1 - here, 0))
+        self.mine = added(mine, self.came, (here, 0))
+        self.came = self.grid.send(out, dim)
+        return [out, self.mine]
 
     def one(self, *others):
-        x, _, _, y = self.place
-        self.left = (after(self.left[0], *others), self.left[1])
-        self.right = (after(self.right[0], *others), self.right[1])
-        out_l, out_r = added(*self.left, (1 - x, 0)), added(*self.right, (1 - y, 0))
-        keep_l, keep_r = added(*self.left, (x, 0)), added(*self.right, (y, 0))
-        self.left = (keep_l, self.grid.send(out_l, X))
-        self.right = (keep_r, self.grid.send(out_r, Y))
-        return [out_l, out_r]
-
-    def two(self):
-        x, _, _, y = self.place
-        out_l, out_r = added(*self.left, (1 - y, 0)), added(*self.right, (1 - x, 0))
-        keep_l, keep_r = added(*self.left, (y, 0)), added(*self.right, (x, 0))
-        self.left = (keep_l, self.grid.send(out_l, Y))
-        self.right = (keep_r, self.grid.send(out_r, X))
-        return [out_l, out_r]
+        return self.cut(self.order[0], others)
+
+    def two(self, *others):
+        return self.cut(self.order[1], others)
 
     def three(self, *others):
         z = self.place[2]
-        self.left = (after(self.left[0], *others), self.left[1])
-        line = jnp.concatenate([added(*self.left), added(*self.right)], axis=1)
-        self.own = pick(line, z, 0)
+        line = added(after(self.mine, *others), self.came)
+        self.mine = pick(line, z, 0)
         self.came = [self.grid.send(pick(line, (z + k) % 4, 0), Z, k) for k in range(1, 4)]
         return [line]
 
     def result(self):
-        total = self.own.astype(F32)
+        total = self.mine.astype(F32)
         for piece in self.came:
             total += piece.astype(F32)
         return total
@@ -722,7 +805,7 @@
     core = core.astype(jnp.int32)[None]
     vectors = [bias_q, bias_v, bias_out, gain_one, shift_one, bias_back, gain_two, shift_two]
     one = Gather(grid, pack_one(device.astype(jnp.int32)[None], w_qkv, w_out, vectors, bias_in), 2)
-    two = Gather(grid, after(pack_two(w_in, w_back), *one.ring), 4)
+    two = Gather(grid, pack_two(w_in, w_back), 4)
     one.one()
     one.two()
     two.one(*one.far)
@@ -730,9 +813,9 @@
     first = first.reshape(5, grid.count * rows, D)
     vec = jnp.sum(first[4].reshape(grid.count, rows, D).astype(F32), axis=0)
     qkv = qkv_call(tokens, first, vec)
-    two.two()
+    two.two(qkv)
     ctx, lse = attend_call(after(qkv, *two.near), lengths)
-    w_in, w_back = place(at, two.parts(), True)
+    w_in, w_back = place(at, two.parts(ctx), True)
     w_in = w_in.reshape(4, grid.count * rows, D)
     w_back = w_back.reshape(grid.count * span, D)
     z1, h1, g, slope, z2, low = ffn_call(tokens, ctx, first, vec, w_in, w_back, False)
@@ -751,46 +834,40 @@
     e2_1, e1_1, dz1, ea_1, dctx, sums_1 = ffn_back_call(grad, z2, z1, slope, w_back, w_in, first, vec)
     count = tokens.shape[0]
 
-    def by_heads(i, low2):
-        spec = pl.BlockSpec((1, count, WIDE), lambda i, n: (i, 0, 0))
-        return wgrad_call(core, low2, low1, heads_2[i][0], heads_1[i][0], rows, spec, 3, WIDE, True)
-
-    right = wgrad_back_call(core, g2, g1, e2_2, e2_1, rows)
-    spec = pl.BlockSpec((count, D), lambda i, n: (0, i))
-    left = wgrad_call(core, after(h2, right[0]), h1, e1_2, e1_1, rows, spec, 4, D, True)
-    wide = Sum(grid, where, left, right)
-    heads_1 = [attend_back_call(qkv, after(dctx, left[0]), lse, lengths, 0)]
-    steps = wide.one()
-    heads_1.append(attend_back_call(qkv, after(dctx, heads_1[0][0], *steps), lse, lengths, 1))
-    spec = pl.BlockSpec((count, WIDE), lambda i, n: (0, i))
-    right = wgrad_call(core, after(ctx2, heads_1[1][0]), ctx1, ea_2, ea_1, rows, spec, 2, WIDE, False)
-    left = by_heads(0, after(low2, right[0]))
-    group_0 = Sum(grid, where, left, right)
-    steps = wide.two()
-    left = by_heads(1, after(low2, left[0], *steps))
-    sums = sums_1 + sums_2
-    by_group = [[a + b for a, b in zip(heads_1[i][1:], heads_2[i][1:])] for i in range(GROUPS)]
-    line_q, line_v = [jnp.concatenate([jnp.sum(by_group[i][j], axis=0) for i in range(GROUPS)], axis=1) for j in range(2)]
-    small = jnp.concatenate([line_q, line_v, sums[2:12]], axis=0).astype(BF)
-    small = jnp.concatenate([small[:, :WIDE], small[:, WIDE:]], axis=0)
-    small = jnp.broadcast_to(small, (2, 2, 4, 1) + small.shape)
-    small = after(small, left[0])
-    group_1 = Sum(grid, where, left, (small, small))
-    steps = group_0.one(left[0]) + wide.three(left[0])
-    grad = dx_call(after(dz1, left[0], *steps), heads_1[0][0], heads_1[1][0], first, BF)
-    group_1.one()
-    group_0.two()
-    group_1.two()
-    group_0.three()
-    group_1.three()
-    total, half_0, half_1 = wide.result(), group_0.result(), group_1.result()
-
-    w_in_grad = total[:4].swapaxes(0, 1).reshape(rows, 4 * D)
-    w_back_grad = total[4:].reshape(4 * rows, D)
+    heads_1 = []
+    back = wgrad_back_call(core, g2, g1, e2_2, e2_1, rows)
+    sum_back = Sum(grid, where, (Y, X), back)
+    into = wgrad_in_call(core, after(h2, back[0]), h1, e1_2, e1_1, rows)
+    sum_in = Sum(grid, where, (X, Y), into)
+    steps = sum_back.one(into[0])
+    heads_1.append(attend_back_call(qkv, after(dctx, *steps), lse, lengths, 0))
+    steps = sum_in.one(heads_1[0][0])
+    heads_1.append(attend_back_call(qkv, after(dctx, *steps), lse, lengths, 1))
+    steps = sum_back.two(heads_1[1][0])
+    group = wgrad_heads_call(
+        core, after(low2, *steps), low1, heads_2[0][0], heads_1[0][0], rows, [ctx2, ctx1, ea_2, ea_1], False
+    )
+    sum_0 = Sum(grid, where, (Y, X), group)
+    steps = sum_in.two(group[0]) + sum_back.three(group[0])
+    lines = [heads[i][j] for i in range(GROUPS) for j in (1, 2) for heads in (heads_1, heads_2)]
+    group = wgrad_heads_call(
+        core, after(low2, *steps), low1, heads_2[1][0], heads_1[1][0], rows, [sums_1, sums_2, *lines], True
+    )
+    sum_1 = Sum(grid, where, (X, Y), group)
+    steps = sum_0.one(group[0]) + sum_1.one()
+    grad = dx_call(after(dz1, *steps), heads_1[0][0], heads_1[1][0], first, BF)
+    sum_in.three(grad)
+    sum_0.two(grad)
+    sum_1.two(grad)
+    sum_0.three()
+    sum_1.three()
+    total_in, total_back, half_0, half_1 = sum_in.result(), sum_back.result(), sum_0.result(), sum_1.result()
+
+    w_in_grad = total_in.swapaxes(0, 1).reshape(rows, 4 * D)
+    w_back_grad = total_back.reshape(4 * rows, D)
     w_qkv_grad = jnp.stack([half_0[:3], half_1[:3]], axis=1).transpose(2, 0, 1, 3).reshape(rows, 3 * D)
     w_out_grad = half_0[3:].swapaxes(0, 1).reshape(rows, D)
-    small = half_1[3]
-    small = jnp.concatenate([small[:12], small[12:]], axis=1)
+    small = jnp.concatenate([half_1[3][: rows // 2], half_1[3][rows // 2 :]], axis=1)
     mine = lax.dynamic_slice(small, (0, device * rows), (8, rows))
     per = D // span
     last = lax.dynamic_slice(small, (8 + device // per, device % per * span), (1, span))[0]

time: 936 us -> 450 us (0.48)
  Pallas kernels: 731 us -> 274 us
  waiting for transfers between devices: 113 us -> 85.9 us
    pallas_call x2, Pallas kernels: 469 us -> 14.5 us  [place(): pl.pallas_call(lambda *refs: place_body(split, *refs), grid_spec=pltpu.Pr...]
    ppermute x49 -> x46, waiting for transfers between devices: 113 us -> 85.9 us  [send(): return lax.ppermute(value, AXES, self.shift(dim, step))]
    ppermute x49 -> x46, starting transfers between devices: 55 us -> 57.1 us  [send(): return lax.ppermute(value, AXES, self.shift(dim, step))]
    pallas_call x4 -> x3, Pallas kernels: 40.3 us -> 39.2 us  [the longest x2 24 us: wgrad_heads_call(): pl.pallas_call(body, grid_spec=pltpu.PrefetchScalarGridSpec(num_scalar_pr...]
  transfers between devices with their start and end apart: 49 -> 46, of which waited for: 23 -> 23; matrix products, arithmetic and copies ran while one was open for 2% -> 5% of each run, Pallas kernels for 30% -> 23%
where the time goes in v4:
time: 450 us; the launch traced here: 447 us
  Pallas kernels  274 us (61%)
  waiting for transfers between devices  85.9 us (19%)
  starting transfers between devices  57.1 us (13%)
  other arithmetic  18.6 us (4%)
  local copies, waits for them, and re-layouts  8.94 us (2%)
    ppermute x46, waiting for transfers between devices, send(): return lax.ppermute(value, AXES, self.shift(dim, step))  85.9 us
    ppermute x46, starting transfers between devices, send(): return lax.ppermute(value, AXES, self.shift(dim, step))  57.1 us
    pallas_call x4, Pallas kernels, attend_back_call(): pl.pallas_call(body, grid_spec=pltpu.PrefetchScalarGridSpec(num_scalar_pr...  49.8 us
    pallas_call x2, Pallas kernels, ffn_back_call(): pl.pallas_call(ffn_back_body, grid=(rows // block,), in_specs=[line, line...  47.5 us
    pallas_call x2, Pallas kernels, ffn_call(): pl.pallas_call(lambda *refs: ffn_body(renorm, *refs), grid=(rows // block...  44.6 us
    pallas_call x2, Pallas kernels, attend_call(): pl.pallas_call(body, grid_spec=pltpu.PrefetchScalarGridSpec(num_scalar_pr...  25.9 us
    pallas_call x2, Pallas kernels, wgrad_heads_call(): pl.pallas_call(body, grid_spec=pltpu.PrefetchScalarGridSpec(num_scalar_pr...  24 us
    pallas_call x2, Pallas kernels, dx_call(): pl.pallas_call(dx_body, grid=(rows // block,), in_specs=[line, part, part...  18.8 us
  transfers between devices with their start and end apart: 46, of which 23 were waited for; matrix products, arithmetic and copies ran while one was open for 5% of the time, Pallas kernels for 23%

profile of v4, /device:TPU:0, one launch (start us, length us, event | category | flops | bytes accessed | tf_op | source)
XLA Modules:
  0.0 446.6 jit_solution(7967239086409072066)
XLA Ops:
  0.7 1.8 pack_one.1
  2.4 3.0 collective-permute-start
  5.4 2.6 collective-permute-start.1
  9.4 3.9 collective-permute-done
  13.2 7.1 %collective-permute-done.1 = bf16[5,24,768]{2,1,0:T(8,128)(2,1)S(1)} collective-permute-done((bf16[5,24,768]{2,1,0:T(8,128)(2,1)}, bf16[5,24,768]{2,1,0:T(8,128)(2,1)S(1)}, u32[]{:S(2)}, u32[]{:S(2)}) %collective-permute-start.1) | collective-permute-done | bytes 184352 | tf_op jit(solution)/shard_map/ppermute | solution.py:602
  21.3 1.6 collective-permute-start.4
  23.8 1.6 collective-permute-start.3
  25.4 8.0 %collective-permute-done.4 = bf16[4,3,24,768]{3,2,1,0:T(8,128)(2,1)S(1)} collective-permute-done((bf16[4,3,24,768]{3,2,1,0:T(8,128)(2,1)S(1)}, bf16[4,3,24,768]{3,2,1,0:T(8,128)(2,1)S(1)}, u32[]{:S(2)}, u32[]{:S(2)}) %collective-permute-start.4) | collective-permute-done | bytes 442400 | tf_op jit(solution)/shard_map/ppermute | solution.py:602
  33.5 1.6 collective-permute-start.6
  35.1 1.6 collective-permute-start.5
  36.7 1.7 pack_two.1
  38.4 4.5 %collective-permute-start.11 = (bf16[8,24,768]{2,1,0:T(8,128)(2,1)}, bf16[8,24,768]{2,1,0:T(8,128)(2,1)S(1)}, u32[]{:S(2)}, u32[]{:S(2)}) collective-permute-start(bf16[8,24,768]{2,1,0:T(8,128)(2,1)} %pack_two.1), channel_id=1, source_target_pairs={{0,2},{1,3},{2,4},{3,5},{4,6},{5,7},{6,0},{7,1},{8,10},{9,11},{10,... | collective-permute-start | bytes 884744 | tf_op jit(solution)/shard_map/ppermute | solution.py:602
  43.5 1.8 collective-permute-start.13
  45.3 5.8 %collective-permute-done.11 = bf16[8,24,768]{2,1,0:T(8,128)(2,1)S(1)} collective-permute-done((bf16[8,24,768]{2,1,0:T(8,128)(2,1)}, bf16[8,24,768]{2,1,0:T(8,128)(2,1)S(1)}, u32[]{:S(2)}, u32[]{:S(2)}) %collective-permute-start.11) | collective-permute-done | bytes 294944 | tf_op jit(solution)/shard_map/ppermute | solution.py:602
  51.1 9.4 %collective-permute-done.12 = bf16[8,24,768]{2,1,0:T(8,128)(2,1)S(1)} collective-permute-done((bf16[8,24,768]{2,1,0:T(8,128)(2,1)}, bf16[8,24,768]{2,1,0:T(8,128)(2,1)S(1)}, u32[]{:S(2)}, u32[]{:S(2)}) %collective-permute-start.12) | collective-permute-done | bytes 294944 | tf_op jit(solution)/shard_map/ppermute | solution.py:602
  61.0 1.4 slice_bitcast_fusion.3
  64.4 2.2 collective-permute-done.7.refs_2_
  68.5 6.2 %place.2 = bf16[5,2,2,4,2,24,768]{6,5,4,3,2,1,0:T(8,128)(2,1)} custom-call(s32[4]{0:T(128)} %pad_add_fusion.refs_0_, bf16[2,4,2,24,768]{4,3,2,1,0:T(8,128)(2,1)} %copy-done.3, bf16[2,4,2,24,768]{4,3,2,1,0:T(8,128)(2,1)} %copy-done.14, bf16[2,4,2,24,768]{4,3,2,1,0:T(8,128)(2,1)} %copy-done.13, bf16[2,4,2,24,768]{4,3,2,1,0:T(8,128)(2,1)} %collective-permute-done.8.refs_4_, ...), custom_call_target="tpu_custom_call" | custom-call | flops 1 | bytes 1 | tf_op jit(solution)/shard_map/place/pallas_call | solution.py:711
  74.7 2.1 convert_reduce_fusion.vec_ref.refs_2_
  76.8 7.8 %qkv.2.refs_1_.refs_2_.refs_3_ = bf16[1024,2304]{1,0:T(8,128)(2,1)} custom-call(bf16[1024,768]{1,0:T(8,128)(2,1)} %c_ref.3, bf16[5,768,768]{2,1,0:T(8,128)(2,1)} %bitcast.162, f32[24,768]{1,0:T(8,128)} %convert_reduce_fusion.vec_ref.refs_2_), custom_call_target="tpu_custom_call" | custom-call | flops 1 | bytes 1 | tf_op jit(solution)/shard_map/qkv/pallas_call | solution.py:66
  85.8 1.6 collective-permute-start.17
  89.2 12.9 %attend.2 = (bf16[1024,768]{1,0:T(8,128)(2,1)}, f32[2,6,2,512]{3,2,1,0:T(2,128)}) custom-call(s32[2]{0:T(128)} %refs_0_.13, bf16[1024,2304]{1,0:T(8,128)(2,1)} %qkv.2.refs_1_.refs_2_.refs_3_, bf16[1024,2304]{1,0:T(8,128)(2,1)} %qkv.2.refs_1_.refs_2_.refs_3_, bf16[1024,2304]{1,0:T(8,128)(2,1)} %qkv.2.refs_1_.refs_2_.refs_3_), custom_call_target="tpu_custom_call" | custom-call | flops 1 | bytes 1 | tf_op jit(solution)/shard_map/attend/pallas_call | solution.py:124
  102.1 11.5 %collective-permute-done.17.refs_7_ = bf16[2,4,4,24,768]{4,3,2,1,0:T(8,128)(2,1)S(1)} collective-permute-done((bf16[2,4,4,24,768]{4,3,2,1,0:T(8,128)(2,1)S(1)}, bf16[2,4,4,24,768]{4,3,2,1,0:T(8,128)(2,1)S(1)}, u32[]{:S(2)}, u32[]{:S(2)}) %collective-permute-start.17) | collective-permute-done | bytes 1179680 | tf_op jit(solution)/shard_map/ppermute | solution.py:602
  113.6 2.5 collective-permute-done.16.refs_3_
  117.1 1.8 collective-permute-done.18.refs_2_
  119.0 3.4 collective-permute-done.19.refs_4_
  122.3 1.7 collective-permute-done.20.refs_6_
  125.1 8.2 %place.3 = (bf16[4,2,2,4,2,24,768]{6,5,4,3,2,1,0:T(8,128)(2,1)}, bf16[2,2,4,2,4,24,768]{6,5,4,3,2,1,0:T(8,128)(2,1)}) custom-call(s32[4]{0:T(128)} %pad_add_fusion.refs_0_, bf16[2,4,4,24,768]{4,3,2,1,0:T(8,128)(2,1)} %copy-done.1, bf16[2,4,4,24,768]{4,3,2,1,0:T(8,128)(2,1)} %copy-done.8, bf16[2,4,4,24,768]{4,3,2,1,0:T(8,128)(2,1)} %copy-done.7, ...), custom_call_target="tpu_custom_call" | custom-call | flops 1 | bytes 1 | tf_op jit(solution)/shard_map/place/pallas_call | solution.py:711
  133.3 22.1 %ffn.2 = (f32[1024,768]{1,0:T(8,128)}, bf16[1024,768]{1,0:T(8,128)(2,1)}, bf16[1024,3072]{1,0:T(8,128)(2,1)}, bf16[1024,3072]{1,0:T(8,128)(2,1)}, f32[1024,768]{1,0:T(8,128)}, /*index=5*/bf16[1024,768]{1,0:T(8,128)(2,1)}) custom-call(bf16[1024,768]{1,0:T(8,128)(2,1)} %c_ref.3, bf16[1024,768]{1,0:T(8,128)(2,1)} %get-tuple-element.118.refs_1_.rest_1_, ...), custom_call_target="tpu_custom_call" | custom-call | flops 1 | bytes 1 | tf_op jit(solution)/shard_map/ffn/pallas_call | solution.py:224
  155.4 7.9 %qkv.3.refs_1_.refs_2_.refs_3_ = bf16[1024,2304]{1,0:T(8,128)(2,1)} custom-call(bf16[1024,768]{1,0:T(8,128)(2,1)} %get-tuple-element.168.x_ref.a_ref, bf16[5,768,768]{2,1,0:T(8,128)(2,1)} %bitcast.164, f32[24,768]{1,0:T(8,128)} %convert_reduce_fusion.vec_ref.refs_2_), custom_call_target="tpu_custom_call" | custom-call | flops 1 | bytes 1 | tf_op jit(solution)/shard_map/qkv/pallas_call | solution.py:66
  163.3 13.0 %attend.3 = (bf16[1024,768]{1,0:T(8,128)(2,1)}, f32[2,6,2,512]{3,2,1,0:T(2,128)}) custom-call(s32[2]{0:T(128)} %refs_0_.13, bf16[1024,2304]{1,0:T(8,128)(2,1)} %qkv.3.refs_1_.refs_2_.refs_3_, bf16[1024,2304]{1,0:T(8,128)(2,1)} %qkv.3.refs_1_.refs_2_.refs_3_, bf16[1024,2304]{1,0:T(8,128)(2,1)} %qkv.3.refs_1_.refs_2_.refs_3_), custom_call_target="tpu_custom_call" | custom-call | flops 1 | bytes 1 | tf_op jit(solution)/shard_map/attend/pallas_call | solution.py:124
  176.3 22.5 %ffn.3 = (f32[1024,768]{1,0:T(8,128)}, bf16[1024,768]{1,0:T(8,128)(2,1)}, bf16[1024,3072]{1,0:T(8,128)(2,1)}, bf16[1024,3072]{1,0:T(8,128)(2,1)}, f32[1024,768]{1,0:T(8,128)}, /*index=5*/bf16[1024,768]{1,0:T(8,128)(2,1)}) custom-call(f32[1024,768]{1,0:T(8,128)} %get-tuple-element.125.refs_0_.z2_ref, bf16[1024,768]{1,0:T(8,128)(2,1)} %get-tuple-element.127.refs_1_.rest_0_, ...), custom_call_target="tpu_custom_call" | custom-call | flops 1 | bytes 1 | tf_op jit(solution)/shard_map/ffn/pallas_call | solution.py:224
  198.8 23.8 %ffn_back.2 = (bf16[1024,768]{1,0:T(8,128)(2,1)}, bf16[1024,3072]{1,0:T(8,128)(2,1)}, f32[1024,768]{1,0:T(8,128)}, bf16[1024,768]{1,0:T(8,128)(2,1)}, bf16[1024,768]{1,0:T(8,128)(2,1)}, /*index=5*/f32[24,768]{1,0:T(8,128)}) custom-call(bf16[1024,768]{1,0:T(8,128)(2,1)} %dy_ref.1, f32[1024,768]{1,0:T(8,128)} %get-tuple-element.129.z2_ref, ...), custom_call_target="tpu_custom_call" | custom-call | flops 1 | bytes 1 | tf_op jit(solution)/shard_map/ffn_back/pallas_call | solution.py:306
  222.6 12.3 %attend_back.5 = (bf16[3,1024,384]{2,1,0:T(8,128)(2,1)}, f32[2,1,384]{2,1,0:T(1,128)}, f32[2,1,384]{2,1,0:T(1,128)}) custom-call(s32[2]{0:T(128)} %refs_0_.13, bf16[1024,2304]{1,0:T(8,128)(2,1)} %qkv.3.refs_1_.refs_2_.refs_3_, bf16[1024,2304]{1,0:T(8,128)(2,1)} %qkv.3.refs_1_.refs_2_.refs_3_, bf16[1024,2304]{1,0:T(8,128)(2,1)} %qkv.3.refs_1_.refs_2_.refs_3_, ...), custom_call_target="tpu_custom_call" | custom-call | flops 1 | bytes 1 | tf_op jit(solution)/shard_map/attend_back/pallas_call | solution.py:382
  234.9 12.5 %attend_back.4 = (bf16[3,1024,384]{2,1,0:T(8,128)(2,1)}, f32[2,1,384]{2,1,0:T(1,128)}, f32[2,1,384]{2,1,0:T(1,128)}) custom-call(s32[2]{0:T(128)} %refs_0_.13, bf16[1024,2304]{1,0:T(8,128)(2,1)} %qkv.3.refs_1_.refs_2_.refs_3_, bf16[1024,2304]{1,0:T(8,128)(2,1)} %qkv.3.refs_1_.refs_2_.refs_3_, bf16[1024,2304]{1,0:T(8,128)(2,1)} %qkv.3.refs_1_.refs_2_.refs_3_, ...), custom_call_target="tpu_custom_call" | custom-call | flops 1 | bytes 1 | tf_op jit(solution)/shard_map/attend_back/pallas_call | solution.py:382
  247.4 9.6 %dx.2.dy_ref = f32[1024,768]{1,0:T(8,128)} custom-call(f32[1024,768]{1,0:T(8,128)} %get-tuple-element.132.dz1_ref, bf16[3,1024,384]{2,1,0:T(8,128)(2,1)} %get-tuple-element.135.e0_ref.b_ref, bf16[3,1024,384]{2,1,0:T(8,128)(2,1)} %get-tuple-element.136.e1_ref.b_ref, bf16[5,768,768]{2,1,0:T(8,128)(2,1)} %bitcast.167), custom_call_target="tpu_custom_call" | custom-call | flops 1 | bytes 1 | tf_op jit(solution)/shard_map/dx/pallas_call | solution.py:415
  257.0 23.7 %ffn_back.3 = (bf16[1024,768]{1,0:T(8,128)(2,1)}, bf16[1024,3072]{1,0:T(8,128)(2,1)}, f32[1024,768]{1,0:T(8,128)}, bf16[1024,768]{1,0:T(8,128)(2,1)}, bf16[1024,768]{1,0:T(8,128)(2,1)}, /*index=5*/f32[24,768]{1,0:T(8,128)}) custom-call(f32[1024,768]{1,0:T(8,128)} %dx.2.dy_ref, f32[1024,768]{1,0:T(8,128)} %get-tuple-element.125.refs_0_.z2_ref, ...), custom_call_target="tpu_custom_call" | custom-call | flops 1 | bytes 1 | tf_op jit(solution)/shard_map/ffn_back/pallas_call | solution.py:306
  280.6 15.0 %wgrad_back.1 = (bf16[2,2,4,4,24,768]{5,4,3,2,1,0:T(8,128)(2,1)}, bf16[2,2,4,4,24,768]{5,4,3,2,1,0:T(8,128)(2,1)}) custom-call(s32[1]{0:T(128)} %bitcast.1.core_ref, bf16[1024,3072]{1,0:T(8,128)(2,1)} %get-tuple-element.140.g2k.g2s, bf16[1024,3072]{1,0:T(8,128)(2,1)} %get-tuple-element.141.g1k.g1s, bf16[1024,3072]{1,0:T(8,128)(2,1)} %get-tuple-element.140.g2k.g2s, ...), custom_call_target="tpu_custom_call" | custom-call | flops 1 | bytes 1 | tf_op jit(solution)/shard_map/wgrad_back/pallas_call | solution.py:556
  295.8 15.2 %wgrad_in.1 = (bf16[2,2,4,4,24,768]{5,4,3,2,1,0:T(8,128)(2,1)}, bf16[2,2,4,4,24,768]{5,4,3,2,1,0:T(8,128)(2,1)}) custom-call(s32[1]{0:T(128)} %bitcast.1.core_ref, bf16[1024,768]{1,0:T(8,128)(2,1)} %get-tuple-element.146.a_ref, bf16[1024,768]{1,0:T(8,128)(2,1)} %get-tuple-element.147.c_ref, bf16[1024,3072]{1,0:T(8,128)(2,1)} %get-tuple-element.148.b_ref, ...), custom_call_target="tpu_custom_call" | custom-call | flops 1 | bytes 1 | tf_op jit(solution)/shard_map/wgrad_in/pallas_call | solution.py:456
  311.4 4.1 fusion
  316.1 12.5 %attend_back.6 = (bf16[3,1024,384]{2,1,0:T(8,128)(2,1)}, f32[2,1,384]{2,1,0:T(1,128)}, f32[2,1,384]{2,1,0:T(1,128)}) custom-call(s32[2]{0:T(128)} %refs_0_.13, bf16[1024,2304]{1,0:T(8,128)(2,1)} %qkv.2.refs_1_.refs_2_.refs_3_, bf16[1024,2304]{1,0:T(8,128)(2,1)} %qkv.2.refs_1_.refs_2_.refs_3_, bf16[1024,2304]{1,0:T(8,128)(2,1)} %qkv.2.refs_1_.refs_2_.refs_3_, ...), custom_call_target="tpu_custom_call" | custom-call | flops 1 | bytes 1 | tf_op jit(solution)/shard_map/attend_back/pallas_call | solution.py:382
  329.9 12.6 %attend_back.7 = (bf16[3,1024,384]{2,1,0:T(8,128)(2,1)}, f32[2,1,384]{2,1,0:T(1,128)}, f32[2,1,384]{2,1,0:T(1,128)}) custom-call(s32[2]{0:T(128)} %refs_0_.13, bf16[1024,2304]{1,0:T(8,128)(2,1)} %qkv.2.refs_1_.refs_2_.refs_3_, bf16[1024,2304]{1,0:T(8,128)(2,1)} %qkv.2.refs_1_.refs_2_.refs_3_, bf16[1024,2304]{1,0:T(8,128)(2,1)} %qkv.2.refs_1_.refs_2_.refs_3_, ...), custom_call_target="tpu_custom_call" | custom-call | flops 1 | bytes 1 | tf_op jit(solution)/shard_map/attend_back/pallas_call | solution.py:382
  343.8 1.5 fusion.7
  345.9 14.6 %wgrad_heads.2 = (bf16[2,2,4,5,24,384]{5,4,3,2,1,0:T(8,128)(2,1)}, bf16[2,2,4,5,24,384]{5,4,3,2,1,0:T(8,128)(2,1)}) custom-call(s32[1]{0:T(128)} %bitcast.1.core_ref, bf16[1024,768]{1,0:T(8,128)(2,1)} %get-tuple-element.168.x_ref.a_ref, bf16[1024,768]{1,0:T(8,128)(2,1)} %c_ref.3, bf16[3,1024,384]{2,1,0:T(8,128)(2,1)} %get-tuple-element.135.e0_ref.b_ref, ...), custom_call_target="tpu_custom_call" | custom-call | flops 1 | bytes 1 | tf_op jit(solution)/shard_map/wgrad_heads/pallas_call | solution.py:520
  361.6 8.1 %collective-permute-done.26 = bf16[4,4,24,768]{3,2,1,0:T(8,128)(2,1)S(1)} collective-permute-done((bf16[4,4,24,768]{3,2,1,0:T(8,128)(2,1)S(1)}, bf16[4,4,24,768]{3,2,1,0:T(8,128)(2,1)S(1)}, u32[]{:S(2)}, u32[]{:S(2)}) %collective-permute-start.26) | collective-permute-done | bytes 589856 | tf_op jit(solution)/shard_map/ppermute | solution.py:602
  369.8 9.4 %wgrad_heads.3 = (bf16[2,2,4,4,24,384]{5,4,3,2,1,0:T(8,128)(2,1)}, bf16[2,2,4,4,24,384]{5,4,3,2,1,0:T(8,128)(2,1)}) custom-call(s32[1]{0:T(128)} %bitcast.1.core_ref, bf16[1024,768]{1,0:T(8,128)(2,1)} %get-tuple-element.168.x_ref.a_ref, bf16[1024,768]{1,0:T(8,128)(2,1)} %c_ref.3, bf16[3,1024,384]{2,1,0:T(8,128)(2,1)} %get-tuple-element.136.e1_ref.b_ref, ...), custom_call_target="tpu_custom_call" | custom-call | flops 1 | bytes 1 | tf_op jit(solution)/shard_map/wgrad_heads/pallas_call | solution.py:520
  379.3 1.5 collective-permute-start.39
  381.5 6.6 %collective-permute-start.43 = (bf16[4,24,768]{2,1,0:T(8,128)(2,1)}, bf16[4,24,768]{2,1,0:T(8,128)(2,1)S(1)}, u32[]{:S(2)}, u32[]{:S(2)}) collective-permute-start(bf16[4,24,768]{2,1,0:T(8,128)(2,1)} %get-tuple-element.203), channel_id=1, source_target_pairs={{0,2},{1,3},{2,4},{3,5},{4,6},{5,7},{6,0},{7,1},{8,10},{9,11},{10,... | collective-permute-start | bytes 442376 | tf_op jit(solution)/shard_map/ppermute | solution.py:602
  388.1 3.3 collective-permute-start.44
  391.4 1.8 fusion.5
  393.9 1.5 fusion.11
  395.4 9.3 %dx.3 = bf16[1024,768]{1,0:T(8,128)(2,1)} custom-call(f32[1024,768]{1,0:T(8,128)} %get-tuple-element.183.dz1_ref, bf16[3,1024,384]{2,1,0:T(8,128)(2,1)} %get-tuple-element.156.d_ref.e0_ref, bf16[3,1024,384]{2,1,0:T(8,128)(2,1)} %get-tuple-element.160.d_ref.e1_ref, bf16[5,768,768]{2,1,0:T(8,128)(2,1)} %bitcast.169), custom_call_target="tpu_custom_call" | custom-call | flops 1 | bytes 1 | tf_op jit(solution)/shard_map/dx/pallas_call | solution.py:415
  405.4 2.0 collective-permute-start.40
  407.5 2.4 collective-permute-start.42
  412.4 1.8 collective-permute-done.40
  414.2 4.3 collective-permute-done.41
  419.3 1.7 collective-permute-done.34
  421.1 1.5 collective-permute-start.35
  422.6 4.6 %collective-permute-done.30 = bf16[4,5,24,384]{3,2,1,0:T(8,128)(2,1)S(1)} collective-permute-done((bf16[4,5,24,384]{3,2,1,0:T(8,128)(2,1)S(1)}, bf16[4,5,24,384]{3,2,1,0:T(8,128)(2,1)S(1)}, u32[]{:S(2)}, u32[]{:S(2)}) %collective-permute-start.30) | collective-permute-done | bytes 368672 | tf_op jit(solution)/shard_map/ppermute | solution.py:602
  427.3 1.7 collective-permute-start.31
  429.0 2.5 collective-permute-start.32
  431.8 1.9 collective-permute-start.36
  434.7 3.2 collective-permute-start.38
  439.9 4.0 collective-permute-done.37
  (130 shorter events, 30.3 us)
Async XLA Ops:
  2.4 10.8 %collective-permute-start = (bf16[5,24,768]{2,1,0:T(8,128)(2,1)}, bf16[5,24,768]{2,1,0:T(8,128)(2,1)S(1)}, u32[]{:S(2)}, u32[]{:S(2)}) collective-permute-start(bf16[5,24,768]{2,1,0:T(8,128)(2,1)} %pack_one.1), channel_id=1, source_target_pairs={{0,2},{1,3},{2,4},{3,5},{4,6},{5,7},{6,0},{7,1},{8,10},{9,11},{10,... | collective-permute-start | bytes 552968 | tf_op jit(solution)/shard_map/ppermute | solution.py:602
  5.4 14.9 %collective-permute-start.1 = (bf16[5,24,768]{2,1,0:T(8,128)(2,1)}, bf16[5,24,768]{2,1,0:T(8,128)(2,1)S(1)}, u32[]{:S(2)}, u32[]{:S(2)}) collective-permute-start(bf16[5,24,768]{2,1,0:T(8,128)(2,1)} %pack_one.1), channel_id=1, source_target_pairs={{0,4},{1,5},{2,6},{3,7},{4,0},{5,1},{6,2},{7,3},{8,12},{9,13},{10,... | collective-permute-start | bytes 552968 | tf_op jit(solution)/shard_map/ppermute | solution.py:602
  8.0 12.3 %collective-permute-start.2 = (bf16[5,24,768]{2,1,0:T(8,128)(2,1)}, bf16[5,24,768]{2,1,0:T(8,128)(2,1)S(1)}, u32[]{:S(2)}, u32[]{:S(2)}) collective-permute-start(bf16[5,24,768]{2,1,0:T(8,128)(2,1)} %pack_one.1), channel_id=1, source_target_pairs={{0,6},{1,7},{2,0},{3,1},{4,2},{5,3},{6,4},{7,5},{8,14},{9,15},{10,... | collective-permute-start | bytes 552968 | tf_op jit(solution)/shard_map/ppermute | solution.py:602
  21.3 12.1 %collective-permute-start.4 = (bf16[4,3,24,768]{3,2,1,0:T(8,128)(2,1)S(1)}, bf16[4,3,24,768]{3,2,1,0:T(8,128)(2,1)S(1)}, u32[]{:S(2)}, u32[]{:S(2)}) collective-permute-start(bf16[4,3,24,768]{3,2,1,0:T(8,128)(2,1)S(1)} %pad_maximum_fusion.6), channel_id=1, source_target_pairs={{0,16},{1,17},{2,18},{3,19},{4,20},{5,21},{6,22},{7,23},{8,24},{9,... | collective-permute-start | bytes 1327112 | tf_op jit(solution)/shard_map/ppermute | solution.py:602
  23.8 11.2 %collective-permute-start.3 = (bf16[4,2,24,768]{3,2,1,0:T(8,128)(2,1)S(1)}, bf16[4,2,24,768]{3,2,1,0:T(8,128)(2,1)S(1)}, u32[]{:S(2)}, u32[]{:S(2)}) collective-permute-start(bf16[4,2,24,768]{3,2,1,0:T(8,128)(2,1)S(1)} %pad_maximum_fusion.7), channel_id=1, source_target_pairs={{0,1},{1,0},{2,3},{3,2},{4,5},{5,4},{6,7},{7,6},{8,9},{9,8},{10,11... | collective-permute-start | bytes 884744 | tf_op jit(solution)/shard_map/ppermute | solution.py:602
  33.5 29.0 %copy-start.2 = (bf16[2,4,3,24,768]{4,3,2,1,0:T(8,128)(2,1)}, bf16[2,4,3,24,768]{4,3,2,1,0:T(8,128)(2,1)S(1)}, u32[]{:S(2)}) copy-start(bf16[2,4,3,24,768]{4,3,2,1,0:T(8,128)(2,1)S(1)} %pad_maximum_fusion.2.refs_5_) | copy-start | bytes 2654212
  33.5 27.5 %collective-permute-start.6 = (bf16[2,4,3,24,768]{4,3,2,1,0:T(8,128)(2,1)S(1)}, bf16[2,4,3,24,768]{4,3,2,1,0:T(8,128)(2,1)S(1)}, u32[]{:S(2)}, u32[]{:S(2)}) collective-permute-start(bf16[2,4,3,24,768]{4,3,2,1,0:T(8,128)(2,1)S(1)} %pad_maximum_fusion.2.refs_5_), channel_id=1, source_target_pairs={{0,1},{1,0},{2,3},{3,2},{4,5},{5,4},{6,7},{7,6},{8,9},{9,8},{10,11... | collective-permute-start | bytes 2654216 | tf_op jit(solution)/shard_map/ppermute | solution.py:602
  35.1 28.4 %copy-start.3 = (bf16[2,4,2,24,768]{4,3,2,1,0:T(8,128)(2,1)}, bf16[2,4,2,24,768]{4,3,2,1,0:T(8,128)(2,1)S(1)}, u32[]{:S(2)}) copy-start(bf16[2,4,2,24,768]{4,3,2,1,0:T(8,128)(2,1)S(1)} %pad_maximum_fusion.3.refs_1_) | copy-start | bytes 1769476
  35.1 25.8 %collective-permute-start.5 = (bf16[2,4,2,24,768]{4,3,2,1,0:T(8,128)(2,1)S(1)}, bf16[2,4,2,24,768]{4,3,2,1,0:T(8,128)(2,1)S(1)}, u32[]{:S(2)}, u32[]{:S(2)}) collective-permute-start(bf16[2,4,2,24,768]{4,3,2,1,0:T(8,128)(2,1)S(1)} %pad_maximum_fusion.3.refs_1_), channel_id=1, source_target_pairs={{0,16},{1,17},{2,18},{3,19},{4,20},{5,21},{6,22},{7,23},{8,24},{9,... | collective-permute-start | bytes 1769480 | tf_op jit(solution)/shard_map/ppermute | solution.py:602
  38.4 12.7 %collective-permute-start.11 = (bf16[8,24,768]{2,1,0:T(8,128)(2,1)}, bf16[8,24,768]{2,1,0:T(8,128)(2,1)S(1)}, u32[]{:S(2)}, u32[]{:S(2)}) collective-permute-start(bf16[8,24,768]{2,1,0:T(8,128)(2,1)} %pack_two.1), channel_id=1, source_target_pairs={{0,2},{1,3},{2,4},{3,5},{4,6},{5,7},{6,0},{7,1},{8,10},{9,11},{10,... | collective-permute-start | bytes 884744 | tf_op jit(solution)/shard_map/ppermute | solution.py:602
  42.9 17.6 %collective-permute-start.12 = (bf16[8,24,768]{2,1,0:T(8,128)(2,1)}, bf16[8,24,768]{2,1,0:T(8,128)(2,1)S(1)}, u32[]{:S(2)}, u32[]{:S(2)}) collective-permute-start(bf16[8,24,768]{2,1,0:T(8,128)(2,1)} %pack_two.1), channel_id=1, source_target_pairs={{0,4},{1,5},{2,6},{3,7},{4,0},{5,1},{6,2},{7,3},{8,12},{9,13},{10,... | collective-permute-start | bytes 884744 | tf_op jit(solution)/shard_map/ppermute | solution.py:602
  43.5 17.5 %collective-permute-start.13 = (bf16[8,24,768]{2,1,0:T(8,128)(2,1)}, bf16[8,24,768]{2,1,0:T(8,128)(2,1)S(1)}, u32[]{:S(2)}, u32[]{:S(2)}) collective-permute-start(bf16[8,24,768]{2,1,0:T(8,128)(2,1)} %pack_two.1), channel_id=1, source_target_pairs={{0,6},{1,7},{2,0},{3,1},{4,2},{5,3},{6,4},{7,5},{8,14},{9,15},{10,... | collective-permute-start | bytes 884744 | tf_op jit(solution)/shard_map/ppermute | solution.py:602
  61.0 2.7 copy-start.13
  61.0 2.7 copy-start.12
  62.4 6.1 %collective-permute-start.10 = (bf16[2,4,3,24,768]{4,3,2,1,0:T(8,128)(2,1)S(1)}, bf16[2,4,3,24,768]{4,3,2,1,0:T(8,128)(2,1)}, u32[]{:S(2)}, u32[]{:S(2)}) collective-permute-start(bf16[2,4,3,24,768]{4,3,2,1,0:T(8,128)(2,1)S(1)} %collective-permute-done.6.refs_7_), channel_id=1, source_target_pairs={{0,8},{1,9},{2,10},{3,11},{4,12},{5,13},{6,14},{7,15},{8,0},{9,1},... | collective-permute-start | bytes 2654216 | tf_op jit(solution)/shard_map/ppermute | solution.py:602
  62.5 6.0 %collective-permute-start.9 = (bf16[2,4,3,24,768]{4,3,2,1,0:T(8,128)(2,1)S(1)}, bf16[2,4,3,24,768]{4,3,2,1,0:T(8,128)(2,1)}, u32[]{:S(2)}, u32[]{:S(2)}) collective-permute-start(bf16[2,4,3,24,768]{4,3,2,1,0:T(8,128)(2,1)S(1)} %pad_maximum_fusion.2.refs_5_), channel_id=1, source_target_pairs={{0,8},{1,9},{2,10},{3,11},{4,12},{5,13},{6,14},{7,15},{8,0},{9,1},... | collective-permute-start | bytes 2654216 | tf_op jit(solution)/shard_map/ppermute | solution.py:602
  63.0 3.6 collective-permute-start.7
  63.1 5.4 %collective-permute-start.8 = (bf16[2,4,2,24,768]{4,3,2,1,0:T(8,128)(2,1)S(1)}, bf16[2,4,2,24,768]{4,3,2,1,0:T(8,128)(2,1)}, u32[]{:S(2)}, u32[]{:S(2)}) collective-permute-start(bf16[2,4,2,24,768]{4,3,2,1,0:T(8,128)(2,1)S(1)} %collective-permute-done.5.refs_3_), channel_id=1, source_target_pairs={{0,8},{1,9},{2,10},{3,11},{4,12},{5,13},{6,14},{7,15},{8,0},{9,1},... | collective-permute-start | bytes 1769480 | tf_op jit(solution)/shard_map/ppermute | solution.py:602
  63.7 20.9 %collective-permute-start.15 = (bf16[4,4,24,768]{3,2,1,0:T(8,128)(2,1)S(1)}, bf16[4,4,24,768]{3,2,1,0:T(8,128)(2,1)}, u32[]{:S(2)}, u32[]{:S(2)}) collective-permute-start(bf16[4,4,24,768]{3,2,1,0:T(8,128)(2,1)S(1)} %pad_maximum_fusion.5), channel_id=1, source_target_pairs={{0,16},{1,17},{2,18},{3,19},{4,20},{5,21},{6,22},{7,23},{8,24},{9,... | collective-permute-start | bytes 1769480 | tf_op jit(solution)/shard_map/ppermute | solution.py:602
  66.6 0.8 copy-start.14
  67.4 20.0 %collective-permute-start.14 = (bf16[4,4,24,768]{3,2,1,0:T(8,128)(2,1)S(1)}, bf16[4,4,24,768]{3,2,1,0:T(8,128)(2,1)}, u32[]{:S(2)}, u32[]{:S(2)}) collective-permute-start(bf16[4,4,24,768]{3,2,1,0:T(8,128)(2,1)S(1)} %pad_maximum_fusion.4), channel_id=1, source_target_pairs={{0,1},{1,0},{2,3},{3,2},{4,5},{5,4},{6,7},{7,6},{8,9},{9,8},{10,11... | collective-permute-start | bytes 1769480 | tf_op jit(solution)/shard_map/ppermute | solution.py:602
  85.8 30.8 %copy-start = (bf16[2,4,4,24,768]{4,3,2,1,0:T(8,128)(2,1)}, bf16[2,4,4,24,768]{4,3,2,1,0:T(8,128)(2,1)S(1)}, u32[]{:S(2)}) copy-start(bf16[2,4,4,24,768]{4,3,2,1,0:T(8,128)(2,1)S(1)} %pad_maximum_fusion.1.refs_5_) | copy-start | bytes 3538948
  85.8 27.8 %collective-permute-start.17 = (bf16[2,4,4,24,768]{4,3,2,1,0:T(8,128)(2,1)S(1)}, bf16[2,4,4,24,768]{4,3,2,1,0:T(8,128)(2,1)S(1)}, u32[]{:S(2)}, u32[]{:S(2)}) collective-permute-start(bf16[2,4,4,24,768]{4,3,2,1,0:T(8,128)(2,1)S(1)} %pad_maximum_fusion.1.refs_5_), channel_id=1, source_target_pairs={{0,1},{1,0},{2,3},{3,2},{4,5},{5,4},{6,7},{7,6},{8,9},{9,8},{10,11... | collective-permute-start | bytes 3538952 | tf_op jit(solution)/shard_map/ppermute | solution.py:602
  88.6 27.5 %copy-start.1 = (bf16[2,4,4,24,768]{4,3,2,1,0:T(8,128)(2,1)}, bf16[2,4,4,24,768]{4,3,2,1,0:T(8,128)(2,1)S(1)}, u32[]{:S(2)}) copy-start(bf16[2,4,4,24,768]{4,3,2,1,0:T(8,128)(2,1)S(1)} %pad_maximum_fusion.refs_1_) | copy-start | bytes 3538948
  88.6 27.5 %collective-permute-start.16 = (bf16[2,4,4,24,768]{4,3,2,1,0:T(8,128)(2,1)S(1)}, bf16[2,4,4,24,768]{4,3,2,1,0:T(8,128)(2,1)S(1)}, u32[]{:S(2)}, u32[]{:S(2)}) collective-permute-start(bf16[2,4,4,24,768]{4,3,2,1,0:T(8,128)(2,1)S(1)} %pad_maximum_fusion.refs_1_), channel_id=1, source_target_pairs={{0,16},{1,17},{2,18},{3,19},{4,20},{5,21},{6,22},{7,23},{8,24},{9,... | collective-permute-start | bytes 3538952 | tf_op jit(solution)/shard_map/ppermute | solution.py:602
  113.6 10.4 %copy-start.6 = (bf16[2,4,4,24,768]{4,3,2,1,0:T(8,128)(2,1)}, bf16[2,4,4,24,768]{4,3,2,1,0:T(8,128)(2,1)S(1)}, u32[]{:S(2)}) copy-start(bf16[2,4,4,24,768]{4,3,2,1,0:T(8,128)(2,1)S(1)} %collective-permute-done.17.refs_7_) | copy-start | bytes 3538948
  116.1 7.9 %copy-start.7 = (bf16[2,4,4,24,768]{4,3,2,1,0:T(8,128)(2,1)}, bf16[2,4,4,24,768]{4,3,2,1,0:T(8,128)(2,1)S(1)}, u32[]{:S(2)}) copy-start(bf16[2,4,4,24,768]{4,3,2,1,0:T(8,128)(2,1)S(1)} %collective-permute-done.16.refs_3_) | copy-start | bytes 3538948
  116.1 2.8 collective-permute-start.18
  116.1 6.2 %collective-permute-start.19 = (bf16[2,4,4,24,768]{4,3,2,1,0:T(8,128)(2,1)S(1)}, bf16[2,4,4,24,768]{4,3,2,1,0:T(8,128)(2,1)S(1)}, u32[]{:S(2)}, u32[]{:S(2)}) collective-permute-start(bf16[2,4,4,24,768]{4,3,2,1,0:T(8,128)(2,1)S(1)} %collective-permute-done.16.refs_3_), channel_id=1, source_target_pairs={{0,8},{1,9},{2,10},{3,11},{4,12},{5,13},{6,14},{7,15},{8,0},{9,1},... | collective-permute-start | bytes 3538952 | tf_op jit(solution)/shard_map/ppermute | solution.py:602
  116.6 7.4 %collective-permute-start.20 = (bf16[2,4,4,24,768]{4,3,2,1,0:T(8,128)(2,1)S(1)}, bf16[2,4,4,24,768]{4,3,2,1,0:T(8,128)(2,1)S(1)}, u32[]{:S(2)}, u32[]{:S(2)}) collective-permute-start(bf16[2,4,4,24,768]{4,3,2,1,0:T(8,128)(2,1)S(1)} %pad_maximum_fusion.1.refs_5_), channel_id=1, source_target_pairs={{0,8},{1,9},{2,10},{3,11},{4,12},{5,13},{6,14},{7,15},{8,0},{9,1},... | collective-permute-start | bytes 3538952 | tf_op jit(solution)/shard_map/ppermute | solution.py:602
  116.7 7.3 %collective-permute-start.21 = (bf16[2,4,4,24,768]{4,3,2,1,0:T(8,128)(2,1)S(1)}, bf16[2,4,4,24,768]{4,3,2,1,0:T(8,128)(2,1)}, u32[]{:S(2)}, u32[]{:S(2)}) collective-permute-start(bf16[2,4,4,24,768]{4,3,2,1,0:T(8,128)(2,1)S(1)} %collective-permute-done.17.refs_7_), channel_id=1, source_target_pairs={{0,8},{1,9},{2,10},{3,11},{4,12},{5,13},{6,14},{7,15},{8,0},{9,1},... | collective-permute-start | bytes 3538952 | tf_op jit(solution)/shard_map/ppermute | solution.py:602
  119.0 5.1 %copy-start.8 = (bf16[2,4,4,24,768]{4,3,2,1,0:T(8,128)(2,1)}, bf16[2,4,4,24,768]{4,3,2,1,0:T(8,128)(2,1)S(1)}, u32[]{:S(2)}) copy-start(bf16[2,4,4,24,768]{4,3,2,1,0:T(8,128)(2,1)S(1)} %collective-permute-done.18.refs_2_) | copy-start | bytes 3538948
  122.3 1.7 copy-start.9
  124.0 1.0 copy-start.10
  295.6 15.7 %collective-permute-start.22 = (bf16[2,2,4,4,24,768]{5,4,3,2,1,0:T(8,128)(2,1)}, bf16[2,2,4,4,24,768]{5,4,3,2,1,0:T(8,128)(2,1)}, u32[]{:S(2)}, u32[]{:S(2)}) collective-permute-start(bf16[2,2,4,4,24,768]{5,4,3,2,1,0:T(8,128)(2,1)} %get-tuple-element.152), channel_id=1, source_target_pairs={{0,8},{1,9},{2,10},{3,11},{4,12},{5,13},{6,14},{7,15},{8,0},{9,1},... | collective-permute-start | bytes 7077896 | tf_op jit(solution)/shard_map/ppermute | solution.py:602
  311.0 17.6 %collective-permute-start.23 = (bf16[2,2,4,4,24,768]{5,4,3,2,1,0:T(8,128)(2,1)}, bf16[2,2,4,4,24,768]{5,4,3,2,1,0:T(8,128)(2,1)S(1)}, u32[]{:S(2)}, u32[]{:S(2)}) collective-permute-start(bf16[2,2,4,4,24,768]{5,4,3,2,1,0:T(8,128)(2,1)} %get-tuple-element.158), channel_id=1, source_target_pairs={{0,8},{1,9},{2,10},{3,11},{4,12},{5,13},{6,14},{7,15},{8,0},{9,1},... | collective-permute-start | bytes 7077896 | tf_op jit(solution)/shard_map/ppermute | solution.py:602
  315.5 28.3 %collective-permute-start.24 = (bf16[2,4,4,24,768]{4,3,2,1,0:T(8,128)(2,1)}, bf16[2,4,4,24,768]{4,3,2,1,0:T(8,128)(2,1)}, u32[]{:S(2)}, u32[]{:S(2)}) collective-permute-start(bf16[2,4,4,24,768]{4,3,2,1,0:T(8,128)(2,1)} %get-tuple-element.190), channel_id=1, source_target_pairs={{0,1},{1,0},{2,3},{3,2},{4,5},{5,4},{6,7},{7,6},{8,9},{9,8},{10,11... | collective-permute-start | bytes 3538952 | tf_op jit(solution)/shard_map/ppermute | solution.py:602
  316.1 12.5 %copy-start.4 = (bf16[2,2,4,4,24,768]{5,4,3,2,1,0:T(8,128)(2,1)S(1)}, bf16[2,2,4,4,24,768]{5,4,3,2,1,0:T(8,128)(2,1)}, u32[]{:S(2)}) copy-start(bf16[2,2,4,4,24,768]{5,4,3,2,1,0:T(8,128)(2,1)} %get-tuple-element.157) | copy-start | bytes 7077892
  329.3 31.2 %collective-permute-start.25 = (bf16[2,4,4,24,768]{4,3,2,1,0:T(8,128)(2,1)S(1)}, bf16[2,4,4,24,768]{4,3,2,1,0:T(8,128)(2,1)S(1)}, u32[]{:S(2)}, u32[]{:S(2)}) collective-permute-start(bf16[2,4,4,24,768]{4,3,2,1,0:T(8,128)(2,1)S(1)} %get-tuple-element.188), channel_id=1, source_target_pairs={{0,16},{1,17},{2,18},{3,19},{4,20},{5,21},{6,22},{7,23},{8,24},{9,... | collective-permute-start | bytes 3538952 | tf_op jit(solution)/shard_map/ppermute | solution.py:602
  345.3 24.4 %collective-permute-start.26 = (bf16[4,4,24,768]{3,2,1,0:T(8,128)(2,1)S(1)}, bf16[4,4,24,768]{3,2,1,0:T(8,128)(2,1)S(1)}, u32[]{:S(2)}, u32[]{:S(2)}) collective-permute-start(bf16[4,4,24,768]{3,2,1,0:T(8,128)(2,1)S(1)} %get-tuple-element.198), channel_id=1, source_target_pairs={{0,16},{1,17},{2,18},{3,19},{4,20},{5,21},{6,22},{7,23},{8,24},{9,... | collective-permute-start | bytes 1769480 | tf_op jit(solution)/shard_map/ppermute | solution.py:602
  360.5 30.9 %collective-permute-start.27 = (bf16[2,2,4,5,24,384]{5,4,3,2,1,0:T(8,128)(2,1)}, bf16[2,2,4,5,24,384]{5,4,3,2,1,0:T(8,128)(2,1)}, u32[]{:S(2)}, u32[]{:S(2)}) collective-permute-start(bf16[2,2,4,5,24,384]{5,4,3,2,1,0:T(8,128)(2,1)} %get-tuple-element.181), channel_id=1, source_target_pairs={{0,8},{1,9},{2,10},{3,11},{4,12},{5,13},{6,14},{7,15},{8,0},{9,1},... | collective-permute-start | bytes 4423688 | tf_op jit(solution)/shard_map/ppermute | solution.py:602
  369.8 21.6 %copy-start.5 = (bf16[2,2,4,5,24,384]{5,4,3,2,1,0:T(8,128)(2,1)S(1)}, bf16[2,2,4,5,24,384]{5,4,3,2,1,0:T(8,128)(2,1)}, u32[]{:S(2)}) copy-start(bf16[2,2,4,5,24,384]{5,4,3,2,1,0:T(8,128)(2,1)} %get-tuple-element.180) | copy-start | bytes 4423684
  379.3 13.9 %collective-permute-start.28 = (bf16[2,2,4,4,24,384]{5,4,3,2,1,0:T(8,128)(2,1)}, bf16[2,2,4,4,24,384]{5,4,3,2,1,0:T(8,128)(2,1)}, u32[]{:S(2)}, u32[]{:S(2)}) collective-permute-start(bf16[2,2,4,4,24,384]{5,4,3,2,1,0:T(8,128)(2,1)} %get-tuple-element.182), channel_id=1, source_target_pairs={{0,8},{1,9},{2,10},{3,11},{4,12},{5,13},{6,14},{7,15},{8,0},{9,1},... | collective-permute-start | bytes 3538952 | tf_op jit(solution)/shard_map/ppermute | solution.py:602
  379.3 25.4 %collective-permute-start.39 = (bf16[4,4,24,768]{3,2,1,0:T(8,128)(2,1)}, bf16[4,4,24,768]{3,2,1,0:T(8,128)(2,1)S(1)}, u32[]{:S(2)}, u32[]{:S(2)}) collective-permute-start(bf16[4,4,24,768]{3,2,1,0:T(8,128)(2,1)} %get-tuple-element.196), channel_id=1, source_target_pairs={{0,1},{1,0},{2,3},{3,2},{4,5},{5,4},{6,7},{7,6},{8,9},{9,8},{10,11... | collective-permute-start | bytes 1769480 | tf_op jit(solution)/shard_map/ppermute | solution.py:602
  381.5 23.9 %collective-permute-start.43 = (bf16[4,24,768]{2,1,0:T(8,128)(2,1)}, bf16[4,24,768]{2,1,0:T(8,128)(2,1)S(1)}, u32[]{:S(2)}, u32[]{:S(2)}) collective-permute-start(bf16[4,24,768]{2,1,0:T(8,128)(2,1)} %get-tuple-element.203), channel_id=1, source_target_pairs={{0,2},{1,3},{2,4},{3,5},{4,6},{5,7},{6,0},{7,1},{8,10},{9,11},{10,... | collective-permute-start | bytes 442376 | tf_op jit(solution)/shard_map/ppermute | solution.py:602
  388.1 19.3 %collective-permute-start.44 = (bf16[4,24,768]{2,1,0:T(8,128)(2,1)}, bf16[4,24,768]{2,1,0:T(8,128)(2,1)S(1)}, u32[]{:S(2)}, u32[]{:S(2)}) collective-permute-start(bf16[4,24,768]{2,1,0:T(8,128)(2,1)} %get-tuple-element.205), channel_id=1, source_target_pairs={{0,4},{1,5},{2,6},{3,7},{4,0},{5,1},{6,2},{7,3},{8,12},{9,13},{10,... | collective-permute-start | bytes 442376 | tf_op jit(solution)/shard_map/ppermute | solution.py:602
  391.4 2.5 copy-start.11
  391.4 16.1 %collective-permute-start.45 = (bf16[4,24,768]{2,1,0:T(8,128)(2,1)}, bf16[4,24,768]{2,1,0:T(8,128)(2,1)S(1)}, u32[]{:S(2)}, u32[]{:S(2)}) collective-permute-start(bf16[4,24,768]{2,1,0:T(8,128)(2,1)} %get-tuple-element.204), channel_id=1, source_target_pairs={{0,6},{1,7},{2,0},{3,1},{4,2},{5,3},{6,4},{7,5},{8,14},{9,15},{10,... | collective-permute-start | bytes 442376 | tf_op jit(solution)/shard_map/ppermute | solution.py:602
  393.2 18.1 %collective-permute-start.29 = (bf16[2,4,5,24,384]{4,3,2,1,0:T(8,128)(2,1)S(1)}, bf16[2,4,5,24,384]{4,3,2,1,0:T(8,128)(2,1)S(1)}, u32[]{:S(2)}, u32[]{:S(2)}) collective-permute-start(bf16[2,4,5,24,384]{4,3,2,1,0:T(8,128)(2,1)S(1)} %get-tuple-element.192), channel_id=1, source_target_pairs={{0,1},{1,0},{2,3},{3,2},{4,5},{5,4},{6,7},{7,6},{8,9},{9,8},{10,11... | collective-permute-start | bytes 2211848 | tf_op jit(solution)/shard_map/ppermute | solution.py:602
  404.7 16.3 %collective-permute-start.34 = (bf16[2,4,4,24,384]{4,3,2,1,0:T(8,128)(2,1)S(1)}, bf16[2,4,4,24,384]{4,3,2,1,0:T(8,128)(2,1)S(1)}, u32[]{:S(2)}, u32[]{:S(2)}) collective-permute-start(bf16[2,4,4,24,384]{4,3,2,1,0:T(8,128)(2,1)S(1)} %get-tuple-element.194), channel_id=1, source_target_pairs={{0,16},{1,17},{2,18},{3,19},{4,20},{5,21},{6,22},{7,23},{8,24},{9,... | collective-permute-start | bytes 1769480 | tf_op jit(solution)/shard_map/ppermute | solution.py:602
  405.4 8.7 %collective-permute-start.40 = (bf16[4,24,768]{2,1,0:T(8,128)(2,1)S(1)}, bf16[4,24,768]{2,1,0:T(8,128)(2,1)S(1)}, u32[]{:S(2)}, u32[]{:S(2)}) collective-permute-start(bf16[4,24,768]{2,1,0:T(8,128)(2,1)S(1)} %get-tuple-element.206), channel_id=1, source_target_pairs={{0,2},{1,3},{2,4},{3,5},{4,6},{5,7},{6,0},{7,1},{8,10},{9,11},{10,... | collective-permute-start | bytes 442376 | tf_op jit(solution)/shard_map/ppermute | solution.py:602
  407.4 11.1 %collective-permute-start.41 = (bf16[4,24,768]{2,1,0:T(8,128)(2,1)S(1)}, bf16[4,24,768]{2,1,0:T(8,128)(2,1)S(1)}, u32[]{:S(2)}, u32[]{:S(2)}) collective-permute-start(bf16[4,24,768]{2,1,0:T(8,128)(2,1)S(1)} %get-tuple-element.208), channel_id=1, source_target_pairs={{0,4},{1,5},{2,6},{3,7},{4,0},{5,1},{6,2},{7,3},{8,12},{9,13},{10,... | collective-permute-start | bytes 442376 | tf_op jit(solution)/shard_map/ppermute | solution.py:602
  407.5 11.0 %collective-permute-start.42 = (bf16[4,24,768]{2,1,0:T(8,128)(2,1)S(1)}, bf16[4,24,768]{2,1,0:T(8,128)(2,1)S(1)}, u32[]{:S(2)}, u32[]{:S(2)}) collective-permute-start(bf16[4,24,768]{2,1,0:T(8,128)(2,1)S(1)} %get-tuple-element.207), channel_id=1, source_target_pairs={{0,6},{1,7},{2,0},{3,1},{4,2},{5,3},{6,4},{7,5},{8,14},{9,15},{10,... | collective-permute-start | bytes 442376 | tf_op jit(solution)/shard_map/ppermute | solution.py:602
  411.5 15.7 %collective-permute-start.30 = (bf16[4,5,24,384]{3,2,1,0:T(8,128)(2,1)S(1)}, bf16[4,5,24,384]{3,2,1,0:T(8,128)(2,1)S(1)}, u32[]{:S(2)}, u32[]{:S(2)}) collective-permute-start(bf16[4,5,24,384]{3,2,1,0:T(8,128)(2,1)S(1)} %get-tuple-element.200), channel_id=1, source_target_pairs={{0,16},{1,17},{2,18},{3,19},{4,20},{5,21},{6,22},{7,23},{8,24},{9,... | collective-permute-start | bytes 1105928 | tf_op jit(solution)/shard_map/ppermute | solution.py:602
  421.1 10.5 %collective-permute-start.35 = (bf16[4,4,24,384]{3,2,1,0:T(8,128)(2,1)S(1)}, bf16[4,4,24,384]{3,2,1,0:T(8,128)(2,1)S(1)}, u32[]{:S(2)}, u32[]{:S(2)}) collective-permute-start(bf16[4,4,24,384]{3,2,1,0:T(8,128)(2,1)S(1)} %get-tuple-element.202), channel_id=1, source_target_pairs={{0,1},{1,0},{2,3},{3,2},{4,5},{5,4},{6,7},{7,6},{8,9},{9,8},{10,11... | collective-permute-start | bytes 884744 | tf_op jit(solution)/shard_map/ppermute | solution.py:602
  427.3 7.4 %collective-permute-start.31 = (bf16[5,24,384]{2,1,0:T(8,128)(2,1)S(1)}, bf16[5,24,384]{2,1,0:T(8,128)(2,1)S(1)}, u32[]{:S(2)}, u32[]{:S(2)}) collective-permute-start(bf16[5,24,384]{2,1,0:T(8,128)(2,1)S(1)} %get-tuple-element.209), channel_id=1, source_target_pairs={{0,2},{1,3},{2,4},{3,5},{4,6},{5,7},{6,0},{7,1},{8,10},{9,11},{10,... | collective-permute-start | bytes 276488 | tf_op jit(solution)/shard_map/ppermute | solution.py:602
  429.0 9.9 %collective-permute-start.32 = (bf16[5,24,384]{2,1,0:T(8,128)(2,1)S(1)}, bf16[5,24,384]{2,1,0:T(8,128)(2,1)S(1)}, u32[]{:S(2)}, u32[]{:S(2)}) collective-permute-start(bf16[5,24,384]{2,1,0:T(8,128)(2,1)S(1)} %get-tuple-element.211), channel_id=1, source_target_pairs={{0,4},{1,5},{2,6},{3,7},{4,0},{5,1},{6,2},{7,3},{8,12},{9,13},{10,... | collective-permute-start | bytes 276488 | tf_op jit(solution)/shard_map/ppermute | solution.py:602
  431.5 7.4 %collective-permute-start.33 = (bf16[5,24,384]{2,1,0:T(8,128)(2,1)S(1)}, bf16[5,24,384]{2,1,0:T(8,128)(2,1)S(1)}, u32[]{:S(2)}, u32[]{:S(2)}) collective-permute-start(bf16[5,24,384]{2,1,0:T(8,128)(2,1)S(1)} %get-tuple-element.210), channel_id=1, source_target_pairs={{0,6},{1,7},{2,0},{3,1},{4,2},{5,3},{6,4},{7,5},{8,14},{9,15},{10,... | collective-permute-start | bytes 276488 | tf_op jit(solution)/shard_map/ppermute | solution.py:602
  431.8 8.1 %collective-permute-start.36 = (bf16[4,24,384]{2,1,0:T(8,128)(2,1)S(1)}, bf16[4,24,384]{2,1,0:T(8,128)(2,1)S(1)}, u32[]{:S(2)}, u32[]{:S(2)}) collective-permute-start(bf16[4,24,384]{2,1,0:T(8,128)(2,1)S(1)} %get-tuple-element.212), channel_id=1, source_target_pairs={{0,2},{1,3},{2,4},{3,5},{4,6},{5,7},{6,0},{7,1},{8,10},{9,11},{10,... | collective-permute-start | bytes 221192 | tf_op jit(solution)/shard_map/ppermute | solution.py:602
  433.7 10.1 %collective-permute-start.37 = (bf16[4,24,384]{2,1,0:T(8,128)(2,1)S(1)}, bf16[4,24,384]{2,1,0:T(8,128)(2,1)S(1)}, u32[]{:S(2)}, u32[]{:S(2)}) collective-permute-start(bf16[4,24,384]{2,1,0:T(8,128)(2,1)S(1)} %get-tuple-element.214), channel_id=1, source_target_pairs={{0,4},{1,5},{2,6},{3,7},{4,0},{5,1},{6,2},{7,3},{8,12},{9,13},{10,... | collective-permute-start | bytes 221192 | tf_op jit(solution)/shard_map/ppermute | solution.py:602
  434.7 9.1 %collective-permute-start.38 = (bf16[4,24,384]{2,1,0:T(8,128)(2,1)S(1)}, bf16[4,24,384]{2,1,0:T(8,128)(2,1)S(1)}, u32[]{:S(2)}, u32[]{:S(2)}) collective-permute-start(bf16[4,24,384]{2,1,0:T(8,128)(2,1)S(1)} %get-tuple-element.213), channel_id=1, source_target_pairs={{0,6},{1,7},{2,0},{3,1},{4,2},{5,3},{6,4},{7,5},{8,14},{9,15},{10,... | collective-permute-start | bytes 221192 | tf_op jit(solution)/shard_map/ppermute | solution.py:602

commit v5 on v4

--- a/solution.py
+++ b/solution.py
@@ -28,8 +28,8 @@
     return pltpu.CompilerParams(vmem_limit_bytes=limit)
 
 
-def cost():
-    return pl.CostEstimate(flops=1, bytes_accessed=1, transcendentals=0)
+def cost(micros):
+    return pl.CostEstimate(flops=int(micros * 2e8), bytes_accessed=int(micros * 1e5), transcendentals=0)
 
 
 def once(shape, index):
@@ -74,7 +74,7 @@
         out_specs=pl.BlockSpec((rows, D), lambda i: (0, i)),
         out_shape=jax.ShapeDtypeStruct((rows, 3 * D), BF),
         compiler_params=params(),
-        cost_estimate=cost(),
+        cost_estimate=cost(8),
         name="qkv",
     )(x, w, vec)
 
@@ -134,7 +134,7 @@
             jax.ShapeDtypeStruct((count, D // PAIR, 2, seq), F32),
         ],
         compiler_params=params(),
-        cost_estimate=cost(),
+        cost_estimate=cost(13),
         name="attend",
     )(lengths, qkv, qkv, qkv)
 
@@ -236,7 +236,7 @@
         ],
         scratch_shapes=weight_scratch(ff),
         compiler_params=params(),
-        cost_estimate=cost(),
+        cost_estimate=cost(22),
         name="ffn",
     )(x, ctx, vec, first, wi, wb)
 
@@ -318,7 +318,7 @@
         ],
         scratch_shapes=weight_scratch(ff),
         compiler_params=params(),
-        cost_estimate=cost(),
+        cost_estimate=cost(24),
         name="ffn_back",
     )(dy, z2, z1, slope, vec, wb, wi, first)
 
@@ -395,7 +395,7 @@
         ),
         out_shape=[jax.ShapeDtypeStruct((3, rows, WIDE), BF)] + [jax.ShapeDtypeStruct((count, 1, WIDE), F32)] * 2,
         compiler_params=params(),
-        cost_estimate=cost(),
+        cost_estimate=cost(12),
         name="attend_back",
     )(lengths, qkv, qkv, qkv, dctx, lse)
 
@@ -419,7 +419,7 @@
         out_specs=line,
         out_shape=jax.ShapeDtypeStruct((rows, D), dtype),
         compiler_params=params(),
-        cost_estimate=cost(),
+        cost_estimate=cost(9),
         name="dx",
     )(dz1, e0, e1, w)
 
@@ -464,7 +464,7 @@
         ),
         out_shape=out_shape,
         compiler_params=params(),
-        cost_estimate=cost(),
+        cost_estimate=cost(15),
         name="wgrad_in",
     )(core, a, c, b, d)
 
@@ -528,7 +528,7 @@
         ),
         out_shape=out_shape,
         compiler_params=params(),
-        cost_estimate=cost(),
+        cost_estimate=cost(12),
         name="wgrad_heads",
     )(core, low2, low1, e2, e1, *others)
 
@@ -563,7 +563,7 @@
         ),
         out_shape=[jax.ShapeDtypeStruct((2, 2, 4, 4, rows, D), BF)] * 2,
         compiler_params=params(),
-        cost_estimate=cost(),
+        cost_estimate=cost(15),
         name="wgrad_back",
     )(core, two, one, two, one, e_two, e_one)
 
@@ -600,6 +600,10 @@
 
     def send(self, value, dim, step=1):
         return lax.ppermute(value, AXES, self.shift(dim, step))
+
+    def swap(self, value, bit):
+        pairs = [(i, i ^ (bit * self.y)) for i in range(self.count)]
+        return lax.ppermute(value, AXES, pairs)
 
 
 X, CORE, Z, Y = range(4)
@@ -676,7 +680,7 @@
             py = (y + (near if side == 0 else far)) % 2
             pc = (core + other) % 2
             for dz in range(4):
-                pz = (z + 4 - dz) % 4
+                pz = lax.bitwise_xor(z, dz) if split else (z + 4 - dz) % 4
                 if split:
                     target = held[side].at[:, px, pc, pz, py] if side == 0 else held[side].at[px, pc, pz, py]
                 else:
@@ -720,7 +724,7 @@
         ),
         out_shape=[jax.ShapeDtypeStruct(shape, BF) for shape in shapes],
         compiler_params=params(),
-        cost_estimate=cost(),
+        cost_estimate=cost(6),
         name="place",
     )(at, *parts)
 
@@ -730,9 +734,14 @@
 
 
 class Gather:
-    def __init__(self, grid, packet, first):
+    def __init__(self, grid, packet, first, by_bits):
         self.grid, self.first = grid, first
-        self.ring = [packet] + [grid.send(packet, Z, k) for k in range(1, 4)]
+        if by_bits:
+            pair = jnp.stack([packet, grid.swap(packet, 1)])
+            far = grid.swap(pair, 2)
+            self.ring = [pair[0], pair[1], far[0], far[1]]
+        else:
+            self.ring = [packet] + [grid.send(packet, Z, k) for k in range(1, 4)]
 
     def one(self, *others):
         ring = lax.optimization_barrier((*self.ring, *others))[:4]
@@ -743,12 +752,13 @@
         held = lax.optimization_barrier((*self.line, *others))
         self.near = [jnp.stack(pair) for pair in zip(held, self.came)]
         self.far = [self.grid.send(v, d) for v, d in zip(self.near, (X, Y))]
+        self.near_core = [self.grid.send(v, CORE) for v in self.near]
 
     def parts(self, *others):
+        far = lax.optimization_barrier((*self.far, *others))[:2]
         out = []
-        held = lax.optimization_barrier((*self.near, *self.far, *others))
-        for near, far in zip(held[:2], held[2:4]):
-            out += [near, self.grid.send(near, CORE), far, self.grid.send(far, CORE)]
+        for i in range(2):
+            out += [self.near[i], self.near_core[i], far[i], self.grid.send(far[i], CORE)]
         return out
 
 
@@ -804,8 +814,8 @@
     at = jnp.stack([x, core, z, y]).astype(jnp.int32)
     core = core.astype(jnp.int32)[None]
     vectors = [bias_q, bias_v, bias_out, gain_one, shift_one, bias_back, gain_two, shift_two]
-    one = Gather(grid, pack_one(device.astype(jnp.int32)[None], w_qkv, w_out, vectors, bias_in), 2)
-    two = Gather(grid, pack_two(w_in, w_back), 4)
+    one = Gather(grid, pack_one(device.astype(jnp.int32)[None], w_qkv, w_out, vectors, bias_in), 2, False)
+    two = Gather(grid, pack_two(w_in, w_back), 4, True)
     one.one()
     one.two()
     two.one(*one.far)
@@ -839,29 +849,28 @@
     sum_back = Sum(grid, where, (Y, X), back)
     into = wgrad_in_call(core, after(h2, back[0]), h1, e1_2, e1_1, rows)
     sum_in = Sum(grid, where, (X, Y), into)
-    steps = sum_back.one(into[0])
+    steps = sum_back.one(into[0]) + sum_in.one(into[0])
     heads_1.append(attend_back_call(qkv, after(dctx, *steps), lse, lengths, 0))
-    steps = sum_in.one(heads_1[0][0])
-    heads_1.append(attend_back_call(qkv, after(dctx, *steps), lse, lengths, 1))
-    steps = sum_back.two(heads_1[1][0])
+    heads_1.append(attend_back_call(qkv, after(dctx, heads_1[0][0]), lse, lengths, 1))
+    steps = sum_back.two(heads_1[1][0]) + sum_in.two(heads_1[1][0])
     group = wgrad_heads_call(
         core, after(low2, *steps), low1, heads_2[0][0], heads_1[0][0], rows, [ctx2, ctx1, ea_2, ea_1], False
     )
     sum_0 = Sum(grid, where, (Y, X), group)
-    steps = sum_in.two(group[0]) + sum_back.three(group[0])
+    steps = sum_back.three(group[0]) + sum_in.three(group[0])
     lines = [heads[i][j] for i in range(GROUPS) for j in (1, 2) for heads in (heads_1, heads_2)]
     group = wgrad_heads_call(
         core, after(low2, *steps), low1, heads_2[1][0], heads_1[1][0], rows, [sums_1, sums_2, *lines], True
     )
     sum_1 = Sum(grid, where, (X, Y), group)
     steps = sum_0.one(group[0]) + sum_1.one()
-    grad = dx_call(after(dz1, *steps), heads_1[0][0], heads_1[1][0], first, BF)
-    sum_in.three(grad)
+    total_back = sum_back.result()
+    grad = dx_call(after(dz1, total_back, *steps), heads_1[0][0], heads_1[1][0], first, BF)
     sum_0.two(grad)
     sum_1.two(grad)
     sum_0.three()
     sum_1.three()
-    total_in, total_back, half_0, half_1 = sum_in.result(), sum_back.result(), sum_0.result(), sum_1.result()
+    total_in, half_0, half_1 = sum_in.result(), sum_0.result(), sum_1.result()
 
     w_in_grad = total_in.swapaxes(0, 1).reshape(rows, 4 * D)
     w_back_grad = total_back.reshape(4 * rows, D)

time: 450 us -> 447 us (level)
  waiting for transfers between devices: 85.9 us -> 77.9 us
    ppermute x46 -> x43, waiting for transfers between devices: 85.9 us -> 54.7 us  [send(): return lax.ppermute(value, AXES, self.shift(dim, step))]
    ppermute x0 -> x2, waiting for transfers between devices: none -> 23.2 us  [swap(): return lax.ppermute(value, AXES, pairs)]
    ppermute x46 -> x43, starting transfers between devices: 57.1 us -> 55.5 us  [send(): return lax.ppermute(value, AXES, self.shift(dim, step))]
  transfers between devices with their start and end apart: 46 -> 45, of which waited for: 23 -> 13; matrix products, arithmetic and copies ran while one was open for 5% -> 5% of each run, Pallas kernels for 23% -> 20%
where the time goes in v5:
time: 447 us; the launch traced here: 443 us
  Pallas kernels  275 us (62%)
  waiting for transfers between devices  77.9 us (17%)
  starting transfers between devices  59.8 us (13%)
  other arithmetic  19.2 us (4%)
  local copies, waits for them, and re-layouts  9.42 us (2%)
    ppermute x43, starting transfers between devices, send(): return lax.ppermute(value, AXES, self.shift(dim, step))  55.5 us
    ppermute x43, waiting for transfers between devices, send(): return lax.ppermute(value, AXES, self.shift(dim, step))  54.7 us
    pallas_call x4, Pallas kernels, attend_back_call(): pl.pallas_call(body, grid_spec=pltpu.PrefetchScalarGridSpec(num_scalar_pr...  49.7 us
    pallas_call x2, Pallas kernels, ffn_back_call(): pl.pallas_call(ffn_back_body, grid=(rows // block,), in_specs=[line, line...  47.5 us
    pallas_call x2, Pallas kernels, ffn_call(): pl.pallas_call(lambda *refs: ffn_body(renorm, *refs), grid=(rows // block...  44.7 us
    pallas_call x2, Pallas kernels, attend_call(): pl.pallas_call(body, grid_spec=pltpu.PrefetchScalarGridSpec(num_scalar_pr...  25.9 us
    pallas_call x2, Pallas kernels, wgrad_heads_call(): pl.pallas_call(body, grid_spec=pltpu.PrefetchScalarGridSpec(num_scalar_pr...  24 us
    ppermute x2, waiting for transfers between devices, swap(): return lax.ppermute(value, AXES, pairs)  23.2 us
  transfers between devices with their start and end apart: 45, of which 13 were waited for; matrix products, arithmetic and copies ran while one was open for 5% of the time, Pallas kernels for 20%

profile of v5, /device:TPU:0, one launch (start us, length us, event | category | flops | bytes accessed | tf_op | source)
XLA Modules:
  0.0 443.0 jit_solution(2276749608870184898)
XLA Ops:
  0.7 1.8 pack_one.1
  2.4 3.0 collective-permute-start
  5.4 2.6 collective-permute-start.1
  8.0 1.3 collective-permute-start.2
  9.4 1.7 pack_two.1
  11.8 1.5 collective-permute-done
  13.2 7.1 %collective-permute-done.1 = bf16[5,24,768]{2,1,0:T(8,128)(2,1)S(1)} collective-permute-done((bf16[5,24,768]{2,1,0:T(8,128)(2,1)}, bf16[5,24,768]{2,1,0:T(8,128)(2,1)S(1)}, u32[]{:S(2)}, u32[]{:S(2)}) %collective-permute-start.1) | collective-permute-done | bytes 184352 | tf_op jit(solution)/shard_map/ppermute | solution.py:602
  21.4 1.6 collective-permute-start.6
  24.0 1.6 collective-permute-start.3
  25.6 7.9 %collective-permute-done.6 = bf16[4,3,24,768]{3,2,1,0:T(8,128)(2,1)S(1)} collective-permute-done((bf16[4,3,24,768]{3,2,1,0:T(8,128)(2,1)S(1)}, bf16[4,3,24,768]{3,2,1,0:T(8,128)(2,1)S(1)}, u32[]{:S(2)}, u32[]{:S(2)}) %collective-permute-start.6) | collective-permute-done | bytes 442400 | tf_op jit(solution)/shard_map/ppermute | solution.py:602
  33.5 1.6 collective-permute-start.7
  36.0 3.6 collective-permute-start.12
  39.7 1.6 collective-permute-start.5
  41.7 23.2 %collective-permute-done.12 = bf16[2,8,24,768]{3,2,1,0:T(8,128)(2,1)} collective-permute-done((bf16[2,8,24,768]{3,2,1,0:T(8,128)(2,1)}, bf16[2,8,24,768]{3,2,1,0:T(8,128)(2,1)}, u32[]{:S(2)}, u32[]{:S(2)}) %collective-permute-start.12) | collective-permute-done | bytes 589856 | tf_op jit(solution)/shard_map/ppermute | solution.py:606
  67.2 1.5 collective-permute-start.14
  72.0 6.2 %place.2 = bf16[5,2,2,4,2,24,768]{6,5,4,3,2,1,0:T(8,128)(2,1)} custom-call(s32[4]{0:T(128)} %pad_add_fusion.refs_0_, bf16[2,4,2,24,768]{4,3,2,1,0:T(8,128)(2,1)} %copy-done.4, bf16[2,4,2,24,768]{4,3,2,1,0:T(8,128)(2,1)} %copy-done.17, bf16[2,4,2,24,768]{4,3,2,1,0:T(8,128)(2,1)} %copy-done.16, bf16[2,4,2,24,768]{4,3,2,1,0:T(8,128)(2,1)} %copy-done.18, ...), custom_call_target="tpu_custom_call" | custom-call | flops 1200000000 | bytes 600000 | tf_op jit(solution)/shard_map/place/pallas_call | solution.py:715
  78.2 2.1 convert_reduce_fusion.vec_ref.refs_2_
  80.3 7.9 %qkv.2.refs_1_.refs_2_.refs_3_ = bf16[1024,2304]{1,0:T(8,128)(2,1)} custom-call(bf16[1024,768]{1,0:T(8,128)(2,1)} %c_ref.3, bf16[5,768,768]{2,1,0:T(8,128)(2,1)} %bitcast.168, f32[24,768]{1,0:T(8,128)} %convert_reduce_fusion.vec_ref.refs_2_), custom_call_target="tpu_custom_call" | custom-call | flops 1600000000 | bytes 800000 | tf_op jit(solution)/shard_map/qkv/pallas_call | solution.py:66
  88.1 1.2 pad_maximum_fusion.1.refs_5_
  89.3 1.6 collective-permute-start.17
  92.2 12.9 %attend.2 = (bf16[1024,768]{1,0:T(8,128)(2,1)}, f32[2,6,2,512]{3,2,1,0:T(2,128)}) custom-call(s32[2]{0:T(128)} %refs_0_.13, bf16[1024,2304]{1,0:T(8,128)(2,1)} %qkv.2.refs_1_.refs_2_.refs_3_, bf16[1024,2304]{1,0:T(8,128)(2,1)} %qkv.2.refs_1_.refs_2_.refs_3_, bf16[1024,2304]{1,0:T(8,128)(2,1)} %qkv.2.refs_1_.refs_2_.refs_3_), custom_call_target="tpu_custom_call" | custom-call | flops 2600000000 | bytes 1300000 | tf_op jit(solution)/shard_map/attend/pallas_call | solution.py:124
  105.1 11.5 %collective-permute-done.17.refs_7_ = bf16[2,4,4,24,768]{4,3,2,1,0:T(8,128)(2,1)S(1)} collective-permute-done((bf16[2,4,4,24,768]{4,3,2,1,0:T(8,128)(2,1)S(1)}, bf16[2,4,4,24,768]{4,3,2,1,0:T(8,128)(2,1)S(1)}, u32[]{:S(2)}, u32[]{:S(2)}) %collective-permute-start.17) | collective-permute-done | bytes 1179680 | tf_op jit(solution)/shard_map/ppermute | solution.py:602
  116.6 1.4 collective-permute-done.16.refs_3_
  118.5 4.0 collective-permute-done.18.refs_4_
  123.5 8.3 %place.3 = (bf16[4,2,2,4,2,24,768]{6,5,4,3,2,1,0:T(8,128)(2,1)}, bf16[2,2,4,2,4,24,768]{6,5,4,3,2,1,0:T(8,128)(2,1)}) custom-call(s32[4]{0:T(128)} %pad_add_fusion.refs_0_, bf16[2,4,4,24,768]{4,3,2,1,0:T(8,128)(2,1)} %copy-done.1, bf16[2,4,4,24,768]{4,3,2,1,0:T(8,128)(2,1)} %copy-done.10, bf16[2,4,4,24,768]{4,3,2,1,0:T(8,128)(2,1)} %copy-done.8, ...), custom_call_target="tpu_custom_call" | custom-call | flops 1200000000 | bytes 600000 | tf_op jit(solution)/shard_map/place/pallas_call | solution.py:715
  131.8 22.2 %ffn.2 = (f32[1024,768]{1,0:T(8,128)}, bf16[1024,768]{1,0:T(8,128)(2,1)}, bf16[1024,3072]{1,0:T(8,128)(2,1)}, bf16[1024,3072]{1,0:T(8,128)(2,1)}, f32[1024,768]{1,0:T(8,128)}, /*index=5*/bf16[1024,768]{1,0:T(8,128)(2,1)}) custom-call(bf16[1024,768]{1,0:T(8,128)(2,1)} %c_ref.3, bf16[1024,768]{1,0:T(8,128)(2,1)} %get-tuple-element.112.refs_1_.rest_1_, ...), custom_call_target="tpu_custom_call" | custom-call | flops 4400000000 | bytes 2200000 | tf_op jit(solution)/shard_map/ffn/pallas_call | solution.py:224
  154.1 7.9 %qkv.3.refs_1_.refs_2_.refs_3_ = bf16[1024,2304]{1,0:T(8,128)(2,1)} custom-call(bf16[1024,768]{1,0:T(8,128)(2,1)} %get-tuple-element.161.x_ref.a_ref, bf16[5,768,768]{2,1,0:T(8,128)(2,1)} %bitcast.170, f32[24,768]{1,0:T(8,128)} %convert_reduce_fusion.vec_ref.refs_2_), custom_call_target="tpu_custom_call" | custom-call | flops 1600000000 | bytes 800000 | tf_op jit(solution)/shard_map/qkv/pallas_call | solution.py:66
  161.9 13.0 %attend.3 = (bf16[1024,768]{1,0:T(8,128)(2,1)}, f32[2,6,2,512]{3,2,1,0:T(2,128)}) custom-call(s32[2]{0:T(128)} %refs_0_.13, bf16[1024,2304]{1,0:T(8,128)(2,1)} %qkv.3.refs_1_.refs_2_.refs_3_, bf16[1024,2304]{1,0:T(8,128)(2,1)} %qkv.3.refs_1_.refs_2_.refs_3_, bf16[1024,2304]{1,0:T(8,128)(2,1)} %qkv.3.refs_1_.refs_2_.refs_3_), custom_call_target="tpu_custom_call" | custom-call | flops 2600000000 | bytes 1300000 | tf_op jit(solution)/shard_map/attend/pallas_call | solution.py:124
  174.9 22.5 %ffn.3 = (f32[1024,768]{1,0:T(8,128)}, bf16[1024,768]{1,0:T(8,128)(2,1)}, bf16[1024,3072]{1,0:T(8,128)(2,1)}, bf16[1024,3072]{1,0:T(8,128)(2,1)}, f32[1024,768]{1,0:T(8,128)}, /*index=5*/bf16[1024,768]{1,0:T(8,128)(2,1)}) custom-call(f32[1024,768]{1,0:T(8,128)} %get-tuple-element.117.refs_0_.z2_ref, bf16[1024,768]{1,0:T(8,128)(2,1)} %get-tuple-element.119.refs_1_.rest_0_, ...), custom_call_target="tpu_custom_call" | custom-call | flops 4400000000 | bytes 2200000 | tf_op jit(solution)/shard_map/ffn/pallas_call | solution.py:224
  197.4 23.8 %ffn_back.2 = (bf16[1024,768]{1,0:T(8,128)(2,1)}, bf16[1024,3072]{1,0:T(8,128)(2,1)}, f32[1024,768]{1,0:T(8,128)}, bf16[1024,768]{1,0:T(8,128)(2,1)}, bf16[1024,768]{1,0:T(8,128)(2,1)}, /*index=5*/f32[24,768]{1,0:T(8,128)}) custom-call(bf16[1024,768]{1,0:T(8,128)(2,1)} %dy_ref.1, f32[1024,768]{1,0:T(8,128)} %get-tuple-element.121.z2_ref, ...), custom_call_target="tpu_custom_call" | custom-call | flops 4800000000 | bytes 2400000 | tf_op jit(solution)/shard_map/ffn_back/pallas_call | solution.py:306
  221.2 12.3 %attend_back.5 = (bf16[3,1024,384]{2,1,0:T(8,128)(2,1)}, f32[2,1,384]{2,1,0:T(1,128)}, f32[2,1,384]{2,1,0:T(1,128)}) custom-call(s32[2]{0:T(128)} %refs_0_.13, bf16[1024,2304]{1,0:T(8,128)(2,1)} %qkv.3.refs_1_.refs_2_.refs_3_, bf16[1024,2304]{1,0:T(8,128)(2,1)} %qkv.3.refs_1_.refs_2_.refs_3_, bf16[1024,2304]{1,0:T(8,128)(2,1)} %qkv.3.refs_1_.refs_2_.refs_3_, ...), custom_call_target="tpu_custom_call" | custom-call | flops 2400000000 | bytes 1200000 | tf_op jit(solution)/shard_map/attend_back/pallas_call | solution.py:382
  233.5 12.5 %attend_back.4 = (bf16[3,1024,384]{2,1,0:T(8,128)(2,1)}, f32[2,1,384]{2,1,0:T(1,128)}, f32[2,1,384]{2,1,0:T(1,128)}) custom-call(s32[2]{0:T(128)} %refs_0_.13, bf16[1024,2304]{1,0:T(8,128)(2,1)} %qkv.3.refs_1_.refs_2_.refs_3_, bf16[1024,2304]{1,0:T(8,128)(2,1)} %qkv.3.refs_1_.refs_2_.refs_3_, bf16[1024,2304]{1,0:T(8,128)(2,1)} %qkv.3.refs_1_.refs_2_.refs_3_, ...), custom_call_target="tpu_custom_call" | custom-call | flops 2400000000 | bytes 1200000 | tf_op jit(solution)/shard_map/attend_back/pallas_call | solution.py:382
  246.0 9.6 %dx.2.dy_ref = f32[1024,768]{1,0:T(8,128)} custom-call(f32[1024,768]{1,0:T(8,128)} %get-tuple-element.124.dz1_ref, bf16[3,1024,384]{2,1,0:T(8,128)(2,1)} %get-tuple-element.127.e0_ref.b_ref, bf16[3,1024,384]{2,1,0:T(8,128)(2,1)} %get-tuple-element.128.e1_ref.b_ref, bf16[5,768,768]{2,1,0:T(8,128)(2,1)} %bitcast.173), custom_call_target="tpu_custom_call" | custom-call | flops 1800000000 | bytes 900000 | tf_op jit(solution)/shard_map/dx/pallas_call | solution.py:415
  255.6 23.7 %ffn_back.3 = (bf16[1024,768]{1,0:T(8,128)(2,1)}, bf16[1024,3072]{1,0:T(8,128)(2,1)}, f32[1024,768]{1,0:T(8,128)}, bf16[1024,768]{1,0:T(8,128)(2,1)}, bf16[1024,768]{1,0:T(8,128)(2,1)}, /*index=5*/f32[24,768]{1,0:T(8,128)}) custom-call(f32[1024,768]{1,0:T(8,128)} %dx.2.dy_ref, f32[1024,768]{1,0:T(8,128)} %get-tuple-element.117.refs_0_.z2_ref, ...), custom_call_target="tpu_custom_call" | custom-call | flops 4800000000 | bytes 2400000 | tf_op jit(solution)/shard_map/ffn_back/pallas_call | solution.py:306
  279.3 15.0 %wgrad_back.1 = (bf16[2,2,4,4,24,768]{5,4,3,2,1,0:T(8,128)(2,1)}, bf16[2,2,4,4,24,768]{5,4,3,2,1,0:T(8,128)(2,1)}) custom-call(s32[1]{0:T(128)} %bitcast.1.core_ref, bf16[1024,3072]{1,0:T(8,128)(2,1)} %get-tuple-element.132.g2k.g2s, bf16[1024,3072]{1,0:T(8,128)(2,1)} %get-tuple-element.133.g1k.g1s, bf16[1024,3072]{1,0:T(8,128)(2,1)} %get-tuple-element.132.g2k.g2s, ...), custom_call_target="tpu_custom_call" | custom-call | flops 3000000000 | bytes 1500000 | tf_op jit(solution)/shard_map/wgrad_back/pallas_call | solution.py:556
  294.2 15.3 %wgrad_in.1 = (bf16[2,2,4,4,24,768]{5,4,3,2,1,0:T(8,128)(2,1)}, bf16[2,2,4,4,24,768]{5,4,3,2,1,0:T(8,128)(2,1)}) custom-call(s32[1]{0:T(128)} %bitcast.1.core_ref, bf16[1024,768]{1,0:T(8,128)(2,1)} %get-tuple-element.138.a_ref, bf16[1024,768]{1,0:T(8,128)(2,1)} %get-tuple-element.139.c_ref, bf16[1024,3072]{1,0:T(8,128)(2,1)} %get-tuple-element.140.b_ref, ...), custom_call_target="tpu_custom_call" | custom-call | flops 3000000000 | bytes 1500000 | tf_op jit(solution)/shard_map/wgrad_in/pallas_call | solution.py:456
  310.1 4.4 collective-permute-done.22
  314.4 4.2 fusion.3
  319.2 2.3 fusion
  321.6 1.6 collective-permute-start.23
  323.1 12.3 %attend_back.6 = (bf16[3,1024,384]{2,1,0:T(8,128)(2,1)}, f32[2,1,384]{2,1,0:T(1,128)}, f32[2,1,384]{2,1,0:T(1,128)}) custom-call(s32[2]{0:T(128)} %refs_0_.13, bf16[1024,2304]{1,0:T(8,128)(2,1)} %qkv.2.refs_1_.refs_2_.refs_3_, bf16[1024,2304]{1,0:T(8,128)(2,1)} %qkv.2.refs_1_.refs_2_.refs_3_, bf16[1024,2304]{1,0:T(8,128)(2,1)} %qkv.2.refs_1_.refs_2_.refs_3_, ...), custom_call_target="tpu_custom_call" | custom-call | flops 2400000000 | bytes 1200000 | tf_op jit(solution)/shard_map/attend_back/pallas_call | solution.py:382
  335.5 12.6 %attend_back.7 = (bf16[3,1024,384]{2,1,0:T(8,128)(2,1)}, f32[2,1,384]{2,1,0:T(1,128)}, f32[2,1,384]{2,1,0:T(1,128)}) custom-call(s32[2]{0:T(128)} %refs_0_.13, bf16[1024,2304]{1,0:T(8,128)(2,1)} %qkv.2.refs_1_.refs_2_.refs_3_, bf16[1024,2304]{1,0:T(8,128)(2,1)} %qkv.2.refs_1_.refs_2_.refs_3_, bf16[1024,2304]{1,0:T(8,128)(2,1)} %qkv.2.refs_1_.refs_2_.refs_3_, ...), custom_call_target="tpu_custom_call" | custom-call | flops 2400000000 | bytes 1200000 | tf_op jit(solution)/shard_map/attend_back/pallas_call | solution.py:382
  348.0 1.5 fusion.9
  350.4 1.5 collective-permute-start.25
  352.0 14.6 %wgrad_heads.2 = (bf16[2,2,4,5,24,384]{5,4,3,2,1,0:T(8,128)(2,1)}, bf16[2,2,4,5,24,384]{5,4,3,2,1,0:T(8,128)(2,1)}) custom-call(s32[1]{0:T(128)} %bitcast.1.core_ref, bf16[1024,768]{1,0:T(8,128)(2,1)} %get-tuple-element.161.x_ref.a_ref, bf16[1024,768]{1,0:T(8,128)(2,1)} %c_ref.3, bf16[3,1024,384]{2,1,0:T(8,128)(2,1)} %get-tuple-element.127.e0_ref.b_ref, ...), custom_call_target="tpu_custom_call" | custom-call | flops 2400000000 | bytes 1200000 | tf_op jit(solution)/shard_map/wgrad_heads/pallas_call | solution.py:520
  366.9 9.4 %wgrad_heads.3 = (bf16[2,2,4,4,24,384]{5,4,3,2,1,0:T(8,128)(2,1)}, bf16[2,2,4,4,24,384]{5,4,3,2,1,0:T(8,128)(2,1)}) custom-call(s32[1]{0:T(128)} %bitcast.1.core_ref, bf16[1024,768]{1,0:T(8,128)(2,1)} %get-tuple-element.161.x_ref.a_ref, bf16[1024,768]{1,0:T(8,128)(2,1)} %c_ref.3, bf16[3,1024,384]{2,1,0:T(8,128)(2,1)} %get-tuple-element.128.e1_ref.b_ref, ...), custom_call_target="tpu_custom_call" | custom-call | flops 2400000000 | bytes 1200000 | tf_op jit(solution)/shard_map/wgrad_heads/pallas_call | solution.py:520
  376.8 1.7 fusion.5
  379.7 3.4 collective-permute-start.27
  383.1 2.1 collective-permute-start.42
  385.2 1.5 fusion.11
  386.8 1.1 collective-permute-done.26
  387.9 1.3 collective-permute-start.43
  389.2 5.0 %collective-permute-done.27 = bf16[4,24,768]{2,1,0:T(8,128)(2,1)S(1)} collective-permute-done((bf16[4,24,768]{2,1,0:T(8,128)(2,1)S(1)}, bf16[4,24,768]{2,1,0:T(8,128)(2,1)S(1)}, u32[]{:S(2)}, u32[]{:S(2)}) %collective-permute-start.27) | collective-permute-done | bytes 147488 | tf_op jit(solution)/shard_map/ppermute | solution.py:602
  394.2 7.3 %collective-permute-start.44 = (bf16[4,24,768]{2,1,0:T(8,128)(2,1)S(1)}, bf16[4,24,768]{2,1,0:T(8,128)(2,1)S(1)}, u32[]{:S(2)}, u32[]{:S(2)}) collective-permute-start(bf16[4,24,768]{2,1,0:T(8,128)(2,1)S(1)} %get-tuple-element.196), channel_id=1, source_target_pairs={{0,6},{1,7},{2,0},{3,1},{4,2},{5,3},{6,4},{7,5},{8,14},{9,15},{10,... | collective-permute-start | bytes 442376 | tf_op jit(solution)/shard_map/ppermute | solution.py:602
  401.5 1.5 collective-permute-start.37
  403.8 9.5 %dx.3 = bf16[1024,768]{1,0:T(8,128)(2,1)} custom-call(f32[1024,768]{1,0:T(8,128)} %get-tuple-element.176.dz1_ref, bf16[3,1024,384]{2,1,0:T(8,128)(2,1)} %get-tuple-element.150.d_ref.e0_ref, bf16[3,1024,384]{2,1,0:T(8,128)(2,1)} %get-tuple-element.152.d_ref.e1_ref, bf16[5,768,768]{2,1,0:T(8,128)(2,1)} %bitcast.175), custom_call_target="tpu_custom_call" | custom-call | flops 1800000000 | bytes 900000 | tf_op jit(solution)/shard_map/dx/pallas_call | solution.py:415
  415.1 1.8 collective-permute-start.38
  416.9 4.2 collective-permute-done.33
  421.3 5.1 %collective-permute-start.34 = (bf16[5,24,384]{2,1,0:T(8,128)(2,1)S(1)}, bf16[5,24,384]{2,1,0:T(8,128)(2,1)S(1)}, u32[]{:S(2)}, u32[]{:S(2)}) collective-permute-start(bf16[5,24,384]{2,1,0:T(8,128)(2,1)S(1)} %get-tuple-element.203), channel_id=1, source_target_pairs={{0,2},{1,3},{2,4},{3,5},{4,6},{5,7},{6,0},{7,1},{8,10},{9,11},{10,... | collective-permute-start | bytes 276488 | tf_op jit(solution)/shard_map/ppermute | solution.py:602
  426.4 2.4 collective-permute-start.36
  429.0 2.5 collective-permute-start.40
  431.5 1.3 collective-permute-start.41
  432.8 3.2 collective-permute-done.35
  436.7 3.5 collective-permute-done.40
  (138 shorter events, 22.1 us)
Async XLA Ops:
  2.4 10.8 %collective-permute-start = (bf16[5,24,768]{2,1,0:T(8,128)(2,1)}, bf16[5,24,768]{2,1,0:T(8,128)(2,1)S(1)}, u32[]{:S(2)}, u32[]{:S(2)}) collective-permute-start(bf16[5,24,768]{2,1,0:T(8,128)(2,1)} %pack_one.1), channel_id=1, source_target_pairs={{0,2},{1,3},{2,4},{3,5},{4,6},{5,7},{6,0},{7,1},{8,10},{9,11},{10,... | collective-permute-start | bytes 552968 | tf_op jit(solution)/shard_map/ppermute | solution.py:602
  5.4 14.9 %collective-permute-start.1 = (bf16[5,24,768]{2,1,0:T(8,128)(2,1)}, bf16[5,24,768]{2,1,0:T(8,128)(2,1)S(1)}, u32[]{:S(2)}, u32[]{:S(2)}) collective-permute-start(bf16[5,24,768]{2,1,0:T(8,128)(2,1)} %pack_one.1), channel_id=1, source_target_pairs={{0,4},{1,5},{2,6},{3,7},{4,0},{5,1},{6,2},{7,3},{8,12},{9,13},{10,... | collective-permute-start | bytes 552968 | tf_op jit(solution)/shard_map/ppermute | solution.py:602
  8.0 12.3 %collective-permute-start.2 = (bf16[5,24,768]{2,1,0:T(8,128)(2,1)}, bf16[5,24,768]{2,1,0:T(8,128)(2,1)S(1)}, u32[]{:S(2)}, u32[]{:S(2)}) collective-permute-start(bf16[5,24,768]{2,1,0:T(8,128)(2,1)} %pack_one.1), channel_id=1, source_target_pairs={{0,6},{1,7},{2,0},{3,1},{4,2},{5,3},{6,4},{7,5},{8,14},{9,15},{10,... | collective-permute-start | bytes 552968 | tf_op jit(solution)/shard_map/ppermute | solution.py:602
  11.1 24.0 %collective-permute-start.11 = (bf16[8,24,768]{2,1,0:T(8,128)(2,1)}, bf16[8,24,768]{2,1,0:T(8,128)(2,1)S(1)}, u32[]{:S(2)}, u32[]{:S(2)}) collective-permute-start(bf16[8,24,768]{2,1,0:T(8,128)(2,1)} %pack_two.1), channel_id=1, source_target_pairs={{0,2},{1,3},{2,0},{3,1},{4,6},{5,7},{6,4},{7,5},{8,10},{9,11},{10,... | collective-permute-start | bytes 884744 | tf_op jit(solution)/shard_map/ppermute | solution.py:606
  21.4 13.8 %copy-start.3 = (bf16[8,24,768]{2,1,0:T(8,128)(2,1)S(1)}, bf16[8,24,768]{2,1,0:T(8,128)(2,1)}, u32[]{:S(2)}) copy-start(bf16[8,24,768]{2,1,0:T(8,128)(2,1)} %pack_two.1) | copy-start | bytes 884740
  21.4 12.1 %collective-permute-start.6 = (bf16[4,3,24,768]{3,2,1,0:T(8,128)(2,1)S(1)}, bf16[4,3,24,768]{3,2,1,0:T(8,128)(2,1)S(1)}, u32[]{:S(2)}, u32[]{:S(2)}) collective-permute-start(bf16[4,3,24,768]{3,2,1,0:T(8,128)(2,1)S(1)} %pad_maximum_fusion.7), channel_id=1, source_target_pairs={{0,16},{1,17},{2,18},{3,19},{4,20},{5,21},{6,22},{7,23},{8,24},{9,... | collective-permute-start | bytes 1327112 | tf_op jit(solution)/shard_map/ppermute | solution.py:602
  24.0 15.6 %collective-permute-start.3 = (bf16[4,2,24,768]{3,2,1,0:T(8,128)(2,1)S(1)}, bf16[4,2,24,768]{3,2,1,0:T(8,128)(2,1)S(1)}, u32[]{:S(2)}, u32[]{:S(2)}) collective-permute-start(bf16[4,2,24,768]{3,2,1,0:T(8,128)(2,1)S(1)} %pad_maximum_fusion.8), channel_id=1, source_target_pairs={{0,1},{1,0},{2,3},{3,2},{4,5},{5,4},{6,7},{7,6},{8,9},{9,8},{10,11... | collective-permute-start | bytes 884744 | tf_op jit(solution)/shard_map/ppermute | solution.py:602
  33.5 32.5 %copy-start.2 = (bf16[2,4,3,24,768]{4,3,2,1,0:T(8,128)(2,1)}, bf16[2,4,3,24,768]{4,3,2,1,0:T(8,128)(2,1)S(1)}, u32[]{:S(2)}) copy-start(bf16[2,4,3,24,768]{4,3,2,1,0:T(8,128)(2,1)S(1)} %pad_maximum_fusion.2.refs_5_) | copy-start | bytes 2654212
  33.5 32.5 %collective-permute-start.7 = (bf16[2,4,3,24,768]{4,3,2,1,0:T(8,128)(2,1)S(1)}, bf16[2,4,3,24,768]{4,3,2,1,0:T(8,128)(2,1)S(1)}, u32[]{:S(2)}, u32[]{:S(2)}) collective-permute-start(bf16[2,4,3,24,768]{4,3,2,1,0:T(8,128)(2,1)S(1)} %pad_maximum_fusion.2.refs_5_), channel_id=1, source_target_pairs={{0,1},{1,0},{2,3},{3,2},{4,5},{5,4},{6,7},{7,6},{8,9},{9,8},{10,11... | collective-permute-start | bytes 2654216 | tf_op jit(solution)/shard_map/ppermute | solution.py:602
  36.0 28.9 %collective-permute-start.12 = (bf16[2,8,24,768]{3,2,1,0:T(8,128)(2,1)}, bf16[2,8,24,768]{3,2,1,0:T(8,128)(2,1)}, u32[]{:S(2)}, u32[]{:S(2)}) collective-permute-start(bf16[2,8,24,768]{3,2,1,0:T(8,128)(2,1)} %pad_maximum_fusion.4), channel_id=1, source_target_pairs={{0,4},{1,5},{2,6},{3,7},{4,0},{5,1},{6,2},{7,3},{8,12},{9,13},{10,... | collective-permute-start | bytes 1769480 | tf_op jit(solution)/shard_map/ppermute | solution.py:606
  39.7 26.6 %copy-start.4 = (bf16[2,4,2,24,768]{4,3,2,1,0:T(8,128)(2,1)}, bf16[2,4,2,24,768]{4,3,2,1,0:T(8,128)(2,1)S(1)}, u32[]{:S(2)}) copy-start(bf16[2,4,2,24,768]{4,3,2,1,0:T(8,128)(2,1)S(1)} %pad_maximum_fusion.3.refs_1_) | copy-start | bytes 1769476
  39.7 26.4 %collective-permute-start.5 = (bf16[2,4,2,24,768]{4,3,2,1,0:T(8,128)(2,1)S(1)}, bf16[2,4,2,24,768]{4,3,2,1,0:T(8,128)(2,1)S(1)}, u32[]{:S(2)}, u32[]{:S(2)}) collective-permute-start(bf16[2,4,2,24,768]{4,3,2,1,0:T(8,128)(2,1)S(1)} %pad_maximum_fusion.3.refs_1_), channel_id=1, source_target_pairs={{0,16},{1,17},{2,18},{3,19},{4,20},{5,21},{6,22},{7,23},{8,24},{9,... | collective-permute-start | bytes 1769480 | tf_op jit(solution)/shard_map/ppermute | solution.py:602
  41.2 27.5 %collective-permute-start.4 = (bf16[2,4,2,24,768]{4,3,2,1,0:T(8,128)(2,1)S(1)}, bf16[2,4,2,24,768]{4,3,2,1,0:T(8,128)(2,1)S(1)}, u32[]{:S(2)}, u32[]{:S(2)}) collective-permute-start(bf16[2,4,2,24,768]{4,3,2,1,0:T(8,128)(2,1)S(1)} %pad_maximum_fusion.3.refs_1_), channel_id=1, source_target_pairs={{0,8},{1,9},{2,10},{3,11},{4,12},{5,13},{6,14},{7,15},{8,0},{9,1},... | collective-permute-start | bytes 1769480 | tf_op jit(solution)/shard_map/ppermute | solution.py:602
  41.2 28.7 %collective-permute-start.9 = (bf16[2,4,3,24,768]{4,3,2,1,0:T(8,128)(2,1)S(1)}, bf16[2,4,3,24,768]{4,3,2,1,0:T(8,128)(2,1)S(1)}, u32[]{:S(2)}, u32[]{:S(2)}) collective-permute-start(bf16[2,4,3,24,768]{4,3,2,1,0:T(8,128)(2,1)S(1)} %pad_maximum_fusion.2.refs_5_), channel_id=1, source_target_pairs={{0,8},{1,9},{2,10},{3,11},{4,12},{5,13},{6,14},{7,15},{8,0},{9,1},... | collective-permute-start | bytes 2654216 | tf_op jit(solution)/shard_map/ppermute | solution.py:602
  66.0 0.9 copy-start.16
  66.1 1.1 copy-start.13
  66.1 3.8 collective-permute-start.10
  66.2 3.7 collective-permute-start.8
  67.2 21.0 %collective-permute-start.14 = (bf16[4,4,24,768]{3,2,1,0:T(8,128)(2,1)S(1)}, bf16[4,4,24,768]{3,2,1,0:T(8,128)(2,1)}, u32[]{:S(2)}, u32[]{:S(2)}) collective-permute-start(bf16[4,4,24,768]{3,2,1,0:T(8,128)(2,1)S(1)} %pad_maximum_fusion.6), channel_id=1, source_target_pairs={{0,16},{1,17},{2,18},{3,19},{4,20},{5,21},{6,22},{7,23},{8,24},{9,... | collective-permute-start | bytes 1769480 | tf_op jit(solution)/shard_map/ppermute | solution.py:602
  68.8 1.2 copy-start.17
  68.8 22.1 %collective-permute-start.13 = (bf16[4,4,24,768]{3,2,1,0:T(8,128)(2,1)S(1)}, bf16[4,4,24,768]{3,2,1,0:T(8,128)(2,1)S(1)}, u32[]{:S(2)}, u32[]{:S(2)}) collective-permute-start(bf16[4,4,24,768]{3,2,1,0:T(8,128)(2,1)S(1)} %pad_maximum_fusion.5), channel_id=1, source_target_pairs={{0,1},{1,0},{2,3},{3,2},{4,5},{5,4},{6,7},{7,6},{8,9},{9,8},{10,11... | collective-permute-start | bytes 1769480 | tf_op jit(solution)/shard_map/ppermute | solution.py:602
  69.9 0.9 copy-start.14
  69.9 1.1 copy-start.18
  71.0 0.9 copy-start.15
  89.3 15.8 %copy-start = (bf16[2,4,4,24,768]{4,3,2,1,0:T(8,128)(2,1)}, bf16[2,4,4,24,768]{4,3,2,1,0:T(8,128)(2,1)S(1)}, u32[]{:S(2)}) copy-start(bf16[2,4,4,24,768]{4,3,2,1,0:T(8,128)(2,1)S(1)} %pad_maximum_fusion.1.refs_5_) | copy-start | bytes 3538948
  89.3 27.3 %collective-permute-start.17 = (bf16[2,4,4,24,768]{4,3,2,1,0:T(8,128)(2,1)S(1)}, bf16[2,4,4,24,768]{4,3,2,1,0:T(8,128)(2,1)S(1)}, u32[]{:S(2)}, u32[]{:S(2)}) collective-permute-start(bf16[2,4,4,24,768]{4,3,2,1,0:T(8,128)(2,1)S(1)} %pad_maximum_fusion.1.refs_5_), channel_id=1, source_target_pairs={{0,1},{1,0},{2,3},{3,2},{4,5},{5,4},{6,7},{7,6},{8,9},{9,8},{10,11... | collective-permute-start | bytes 3538952 | tf_op jit(solution)/shard_map/ppermute | solution.py:602
  91.0 14.1 %copy-start.1 = (bf16[2,4,4,24,768]{4,3,2,1,0:T(8,128)(2,1)}, bf16[2,4,4,24,768]{4,3,2,1,0:T(8,128)(2,1)S(1)}, u32[]{:S(2)}) copy-start(bf16[2,4,4,24,768]{4,3,2,1,0:T(8,128)(2,1)S(1)} %pad_maximum_fusion.refs_1_) | copy-start | bytes 3538948
  91.0 26.9 %collective-permute-start.16 = (bf16[2,4,4,24,768]{4,3,2,1,0:T(8,128)(2,1)S(1)}, bf16[2,4,4,24,768]{4,3,2,1,0:T(8,128)(2,1)S(1)}, u32[]{:S(2)}, u32[]{:S(2)}) collective-permute-start(bf16[2,4,4,24,768]{4,3,2,1,0:T(8,128)(2,1)S(1)} %pad_maximum_fusion.refs_1_), channel_id=1, source_target_pairs={{0,16},{1,17},{2,18},{3,19},{4,20},{5,21},{6,22},{7,23},{8,24},{9,... | collective-permute-start | bytes 3538952 | tf_op jit(solution)/shard_map/ppermute | solution.py:602
  91.6 26.9 %collective-permute-start.19 = (bf16[2,4,4,24,768]{4,3,2,1,0:T(8,128)(2,1)S(1)}, bf16[2,4,4,24,768]{4,3,2,1,0:T(8,128)(2,1)S(1)}, u32[]{:S(2)}, u32[]{:S(2)}) collective-permute-start(bf16[2,4,4,24,768]{4,3,2,1,0:T(8,128)(2,1)S(1)} %pad_maximum_fusion.1.refs_5_), channel_id=1, source_target_pairs={{0,8},{1,9},{2,10},{3,11},{4,12},{5,13},{6,14},{7,15},{8,0},{9,1},... | collective-permute-start | bytes 3538952 | tf_op jit(solution)/shard_map/ppermute | solution.py:602
  91.6 26.9 %collective-permute-start.15 = (bf16[2,4,4,24,768]{4,3,2,1,0:T(8,128)(2,1)S(1)}, bf16[2,4,4,24,768]{4,3,2,1,0:T(8,128)(2,1)S(1)}, u32[]{:S(2)}, u32[]{:S(2)}) collective-permute-start(bf16[2,4,4,24,768]{4,3,2,1,0:T(8,128)(2,1)S(1)} %pad_maximum_fusion.refs_1_), channel_id=1, source_target_pairs={{0,8},{1,9},{2,10},{3,11},{4,12},{5,13},{6,14},{7,15},{8,0},{9,1},... | collective-permute-start | bytes 3538952 | tf_op jit(solution)/shard_map/ppermute | solution.py:602
  116.6 6.9 %copy-start.7 = (bf16[2,4,4,24,768]{4,3,2,1,0:T(8,128)(2,1)}, bf16[2,4,4,24,768]{4,3,2,1,0:T(8,128)(2,1)S(1)}, u32[]{:S(2)}) copy-start(bf16[2,4,4,24,768]{4,3,2,1,0:T(8,128)(2,1)S(1)} %collective-permute-done.17.refs_7_) | copy-start | bytes 3538948
  118.0 5.5 %copy-start.8 = (bf16[2,4,4,24,768]{4,3,2,1,0:T(8,128)(2,1)}, bf16[2,4,4,24,768]{4,3,2,1,0:T(8,128)(2,1)S(1)}, u32[]{:S(2)}) copy-start(bf16[2,4,4,24,768]{4,3,2,1,0:T(8,128)(2,1)S(1)} %collective-permute-done.16.refs_3_) | copy-start | bytes 3538948
  118.0 4.5 %collective-permute-start.18 = (bf16[2,4,4,24,768]{4,3,2,1,0:T(8,128)(2,1)S(1)}, bf16[2,4,4,24,768]{4,3,2,1,0:T(8,128)(2,1)S(1)}, u32[]{:S(2)}, u32[]{:S(2)}) collective-permute-start(bf16[2,4,4,24,768]{4,3,2,1,0:T(8,128)(2,1)S(1)} %collective-permute-done.16.refs_3_), channel_id=1, source_target_pairs={{0,8},{1,9},{2,10},{3,11},{4,12},{5,13},{6,14},{7,15},{8,0},{9,1},... | collective-permute-start | bytes 3538952 | tf_op jit(solution)/shard_map/ppermute | solution.py:602
  118.0 5.5 %collective-permute-start.20 = (bf16[2,4,4,24,768]{4,3,2,1,0:T(8,128)(2,1)S(1)}, bf16[2,4,4,24,768]{4,3,2,1,0:T(8,128)(2,1)}, u32[]{:S(2)}, u32[]{:S(2)}) collective-permute-start(bf16[2,4,4,24,768]{4,3,2,1,0:T(8,128)(2,1)S(1)} %collective-permute-done.17.refs_7_), channel_id=1, source_target_pairs={{0,8},{1,9},{2,10},{3,11},{4,12},{5,13},{6,14},{7,15},{8,0},{9,1},... | collective-permute-start | bytes 3538952 | tf_op jit(solution)/shard_map/ppermute | solution.py:602
  118.5 5.0 %copy-start.9 = (bf16[2,4,4,24,768]{4,3,2,1,0:T(8,128)(2,1)}, bf16[2,4,4,24,768]{4,3,2,1,0:T(8,128)(2,1)S(1)}, u32[]{:S(2)}) copy-start(bf16[2,4,4,24,768]{4,3,2,1,0:T(8,128)(2,1)S(1)} %collective-permute-done.19.refs_6_) | copy-start | bytes 3538948
  118.5 5.0 %copy-start.10 = (bf16[2,4,4,24,768]{4,3,2,1,0:T(8,128)(2,1)}, bf16[2,4,4,24,768]{4,3,2,1,0:T(8,128)(2,1)S(1)}, u32[]{:S(2)}) copy-start(bf16[2,4,4,24,768]{4,3,2,1,0:T(8,128)(2,1)S(1)} %collective-permute-done.15.refs_2_) | copy-start | bytes 3538948
  122.5 1.0 copy-start.11
  309.6 4.9 %collective-permute-start.22 = (bf16[2,2,4,4,24,768]{5,4,3,2,1,0:T(8,128)(2,1)}, bf16[2,2,4,4,24,768]{5,4,3,2,1,0:T(8,128)(2,1)}, u32[]{:S(2)}, u32[]{:S(2)}) collective-permute-start(bf16[2,2,4,4,24,768]{5,4,3,2,1,0:T(8,128)(2,1)} %get-tuple-element.147), channel_id=1, source_target_pairs={{0,8},{1,9},{2,10},{3,11},{4,12},{5,13},{6,14},{7,15},{8,0},{9,1},... | collective-permute-start | bytes 7077896 | tf_op jit(solution)/shard_map/ppermute | solution.py:602
  309.7 9.5 %collective-permute-start.21 = (bf16[2,2,4,4,24,768]{5,4,3,2,1,0:T(8,128)(2,1)}, bf16[2,2,4,4,24,768]{5,4,3,2,1,0:T(8,128)(2,1)}, u32[]{:S(2)}, u32[]{:S(2)}) collective-permute-start(bf16[2,2,4,4,24,768]{5,4,3,2,1,0:T(8,128)(2,1)} %get-tuple-element.144), channel_id=1, source_target_pairs={{0,8},{1,9},{2,10},{3,11},{4,12},{5,13},{6,14},{7,15},{8,0},{9,1},... | collective-permute-start | bytes 7077896 | tf_op jit(solution)/shard_map/ppermute | solution.py:602
  314.4 4.8 %copy-start.5 = (bf16[2,2,4,4,24,768]{5,4,3,2,1,0:T(8,128)(2,1)S(1)}, bf16[2,2,4,4,24,768]{5,4,3,2,1,0:T(8,128)(2,1)}, u32[]{:S(2)}) copy-start(bf16[2,2,4,4,24,768]{5,4,3,2,1,0:T(8,128)(2,1)} %get-tuple-element.143) | copy-start | bytes 7077892
  318.7 29.4 %collective-permute-start.24 = (bf16[2,4,4,24,768]{4,3,2,1,0:T(8,128)(2,1)}, bf16[2,4,4,24,768]{4,3,2,1,0:T(8,128)(2,1)}, u32[]{:S(2)}, u32[]{:S(2)}) collective-permute-start(bf16[2,4,4,24,768]{4,3,2,1,0:T(8,128)(2,1)} %get-tuple-element.180), channel_id=1, source_target_pairs={{0,16},{1,17},{2,18},{3,19},{4,20},{5,21},{6,22},{7,23},{8,24},{9,... | collective-permute-start | bytes 3538952 | tf_op jit(solution)/shard_map/ppermute | solution.py:602
  321.6 28.6 %collective-permute-start.23 = (bf16[2,4,4,24,768]{4,3,2,1,0:T(8,128)(2,1)S(1)}, bf16[2,4,4,24,768]{4,3,2,1,0:T(8,128)(2,1)S(1)}, u32[]{:S(2)}, u32[]{:S(2)}) collective-permute-start(bf16[2,4,4,24,768]{4,3,2,1,0:T(8,128)(2,1)S(1)} %get-tuple-element.182), channel_id=1, source_target_pairs={{0,1},{1,0},{2,3},{3,2},{4,5},{5,4},{6,7},{7,6},{8,9},{9,8},{10,11... | collective-permute-start | bytes 3538952 | tf_op jit(solution)/shard_map/ppermute | solution.py:602
  349.6 17.0 %collective-permute-start.29 = (bf16[4,4,24,768]{3,2,1,0:T(8,128)(2,1)S(1)}, bf16[4,4,24,768]{3,2,1,0:T(8,128)(2,1)S(1)}, u32[]{:S(2)}, u32[]{:S(2)}) collective-permute-start(bf16[4,4,24,768]{3,2,1,0:T(8,128)(2,1)S(1)} %get-tuple-element.188), channel_id=1, source_target_pairs={{0,1},{1,0},{2,3},{3,2},{4,5},{5,4},{6,7},{7,6},{8,9},{9,8},{10,11... | collective-permute-start | bytes 1769480 | tf_op jit(solution)/shard_map/ppermute | solution.py:602
  350.4 16.3 %collective-permute-start.25 = (bf16[4,4,24,768]{3,2,1,0:T(8,128)(2,1)S(1)}, bf16[4,4,24,768]{3,2,1,0:T(8,128)(2,1)S(1)}, u32[]{:S(2)}, u32[]{:S(2)}) collective-permute-start(bf16[4,4,24,768]{3,2,1,0:T(8,128)(2,1)S(1)} %get-tuple-element.190), channel_id=1, source_target_pairs={{0,16},{1,17},{2,18},{3,19},{4,20},{5,21},{6,22},{7,23},{8,24},{9,... | collective-permute-start | bytes 1769480 | tf_op jit(solution)/shard_map/ppermute | solution.py:602
  366.5 10.3 %collective-permute-start.30 = (bf16[2,2,4,5,24,384]{5,4,3,2,1,0:T(8,128)(2,1)}, bf16[2,2,4,5,24,384]{5,4,3,2,1,0:T(8,128)(2,1)}, u32[]{:S(2)}, u32[]{:S(2)}) collective-permute-start(bf16[2,2,4,5,24,384]{5,4,3,2,1,0:T(8,128)(2,1)} %get-tuple-element.174), channel_id=1, source_target_pairs={{0,8},{1,9},{2,10},{3,11},{4,12},{5,13},{6,14},{7,15},{8,0},{9,1},... | collective-permute-start | bytes 4423688 | tf_op jit(solution)/shard_map/ppermute | solution.py:602
  366.9 10.0 %copy-start.6 = (bf16[2,2,4,5,24,384]{5,4,3,2,1,0:T(8,128)(2,1)S(1)}, bf16[2,2,4,5,24,384]{5,4,3,2,1,0:T(8,128)(2,1)}, u32[]{:S(2)}) copy-start(bf16[2,2,4,5,24,384]{5,4,3,2,1,0:T(8,128)(2,1)} %get-tuple-element.173) | copy-start | bytes 4423684
  376.3 6.8 %collective-permute-start.31 = (bf16[2,2,4,4,24,384]{5,4,3,2,1,0:T(8,128)(2,1)}, bf16[2,2,4,4,24,384]{5,4,3,2,1,0:T(8,128)(2,1)}, u32[]{:S(2)}, u32[]{:S(2)}) collective-permute-start(bf16[2,2,4,4,24,384]{5,4,3,2,1,0:T(8,128)(2,1)} %get-tuple-element.175), channel_id=1, source_target_pairs={{0,8},{1,9},{2,10},{3,11},{4,12},{5,13},{6,14},{7,15},{8,0},{9,1},... | collective-permute-start | bytes 3538952 | tf_op jit(solution)/shard_map/ppermute | solution.py:602
  378.5 6.7 %copy-start.12 = (bf16[2,2,4,4,24,384]{5,4,3,2,1,0:T(8,128)(2,1)S(1)}, bf16[2,2,4,4,24,384]{5,4,3,2,1,0:T(8,128)(2,1)}, u32[]{:S(2)}) copy-start(bf16[2,2,4,4,24,384]{5,4,3,2,1,0:T(8,128)(2,1)} %get-tuple-element.172) | copy-start | bytes 3538948
  378.5 34.8 %collective-permute-start.32 = (bf16[2,4,5,24,384]{4,3,2,1,0:T(8,128)(2,1)S(1)}, bf16[2,4,5,24,384]{4,3,2,1,0:T(8,128)(2,1)S(1)}, u32[]{:S(2)}, u32[]{:S(2)}) collective-permute-start(bf16[2,4,5,24,384]{4,3,2,1,0:T(8,128)(2,1)S(1)} %get-tuple-element.184), channel_id=1, source_target_pairs={{0,1},{1,0},{2,3},{3,2},{4,5},{5,4},{6,7},{7,6},{8,9},{9,8},{10,11... | collective-permute-start | bytes 2211848 | tf_op jit(solution)/shard_map/ppermute | solution.py:602
  379.2 8.7 %collective-permute-start.26 = (bf16[4,24,768]{2,1,0:T(8,128)(2,1)S(1)}, bf16[4,24,768]{2,1,0:T(8,128)(2,1)S(1)}, u32[]{:S(2)}, u32[]{:S(2)}) collective-permute-start(bf16[4,24,768]{2,1,0:T(8,128)(2,1)S(1)} %get-tuple-element.198), channel_id=1, source_target_pairs={{0,2},{1,3},{2,4},{3,5},{4,6},{5,7},{6,0},{7,1},{8,10},{9,11},{10,... | collective-permute-start | bytes 442376 | tf_op jit(solution)/shard_map/ppermute | solution.py:602
  379.7 14.5 %collective-permute-start.27 = (bf16[4,24,768]{2,1,0:T(8,128)(2,1)S(1)}, bf16[4,24,768]{2,1,0:T(8,128)(2,1)S(1)}, u32[]{:S(2)}, u32[]{:S(2)}) collective-permute-start(bf16[4,24,768]{2,1,0:T(8,128)(2,1)S(1)} %get-tuple-element.200), channel_id=1, source_target_pairs={{0,4},{1,5},{2,6},{3,7},{4,0},{5,1},{6,2},{7,3},{8,12},{9,13},{10,... | collective-permute-start | bytes 442376 | tf_op jit(solution)/shard_map/ppermute | solution.py:602
  383.1 18.4 %collective-permute-start.28 = (bf16[4,24,768]{2,1,0:T(8,128)(2,1)S(1)}, bf16[4,24,768]{2,1,0:T(8,128)(2,1)S(1)}, u32[]{:S(2)}, u32[]{:S(2)}) collective-permute-start(bf16[4,24,768]{2,1,0:T(8,128)(2,1)S(1)} %get-tuple-element.199), channel_id=1, source_target_pairs={{0,6},{1,7},{2,0},{3,1},{4,2},{5,3},{6,4},{7,5},{8,14},{9,15},{10,... | collective-permute-start | bytes 442376 | tf_op jit(solution)/shard_map/ppermute | solution.py:602
  383.1 31.0 %collective-permute-start.42 = (bf16[4,24,768]{2,1,0:T(8,128)(2,1)S(1)}, bf16[4,24,768]{2,1,0:T(8,128)(2,1)S(1)}, u32[]{:S(2)}, u32[]{:S(2)}) collective-permute-start(bf16[4,24,768]{2,1,0:T(8,128)(2,1)S(1)} %get-tuple-element.195), channel_id=1, source_target_pairs={{0,2},{1,3},{2,4},{3,5},{4,6},{5,7},{6,0},{7,1},{8,10},{9,11},{10,... | collective-permute-start | bytes 442376 | tf_op jit(solution)/shard_map/ppermute | solution.py:602
  387.9 26.3 %collective-permute-start.43 = (bf16[4,24,768]{2,1,0:T(8,128)(2,1)S(1)}, bf16[4,24,768]{2,1,0:T(8,128)(2,1)S(1)}, u32[]{:S(2)}, u32[]{:S(2)}) collective-permute-start(bf16[4,24,768]{2,1,0:T(8,128)(2,1)S(1)} %get-tuple-element.197), channel_id=1, source_target_pairs={{0,4},{1,5},{2,6},{3,7},{4,0},{5,1},{6,2},{7,3},{8,12},{9,13},{10,... | collective-permute-start | bytes 442376 | tf_op jit(solution)/shard_map/ppermute | solution.py:602
  394.2 19.9 %collective-permute-start.44 = (bf16[4,24,768]{2,1,0:T(8,128)(2,1)S(1)}, bf16[4,24,768]{2,1,0:T(8,128)(2,1)S(1)}, u32[]{:S(2)}, u32[]{:S(2)}) collective-permute-start(bf16[4,24,768]{2,1,0:T(8,128)(2,1)S(1)} %get-tuple-element.196), channel_id=1, source_target_pairs={{0,6},{1,7},{2,0},{3,1},{4,2},{5,3},{6,4},{7,5},{8,14},{9,15},{10,... | collective-permute-start | bytes 442376 | tf_op jit(solution)/shard_map/ppermute | solution.py:602
  401.5 13.4 %collective-permute-start.37 = (bf16[2,4,4,24,384]{4,3,2,1,0:T(8,128)(2,1)S(1)}, bf16[2,4,4,24,384]{4,3,2,1,0:T(8,128)(2,1)S(1)}, u32[]{:S(2)}, u32[]{:S(2)}) collective-permute-start(bf16[2,4,4,24,384]{4,3,2,1,0:T(8,128)(2,1)S(1)} %get-tuple-element.186), channel_id=1, source_target_pairs={{0,16},{1,17},{2,18},{3,19},{4,20},{5,21},{6,22},{7,23},{8,24},{9,... | collective-permute-start | bytes 1769480 | tf_op jit(solution)/shard_map/ppermute | solution.py:602
  413.5 7.6 %collective-permute-start.33 = (bf16[4,5,24,384]{3,2,1,0:T(8,128)(2,1)S(1)}, bf16[4,5,24,384]{3,2,1,0:T(8,128)(2,1)S(1)}, u32[]{:S(2)}, u32[]{:S(2)}) collective-permute-start(bf16[4,5,24,384]{3,2,1,0:T(8,128)(2,1)S(1)} %get-tuple-element.192), channel_id=1, source_target_pairs={{0,16},{1,17},{2,18},{3,19},{4,20},{5,21},{6,22},{7,23},{8,24},{9,... | collective-permute-start | bytes 1105928 | tf_op jit(solution)/shard_map/ppermute | solution.py:602
  415.1 13.7 %collective-permute-start.38 = (bf16[4,4,24,384]{3,2,1,0:T(8,128)(2,1)S(1)}, bf16[4,4,24,384]{3,2,1,0:T(8,128)(2,1)S(1)}, u32[]{:S(2)}, u32[]{:S(2)}) collective-permute-start(bf16[4,4,24,384]{3,2,1,0:T(8,128)(2,1)S(1)} %get-tuple-element.194), channel_id=1, source_target_pairs={{0,1},{1,0},{2,3},{3,2},{4,5},{5,4},{6,7},{7,6},{8,9},{9,8},{10,11... | collective-permute-start | bytes 884744 | tf_op jit(solution)/shard_map/ppermute | solution.py:602
  421.3 10.2 %collective-permute-start.34 = (bf16[5,24,384]{2,1,0:T(8,128)(2,1)S(1)}, bf16[5,24,384]{2,1,0:T(8,128)(2,1)S(1)}, u32[]{:S(2)}, u32[]{:S(2)}) collective-permute-start(bf16[5,24,384]{2,1,0:T(8,128)(2,1)S(1)} %get-tuple-element.203), channel_id=1, source_target_pairs={{0,2},{1,3},{2,4},{3,5},{4,6},{5,7},{6,0},{7,1},{8,10},{9,11},{10,... | collective-permute-start | bytes 276488 | tf_op jit(solution)/shard_map/ppermute | solution.py:602
  426.4 9.6 %collective-permute-start.35 = (bf16[5,24,384]{2,1,0:T(8,128)(2,1)S(1)}, bf16[5,24,384]{2,1,0:T(8,128)(2,1)S(1)}, u32[]{:S(2)}, u32[]{:S(2)}) collective-permute-start(bf16[5,24,384]{2,1,0:T(8,128)(2,1)S(1)} %get-tuple-element.205), channel_id=1, source_target_pairs={{0,4},{1,5},{2,6},{3,7},{4,0},{5,1},{6,2},{7,3},{8,12},{9,13},{10,... | collective-permute-start | bytes 276488 | tf_op jit(solution)/shard_map/ppermute | solution.py:602
  426.4 9.6 %collective-permute-start.36 = (bf16[5,24,384]{2,1,0:T(8,128)(2,1)S(1)}, bf16[5,24,384]{2,1,0:T(8,128)(2,1)S(1)}, u32[]{:S(2)}, u32[]{:S(2)}) collective-permute-start(bf16[5,24,384]{2,1,0:T(8,128)(2,1)S(1)} %get-tuple-element.204), channel_id=1, source_target_pairs={{0,6},{1,7},{2,0},{3,1},{4,2},{5,3},{6,4},{7,5},{8,14},{9,15},{10,... | collective-permute-start | bytes 276488 | tf_op jit(solution)/shard_map/ppermute | solution.py:602
  428.9 7.8 %collective-permute-start.39 = (bf16[4,24,384]{2,1,0:T(8,128)(2,1)S(1)}, bf16[4,24,384]{2,1,0:T(8,128)(2,1)S(1)}, u32[]{:S(2)}, u32[]{:S(2)}) collective-permute-start(bf16[4,24,384]{2,1,0:T(8,128)(2,1)S(1)} %get-tuple-element.206), channel_id=1, source_target_pairs={{0,2},{1,3},{2,4},{3,5},{4,6},{5,7},{6,0},{7,1},{8,10},{9,11},{10,... | collective-permute-start | bytes 221192 | tf_op jit(solution)/shard_map/ppermute | solution.py:602
  429.0 11.2 %collective-permute-start.40 = (bf16[4,24,384]{2,1,0:T(8,128)(2,1)S(1)}, bf16[4,24,384]{2,1,0:T(8,128)(2,1)S(1)}, u32[]{:S(2)}, u32[]{:S(2)}) collective-permute-start(bf16[4,24,384]{2,1,0:T(8,128)(2,1)S(1)} %get-tuple-element.208), channel_id=1, source_target_pairs={{0,4},{1,5},{2,6},{3,7},{4,0},{5,1},{6,2},{7,3},{8,12},{9,13},{10,... | collective-permute-start | bytes 221192 | tf_op jit(solution)/shard_map/ppermute | solution.py:602
  431.5 8.7 %collective-permute-start.41 = (bf16[4,24,384]{2,1,0:T(8,128)(2,1)S(1)}, bf16[4,24,384]{2,1,0:T(8,128)(2,1)S(1)}, u32[]{:S(2)}, u32[]{:S(2)}) collective-permute-start(bf16[4,24,384]{2,1,0:T(8,128)(2,1)S(1)} %get-tuple-element.207), channel_id=1, source_target_pairs={{0,6},{1,7},{2,0},{3,1},{4,2},{5,3},{6,4},{7,5},{8,14},{9,15},{10,... | collective-permute-start | bytes 221192 | tf_op jit(solution)/shard_map/ppermute | solution.py:602

commit v6 on v5

--- a/solution.py
+++ b/solution.py
@@ -601,9 +601,9 @@
     def send(self, value, dim, step=1):
         return lax.ppermute(value, AXES, self.shift(dim, step))
 
-    def swap(self, value, bit):
-        pairs = [(i, i ^ (bit * self.y)) for i in range(self.count)]
-        return lax.ppermute(value, AXES, pairs)
+    def trade(self, value):
+        groups = [[z * self.y + y for z in range(self.z)] for y in range(self.y)]
+        return lax.all_to_all(value, "fsdp", 0, 0, tiled=True, axis_index_groups=groups)
 
 
 X, CORE, Z, Y = range(4)
@@ -680,7 +680,7 @@
             py = (y + (near if side == 0 else far)) % 2
             pc = (core + other) % 2
             for dz in range(4):
-                pz = lax.bitwise_xor(z, dz) if split else (z + 4 - dz) % 4
+                pz = dz if split else (z + 4 - dz) % 4
                 if split:
                     target = held[side].at[:, px, pc, pz, py] if side == 0 else held[side].at[px, pc, pz, py]
                 else:
@@ -734,18 +734,16 @@
 
 
 class Gather:
-    def __init__(self, grid, packet, first, by_bits):
+    def __init__(self, grid, packet, first, at_once):
         self.grid, self.first = grid, first
-        if by_bits:
-            pair = jnp.stack([packet, grid.swap(packet, 1)])
-            far = grid.swap(pair, 2)
-            self.ring = [pair[0], pair[1], far[0], far[1]]
+        if at_once:
+            self.ring = grid.trade(jnp.broadcast_to(packet, (4,) + packet.shape))
         else:
-            self.ring = [packet] + [grid.send(packet, Z, k) for k in range(1, 4)]
+            self.ring = jnp.stack([packet] + [grid.send(packet, Z, k) for k in range(1, 4)])
 
     def one(self, *others):
-        ring = lax.optimization_barrier((*self.ring, *others))[:4]
-        self.line = [jnp.stack([r[: self.first] for r in ring]), jnp.stack([r[self.first :] for r in ring])]
+        ring = after(self.ring, *others)
+        self.line = [ring[:, : self.first], ring[:, self.first :]]
         self.came = [self.grid.send(v, d) for v, d in zip(self.line, (Y, X))]
 
     def two(self, *others):
@@ -823,7 +821,7 @@
     first = first.reshape(5, grid.count * rows, D)
     vec = jnp.sum(first[4].reshape(grid.count, rows, D).astype(F32), axis=0)
     qkv = qkv_call(tokens, first, vec)
-    two.two(qkv)
+    two.two()
     ctx, lse = attend_call(after(qkv, *two.near), lengths)
     w_in, w_back = place(at, two.parts(ctx), True)
     w_in = w_in.reshape(4, grid.count * rows, D)

time: 447 us -> 438 us (0.980)
  waiting for transfers between devices: 77.9 us -> 64.5 us
  starting transfers between devices: 59.8 us -> 66.9 us
    ppermute x2 -> x0, waiting for transfers between devices: 23.2 us -> none  [swap(): return lax.ppermute(value, AXES, pairs)]
    ppermute x43, waiting for transfers between devices: 54.7 us -> 64.5 us  [send(): return lax.ppermute(value, AXES, self.shift(dim, step))]
    ppermute x43, starting transfers between devices: 55.5 us -> 63.2 us  [send(): return lax.ppermute(value, AXES, self.shift(dim, step))]
  transfers between devices with their start and end apart: 45 -> 44, of which waited for: 13 -> 15; matrix products, arithmetic and copies ran while one was open for 5% -> 5% of each run, Pallas kernels for 20% -> 20%
where the time goes in v6:
time: 438 us; the launch traced here: 431 us
  Pallas kernels  274 us (63%)
  starting transfers between devices  66.9 us (15%)
  waiting for transfers between devices  64.5 us (15%)
  other arithmetic  18 us (4%)
  local copies, waits for them, and re-layouts  6.39 us (1%)
    ppermute x43, waiting for transfers between devices, send(): return lax.ppermute(value, AXES, self.shift(dim, step))  64.5 us
    ppermute x43, starting transfers between devices, send(): return lax.ppermute(value, AXES, self.shift(dim, step))  63.2 us
    pallas_call x4, Pallas kernels, attend_back_call(): pl.pallas_call(body, grid_spec=pltpu.PrefetchScalarGridSpec(num_scalar_pr...  49.8 us
    pallas_call x2, Pallas kernels, ffn_back_call(): pl.pallas_call(ffn_back_body, grid=(rows // block,), in_specs=[line, line...  47.2 us
    pallas_call x2, Pallas kernels, ffn_call(): pl.pallas_call(lambda *refs: ffn_body(renorm, *refs), grid=(rows // block...  45 us
    pallas_call x2, Pallas kernels, attend_call(): pl.pallas_call(body, grid_spec=pltpu.PrefetchScalarGridSpec(num_scalar_pr...  25.9 us
    pallas_call x2, Pallas kernels, wgrad_heads_call(): pl.pallas_call(body, grid_spec=pltpu.PrefetchScalarGridSpec(num_scalar_pr...  24.2 us
    pallas_call x2, Pallas kernels, dx_call(): pl.pallas_call(dx_body, grid=(rows // block,), in_specs=[line, part, part...  18.8 us
  transfers between devices with their start and end apart: 44, of which 15 were waited for; matrix products, arithmetic and copies ran while one was open for 5% of the time, Pallas kernels for 20%

profile of v6, /device:TPU:0, one launch (start us, length us, event | category | flops | bytes accessed | tf_op | source)
XLA Modules:
  0.0 431.5 jit_solution(16589580772768207547)
XLA Ops:
  0.7 1.8 pack_one.1
  2.4 3.0 collective-permute-start
  5.4 2.6 collective-permute-start.1
  8.0 1.3 collective-permute-start.2
  9.4 1.7 pack_two.1
  11.1 2.0 broadcast_in_dim.44
  13.2 3.7 all-to-all-start
  16.8 3.5 collective-permute-done.1
  20.5 1.6 collective-permute-start.6
  22.1 1.6 collective-permute-start.3
  23.6 8.9 %collective-permute-done.6 = bf16[4,3,24,768]{3,2,1,0:T(8,128)(2,1)S(1)} collective-permute-done((bf16[4,3,24,768]{3,2,1,0:T(8,128)(2,1)S(1)}, bf16[4,3,24,768]{3,2,1,0:T(8,128)(2,1)S(1)}, u32[]{:S(2)}, u32[]{:S(2)}) %collective-permute-start.6) | collective-permute-done | bytes 442400 | tf_op jit(solution)/shard_map/ppermute | solution.py:602
  32.6 1.6 collective-permute-start.7
  35.1 1.5 collective-permute-start.5
  36.6 12.8 %collective-permute-done.5.refs_3_ = bf16[2,4,2,24,768]{4,3,2,1,0:T(8,128)(2,1)} collective-permute-done((bf16[2,4,2,24,768]{4,3,2,1,0:T(8,128)(2,1)}, bf16[2,4,2,24,768]{4,3,2,1,0:T(8,128)(2,1)}, u32[]{:S(2)}, u32[]{:S(2)}) %collective-permute-start.5) | collective-permute-done | bytes 589856 | tf_op jit(solution)/shard_map/ppermute | solution.py:602
  49.4 3.9 collective-permute-done.7.refs_7_
  53.5 1.6 collective-permute-start.12
  55.0 1.5 collective-permute-start.11
  57.1 9.8 %collective-permute-done.12 = bf16[4,4,24,768]{3,2,1,0:T(8,128)(2,1)S(1)} collective-permute-done((bf16[4,4,24,768]{3,2,1,0:T(8,128)(2,1)S(1)}, bf16[4,4,24,768]{3,2,1,0:T(8,128)(2,1)S(1)}, u32[]{:S(2)}, u32[]{:S(2)}) %collective-permute-start.12) | collective-permute-done | bytes 589856 | tf_op jit(solution)/shard_map/ppermute | solution.py:602
  68.1 1.5 collective-permute-start.15
  71.5 6.2 %place.2 = bf16[5,2,2,4,2,24,768]{6,5,4,3,2,1,0:T(8,128)(2,1)} custom-call(s32[4]{0:T(128)} %pad_add_fusion.refs_0_, bf16[2,4,2,24,768]{4,3,2,1,0:T(8,128)(2,1)} %pad_maximum_fusion.4.refs_1_, bf16[2,4,2,24,768]{4,3,2,1,0:T(8,128)(2,1)} %collective-permute-done.4.refs_2_, bf16[2,4,2,24,768]{4,3,2,1,0:T(8,128)(2,1)} %collective-permute-done.5.refs_3_, ...), custom_call_target="tpu_custom_call" | custom-call | flops 1200000000 | bytes 600000 | tf_op jit(solution)/shard_map/place/pallas_call | solution.py:715
  77.8 2.1 convert_reduce_fusion.vec_ref.refs_2_
  79.8 7.7 %qkv.2.refs_1_.refs_2_.refs_3_ = bf16[1024,2304]{1,0:T(8,128)(2,1)} custom-call(bf16[1024,768]{1,0:T(8,128)(2,1)} %c_ref.3, bf16[5,768,768]{2,1,0:T(8,128)(2,1)} %bitcast.134, f32[24,768]{1,0:T(8,128)} %convert_reduce_fusion.vec_ref.refs_2_), custom_call_target="tpu_custom_call" | custom-call | flops 1600000000 | bytes 800000 | tf_op jit(solution)/shard_map/qkv/pallas_call | solution.py:66
  87.5 12.9 %attend.2 = (bf16[1024,768]{1,0:T(8,128)(2,1)}, f32[2,6,2,512]{3,2,1,0:T(2,128)}) custom-call(s32[2]{0:T(128)} %refs_0_.13, bf16[1024,2304]{1,0:T(8,128)(2,1)} %qkv.2.refs_1_.refs_2_.refs_3_, bf16[1024,2304]{1,0:T(8,128)(2,1)} %qkv.2.refs_1_.refs_2_.refs_3_, bf16[1024,2304]{1,0:T(8,128)(2,1)} %qkv.2.refs_1_.refs_2_.refs_3_), custom_call_target="tpu_custom_call" | custom-call | flops 2600000000 | bytes 1300000 | tf_op jit(solution)/shard_map/attend/pallas_call | solution.py:124
  101.1 2.5 collective-permute-done.16.refs_4_
  103.6 1.7 collective-permute-done.18.refs_8_
  106.4 8.2 %place.3 = (bf16[4,2,2,4,2,24,768]{6,5,4,3,2,1,0:T(8,128)(2,1)}, bf16[2,2,4,2,4,24,768]{6,5,4,3,2,1,0:T(8,128)(2,1)}) custom-call(s32[4]{0:T(128)} %pad_add_fusion.refs_0_, bf16[2,4,4,24,768]{4,3,2,1,0:T(8,128)(2,1)} %copy-done.1, bf16[2,4,4,24,768]{4,3,2,1,0:T(8,128)(2,1)} %copy-done.6, bf16[2,4,4,24,768]{4,3,2,1,0:T(8,128)(2,1)} %collective-permute-done.14.refs_3_, ...), custom_call_target="tpu_custom_call" | custom-call | flops 1200000000 | bytes 600000 | tf_op jit(solution)/shard_map/place/pallas_call | solution.py:715
  114.6 22.3 %ffn.2 = (f32[1024,768]{1,0:T(8,128)}, bf16[1024,768]{1,0:T(8,128)(2,1)}, bf16[1024,3072]{1,0:T(8,128)(2,1)}, bf16[1024,3072]{1,0:T(8,128)(2,1)}, f32[1024,768]{1,0:T(8,128)}, /*index=5*/bf16[1024,768]{1,0:T(8,128)(2,1)}) custom-call(bf16[1024,768]{1,0:T(8,128)(2,1)} %c_ref.3, bf16[1024,768]{1,0:T(8,128)(2,1)} %get-tuple-element.98.refs_1_.rest_1_, ...), custom_call_target="tpu_custom_call" | custom-call | flops 4400000000 | bytes 2200000 | tf_op jit(solution)/shard_map/ffn/pallas_call | solution.py:224
  136.9 7.6 %qkv.3.refs_1_.refs_2_.refs_3_ = bf16[1024,2304]{1,0:T(8,128)(2,1)} custom-call(bf16[1024,768]{1,0:T(8,128)(2,1)} %get-tuple-element.147.x_ref.a_ref, bf16[5,768,768]{2,1,0:T(8,128)(2,1)} %bitcast.136, f32[24,768]{1,0:T(8,128)} %convert_reduce_fusion.vec_ref.refs_2_), custom_call_target="tpu_custom_call" | custom-call | flops 1600000000 | bytes 800000 | tf_op jit(solution)/shard_map/qkv/pallas_call | solution.py:66
  144.6 13.0 %attend.3 = (bf16[1024,768]{1,0:T(8,128)(2,1)}, f32[2,6,2,512]{3,2,1,0:T(2,128)}) custom-call(s32[2]{0:T(128)} %refs_0_.13, bf16[1024,2304]{1,0:T(8,128)(2,1)} %qkv.3.refs_1_.refs_2_.refs_3_, bf16[1024,2304]{1,0:T(8,128)(2,1)} %qkv.3.refs_1_.refs_2_.refs_3_, bf16[1024,2304]{1,0:T(8,128)(2,1)} %qkv.3.refs_1_.refs_2_.refs_3_), custom_call_target="tpu_custom_call" | custom-call | flops 2600000000 | bytes 1300000 | tf_op jit(solution)/shard_map/attend/pallas_call | solution.py:124
  157.6 22.7 %ffn.3 = (f32[1024,768]{1,0:T(8,128)}, bf16[1024,768]{1,0:T(8,128)(2,1)}, bf16[1024,3072]{1,0:T(8,128)(2,1)}, bf16[1024,3072]{1,0:T(8,128)(2,1)}, f32[1024,768]{1,0:T(8,128)}, /*index=5*/bf16[1024,768]{1,0:T(8,128)(2,1)}) custom-call(f32[1024,768]{1,0:T(8,128)} %get-tuple-element.103.refs_0_.z2_ref, bf16[1024,768]{1,0:T(8,128)(2,1)} %get-tuple-element.105.refs_1_.rest_0_, ...), custom_call_target="tpu_custom_call" | custom-call | flops 4400000000 | bytes 2200000 | tf_op jit(solution)/shard_map/ffn/pallas_call | solution.py:224
  180.2 23.4 %ffn_back.2 = (bf16[1024,768]{1,0:T(8,128)(2,1)}, bf16[1024,3072]{1,0:T(8,128)(2,1)}, f32[1024,768]{1,0:T(8,128)}, bf16[1024,768]{1,0:T(8,128)(2,1)}, bf16[1024,768]{1,0:T(8,128)(2,1)}, /*index=5*/f32[24,768]{1,0:T(8,128)}) custom-call(bf16[1024,768]{1,0:T(8,128)(2,1)} %dy_ref.1, f32[1024,768]{1,0:T(8,128)} %get-tuple-element.107.z2_ref, ...), custom_call_target="tpu_custom_call" | custom-call | flops 4800000000 | bytes 2400000 | tf_op jit(solution)/shard_map/ffn_back/pallas_call | solution.py:306
  203.6 12.7 %attend_back.5 = (bf16[3,1024,384]{2,1,0:T(8,128)(2,1)}, f32[2,1,384]{2,1,0:T(1,128)}, f32[2,1,384]{2,1,0:T(1,128)}) custom-call(s32[2]{0:T(128)} %refs_0_.13, bf16[1024,2304]{1,0:T(8,128)(2,1)} %qkv.3.refs_1_.refs_2_.refs_3_, bf16[1024,2304]{1,0:T(8,128)(2,1)} %qkv.3.refs_1_.refs_2_.refs_3_, bf16[1024,2304]{1,0:T(8,128)(2,1)} %qkv.3.refs_1_.refs_2_.refs_3_, ...), custom_call_target="tpu_custom_call" | custom-call | flops 2400000000 | bytes 1200000 | tf_op jit(solution)/shard_map/attend_back/pallas_call | solution.py:382
  216.3 12.3 %attend_back.4 = (bf16[3,1024,384]{2,1,0:T(8,128)(2,1)}, f32[2,1,384]{2,1,0:T(1,128)}, f32[2,1,384]{2,1,0:T(1,128)}) custom-call(s32[2]{0:T(128)} %refs_0_.13, bf16[1024,2304]{1,0:T(8,128)(2,1)} %qkv.3.refs_1_.refs_2_.refs_3_, bf16[1024,2304]{1,0:T(8,128)(2,1)} %qkv.3.refs_1_.refs_2_.refs_3_, bf16[1024,2304]{1,0:T(8,128)(2,1)} %qkv.3.refs_1_.refs_2_.refs_3_, ...), custom_call_target="tpu_custom_call" | custom-call | flops 2400000000 | bytes 1200000 | tf_op jit(solution)/shard_map/attend_back/pallas_call | solution.py:382
  228.6 9.6 %dx.2.dy_ref = f32[1024,768]{1,0:T(8,128)} custom-call(f32[1024,768]{1,0:T(8,128)} %get-tuple-element.110.dz1_ref, bf16[3,1024,384]{2,1,0:T(8,128)(2,1)} %get-tuple-element.113.e0_ref.b_ref, bf16[3,1024,384]{2,1,0:T(8,128)(2,1)} %get-tuple-element.114.e1_ref.b_ref, bf16[5,768,768]{2,1,0:T(8,128)(2,1)} %bitcast.139), custom_call_target="tpu_custom_call" | custom-call | flops 1800000000 | bytes 900000 | tf_op jit(solution)/shard_map/dx/pallas_call | solution.py:415
  238.2 23.9 %ffn_back.3 = (bf16[1024,768]{1,0:T(8,128)(2,1)}, bf16[1024,3072]{1,0:T(8,128)(2,1)}, f32[1024,768]{1,0:T(8,128)}, bf16[1024,768]{1,0:T(8,128)(2,1)}, bf16[1024,768]{1,0:T(8,128)(2,1)}, /*index=5*/f32[24,768]{1,0:T(8,128)}) custom-call(f32[1024,768]{1,0:T(8,128)} %dx.2.dy_ref, f32[1024,768]{1,0:T(8,128)} %get-tuple-element.103.refs_0_.z2_ref, ...), custom_call_target="tpu_custom_call" | custom-call | flops 4800000000 | bytes 2400000 | tf_op jit(solution)/shard_map/ffn_back/pallas_call | solution.py:306
  262.1 15.0 %wgrad_back.1 = (bf16[2,2,4,4,24,768]{5,4,3,2,1,0:T(8,128)(2,1)}, bf16[2,2,4,4,24,768]{5,4,3,2,1,0:T(8,128)(2,1)}) custom-call(s32[1]{0:T(128)} %bitcast.1.core_ref, bf16[1024,3072]{1,0:T(8,128)(2,1)} %get-tuple-element.118.g2k.g2s, bf16[1024,3072]{1,0:T(8,128)(2,1)} %get-tuple-element.119.g1k.g1s, bf16[1024,3072]{1,0:T(8,128)(2,1)} %get-tuple-element.118.g2k.g2s, ...), custom_call_target="tpu_custom_call" | custom-call | flops 3000000000 | bytes 1500000 | tf_op jit(solution)/shard_map/wgrad_back/pallas_call | solution.py:556
  277.0 15.1 %wgrad_in.1 = (bf16[2,2,4,4,24,768]{5,4,3,2,1,0:T(8,128)(2,1)}, bf16[2,2,4,4,24,768]{5,4,3,2,1,0:T(8,128)(2,1)}) custom-call(s32[1]{0:T(128)} %bitcast.1.core_ref, bf16[1024,768]{1,0:T(8,128)(2,1)} %get-tuple-element.124.a_ref, bf16[1024,768]{1,0:T(8,128)(2,1)} %get-tuple-element.125.c_ref, bf16[1024,3072]{1,0:T(8,128)(2,1)} %get-tuple-element.126.b_ref, ...), custom_call_target="tpu_custom_call" | custom-call | flops 3000000000 | bytes 1500000 | tf_op jit(solution)/shard_map/wgrad_in/pallas_call | solution.py:456
  292.6 4.4 %collective-permute-done.20 = bf16[2,2,4,4,24,768]{5,4,3,2,1,0:T(8,128)(2,1)} collective-permute-done((bf16[2,2,4,4,24,768]{5,4,3,2,1,0:T(8,128)(2,1)}, bf16[2,2,4,4,24,768]{5,4,3,2,1,0:T(8,128)(2,1)}, u32[]{:S(2)}, u32[]{:S(2)}) %collective-permute-start.20) | collective-permute-done | bytes 2359328 | tf_op jit(solution)/shard_map/ppermute | solution.py:602
  297.0 4.2 fusion.3
  301.2 1.5 collective-permute-start.22
  302.7 2.3 fusion
  305.6 12.5 %attend_back.6 = (bf16[3,1024,384]{2,1,0:T(8,128)(2,1)}, f32[2,1,384]{2,1,0:T(1,128)}, f32[2,1,384]{2,1,0:T(1,128)}) custom-call(s32[2]{0:T(128)} %refs_0_.13, bf16[1024,2304]{1,0:T(8,128)(2,1)} %qkv.2.refs_1_.refs_2_.refs_3_, bf16[1024,2304]{1,0:T(8,128)(2,1)} %qkv.2.refs_1_.refs_2_.refs_3_, bf16[1024,2304]{1,0:T(8,128)(2,1)} %qkv.2.refs_1_.refs_2_.refs_3_, ...), custom_call_target="tpu_custom_call" | custom-call | flops 2400000000 | bytes 1200000 | tf_op jit(solution)/shard_map/attend_back/pallas_call | solution.py:382
  318.1 12.3 %attend_back.7 = (bf16[3,1024,384]{2,1,0:T(8,128)(2,1)}, f32[2,1,384]{2,1,0:T(1,128)}, f32[2,1,384]{2,1,0:T(1,128)}) custom-call(s32[2]{0:T(128)} %refs_0_.13, bf16[1024,2304]{1,0:T(8,128)(2,1)} %qkv.2.refs_1_.refs_2_.refs_3_, bf16[1024,2304]{1,0:T(8,128)(2,1)} %qkv.2.refs_1_.refs_2_.refs_3_, bf16[1024,2304]{1,0:T(8,128)(2,1)} %qkv.2.refs_1_.refs_2_.refs_3_, ...), custom_call_target="tpu_custom_call" | custom-call | flops 2400000000 | bytes 1200000 | tf_op jit(solution)/shard_map/attend_back/pallas_call | solution.py:382
  330.5 1.5 fusion.9
  332.0 1.6 collective-permute-start.27
  334.5 14.8 %wgrad_heads.2 = (bf16[2,2,4,5,24,384]{5,4,3,2,1,0:T(8,128)(2,1)}, bf16[2,2,4,5,24,384]{5,4,3,2,1,0:T(8,128)(2,1)}) custom-call(s32[1]{0:T(128)} %bitcast.1.core_ref, bf16[1024,768]{1,0:T(8,128)(2,1)} %get-tuple-element.147.x_ref.a_ref, bf16[1024,768]{1,0:T(8,128)(2,1)} %c_ref.3, bf16[3,1024,384]{2,1,0:T(8,128)(2,1)} %get-tuple-element.113.e0_ref.b_ref, ...), custom_call_target="tpu_custom_call" | custom-call | flops 2400000000 | bytes 1200000 | tf_op jit(solution)/shard_map/wgrad_heads/pallas_call | solution.py:520
  349.6 9.4 %wgrad_heads.3 = (bf16[2,2,4,4,24,384]{5,4,3,2,1,0:T(8,128)(2,1)}, bf16[2,2,4,4,24,384]{5,4,3,2,1,0:T(8,128)(2,1)}) custom-call(s32[1]{0:T(128)} %bitcast.1.core_ref, bf16[1024,768]{1,0:T(8,128)(2,1)} %get-tuple-element.147.x_ref.a_ref, bf16[1024,768]{1,0:T(8,128)(2,1)} %c_ref.3, bf16[3,1024,384]{2,1,0:T(8,128)(2,1)} %get-tuple-element.114.e1_ref.b_ref, ...), custom_call_target="tpu_custom_call" | custom-call | flops 2400000000 | bytes 1200000 | tf_op jit(solution)/shard_map/wgrad_heads/pallas_call | solution.py:520
  359.5 1.7 fusion.5
  361.9 10.9 %collective-permute-start.24 = (bf16[4,24,768]{2,1,0:T(8,128)(2,1)S(1)}, bf16[4,24,768]{2,1,0:T(8,128)(2,1)S(1)}, u32[]{:S(2)}, u32[]{:S(2)}) collective-permute-start(bf16[4,24,768]{2,1,0:T(8,128)(2,1)S(1)} %get-tuple-element.186), channel_id=1, source_target_pairs={{0,2},{1,3},{2,4},{3,5},{4,6},{5,7},{6,0},{7,1},{8,10},{9,11},{10,... | collective-permute-start | bytes 442376 | tf_op jit(solution)/shard_map/ppermute | solution.py:602
  372.8 2.4 collective-permute-start.26
  375.4 1.5 fusion.11
  377.1 2.6 collective-permute-start.41
  379.7 3.5 collective-permute-done.25
  383.2 6.8 %collective-permute-start.42 = (bf16[4,24,768]{2,1,0:T(8,128)(2,1)S(1)}, bf16[4,24,768]{2,1,0:T(8,128)(2,1)S(1)}, u32[]{:S(2)}, u32[]{:S(2)}) collective-permute-start(bf16[4,24,768]{2,1,0:T(8,128)(2,1)S(1)} %get-tuple-element.184), channel_id=1, source_target_pairs={{0,6},{1,7},{2,0},{3,1},{4,2},{5,3},{6,4},{7,5},{8,14},{9,15},{10,... | collective-permute-start | bytes 442376 | tf_op jit(solution)/shard_map/ppermute | solution.py:602
  390.0 1.5 collective-permute-start.35
  392.3 9.2 %dx.3 = bf16[1024,768]{1,0:T(8,128)(2,1)} custom-call(f32[1024,768]{1,0:T(8,128)} %get-tuple-element.162.dz1_ref, bf16[3,1024,384]{2,1,0:T(8,128)(2,1)} %get-tuple-element.136.d_ref.e0_ref, bf16[3,1024,384]{2,1,0:T(8,128)(2,1)} %get-tuple-element.138.d_ref.e1_ref, bf16[5,768,768]{2,1,0:T(8,128)(2,1)} %bitcast.141), custom_call_target="tpu_custom_call" | custom-call | flops 1800000000 | bytes 900000 | tf_op jit(solution)/shard_map/dx/pallas_call | solution.py:415
  404.0 1.5 collective-permute-start.36
  405.5 5.1 %collective-permute-done.31 = bf16[4,5,24,384]{3,2,1,0:T(8,128)(2,1)S(1)} collective-permute-done((bf16[4,5,24,384]{3,2,1,0:T(8,128)(2,1)S(1)}, bf16[4,5,24,384]{3,2,1,0:T(8,128)(2,1)S(1)}, u32[]{:S(2)}, u32[]{:S(2)}) %collective-permute-start.31) | collective-permute-done | bytes 368672 | tf_op jit(solution)/shard_map/ppermute | solution.py:602
  410.8 4.6 %collective-permute-start.32 = (bf16[5,24,384]{2,1,0:T(8,128)(2,1)S(1)}, bf16[5,24,384]{2,1,0:T(8,128)(2,1)S(1)}, u32[]{:S(2)}, u32[]{:S(2)}) collective-permute-start(bf16[5,24,384]{2,1,0:T(8,128)(2,1)S(1)} %get-tuple-element.189), channel_id=1, source_target_pairs={{0,2},{1,3},{2,4},{3,5},{4,6},{5,7},{6,0},{7,1},{8,10},{9,11},{10,... | collective-permute-start | bytes 276488 | tf_op jit(solution)/shard_map/ppermute | solution.py:602
  415.4 2.4 collective-permute-start.34
  418.0 2.5 collective-permute-start.38
  420.5 1.3 collective-permute-start.39
  421.8 3.1 collective-permute-done.33
  425.7 3.2 collective-permute-done.38
  (111 shorter events, 16.7 us)
Async XLA Ops:
  2.4 14.4 %collective-permute-start = (bf16[5,24,768]{2,1,0:T(8,128)(2,1)}, bf16[5,24,768]{2,1,0:T(8,128)(2,1)S(1)}, u32[]{:S(2)}, u32[]{:S(2)}) collective-permute-start(bf16[5,24,768]{2,1,0:T(8,128)(2,1)} %pack_one.1), channel_id=1, source_target_pairs={{0,2},{1,3},{2,4},{3,5},{4,6},{5,7},{6,0},{7,1},{8,10},{9,11},{10,... | collective-permute-start | bytes 552968 | tf_op jit(solution)/shard_map/ppermute | solution.py:602
  5.4 14.9 %collective-permute-start.1 = (bf16[5,24,768]{2,1,0:T(8,128)(2,1)}, bf16[5,24,768]{2,1,0:T(8,128)(2,1)S(1)}, u32[]{:S(2)}, u32[]{:S(2)}) collective-permute-start(bf16[5,24,768]{2,1,0:T(8,128)(2,1)} %pack_one.1), channel_id=1, source_target_pairs={{0,4},{1,5},{2,6},{3,7},{4,0},{5,1},{6,2},{7,3},{8,12},{9,13},{10,... | collective-permute-start | bytes 552968 | tf_op jit(solution)/shard_map/ppermute | solution.py:602
  8.0 12.3 %collective-permute-start.2 = (bf16[5,24,768]{2,1,0:T(8,128)(2,1)}, bf16[5,24,768]{2,1,0:T(8,128)(2,1)S(1)}, u32[]{:S(2)}, u32[]{:S(2)}) collective-permute-start(bf16[5,24,768]{2,1,0:T(8,128)(2,1)} %pack_one.1), channel_id=1, source_target_pairs={{0,6},{1,7},{2,0},{3,1},{4,2},{5,3},{6,4},{7,5},{8,14},{9,15},{10,... | collective-permute-start | bytes 552968 | tf_op jit(solution)/shard_map/ppermute | solution.py:602
  13.1 7.2 %copy-start.10 = (bf16[5,24,768]{2,1,0:T(8,128)(2,1)S(1)}, bf16[5,24,768]{2,1,0:T(8,128)(2,1)}, u32[]{:S(2)}) copy-start(bf16[5,24,768]{2,1,0:T(8,128)(2,1)} %pack_one.1) | copy-start | bytes 552964
  13.2 40.2 %all-to-all-start = ((bf16[4,8,24,768]{3,2,1,0:T(8,128)(2,1)}), bf16[4,8,24,768]{3,2,1,0:T(8,128)(2,1)S(1)}, u32[]{:S(2)}, u32[]{:S(2)}) async-start(bf16[4,8,24,768]{3,2,1,0:T(8,128)(2,1)} %broadcast_in_dim.44), calls=%async_computation | async-start | bytes 2359296 | tf_op jit(solution)/shard_map/all_to_all | solution.py:606
  20.5 12.1 %collective-permute-start.6 = (bf16[4,3,24,768]{3,2,1,0:T(8,128)(2,1)S(1)}, bf16[4,3,24,768]{3,2,1,0:T(8,128)(2,1)S(1)}, u32[]{:S(2)}, u32[]{:S(2)}) collective-permute-start(bf16[4,3,24,768]{3,2,1,0:T(8,128)(2,1)S(1)} %slice.86), channel_id=1, source_target_pairs={{0,16},{1,17},{2,18},{3,19},{4,20},{5,21},{6,22},{7,23},{8,24},{9,... | collective-permute-start | bytes 1327112 | tf_op jit(solution)/shard_map/ppermute | solution.py:602
  22.1 12.2 %collective-permute-start.3 = (bf16[4,2,24,768]{3,2,1,0:T(8,128)(2,1)S(1)}, bf16[4,2,24,768]{3,2,1,0:T(8,128)(2,1)S(1)}, u32[]{:S(2)}, u32[]{:S(2)}) collective-permute-start(bf16[4,2,24,768]{3,2,1,0:T(8,128)(2,1)S(1)} %slice.85), channel_id=1, source_target_pairs={{0,1},{1,0},{2,3},{3,2},{4,5},{5,4},{6,7},{7,6},{8,9},{9,8},{10,11... | collective-permute-start | bytes 884744 | tf_op jit(solution)/shard_map/ppermute | solution.py:602
  32.6 24.0 %copy-start.2 = (bf16[2,4,3,24,768]{4,3,2,1,0:T(8,128)(2,1)}, bf16[2,4,3,24,768]{4,3,2,1,0:T(8,128)(2,1)S(1)}, u32[]{:S(2)}) copy-start(bf16[2,4,3,24,768]{4,3,2,1,0:T(8,128)(2,1)S(1)} %pad_maximum_fusion.2.refs_5_) | copy-start | bytes 2654212
  32.6 20.8 %collective-permute-start.7 = (bf16[2,4,3,24,768]{4,3,2,1,0:T(8,128)(2,1)S(1)}, bf16[2,4,3,24,768]{4,3,2,1,0:T(8,128)(2,1)}, u32[]{:S(2)}, u32[]{:S(2)}) collective-permute-start(bf16[2,4,3,24,768]{4,3,2,1,0:T(8,128)(2,1)S(1)} %pad_maximum_fusion.2.refs_5_), channel_id=1, source_target_pairs={{0,1},{1,0},{2,3},{3,2},{4,5},{5,4},{6,7},{7,6},{8,9},{9,8},{10,11... | collective-permute-start | bytes 2654216 | tf_op jit(solution)/shard_map/ppermute | solution.py:602
  35.1 14.3 %collective-permute-start.5 = (bf16[2,4,2,24,768]{4,3,2,1,0:T(8,128)(2,1)}, bf16[2,4,2,24,768]{4,3,2,1,0:T(8,128)(2,1)}, u32[]{:S(2)}, u32[]{:S(2)}) collective-permute-start(bf16[2,4,2,24,768]{4,3,2,1,0:T(8,128)(2,1)} %pad_maximum_fusion.4.refs_1_), channel_id=1, source_target_pairs={{0,16},{1,17},{2,18},{3,19},{4,20},{5,21},{6,22},{7,23},{8,24},{9,... | collective-permute-start | bytes 1769480 | tf_op jit(solution)/shard_map/ppermute | solution.py:602
  53.5 13.4 %collective-permute-start.12 = (bf16[4,4,24,768]{3,2,1,0:T(8,128)(2,1)S(1)}, bf16[4,4,24,768]{3,2,1,0:T(8,128)(2,1)S(1)}, u32[]{:S(2)}, u32[]{:S(2)}) collective-permute-start(bf16[4,4,24,768]{3,2,1,0:T(8,128)(2,1)S(1)} %get-tuple-element.96), channel_id=1, source_target_pairs={{0,16},{1,17},{2,18},{3,19},{4,20},{5,21},{6,22},{7,23},{8,24},{9,... | collective-permute-start | bytes 1769480 | tf_op jit(solution)/shard_map/ppermute | solution.py:602
  55.0 13.1 %collective-permute-start.11 = (bf16[4,4,24,768]{3,2,1,0:T(8,128)(2,1)S(1)}, bf16[4,4,24,768]{3,2,1,0:T(8,128)(2,1)S(1)}, u32[]{:S(2)}, u32[]{:S(2)}) collective-permute-start(bf16[4,4,24,768]{3,2,1,0:T(8,128)(2,1)S(1)} %get-tuple-element.95), channel_id=1, source_target_pairs={{0,1},{1,0},{2,3},{3,2},{4,5},{5,4},{6,7},{7,6},{8,9},{9,8},{10,11... | collective-permute-start | bytes 1769480 | tf_op jit(solution)/shard_map/ppermute | solution.py:602
  56.6 13.2 %collective-permute-start.4 = (bf16[2,4,2,24,768]{4,3,2,1,0:T(8,128)(2,1)}, bf16[2,4,2,24,768]{4,3,2,1,0:T(8,128)(2,1)}, u32[]{:S(2)}, u32[]{:S(2)}) collective-permute-start(bf16[2,4,2,24,768]{4,3,2,1,0:T(8,128)(2,1)} %pad_maximum_fusion.4.refs_1_), channel_id=1, source_target_pairs={{0,8},{1,9},{2,10},{3,11},{4,12},{5,13},{6,14},{7,15},{8,0},{9,1},... | collective-permute-start | bytes 1769480 | tf_op jit(solution)/shard_map/ppermute | solution.py:602
  56.6 14.4 %collective-permute-start.9 = (bf16[2,4,3,24,768]{4,3,2,1,0:T(8,128)(2,1)S(1)}, bf16[2,4,3,24,768]{4,3,2,1,0:T(8,128)(2,1)}, u32[]{:S(2)}, u32[]{:S(2)}) collective-permute-start(bf16[2,4,3,24,768]{4,3,2,1,0:T(8,128)(2,1)S(1)} %pad_maximum_fusion.2.refs_5_), channel_id=1, source_target_pairs={{0,8},{1,9},{2,10},{3,11},{4,12},{5,13},{6,14},{7,15},{8,0},{9,1},... | collective-permute-start | bytes 2654216 | tf_op jit(solution)/shard_map/ppermute | solution.py:602
  57.1 14.4 %collective-permute-start.10 = (bf16[2,4,3,24,768]{4,3,2,1,0:T(8,128)(2,1)}, bf16[2,4,3,24,768]{4,3,2,1,0:T(8,128)(2,1)}, u32[]{:S(2)}, u32[]{:S(2)}) collective-permute-start(bf16[2,4,3,24,768]{4,3,2,1,0:T(8,128)(2,1)} %collective-permute-done.7.refs_7_), channel_id=1, source_target_pairs={{0,8},{1,9},{2,10},{3,11},{4,12},{5,13},{6,14},{7,15},{8,0},{9,1},... | collective-permute-start | bytes 2654216 | tf_op jit(solution)/shard_map/ppermute | solution.py:602
  66.9 4.1 collective-permute-start.8
  67.0 10.7 %copy-start = (bf16[2,4,4,24,768]{4,3,2,1,0:T(8,128)(2,1)}, bf16[2,4,4,24,768]{4,3,2,1,0:T(8,128)(2,1)S(1)}, u32[]{:S(2)}) copy-start(bf16[2,4,4,24,768]{4,3,2,1,0:T(8,128)(2,1)S(1)} %pad_maximum_fusion.1.refs_5_) | copy-start | bytes 3538948
  68.1 32.3 %collective-permute-start.15 = (bf16[2,4,4,24,768]{4,3,2,1,0:T(8,128)(2,1)S(1)}, bf16[2,4,4,24,768]{4,3,2,1,0:T(8,128)(2,1)}, u32[]{:S(2)}, u32[]{:S(2)}) collective-permute-start(bf16[2,4,4,24,768]{4,3,2,1,0:T(8,128)(2,1)S(1)} %pad_maximum_fusion.1.refs_5_), channel_id=1, source_target_pairs={{0,1},{1,0},{2,3},{3,2},{4,5},{5,4},{6,7},{7,6},{8,9},{9,8},{10,11... | collective-permute-start | bytes 3538952 | tf_op jit(solution)/shard_map/ppermute | solution.py:602
  69.8 8.0 %copy-start.1 = (bf16[2,4,4,24,768]{4,3,2,1,0:T(8,128)(2,1)}, bf16[2,4,4,24,768]{4,3,2,1,0:T(8,128)(2,1)S(1)}, u32[]{:S(2)}) copy-start(bf16[2,4,4,24,768]{4,3,2,1,0:T(8,128)(2,1)S(1)} %pad_maximum_fusion.refs_1_) | copy-start | bytes 3538948
  69.8 30.7 %collective-permute-start.14 = (bf16[2,4,4,24,768]{4,3,2,1,0:T(8,128)(2,1)S(1)}, bf16[2,4,4,24,768]{4,3,2,1,0:T(8,128)(2,1)}, u32[]{:S(2)}, u32[]{:S(2)}) collective-permute-start(bf16[2,4,4,24,768]{4,3,2,1,0:T(8,128)(2,1)S(1)} %pad_maximum_fusion.refs_1_), channel_id=1, source_target_pairs={{0,16},{1,17},{2,18},{3,19},{4,20},{5,21},{6,22},{7,23},{8,24},{9,... | collective-permute-start | bytes 3538952 | tf_op jit(solution)/shard_map/ppermute | solution.py:602
  71.0 30.1 %collective-permute-start.17 = (bf16[2,4,4,24,768]{4,3,2,1,0:T(8,128)(2,1)S(1)}, bf16[2,4,4,24,768]{4,3,2,1,0:T(8,128)(2,1)S(1)}, u32[]{:S(2)}, u32[]{:S(2)}) collective-permute-start(bf16[2,4,4,24,768]{4,3,2,1,0:T(8,128)(2,1)S(1)} %pad_maximum_fusion.1.refs_5_), channel_id=1, source_target_pairs={{0,8},{1,9},{2,10},{3,11},{4,12},{5,13},{6,14},{7,15},{8,0},{9,1},... | collective-permute-start | bytes 3538952 | tf_op jit(solution)/shard_map/ppermute | solution.py:602
  71.0 30.1 %collective-permute-start.13 = (bf16[2,4,4,24,768]{4,3,2,1,0:T(8,128)(2,1)S(1)}, bf16[2,4,4,24,768]{4,3,2,1,0:T(8,128)(2,1)S(1)}, u32[]{:S(2)}, u32[]{:S(2)}) collective-permute-start(bf16[2,4,4,24,768]{4,3,2,1,0:T(8,128)(2,1)S(1)} %pad_maximum_fusion.refs_1_), channel_id=1, source_target_pairs={{0,8},{1,9},{2,10},{3,11},{4,12},{5,13},{6,14},{7,15},{8,0},{9,1},... | collective-permute-start | bytes 3538952 | tf_op jit(solution)/shard_map/ppermute | solution.py:602
  100.5 3.1 collective-permute-start.16
  100.6 4.7 %collective-permute-start.18 = (bf16[2,4,4,24,768]{4,3,2,1,0:T(8,128)(2,1)}, bf16[2,4,4,24,768]{4,3,2,1,0:T(8,128)(2,1)S(1)}, u32[]{:S(2)}, u32[]{:S(2)}) collective-permute-start(bf16[2,4,4,24,768]{4,3,2,1,0:T(8,128)(2,1)} %collective-permute-done.15.refs_7_), channel_id=1, source_target_pairs={{0,8},{1,9},{2,10},{3,11},{4,12},{5,13},{6,14},{7,15},{8,0},{9,1},... | collective-permute-start | bytes 3538952 | tf_op jit(solution)/shard_map/ppermute | solution.py:602
  101.0 4.2 copy-start.5
  101.1 4.2 copy-start.6
  103.6 1.7 copy-start.7
  105.3 1.1 copy-start.8
  292.1 4.9 %collective-permute-start.20 = (bf16[2,2,4,4,24,768]{5,4,3,2,1,0:T(8,128)(2,1)}, bf16[2,2,4,4,24,768]{5,4,3,2,1,0:T(8,128)(2,1)}, u32[]{:S(2)}, u32[]{:S(2)}) collective-permute-start(bf16[2,2,4,4,24,768]{5,4,3,2,1,0:T(8,128)(2,1)} %get-tuple-element.133), channel_id=1, source_target_pairs={{0,8},{1,9},{2,10},{3,11},{4,12},{5,13},{6,14},{7,15},{8,0},{9,1},... | collective-permute-start | bytes 7077896 | tf_op jit(solution)/shard_map/ppermute | solution.py:602
  292.2 10.5 %collective-permute-start.19 = (bf16[2,2,4,4,24,768]{5,4,3,2,1,0:T(8,128)(2,1)}, bf16[2,2,4,4,24,768]{5,4,3,2,1,0:T(8,128)(2,1)}, u32[]{:S(2)}, u32[]{:S(2)}) collective-permute-start(bf16[2,2,4,4,24,768]{5,4,3,2,1,0:T(8,128)(2,1)} %get-tuple-element.130), channel_id=1, source_target_pairs={{0,8},{1,9},{2,10},{3,11},{4,12},{5,13},{6,14},{7,15},{8,0},{9,1},... | collective-permute-start | bytes 7077896 | tf_op jit(solution)/shard_map/ppermute | solution.py:602
  297.0 5.7 %copy-start.3 = (bf16[2,2,4,4,24,768]{5,4,3,2,1,0:T(8,128)(2,1)S(1)}, bf16[2,2,4,4,24,768]{5,4,3,2,1,0:T(8,128)(2,1)}, u32[]{:S(2)}) copy-start(bf16[2,2,4,4,24,768]{5,4,3,2,1,0:T(8,128)(2,1)} %get-tuple-element.129) | copy-start | bytes 7077892
  301.2 29.2 %collective-permute-start.22 = (bf16[2,4,4,24,768]{4,3,2,1,0:T(8,128)(2,1)}, bf16[2,4,4,24,768]{4,3,2,1,0:T(8,128)(2,1)}, u32[]{:S(2)}, u32[]{:S(2)}) collective-permute-start(bf16[2,4,4,24,768]{4,3,2,1,0:T(8,128)(2,1)} %get-tuple-element.166), channel_id=1, source_target_pairs={{0,16},{1,17},{2,18},{3,19},{4,20},{5,21},{6,22},{7,23},{8,24},{9,... | collective-permute-start | bytes 3538952 | tf_op jit(solution)/shard_map/ppermute | solution.py:602
  305.1 28.5 %collective-permute-start.21 = (bf16[2,4,4,24,768]{4,3,2,1,0:T(8,128)(2,1)S(1)}, bf16[2,4,4,24,768]{4,3,2,1,0:T(8,128)(2,1)S(1)}, u32[]{:S(2)}, u32[]{:S(2)}) collective-permute-start(bf16[2,4,4,24,768]{4,3,2,1,0:T(8,128)(2,1)S(1)} %get-tuple-element.168), channel_id=1, source_target_pairs={{0,1},{1,0},{2,3},{3,2},{4,5},{5,4},{6,7},{7,6},{8,9},{9,8},{10,11... | collective-permute-start | bytes 3538952 | tf_op jit(solution)/shard_map/ppermute | solution.py:602
  332.0 17.3 %collective-permute-start.27 = (bf16[4,4,24,768]{3,2,1,0:T(8,128)(2,1)S(1)}, bf16[4,4,24,768]{3,2,1,0:T(8,128)(2,1)S(1)}, u32[]{:S(2)}, u32[]{:S(2)}) collective-permute-start(bf16[4,4,24,768]{3,2,1,0:T(8,128)(2,1)S(1)} %get-tuple-element.174), channel_id=1, source_target_pairs={{0,1},{1,0},{2,3},{3,2},{4,5},{5,4},{6,7},{7,6},{8,9},{9,8},{10,11... | collective-permute-start | bytes 1769480 | tf_op jit(solution)/shard_map/ppermute | solution.py:602
  333.9 15.6 %collective-permute-start.23 = (bf16[4,4,24,768]{3,2,1,0:T(8,128)(2,1)S(1)}, bf16[4,4,24,768]{3,2,1,0:T(8,128)(2,1)S(1)}, u32[]{:S(2)}, u32[]{:S(2)}) collective-permute-start(bf16[4,4,24,768]{3,2,1,0:T(8,128)(2,1)S(1)} %get-tuple-element.176), channel_id=1, source_target_pairs={{0,16},{1,17},{2,18},{3,19},{4,20},{5,21},{6,22},{7,23},{8,24},{9,... | collective-permute-start | bytes 1769480 | tf_op jit(solution)/shard_map/ppermute | solution.py:602
  349.3 10.3 %collective-permute-start.28 = (bf16[2,2,4,5,24,384]{5,4,3,2,1,0:T(8,128)(2,1)}, bf16[2,2,4,5,24,384]{5,4,3,2,1,0:T(8,128)(2,1)}, u32[]{:S(2)}, u32[]{:S(2)}) collective-permute-start(bf16[2,2,4,5,24,384]{5,4,3,2,1,0:T(8,128)(2,1)} %get-tuple-element.160), channel_id=1, source_target_pairs={{0,8},{1,9},{2,10},{3,11},{4,12},{5,13},{6,14},{7,15},{8,0},{9,1},... | collective-permute-start | bytes 4423688 | tf_op jit(solution)/shard_map/ppermute | solution.py:602
  349.6 9.9 %copy-start.4 = (bf16[2,2,4,5,24,384]{5,4,3,2,1,0:T(8,128)(2,1)S(1)}, bf16[2,2,4,5,24,384]{5,4,3,2,1,0:T(8,128)(2,1)}, u32[]{:S(2)}) copy-start(bf16[2,2,4,5,24,384]{5,4,3,2,1,0:T(8,128)(2,1)} %get-tuple-element.159) | copy-start | bytes 4423684
  359.0 16.3 %collective-permute-start.29 = (bf16[2,2,4,4,24,384]{5,4,3,2,1,0:T(8,128)(2,1)}, bf16[2,2,4,4,24,384]{5,4,3,2,1,0:T(8,128)(2,1)}, u32[]{:S(2)}, u32[]{:S(2)}) collective-permute-start(bf16[2,2,4,4,24,384]{5,4,3,2,1,0:T(8,128)(2,1)} %get-tuple-element.161), channel_id=1, source_target_pairs={{0,8},{1,9},{2,10},{3,11},{4,12},{5,13},{6,14},{7,15},{8,0},{9,1},... | collective-permute-start | bytes 3538952 | tf_op jit(solution)/shard_map/ppermute | solution.py:602
  361.3 14.1 %copy-start.9 = (bf16[2,2,4,4,24,384]{5,4,3,2,1,0:T(8,128)(2,1)S(1)}, bf16[2,2,4,4,24,384]{5,4,3,2,1,0:T(8,128)(2,1)}, u32[]{:S(2)}) copy-start(bf16[2,2,4,4,24,384]{5,4,3,2,1,0:T(8,128)(2,1)} %get-tuple-element.158) | copy-start | bytes 3538948
  361.3 40.3 %collective-permute-start.30 = (bf16[2,4,5,24,384]{4,3,2,1,0:T(8,128)(2,1)S(1)}, bf16[2,4,5,24,384]{4,3,2,1,0:T(8,128)(2,1)S(1)}, u32[]{:S(2)}, u32[]{:S(2)}) collective-permute-start(bf16[2,4,5,24,384]{4,3,2,1,0:T(8,128)(2,1)S(1)} %get-tuple-element.170), channel_id=1, source_target_pairs={{0,1},{1,0},{2,3},{3,2},{4,5},{5,4},{6,7},{7,6},{8,9},{9,8},{10,11... | collective-permute-start | bytes 2211848 | tf_op jit(solution)/shard_map/ppermute | solution.py:602
  361.9 15.2 %collective-permute-start.24 = (bf16[4,24,768]{2,1,0:T(8,128)(2,1)S(1)}, bf16[4,24,768]{2,1,0:T(8,128)(2,1)S(1)}, u32[]{:S(2)}, u32[]{:S(2)}) collective-permute-start(bf16[4,24,768]{2,1,0:T(8,128)(2,1)S(1)} %get-tuple-element.186), channel_id=1, source_target_pairs={{0,2},{1,3},{2,4},{3,5},{4,6},{5,7},{6,0},{7,1},{8,10},{9,11},{10,... | collective-permute-start | bytes 442376 | tf_op jit(solution)/shard_map/ppermute | solution.py:602
  372.8 10.4 %collective-permute-start.25 = (bf16[4,24,768]{2,1,0:T(8,128)(2,1)S(1)}, bf16[4,24,768]{2,1,0:T(8,128)(2,1)S(1)}, u32[]{:S(2)}, u32[]{:S(2)}) collective-permute-start(bf16[4,24,768]{2,1,0:T(8,128)(2,1)S(1)} %get-tuple-element.188), channel_id=1, source_target_pairs={{0,4},{1,5},{2,6},{3,7},{4,0},{5,1},{6,2},{7,3},{8,12},{9,13},{10,... | collective-permute-start | bytes 442376 | tf_op jit(solution)/shard_map/ppermute | solution.py:602
  372.8 17.2 %collective-permute-start.26 = (bf16[4,24,768]{2,1,0:T(8,128)(2,1)S(1)}, bf16[4,24,768]{2,1,0:T(8,128)(2,1)S(1)}, u32[]{:S(2)}, u32[]{:S(2)}) collective-permute-start(bf16[4,24,768]{2,1,0:T(8,128)(2,1)S(1)} %get-tuple-element.187), channel_id=1, source_target_pairs={{0,6},{1,7},{2,0},{3,1},{4,2},{5,3},{6,4},{7,5},{8,14},{9,15},{10,... | collective-permute-start | bytes 442376 | tf_op jit(solution)/shard_map/ppermute | solution.py:602
  375.3 27.1 %collective-permute-start.40 = (bf16[4,24,768]{2,1,0:T(8,128)(2,1)S(1)}, bf16[4,24,768]{2,1,0:T(8,128)(2,1)S(1)}, u32[]{:S(2)}, u32[]{:S(2)}) collective-permute-start(bf16[4,24,768]{2,1,0:T(8,128)(2,1)S(1)} %get-tuple-element.183), channel_id=1, source_target_pairs={{0,2},{1,3},{2,4},{3,5},{4,6},{5,7},{6,0},{7,1},{8,10},{9,11},{10,... | collective-permute-start | bytes 442376 | tf_op jit(solution)/shard_map/ppermute | solution.py:602
  377.1 25.3 %collective-permute-start.41 = (bf16[4,24,768]{2,1,0:T(8,128)(2,1)S(1)}, bf16[4,24,768]{2,1,0:T(8,128)(2,1)S(1)}, u32[]{:S(2)}, u32[]{:S(2)}) collective-permute-start(bf16[4,24,768]{2,1,0:T(8,128)(2,1)S(1)} %get-tuple-element.185), channel_id=1, source_target_pairs={{0,4},{1,5},{2,6},{3,7},{4,0},{5,1},{6,2},{7,3},{8,12},{9,13},{10,... | collective-permute-start | bytes 442376 | tf_op jit(solution)/shard_map/ppermute | solution.py:602
  383.2 19.1 %collective-permute-start.42 = (bf16[4,24,768]{2,1,0:T(8,128)(2,1)S(1)}, bf16[4,24,768]{2,1,0:T(8,128)(2,1)S(1)}, u32[]{:S(2)}, u32[]{:S(2)}) collective-permute-start(bf16[4,24,768]{2,1,0:T(8,128)(2,1)S(1)} %get-tuple-element.184), channel_id=1, source_target_pairs={{0,6},{1,7},{2,0},{3,1},{4,2},{5,3},{6,4},{7,5},{8,14},{9,15},{10,... | collective-permute-start | bytes 442376 | tf_op jit(solution)/shard_map/ppermute | solution.py:602
  390.0 13.8 %collective-permute-start.35 = (bf16[2,4,4,24,384]{4,3,2,1,0:T(8,128)(2,1)S(1)}, bf16[2,4,4,24,384]{4,3,2,1,0:T(8,128)(2,1)S(1)}, u32[]{:S(2)}, u32[]{:S(2)}) collective-permute-start(bf16[2,4,4,24,384]{4,3,2,1,0:T(8,128)(2,1)S(1)} %get-tuple-element.172), channel_id=1, source_target_pairs={{0,16},{1,17},{2,18},{3,19},{4,20},{5,21},{6,22},{7,23},{8,24},{9,... | collective-permute-start | bytes 1769480 | tf_op jit(solution)/shard_map/ppermute | solution.py:602
  401.7 8.9 %collective-permute-start.31 = (bf16[4,5,24,384]{3,2,1,0:T(8,128)(2,1)S(1)}, bf16[4,5,24,384]{3,2,1,0:T(8,128)(2,1)S(1)}, u32[]{:S(2)}, u32[]{:S(2)}) collective-permute-start(bf16[4,5,24,384]{3,2,1,0:T(8,128)(2,1)S(1)} %get-tuple-element.178), channel_id=1, source_target_pairs={{0,16},{1,17},{2,18},{3,19},{4,20},{5,21},{6,22},{7,23},{8,24},{9,... | collective-permute-start | bytes 1105928 | tf_op jit(solution)/shard_map/ppermute | solution.py:602
  404.0 13.8 %collective-permute-start.36 = (bf16[4,4,24,384]{3,2,1,0:T(8,128)(2,1)S(1)}, bf16[4,4,24,384]{3,2,1,0:T(8,128)(2,1)S(1)}, u32[]{:S(2)}, u32[]{:S(2)}) collective-permute-start(bf16[4,4,24,384]{3,2,1,0:T(8,128)(2,1)S(1)} %get-tuple-element.180), channel_id=1, source_target_pairs={{0,1},{1,0},{2,3},{3,2},{4,5},{5,4},{6,7},{7,6},{8,9},{9,8},{10,11... | collective-permute-start | bytes 884744 | tf_op jit(solution)/shard_map/ppermute | solution.py:602
  410.8 9.7 %collective-permute-start.32 = (bf16[5,24,384]{2,1,0:T(8,128)(2,1)S(1)}, bf16[5,24,384]{2,1,0:T(8,128)(2,1)S(1)}, u32[]{:S(2)}, u32[]{:S(2)}) collective-permute-start(bf16[5,24,384]{2,1,0:T(8,128)(2,1)S(1)} %get-tuple-element.189), channel_id=1, source_target_pairs={{0,2},{1,3},{2,4},{3,5},{4,6},{5,7},{6,0},{7,1},{8,10},{9,11},{10,... | collective-permute-start | bytes 276488 | tf_op jit(solution)/shard_map/ppermute | solution.py:602
  415.4 9.6 %collective-permute-start.33 = (bf16[5,24,384]{2,1,0:T(8,128)(2,1)S(1)}, bf16[5,24,384]{2,1,0:T(8,128)(2,1)S(1)}, u32[]{:S(2)}, u32[]{:S(2)}) collective-permute-start(bf16[5,24,384]{2,1,0:T(8,128)(2,1)S(1)} %get-tuple-element.191), channel_id=1, source_target_pairs={{0,4},{1,5},{2,6},{3,7},{4,0},{5,1},{6,2},{7,3},{8,12},{9,13},{10,... | collective-permute-start | bytes 276488 | tf_op jit(solution)/shard_map/ppermute | solution.py:602
  415.4 9.6 %collective-permute-start.34 = (bf16[5,24,384]{2,1,0:T(8,128)(2,1)S(1)}, bf16[5,24,384]{2,1,0:T(8,128)(2,1)S(1)}, u32[]{:S(2)}, u32[]{:S(2)}) collective-permute-start(bf16[5,24,384]{2,1,0:T(8,128)(2,1)S(1)} %get-tuple-element.190), channel_id=1, source_target_pairs={{0,6},{1,7},{2,0},{3,1},{4,2},{5,3},{6,4},{7,5},{8,14},{9,15},{10,... | collective-permute-start | bytes 276488 | tf_op jit(solution)/shard_map/ppermute | solution.py:602
  417.9 7.8 %collective-permute-start.37 = (bf16[4,24,384]{2,1,0:T(8,128)(2,1)S(1)}, bf16[4,24,384]{2,1,0:T(8,128)(2,1)S(1)}, u32[]{:S(2)}, u32[]{:S(2)}) collective-permute-start(bf16[4,24,384]{2,1,0:T(8,128)(2,1)S(1)} %get-tuple-element.192), channel_id=1, source_target_pairs={{0,2},{1,3},{2,4},{3,5},{4,6},{5,7},{6,0},{7,1},{8,10},{9,11},{10,... | collective-permute-start | bytes 221192 | tf_op jit(solution)/shard_map/ppermute | solution.py:602
  418.0 10.9 %collective-permute-start.38 = (bf16[4,24,384]{2,1,0:T(8,128)(2,1)S(1)}, bf16[4,24,384]{2,1,0:T(8,128)(2,1)S(1)}, u32[]{:S(2)}, u32[]{:S(2)}) collective-permute-start(bf16[4,24,384]{2,1,0:T(8,128)(2,1)S(1)} %get-tuple-element.194), channel_id=1, source_target_pairs={{0,4},{1,5},{2,6},{3,7},{4,0},{5,1},{6,2},{7,3},{8,12},{9,13},{10,... | collective-permute-start | bytes 221192 | tf_op jit(solution)/shard_map/ppermute | solution.py:602
  420.5 8.4 %collective-permute-start.39 = (bf16[4,24,384]{2,1,0:T(8,128)(2,1)S(1)}, bf16[4,24,384]{2,1,0:T(8,128)(2,1)S(1)}, u32[]{:S(2)}, u32[]{:S(2)}) collective-permute-start(bf16[4,24,384]{2,1,0:T(8,128)(2,1)S(1)} %get-tuple-element.193), channel_id=1, source_target_pairs={{0,6},{1,7},{2,0},{3,1},{4,2},{5,3},{6,4},{7,5},{8,14},{9,15},{10,... | collective-permute-start | bytes 221192 | tf_op jit(solution)/shard_map/ppermute | solution.py:602

commit v7 on v6

--- a/solution.py
+++ b/solution.py
@@ -82,15 +82,18 @@
 def attend_body(seq, pairs, len_ref, q_ref, k_ref, v_ref, o_ref, l_ref):
     count = len_ref[pl.program_id(0)]
     lane = lax.broadcasted_iota(jnp.int32, (seq, PAIR), 1)
-    ok = lax.broadcasted_iota(jnp.int32, (1, seq), 1) < count
+    row = lax.broadcasted_iota(jnp.int32, (seq, PAIR), 0)
+    mask = jnp.where(row < count, 0.0, -1e30).astype(BF)
     units = [(pr, h) for pr in range(pairs) for h in range(2)]
 
     def score(unit):
         pr, h = unit
         cols = slice(pr * PAIR, (pr + 1) * PAIR)
         mine = (lane >= HEAD_DIM) == (h == 1)
-        q = jnp.where(mine, q_ref[:, cols] * BF(0.125), BF(0))
-        return jnp.where(ok, mm(q, k_ref[:, cols], NT), -1e30)
+        spare = lane == HEAD_DIM * (1 - h)
+        q = jnp.where(mine, q_ref[:, cols] * BF(0.125), jnp.where(spare, BF(1), BF(0)))
+        k = jnp.where(mine, k_ref[:, cols], jnp.where(spare, mask, BF(0)))
+        return mm(q, k, NT)
 
     ahead = score(units[0])
     held = {}
@@ -362,66 +365,71 @@
             bv_ref[0, :, cols] = colsum(low.astype(F32))
 
 
-GROUPS = 2
-WIDE = D // GROUPS
-
-
-def attend_back_call(qkv, dctx, lse, lengths, group):
+WIDE = 3 * PAIR
+PARTS = D // WIDE
+
+
+def attend_back_call(qkv, dctx, lse, lengths, start, number):
     rows = qkv.shape[0]
     count = lengths.shape[0]
     seq = rows // count
     pairs = WIDE // PAIR
 
     def part(o):
-        return pl.BlockSpec((seq, WIDE), lambda s, n: (s, o * GROUPS + group))
+        return pl.BlockSpec((seq, WIDE), lambda s, p, n: (s, o * PARTS + start + p))
 
     def body(*refs):
         attend_back_body(seq, pairs, *refs)
 
-    line = pl.BlockSpec((1, 1, WIDE), lambda s, n: (s, 0, 0))
+    line = pl.BlockSpec((1, 1, WIDE), lambda s, p, n: (s, 0, p))
     return pl.pallas_call(
         body,
         grid_spec=pltpu.PrefetchScalarGridSpec(
             num_scalar_prefetch=1,
-            grid=(count,),
+            grid=(count, number),
             in_specs=[
                 part(0),
                 part(1),
                 part(2),
                 part(0),
-                pl.BlockSpec((1, pairs, 2, seq), lambda s, n: (s, group, 0, 0)),
+                pl.BlockSpec((1, pairs, 2, seq), lambda s, p, n: (s, start + p, 0, 0)),
             ],
-            out_specs=[pl.BlockSpec((3, seq, WIDE), lambda s, n: (0, s, 0)), line, line],
+            out_specs=[pl.BlockSpec((3, seq, WIDE), lambda s, p, n: (0, s, p)), line, line],
         ),
-        out_shape=[jax.ShapeDtypeStruct((3, rows, WIDE), BF)] + [jax.ShapeDtypeStruct((count, 1, WIDE), F32)] * 2,
-        compiler_params=params(),
-        cost_estimate=cost(12),
+        out_shape=[jax.ShapeDtypeStruct((3, rows, number * WIDE), BF)]
+        + [jax.ShapeDtypeStruct((count, 1, number * WIDE), F32)] * 2,
+        compiler_params=params(),
+        cost_estimate=cost(12 * number),
         name="attend_back",
     )(lengths, qkv, qkv, qkv, dctx, lse)
 
 
-def dx_body(dz1_ref, e0_ref, e1_ref, w_ref, o_ref):
+def dx_body(dz1_ref, *rest):
+    e_refs, w_ref, o_ref = rest[:-2], rest[-2], rest[-1]
     acc = dz1_ref[...]
     for i in range(3):
-        acc += mm(e0_ref[i], w_ref[i, :, :WIDE], NT)
-        acc += mm(e1_ref[i], w_ref[i, :, WIDE:], NT)
+        at = 0
+        for e_ref in e_refs:
+            width = e_ref.shape[2]
+            acc += mm(e_ref[i], w_ref[i, :, at : at + width], NT)
+            at += width
     o_ref[...] = acc.astype(o_ref.dtype)
 
 
-def dx_call(dz1, e0, e1, w, dtype, block=256):
+def dx_call(dz1, parts, w, dtype, block=256):
     rows = dz1.shape[0]
     line = pl.BlockSpec((block, D), lambda i: (i, 0))
-    part = pl.BlockSpec((3, block, WIDE), lambda i: (0, i, 0))
+    specs = [pl.BlockSpec((3, block, e.shape[2]), lambda i: (0, i, 0)) for e in parts]
     return pl.pallas_call(
         dx_body,
         grid=(rows // block,),
-        in_specs=[line, part, part, once((3, D, D), lambda i: (0, 0, 0))],
+        in_specs=[line, *specs, once((3, D, D), lambda i: (0, 0, 0))],
         out_specs=line,
         out_shape=jax.ShapeDtypeStruct((rows, D), dtype),
         compiler_params=params(),
         cost_estimate=cost(9),
         name="dx",
-    )(dz1, e0, e1, w)
+    )(dz1, *parts, w)
 
 
 def deal(acc_s, rows, x_first, core_ref, keep_ref, send_ref):
@@ -469,11 +477,12 @@
     )(core, a, c, b, d)
 
 
-def wgrad_heads_call(core, low2, low1, e2, e1, rows, others, x_first):
+def wgrad_heads_call(core, low2, low1, e2, e1, rows, group, others, x_first):
     k = low2.shape[0]
     last = len(others) == 4
     held = once((k, D), lambda i, n: (0, 0))
-    spec = pl.BlockSpec((1, k, WIDE), lambda i, n: (jnp.minimum(i, 2), 0, 0))
+    spec_2 = pl.BlockSpec((1, k, WIDE), lambda i, n: (jnp.minimum(i, 2), 0, group))
+    spec_1 = pl.BlockSpec((1, k, WIDE), lambda i, n: (jnp.minimum(i, 2), 0, 0))
     units = 5 if last else 4
     out_specs, out_shape = packet(rows, units, WIDE)
     if last:
@@ -507,10 +516,10 @@
             def _():
                 sums = rest[0][...] + rest[1][...]
                 small = []
-                for g in range(GROUPS):
-                    lines = rest[2 + 4 * g : 6 + 4 * g]
-                    small.append(colsum(lines[0][:, 0, :] + lines[1][:, 0, :]))
-                    small.append(colsum(lines[2][:, 0, :] + lines[3][:, 0, :]))
+                for g in range(PARTS):
+                    cols = slice(g * WIDE, (g + 1) * WIDE)
+                    for j in range(2):
+                        small.append(colsum(rest[2 + j][:, 0, cols] + rest[4 + 2 * g + j][:, 0, :]))
                     small.append(sums[2 : rows // 2, g * WIDE : (g + 1) * WIDE])
                 small = jnp.concatenate(small, axis=0).astype(BF)
                 for i in range(16):
@@ -522,7 +531,7 @@
         grid_spec=pltpu.PrefetchScalarGridSpec(
             num_scalar_prefetch=1,
             grid=(units,),
-            in_specs=[held, held, spec, spec] + more,
+            in_specs=[held, held, spec_2, spec_1] + more,
             out_specs=out_specs,
             scratch_shapes=[pltpu.VMEM((D, WIDE), F32)],
         ),
@@ -771,9 +780,9 @@
 
 
 class Sum:
-    def __init__(self, grid, place, order, pair):
+    def __init__(self, grid, place, order, pair, later=()):
         self.grid, self.place, self.order = grid, place, order
-        self.mine, self.came = pair[0], grid.send(pair[1], CORE)
+        self.mine, self.came = pair[0], grid.send(after(pair[1], *later), CORE)
 
     def cut(self, dim, others):
         here = self.place[dim]
@@ -790,17 +799,12 @@
         return self.cut(self.order[1], others)
 
     def three(self, *others):
-        z = self.place[2]
-        line = added(after(self.mine, *others), self.came)
-        self.mine = pick(line, z, 0)
-        self.came = [self.grid.send(pick(line, (z + k) % 4, 0), Z, k) for k in range(1, 4)]
-        return [line]
-
-    def result(self):
-        total = self.mine.astype(F32)
-        for piece in self.came:
-            total += piece.astype(F32)
-        return total
+        return added(after(self.mine, *others), self.came)
+
+
+def along_z(grid, lines):
+    line = jnp.concatenate(lines, axis=1)
+    return line, jnp.sum(grid.trade(line).astype(F32), axis=0)
 
 
 def staged(grid, lengths, tokens, cotangent, shards):
@@ -813,7 +817,8 @@
     core = core.astype(jnp.int32)[None]
     vectors = [bias_q, bias_v, bias_out, gain_one, shift_one, bias_back, gain_two, shift_two]
     one = Gather(grid, pack_one(device.astype(jnp.int32)[None], w_qkv, w_out, vectors, bias_in), 2, False)
-    two = Gather(grid, pack_two(w_in, w_back), 4, True)
+    packet = after(pack_two(w_in, w_back), one.ring)
+    two = Gather(grid, packet, 4, True)
     one.one()
     one.two()
     two.one(*one.far)
@@ -821,7 +826,7 @@
     first = first.reshape(5, grid.count * rows, D)
     vec = jnp.sum(first[4].reshape(grid.count, rows, D).astype(F32), axis=0)
     qkv = qkv_call(tokens, first, vec)
-    two.two()
+    two.two(first)
     ctx, lse = attend_call(after(qkv, *two.near), lengths)
     w_in, w_back = place(at, two.parts(ctx), True)
     w_in = w_in.reshape(4, grid.count * rows, D)
@@ -835,40 +840,35 @@
 
     low2, qkv, lse, ctx2, z1, h2, g2, slope, z2 = saved[1]
     e2_2, e1_2, dz1, ea_2, dctx, sums_2 = ffn_back_call(cotangent, z2, z1, slope, w_back, w_in, first, vec)
-    heads_2 = [attend_back_call(qkv, dctx, lse, lengths, i) for i in range(GROUPS)]
-    grad = dx_call(dz1, heads_2[0][0], heads_2[1][0], first, F32)
+    e_qkv_2, *lines_2 = attend_back_call(qkv, dctx, lse, lengths, 0, PARTS)
+    grad = dx_call(dz1, [e_qkv_2], first, F32)
 
     low1, qkv, lse, ctx1, z1, h1, g1, slope, z2 = saved[0]
     e2_1, e1_1, dz1, ea_1, dctx, sums_1 = ffn_back_call(grad, z2, z1, slope, w_back, w_in, first, vec)
     count = tokens.shape[0]
 
-    heads_1 = []
     back = wgrad_back_call(core, g2, g1, e2_2, e2_1, rows)
     sum_back = Sum(grid, where, (Y, X), back)
     into = wgrad_in_call(core, after(h2, back[0]), h1, e1_2, e1_1, rows)
     sum_in = Sum(grid, where, (X, Y), into)
     steps = sum_back.one(into[0]) + sum_in.one(into[0])
-    heads_1.append(attend_back_call(qkv, after(dctx, *steps), lse, lengths, 0))
-    heads_1.append(attend_back_call(qkv, after(dctx, heads_1[0][0]), lse, lengths, 1))
-    steps = sum_back.two(heads_1[1][0]) + sum_in.two(heads_1[1][0])
-    group = wgrad_heads_call(
-        core, after(low2, *steps), low1, heads_2[0][0], heads_1[0][0], rows, [ctx2, ctx1, ea_2, ea_1], False
-    )
-    sum_0 = Sum(grid, where, (Y, X), group)
-    steps = sum_back.three(group[0]) + sum_in.three(group[0])
-    lines = [heads[i][j] for i in range(GROUPS) for j in (1, 2) for heads in (heads_1, heads_2)]
-    group = wgrad_heads_call(
-        core, after(low2, *steps), low1, heads_2[1][0], heads_1[1][0], rows, [sums_1, sums_2, *lines], True
-    )
+    e_0, *lines_0 = attend_back_call(qkv, after(dctx, *steps), lse, lengths, 0, 1)
+    e_1, *lines_1 = attend_back_call(qkv, after(dctx, e_0), lse, lengths, 1, 1)
+    steps = sum_back.two(e_1) + sum_in.two(e_1)
+    others = [ctx2, ctx1, ea_2, ea_1]
+    group = wgrad_heads_call(core, after(low2, *steps), low1, e_qkv_2, e_0, rows, 0, others, False)
+    line, total = along_z(grid, [sum_in.three(group[0]), sum_back.three(group[0])])
+    sum_0 = Sum(grid, where, (Y, X), group, [line])
+    steps = [line]
+    sums = [sums_1, sums_2, *lines_2, *lines_0, *lines_1]
+    group = wgrad_heads_call(core, after(low2, *steps), low1, e_qkv_2, e_1, rows, 1, sums, True)
     sum_1 = Sum(grid, where, (X, Y), group)
     steps = sum_0.one(group[0]) + sum_1.one()
-    total_back = sum_back.result()
-    grad = dx_call(after(dz1, total_back, *steps), heads_1[0][0], heads_1[1][0], first, BF)
+    grad = dx_call(after(dz1, *steps), [e_0, e_1], first, BF)
     sum_0.two(grad)
     sum_1.two(grad)
-    sum_0.three()
-    sum_1.three()
-    total_in, half_0, half_1 = sum_in.result(), sum_0.result(), sum_1.result()
+    _, halves = along_z(grid, [sum_0.three(), sum_1.three()])
+    total_in, total_back, half_0, half_1 = total[:4], total[4:], halves[:5], halves[5:]
 
     w_in_grad = total_in.swapaxes(0, 1).reshape(rows, 4 * D)
     w_back_grad = total_back.reshape(4 * rows, D)
@@ -906,10 +906,10 @@
     for step in reversed(range(APPS)):
         low, qkv, lse, ctx, z1, h1, g, slope, z2 = saved[step]
         e2, e1, dz1, ea, dctx, sums = ffn_back_call(grad, z2, z1, slope, w_back, w_in, first, vec)
-        heads = [attend_back_call(qkv, dctx, lse, lengths, i) for i in range(GROUPS)]
-        grad = dx_call(dz1, heads[0][0], heads[1][0], first, F32 if step else BF)
-        e = jnp.concatenate([heads[i][0] for i in range(GROUPS)], axis=2).swapaxes(0, 1).reshape(-1, 3 * D)
-        lines = [jnp.concatenate([jnp.sum(heads[i][j], axis=0) for i in range(GROUPS)], axis=1) for j in (1, 2)]
+        e, *lines = attend_back_call(qkv, dctx, lse, lengths, 0, PARTS)
+        grad = dx_call(dz1, [e], first, F32 if step else BF)
+        e = e.swapaxes(0, 1).reshape(-1, 3 * D)
+        lines = [jnp.sum(v, axis=0) for v in lines]
         grads = [mm(low, e, TN), mm(ctx, ea, TN), mm(h1, e1, TN), mm(g, e2, TN)]
         grads += [jnp.concatenate(lines + [sums[2:]], axis=0)]
         totals = grads if totals is None else [a + b for a, b in zip(totals, grads)]

time: 438 us -> 427 us (0.975)
  starting transfers between devices: 66.9 us -> 46.7 us
  waiting for transfers between devices: 64.5 us -> 76.8 us
  Pallas kernels: 274 us -> 269 us
    ppermute x43 -> x31, starting transfers between devices: 63.2 us -> 30 us  [send(): return lax.ppermute(value, AXES, self.shift(dim, step))]
    all_to_all x1 -> x3, starting transfers between devices: 3.66 us -> 16.7 us  [trade(): lax.all_to_all(value, 'fsdp', 0, 0, tiled=True, axis_index_groups=groups)]
    all_to_all x1 -> x3, waiting for transfers between devices: 0.01 us -> 11.6 us  [trade(): lax.all_to_all(value, 'fsdp', 0, 0, tiled=True, axis_index_groups=groups)]
    pallas_call x4 -> x3, Pallas kernels: 49.8 us -> 46.8 us  [attend_back_call(): pl.pallas_call(body, grid_spec=pltpu.PrefetchScalarGridSpec(num_scalar_pr...]
    ppermute x43 -> x31, waiting for transfers between devices: 64.5 us -> 65.3 us  [send(): return lax.ppermute(value, AXES, self.shift(dim, step))]
  transfers between devices with their start and end apart: 44 -> 34, of which waited for: 15 -> 16; matrix products, arithmetic and copies ran while one was open for 5% -> 5% of each run, Pallas kernels for 20% -> 20%
where the time goes in v7:
time: 427 us; the launch traced here: 420 us
  Pallas kernels  269 us (63%)
  waiting for transfers between devices  76.8 us (18%)
  starting transfers between devices  46.7 us (11%)
  other arithmetic  19.7 us (5%)
  local copies, waits for them, and re-layouts  6.64 us (2%)
    ppermute x31, waiting for transfers between devices, send(): return lax.ppermute(value, AXES, self.shift(dim, step))  65.3 us
    pallas_call x2, Pallas kernels, ffn_back_call(): pl.pallas_call(ffn_back_body, grid=(rows // block,), in_specs=[line, line...  47.1 us
    pallas_call x3, Pallas kernels, attend_back_call(): pl.pallas_call(body, grid_spec=pltpu.PrefetchScalarGridSpec(num_scalar_pr...  46.8 us
    pallas_call x2, Pallas kernels, ffn_call(): pl.pallas_call(lambda *refs: ffn_body(renorm, *refs), grid=(rows // block...  45.2 us
    ppermute x31, starting transfers between devices, send(): return lax.ppermute(value, AXES, self.shift(dim, step))  30 us
    pallas_call x2, Pallas kernels, attend_call(): pl.pallas_call(body, grid_spec=pltpu.PrefetchScalarGridSpec(num_scalar_pr...  24.6 us
    pallas_call x2, Pallas kernels, wgrad_heads_call(): pl.pallas_call(body, grid_spec=pltpu.PrefetchScalarGridSpec(num_scalar_pr...  23.9 us
    pallas_call x2, Pallas kernels, dx_call(): pl.pallas_call(dx_body, grid=(rows // block,), in_specs=[line, *specs, on...  18.1 us
  transfers between devices with their start and end apart: 34, of which 16 were waited for; matrix products, arithmetic and copies ran while one was open for 5% of the time, Pallas kernels for 20%

profile of v7, /device:TPU:0, one launch (start us, length us, event | category | flops | bytes accessed | tf_op | source)
XLA Modules:
  0.0 420.4 jit_solution(13094828819870443477)
XLA Ops:
  0.7 1.8 pack_one.1
  2.4 3.0 collective-permute-start
  5.4 2.6 collective-permute-start.1
  8.0 1.3 collective-permute-start.2
  9.4 1.7 pack_two.1
  11.1 2.1 collective-permute-done
  13.2 7.1 %collective-permute-done.1 = bf16[5,24,768]{2,1,0:T(8,128)(2,1)S(1)} collective-permute-done((bf16[5,24,768]{2,1,0:T(8,128)(2,1)}, bf16[5,24,768]{2,1,0:T(8,128)(2,1)S(1)}, u32[]{:S(2)}, u32[]{:S(2)}) %collective-permute-start.1) | collective-permute-done | bytes 184352 | tf_op jit(solution)/shard_map/ppermute | solution.py:611
  20.3 1.0 pad_maximum_fusion.4
  21.3 1.1 broadcast_in_dim.44
  22.4 6.8 %all-to-all-start = ((bf16[4,8,24,768]{3,2,1,0:T(8,128)(2,1)}), bf16[4,8,24,768]{3,2,1,0:T(8,128)(2,1)S(1)}, u32[]{:S(2)}, u32[]{:S(2)}) async-start(bf16[4,8,24,768]{3,2,1,0:T(8,128)(2,1)} %broadcast_in_dim.44), calls=%async_computation | async-start | bytes 2359296 | tf_op jit(solution)/shard_map/all_to_all | solution.py:615
  29.2 1.6 collective-permute-start.6
  30.8 1.6 collective-permute-start.3
  32.4 7.7 %collective-permute-done.6 = bf16[4,3,24,768]{3,2,1,0:T(8,128)(2,1)S(1)} collective-permute-done((bf16[4,3,24,768]{3,2,1,0:T(8,128)(2,1)S(1)}, bf16[4,3,24,768]{3,2,1,0:T(8,128)(2,1)S(1)}, u32[]{:S(2)}, u32[]{:S(2)}) %collective-permute-start.6) | collective-permute-done | bytes 442400 | tf_op jit(solution)/shard_map/ppermute | solution.py:611
  40.1 1.6 collective-permute-start.7
  41.8 1.6 collective-permute-start.5
  43.9 10.8 %collective-permute-done.5.refs_3_ = bf16[2,4,2,24,768]{4,3,2,1,0:T(8,128)(2,1)} collective-permute-done((bf16[2,4,2,24,768]{4,3,2,1,0:T(8,128)(2,1)S(1)}, bf16[2,4,2,24,768]{4,3,2,1,0:T(8,128)(2,1)}, u32[]{:S(2)}, u32[]{:S(2)}) %collective-permute-start.5) | collective-permute-done | bytes 589856 | tf_op jit(solution)/shard_map/ppermute | solution.py:611
  54.7 4.9 %collective-permute-done.7.refs_7_ = bf16[2,4,3,24,768]{4,3,2,1,0:T(8,128)(2,1)} collective-permute-done((bf16[2,4,3,24,768]{4,3,2,1,0:T(8,128)(2,1)S(1)}, bf16[2,4,3,24,768]{4,3,2,1,0:T(8,128)(2,1)}, u32[]{:S(2)}, u32[]{:S(2)}) %collective-permute-start.7) | collective-permute-done | bytes 884768 | tf_op jit(solution)/shard_map/ppermute | solution.py:611
  60.1 0.9 fusion.17
  61.0 1.5 collective-permute-start.12
  62.5 1.5 collective-permute-start.11
  64.7 6.3 %place.2 = bf16[5,2,2,4,2,24,768]{6,5,4,3,2,1,0:T(8,128)(2,1)} custom-call(s32[4]{0:T(128)} %pad_add_fusion.refs_0_, bf16[2,4,2,24,768]{4,3,2,1,0:T(8,128)(2,1)} %copy-done.3, bf16[2,4,2,24,768]{4,3,2,1,0:T(8,128)(2,1)} %collective-permute-done.4.refs_2_, bf16[2,4,2,24,768]{4,3,2,1,0:T(8,128)(2,1)} %collective-permute-done.5.refs_3_, ...), custom_call_target="tpu_custom_call" | custom-call | flops 1200000000 | bytes 600000 | tf_op jit(solution)/shard_map/place/pallas_call | solution.py:724
  70.9 5.5 %collective-permute-done.12 = bf16[4,4,24,768]{3,2,1,0:T(8,128)(2,1)S(1)} collective-permute-done((bf16[4,4,24,768]{3,2,1,0:T(8,128)(2,1)}, bf16[4,4,24,768]{3,2,1,0:T(8,128)(2,1)S(1)}, u32[]{:S(2)}, u32[]{:S(2)}) %collective-permute-start.12) | collective-permute-done | bytes 589856 | tf_op jit(solution)/shard_map/ppermute | solution.py:611
  76.5 1.2 pad_maximum_fusion.1.refs_5_
  77.7 1.6 collective-permute-start.15
  79.4 1.6 collective-permute-start.14
  81.0 2.1 convert_reduce_fusion.1.vec_ref.refs_2_
  83.0 7.7 %qkv.2.refs_1_.refs_2_.refs_3_ = bf16[1024,2304]{1,0:T(8,128)(2,1)} custom-call(bf16[1024,768]{1,0:T(8,128)(2,1)} %c_ref.3, bf16[5,768,768]{2,1,0:T(8,128)(2,1)} %bitcast.98, f32[24,768]{1,0:T(8,128)} %convert_reduce_fusion.1.vec_ref.refs_2_), custom_call_target="tpu_custom_call" | custom-call | flops 1600000000 | bytes 800000 | tf_op jit(solution)/shard_map/qkv/pallas_call | solution.py:66
  91.2 12.3 %attend.2 = (bf16[1024,768]{1,0:T(8,128)(2,1)}, f32[2,6,2,512]{3,2,1,0:T(2,128)}) custom-call(s32[2]{0:T(128)} %refs_0_.11, bf16[1024,2304]{1,0:T(8,128)(2,1)} %qkv.2.refs_1_.refs_2_.refs_3_, bf16[1024,2304]{1,0:T(8,128)(2,1)} %qkv.2.refs_1_.refs_2_.refs_3_, bf16[1024,2304]{1,0:T(8,128)(2,1)} %qkv.2.refs_1_.refs_2_.refs_3_), custom_call_target="tpu_custom_call" | custom-call | flops 2600000000 | bytes 1300000 | tf_op jit(solution)/shard_map/attend/pallas_call | solution.py:127
  103.5 1.3 collective-permute-done.15.refs_7_
  104.8 1.4 collective-permute-done.14.refs_3_
  106.7 4.0 collective-permute-done.16.refs_4_
  111.8 8.3 %place.3 = (bf16[4,2,2,4,2,24,768]{6,5,4,3,2,1,0:T(8,128)(2,1)}, bf16[2,2,4,2,4,24,768]{6,5,4,3,2,1,0:T(8,128)(2,1)}) custom-call(s32[4]{0:T(128)} %pad_add_fusion.refs_0_, bf16[2,4,4,24,768]{4,3,2,1,0:T(8,128)(2,1)} %copy-done.1, bf16[2,4,4,24,768]{4,3,2,1,0:T(8,128)(2,1)} %copy-done.9, bf16[2,4,4,24,768]{4,3,2,1,0:T(8,128)(2,1)} %copy-done.7, ...), custom_call_target="tpu_custom_call" | custom-call | flops 1200000000 | bytes 600000 | tf_op jit(solution)/shard_map/place/pallas_call | solution.py:724
  120.1 22.3 %ffn.2 = (f32[1024,768]{1,0:T(8,128)}, bf16[1024,768]{1,0:T(8,128)(2,1)}, bf16[1024,3072]{1,0:T(8,128)(2,1)}, bf16[1024,3072]{1,0:T(8,128)(2,1)}, f32[1024,768]{1,0:T(8,128)}, /*index=5*/bf16[1024,768]{1,0:T(8,128)(2,1)}) custom-call(bf16[1024,768]{1,0:T(8,128)(2,1)} %c_ref.3, bf16[1024,768]{1,0:T(8,128)(2,1)} %get-tuple-element.98.refs_1_.rest_1_, ...), custom_call_target="tpu_custom_call" | custom-call | flops 4400000000 | bytes 2200000 | tf_op jit(solution)/shard_map/ffn/pallas_call | solution.py:227
  142.4 7.6 %qkv.3.refs_1_.refs_2_.refs_3_ = bf16[1024,2304]{1,0:T(8,128)(2,1)} custom-call(bf16[1024,768]{1,0:T(8,128)(2,1)} %get-tuple-element.146.x_ref.a_ref, bf16[5,768,768]{2,1,0:T(8,128)(2,1)} %bitcast.100, f32[24,768]{1,0:T(8,128)} %convert_reduce_fusion.1.vec_ref.refs_2_), custom_call_target="tpu_custom_call" | custom-call | flops 1600000000 | bytes 800000 | tf_op jit(solution)/shard_map/qkv/pallas_call | solution.py:66
  150.0 12.3 %attend.3 = (bf16[1024,768]{1,0:T(8,128)(2,1)}, f32[2,6,2,512]{3,2,1,0:T(2,128)}) custom-call(s32[2]{0:T(128)} %refs_0_.11, bf16[1024,2304]{1,0:T(8,128)(2,1)} %qkv.3.refs_1_.refs_2_.refs_3_, bf16[1024,2304]{1,0:T(8,128)(2,1)} %qkv.3.refs_1_.refs_2_.refs_3_, bf16[1024,2304]{1,0:T(8,128)(2,1)} %qkv.3.refs_1_.refs_2_.refs_3_), custom_call_target="tpu_custom_call" | custom-call | flops 2600000000 | bytes 1300000 | tf_op jit(solution)/shard_map/attend/pallas_call | solution.py:127
  162.3 22.9 %ffn.3 = (f32[1024,768]{1,0:T(8,128)}, bf16[1024,768]{1,0:T(8,128)(2,1)}, bf16[1024,3072]{1,0:T(8,128)(2,1)}, bf16[1024,3072]{1,0:T(8,128)(2,1)}, f32[1024,768]{1,0:T(8,128)}, /*index=5*/bf16[1024,768]{1,0:T(8,128)(2,1)}) custom-call(f32[1024,768]{1,0:T(8,128)} %get-tuple-element.103.refs_0_.z2_ref, bf16[1024,768]{1,0:T(8,128)(2,1)} %get-tuple-element.105.refs_1_.rest_0_, ...), custom_call_target="tpu_custom_call" | custom-call | flops 4400000000 | bytes 2200000 | tf_op jit(solution)/shard_map/ffn/pallas_call | solution.py:227
  185.2 23.4 %ffn_back.2 = (bf16[1024,768]{1,0:T(8,128)(2,1)}, bf16[1024,3072]{1,0:T(8,128)(2,1)}, f32[1024,768]{1,0:T(8,128)}, bf16[1024,768]{1,0:T(8,128)(2,1)}, bf16[1024,768]{1,0:T(8,128)(2,1)}, /*index=5*/f32[24,768]{1,0:T(8,128)}) custom-call(bf16[1024,768]{1,0:T(8,128)(2,1)} %dy_ref.1, f32[1024,768]{1,0:T(8,128)} %get-tuple-element.107.z2_ref, ...), custom_call_target="tpu_custom_call" | custom-call | flops 4800000000 | bytes 2400000 | tf_op jit(solution)/shard_map/ffn_back/pallas_call | solution.py:309
  208.6 21.9 %attend_back.3 = (bf16[3,1024,768]{2,1,0:T(8,128)(2,1)}, f32[2,1,768]{2,1,0:T(1,128)}, f32[2,1,768]{2,1,0:T(1,128)}) custom-call(s32[2]{0:T(128)} %refs_0_.11, bf16[1024,2304]{1,0:T(8,128)(2,1)} %qkv.3.refs_1_.refs_2_.refs_3_, bf16[1024,2304]{1,0:T(8,128)(2,1)} %qkv.3.refs_1_.refs_2_.refs_3_, bf16[1024,2304]{1,0:T(8,128)(2,1)} %qkv.3.refs_1_.refs_2_.refs_3_, ...), custom_call_target="tpu_custom_call" | custom-call | flops 4800000000 | bytes 2400000 | tf_op jit(solution)/shard_map/attend_back/pallas_call | solution.py:385
  230.5 8.8 %dx.2.dy_ref = f32[1024,768]{1,0:T(8,128)} custom-call(f32[1024,768]{1,0:T(8,128)} %get-tuple-element.110.dz1_ref, bf16[3,1024,768]{2,1,0:T(8,128)(2,1)} %get-tuple-element.113.rest_0_.b_ref, bf16[5,768,768]{2,1,0:T(8,128)(2,1)} %bitcast.103), custom_call_target="tpu_custom_call" | custom-call | flops 1800000000 | bytes 900000 | tf_op jit(solution)/shard_map/dx/pallas_call | solution.py:423
  239.3 23.7 %ffn_back.3 = (bf16[1024,768]{1,0:T(8,128)(2,1)}, bf16[1024,3072]{1,0:T(8,128)(2,1)}, f32[1024,768]{1,0:T(8,128)}, bf16[1024,768]{1,0:T(8,128)(2,1)}, bf16[1024,768]{1,0:T(8,128)(2,1)}, /*index=5*/f32[24,768]{1,0:T(8,128)}) custom-call(f32[1024,768]{1,0:T(8,128)} %dx.2.dy_ref, f32[1024,768]{1,0:T(8,128)} %get-tuple-element.103.refs_0_.z2_ref, ...), custom_call_target="tpu_custom_call" | custom-call | flops 4800000000 | bytes 2400000 | tf_op jit(solution)/shard_map/ffn_back/pallas_call | solution.py:309
  263.0 15.0 %wgrad_back.1 = (bf16[2,2,4,4,24,768]{5,4,3,2,1,0:T(8,128)(2,1)}, bf16[2,2,4,4,24,768]{5,4,3,2,1,0:T(8,128)(2,1)}) custom-call(s32[1]{0:T(128)} %bitcast.1.core_ref, bf16[1024,3072]{1,0:T(8,128)(2,1)} %get-tuple-element.117.g2k.g2s, bf16[1024,3072]{1,0:T(8,128)(2,1)} %get-tuple-element.118.g1k.g1s, bf16[1024,3072]{1,0:T(8,128)(2,1)} %get-tuple-element.117.g2k.g2s, ...), custom_call_target="tpu_custom_call" | custom-call | flops 3000000000 | bytes 1500000 | tf_op jit(solution)/shard_map/wgrad_back/pallas_call | solution.py:565
  278.0 15.3 %wgrad_in.1 = (bf16[2,2,4,4,24,768]{5,4,3,2,1,0:T(8,128)(2,1)}, bf16[2,2,4,4,24,768]{5,4,3,2,1,0:T(8,128)(2,1)}) custom-call(s32[1]{0:T(128)} %bitcast.1.core_ref, bf16[1024,768]{1,0:T(8,128)(2,1)} %get-tuple-element.123.a_ref, bf16[1024,768]{1,0:T(8,128)(2,1)} %get-tuple-element.124.c_ref, bf16[1024,3072]{1,0:T(8,128)(2,1)} %get-tuple-element.125.b_ref, ...), custom_call_target="tpu_custom_call" | custom-call | flops 3000000000 | bytes 1500000 | tf_op jit(solution)/shard_map/wgrad_in/pallas_call | solution.py:464
  293.7 4.4 %collective-permute-done.20 = bf16[2,2,4,4,24,768]{5,4,3,2,1,0:T(8,128)(2,1)} collective-permute-done((bf16[2,2,4,4,24,768]{5,4,3,2,1,0:T(8,128)(2,1)}, bf16[2,2,4,4,24,768]{5,4,3,2,1,0:T(8,128)(2,1)}, u32[]{:S(2)}, u32[]{:S(2)}) %collective-permute-start.20) | collective-permute-done | bytes 2359328 | tf_op jit(solution)/shard_map/ppermute | solution.py:611
  298.1 4.3 %fusion.3 = (bf16[2,4,4,24,768]{4,3,2,1,0:T(8,128)(2,1)S(1)}, bf16[2,4,4,24,768]{4,3,2,1,0:T(8,128)(2,1)}) fusion(bf16[2,2,4,4,24,768]{5,4,3,2,1,0:T(8,128)(2,1)} %collective-permute-done.20, s32[]{:T(128)S(6)} %select_n.87, bf16[2,2,4,4,24,768]{5,4,3,2,1,0:T(8,128)(2,1)} %get-tuple-element.131, s32[]{:T(128)S(6)} %select_n.86), kind=kLoop, calls=%fused_computation.12 | loop fusion | flops 4718592 | bytes 7077896 | tf_op jit(solution)/shard_map/convert_element_type | solution.py:779
  302.4 1.5 collective-permute-start.22
  303.9 2.3 fusion
  306.8 12.3 %attend_back.4 = (bf16[3,1024,384]{2,1,0:T(8,128)(2,1)}, f32[2,1,384]{2,1,0:T(1,128)}, f32[2,1,384]{2,1,0:T(1,128)}) custom-call(s32[2]{0:T(128)} %refs_0_.11, bf16[1024,2304]{1,0:T(8,128)(2,1)} %qkv.2.refs_1_.refs_2_.refs_3_, bf16[1024,2304]{1,0:T(8,128)(2,1)} %qkv.2.refs_1_.refs_2_.refs_3_, bf16[1024,2304]{1,0:T(8,128)(2,1)} %qkv.2.refs_1_.refs_2_.refs_3_, ...), custom_call_target="tpu_custom_call" | custom-call | flops 2400000000 | bytes 1200000 | tf_op jit(solution)/shard_map/attend_back/pallas_call | solution.py:385
  319.1 12.5 %attend_back.5 = (bf16[3,1024,384]{2,1,0:T(8,128)(2,1)}, f32[2,1,384]{2,1,0:T(1,128)}, f32[2,1,384]{2,1,0:T(1,128)}) custom-call(s32[2]{0:T(128)} %refs_0_.11, bf16[1024,2304]{1,0:T(8,128)(2,1)} %qkv.2.refs_1_.refs_2_.refs_3_, bf16[1024,2304]{1,0:T(8,128)(2,1)} %qkv.2.refs_1_.refs_2_.refs_3_, bf16[1024,2304]{1,0:T(8,128)(2,1)} %qkv.2.refs_1_.refs_2_.refs_3_, ...), custom_call_target="tpu_custom_call" | custom-call | flops 2400000000 | bytes 1200000 | tf_op jit(solution)/shard_map/attend_back/pallas_call | solution.py:385
  331.6 1.5 fusion.9
  333.2 1.6 collective-permute-start.23
  335.6 14.6 %wgrad_heads.2 = (bf16[2,2,4,5,24,384]{5,4,3,2,1,0:T(8,128)(2,1)}, bf16[2,2,4,5,24,384]{5,4,3,2,1,0:T(8,128)(2,1)}) custom-call(s32[1]{0:T(128)} %bitcast.1.core_ref, bf16[1024,768]{1,0:T(8,128)(2,1)} %get-tuple-element.146.x_ref.a_ref, bf16[1024,768]{1,0:T(8,128)(2,1)} %c_ref.3, bf16[3,1024,768]{2,1,0:T(8,128)(2,1)} %get-tuple-element.113.rest_0_.b_ref, ...), custom_call_target="tpu_custom_call" | custom-call | flops 2400000000 | bytes 1200000 | tf_op jit(solution)/shard_map/wgrad_heads/pallas_call | solution.py:529
  350.5 1.2 pad_maximum_fusion.2
  351.7 9.3 %wgrad_heads.3 = (bf16[2,2,4,4,24,384]{5,4,3,2,1,0:T(8,128)(2,1)}, bf16[2,2,4,4,24,384]{5,4,3,2,1,0:T(8,128)(2,1)}) custom-call(s32[1]{0:T(128)} %bitcast.1.core_ref, bf16[1024,768]{1,0:T(8,128)(2,1)} %get-tuple-element.146.x_ref.a_ref, bf16[1024,768]{1,0:T(8,128)(2,1)} %c_ref.3, bf16[3,1024,768]{2,1,0:T(8,128)(2,1)} %get-tuple-element.113.rest_0_.b_ref, ...), custom_call_target="tpu_custom_call" | custom-call | flops 2400000000 | bytes 1200000 | tf_op jit(solution)/shard_map/wgrad_heads/pallas_call | solution.py:529
  361.5 4.8 %all-to-all-start.2 = ((bf16[4,8,24,768]{3,2,1,0:T(8,128)(2,1)}), bf16[4,8,24,768]{3,2,1,0:T(8,128)(2,1)S(1)}, u32[]{:S(2)}, u32[]{:S(2)}) async-start(bf16[4,8,24,768]{3,2,1,0:T(8,128)(2,1)} %pad_maximum_fusion.2), calls=%async_computation.2 | async-start | bytes 2359296 | tf_op jit(solution)/shard_map/all_to_all | solution.py:615
  366.3 2.0 fusion.11
  368.3 1.6 collective-permute-start.29
  370.8 9.2 %dx.3 = bf16[1024,768]{1,0:T(8,128)(2,1)} custom-call(f32[1024,768]{1,0:T(8,128)} %get-tuple-element.160.dz1_ref, bf16[3,1024,384]{2,1,0:T(8,128)(2,1)} %get-tuple-element.135.d_ref.rest_0_, bf16[3,1024,384]{2,1,0:T(8,128)(2,1)} %get-tuple-element.137.d_ref.rest_1_, bf16[5,768,768]{2,1,0:T(8,128)(2,1)} %bitcast.105), custom_call_target="tpu_custom_call" | custom-call | flops 1800000000 | bytes 900000 | tf_op jit(solution)/shard_map/dx/pallas_call | solution.py:423
  380.1 3.3 collective-permute-done.29
  384.1 5.6 %collective-permute-done.27 = bf16[2,4,5,24,384]{4,3,2,1,0:T(8,128)(2,1)S(1)} collective-permute-done((bf16[2,4,5,24,384]{4,3,2,1,0:T(8,128)(2,1)S(1)}, bf16[2,4,5,24,384]{4,3,2,1,0:T(8,128)(2,1)S(1)}, u32[]{:S(2)}, u32[]{:S(2)}) %collective-permute-start.27) | collective-permute-done | bytes 737312 | tf_op jit(solution)/shard_map/ppermute | solution.py:611
  390.5 4.0 collective-permute-done.30
  394.6 2.9 collective-permute-done.28
  397.6 0.9 pad_maximum_fusion.5
  398.6 5.1 %all-to-all-start.1 = ((bf16[4,9,24,384]{3,2,1,0:T(8,128)(2,1)}), bf16[4,9,24,384]{3,2,1,0:T(8,128)(2,1)S(1)}, u32[]{:S(2)}, u32[]{:S(2)}) async-start(bf16[4,9,24,384]{3,2,1,0:T(8,128)(2,1)} %pad_maximum_fusion.5), calls=%async_computation.1 | async-start | bytes 1327104 | tf_op jit(solution)/shard_map/all_to_all | solution.py:615
  405.3 11.6 %all-to-all-done.1 = bf16[4,9,24,384]{3,2,1,0:T(8,128)(2,1)S(1)} async-done(((bf16[4,9,24,384]{3,2,1,0:T(8,128)(2,1)}), bf16[4,9,24,384]{3,2,1,0:T(8,128)(2,1)S(1)}, u32[]{:S(2)}, u32[]{:S(2)}) %all-to-all-start.1) | async-done | bytes 663584 | tf_op jit(solution)/shard_map/all_to_all | solution.py:615
  (88 shorter events, 14.1 us)
Async XLA Ops:
  2.4 10.8 %collective-permute-start = (bf16[5,24,768]{2,1,0:T(8,128)(2,1)}, bf16[5,24,768]{2,1,0:T(8,128)(2,1)S(1)}, u32[]{:S(2)}, u32[]{:S(2)}) collective-permute-start(bf16[5,24,768]{2,1,0:T(8,128)(2,1)} %pack_one.1), channel_id=1, source_target_pairs={{0,2},{1,3},{2,4},{3,5},{4,6},{5,7},{6,0},{7,1},{8,10},{9,11},{10,... | collective-permute-start | bytes 552968 | tf_op jit(solution)/shard_map/ppermute | solution.py:611
  5.4 14.9 %collective-permute-start.1 = (bf16[5,24,768]{2,1,0:T(8,128)(2,1)}, bf16[5,24,768]{2,1,0:T(8,128)(2,1)S(1)}, u32[]{:S(2)}, u32[]{:S(2)}) collective-permute-start(bf16[5,24,768]{2,1,0:T(8,128)(2,1)} %pack_one.1), channel_id=1, source_target_pairs={{0,4},{1,5},{2,6},{3,7},{4,0},{5,1},{6,2},{7,3},{8,12},{9,13},{10,... | collective-permute-start | bytes 552968 | tf_op jit(solution)/shard_map/ppermute | solution.py:611
  8.0 12.3 %collective-permute-start.2 = (bf16[5,24,768]{2,1,0:T(8,128)(2,1)}, bf16[5,24,768]{2,1,0:T(8,128)(2,1)S(1)}, u32[]{:S(2)}, u32[]{:S(2)}) collective-permute-start(bf16[5,24,768]{2,1,0:T(8,128)(2,1)} %pack_one.1), channel_id=1, source_target_pairs={{0,6},{1,7},{2,0},{3,1},{4,2},{5,3},{6,4},{7,5},{8,14},{9,15},{10,... | collective-permute-start | bytes 552968 | tf_op jit(solution)/shard_map/ppermute | solution.py:611
  11.1 10.2 %copy-start.11 = (bf16[8,24,768]{2,1,0:T(8,128)(2,1)S(1)}, bf16[8,24,768]{2,1,0:T(8,128)(2,1)}, u32[]{:S(2)}) copy-start(bf16[8,24,768]{2,1,0:T(8,128)(2,1)} %pack_two.1) | copy-start | bytes 884740
  22.4 37.7 %all-to-all-start = ((bf16[4,8,24,768]{3,2,1,0:T(8,128)(2,1)}), bf16[4,8,24,768]{3,2,1,0:T(8,128)(2,1)S(1)}, u32[]{:S(2)}, u32[]{:S(2)}) async-start(bf16[4,8,24,768]{3,2,1,0:T(8,128)(2,1)} %broadcast_in_dim.44), calls=%async_computation | async-start | bytes 2359296 | tf_op jit(solution)/shard_map/all_to_all | solution.py:615
  29.2 10.8 %collective-permute-start.6 = (bf16[4,3,24,768]{3,2,1,0:T(8,128)(2,1)S(1)}, bf16[4,3,24,768]{3,2,1,0:T(8,128)(2,1)S(1)}, u32[]{:S(2)}, u32[]{:S(2)}) collective-permute-start(bf16[4,3,24,768]{3,2,1,0:T(8,128)(2,1)S(1)} %slice.100), channel_id=1, source_target_pairs={{0,16},{1,17},{2,18},{3,19},{4,20},{5,21},{6,22},{7,23},{8,24},{9,... | collective-permute-start | bytes 1327112 | tf_op jit(solution)/shard_map/ppermute | solution.py:611
  30.8 10.9 %collective-permute-start.3 = (bf16[4,2,24,768]{3,2,1,0:T(8,128)(2,1)S(1)}, bf16[4,2,24,768]{3,2,1,0:T(8,128)(2,1)S(1)}, u32[]{:S(2)}, u32[]{:S(2)}) collective-permute-start(bf16[4,2,24,768]{3,2,1,0:T(8,128)(2,1)S(1)} %slice.99), channel_id=1, source_target_pairs={{0,1},{1,0},{2,3},{3,2},{4,5},{5,4},{6,7},{7,6},{8,9},{9,8},{10,11... | collective-permute-start | bytes 884744 | tf_op jit(solution)/shard_map/ppermute | solution.py:611
  40.1 20.9 %copy-start.2 = (bf16[2,4,3,24,768]{4,3,2,1,0:T(8,128)(2,1)}, bf16[2,4,3,24,768]{4,3,2,1,0:T(8,128)(2,1)S(1)}, u32[]{:S(2)}) copy-start(bf16[2,4,3,24,768]{4,3,2,1,0:T(8,128)(2,1)S(1)} %pad_maximum_fusion.3.refs_5_) | copy-start | bytes 2654212
  40.1 19.5 %collective-permute-start.7 = (bf16[2,4,3,24,768]{4,3,2,1,0:T(8,128)(2,1)S(1)}, bf16[2,4,3,24,768]{4,3,2,1,0:T(8,128)(2,1)}, u32[]{:S(2)}, u32[]{:S(2)}) collective-permute-start(bf16[2,4,3,24,768]{4,3,2,1,0:T(8,128)(2,1)S(1)} %pad_maximum_fusion.3.refs_5_), channel_id=1, source_target_pairs={{0,1},{1,0},{2,3},{3,2},{4,5},{5,4},{6,7},{7,6},{8,9},{9,8},{10,11... | collective-permute-start | bytes 2654216 | tf_op jit(solution)/shard_map/ppermute | solution.py:611
  41.8 19.3 %copy-start.3 = (bf16[2,4,2,24,768]{4,3,2,1,0:T(8,128)(2,1)}, bf16[2,4,2,24,768]{4,3,2,1,0:T(8,128)(2,1)S(1)}, u32[]{:S(2)}) copy-start(bf16[2,4,2,24,768]{4,3,2,1,0:T(8,128)(2,1)S(1)} %pad_maximum_fusion.6.refs_1_) | copy-start | bytes 1769476
  41.8 12.9 %collective-permute-start.5 = (bf16[2,4,2,24,768]{4,3,2,1,0:T(8,128)(2,1)S(1)}, bf16[2,4,2,24,768]{4,3,2,1,0:T(8,128)(2,1)}, u32[]{:S(2)}, u32[]{:S(2)}) collective-permute-start(bf16[2,4,2,24,768]{4,3,2,1,0:T(8,128)(2,1)S(1)} %pad_maximum_fusion.6.refs_1_), channel_id=1, source_target_pairs={{0,16},{1,17},{2,18},{3,19},{4,20},{5,21},{6,22},{7,23},{8,24},{9,... | collective-permute-start | bytes 1769480 | tf_op jit(solution)/shard_map/ppermute | solution.py:611
  43.4 19.2 %collective-permute-start.4 = (bf16[2,4,2,24,768]{4,3,2,1,0:T(8,128)(2,1)S(1)}, bf16[2,4,2,24,768]{4,3,2,1,0:T(8,128)(2,1)}, u32[]{:S(2)}, u32[]{:S(2)}) collective-permute-start(bf16[2,4,2,24,768]{4,3,2,1,0:T(8,128)(2,1)S(1)} %pad_maximum_fusion.6.refs_1_), channel_id=1, source_target_pairs={{0,8},{1,9},{2,10},{3,11},{4,12},{5,13},{6,14},{7,15},{8,0},{9,1},... | collective-permute-start | bytes 1769480 | tf_op jit(solution)/shard_map/ppermute | solution.py:611
  43.4 21.3 %collective-permute-start.9 = (bf16[2,4,3,24,768]{4,3,2,1,0:T(8,128)(2,1)S(1)}, bf16[2,4,3,24,768]{4,3,2,1,0:T(8,128)(2,1)}, u32[]{:S(2)}, u32[]{:S(2)}) collective-permute-start(bf16[2,4,3,24,768]{4,3,2,1,0:T(8,128)(2,1)S(1)} %pad_maximum_fusion.3.refs_5_), channel_id=1, source_target_pairs={{0,8},{1,9},{2,10},{3,11},{4,12},{5,13},{6,14},{7,15},{8,0},{9,1},... | collective-permute-start | bytes 2654216 | tf_op jit(solution)/shard_map/ppermute | solution.py:611
  59.6 5.0 %collective-permute-start.10 = (bf16[2,4,3,24,768]{4,3,2,1,0:T(8,128)(2,1)}, bf16[2,4,3,24,768]{4,3,2,1,0:T(8,128)(2,1)}, u32[]{:S(2)}, u32[]{:S(2)}) collective-permute-start(bf16[2,4,3,24,768]{4,3,2,1,0:T(8,128)(2,1)} %collective-permute-done.7.refs_7_), channel_id=1, source_target_pairs={{0,8},{1,9},{2,10},{3,11},{4,12},{5,13},{6,14},{7,15},{8,0},{9,1},... | collective-permute-start | bytes 2654216 | tf_op jit(solution)/shard_map/ppermute | solution.py:611
  59.6 5.0 %collective-permute-start.8 = (bf16[2,4,2,24,768]{4,3,2,1,0:T(8,128)(2,1)}, bf16[2,4,2,24,768]{4,3,2,1,0:T(8,128)(2,1)}, u32[]{:S(2)}, u32[]{:S(2)}) collective-permute-start(bf16[2,4,2,24,768]{4,3,2,1,0:T(8,128)(2,1)} %collective-permute-done.5.refs_3_), channel_id=1, source_target_pairs={{0,8},{1,9},{2,10},{3,11},{4,12},{5,13},{6,14},{7,15},{8,0},{9,1},... | collective-permute-start | bytes 1769480 | tf_op jit(solution)/shard_map/ppermute | solution.py:611
  61.0 15.4 %collective-permute-start.12 = (bf16[4,4,24,768]{3,2,1,0:T(8,128)(2,1)}, bf16[4,4,24,768]{3,2,1,0:T(8,128)(2,1)S(1)}, u32[]{:S(2)}, u32[]{:S(2)}) collective-permute-start(bf16[4,4,24,768]{3,2,1,0:T(8,128)(2,1)} %get-tuple-element.96), channel_id=1, source_target_pairs={{0,16},{1,17},{2,18},{3,19},{4,20},{5,21},{6,22},{7,23},{8,24},{9,... | collective-permute-start | bytes 1769480 | tf_op jit(solution)/shard_map/ppermute | solution.py:611
  62.5 16.7 %collective-permute-start.11 = (bf16[4,4,24,768]{3,2,1,0:T(8,128)(2,1)S(1)}, bf16[4,4,24,768]{3,2,1,0:T(8,128)(2,1)S(1)}, u32[]{:S(2)}, u32[]{:S(2)}) collective-permute-start(bf16[4,4,24,768]{3,2,1,0:T(8,128)(2,1)S(1)} %get-tuple-element.95), channel_id=1, source_target_pairs={{0,1},{1,0},{2,3},{3,2},{4,5},{5,4},{6,7},{7,6},{8,9},{9,8},{10,11... | collective-permute-start | bytes 1769480 | tf_op jit(solution)/shard_map/ppermute | solution.py:611
  77.7 13.0 %copy-start = (bf16[2,4,4,24,768]{4,3,2,1,0:T(8,128)(2,1)}, bf16[2,4,4,24,768]{4,3,2,1,0:T(8,128)(2,1)S(1)}, u32[]{:S(2)}) copy-start(bf16[2,4,4,24,768]{4,3,2,1,0:T(8,128)(2,1)S(1)} %pad_maximum_fusion.1.refs_5_) | copy-start | bytes 3538948
  77.7 27.1 %collective-permute-start.15 = (bf16[2,4,4,24,768]{4,3,2,1,0:T(8,128)(2,1)S(1)}, bf16[2,4,4,24,768]{4,3,2,1,0:T(8,128)(2,1)S(1)}, u32[]{:S(2)}, u32[]{:S(2)}) collective-permute-start(bf16[2,4,4,24,768]{4,3,2,1,0:T(8,128)(2,1)S(1)} %pad_maximum_fusion.1.refs_5_), channel_id=1, source_target_pairs={{0,1},{1,0},{2,3},{3,2},{4,5},{5,4},{6,7},{7,6},{8,9},{9,8},{10,11... | collective-permute-start | bytes 3538952 | tf_op jit(solution)/shard_map/ppermute | solution.py:611
  79.4 11.3 %copy-start.1 = (bf16[2,4,4,24,768]{4,3,2,1,0:T(8,128)(2,1)}, bf16[2,4,4,24,768]{4,3,2,1,0:T(8,128)(2,1)S(1)}, u32[]{:S(2)}) copy-start(bf16[2,4,4,24,768]{4,3,2,1,0:T(8,128)(2,1)S(1)} %pad_maximum_fusion.refs_1_) | copy-start | bytes 3538948
  79.4 26.8 %collective-permute-start.14 = (bf16[2,4,4,24,768]{4,3,2,1,0:T(8,128)(2,1)S(1)}, bf16[2,4,4,24,768]{4,3,2,1,0:T(8,128)(2,1)S(1)}, u32[]{:S(2)}, u32[]{:S(2)}) collective-permute-start(bf16[2,4,4,24,768]{4,3,2,1,0:T(8,128)(2,1)S(1)} %pad_maximum_fusion.refs_1_), channel_id=1, source_target_pairs={{0,16},{1,17},{2,18},{3,19},{4,20},{5,21},{6,22},{7,23},{8,24},{9,... | collective-permute-start | bytes 3538952 | tf_op jit(solution)/shard_map/ppermute | solution.py:611
  90.7 16.0 %collective-permute-start.17 = (bf16[2,4,4,24,768]{4,3,2,1,0:T(8,128)(2,1)S(1)}, bf16[2,4,4,24,768]{4,3,2,1,0:T(8,128)(2,1)S(1)}, u32[]{:S(2)}, u32[]{:S(2)}) collective-permute-start(bf16[2,4,4,24,768]{4,3,2,1,0:T(8,128)(2,1)S(1)} %pad_maximum_fusion.1.refs_5_), channel_id=1, source_target_pairs={{0,8},{1,9},{2,10},{3,11},{4,12},{5,13},{6,14},{7,15},{8,0},{9,1},... | collective-permute-start | bytes 3538952 | tf_op jit(solution)/shard_map/ppermute | solution.py:611
  90.7 16.0 %collective-permute-start.13 = (bf16[2,4,4,24,768]{4,3,2,1,0:T(8,128)(2,1)S(1)}, bf16[2,4,4,24,768]{4,3,2,1,0:T(8,128)(2,1)S(1)}, u32[]{:S(2)}, u32[]{:S(2)}) collective-permute-start(bf16[2,4,4,24,768]{4,3,2,1,0:T(8,128)(2,1)S(1)} %pad_maximum_fusion.refs_1_), channel_id=1, source_target_pairs={{0,8},{1,9},{2,10},{3,11},{4,12},{5,13},{6,14},{7,15},{8,0},{9,1},... | collective-permute-start | bytes 3538952 | tf_op jit(solution)/shard_map/ppermute | solution.py:611
  104.8 6.1 %copy-start.6 = (bf16[2,4,4,24,768]{4,3,2,1,0:T(8,128)(2,1)}, bf16[2,4,4,24,768]{4,3,2,1,0:T(8,128)(2,1)S(1)}, u32[]{:S(2)}) copy-start(bf16[2,4,4,24,768]{4,3,2,1,0:T(8,128)(2,1)S(1)} %collective-permute-done.15.refs_7_) | copy-start | bytes 3538948
  106.2 4.7 %copy-start.7 = (bf16[2,4,4,24,768]{4,3,2,1,0:T(8,128)(2,1)}, bf16[2,4,4,24,768]{4,3,2,1,0:T(8,128)(2,1)S(1)}, u32[]{:S(2)}) copy-start(bf16[2,4,4,24,768]{4,3,2,1,0:T(8,128)(2,1)S(1)} %collective-permute-done.14.refs_3_) | copy-start | bytes 3538948
  106.2 4.5 %collective-permute-start.16 = (bf16[2,4,4,24,768]{4,3,2,1,0:T(8,128)(2,1)S(1)}, bf16[2,4,4,24,768]{4,3,2,1,0:T(8,128)(2,1)S(1)}, u32[]{:S(2)}, u32[]{:S(2)}) collective-permute-start(bf16[2,4,4,24,768]{4,3,2,1,0:T(8,128)(2,1)S(1)} %collective-permute-done.14.refs_3_), channel_id=1, source_target_pairs={{0,8},{1,9},{2,10},{3,11},{4,12},{5,13},{6,14},{7,15},{8,0},{9,1},... | collective-permute-start | bytes 3538952 | tf_op jit(solution)/shard_map/ppermute | solution.py:611
  106.2 4.7 %collective-permute-start.18 = (bf16[2,4,4,24,768]{4,3,2,1,0:T(8,128)(2,1)S(1)}, bf16[2,4,4,24,768]{4,3,2,1,0:T(8,128)(2,1)}, u32[]{:S(2)}, u32[]{:S(2)}) collective-permute-start(bf16[2,4,4,24,768]{4,3,2,1,0:T(8,128)(2,1)S(1)} %collective-permute-done.15.refs_7_), channel_id=1, source_target_pairs={{0,8},{1,9},{2,10},{3,11},{4,12},{5,13},{6,14},{7,15},{8,0},{9,1},... | collective-permute-start | bytes 3538952 | tf_op jit(solution)/shard_map/ppermute | solution.py:611
  106.7 4.2 copy-start.8
  106.7 4.2 copy-start.9
  110.7 1.1 copy-start.10
  293.2 4.9 %collective-permute-start.20 = (bf16[2,2,4,4,24,768]{5,4,3,2,1,0:T(8,128)(2,1)}, bf16[2,2,4,4,24,768]{5,4,3,2,1,0:T(8,128)(2,1)}, u32[]{:S(2)}, u32[]{:S(2)}) collective-permute-start(bf16[2,2,4,4,24,768]{5,4,3,2,1,0:T(8,128)(2,1)} %get-tuple-element.132), channel_id=1, source_target_pairs={{0,8},{1,9},{2,10},{3,11},{4,12},{5,13},{6,14},{7,15},{8,0},{9,1},... | collective-permute-start | bytes 7077896 | tf_op jit(solution)/shard_map/ppermute | solution.py:611
  293.4 10.5 %collective-permute-start.19 = (bf16[2,2,4,4,24,768]{5,4,3,2,1,0:T(8,128)(2,1)}, bf16[2,2,4,4,24,768]{5,4,3,2,1,0:T(8,128)(2,1)}, u32[]{:S(2)}, u32[]{:S(2)}) collective-permute-start(bf16[2,2,4,4,24,768]{5,4,3,2,1,0:T(8,128)(2,1)} %get-tuple-element.129), channel_id=1, source_target_pairs={{0,8},{1,9},{2,10},{3,11},{4,12},{5,13},{6,14},{7,15},{8,0},{9,1},... | collective-permute-start | bytes 7077896 | tf_op jit(solution)/shard_map/ppermute | solution.py:611
  298.1 5.7 %copy-start.4 = (bf16[2,2,4,4,24,768]{5,4,3,2,1,0:T(8,128)(2,1)S(1)}, bf16[2,2,4,4,24,768]{5,4,3,2,1,0:T(8,128)(2,1)}, u32[]{:S(2)}) copy-start(bf16[2,2,4,4,24,768]{5,4,3,2,1,0:T(8,128)(2,1)} %get-tuple-element.128) | copy-start | bytes 7077892
  302.4 29.2 %collective-permute-start.22 = (bf16[2,4,4,24,768]{4,3,2,1,0:T(8,128)(2,1)}, bf16[2,4,4,24,768]{4,3,2,1,0:T(8,128)(2,1)}, u32[]{:S(2)}, u32[]{:S(2)}) collective-permute-start(bf16[2,4,4,24,768]{4,3,2,1,0:T(8,128)(2,1)} %get-tuple-element.164), channel_id=1, source_target_pairs={{0,16},{1,17},{2,18},{3,19},{4,20},{5,21},{6,22},{7,23},{8,24},{9,... | collective-permute-start | bytes 3538952 | tf_op jit(solution)/shard_map/ppermute | solution.py:611
  306.2 28.5 %collective-permute-start.21 = (bf16[2,4,4,24,768]{4,3,2,1,0:T(8,128)(2,1)S(1)}, bf16[2,4,4,24,768]{4,3,2,1,0:T(8,128)(2,1)S(1)}, u32[]{:S(2)}, u32[]{:S(2)}) collective-permute-start(bf16[2,4,4,24,768]{4,3,2,1,0:T(8,128)(2,1)S(1)} %get-tuple-element.166), channel_id=1, source_target_pairs={{0,1},{1,0},{2,3},{3,2},{4,5},{5,4},{6,7},{7,6},{8,9},{9,8},{10,11... | collective-permute-start | bytes 3538952 | tf_op jit(solution)/shard_map/ppermute | solution.py:611
  333.2 17.0 %collective-permute-start.23 = (bf16[4,4,24,768]{3,2,1,0:T(8,128)(2,1)S(1)}, bf16[4,4,24,768]{3,2,1,0:T(8,128)(2,1)S(1)}, u32[]{:S(2)}, u32[]{:S(2)}) collective-permute-start(bf16[4,4,24,768]{3,2,1,0:T(8,128)(2,1)S(1)} %get-tuple-element.172), channel_id=1, source_target_pairs={{0,1},{1,0},{2,3},{3,2},{4,5},{5,4},{6,7},{7,6},{8,9},{9,8},{10,11... | collective-permute-start | bytes 1769480 | tf_op jit(solution)/shard_map/ppermute | solution.py:611
  335.0 15.3 %collective-permute-start.24 = (bf16[4,4,24,768]{3,2,1,0:T(8,128)(2,1)S(1)}, bf16[4,4,24,768]{3,2,1,0:T(8,128)(2,1)S(1)}, u32[]{:S(2)}, u32[]{:S(2)}) collective-permute-start(bf16[4,4,24,768]{3,2,1,0:T(8,128)(2,1)S(1)} %get-tuple-element.174), channel_id=1, source_target_pairs={{0,16},{1,17},{2,18},{3,19},{4,20},{5,21},{6,22},{7,23},{8,24},{9,... | collective-permute-start | bytes 1769480 | tf_op jit(solution)/shard_map/ppermute | solution.py:611
  351.7 18.2 %collective-permute-start.25 = (bf16[2,2,4,5,24,384]{5,4,3,2,1,0:T(8,128)(2,1)}, bf16[2,2,4,5,24,384]{5,4,3,2,1,0:T(8,128)(2,1)S(1)}, u32[]{:S(2)}, u32[]{:S(2)}) collective-permute-start(bf16[2,2,4,5,24,384]{5,4,3,2,1,0:T(8,128)(2,1)} %get-tuple-element.158), channel_id=1, source_target_pairs={{0,8},{1,9},{2,10},{3,11},{4,12},{5,13},{6,14},{7,15},{8,0},{9,1},... | collective-permute-start | bytes 4423688 | tf_op jit(solution)/shard_map/ppermute | solution.py:611
  361.0 5.3 %collective-permute-start.26 = (bf16[2,2,4,4,24,384]{5,4,3,2,1,0:T(8,128)(2,1)}, bf16[2,2,4,4,24,384]{5,4,3,2,1,0:T(8,128)(2,1)}, u32[]{:S(2)}, u32[]{:S(2)}) collective-permute-start(bf16[2,2,4,4,24,384]{5,4,3,2,1,0:T(8,128)(2,1)} %get-tuple-element.159), channel_id=1, source_target_pairs={{0,8},{1,9},{2,10},{3,11},{4,12},{5,13},{6,14},{7,15},{8,0},{9,1},... | collective-permute-start | bytes 3538952 | tf_op jit(solution)/shard_map/ppermute | solution.py:611
  361.5 37.1 %all-to-all-start.2 = ((bf16[4,8,24,768]{3,2,1,0:T(8,128)(2,1)}), bf16[4,8,24,768]{3,2,1,0:T(8,128)(2,1)S(1)}, u32[]{:S(2)}, u32[]{:S(2)}) async-start(bf16[4,8,24,768]{3,2,1,0:T(8,128)(2,1)} %pad_maximum_fusion.2), calls=%async_computation.2 | async-start | bytes 2359296 | tf_op jit(solution)/shard_map/all_to_all | solution.py:615
  366.3 3.6 copy-start.5
  368.3 15.1 %collective-permute-start.29 = (bf16[2,4,4,24,384]{4,3,2,1,0:T(8,128)(2,1)S(1)}, bf16[2,4,4,24,384]{4,3,2,1,0:T(8,128)(2,1)S(1)}, u32[]{:S(2)}, u32[]{:S(2)}) collective-permute-start(bf16[2,4,4,24,384]{4,3,2,1,0:T(8,128)(2,1)S(1)} %get-tuple-element.170), channel_id=1, source_target_pairs={{0,16},{1,17},{2,18},{3,19},{4,20},{5,21},{6,22},{7,23},{8,24},{9,... | collective-permute-start | bytes 1769480 | tf_op jit(solution)/shard_map/ppermute | solution.py:611
  370.2 19.5 %collective-permute-start.27 = (bf16[2,4,5,24,384]{4,3,2,1,0:T(8,128)(2,1)S(1)}, bf16[2,4,5,24,384]{4,3,2,1,0:T(8,128)(2,1)S(1)}, u32[]{:S(2)}, u32[]{:S(2)}) collective-permute-start(bf16[2,4,5,24,384]{4,3,2,1,0:T(8,128)(2,1)S(1)} %get-tuple-element.168), channel_id=1, source_target_pairs={{0,1},{1,0},{2,3},{3,2},{4,5},{5,4},{6,7},{7,6},{8,9},{9,8},{10,11... | collective-permute-start | bytes 2211848 | tf_op jit(solution)/shard_map/ppermute | solution.py:611
  383.5 11.0 %collective-permute-start.30 = (bf16[4,4,24,384]{3,2,1,0:T(8,128)(2,1)S(1)}, bf16[4,4,24,384]{3,2,1,0:T(8,128)(2,1)S(1)}, u32[]{:S(2)}, u32[]{:S(2)}) collective-permute-start(bf16[4,4,24,384]{3,2,1,0:T(8,128)(2,1)S(1)} %get-tuple-element.178), channel_id=1, source_target_pairs={{0,1},{1,0},{2,3},{3,2},{4,5},{5,4},{6,7},{7,6},{8,9},{9,8},{10,11... | collective-permute-start | bytes 884744 | tf_op jit(solution)/shard_map/ppermute | solution.py:611
  389.9 7.6 %collective-permute-start.28 = (bf16[4,5,24,384]{3,2,1,0:T(8,128)(2,1)S(1)}, bf16[4,5,24,384]{3,2,1,0:T(8,128)(2,1)S(1)}, u32[]{:S(2)}, u32[]{:S(2)}) collective-permute-start(bf16[4,5,24,384]{3,2,1,0:T(8,128)(2,1)S(1)} %get-tuple-element.176), channel_id=1, source_target_pairs={{0,16},{1,17},{2,18},{3,19},{4,20},{5,21},{6,22},{7,23},{8,24},{9,... | collective-permute-start | bytes 1105928 | tf_op jit(solution)/shard_map/ppermute | solution.py:611
  398.6 18.3 %all-to-all-start.1 = ((bf16[4,9,24,384]{3,2,1,0:T(8,128)(2,1)}), bf16[4,9,24,384]{3,2,1,0:T(8,128)(2,1)S(1)}, u32[]{:S(2)}, u32[]{:S(2)}) async-start(bf16[4,9,24,384]{3,2,1,0:T(8,128)(2,1)} %pad_maximum_fusion.5), calls=%async_computation.1 | async-start | bytes 1327104 | tf_op jit(solution)/shard_map/all_to_all | solution.py:615

commit v8 on v7

--- a/solution.py
+++ b/solution.py
@@ -54,21 +54,31 @@
     return jnp.sum(v, axis=0, keepdims=True)
 
 
-def qkv_body(x_ref, w_ref, vec_ref, o_ref):
+def qkv_body(x_ref, a_ref, b_ref, vec_ref, o_ref):
     part = pl.program_id(0)
-    acc = mm(x_ref[...], w_ref[0], NN)
-    bias = jnp.where(part == 0, vec_ref[BQ : BQ + 1, :], jnp.where(part == 2, vec_ref[BV : BV + 1, :], 0.0))
-    o_ref[...] = (acc + bias).astype(BF)
-
-
-def qkv_call(x, w, vec):
+
+    @pl.when(part == 0)
+    def _():
+        o_ref[...] = (mm(x_ref[...], a_ref[0], NN) + vec_ref[BQ : BQ + 1, :]).astype(BF)
+
+    @pl.when(part == 1)
+    def _():
+        o_ref[...] = mm(x_ref[...], a_ref[0], NN).astype(BF)
+
+    @pl.when(part == 2)
+    def _():
+        o_ref[...] = (mm(x_ref[...], b_ref[0], NN) + vec_ref[BV : BV + 1, :]).astype(BF)
+
+
+def qkv_call(x, first, vec):
     rows = x.shape[0]
     return pl.pallas_call(
         qkv_body,
         grid=(3,),
         in_specs=[
             once((rows, D), lambda i: (0, 0)),
-            pl.BlockSpec((1, D, D), lambda i: (i, 0, 0)),
+            pl.BlockSpec((1, D, D), lambda i: (jnp.minimum(i, 1), 0, 0)),
+            once((1, D, D), lambda i: (0, 0, 0)),
             once(vec.shape, lambda i: (0, 0)),
         ],
         out_specs=pl.BlockSpec((rows, D), lambda i: (0, i)),
@@ -76,7 +86,7 @@
         compiler_params=params(),
         cost_estimate=cost(8),
         name="qkv",
-    )(x, w, vec)
+    )(x, *first, vec)
 
 
 def attend_body(seq, pairs, len_ref, q_ref, k_ref, v_ref, o_ref, l_ref):
@@ -163,7 +173,7 @@
 ):
     step = pl.program_id(0)
     copies = [
-        pltpu.make_async_copy(wo_h.at[3], wo_s, sems.at[0]),
+        pltpu.make_async_copy(wo_h.at[1], wo_s, sems.at[0]),
         pltpu.make_async_copy(wi_h, wi_s, sems.at[1]),
         pltpu.make_async_copy(wb_h, wb_s, sems.at[2]),
     ]
@@ -241,7 +251,7 @@
         compiler_params=params(),
         cost_estimate=cost(22),
         name="ffn",
-    )(x, ctx, vec, first, wi, wb)
+    )(x, ctx, vec, first[1], wi, wb)
 
 
 def ffn_back_body(
@@ -252,7 +262,7 @@
     copies = [
         pltpu.make_async_copy(wb_h, wb_s, sems.at[0]),
         pltpu.make_async_copy(wi_h, wi_s, sems.at[1]),
-        pltpu.make_async_copy(wo_h.at[3], wo_s, sems.at[2]),
+        pltpu.make_async_copy(wo_h.at[1], wo_s, sems.at[2]),
     ]
 
     @pl.when(step == 0)
@@ -323,7 +333,7 @@
         compiler_params=params(),
         cost_estimate=cost(24),
         name="ffn_back",
-    )(dy, z2, z1, slope, vec, wb, wi, first)
+    )(dy, z2, z1, slope, vec, wb, wi, first[1])
 
 
 def attend_back_body(seq, pairs, len_ref, q_ref, k_ref, v_ref, d_ref, l_ref, e_ref, bq_ref, bv_ref):
@@ -405,13 +415,14 @@
 
 
 def dx_body(dz1_ref, *rest):
-    e_refs, w_ref, o_ref = rest[:-2], rest[-2], rest[-1]
+    e_refs, (a_ref, b_ref, o_ref) = rest[:-3], rest[-3:]
     acc = dz1_ref[...]
     for i in range(3):
         at = 0
         for e_ref in e_refs:
             width = e_ref.shape[2]
-            acc += mm(e_ref[i], w_ref[i, :, at : at + width], NT)
+            w = a_ref[i, :, at : at + width] if i < 2 else b_ref[0, :, at : at + width]
+            acc += mm(e_ref[i], w, NT)
             at += width
     o_ref[...] = acc.astype(o_ref.dtype)
 
@@ -423,13 +434,13 @@
     return pl.pallas_call(
         dx_body,
         grid=(rows // block,),
-        in_specs=[line, *specs, once((3, D, D), lambda i: (0, 0, 0))],
+        in_specs=[line, *specs, once((2, D, D), lambda i: (0, 0, 0)), once((1, D, D), lambda i: (0, 0, 0))],
         out_specs=line,
         out_shape=jax.ShapeDtypeStruct((rows, D), dtype),
         compiler_params=params(),
         cost_estimate=cost(9),
         name="dx",
-    )(dz1, *parts, w)
+    )(dz1, *parts, *w)
 
 
 def deal(acc_s, rows, x_first, core_ref, keep_ref, send_ref):
@@ -618,42 +629,37 @@
 X, CORE, Z, Y = range(4)
 
 
-def pack_one_body(at_ref, wq_ref, wo_ref, *rest):
+def pack_one_body(wq_ref, wo_ref, *rest):
     vectors, span_ref, one_ref, line_s = rest[:8], rest[8], rest[9], rest[10]
     rows = wq_ref.shape[0]
-    for i in range(3):
-        one_ref[i] = wq_ref[:, i * D : (i + 1) * D]
-    one_ref[3] = wo_ref[...]
+    groups = rows // 8
+    for i in range(4):
+        for g in range(groups):
+            lines = slice(8 * g, 8 * g + 8)
+            one_ref[i * groups + g] = wo_ref[lines, :] if i == 3 else wq_ref[lines, i * D : (i + 1) * D]
     line_s[...] = jnp.zeros_like(line_s)
     for i, ref in enumerate(vectors):
         line_s[i : i + 1, :rows] = ref[...].astype(F32)
-    span = span_ref.shape[1]
-    line_s[8:9, :span] = span_ref[...].astype(F32)
-    device = at_ref[0]
-    per = D // span
-    top = pltpu.roll(line_s[:8], device * rows, 1)
-    low = pltpu.roll(line_s[8:16], lax.rem(device, per) * span, 1)
-    here = lax.broadcasted_iota(jnp.int32, (8, D), 0) == lax.div(device, per)
-    low = jnp.where(here, jnp.broadcast_to(low[:1], (8, D)), 0.0)
-    one_ref[4] = jnp.concatenate([top, low, jnp.zeros((rows - 16, D), F32)], axis=0).astype(BF)
-
-
-def pack_one(device, w_qkv, w_out, vectors, span):
-    rows = w_qkv.shape[0]
+    line_s[0:1, SHARE : SHARE + span_ref.shape[1]] = span_ref[...].astype(F32)
+    one_ref[4 * groups] = line_s[...].astype(BF)
+
+
+SHARE = 128
+
+
+def pack_one(w_qkv, w_out, vectors, span):
+    groups = 4 * w_qkv.shape[0] // 8 + 1
     operands = [w_qkv, w_out, *[v[None] for v in vectors], span[None]]
     return pl.pallas_call(
         pack_one_body,
-        grid_spec=pltpu.PrefetchScalarGridSpec(
-            num_scalar_prefetch=1,
-            grid=(1,),
-            in_specs=[whole_block(v) for v in operands],
-            out_specs=pl.BlockSpec((5, rows, D), lambda *_: (0, 0, 0)),
-            scratch_shapes=[pltpu.VMEM((16, D), F32)],
-        ),
-        out_shape=jax.ShapeDtypeStruct((5, rows, D), BF),
+        grid=(1,),
+        in_specs=[whole_block(v) for v in operands],
+        out_specs=pl.BlockSpec((groups, 8, D), lambda *_: (0, 0, 0)),
+        out_shape=jax.ShapeDtypeStruct((groups, 8, D), BF),
+        scratch_shapes=[pltpu.VMEM((8, D), F32)],
         compiler_params=params(),
         name="pack_one",
-    )(device, *operands)
+    )(*operands)
 
 
 def pack_two_body(wi_ref, wb_ref, two_ref):
@@ -677,25 +683,30 @@
 
 
 def place_body(split, at_ref, *refs):
-    outs = 2 if split else 1
+    outs = 2 if split else 3
     parts, outs, held, sems, out_sems = refs[:8], refs[8 : 8 + outs], refs[8 + outs : -2], refs[-2], refs[-1]
     x, core, z, y = at_ref[0], at_ref[1], at_ref[2], at_ref[3]
     sides = ([], [])
     for i, part in enumerate(parts):
         side, far, other = i >> 2, (i >> 1) & 1, i & 1
-        count = part.shape[2]
         for near in range(2):
             px = (x + (far if side == 0 else near)) % 2
             py = (y + (near if side == 0 else far)) % 2
             pc = (core + other) % 2
             for dz in range(4):
                 pz = dz if split else (z + 4 - dz) % 4
-                if split:
-                    target = held[side].at[:, px, pc, pz, py] if side == 0 else held[side].at[px, pc, pz, py]
+                source = part.at[near, dz]
+                if side == 0:
+                    pairs = [(source, held[0].at[:, px, pc, pz, py])]
+                elif split:
+                    pairs = [(source, held[1].at[px, pc, pz, py])]
                 else:
-                    target = held[0].at[pl.ds(0 if side == 0 else 5 - count, count), px, pc, pz, py]
-                sem = sems.at[i * 8 + near * 4 + dz]
-                sides[side].append(pltpu.make_async_copy(part.at[near, dz], target, sem))
+                    count = held[1].shape[5]
+                    pairs = [(source.at[pl.ds(u * count, count)], held[1].at[u, px, pc, pz, py]) for u in range(2)]
+                    pairs.append((source.at[2 * count], held[2].at[px, pc, pz, py]))
+                for pair in pairs:
+                    at = len(sides[0]) + len(sides[1])
+                    sides[side].append(pltpu.make_async_copy(*pair, sems.at[at]))
     for side in sides:
         for copy in side:
             copy.start()
@@ -703,35 +714,48 @@
     for side in range(2):
         for copy in sides[side]:
             copy.wait()
-        if split:
-            pair = held[side], outs[side]
-        else:
-            count = parts[4 * side].shape[2]
-            span = pl.ds(0 if side == 0 else 5 - count, count)
-            pair = held[0].at[span], outs[0].at[span]
-        back.append(pltpu.make_async_copy(*pair, out_sems.at[side]))
+        back.append(pltpu.make_async_copy(held[side], outs[side], out_sems.at[side]))
         back[-1].start()
+    if not split:
+        shares, vec_ref, rows = held[2], outs[2], D // 32
+        span = 4 * rows
+        lines = lax.broadcasted_iota(jnp.int32, (8, D), 0)
+        lane = lax.broadcasted_iota(jnp.int32, (8, D), 1)
+        top, low = jnp.zeros((8, D), F32), jnp.zeros((8, D), F32)
+        for i in range(32):
+            share = shares[i // 16, i // 8 % 2, i // 2 % 4, i % 2].astype(F32)
+            top += pltpu.roll(jnp.where(lane < rows, share, 0.0), i * rows, 1)
+            wide = jnp.where((lane >= SHARE) & (lane < SHARE + span), share, 0.0)
+            wide = pltpu.roll(wide, (i % 8 * span - SHARE) % D, 1)
+            low += jnp.where(lines == i // 8, jnp.broadcast_to(wide[:1], (8, D)), 0.0)
+        vec_ref[...] = jnp.concatenate([top, low, jnp.zeros((8, D), F32)], axis=0)
     for copy in back:
         copy.wait()
 
 
 def place(at, parts, split):
-    rows = parts[0].shape[3]
+    rows = parts[0].shape[-2]
     if split:
         shapes = [(4, 2, 2, 4, 2, rows, D), (2, 2, 4, 2, 4, rows, D)]
     else:
-        shapes = [(5, 2, 2, 4, 2, rows, D)]
+        shapes = [(2, 2, 2, 4, 2, rows, D), (2, 2, 2, 4, 2, rows // 8, 8, D)]
+    held = [pltpu.VMEM(shape, BF) for shape in shapes]
+    out_specs = [ANY, ANY]
+    out_shape = [jax.ShapeDtypeStruct(shape, BF) for shape in shapes]
+    if not split:
+        held.append(pltpu.VMEM((2, 2, 4, 2, 8, D), BF))
+        out_specs.append(pl.BlockSpec((24, D), lambda *_: (0, 0)))
+        out_shape.append(jax.ShapeDtypeStruct((24, D), F32))
     return pl.pallas_call(
         lambda *refs: place_body(split, *refs),
         grid_spec=pltpu.PrefetchScalarGridSpec(
             num_scalar_prefetch=1,
             grid=(1,),
             in_specs=[ANY] * 8,
-            out_specs=[ANY] * len(shapes),
-            scratch_shapes=[pltpu.VMEM(shape, BF) for shape in shapes]
-            + [pltpu.SemaphoreType.DMA((64,)), pltpu.SemaphoreType.DMA((2,))],
+            out_specs=out_specs,
+            scratch_shapes=held + [pltpu.SemaphoreType.DMA((64 if split else 128,)), pltpu.SemaphoreType.DMA((2,))],
         ),
-        out_shape=[jax.ShapeDtypeStruct(shape, BF) for shape in shapes],
+        out_shape=out_shape,
         compiler_params=params(),
         cost_estimate=cost(6),
         name="place",
@@ -753,6 +777,8 @@
     def one(self, *others):
         ring = after(self.ring, *others)
         self.line = [ring[:, : self.first], ring[:, self.first :]]
+        if ring.shape[2] == 8:
+            self.line[0] = self.line[0].reshape(4, 2, -1, D)
         self.came = [self.grid.send(v, d) for v, d in zip(self.line, (Y, X))]
 
     def two(self, *others):
@@ -816,17 +842,16 @@
     at = jnp.stack([x, core, z, y]).astype(jnp.int32)
     core = core.astype(jnp.int32)[None]
     vectors = [bias_q, bias_v, bias_out, gain_one, shift_one, bias_back, gain_two, shift_two]
-    one = Gather(grid, pack_one(device.astype(jnp.int32)[None], w_qkv, w_out, vectors, bias_in), 2, False)
+    one = Gather(grid, pack_one(w_qkv, w_out, vectors, bias_in), 2 * rows // 8, False)
     packet = after(pack_two(w_in, w_back), one.ring)
     two = Gather(grid, packet, 4, True)
     one.one()
     one.two()
     two.one(*one.far)
-    (first,) = place(at, one.parts(), False)
-    first = first.reshape(5, grid.count * rows, D)
-    vec = jnp.sum(first[4].reshape(grid.count, rows, D).astype(F32), axis=0)
+    w_a, w_b, vec = place(at, one.parts(), False)
+    first = (w_a.reshape(2, grid.count * rows, D), w_b.reshape(2, grid.count * rows, D))
     qkv = qkv_call(tokens, first, vec)
-    two.two(first)
+    two.two(vec)
     ctx, lse = attend_call(after(qkv, *two.near), lengths)
     w_in, w_back = place(at, two.parts(ctx), True)
     w_in = w_in.reshape(4, grid.count * rows, D)
@@ -894,7 +919,8 @@
     def blocks(w):
         return w.reshape(D, -1, D).swapaxes(0, 1)
 
-    first = jnp.concatenate([blocks(whole(w_qkv)), whole(w_out)[None], jnp.zeros((1, D, D), BF)], axis=0)
+    first = jnp.concatenate([blocks(whole(w_qkv)), whole(w_out)[None]], axis=0)
+    first = (first[:2], first[2:])
     w_in, w_back = blocks(whole(w_in)), whole(w_back)
     weights = (first, w_in, w_back, vec)
     value, low = tokens, tokens

time: 427 us -> 420 us (0.984)
    ppermute x31, waiting for transfers between devices: 65.3 us -> 57.9 us  [send(): return lax.ppermute(value, AXES, self.shift(dim, step))]
  transfers between devices with their start and end apart: 34 -> 34, of which waited for: 16 -> 17; matrix products, arithmetic and copies ran while one was open for 5% -> 4% of each run, Pallas kernels for 20% -> 21%
where the time goes in v8:
time: 420 us; the launch traced here: 412 us
  Pallas kernels  269 us (64%)
  waiting for transfers between devices  73.1 us (17%)
  starting transfers between devices  44.2 us (11%)
  other arithmetic  17.6 us (4%)
  local copies, waits for them, and re-layouts  6.6 us (2%)
    ppermute x31, waiting for transfers between devices, send(): return lax.ppermute(value, AXES, self.shift(dim, step))  57.9 us
    pallas_call x2, Pallas kernels, ffn_back_call(): pl.pallas_call(ffn_back_body, grid=(rows // block,), in_specs=[line, line...  47.6 us
    pallas_call x3, Pallas kernels, attend_back_call(): pl.pallas_call(body, grid_spec=pltpu.PrefetchScalarGridSpec(num_scalar_pr...  46.6 us
    pallas_call x2, Pallas kernels, ffn_call(): pl.pallas_call(lambda *refs: ffn_body(renorm, *refs), grid=(rows // block...  44.7 us
    ppermute x31, starting transfers between devices, send(): return lax.ppermute(value, AXES, self.shift(dim, step))  30 us
    pallas_call x2, Pallas kernels, attend_call(): pl.pallas_call(body, grid_spec=pltpu.PrefetchScalarGridSpec(num_scalar_pr...  24.8 us
    pallas_call x2, Pallas kernels, wgrad_heads_call(): pl.pallas_call(body, grid_spec=pltpu.PrefetchScalarGridSpec(num_scalar_pr...  24.1 us
    pallas_call x2, Pallas kernels, dx_call(): pl.pallas_call(dx_body, grid=(rows // block,), in_specs=[line, *specs, on...  18 us
  transfers between devices with their start and end apart: 34, of which 17 were waited for; matrix products, arithmetic and copies ran while one was open for 4% of the time, Pallas kernels for 21%

profile of v8, /device:TPU:0, one launch (start us, length us, event | category | flops | bytes accessed | tf_op | source)
XLA Modules:
  0.0 412.2 jit_solution(13020637530503995110)
XLA Ops:
  0.7 1.7 pack_one.1
  2.3 3.0 collective-permute-start
  5.4 2.6 collective-permute-start.1
  7.9 1.3 collective-permute-start.2
  9.3 1.7 pack_two.1
  11.0 1.6 collective-permute-done
  12.6 6.0 %collective-permute-done.1 = bf16[13,8,768]{2,1,0:T(8,128)(2,1)S(1)} collective-permute-done((bf16[13,8,768]{2,1,0:T(8,128)(2,1)}, bf16[13,8,768]{2,1,0:T(8,128)(2,1)S(1)}, u32[]{:S(2)}, u32[]{:S(2)}) %collective-permute-start.1) | collective-permute-done | bytes 159776 | tf_op jit(solution)/shard_map/ppermute | solution.py:622
  18.6 1.0 pad_maximum_fusion.5
  19.7 1.1 broadcast_in_dim.40
  20.7 6.2 %all-to-all-start = ((bf16[4,8,24,768]{3,2,1,0:T(8,128)(2,1)}), bf16[4,8,24,768]{3,2,1,0:T(8,128)(2,1)S(1)}, u32[]{:S(2)}, u32[]{:S(2)}) async-start(bf16[4,8,24,768]{3,2,1,0:T(8,128)(2,1)} %broadcast_in_dim.40), calls=%async_computation | async-start | bytes 2359296 | tf_op jit(solution)/shard_map/all_to_all | solution.py:626
  27.0 1.6 collective-permute-start.6
  28.6 1.6 collective-permute-start.3
  30.2 5.6 %collective-permute-done.6 = bf16[4,7,8,768]{3,2,1,0:T(8,128)(2,1)S(1)} collective-permute-done((bf16[4,7,8,768]{3,2,1,0:T(8,128)(2,1)S(1)}, bf16[4,7,8,768]{3,2,1,0:T(8,128)(2,1)S(1)}, u32[]{:S(2)}, u32[]{:S(2)}) %collective-permute-start.6) | collective-permute-done | bytes 344096 | tf_op jit(solution)/shard_map/ppermute | solution.py:622
  35.8 1.6 collective-permute-start.7
  37.5 1.6 collective-permute-start.5
  39.5 10.8 %collective-permute-done.5.refs_3_ = bf16[2,4,2,24,768]{4,3,2,1,0:T(8,128)(2,1)} collective-permute-done((bf16[2,4,2,24,768]{4,3,2,1,0:T(8,128)(2,1)S(1)}, bf16[2,4,2,24,768]{4,3,2,1,0:T(8,128)(2,1)}, u32[]{:S(2)}, u32[]{:S(2)}) %collective-permute-start.5) | collective-permute-done | bytes 589856 | tf_op jit(solution)/shard_map/ppermute | solution.py:622
  51.6 3.1 all-to-all-done
  54.6 0.9 fusion.17
  55.5 1.5 collective-permute-start.12
  57.0 1.5 collective-permute-start.11
  59.2 6.4 %place.2 = (bf16[2,2,2,4,2,24,768]{6,5,4,3,2,1,0:T(8,128)(2,1)}, bf16[2,2,2,4,2,3,8,768]{7,6,5,4,3,2,1,0:T(8,128)(2,1)}, f32[24,768]{1,0:T(8,128)}) custom-call(s32[4]{0:T(128)} %pad_add_fusion.refs_0_, bf16[2,4,2,24,768]{4,3,2,1,0:T(8,128)(2,1)} %copy-done.3, bf16[2,4,2,24,768]{4,3,2,1,0:T(8,128)(2,1)} %collective-permute-done.4.refs_2_, ...), custom_call_target="tpu_custom_call" | custom-call | flops 1200000000 | bytes 600000 | tf_op jit(solution)/shard_map/place/pallas_call | solution.py:749
  65.6 4.5 %collective-permute-done.12 = bf16[4,4,24,768]{3,2,1,0:T(8,128)(2,1)S(1)} collective-permute-done((bf16[4,4,24,768]{3,2,1,0:T(8,128)(2,1)}, bf16[4,4,24,768]{3,2,1,0:T(8,128)(2,1)S(1)}, u32[]{:S(2)}, u32[]{:S(2)}) %collective-permute-start.12) | collective-permute-done | bytes 589856 | tf_op jit(solution)/shard_map/ppermute | solution.py:622
  70.0 1.2 pad_maximum_fusion.1.refs_5_
  71.2 1.6 collective-permute-start.15
  72.9 1.6 collective-permute-start.14
  74.5 7.7 %qkv.2.refs_1_.refs_2_.refs_3_ = bf16[1024,2304]{1,0:T(8,128)(2,1)} custom-call(bf16[1024,768]{1,0:T(8,128)(2,1)} %c_ref.3, bf16[2,768,768]{2,1,0:T(8,128)(2,1)} %bitcast.115, bf16[2,768,768]{2,1,0:T(8,128)(2,1)} %bitcast.99, f32[24,768]{1,0:T(8,128)} %get-tuple-element.98.vec_ref.refs_2_), custom_call_target="tpu_custom_call" | custom-call | flops 1600000000 | bytes 800000 | tf_op jit(solution)/shard_map/qkv/pallas_call | solution.py:75
  82.7 12.3 %attend.2 = (bf16[1024,768]{1,0:T(8,128)(2,1)}, f32[2,6,2,512]{3,2,1,0:T(2,128)}) custom-call(s32[2]{0:T(128)} %refs_0_.11, bf16[1024,2304]{1,0:T(8,128)(2,1)} %qkv.2.refs_1_.refs_2_.refs_3_, bf16[1024,2304]{1,0:T(8,128)(2,1)} %qkv.2.refs_1_.refs_2_.refs_3_, bf16[1024,2304]{1,0:T(8,128)(2,1)} %qkv.2.refs_1_.refs_2_.refs_3_), custom_call_target="tpu_custom_call" | custom-call | flops 2600000000 | bytes 1300000 | tf_op jit(solution)/shard_map/attend/pallas_call | solution.py:137
  94.9 2.4 collective-permute-done.15.refs_7_
  97.3 1.4 collective-permute-done.14.refs_3_
  99.3 4.0 collective-permute-done.16.refs_4_
  104.3 8.2 %place.3 = (bf16[4,2,2,4,2,24,768]{6,5,4,3,2,1,0:T(8,128)(2,1)}, bf16[2,2,4,2,4,24,768]{6,5,4,3,2,1,0:T(8,128)(2,1)}) custom-call(s32[4]{0:T(128)} %pad_add_fusion.refs_0_, bf16[2,4,4,24,768]{4,3,2,1,0:T(8,128)(2,1)} %copy-done.1, bf16[2,4,4,24,768]{4,3,2,1,0:T(8,128)(2,1)} %copy-done.9, bf16[2,4,4,24,768]{4,3,2,1,0:T(8,128)(2,1)} %copy-done.7, ...), custom_call_target="tpu_custom_call" | custom-call | flops 1200000000 | bytes 600000 | tf_op jit(solution)/shard_map/place/pallas_call | solution.py:749
  112.5 22.2 %ffn.2 = (f32[1024,768]{1,0:T(8,128)}, bf16[1024,768]{1,0:T(8,128)(2,1)}, bf16[1024,3072]{1,0:T(8,128)(2,1)}, bf16[1024,3072]{1,0:T(8,128)(2,1)}, f32[1024,768]{1,0:T(8,128)}, /*index=5*/bf16[1024,768]{1,0:T(8,128)(2,1)}) custom-call(bf16[1024,768]{1,0:T(8,128)(2,1)} %c_ref.3, bf16[1024,768]{1,0:T(8,128)(2,1)} %get-tuple-element.104.refs_1_.rest_1_, ...), custom_call_target="tpu_custom_call" | custom-call | flops 4400000000 | bytes 2200000 | tf_op jit(solution)/shard_map/ffn/pallas_call | solution.py:237
  134.7 7.7 %qkv.3.refs_1_.refs_2_.refs_3_ = bf16[1024,2304]{1,0:T(8,128)(2,1)} custom-call(bf16[1024,768]{1,0:T(8,128)(2,1)} %get-tuple-element.152.x_ref.a_ref, bf16[2,768,768]{2,1,0:T(8,128)(2,1)} %bitcast.116, bf16[2,768,768]{2,1,0:T(8,128)(2,1)} %bitcast.101, f32[24,768]{1,0:T(8,128)} %get-tuple-element.98.vec_ref.refs_2_), custom_call_target="tpu_custom_call" | custom-call | flops 1600000000 | bytes 800000 | tf_op jit(solution)/shard_map/qkv/pallas_call | solution.py:75
  142.4 12.5 %attend.3 = (bf16[1024,768]{1,0:T(8,128)(2,1)}, f32[2,6,2,512]{3,2,1,0:T(2,128)}) custom-call(s32[2]{0:T(128)} %refs_0_.11, bf16[1024,2304]{1,0:T(8,128)(2,1)} %qkv.3.refs_1_.refs_2_.refs_3_, bf16[1024,2304]{1,0:T(8,128)(2,1)} %qkv.3.refs_1_.refs_2_.refs_3_, bf16[1024,2304]{1,0:T(8,128)(2,1)} %qkv.3.refs_1_.refs_2_.refs_3_), custom_call_target="tpu_custom_call" | custom-call | flops 2600000000 | bytes 1300000 | tf_op jit(solution)/shard_map/attend/pallas_call | solution.py:137
  155.0 22.5 %ffn.3 = (f32[1024,768]{1,0:T(8,128)}, bf16[1024,768]{1,0:T(8,128)(2,1)}, bf16[1024,3072]{1,0:T(8,128)(2,1)}, bf16[1024,3072]{1,0:T(8,128)(2,1)}, f32[1024,768]{1,0:T(8,128)}, /*index=5*/bf16[1024,768]{1,0:T(8,128)(2,1)}) custom-call(f32[1024,768]{1,0:T(8,128)} %get-tuple-element.109.refs_0_.z2_ref, bf16[1024,768]{1,0:T(8,128)(2,1)} %get-tuple-element.111.refs_1_.rest_0_, ...), custom_call_target="tpu_custom_call" | custom-call | flops 4400000000 | bytes 2200000 | tf_op jit(solution)/shard_map/ffn/pallas_call | solution.py:237
  177.4 23.8 %ffn_back.2 = (bf16[1024,768]{1,0:T(8,128)(2,1)}, bf16[1024,3072]{1,0:T(8,128)(2,1)}, f32[1024,768]{1,0:T(8,128)}, bf16[1024,768]{1,0:T(8,128)(2,1)}, bf16[1024,768]{1,0:T(8,128)(2,1)}, /*index=5*/f32[24,768]{1,0:T(8,128)}) custom-call(bf16[1024,768]{1,0:T(8,128)(2,1)} %dy_ref.1, f32[1024,768]{1,0:T(8,128)} %get-tuple-element.113.z2_ref, ...), custom_call_target="tpu_custom_call" | custom-call | flops 4800000000 | bytes 2400000 | tf_op jit(solution)/shard_map/ffn_back/pallas_call | solution.py:319
  201.2 21.7 %attend_back.3 = (bf16[3,1024,768]{2,1,0:T(8,128)(2,1)}, f32[2,1,768]{2,1,0:T(1,128)}, f32[2,1,768]{2,1,0:T(1,128)}) custom-call(s32[2]{0:T(128)} %refs_0_.11, bf16[1024,2304]{1,0:T(8,128)(2,1)} %qkv.3.refs_1_.refs_2_.refs_3_, bf16[1024,2304]{1,0:T(8,128)(2,1)} %qkv.3.refs_1_.refs_2_.refs_3_, bf16[1024,2304]{1,0:T(8,128)(2,1)} %qkv.3.refs_1_.refs_2_.refs_3_, ...), custom_call_target="tpu_custom_call" | custom-call | flops 4800000000 | bytes 2400000 | tf_op jit(solution)/shard_map/attend_back/pallas_call | solution.py:395
  223.0 8.8 %dx.2.dy_ref = f32[1024,768]{1,0:T(8,128)} custom-call(f32[1024,768]{1,0:T(8,128)} %get-tuple-element.116.dz1_ref, bf16[3,1024,768]{2,1,0:T(8,128)(2,1)} %get-tuple-element.119.rest_0_.b_ref, bf16[2,768,768]{2,1,0:T(8,128)(2,1)} %bitcast.117, bf16[2,768,768]{2,1,0:T(8,128)(2,1)} %bitcast.104), custom_call_target="tpu_custom_call" | custom-call | flops 1800000000 | bytes 900000 | tf_op jit(solution)/shard_map/dx/pallas_call | solution.py:434
  231.8 23.9 %ffn_back.3 = (bf16[1024,768]{1,0:T(8,128)(2,1)}, bf16[1024,3072]{1,0:T(8,128)(2,1)}, f32[1024,768]{1,0:T(8,128)}, bf16[1024,768]{1,0:T(8,128)(2,1)}, bf16[1024,768]{1,0:T(8,128)(2,1)}, /*index=5*/f32[24,768]{1,0:T(8,128)}) custom-call(f32[1024,768]{1,0:T(8,128)} %dx.2.dy_ref, f32[1024,768]{1,0:T(8,128)} %get-tuple-element.109.refs_0_.z2_ref, ...), custom_call_target="tpu_custom_call" | custom-call | flops 4800000000 | bytes 2400000 | tf_op jit(solution)/shard_map/ffn_back/pallas_call | solution.py:319
  255.7 15.0 %wgrad_back.1 = (bf16[2,2,4,4,24,768]{5,4,3,2,1,0:T(8,128)(2,1)}, bf16[2,2,4,4,24,768]{5,4,3,2,1,0:T(8,128)(2,1)}) custom-call(s32[1]{0:T(128)} %bitcast.1.core_ref, bf16[1024,3072]{1,0:T(8,128)(2,1)} %get-tuple-element.123.g2k.g2s, bf16[1024,3072]{1,0:T(8,128)(2,1)} %get-tuple-element.124.g1k.g1s, bf16[1024,3072]{1,0:T(8,128)(2,1)} %get-tuple-element.123.g2k.g2s, ...), custom_call_target="tpu_custom_call" | custom-call | flops 3000000000 | bytes 1500000 | tf_op jit(solution)/shard_map/wgrad_back/pallas_call | solution.py:576
  270.6 15.1 %wgrad_in.1 = (bf16[2,2,4,4,24,768]{5,4,3,2,1,0:T(8,128)(2,1)}, bf16[2,2,4,4,24,768]{5,4,3,2,1,0:T(8,128)(2,1)}) custom-call(s32[1]{0:T(128)} %bitcast.1.core_ref, bf16[1024,768]{1,0:T(8,128)(2,1)} %get-tuple-element.129.a_ref, bf16[1024,768]{1,0:T(8,128)(2,1)} %get-tuple-element.130.c_ref, bf16[1024,3072]{1,0:T(8,128)(2,1)} %get-tuple-element.131.b_ref, ...), custom_call_target="tpu_custom_call" | custom-call | flops 3000000000 | bytes 1500000 | tf_op jit(solution)/shard_map/wgrad_in/pallas_call | solution.py:475
  286.2 4.4 %collective-permute-done.20 = bf16[2,2,4,4,24,768]{5,4,3,2,1,0:T(8,128)(2,1)} collective-permute-done((bf16[2,2,4,4,24,768]{5,4,3,2,1,0:T(8,128)(2,1)}, bf16[2,2,4,4,24,768]{5,4,3,2,1,0:T(8,128)(2,1)}, u32[]{:S(2)}, u32[]{:S(2)}) %collective-permute-start.20) | collective-permute-done | bytes 2359328 | tf_op jit(solution)/shard_map/ppermute | solution.py:622
  290.6 4.2 %fusion.3 = (bf16[2,4,4,24,768]{4,3,2,1,0:T(8,128)(2,1)S(1)}, bf16[2,4,4,24,768]{4,3,2,1,0:T(8,128)(2,1)}) fusion(bf16[2,2,4,4,24,768]{5,4,3,2,1,0:T(8,128)(2,1)} %collective-permute-done.20, s32[]{:T(128)S(6)} %select_n.87, bf16[2,2,4,4,24,768]{5,4,3,2,1,0:T(8,128)(2,1)} %get-tuple-element.137, s32[]{:T(128)S(6)} %select_n.86), kind=kLoop, calls=%fused_computation.11 | loop fusion | flops 4718592 | bytes 7077896 | tf_op jit(solution)/shard_map/convert_element_type | solution.py:805
  294.8 1.5 collective-permute-start.22
  296.3 2.3 fusion
  299.2 12.5 %attend_back.4 = (bf16[3,1024,384]{2,1,0:T(8,128)(2,1)}, f32[2,1,384]{2,1,0:T(1,128)}, f32[2,1,384]{2,1,0:T(1,128)}) custom-call(s32[2]{0:T(128)} %refs_0_.11, bf16[1024,2304]{1,0:T(8,128)(2,1)} %qkv.2.refs_1_.refs_2_.refs_3_, bf16[1024,2304]{1,0:T(8,128)(2,1)} %qkv.2.refs_1_.refs_2_.refs_3_, bf16[1024,2304]{1,0:T(8,128)(2,1)} %qkv.2.refs_1_.refs_2_.refs_3_, ...), custom_call_target="tpu_custom_call" | custom-call | flops 2400000000 | bytes 1200000 | tf_op jit(solution)/shard_map/attend_back/pallas_call | solution.py:395
  311.7 12.3 %attend_back.5 = (bf16[3,1024,384]{2,1,0:T(8,128)(2,1)}, f32[2,1,384]{2,1,0:T(1,128)}, f32[2,1,384]{2,1,0:T(1,128)}) custom-call(s32[2]{0:T(128)} %refs_0_.11, bf16[1024,2304]{1,0:T(8,128)(2,1)} %qkv.2.refs_1_.refs_2_.refs_3_, bf16[1024,2304]{1,0:T(8,128)(2,1)} %qkv.2.refs_1_.refs_2_.refs_3_, bf16[1024,2304]{1,0:T(8,128)(2,1)} %qkv.2.refs_1_.refs_2_.refs_3_, ...), custom_call_target="tpu_custom_call" | custom-call | flops 2400000000 | bytes 1200000 | tf_op jit(solution)/shard_map/attend_back/pallas_call | solution.py:395
  324.1 1.5 fusion.9
  325.6 1.6 collective-permute-start.23
  328.1 14.8 %wgrad_heads.2 = (bf16[2,2,4,5,24,384]{5,4,3,2,1,0:T(8,128)(2,1)}, bf16[2,2,4,5,24,384]{5,4,3,2,1,0:T(8,128)(2,1)}) custom-call(s32[1]{0:T(128)} %bitcast.1.core_ref, bf16[1024,768]{1,0:T(8,128)(2,1)} %get-tuple-element.152.x_ref.a_ref, bf16[1024,768]{1,0:T(8,128)(2,1)} %c_ref.3, bf16[3,1024,768]{2,1,0:T(8,128)(2,1)} %get-tuple-element.119.rest_0_.b_ref, ...), custom_call_target="tpu_custom_call" | custom-call | flops 2400000000 | bytes 1200000 | tf_op jit(solution)/shard_map/wgrad_heads/pallas_call | solution.py:540
  343.2 1.2 pad_maximum_fusion.2
  344.3 9.3 %wgrad_heads.3 = (bf16[2,2,4,4,24,384]{5,4,3,2,1,0:T(8,128)(2,1)}, bf16[2,2,4,4,24,384]{5,4,3,2,1,0:T(8,128)(2,1)}) custom-call(s32[1]{0:T(128)} %bitcast.1.core_ref, bf16[1024,768]{1,0:T(8,128)(2,1)} %get-tuple-element.152.x_ref.a_ref, bf16[1024,768]{1,0:T(8,128)(2,1)} %c_ref.3, bf16[3,1024,768]{2,1,0:T(8,128)(2,1)} %get-tuple-element.119.rest_0_.b_ref, ...), custom_call_target="tpu_custom_call" | custom-call | flops 2400000000 | bytes 1200000 | tf_op jit(solution)/shard_map/wgrad_heads/pallas_call | solution.py:540
  354.1 3.5 all-to-all-start.2
  357.7 2.0 fusion.11
  359.7 1.6 collective-permute-start.29
  362.2 9.2 %dx.3 = bf16[1024,768]{1,0:T(8,128)(2,1)} custom-call(f32[1024,768]{1,0:T(8,128)} %get-tuple-element.166.dz1_ref, bf16[3,1024,384]{2,1,0:T(8,128)(2,1)} %get-tuple-element.141.d_ref.rest_0_, bf16[3,1024,384]{2,1,0:T(8,128)(2,1)} %get-tuple-element.143.d_ref.rest_1_, bf16[2,768,768]{2,1,0:T(8,128)(2,1)} %bitcast.118, bf16[2,768,768]{2,1,0:T(8,128)(2,1)} %bitcast.106), custom_call_target="tpu_custom_call" | custom-call | flops 1800000000 | bytes 900000 | tf_op jit(solution)/shard_map/dx/pallas_call | solution.py:434
  371.4 3.6 collective-permute-done.29
  375.8 5.3 %collective-permute-done.27 = bf16[2,4,5,24,384]{4,3,2,1,0:T(8,128)(2,1)S(1)} collective-permute-done((bf16[2,4,5,24,384]{4,3,2,1,0:T(8,128)(2,1)S(1)}, bf16[2,4,5,24,384]{4,3,2,1,0:T(8,128)(2,1)S(1)}, u32[]{:S(2)}, u32[]{:S(2)}) %collective-permute-start.27) | collective-permute-done | bytes 737312 | tf_op jit(solution)/shard_map/ppermute | solution.py:622
  381.9 4.3 %collective-permute-done.30 = bf16[4,4,24,384]{3,2,1,0:T(8,128)(2,1)S(1)} collective-permute-done((bf16[4,4,24,384]{3,2,1,0:T(8,128)(2,1)S(1)}, bf16[4,4,24,384]{3,2,1,0:T(8,128)(2,1)S(1)}, u32[]{:S(2)}, u32[]{:S(2)}) %collective-permute-start.30) | collective-permute-done | bytes 294944 | tf_op jit(solution)/shard_map/ppermute | solution.py:622
  386.2 3.2 collective-permute-done.28
  389.5 1.0 pad_maximum_fusion.4
  390.5 4.5 %all-to-all-start.1 = ((bf16[4,9,24,384]{3,2,1,0:T(8,128)(2,1)}), bf16[4,9,24,384]{3,2,1,0:T(8,128)(2,1)S(1)}, u32[]{:S(2)}, u32[]{:S(2)}) async-start(bf16[4,9,24,384]{3,2,1,0:T(8,128)(2,1)} %pad_maximum_fusion.4), calls=%async_computation.1 | async-start | bytes 1327104 | tf_op jit(solution)/shard_map/all_to_all | solution.py:626
  396.6 12.1 %all-to-all-done.1 = bf16[4,9,24,384]{3,2,1,0:T(8,128)(2,1)S(1)} async-done(((bf16[4,9,24,384]{3,2,1,0:T(8,128)(2,1)}), bf16[4,9,24,384]{3,2,1,0:T(8,128)(2,1)S(1)}, u32[]{:S(2)}, u32[]{:S(2)}) %all-to-all-start.1) | async-done | bytes 663584 | tf_op jit(solution)/shard_map/all_to_all | solution.py:626
  409.7 0.9 reshape.128
  (87 shorter events, 13.9 us)
Async XLA Ops:
  2.3 10.3 %collective-permute-start = (bf16[13,8,768]{2,1,0:T(8,128)(2,1)}, bf16[13,8,768]{2,1,0:T(8,128)(2,1)S(1)}, u32[]{:S(2)}, u32[]{:S(2)}) collective-permute-start(bf16[13,8,768]{2,1,0:T(8,128)(2,1)} %pack_one.1), channel_id=1, source_target_pairs={{0,2},{1,3},{2,4},{3,5},{4,6},{5,7},{6,0},{7,1},{8,10},{9,11},{10,... | collective-permute-start | bytes 479240 | tf_op jit(solution)/shard_map/ppermute | solution.py:622
  5.4 13.3 %collective-permute-start.1 = (bf16[13,8,768]{2,1,0:T(8,128)(2,1)}, bf16[13,8,768]{2,1,0:T(8,128)(2,1)S(1)}, u32[]{:S(2)}, u32[]{:S(2)}) collective-permute-start(bf16[13,8,768]{2,1,0:T(8,128)(2,1)} %pack_one.1), channel_id=1, source_target_pairs={{0,4},{1,5},{2,6},{3,7},{4,0},{5,1},{6,2},{7,3},{8,12},{9,13},{10,... | collective-permute-start | bytes 479240 | tf_op jit(solution)/shard_map/ppermute | solution.py:622
  7.9 10.7 %collective-permute-start.2 = (bf16[13,8,768]{2,1,0:T(8,128)(2,1)}, bf16[13,8,768]{2,1,0:T(8,128)(2,1)S(1)}, u32[]{:S(2)}, u32[]{:S(2)}) collective-permute-start(bf16[13,8,768]{2,1,0:T(8,128)(2,1)} %pack_one.1), channel_id=1, source_target_pairs={{0,6},{1,7},{2,0},{3,1},{4,2},{5,3},{6,4},{7,5},{8,14},{9,15},{10,... | collective-permute-start | bytes 479240 | tf_op jit(solution)/shard_map/ppermute | solution.py:622
  11.0 8.6 %copy-start.11 = (bf16[8,24,768]{2,1,0:T(8,128)(2,1)S(1)}, bf16[8,24,768]{2,1,0:T(8,128)(2,1)}, u32[]{:S(2)}) copy-start(bf16[8,24,768]{2,1,0:T(8,128)(2,1)} %pack_two.1) | copy-start | bytes 884740
  20.7 33.9 %all-to-all-start = ((bf16[4,8,24,768]{3,2,1,0:T(8,128)(2,1)}), bf16[4,8,24,768]{3,2,1,0:T(8,128)(2,1)S(1)}, u32[]{:S(2)}, u32[]{:S(2)}) async-start(bf16[4,8,24,768]{3,2,1,0:T(8,128)(2,1)} %broadcast_in_dim.40), calls=%async_computation | async-start | bytes 2359296 | tf_op jit(solution)/shard_map/all_to_all | solution.py:626
  27.0 8.7 %collective-permute-start.6 = (bf16[4,7,8,768]{3,2,1,0:T(8,128)(2,1)S(1)}, bf16[4,7,8,768]{3,2,1,0:T(8,128)(2,1)S(1)}, u32[]{:S(2)}, u32[]{:S(2)}) collective-permute-start(bf16[4,7,8,768]{3,2,1,0:T(8,128)(2,1)S(1)} %slice.95), channel_id=1, source_target_pairs={{0,16},{1,17},{2,18},{3,19},{4,20},{5,21},{6,22},{7,23},{8,24},{9,... | collective-permute-start | bytes 1032200 | tf_op jit(solution)/shard_map/ppermute | solution.py:622
  28.6 8.8 %collective-permute-start.3 = (bf16[4,2,24,768]{3,2,1,0:T(8,128)(2,1)S(1)}, bf16[4,2,24,768]{3,2,1,0:T(8,128)(2,1)S(1)}, u32[]{:S(2)}, u32[]{:S(2)}) collective-permute-start(bf16[4,2,24,768]{3,2,1,0:T(8,128)(2,1)S(1)} %bitcast.121), channel_id=1, source_target_pairs={{0,1},{1,0},{2,3},{3,2},{4,5},{5,4},{6,7},{7,6},{8,9},{9,8},{10,11... | collective-permute-start | bytes 884744 | tf_op jit(solution)/shard_map/ppermute | solution.py:622
  35.8 19.8 %copy-start.2 = (bf16[2,4,7,8,768]{4,3,2,1,0:T(8,128)(2,1)}, bf16[2,4,7,8,768]{4,3,2,1,0:T(8,128)(2,1)S(1)}, u32[]{:S(2)}) copy-start(bf16[2,4,7,8,768]{4,3,2,1,0:T(8,128)(2,1)S(1)} %pad_maximum_fusion.3.refs_5_) | copy-start | bytes 2064388
  35.8 15.3 %collective-permute-start.7 = (bf16[2,4,7,8,768]{4,3,2,1,0:T(8,128)(2,1)S(1)}, bf16[2,4,7,8,768]{4,3,2,1,0:T(8,128)(2,1)}, u32[]{:S(2)}, u32[]{:S(2)}) collective-permute-start(bf16[2,4,7,8,768]{4,3,2,1,0:T(8,128)(2,1)S(1)} %pad_maximum_fusion.3.refs_5_), channel_id=1, source_target_pairs={{0,1},{1,0},{2,3},{3,2},{4,5},{5,4},{6,7},{7,6},{8,9},{9,8},{10,11... | collective-permute-start | bytes 2064392 | tf_op jit(solution)/shard_map/ppermute | solution.py:622
  37.4 18.1 %copy-start.3 = (bf16[2,4,2,24,768]{4,3,2,1,0:T(8,128)(2,1)}, bf16[2,4,2,24,768]{4,3,2,1,0:T(8,128)(2,1)S(1)}, u32[]{:S(2)}) copy-start(bf16[2,4,2,24,768]{4,3,2,1,0:T(8,128)(2,1)S(1)} %pad_maximum_fusion.6.refs_1_) | copy-start | bytes 1769476
  37.5 12.9 %collective-permute-start.5 = (bf16[2,4,2,24,768]{4,3,2,1,0:T(8,128)(2,1)S(1)}, bf16[2,4,2,24,768]{4,3,2,1,0:T(8,128)(2,1)}, u32[]{:S(2)}, u32[]{:S(2)}) collective-permute-start(bf16[2,4,2,24,768]{4,3,2,1,0:T(8,128)(2,1)S(1)} %pad_maximum_fusion.6.refs_1_), channel_id=1, source_target_pairs={{0,16},{1,17},{2,18},{3,19},{4,20},{5,21},{6,22},{7,23},{8,24},{9,... | collective-permute-start | bytes 1769480 | tf_op jit(solution)/shard_map/ppermute | solution.py:622
  39.0 18.0 %collective-permute-start.4 = (bf16[2,4,2,24,768]{4,3,2,1,0:T(8,128)(2,1)S(1)}, bf16[2,4,2,24,768]{4,3,2,1,0:T(8,128)(2,1)}, u32[]{:S(2)}, u32[]{:S(2)}) collective-permute-start(bf16[2,4,2,24,768]{4,3,2,1,0:T(8,128)(2,1)S(1)} %pad_maximum_fusion.6.refs_1_), channel_id=1, source_target_pairs={{0,8},{1,9},{2,10},{3,11},{4,12},{5,13},{6,14},{7,15},{8,0},{9,1},... | collective-permute-start | bytes 1769480 | tf_op jit(solution)/shard_map/ppermute | solution.py:622
  39.0 20.1 %collective-permute-start.9 = (bf16[2,4,7,8,768]{4,3,2,1,0:T(8,128)(2,1)S(1)}, bf16[2,4,7,8,768]{4,3,2,1,0:T(8,128)(2,1)}, u32[]{:S(2)}, u32[]{:S(2)}) collective-permute-start(bf16[2,4,7,8,768]{4,3,2,1,0:T(8,128)(2,1)S(1)} %pad_maximum_fusion.3.refs_5_), channel_id=1, source_target_pairs={{0,8},{1,9},{2,10},{3,11},{4,12},{5,13},{6,14},{7,15},{8,0},{9,1},... | collective-permute-start | bytes 2064392 | tf_op jit(solution)/shard_map/ppermute | solution.py:622
  51.1 8.1 %collective-permute-start.10 = (bf16[2,4,7,8,768]{4,3,2,1,0:T(8,128)(2,1)}, bf16[2,4,7,8,768]{4,3,2,1,0:T(8,128)(2,1)}, u32[]{:S(2)}, u32[]{:S(2)}) collective-permute-start(bf16[2,4,7,8,768]{4,3,2,1,0:T(8,128)(2,1)} %collective-permute-done.7.refs_7_), channel_id=1, source_target_pairs={{0,8},{1,9},{2,10},{3,11},{4,12},{5,13},{6,14},{7,15},{8,0},{9,1},... | collective-permute-start | bytes 2064392 | tf_op jit(solution)/shard_map/ppermute | solution.py:622
  51.1 8.1 %collective-permute-start.8 = (bf16[2,4,2,24,768]{4,3,2,1,0:T(8,128)(2,1)}, bf16[2,4,2,24,768]{4,3,2,1,0:T(8,128)(2,1)}, u32[]{:S(2)}, u32[]{:S(2)}) collective-permute-start(bf16[2,4,2,24,768]{4,3,2,1,0:T(8,128)(2,1)} %collective-permute-done.5.refs_3_), channel_id=1, source_target_pairs={{0,8},{1,9},{2,10},{3,11},{4,12},{5,13},{6,14},{7,15},{8,0},{9,1},... | collective-permute-start | bytes 1769480 | tf_op jit(solution)/shard_map/ppermute | solution.py:622
  55.5 14.5 %collective-permute-start.12 = (bf16[4,4,24,768]{3,2,1,0:T(8,128)(2,1)}, bf16[4,4,24,768]{3,2,1,0:T(8,128)(2,1)S(1)}, u32[]{:S(2)}, u32[]{:S(2)}) collective-permute-start(bf16[4,4,24,768]{3,2,1,0:T(8,128)(2,1)} %get-tuple-element.102), channel_id=1, source_target_pairs={{0,16},{1,17},{2,18},{3,19},{4,20},{5,21},{6,22},{7,23},{8,24},{9,... | collective-permute-start | bytes 1769480 | tf_op jit(solution)/shard_map/ppermute | solution.py:622
  57.0 15.8 %collective-permute-start.11 = (bf16[4,4,24,768]{3,2,1,0:T(8,128)(2,1)S(1)}, bf16[4,4,24,768]{3,2,1,0:T(8,128)(2,1)S(1)}, u32[]{:S(2)}, u32[]{:S(2)}) collective-permute-start(bf16[4,4,24,768]{3,2,1,0:T(8,128)(2,1)S(1)} %get-tuple-element.101), channel_id=1, source_target_pairs={{0,1},{1,0},{2,3},{3,2},{4,5},{5,4},{6,7},{7,6},{8,9},{9,8},{10,11... | collective-permute-start | bytes 1769480 | tf_op jit(solution)/shard_map/ppermute | solution.py:622
  71.2 10.9 %copy-start = (bf16[2,4,4,24,768]{4,3,2,1,0:T(8,128)(2,1)}, bf16[2,4,4,24,768]{4,3,2,1,0:T(8,128)(2,1)S(1)}, u32[]{:S(2)}) copy-start(bf16[2,4,4,24,768]{4,3,2,1,0:T(8,128)(2,1)S(1)} %pad_maximum_fusion.1.refs_5_) | copy-start | bytes 3538948
  71.2 26.1 %collective-permute-start.15 = (bf16[2,4,4,24,768]{4,3,2,1,0:T(8,128)(2,1)S(1)}, bf16[2,4,4,24,768]{4,3,2,1,0:T(8,128)(2,1)S(1)}, u32[]{:S(2)}, u32[]{:S(2)}) collective-permute-start(bf16[2,4,4,24,768]{4,3,2,1,0:T(8,128)(2,1)S(1)} %pad_maximum_fusion.1.refs_5_), channel_id=1, source_target_pairs={{0,1},{1,0},{2,3},{3,2},{4,5},{5,4},{6,7},{7,6},{8,9},{9,8},{10,11... | collective-permute-start | bytes 3538952 | tf_op jit(solution)/shard_map/ppermute | solution.py:622
  72.9 9.2 %copy-start.1 = (bf16[2,4,4,24,768]{4,3,2,1,0:T(8,128)(2,1)}, bf16[2,4,4,24,768]{4,3,2,1,0:T(8,128)(2,1)S(1)}, u32[]{:S(2)}) copy-start(bf16[2,4,4,24,768]{4,3,2,1,0:T(8,128)(2,1)S(1)} %pad_maximum_fusion.refs_1_) | copy-start | bytes 3538948
  72.9 25.8 %collective-permute-start.14 = (bf16[2,4,4,24,768]{4,3,2,1,0:T(8,128)(2,1)S(1)}, bf16[2,4,4,24,768]{4,3,2,1,0:T(8,128)(2,1)S(1)}, u32[]{:S(2)}, u32[]{:S(2)}) collective-permute-start(bf16[2,4,4,24,768]{4,3,2,1,0:T(8,128)(2,1)S(1)} %pad_maximum_fusion.refs_1_), channel_id=1, source_target_pairs={{0,16},{1,17},{2,18},{3,19},{4,20},{5,21},{6,22},{7,23},{8,24},{9,... | collective-permute-start | bytes 3538952 | tf_op jit(solution)/shard_map/ppermute | solution.py:622
  82.1 17.1 %collective-permute-start.17 = (bf16[2,4,4,24,768]{4,3,2,1,0:T(8,128)(2,1)S(1)}, bf16[2,4,4,24,768]{4,3,2,1,0:T(8,128)(2,1)S(1)}, u32[]{:S(2)}, u32[]{:S(2)}) collective-permute-start(bf16[2,4,4,24,768]{4,3,2,1,0:T(8,128)(2,1)S(1)} %pad_maximum_fusion.1.refs_5_), channel_id=1, source_target_pairs={{0,8},{1,9},{2,10},{3,11},{4,12},{5,13},{6,14},{7,15},{8,0},{9,1},... | collective-permute-start | bytes 3538952 | tf_op jit(solution)/shard_map/ppermute | solution.py:622
  82.2 17.1 %collective-permute-start.13 = (bf16[2,4,4,24,768]{4,3,2,1,0:T(8,128)(2,1)S(1)}, bf16[2,4,4,24,768]{4,3,2,1,0:T(8,128)(2,1)S(1)}, u32[]{:S(2)}, u32[]{:S(2)}) collective-permute-start(bf16[2,4,4,24,768]{4,3,2,1,0:T(8,128)(2,1)S(1)} %pad_maximum_fusion.refs_1_), channel_id=1, source_target_pairs={{0,8},{1,9},{2,10},{3,11},{4,12},{5,13},{6,14},{7,15},{8,0},{9,1},... | collective-permute-start | bytes 3538952 | tf_op jit(solution)/shard_map/ppermute | solution.py:622
  97.3 6.1 %copy-start.6 = (bf16[2,4,4,24,768]{4,3,2,1,0:T(8,128)(2,1)}, bf16[2,4,4,24,768]{4,3,2,1,0:T(8,128)(2,1)S(1)}, u32[]{:S(2)}) copy-start(bf16[2,4,4,24,768]{4,3,2,1,0:T(8,128)(2,1)S(1)} %collective-permute-done.15.refs_7_) | copy-start | bytes 3538948
  98.7 4.7 %copy-start.7 = (bf16[2,4,4,24,768]{4,3,2,1,0:T(8,128)(2,1)}, bf16[2,4,4,24,768]{4,3,2,1,0:T(8,128)(2,1)S(1)}, u32[]{:S(2)}) copy-start(bf16[2,4,4,24,768]{4,3,2,1,0:T(8,128)(2,1)S(1)} %collective-permute-done.14.refs_3_) | copy-start | bytes 3538948
  98.7 4.5 %collective-permute-start.16 = (bf16[2,4,4,24,768]{4,3,2,1,0:T(8,128)(2,1)S(1)}, bf16[2,4,4,24,768]{4,3,2,1,0:T(8,128)(2,1)S(1)}, u32[]{:S(2)}, u32[]{:S(2)}) collective-permute-start(bf16[2,4,4,24,768]{4,3,2,1,0:T(8,128)(2,1)S(1)} %collective-permute-done.14.refs_3_), channel_id=1, source_target_pairs={{0,8},{1,9},{2,10},{3,11},{4,12},{5,13},{6,14},{7,15},{8,0},{9,1},... | collective-permute-start | bytes 3538952 | tf_op jit(solution)/shard_map/ppermute | solution.py:622
  98.7 4.7 %collective-permute-start.18 = (bf16[2,4,4,24,768]{4,3,2,1,0:T(8,128)(2,1)S(1)}, bf16[2,4,4,24,768]{4,3,2,1,0:T(8,128)(2,1)}, u32[]{:S(2)}, u32[]{:S(2)}) collective-permute-start(bf16[2,4,4,24,768]{4,3,2,1,0:T(8,128)(2,1)S(1)} %collective-permute-done.15.refs_7_), channel_id=1, source_target_pairs={{0,8},{1,9},{2,10},{3,11},{4,12},{5,13},{6,14},{7,15},{8,0},{9,1},... | collective-permute-start | bytes 3538952 | tf_op jit(solution)/shard_map/ppermute | solution.py:622
  99.2 4.2 %copy-start.8 = (bf16[2,4,4,24,768]{4,3,2,1,0:T(8,128)(2,1)}, bf16[2,4,4,24,768]{4,3,2,1,0:T(8,128)(2,1)S(1)}, u32[]{:S(2)}) copy-start(bf16[2,4,4,24,768]{4,3,2,1,0:T(8,128)(2,1)S(1)} %collective-permute-done.17.refs_6_) | copy-start | bytes 3538948
  99.2 4.2 %copy-start.9 = (bf16[2,4,4,24,768]{4,3,2,1,0:T(8,128)(2,1)}, bf16[2,4,4,24,768]{4,3,2,1,0:T(8,128)(2,1)S(1)}, u32[]{:S(2)}) copy-start(bf16[2,4,4,24,768]{4,3,2,1,0:T(8,128)(2,1)S(1)} %collective-permute-done.13.refs_2_) | copy-start | bytes 3538948
  103.2 1.0 copy-start.10
  285.7 4.9 %collective-permute-start.20 = (bf16[2,2,4,4,24,768]{5,4,3,2,1,0:T(8,128)(2,1)}, bf16[2,2,4,4,24,768]{5,4,3,2,1,0:T(8,128)(2,1)}, u32[]{:S(2)}, u32[]{:S(2)}) collective-permute-start(bf16[2,2,4,4,24,768]{5,4,3,2,1,0:T(8,128)(2,1)} %get-tuple-element.138), channel_id=1, source_target_pairs={{0,8},{1,9},{2,10},{3,11},{4,12},{5,13},{6,14},{7,15},{8,0},{9,1},... | collective-permute-start | bytes 7077896 | tf_op jit(solution)/shard_map/ppermute | solution.py:622
  285.9 10.5 %collective-permute-start.19 = (bf16[2,2,4,4,24,768]{5,4,3,2,1,0:T(8,128)(2,1)}, bf16[2,2,4,4,24,768]{5,4,3,2,1,0:T(8,128)(2,1)}, u32[]{:S(2)}, u32[]{:S(2)}) collective-permute-start(bf16[2,2,4,4,24,768]{5,4,3,2,1,0:T(8,128)(2,1)} %get-tuple-element.135), channel_id=1, source_target_pairs={{0,8},{1,9},{2,10},{3,11},{4,12},{5,13},{6,14},{7,15},{8,0},{9,1},... | collective-permute-start | bytes 7077896 | tf_op jit(solution)/shard_map/ppermute | solution.py:622
  290.6 5.7 %copy-start.4 = (bf16[2,2,4,4,24,768]{5,4,3,2,1,0:T(8,128)(2,1)S(1)}, bf16[2,2,4,4,24,768]{5,4,3,2,1,0:T(8,128)(2,1)}, u32[]{:S(2)}) copy-start(bf16[2,2,4,4,24,768]{5,4,3,2,1,0:T(8,128)(2,1)} %get-tuple-element.134) | copy-start | bytes 7077892
  294.8 29.2 %collective-permute-start.22 = (bf16[2,4,4,24,768]{4,3,2,1,0:T(8,128)(2,1)}, bf16[2,4,4,24,768]{4,3,2,1,0:T(8,128)(2,1)}, u32[]{:S(2)}, u32[]{:S(2)}) collective-permute-start(bf16[2,4,4,24,768]{4,3,2,1,0:T(8,128)(2,1)} %get-tuple-element.170), channel_id=1, source_target_pairs={{0,16},{1,17},{2,18},{3,19},{4,20},{5,21},{6,22},{7,23},{8,24},{9,... | collective-permute-start | bytes 3538952 | tf_op jit(solution)/shard_map/ppermute | solution.py:622
  298.7 28.5 %collective-permute-start.21 = (bf16[2,4,4,24,768]{4,3,2,1,0:T(8,128)(2,1)S(1)}, bf16[2,4,4,24,768]{4,3,2,1,0:T(8,128)(2,1)S(1)}, u32[]{:S(2)}, u32[]{:S(2)}) collective-permute-start(bf16[2,4,4,24,768]{4,3,2,1,0:T(8,128)(2,1)S(1)} %get-tuple-element.172), channel_id=1, source_target_pairs={{0,1},{1,0},{2,3},{3,2},{4,5},{5,4},{6,7},{7,6},{8,9},{9,8},{10,11... | collective-permute-start | bytes 3538952 | tf_op jit(solution)/shard_map/ppermute | solution.py:622
  325.6 17.3 %collective-permute-start.23 = (bf16[4,4,24,768]{3,2,1,0:T(8,128)(2,1)S(1)}, bf16[4,4,24,768]{3,2,1,0:T(8,128)(2,1)S(1)}, u32[]{:S(2)}, u32[]{:S(2)}) collective-permute-start(bf16[4,4,24,768]{3,2,1,0:T(8,128)(2,1)S(1)} %get-tuple-element.178), channel_id=1, source_target_pairs={{0,1},{1,0},{2,3},{3,2},{4,5},{5,4},{6,7},{7,6},{8,9},{9,8},{10,11... | collective-permute-start | bytes 1769480 | tf_op jit(solution)/shard_map/ppermute | solution.py:622
  327.5 15.5 %collective-permute-start.24 = (bf16[4,4,24,768]{3,2,1,0:T(8,128)(2,1)S(1)}, bf16[4,4,24,768]{3,2,1,0:T(8,128)(2,1)S(1)}, u32[]{:S(2)}, u32[]{:S(2)}) collective-permute-start(bf16[4,4,24,768]{3,2,1,0:T(8,128)(2,1)S(1)} %get-tuple-element.180), channel_id=1, source_target_pairs={{0,16},{1,17},{2,18},{3,19},{4,20},{5,21},{6,22},{7,23},{8,24},{9,... | collective-permute-start | bytes 1769480 | tf_op jit(solution)/shard_map/ppermute | solution.py:622
  344.3 16.9 %collective-permute-start.25 = (bf16[2,2,4,5,24,384]{5,4,3,2,1,0:T(8,128)(2,1)}, bf16[2,2,4,5,24,384]{5,4,3,2,1,0:T(8,128)(2,1)S(1)}, u32[]{:S(2)}, u32[]{:S(2)}) collective-permute-start(bf16[2,2,4,5,24,384]{5,4,3,2,1,0:T(8,128)(2,1)} %get-tuple-element.164), channel_id=1, source_target_pairs={{0,8},{1,9},{2,10},{3,11},{4,12},{5,13},{6,14},{7,15},{8,0},{9,1},... | collective-permute-start | bytes 4423688 | tf_op jit(solution)/shard_map/ppermute | solution.py:622
  353.6 4.0 collective-permute-start.26
  354.1 36.4 %all-to-all-start.2 = ((bf16[4,8,24,768]{3,2,1,0:T(8,128)(2,1)}), bf16[4,8,24,768]{3,2,1,0:T(8,128)(2,1)S(1)}, u32[]{:S(2)}, u32[]{:S(2)}) async-start(bf16[4,8,24,768]{3,2,1,0:T(8,128)(2,1)} %pad_maximum_fusion.2), calls=%async_computation.2 | async-start | bytes 2359296 | tf_op jit(solution)/shard_map/all_to_all | solution.py:626
  357.6 3.6 copy-start.5
  359.7 15.3 %collective-permute-start.29 = (bf16[2,4,4,24,384]{4,3,2,1,0:T(8,128)(2,1)S(1)}, bf16[2,4,4,24,384]{4,3,2,1,0:T(8,128)(2,1)S(1)}, u32[]{:S(2)}, u32[]{:S(2)}) collective-permute-start(bf16[2,4,4,24,384]{4,3,2,1,0:T(8,128)(2,1)S(1)} %get-tuple-element.176), channel_id=1, source_target_pairs={{0,16},{1,17},{2,18},{3,19},{4,20},{5,21},{6,22},{7,23},{8,24},{9,... | collective-permute-start | bytes 1769480 | tf_op jit(solution)/shard_map/ppermute | solution.py:622
  361.6 19.5 %collective-permute-start.27 = (bf16[2,4,5,24,384]{4,3,2,1,0:T(8,128)(2,1)S(1)}, bf16[2,4,5,24,384]{4,3,2,1,0:T(8,128)(2,1)S(1)}, u32[]{:S(2)}, u32[]{:S(2)}) collective-permute-start(bf16[2,4,5,24,384]{4,3,2,1,0:T(8,128)(2,1)S(1)} %get-tuple-element.174), channel_id=1, source_target_pairs={{0,1},{1,0},{2,3},{3,2},{4,5},{5,4},{6,7},{7,6},{8,9},{9,8},{10,11... | collective-permute-start | bytes 2211848 | tf_op jit(solution)/shard_map/ppermute | solution.py:622
  375.2 11.0 %collective-permute-start.30 = (bf16[4,4,24,384]{3,2,1,0:T(8,128)(2,1)S(1)}, bf16[4,4,24,384]{3,2,1,0:T(8,128)(2,1)S(1)}, u32[]{:S(2)}, u32[]{:S(2)}) collective-permute-start(bf16[4,4,24,384]{3,2,1,0:T(8,128)(2,1)S(1)} %get-tuple-element.184), channel_id=1, source_target_pairs={{0,1},{1,0},{2,3},{3,2},{4,5},{5,4},{6,7},{7,6},{8,9},{9,8},{10,11... | collective-permute-start | bytes 884744 | tf_op jit(solution)/shard_map/ppermute | solution.py:622
  381.3 8.2 %collective-permute-start.28 = (bf16[4,5,24,384]{3,2,1,0:T(8,128)(2,1)S(1)}, bf16[4,5,24,384]{3,2,1,0:T(8,128)(2,1)S(1)}, u32[]{:S(2)}, u32[]{:S(2)}) collective-permute-start(bf16[4,5,24,384]{3,2,1,0:T(8,128)(2,1)S(1)} %get-tuple-element.182), channel_id=1, source_target_pairs={{0,16},{1,17},{2,18},{3,19},{4,20},{5,21},{6,22},{7,23},{8,24},{9,... | collective-permute-start | bytes 1105928 | tf_op jit(solution)/shard_map/ppermute | solution.py:622
  390.5 18.2 %all-to-all-start.1 = ((bf16[4,9,24,384]{3,2,1,0:T(8,128)(2,1)}), bf16[4,9,24,384]{3,2,1,0:T(8,128)(2,1)S(1)}, u32[]{:S(2)}, u32[]{:S(2)}) async-start(bf16[4,9,24,384]{3,2,1,0:T(8,128)(2,1)} %pad_maximum_fusion.4), calls=%async_computation.1 | async-start | bytes 1327104 | tf_op jit(solution)/shard_map/all_to_all | solution.py:626

commit v9 on v8

--- a/solution.py
+++ b/solution.py
@@ -427,7 +427,7 @@
     o_ref[...] = acc.astype(o_ref.dtype)
 
 
-def dx_call(dz1, parts, w, dtype, block=256):
+def dx_call(dz1, parts, w, dtype, block=512):
     rows = dz1.shape[0]
     line = pl.BlockSpec((block, D), lambda i: (i, 0))
     specs = [pl.BlockSpec((3, block, e.shape[2]), lambda i: (0, i, 0)) for e in parts]
@@ -876,18 +876,19 @@
     sum_back = Sum(grid, where, (Y, X), back)
     into = wgrad_in_call(core, after(h2, back[0]), h1, e1_2, e1_1, rows)
     sum_in = Sum(grid, where, (X, Y), into)
-    steps = sum_back.one(into[0]) + sum_in.one(into[0])
+    steps = sum_back.one(into[0])
+    steps += sum_in.one(*steps)
     e_0, *lines_0 = attend_back_call(qkv, after(dctx, *steps), lse, lengths, 0, 1)
     e_1, *lines_1 = attend_back_call(qkv, after(dctx, e_0), lse, lengths, 1, 1)
     steps = sum_back.two(e_1) + sum_in.two(e_1)
     others = [ctx2, ctx1, ea_2, ea_1]
-    group = wgrad_heads_call(core, after(low2, *steps), low1, e_qkv_2, e_0, rows, 0, others, False)
+    group = wgrad_heads_call(core, after(low2, *steps), low1, e_qkv_2, e_0, rows, 0, others, True)
     line, total = along_z(grid, [sum_in.three(group[0]), sum_back.three(group[0])])
-    sum_0 = Sum(grid, where, (Y, X), group, [line])
+    sum_0 = Sum(grid, where, (X, Y), group, [line])
     steps = [line]
     sums = [sums_1, sums_2, *lines_2, *lines_0, *lines_1]
-    group = wgrad_heads_call(core, after(low2, *steps), low1, e_qkv_2, e_1, rows, 1, sums, True)
-    sum_1 = Sum(grid, where, (X, Y), group)
+    group = wgrad_heads_call(core, after(low2, *steps), low1, e_qkv_2, e_1, rows, 1, sums, False)
+    sum_1 = Sum(grid, where, (Y, X), group)
     steps = sum_0.one(group[0]) + sum_1.one()
     grad = dx_call(after(dz1, *steps), [e_0, e_1], first, BF)
     sum_0.two(grad)

time: 420 us -> 416 us (level)
  transfers between devices with their start and end apart: 34 -> 34, of which waited for: 17 -> 19; matrix products, arithmetic and copies ran while one was open for 4% -> 3% of each run, Pallas kernels for 21% -> 25%
where the time goes in v9:
time: 416 us; the launch traced here: 408 us
  Pallas kernels  269 us (65%)
  waiting for transfers between devices  72.2 us (17%)
  starting transfers between devices  44.2 us (11%)
  other arithmetic  14.6 us (4%)
  local copies, waits for them, and re-layouts  6.6 us (2%)
    ppermute x31, waiting for transfers between devices, send(): return lax.ppermute(value, AXES, self.shift(dim, step))  57 us
    pallas_call x2, Pallas kernels, ffn_back_call(): pl.pallas_call(ffn_back_body, grid=(rows // block,), in_specs=[line, line...  47.7 us
    pallas_call x3, Pallas kernels, attend_back_call(): pl.pallas_call(body, grid_spec=pltpu.PrefetchScalarGridSpec(num_scalar_pr...  46.6 us
    pallas_call x2, Pallas kernels, ffn_call(): pl.pallas_call(lambda *refs: ffn_body(renorm, *refs), grid=(rows // block...  44.7 us
    ppermute x31, starting transfers between devices, send(): return lax.ppermute(value, AXES, self.shift(dim, step))  30 us
    pallas_call x2, Pallas kernels, attend_call(): pl.pallas_call(body, grid_spec=pltpu.PrefetchScalarGridSpec(num_scalar_pr...  24.8 us
    pallas_call x2, Pallas kernels, wgrad_heads_call(): pl.pallas_call(body, grid_spec=pltpu.PrefetchScalarGridSpec(num_scalar_pr...  24.2 us
    pallas_call x2, Pallas kernels, dx_call(): pl.pallas_call(dx_body, grid=(rows // block,), in_specs=[line, *specs, on...  17.7 us
  transfers between devices with their start and end apart: 34, of which 19 were waited for; matrix products, arithmetic and copies ran while one was open for 3% of the time, Pallas kernels for 25%

profile of v9, /device:TPU:0, one launch (start us, length us, event | category | flops | bytes accessed | tf_op | source)
XLA Modules:
  0.0 408.0 jit_solution(4999717232790083628)
XLA Ops:
  0.7 1.7 pack_one.1
  2.3 3.0 collective-permute-start
  5.4 2.6 collective-permute-start.1
  7.9 1.3 collective-permute-start.2
  9.3 1.7 pack_two.1
  11.0 1.6 collective-permute-done
  12.6 6.0 %collective-permute-done.1 = bf16[13,8,768]{2,1,0:T(8,128)(2,1)S(1)} collective-permute-done((bf16[13,8,768]{2,1,0:T(8,128)(2,1)}, bf16[13,8,768]{2,1,0:T(8,128)(2,1)S(1)}, u32[]{:S(2)}, u32[]{:S(2)}) %collective-permute-start.1) | collective-permute-done | bytes 159776 | tf_op jit(solution)/shard_map/ppermute | solution.py:622
  18.6 1.0 pad_maximum_fusion.5
  19.7 1.1 broadcast_in_dim.40
  20.7 6.2 %all-to-all-start = ((bf16[4,8,24,768]{3,2,1,0:T(8,128)(2,1)}), bf16[4,8,24,768]{3,2,1,0:T(8,128)(2,1)S(1)}, u32[]{:S(2)}, u32[]{:S(2)}) async-start(bf16[4,8,24,768]{3,2,1,0:T(8,128)(2,1)} %broadcast_in_dim.40), calls=%async_computation | async-start | bytes 2359296 | tf_op jit(solution)/shard_map/all_to_all | solution.py:626
  27.0 1.6 collective-permute-start.6
  28.6 1.6 collective-permute-start.3
  30.2 5.6 %collective-permute-done.6 = bf16[4,7,8,768]{3,2,1,0:T(8,128)(2,1)S(1)} collective-permute-done((bf16[4,7,8,768]{3,2,1,0:T(8,128)(2,1)S(1)}, bf16[4,7,8,768]{3,2,1,0:T(8,128)(2,1)S(1)}, u32[]{:S(2)}, u32[]{:S(2)}) %collective-permute-start.6) | collective-permute-done | bytes 344096 | tf_op jit(solution)/shard_map/ppermute | solution.py:622
  35.8 1.6 collective-permute-start.7
  37.5 1.6 collective-permute-start.5
  39.5 10.8 %collective-permute-done.5.refs_3_ = bf16[2,4,2,24,768]{4,3,2,1,0:T(8,128)(2,1)} collective-permute-done((bf16[2,4,2,24,768]{4,3,2,1,0:T(8,128)(2,1)S(1)}, bf16[2,4,2,24,768]{4,3,2,1,0:T(8,128)(2,1)}, u32[]{:S(2)}, u32[]{:S(2)}) %collective-permute-start.5) | collective-permute-done | bytes 589856 | tf_op jit(solution)/shard_map/ppermute | solution.py:622
  51.6 3.1 all-to-all-done
  54.6 0.9 fusion.17
  55.5 1.5 collective-permute-start.12
  57.0 1.5 collective-permute-start.11
  59.2 6.4 %place.2 = (bf16[2,2,2,4,2,24,768]{6,5,4,3,2,1,0:T(8,128)(2,1)}, bf16[2,2,2,4,2,3,8,768]{7,6,5,4,3,2,1,0:T(8,128)(2,1)}, f32[24,768]{1,0:T(8,128)}) custom-call(s32[4]{0:T(128)} %pad_add_fusion.refs_0_, bf16[2,4,2,24,768]{4,3,2,1,0:T(8,128)(2,1)} %copy-done.3, bf16[2,4,2,24,768]{4,3,2,1,0:T(8,128)(2,1)} %collective-permute-done.4.refs_2_, ...), custom_call_target="tpu_custom_call" | custom-call | flops 1200000000 | bytes 600000 | tf_op jit(solution)/shard_map/place/pallas_call | solution.py:749
  65.6 4.5 %collective-permute-done.12 = bf16[4,4,24,768]{3,2,1,0:T(8,128)(2,1)S(1)} collective-permute-done((bf16[4,4,24,768]{3,2,1,0:T(8,128)(2,1)}, bf16[4,4,24,768]{3,2,1,0:T(8,128)(2,1)S(1)}, u32[]{:S(2)}, u32[]{:S(2)}) %collective-permute-start.12) | collective-permute-done | bytes 589856 | tf_op jit(solution)/shard_map/ppermute | solution.py:622
  70.0 1.2 pad_maximum_fusion.1.refs_5_
  71.2 1.6 collective-permute-start.15
  72.9 1.6 collective-permute-start.14
  74.5 7.6 %qkv.2.refs_1_.refs_2_.refs_3_ = bf16[1024,2304]{1,0:T(8,128)(2,1)} custom-call(bf16[1024,768]{1,0:T(8,128)(2,1)} %c_ref.3, bf16[2,768,768]{2,1,0:T(8,128)(2,1)} %bitcast.115, bf16[2,768,768]{2,1,0:T(8,128)(2,1)} %bitcast.99, f32[24,768]{1,0:T(8,128)} %get-tuple-element.98.vec_ref.refs_2_), custom_call_target="tpu_custom_call" | custom-call | flops 1600000000 | bytes 800000 | tf_op jit(solution)/shard_map/qkv/pallas_call | solution.py:75
  82.6 12.3 %attend.2 = (bf16[1024,768]{1,0:T(8,128)(2,1)}, f32[2,6,2,512]{3,2,1,0:T(2,128)}) custom-call(s32[2]{0:T(128)} %refs_0_.11, bf16[1024,2304]{1,0:T(8,128)(2,1)} %qkv.2.refs_1_.refs_2_.refs_3_, bf16[1024,2304]{1,0:T(8,128)(2,1)} %qkv.2.refs_1_.refs_2_.refs_3_, bf16[1024,2304]{1,0:T(8,128)(2,1)} %qkv.2.refs_1_.refs_2_.refs_3_), custom_call_target="tpu_custom_call" | custom-call | flops 2600000000 | bytes 1300000 | tf_op jit(solution)/shard_map/attend/pallas_call | solution.py:137
  94.8 2.4 collective-permute-done.15.refs_7_
  97.3 1.4 collective-permute-done.14.refs_3_
  99.3 4.0 collective-permute-done.16.refs_4_
  104.3 8.2 %place.3 = (bf16[4,2,2,4,2,24,768]{6,5,4,3,2,1,0:T(8,128)(2,1)}, bf16[2,2,4,2,4,24,768]{6,5,4,3,2,1,0:T(8,128)(2,1)}) custom-call(s32[4]{0:T(128)} %pad_add_fusion.refs_0_, bf16[2,4,4,24,768]{4,3,2,1,0:T(8,128)(2,1)} %copy-done.1, bf16[2,4,4,24,768]{4,3,2,1,0:T(8,128)(2,1)} %copy-done.10, bf16[2,4,4,24,768]{4,3,2,1,0:T(8,128)(2,1)} %copy-done.8, ...), custom_call_target="tpu_custom_call" | custom-call | flops 1200000000 | bytes 600000 | tf_op jit(solution)/shard_map/place/pallas_call | solution.py:749
  112.5 22.3 %ffn.2 = (f32[1024,768]{1,0:T(8,128)}, bf16[1024,768]{1,0:T(8,128)(2,1)}, bf16[1024,3072]{1,0:T(8,128)(2,1)}, bf16[1024,3072]{1,0:T(8,128)(2,1)}, f32[1024,768]{1,0:T(8,128)}, /*index=5*/bf16[1024,768]{1,0:T(8,128)(2,1)}) custom-call(bf16[1024,768]{1,0:T(8,128)(2,1)} %c_ref.3, bf16[1024,768]{1,0:T(8,128)(2,1)} %get-tuple-element.104.refs_1_.rest_1_, ...), custom_call_target="tpu_custom_call" | custom-call | flops 4400000000 | bytes 2200000 | tf_op jit(solution)/shard_map/ffn/pallas_call | solution.py:237
  134.8 7.6 %qkv.3.refs_1_.refs_2_.refs_3_ = bf16[1024,2304]{1,0:T(8,128)(2,1)} custom-call(bf16[1024,768]{1,0:T(8,128)(2,1)} %get-tuple-element.152.x_ref.a_ref, bf16[2,768,768]{2,1,0:T(8,128)(2,1)} %bitcast.116, bf16[2,768,768]{2,1,0:T(8,128)(2,1)} %bitcast.101, f32[24,768]{1,0:T(8,128)} %get-tuple-element.98.vec_ref.refs_2_), custom_call_target="tpu_custom_call" | custom-call | flops 1600000000 | bytes 800000 | tf_op jit(solution)/shard_map/qkv/pallas_call | solution.py:75
  142.4 12.5 %attend.3 = (bf16[1024,768]{1,0:T(8,128)(2,1)}, f32[2,6,2,512]{3,2,1,0:T(2,128)}) custom-call(s32[2]{0:T(128)} %refs_0_.11, bf16[1024,2304]{1,0:T(8,128)(2,1)} %qkv.3.refs_1_.refs_2_.refs_3_, bf16[1024,2304]{1,0:T(8,128)(2,1)} %qkv.3.refs_1_.refs_2_.refs_3_, bf16[1024,2304]{1,0:T(8,128)(2,1)} %qkv.3.refs_1_.refs_2_.refs_3_), custom_call_target="tpu_custom_call" | custom-call | flops 2600000000 | bytes 1300000 | tf_op jit(solution)/shard_map/attend/pallas_call | solution.py:137
  154.9 22.5 %ffn.3 = (f32[1024,768]{1,0:T(8,128)}, bf16[1024,768]{1,0:T(8,128)(2,1)}, bf16[1024,3072]{1,0:T(8,128)(2,1)}, bf16[1024,3072]{1,0:T(8,128)(2,1)}, f32[1024,768]{1,0:T(8,128)}, /*index=5*/bf16[1024,768]{1,0:T(8,128)(2,1)}) custom-call(f32[1024,768]{1,0:T(8,128)} %get-tuple-element.109.refs_0_.z2_ref, bf16[1024,768]{1,0:T(8,128)(2,1)} %get-tuple-element.111.refs_1_.rest_0_, ...), custom_call_target="tpu_custom_call" | custom-call | flops 4400000000 | bytes 2200000 | tf_op jit(solution)/shard_map/ffn/pallas_call | solution.py:237
  177.4 23.8 %ffn_back.2 = (bf16[1024,768]{1,0:T(8,128)(2,1)}, bf16[1024,3072]{1,0:T(8,128)(2,1)}, f32[1024,768]{1,0:T(8,128)}, bf16[1024,768]{1,0:T(8,128)(2,1)}, bf16[1024,768]{1,0:T(8,128)(2,1)}, /*index=5*/f32[24,768]{1,0:T(8,128)}) custom-call(bf16[1024,768]{1,0:T(8,128)(2,1)} %dy_ref.1, f32[1024,768]{1,0:T(8,128)} %get-tuple-element.113.z2_ref, ...), custom_call_target="tpu_custom_call" | custom-call | flops 4800000000 | bytes 2400000 | tf_op jit(solution)/shard_map/ffn_back/pallas_call | solution.py:319
  201.1 21.7 %attend_back.3 = (bf16[3,1024,768]{2,1,0:T(8,128)(2,1)}, f32[2,1,768]{2,1,0:T(1,128)}, f32[2,1,768]{2,1,0:T(1,128)}) custom-call(s32[2]{0:T(128)} %refs_0_.11, bf16[1024,2304]{1,0:T(8,128)(2,1)} %qkv.3.refs_1_.refs_2_.refs_3_, bf16[1024,2304]{1,0:T(8,128)(2,1)} %qkv.3.refs_1_.refs_2_.refs_3_, bf16[1024,2304]{1,0:T(8,128)(2,1)} %qkv.3.refs_1_.refs_2_.refs_3_, ...), custom_call_target="tpu_custom_call" | custom-call | flops 4800000000 | bytes 2400000 | tf_op jit(solution)/shard_map/attend_back/pallas_call | solution.py:395
  222.9 8.4 %dx.2.dy_ref = f32[1024,768]{1,0:T(8,128)} custom-call(f32[1024,768]{1,0:T(8,128)} %get-tuple-element.116.dz1_ref, bf16[3,1024,768]{2,1,0:T(8,128)(2,1)} %get-tuple-element.119.rest_0_.b_ref, bf16[2,768,768]{2,1,0:T(8,128)(2,1)} %bitcast.117, bf16[2,768,768]{2,1,0:T(8,128)(2,1)} %bitcast.104), custom_call_target="tpu_custom_call" | custom-call | flops 1800000000 | bytes 900000 | tf_op jit(solution)/shard_map/dx/pallas_call | solution.py:434
  231.3 23.9 %ffn_back.3 = (bf16[1024,768]{1,0:T(8,128)(2,1)}, bf16[1024,3072]{1,0:T(8,128)(2,1)}, f32[1024,768]{1,0:T(8,128)}, bf16[1024,768]{1,0:T(8,128)(2,1)}, bf16[1024,768]{1,0:T(8,128)(2,1)}, /*index=5*/f32[24,768]{1,0:T(8,128)}) custom-call(f32[1024,768]{1,0:T(8,128)} %dx.2.dy_ref, f32[1024,768]{1,0:T(8,128)} %get-tuple-element.109.refs_0_.z2_ref, ...), custom_call_target="tpu_custom_call" | custom-call | flops 4800000000 | bytes 2400000 | tf_op jit(solution)/shard_map/ffn_back/pallas_call | solution.py:319
  255.2 15.0 %wgrad_back.1 = (bf16[2,2,4,4,24,768]{5,4,3,2,1,0:T(8,128)(2,1)}, bf16[2,2,4,4,24,768]{5,4,3,2,1,0:T(8,128)(2,1)}) custom-call(s32[1]{0:T(128)} %bitcast.1.core_ref, bf16[1024,3072]{1,0:T(8,128)(2,1)} %get-tuple-element.123.g2k.g2s, bf16[1024,3072]{1,0:T(8,128)(2,1)} %get-tuple-element.124.g1k.g1s, bf16[1024,3072]{1,0:T(8,128)(2,1)} %get-tuple-element.123.g2k.g2s, ...), custom_call_target="tpu_custom_call" | custom-call | flops 3000000000 | bytes 1500000 | tf_op jit(solution)/shard_map/wgrad_back/pallas_call | solution.py:576
  270.3 15.2 %wgrad_in.1 = (bf16[2,2,4,4,24,768]{5,4,3,2,1,0:T(8,128)(2,1)}, bf16[2,2,4,4,24,768]{5,4,3,2,1,0:T(8,128)(2,1)}) custom-call(s32[1]{0:T(128)} %bitcast.1.core_ref, bf16[1024,768]{1,0:T(8,128)(2,1)} %get-tuple-element.129.a_ref, bf16[1024,768]{1,0:T(8,128)(2,1)} %get-tuple-element.130.c_ref, bf16[1024,3072]{1,0:T(8,128)(2,1)} %get-tuple-element.131.b_ref, ...), custom_call_target="tpu_custom_call" | custom-call | flops 3000000000 | bytes 1500000 | tf_op jit(solution)/shard_map/wgrad_in/pallas_call | solution.py:475
  285.8 2.5 fusion
  288.3 2.0 collective-permute-done.20
  290.3 2.3 fusion.3
  292.7 1.6 collective-permute-start.22
  294.7 12.5 %attend_back.4 = (bf16[3,1024,384]{2,1,0:T(8,128)(2,1)}, f32[2,1,384]{2,1,0:T(1,128)}, f32[2,1,384]{2,1,0:T(1,128)}) custom-call(s32[2]{0:T(128)} %refs_0_.11, bf16[1024,2304]{1,0:T(8,128)(2,1)} %qkv.2.refs_1_.refs_2_.refs_3_, bf16[1024,2304]{1,0:T(8,128)(2,1)} %qkv.2.refs_1_.refs_2_.refs_3_, bf16[1024,2304]{1,0:T(8,128)(2,1)} %qkv.2.refs_1_.refs_2_.refs_3_, ...), custom_call_target="tpu_custom_call" | custom-call | flops 2400000000 | bytes 1200000 | tf_op jit(solution)/shard_map/attend_back/pallas_call | solution.py:395
  307.3 12.3 %attend_back.5 = (bf16[3,1024,384]{2,1,0:T(8,128)(2,1)}, f32[2,1,384]{2,1,0:T(1,128)}, f32[2,1,384]{2,1,0:T(1,128)}) custom-call(s32[2]{0:T(128)} %refs_0_.11, bf16[1024,2304]{1,0:T(8,128)(2,1)} %qkv.2.refs_1_.refs_2_.refs_3_, bf16[1024,2304]{1,0:T(8,128)(2,1)} %qkv.2.refs_1_.refs_2_.refs_3_, bf16[1024,2304]{1,0:T(8,128)(2,1)} %qkv.2.refs_1_.refs_2_.refs_3_, ...), custom_call_target="tpu_custom_call" | custom-call | flops 2400000000 | bytes 1200000 | tf_op jit(solution)/shard_map/attend_back/pallas_call | solution.py:395
  319.6 1.4 collective-permute-done.22
  322.5 1.2 collective-permute-start.24
  323.7 14.9 %wgrad_heads.2 = (bf16[2,2,4,5,24,384]{5,4,3,2,1,0:T(8,128)(2,1)}, bf16[2,2,4,5,24,384]{5,4,3,2,1,0:T(8,128)(2,1)}) custom-call(s32[1]{0:T(128)} %bitcast.1.core_ref, bf16[1024,768]{1,0:T(8,128)(2,1)} %get-tuple-element.152.x_ref.a_ref, bf16[1024,768]{1,0:T(8,128)(2,1)} %c_ref.3, bf16[3,1024,768]{2,1,0:T(8,128)(2,1)} %get-tuple-element.119.rest_0_.b_ref, ...), custom_call_target="tpu_custom_call" | custom-call | flops 2400000000 | bytes 1200000 | tf_op jit(solution)/shard_map/wgrad_heads/pallas_call | solution.py:540
  338.9 1.2 pad_maximum_fusion.2
  340.1 9.3 %wgrad_heads.3 = (bf16[2,2,4,4,24,384]{5,4,3,2,1,0:T(8,128)(2,1)}, bf16[2,2,4,4,24,384]{5,4,3,2,1,0:T(8,128)(2,1)}) custom-call(s32[1]{0:T(128)} %bitcast.1.core_ref, bf16[1024,768]{1,0:T(8,128)(2,1)} %get-tuple-element.152.x_ref.a_ref, bf16[1024,768]{1,0:T(8,128)(2,1)} %c_ref.3, bf16[3,1024,768]{2,1,0:T(8,128)(2,1)} %get-tuple-element.119.rest_0_.b_ref, ...), custom_call_target="tpu_custom_call" | custom-call | flops 2400000000 | bytes 1200000 | tf_op jit(solution)/shard_map/wgrad_heads/pallas_call | solution.py:540
  349.9 3.5 all-to-all-start.2
  353.4 2.0 fusion.11
  355.5 1.6 collective-permute-start.29
  358.0 9.3 %dx.3 = bf16[1024,768]{1,0:T(8,128)(2,1)} custom-call(f32[1024,768]{1,0:T(8,128)} %get-tuple-element.166.dz1_ref, bf16[3,1024,384]{2,1,0:T(8,128)(2,1)} %get-tuple-element.141.d_ref.rest_0_, bf16[3,1024,384]{2,1,0:T(8,128)(2,1)} %get-tuple-element.143.d_ref.rest_1_, bf16[2,768,768]{2,1,0:T(8,128)(2,1)} %bitcast.118, bf16[2,768,768]{2,1,0:T(8,128)(2,1)} %bitcast.106), custom_call_target="tpu_custom_call" | custom-call | flops 1800000000 | bytes 900000 | tf_op jit(solution)/shard_map/dx/pallas_call | solution.py:434
  367.3 3.5 collective-permute-done.29
  370.9 0.9 collective-permute-start.30
  371.9 5.0 %collective-permute-done.27 = bf16[2,4,5,24,384]{4,3,2,1,0:T(8,128)(2,1)S(1)} collective-permute-done((bf16[2,4,5,24,384]{4,3,2,1,0:T(8,128)(2,1)S(1)}, bf16[2,4,5,24,384]{4,3,2,1,0:T(8,128)(2,1)S(1)}, u32[]{:S(2)}, u32[]{:S(2)}) %collective-permute-start.27) | collective-permute-done | bytes 737312 | tf_op jit(solution)/shard_map/ppermute | solution.py:622
  377.6 4.3 %collective-permute-done.30 = bf16[4,4,24,384]{3,2,1,0:T(8,128)(2,1)S(1)} collective-permute-done((bf16[4,4,24,384]{3,2,1,0:T(8,128)(2,1)S(1)}, bf16[4,4,24,384]{3,2,1,0:T(8,128)(2,1)S(1)}, u32[]{:S(2)}, u32[]{:S(2)}) %collective-permute-start.30) | collective-permute-done | bytes 294944 | tf_op jit(solution)/shard_map/ppermute | solution.py:622
  382.0 3.2 collective-permute-done.28
  385.4 1.0 pad_maximum_fusion.4
  386.3 4.5 %all-to-all-start.1 = ((bf16[4,9,24,384]{3,2,1,0:T(8,128)(2,1)}), bf16[4,9,24,384]{3,2,1,0:T(8,128)(2,1)S(1)}, u32[]{:S(2)}, u32[]{:S(2)}) async-start(bf16[4,9,24,384]{3,2,1,0:T(8,128)(2,1)} %pad_maximum_fusion.4), calls=%async_computation.1 | async-start | bytes 1327104 | tf_op jit(solution)/shard_map/all_to_all | solution.py:626
  392.4 12.1 %all-to-all-done.1 = bf16[4,9,24,384]{3,2,1,0:T(8,128)(2,1)S(1)} async-done(((bf16[4,9,24,384]{3,2,1,0:T(8,128)(2,1)}), bf16[4,9,24,384]{3,2,1,0:T(8,128)(2,1)S(1)}, u32[]{:S(2)}, u32[]{:S(2)}) %all-to-all-start.1) | async-done | bytes 663584 | tf_op jit(solution)/shard_map/all_to_all | solution.py:626
  (89 shorter events, 14.6 us)
Async XLA Ops:
  2.3 10.3 %collective-permute-start = (bf16[13,8,768]{2,1,0:T(8,128)(2,1)}, bf16[13,8,768]{2,1,0:T(8,128)(2,1)S(1)}, u32[]{:S(2)}, u32[]{:S(2)}) collective-permute-start(bf16[13,8,768]{2,1,0:T(8,128)(2,1)} %pack_one.1), channel_id=1, source_target_pairs={{0,2},{1,3},{2,4},{3,5},{4,6},{5,7},{6,0},{7,1},{8,10},{9,11},{10,... | collective-permute-start | bytes 479240 | tf_op jit(solution)/shard_map/ppermute | solution.py:622
  5.4 13.3 %collective-permute-start.1 = (bf16[13,8,768]{2,1,0:T(8,128)(2,1)}, bf16[13,8,768]{2,1,0:T(8,128)(2,1)S(1)}, u32[]{:S(2)}, u32[]{:S(2)}) collective-permute-start(bf16[13,8,768]{2,1,0:T(8,128)(2,1)} %pack_one.1), channel_id=1, source_target_pairs={{0,4},{1,5},{2,6},{3,7},{4,0},{5,1},{6,2},{7,3},{8,12},{9,13},{10,... | collective-permute-start | bytes 479240 | tf_op jit(solution)/shard_map/ppermute | solution.py:622
  7.9 10.7 %collective-permute-start.2 = (bf16[13,8,768]{2,1,0:T(8,128)(2,1)}, bf16[13,8,768]{2,1,0:T(8,128)(2,1)S(1)}, u32[]{:S(2)}, u32[]{:S(2)}) collective-permute-start(bf16[13,8,768]{2,1,0:T(8,128)(2,1)} %pack_one.1), channel_id=1, source_target_pairs={{0,6},{1,7},{2,0},{3,1},{4,2},{5,3},{6,4},{7,5},{8,14},{9,15},{10,... | collective-permute-start | bytes 479240 | tf_op jit(solution)/shard_map/ppermute | solution.py:622
  11.0 8.6 %copy-start.12 = (bf16[8,24,768]{2,1,0:T(8,128)(2,1)S(1)}, bf16[8,24,768]{2,1,0:T(8,128)(2,1)}, u32[]{:S(2)}) copy-start(bf16[8,24,768]{2,1,0:T(8,128)(2,1)} %pack_two.1) | copy-start | bytes 884740
  20.7 33.9 %all-to-all-start = ((bf16[4,8,24,768]{3,2,1,0:T(8,128)(2,1)}), bf16[4,8,24,768]{3,2,1,0:T(8,128)(2,1)S(1)}, u32[]{:S(2)}, u32[]{:S(2)}) async-start(bf16[4,8,24,768]{3,2,1,0:T(8,128)(2,1)} %broadcast_in_dim.40), calls=%async_computation | async-start | bytes 2359296 | tf_op jit(solution)/shard_map/all_to_all | solution.py:626
  27.0 8.7 %collective-permute-start.6 = (bf16[4,7,8,768]{3,2,1,0:T(8,128)(2,1)S(1)}, bf16[4,7,8,768]{3,2,1,0:T(8,128)(2,1)S(1)}, u32[]{:S(2)}, u32[]{:S(2)}) collective-permute-start(bf16[4,7,8,768]{3,2,1,0:T(8,128)(2,1)S(1)} %slice.95), channel_id=1, source_target_pairs={{0,16},{1,17},{2,18},{3,19},{4,20},{5,21},{6,22},{7,23},{8,24},{9,... | collective-permute-start | bytes 1032200 | tf_op jit(solution)/shard_map/ppermute | solution.py:622
  28.6 8.8 %collective-permute-start.3 = (bf16[4,2,24,768]{3,2,1,0:T(8,128)(2,1)S(1)}, bf16[4,2,24,768]{3,2,1,0:T(8,128)(2,1)S(1)}, u32[]{:S(2)}, u32[]{:S(2)}) collective-permute-start(bf16[4,2,24,768]{3,2,1,0:T(8,128)(2,1)S(1)} %bitcast.121), channel_id=1, source_target_pairs={{0,1},{1,0},{2,3},{3,2},{4,5},{5,4},{6,7},{7,6},{8,9},{9,8},{10,11... | collective-permute-start | bytes 884744 | tf_op jit(solution)/shard_map/ppermute | solution.py:622
  35.8 19.8 %copy-start.2 = (bf16[2,4,7,8,768]{4,3,2,1,0:T(8,128)(2,1)}, bf16[2,4,7,8,768]{4,3,2,1,0:T(8,128)(2,1)S(1)}, u32[]{:S(2)}) copy-start(bf16[2,4,7,8,768]{4,3,2,1,0:T(8,128)(2,1)S(1)} %pad_maximum_fusion.3.refs_5_) | copy-start | bytes 2064388
  35.8 15.3 %collective-permute-start.7 = (bf16[2,4,7,8,768]{4,3,2,1,0:T(8,128)(2,1)S(1)}, bf16[2,4,7,8,768]{4,3,2,1,0:T(8,128)(2,1)}, u32[]{:S(2)}, u32[]{:S(2)}) collective-permute-start(bf16[2,4,7,8,768]{4,3,2,1,0:T(8,128)(2,1)S(1)} %pad_maximum_fusion.3.refs_5_), channel_id=1, source_target_pairs={{0,1},{1,0},{2,3},{3,2},{4,5},{5,4},{6,7},{7,6},{8,9},{9,8},{10,11... | collective-permute-start | bytes 2064392 | tf_op jit(solution)/shard_map/ppermute | solution.py:622
  37.4 18.1 %copy-start.3 = (bf16[2,4,2,24,768]{4,3,2,1,0:T(8,128)(2,1)}, bf16[2,4,2,24,768]{4,3,2,1,0:T(8,128)(2,1)S(1)}, u32[]{:S(2)}) copy-start(bf16[2,4,2,24,768]{4,3,2,1,0:T(8,128)(2,1)S(1)} %pad_maximum_fusion.6.refs_1_) | copy-start | bytes 1769476
  37.5 12.9 %collective-permute-start.5 = (bf16[2,4,2,24,768]{4,3,2,1,0:T(8,128)(2,1)S(1)}, bf16[2,4,2,24,768]{4,3,2,1,0:T(8,128)(2,1)}, u32[]{:S(2)}, u32[]{:S(2)}) collective-permute-start(bf16[2,4,2,24,768]{4,3,2,1,0:T(8,128)(2,1)S(1)} %pad_maximum_fusion.6.refs_1_), channel_id=1, source_target_pairs={{0,16},{1,17},{2,18},{3,19},{4,20},{5,21},{6,22},{7,23},{8,24},{9,... | collective-permute-start | bytes 1769480 | tf_op jit(solution)/shard_map/ppermute | solution.py:622
  39.0 18.0 %collective-permute-start.4 = (bf16[2,4,2,24,768]{4,3,2,1,0:T(8,128)(2,1)S(1)}, bf16[2,4,2,24,768]{4,3,2,1,0:T(8,128)(2,1)}, u32[]{:S(2)}, u32[]{:S(2)}) collective-permute-start(bf16[2,4,2,24,768]{4,3,2,1,0:T(8,128)(2,1)S(1)} %pad_maximum_fusion.6.refs_1_), channel_id=1, source_target_pairs={{0,8},{1,9},{2,10},{3,11},{4,12},{5,13},{6,14},{7,15},{8,0},{9,1},... | collective-permute-start | bytes 1769480 | tf_op jit(solution)/shard_map/ppermute | solution.py:622
  39.0 20.1 %collective-permute-start.9 = (bf16[2,4,7,8,768]{4,3,2,1,0:T(8,128)(2,1)S(1)}, bf16[2,4,7,8,768]{4,3,2,1,0:T(8,128)(2,1)}, u32[]{:S(2)}, u32[]{:S(2)}) collective-permute-start(bf16[2,4,7,8,768]{4,3,2,1,0:T(8,128)(2,1)S(1)} %pad_maximum_fusion.3.refs_5_), channel_id=1, source_target_pairs={{0,8},{1,9},{2,10},{3,11},{4,12},{5,13},{6,14},{7,15},{8,0},{9,1},... | collective-permute-start | bytes 2064392 | tf_op jit(solution)/shard_map/ppermute | solution.py:622
  51.1 8.1 %collective-permute-start.10 = (bf16[2,4,7,8,768]{4,3,2,1,0:T(8,128)(2,1)}, bf16[2,4,7,8,768]{4,3,2,1,0:T(8,128)(2,1)}, u32[]{:S(2)}, u32[]{:S(2)}) collective-permute-start(bf16[2,4,7,8,768]{4,3,2,1,0:T(8,128)(2,1)} %collective-permute-done.7.refs_7_), channel_id=1, source_target_pairs={{0,8},{1,9},{2,10},{3,11},{4,12},{5,13},{6,14},{7,15},{8,0},{9,1},... | collective-permute-start | bytes 2064392 | tf_op jit(solution)/shard_map/ppermute | solution.py:622
  51.1 8.1 %collective-permute-start.8 = (bf16[2,4,2,24,768]{4,3,2,1,0:T(8,128)(2,1)}, bf16[2,4,2,24,768]{4,3,2,1,0:T(8,128)(2,1)}, u32[]{:S(2)}, u32[]{:S(2)}) collective-permute-start(bf16[2,4,2,24,768]{4,3,2,1,0:T(8,128)(2,1)} %collective-permute-done.5.refs_3_), channel_id=1, source_target_pairs={{0,8},{1,9},{2,10},{3,11},{4,12},{5,13},{6,14},{7,15},{8,0},{9,1},... | collective-permute-start | bytes 1769480 | tf_op jit(solution)/shard_map/ppermute | solution.py:622
  55.5 14.5 %collective-permute-start.12 = (bf16[4,4,24,768]{3,2,1,0:T(8,128)(2,1)}, bf16[4,4,24,768]{3,2,1,0:T(8,128)(2,1)S(1)}, u32[]{:S(2)}, u32[]{:S(2)}) collective-permute-start(bf16[4,4,24,768]{3,2,1,0:T(8,128)(2,1)} %get-tuple-element.102), channel_id=1, source_target_pairs={{0,16},{1,17},{2,18},{3,19},{4,20},{5,21},{6,22},{7,23},{8,24},{9,... | collective-permute-start | bytes 1769480 | tf_op jit(solution)/shard_map/ppermute | solution.py:622
  57.0 15.8 %collective-permute-start.11 = (bf16[4,4,24,768]{3,2,1,0:T(8,128)(2,1)S(1)}, bf16[4,4,24,768]{3,2,1,0:T(8,128)(2,1)S(1)}, u32[]{:S(2)}, u32[]{:S(2)}) collective-permute-start(bf16[4,4,24,768]{3,2,1,0:T(8,128)(2,1)S(1)} %get-tuple-element.101), channel_id=1, source_target_pairs={{0,1},{1,0},{2,3},{3,2},{4,5},{5,4},{6,7},{7,6},{8,9},{9,8},{10,11... | collective-permute-start | bytes 1769480 | tf_op jit(solution)/shard_map/ppermute | solution.py:622
  71.2 10.9 %copy-start = (bf16[2,4,4,24,768]{4,3,2,1,0:T(8,128)(2,1)}, bf16[2,4,4,24,768]{4,3,2,1,0:T(8,128)(2,1)S(1)}, u32[]{:S(2)}) copy-start(bf16[2,4,4,24,768]{4,3,2,1,0:T(8,128)(2,1)S(1)} %pad_maximum_fusion.1.refs_5_) | copy-start | bytes 3538948
  71.2 26.1 %collective-permute-start.15 = (bf16[2,4,4,24,768]{4,3,2,1,0:T(8,128)(2,1)S(1)}, bf16[2,4,4,24,768]{4,3,2,1,0:T(8,128)(2,1)S(1)}, u32[]{:S(2)}, u32[]{:S(2)}) collective-permute-start(bf16[2,4,4,24,768]{4,3,2,1,0:T(8,128)(2,1)S(1)} %pad_maximum_fusion.1.refs_5_), channel_id=1, source_target_pairs={{0,1},{1,0},{2,3},{3,2},{4,5},{5,4},{6,7},{7,6},{8,9},{9,8},{10,11... | collective-permute-start | bytes 3538952 | tf_op jit(solution)/shard_map/ppermute | solution.py:622
  72.9 9.2 %copy-start.1 = (bf16[2,4,4,24,768]{4,3,2,1,0:T(8,128)(2,1)}, bf16[2,4,4,24,768]{4,3,2,1,0:T(8,128)(2,1)S(1)}, u32[]{:S(2)}) copy-start(bf16[2,4,4,24,768]{4,3,2,1,0:T(8,128)(2,1)S(1)} %pad_maximum_fusion.refs_1_) | copy-start | bytes 3538948
  72.9 25.8 %collective-permute-start.14 = (bf16[2,4,4,24,768]{4,3,2,1,0:T(8,128)(2,1)S(1)}, bf16[2,4,4,24,768]{4,3,2,1,0:T(8,128)(2,1)S(1)}, u32[]{:S(2)}, u32[]{:S(2)}) collective-permute-start(bf16[2,4,4,24,768]{4,3,2,1,0:T(8,128)(2,1)S(1)} %pad_maximum_fusion.refs_1_), channel_id=1, source_target_pairs={{0,16},{1,17},{2,18},{3,19},{4,20},{5,21},{6,22},{7,23},{8,24},{9,... | collective-permute-start | bytes 3538952 | tf_op jit(solution)/shard_map/ppermute | solution.py:622
  82.1 17.2 %collective-permute-start.17 = (bf16[2,4,4,24,768]{4,3,2,1,0:T(8,128)(2,1)S(1)}, bf16[2,4,4,24,768]{4,3,2,1,0:T(8,128)(2,1)S(1)}, u32[]{:S(2)}, u32[]{:S(2)}) collective-permute-start(bf16[2,4,4,24,768]{4,3,2,1,0:T(8,128)(2,1)S(1)} %pad_maximum_fusion.1.refs_5_), channel_id=1, source_target_pairs={{0,8},{1,9},{2,10},{3,11},{4,12},{5,13},{6,14},{7,15},{8,0},{9,1},... | collective-permute-start | bytes 3538952 | tf_op jit(solution)/shard_map/ppermute | solution.py:622
  82.1 17.1 %collective-permute-start.13 = (bf16[2,4,4,24,768]{4,3,2,1,0:T(8,128)(2,1)S(1)}, bf16[2,4,4,24,768]{4,3,2,1,0:T(8,128)(2,1)S(1)}, u32[]{:S(2)}, u32[]{:S(2)}) collective-permute-start(bf16[2,4,4,24,768]{4,3,2,1,0:T(8,128)(2,1)S(1)} %pad_maximum_fusion.refs_1_), channel_id=1, source_target_pairs={{0,8},{1,9},{2,10},{3,11},{4,12},{5,13},{6,14},{7,15},{8,0},{9,1},... | collective-permute-start | bytes 3538952 | tf_op jit(solution)/shard_map/ppermute | solution.py:622
  97.3 6.1 %copy-start.7 = (bf16[2,4,4,24,768]{4,3,2,1,0:T(8,128)(2,1)}, bf16[2,4,4,24,768]{4,3,2,1,0:T(8,128)(2,1)S(1)}, u32[]{:S(2)}) copy-start(bf16[2,4,4,24,768]{4,3,2,1,0:T(8,128)(2,1)S(1)} %collective-permute-done.15.refs_7_) | copy-start | bytes 3538948
  98.7 4.7 %copy-start.8 = (bf16[2,4,4,24,768]{4,3,2,1,0:T(8,128)(2,1)}, bf16[2,4,4,24,768]{4,3,2,1,0:T(8,128)(2,1)S(1)}, u32[]{:S(2)}) copy-start(bf16[2,4,4,24,768]{4,3,2,1,0:T(8,128)(2,1)S(1)} %collective-permute-done.14.refs_3_) | copy-start | bytes 3538948
  98.7 4.5 %collective-permute-start.16 = (bf16[2,4,4,24,768]{4,3,2,1,0:T(8,128)(2,1)S(1)}, bf16[2,4,4,24,768]{4,3,2,1,0:T(8,128)(2,1)S(1)}, u32[]{:S(2)}, u32[]{:S(2)}) collective-permute-start(bf16[2,4,4,24,768]{4,3,2,1,0:T(8,128)(2,1)S(1)} %collective-permute-done.14.refs_3_), channel_id=1, source_target_pairs={{0,8},{1,9},{2,10},{3,11},{4,12},{5,13},{6,14},{7,15},{8,0},{9,1},... | collective-permute-start | bytes 3538952 | tf_op jit(solution)/shard_map/ppermute | solution.py:622
  98.7 4.7 %collective-permute-start.18 = (bf16[2,4,4,24,768]{4,3,2,1,0:T(8,128)(2,1)S(1)}, bf16[2,4,4,24,768]{4,3,2,1,0:T(8,128)(2,1)}, u32[]{:S(2)}, u32[]{:S(2)}) collective-permute-start(bf16[2,4,4,24,768]{4,3,2,1,0:T(8,128)(2,1)S(1)} %collective-permute-done.15.refs_7_), channel_id=1, source_target_pairs={{0,8},{1,9},{2,10},{3,11},{4,12},{5,13},{6,14},{7,15},{8,0},{9,1},... | collective-permute-start | bytes 3538952 | tf_op jit(solution)/shard_map/ppermute | solution.py:622
  99.2 4.2 %copy-start.9 = (bf16[2,4,4,24,768]{4,3,2,1,0:T(8,128)(2,1)}, bf16[2,4,4,24,768]{4,3,2,1,0:T(8,128)(2,1)S(1)}, u32[]{:S(2)}) copy-start(bf16[2,4,4,24,768]{4,3,2,1,0:T(8,128)(2,1)S(1)} %collective-permute-done.17.refs_6_) | copy-start | bytes 3538948
  99.2 4.2 %copy-start.10 = (bf16[2,4,4,24,768]{4,3,2,1,0:T(8,128)(2,1)}, bf16[2,4,4,24,768]{4,3,2,1,0:T(8,128)(2,1)S(1)}, u32[]{:S(2)}) copy-start(bf16[2,4,4,24,768]{4,3,2,1,0:T(8,128)(2,1)S(1)} %collective-permute-done.13.refs_2_) | copy-start | bytes 3538948
  103.2 1.0 copy-start.11
  270.2 15.7 %collective-permute-start.19 = (bf16[2,2,4,4,24,768]{5,4,3,2,1,0:T(8,128)(2,1)}, bf16[2,2,4,4,24,768]{5,4,3,2,1,0:T(8,128)(2,1)}, u32[]{:S(2)}, u32[]{:S(2)}) collective-permute-start(bf16[2,2,4,4,24,768]{5,4,3,2,1,0:T(8,128)(2,1)} %get-tuple-element.135), channel_id=1, source_target_pairs={{0,8},{1,9},{2,10},{3,11},{4,12},{5,13},{6,14},{7,15},{8,0},{9,1},... | collective-permute-start | bytes 7077896 | tf_op jit(solution)/shard_map/ppermute | solution.py:622
  270.3 15.5 %copy-start.4 = (bf16[2,2,4,4,24,768]{5,4,3,2,1,0:T(8,128)(2,1)S(1)}, bf16[2,2,4,4,24,768]{5,4,3,2,1,0:T(8,128)(2,1)}, u32[]{:S(2)}) copy-start(bf16[2,2,4,4,24,768]{5,4,3,2,1,0:T(8,128)(2,1)} %get-tuple-element.134) | copy-start | bytes 7077892
  285.5 4.9 %collective-permute-start.20 = (bf16[2,2,4,4,24,768]{5,4,3,2,1,0:T(8,128)(2,1)}, bf16[2,2,4,4,24,768]{5,4,3,2,1,0:T(8,128)(2,1)}, u32[]{:S(2)}, u32[]{:S(2)}) collective-permute-start(bf16[2,2,4,4,24,768]{5,4,3,2,1,0:T(8,128)(2,1)} %get-tuple-element.138), channel_id=1, source_target_pairs={{0,8},{1,9},{2,10},{3,11},{4,12},{5,13},{6,14},{7,15},{8,0},{9,1},... | collective-permute-start | bytes 7077896 | tf_op jit(solution)/shard_map/ppermute | solution.py:622
  285.8 4.5 %copy-start.5 = (bf16[2,2,4,4,24,768]{5,4,3,2,1,0:T(8,128)(2,1)S(1)}, bf16[2,2,4,4,24,768]{5,4,3,2,1,0:T(8,128)(2,1)}, u32[]{:S(2)}) copy-start(bf16[2,2,4,4,24,768]{5,4,3,2,1,0:T(8,128)(2,1)} %get-tuple-element.137) | copy-start | bytes 7077892
  292.7 28.3 %collective-permute-start.22 = (bf16[2,4,4,24,768]{4,3,2,1,0:T(8,128)(2,1)S(1)}, bf16[2,4,4,24,768]{4,3,2,1,0:T(8,128)(2,1)S(1)}, u32[]{:S(2)}, u32[]{:S(2)}) collective-permute-start(bf16[2,4,4,24,768]{4,3,2,1,0:T(8,128)(2,1)S(1)} %get-tuple-element.170), channel_id=1, source_target_pairs={{0,16},{1,17},{2,18},{3,19},{4,20},{5,21},{6,22},{7,23},{8,24},{9,... | collective-permute-start | bytes 3538952 | tf_op jit(solution)/shard_map/ppermute | solution.py:622
  294.2 27.9 %collective-permute-start.21 = (bf16[2,4,4,24,768]{4,3,2,1,0:T(8,128)(2,1)S(1)}, bf16[2,4,4,24,768]{4,3,2,1,0:T(8,128)(2,1)S(1)}, u32[]{:S(2)}, u32[]{:S(2)}) collective-permute-start(bf16[2,4,4,24,768]{4,3,2,1,0:T(8,128)(2,1)S(1)} %get-tuple-element.172), channel_id=1, source_target_pairs={{0,1},{1,0},{2,3},{3,2},{4,5},{5,4},{6,7},{7,6},{8,9},{9,8},{10,11... | collective-permute-start | bytes 3538952 | tf_op jit(solution)/shard_map/ppermute | solution.py:622
  321.3 17.4 %collective-permute-start.23 = (bf16[4,4,24,768]{3,2,1,0:T(8,128)(2,1)S(1)}, bf16[4,4,24,768]{3,2,1,0:T(8,128)(2,1)S(1)}, u32[]{:S(2)}, u32[]{:S(2)}) collective-permute-start(bf16[4,4,24,768]{3,2,1,0:T(8,128)(2,1)S(1)} %get-tuple-element.178), channel_id=1, source_target_pairs={{0,1},{1,0},{2,3},{3,2},{4,5},{5,4},{6,7},{7,6},{8,9},{9,8},{10,11... | collective-permute-start | bytes 1769480 | tf_op jit(solution)/shard_map/ppermute | solution.py:622
  322.5 16.3 %collective-permute-start.24 = (bf16[4,4,24,768]{3,2,1,0:T(8,128)(2,1)S(1)}, bf16[4,4,24,768]{3,2,1,0:T(8,128)(2,1)S(1)}, u32[]{:S(2)}, u32[]{:S(2)}) collective-permute-start(bf16[4,4,24,768]{3,2,1,0:T(8,128)(2,1)S(1)} %get-tuple-element.180), channel_id=1, source_target_pairs={{0,16},{1,17},{2,18},{3,19},{4,20},{5,21},{6,22},{7,23},{8,24},{9,... | collective-permute-start | bytes 1769480 | tf_op jit(solution)/shard_map/ppermute | solution.py:622
  340.1 16.9 %collective-permute-start.25 = (bf16[2,2,4,5,24,384]{5,4,3,2,1,0:T(8,128)(2,1)}, bf16[2,2,4,5,24,384]{5,4,3,2,1,0:T(8,128)(2,1)S(1)}, u32[]{:S(2)}, u32[]{:S(2)}) collective-permute-start(bf16[2,2,4,5,24,384]{5,4,3,2,1,0:T(8,128)(2,1)} %get-tuple-element.164), channel_id=1, source_target_pairs={{0,8},{1,9},{2,10},{3,11},{4,12},{5,13},{6,14},{7,15},{8,0},{9,1},... | collective-permute-start | bytes 4423688 | tf_op jit(solution)/shard_map/ppermute | solution.py:622
  349.4 4.0 collective-permute-start.26
  349.9 36.4 %all-to-all-start.2 = ((bf16[4,8,24,768]{3,2,1,0:T(8,128)(2,1)}), bf16[4,8,24,768]{3,2,1,0:T(8,128)(2,1)S(1)}, u32[]{:S(2)}, u32[]{:S(2)}) async-start(bf16[4,8,24,768]{3,2,1,0:T(8,128)(2,1)} %pad_maximum_fusion.2), calls=%async_computation.2 | async-start | bytes 2359296 | tf_op jit(solution)/shard_map/all_to_all | solution.py:626
  353.4 3.6 copy-start.6
  355.5 15.3 %collective-permute-start.29 = (bf16[2,4,4,24,384]{4,3,2,1,0:T(8,128)(2,1)S(1)}, bf16[2,4,4,24,384]{4,3,2,1,0:T(8,128)(2,1)S(1)}, u32[]{:S(2)}, u32[]{:S(2)}) collective-permute-start(bf16[2,4,4,24,384]{4,3,2,1,0:T(8,128)(2,1)S(1)} %get-tuple-element.176), channel_id=1, source_target_pairs={{0,1},{1,0},{2,3},{3,2},{4,5},{5,4},{6,7},{7,6},{8,9},{9,8},{10,11... | collective-permute-start | bytes 1769480 | tf_op jit(solution)/shard_map/ppermute | solution.py:622
  357.4 19.5 %collective-permute-start.27 = (bf16[2,4,5,24,384]{4,3,2,1,0:T(8,128)(2,1)S(1)}, bf16[2,4,5,24,384]{4,3,2,1,0:T(8,128)(2,1)S(1)}, u32[]{:S(2)}, u32[]{:S(2)}) collective-permute-start(bf16[2,4,5,24,384]{4,3,2,1,0:T(8,128)(2,1)S(1)} %get-tuple-element.174), channel_id=1, source_target_pairs={{0,16},{1,17},{2,18},{3,19},{4,20},{5,21},{6,22},{7,23},{8,24},{9,... | collective-permute-start | bytes 2211848 | tf_op jit(solution)/shard_map/ppermute | solution.py:622
  370.9 11.0 %collective-permute-start.30 = (bf16[4,4,24,384]{3,2,1,0:T(8,128)(2,1)S(1)}, bf16[4,4,24,384]{3,2,1,0:T(8,128)(2,1)S(1)}, u32[]{:S(2)}, u32[]{:S(2)}) collective-permute-start(bf16[4,4,24,384]{3,2,1,0:T(8,128)(2,1)S(1)} %get-tuple-element.184), channel_id=1, source_target_pairs={{0,16},{1,17},{2,18},{3,19},{4,20},{5,21},{6,22},{7,23},{8,24},{9,... | collective-permute-start | bytes 884744 | tf_op jit(solution)/shard_map/ppermute | solution.py:622
  377.1 8.2 %collective-permute-start.28 = (bf16[4,5,24,384]{3,2,1,0:T(8,128)(2,1)S(1)}, bf16[4,5,24,384]{3,2,1,0:T(8,128)(2,1)S(1)}, u32[]{:S(2)}, u32[]{:S(2)}) collective-permute-start(bf16[4,5,24,384]{3,2,1,0:T(8,128)(2,1)S(1)} %get-tuple-element.182), channel_id=1, source_target_pairs={{0,1},{1,0},{2,3},{3,2},{4,5},{5,4},{6,7},{7,6},{8,9},{9,8},{10,11... | collective-permute-start | bytes 1105928 | tf_op jit(solution)/shard_map/ppermute | solution.py:622
  386.3 18.2 %all-to-all-start.1 = ((bf16[4,9,24,384]{3,2,1,0:T(8,128)(2,1)}), bf16[4,9,24,384]{3,2,1,0:T(8,128)(2,1)S(1)}, u32[]{:S(2)}, u32[]{:S(2)}) async-start(bf16[4,9,24,384]{3,2,1,0:T(8,128)(2,1)} %pad_maximum_fusion.4), calls=%async_computation.1 | async-start | bytes 1327104 | tf_op jit(solution)/shard_map/all_to_all | solution.py:626

commit v10 on v9

--- a/solution.py
+++ b/solution.py
@@ -665,8 +665,9 @@
 def pack_two_body(wi_ref, wb_ref, two_ref):
     rows = wi_ref.shape[0]
     for i in range(4):
-        two_ref[i] = wi_ref[:, i * D : (i + 1) * D]
-        two_ref[4 + i] = wb_ref[i * rows : (i + 1) * rows]
+        for to in range(4):
+            two_ref[to, i] = wi_ref[:, i * D : (i + 1) * D]
+            two_ref[to, 4 + i] = wb_ref[i * rows : (i + 1) * rows]
 
 
 def pack_two(w_in, w_back):
@@ -675,8 +676,8 @@
         pack_two_body,
         grid=(1,),
         in_specs=[whole_block(w_in), whole_block(w_back)],
-        out_specs=pl.BlockSpec((8, rows, D), lambda *_: (0, 0, 0)),
-        out_shape=jax.ShapeDtypeStruct((8, rows, D), BF),
+        out_specs=pl.BlockSpec((4, 8, rows, D), lambda *_: (0, 0, 0, 0)),
+        out_shape=jax.ShapeDtypeStruct((4, 8, rows, D), BF),
         compiler_params=params(),
         name="pack_two",
     )(w_in, w_back)
@@ -767,10 +768,10 @@
 
 
 class Gather:
-    def __init__(self, grid, packet, first, at_once):
+    def __init__(self, grid, packet, first, at_once, *others):
         self.grid, self.first = grid, first
         if at_once:
-            self.ring = grid.trade(jnp.broadcast_to(packet, (4,) + packet.shape))
+            self.ring = grid.trade(after(packet, *others))
         else:
             self.ring = jnp.stack([packet] + [grid.send(packet, Z, k) for k in range(1, 4)])
 
@@ -843,8 +844,7 @@
     core = core.astype(jnp.int32)[None]
     vectors = [bias_q, bias_v, bias_out, gain_one, shift_one, bias_back, gain_two, shift_two]
     one = Gather(grid, pack_one(w_qkv, w_out, vectors, bias_in), 2 * rows // 8, False)
-    packet = after(pack_two(w_in, w_back), one.ring)
-    two = Gather(grid, packet, 4, True)
+    two = Gather(grid, pack_two(w_in, w_back), 4, True, one.ring)
     one.one()
     one.two()
     two.one(*one.far)
@@ -880,7 +880,8 @@
     steps += sum_in.one(*steps)
     e_0, *lines_0 = attend_back_call(qkv, after(dctx, *steps), lse, lengths, 0, 1)
     e_1, *lines_1 = attend_back_call(qkv, after(dctx, e_0), lse, lengths, 1, 1)
-    steps = sum_back.two(e_1) + sum_in.two(e_1)
+    steps = sum_back.two(e_1)
+    steps += sum_in.two(*steps)
     others = [ctx2, ctx1, ea_2, ea_1]
     group = wgrad_heads_call(core, after(low2, *steps), low1, e_qkv_2, e_0, rows, 0, others, True)
     line, total = along_z(grid, [sum_in.three(group[0]), sum_back.three(group[0])])

time: 416 us -> 413 us (level)
  transfers between devices with their start and end apart: 34 -> 34, of which waited for: 19 -> 18; matrix products, arithmetic and copies ran while one was open for 3% -> 3% of each run, Pallas kernels for 25% -> 25%
where the time goes in v10:
time: 413 us; the launch traced here: 406 us
  Pallas kernels  269 us (65%)
  waiting for transfers between devices  71.6 us (17%)
  starting transfers between devices  44.2 us (11%)
  other arithmetic  13.7 us (3%)
  local copies, waits for them, and re-layouts  5.51 us (1%)
    ppermute x31, waiting for transfers between devices, send(): return lax.ppermute(value, AXES, self.shift(dim, step))  56.5 us
    pallas_call x2, Pallas kernels, ffn_back_call(): pl.pallas_call(ffn_back_body, grid=(rows // block,), in_specs=[line, line...  47.7 us
    pallas_call x3, Pallas kernels, attend_back_call(): pl.pallas_call(body, grid_spec=pltpu.PrefetchScalarGridSpec(num_scalar_pr...  46.6 us
    pallas_call x2, Pallas kernels, ffn_call(): pl.pallas_call(lambda *refs: ffn_body(renorm, *refs), grid=(rows // block...  44.7 us
    ppermute x31, starting transfers between devices, send(): return lax.ppermute(value, AXES, self.shift(dim, step))  30 us
    pallas_call x2, Pallas kernels, attend_call(): pl.pallas_call(body, grid_spec=pltpu.PrefetchScalarGridSpec(num_scalar_pr...  24.8 us
    pallas_call x2, Pallas kernels, wgrad_heads_call(): pl.pallas_call(body, grid_spec=pltpu.PrefetchScalarGridSpec(num_scalar_pr...  24.2 us
    pallas_call x2, Pallas kernels, dx_call(): pl.pallas_call(dx_body, grid=(rows // block,), in_specs=[line, *specs, on...  17.7 us
  transfers between devices with their start and end apart: 34, of which 18 were waited for; matrix products, arithmetic and copies ran while one was open for 3% of the time, Pallas kernels for 25%

profile of v10, /device:TPU:0, one launch (start us, length us, event | category | flops | bytes accessed | tf_op | source)
XLA Modules:
  0.0 405.7 jit_solution(11858785895646578772)
XLA Ops:
  0.7 1.7 pack_one.1
  2.3 3.0 collective-permute-start
  5.4 2.6 collective-permute-start.1
  7.9 1.3 collective-permute-start.2
  9.3 2.1 pack_two.1
  11.4 1.3 collective-permute-done
  12.7 6.0 %collective-permute-done.1 = bf16[13,8,768]{2,1,0:T(8,128)(2,1)S(1)} collective-permute-done((bf16[13,8,768]{2,1,0:T(8,128)(2,1)}, bf16[13,8,768]{2,1,0:T(8,128)(2,1)S(1)}, u32[]{:S(2)}, u32[]{:S(2)}) %collective-permute-start.1) | collective-permute-done | bytes 159776 | tf_op jit(solution)/shard_map/ppermute | solution.py:622
  18.8 6.2 %all-to-all-start = ((bf16[4,8,24,768]{3,2,1,0:T(8,128)(2,1)}), bf16[4,8,24,768]{3,2,1,0:T(8,128)(2,1)S(1)}, u32[]{:S(2)}, u32[]{:S(2)}) async-start(bf16[4,8,24,768]{3,2,1,0:T(8,128)(2,1)} %pack_two.1), calls=%async_computation | async-start | bytes 2359296 | tf_op jit(solution)/shard_map/all_to_all | solution.py:626
  25.0 1.6 collective-permute-start.6
  26.6 1.6 collective-permute-start.3
  28.2 5.6 %collective-permute-done.6 = bf16[4,7,8,768]{3,2,1,0:T(8,128)(2,1)S(1)} collective-permute-done((bf16[4,7,8,768]{3,2,1,0:T(8,128)(2,1)S(1)}, bf16[4,7,8,768]{3,2,1,0:T(8,128)(2,1)S(1)}, u32[]{:S(2)}, u32[]{:S(2)}) %collective-permute-start.6) | collective-permute-done | bytes 344096 | tf_op jit(solution)/shard_map/ppermute | solution.py:622
  33.9 1.6 collective-permute-start.7
  35.5 1.6 collective-permute-start.5
  37.6 10.9 %collective-permute-done.5.refs_3_ = bf16[2,4,2,24,768]{4,3,2,1,0:T(8,128)(2,1)} collective-permute-done((bf16[2,4,2,24,768]{4,3,2,1,0:T(8,128)(2,1)S(1)}, bf16[2,4,2,24,768]{4,3,2,1,0:T(8,128)(2,1)}, u32[]{:S(2)}, u32[]{:S(2)}) %collective-permute-start.5) | collective-permute-done | bytes 589856 | tf_op jit(solution)/shard_map/ppermute | solution.py:622
  49.7 3.0 all-to-all-done
  52.7 0.9 fusion.17
  53.6 1.5 collective-permute-start.12
  55.1 1.5 collective-permute-start.11
  57.2 6.4 %place.2 = (bf16[2,2,2,4,2,24,768]{6,5,4,3,2,1,0:T(8,128)(2,1)}, bf16[2,2,2,4,2,3,8,768]{7,6,5,4,3,2,1,0:T(8,128)(2,1)}, f32[24,768]{1,0:T(8,128)}) custom-call(s32[4]{0:T(128)} %pad_add_fusion.refs_0_, bf16[2,4,2,24,768]{4,3,2,1,0:T(8,128)(2,1)} %copy-done.3, bf16[2,4,2,24,768]{4,3,2,1,0:T(8,128)(2,1)} %collective-permute-done.4.refs_2_, ...), custom_call_target="tpu_custom_call" | custom-call | flops 1200000000 | bytes 600000 | tf_op jit(solution)/shard_map/place/pallas_call | solution.py:750
  63.6 4.5 %collective-permute-done.12 = bf16[4,4,24,768]{3,2,1,0:T(8,128)(2,1)S(1)} collective-permute-done((bf16[4,4,24,768]{3,2,1,0:T(8,128)(2,1)}, bf16[4,4,24,768]{3,2,1,0:T(8,128)(2,1)S(1)}, u32[]{:S(2)}, u32[]{:S(2)}) %collective-permute-start.12) | collective-permute-done | bytes 589856 | tf_op jit(solution)/shard_map/ppermute | solution.py:622
  68.1 1.2 pad_maximum_fusion.1.refs_5_
  69.3 1.6 collective-permute-start.15
  71.0 1.6 collective-permute-start.14
  72.5 7.6 %qkv.2.refs_1_.refs_2_.refs_3_ = bf16[1024,2304]{1,0:T(8,128)(2,1)} custom-call(bf16[1024,768]{1,0:T(8,128)(2,1)} %c_ref.3, bf16[2,768,768]{2,1,0:T(8,128)(2,1)} %bitcast.115, bf16[2,768,768]{2,1,0:T(8,128)(2,1)} %bitcast.99, f32[24,768]{1,0:T(8,128)} %get-tuple-element.98.vec_ref.refs_2_), custom_call_target="tpu_custom_call" | custom-call | flops 1600000000 | bytes 800000 | tf_op jit(solution)/shard_map/qkv/pallas_call | solution.py:75
  80.7 12.2 %attend.2 = (bf16[1024,768]{1,0:T(8,128)(2,1)}, f32[2,6,2,512]{3,2,1,0:T(2,128)}) custom-call(s32[2]{0:T(128)} %refs_0_.11, bf16[1024,2304]{1,0:T(8,128)(2,1)} %qkv.2.refs_1_.refs_2_.refs_3_, bf16[1024,2304]{1,0:T(8,128)(2,1)} %qkv.2.refs_1_.refs_2_.refs_3_, bf16[1024,2304]{1,0:T(8,128)(2,1)} %qkv.2.refs_1_.refs_2_.refs_3_), custom_call_target="tpu_custom_call" | custom-call | flops 2600000000 | bytes 1300000 | tf_op jit(solution)/shard_map/attend/pallas_call | solution.py:137
  92.9 2.4 collective-permute-done.15.refs_7_
  95.3 1.4 collective-permute-done.14.refs_3_
  97.3 4.0 collective-permute-done.16.refs_4_
  101.5 0.8 copy-done.11
  102.3 8.2 %place.3 = (bf16[4,2,2,4,2,24,768]{6,5,4,3,2,1,0:T(8,128)(2,1)}, bf16[2,2,4,2,4,24,768]{6,5,4,3,2,1,0:T(8,128)(2,1)}) custom-call(s32[4]{0:T(128)} %pad_add_fusion.refs_0_, bf16[2,4,4,24,768]{4,3,2,1,0:T(8,128)(2,1)} %copy-done.1, bf16[2,4,4,24,768]{4,3,2,1,0:T(8,128)(2,1)} %copy-done.10, bf16[2,4,4,24,768]{4,3,2,1,0:T(8,128)(2,1)} %copy-done.8, ...), custom_call_target="tpu_custom_call" | custom-call | flops 1200000000 | bytes 600000 | tf_op jit(solution)/shard_map/place/pallas_call | solution.py:750
  110.6 22.3 %ffn.2 = (f32[1024,768]{1,0:T(8,128)}, bf16[1024,768]{1,0:T(8,128)(2,1)}, bf16[1024,3072]{1,0:T(8,128)(2,1)}, bf16[1024,3072]{1,0:T(8,128)(2,1)}, f32[1024,768]{1,0:T(8,128)}, /*index=5*/bf16[1024,768]{1,0:T(8,128)(2,1)}) custom-call(bf16[1024,768]{1,0:T(8,128)(2,1)} %c_ref.3, bf16[1024,768]{1,0:T(8,128)(2,1)} %get-tuple-element.104.refs_1_.rest_1_, ...), custom_call_target="tpu_custom_call" | custom-call | flops 4400000000 | bytes 2200000 | tf_op jit(solution)/shard_map/ffn/pallas_call | solution.py:237
  132.8 7.6 %qkv.3.refs_1_.refs_2_.refs_3_ = bf16[1024,2304]{1,0:T(8,128)(2,1)} custom-call(bf16[1024,768]{1,0:T(8,128)(2,1)} %get-tuple-element.152.x_ref.a_ref, bf16[2,768,768]{2,1,0:T(8,128)(2,1)} %bitcast.116, bf16[2,768,768]{2,1,0:T(8,128)(2,1)} %bitcast.101, f32[24,768]{1,0:T(8,128)} %get-tuple-element.98.vec_ref.refs_2_), custom_call_target="tpu_custom_call" | custom-call | flops 1600000000 | bytes 800000 | tf_op jit(solution)/shard_map/qkv/pallas_call | solution.py:75
  140.4 12.5 %attend.3 = (bf16[1024,768]{1,0:T(8,128)(2,1)}, f32[2,6,2,512]{3,2,1,0:T(2,128)}) custom-call(s32[2]{0:T(128)} %refs_0_.11, bf16[1024,2304]{1,0:T(8,128)(2,1)} %qkv.3.refs_1_.refs_2_.refs_3_, bf16[1024,2304]{1,0:T(8,128)(2,1)} %qkv.3.refs_1_.refs_2_.refs_3_, bf16[1024,2304]{1,0:T(8,128)(2,1)} %qkv.3.refs_1_.refs_2_.refs_3_), custom_call_target="tpu_custom_call" | custom-call | flops 2600000000 | bytes 1300000 | tf_op jit(solution)/shard_map/attend/pallas_call | solution.py:137
  152.9 22.5 %ffn.3 = (f32[1024,768]{1,0:T(8,128)}, bf16[1024,768]{1,0:T(8,128)(2,1)}, bf16[1024,3072]{1,0:T(8,128)(2,1)}, bf16[1024,3072]{1,0:T(8,128)(2,1)}, f32[1024,768]{1,0:T(8,128)}, /*index=5*/bf16[1024,768]{1,0:T(8,128)(2,1)}) custom-call(f32[1024,768]{1,0:T(8,128)} %get-tuple-element.109.refs_0_.z2_ref, bf16[1024,768]{1,0:T(8,128)(2,1)} %get-tuple-element.111.refs_1_.rest_0_, ...), custom_call_target="tpu_custom_call" | custom-call | flops 4400000000 | bytes 2200000 | tf_op jit(solution)/shard_map/ffn/pallas_call | solution.py:237
  175.4 23.8 %ffn_back.2 = (bf16[1024,768]{1,0:T(8,128)(2,1)}, bf16[1024,3072]{1,0:T(8,128)(2,1)}, f32[1024,768]{1,0:T(8,128)}, bf16[1024,768]{1,0:T(8,128)(2,1)}, bf16[1024,768]{1,0:T(8,128)(2,1)}, /*index=5*/f32[24,768]{1,0:T(8,128)}) custom-call(bf16[1024,768]{1,0:T(8,128)(2,1)} %dy_ref.1, f32[1024,768]{1,0:T(8,128)} %get-tuple-element.113.z2_ref, ...), custom_call_target="tpu_custom_call" | custom-call | flops 4800000000 | bytes 2400000 | tf_op jit(solution)/shard_map/ffn_back/pallas_call | solution.py:319
  199.2 21.7 %attend_back.3 = (bf16[3,1024,768]{2,1,0:T(8,128)(2,1)}, f32[2,1,768]{2,1,0:T(1,128)}, f32[2,1,768]{2,1,0:T(1,128)}) custom-call(s32[2]{0:T(128)} %refs_0_.11, bf16[1024,2304]{1,0:T(8,128)(2,1)} %qkv.3.refs_1_.refs_2_.refs_3_, bf16[1024,2304]{1,0:T(8,128)(2,1)} %qkv.3.refs_1_.refs_2_.refs_3_, bf16[1024,2304]{1,0:T(8,128)(2,1)} %qkv.3.refs_1_.refs_2_.refs_3_, ...), custom_call_target="tpu_custom_call" | custom-call | flops 4800000000 | bytes 2400000 | tf_op jit(solution)/shard_map/attend_back/pallas_call | solution.py:395
  220.9 8.4 %dx.2.dy_ref = f32[1024,768]{1,0:T(8,128)} custom-call(f32[1024,768]{1,0:T(8,128)} %get-tuple-element.116.dz1_ref, bf16[3,1024,768]{2,1,0:T(8,128)(2,1)} %get-tuple-element.119.rest_0_.b_ref, bf16[2,768,768]{2,1,0:T(8,128)(2,1)} %bitcast.117, bf16[2,768,768]{2,1,0:T(8,128)(2,1)} %bitcast.104), custom_call_target="tpu_custom_call" | custom-call | flops 1800000000 | bytes 900000 | tf_op jit(solution)/shard_map/dx/pallas_call | solution.py:434
  229.4 23.9 %ffn_back.3 = (bf16[1024,768]{1,0:T(8,128)(2,1)}, bf16[1024,3072]{1,0:T(8,128)(2,1)}, f32[1024,768]{1,0:T(8,128)}, bf16[1024,768]{1,0:T(8,128)(2,1)}, bf16[1024,768]{1,0:T(8,128)(2,1)}, /*index=5*/f32[24,768]{1,0:T(8,128)}) custom-call(f32[1024,768]{1,0:T(8,128)} %dx.2.dy_ref, f32[1024,768]{1,0:T(8,128)} %get-tuple-element.109.refs_0_.z2_ref, ...), custom_call_target="tpu_custom_call" | custom-call | flops 4800000000 | bytes 2400000 | tf_op jit(solution)/shard_map/ffn_back/pallas_call | solution.py:319
  253.2 15.0 %wgrad_back.1 = (bf16[2,2,4,4,24,768]{5,4,3,2,1,0:T(8,128)(2,1)}, bf16[2,2,4,4,24,768]{5,4,3,2,1,0:T(8,128)(2,1)}) custom-call(s32[1]{0:T(128)} %bitcast.1.core_ref, bf16[1024,3072]{1,0:T(8,128)(2,1)} %get-tuple-element.123.g2k.g2s, bf16[1024,3072]{1,0:T(8,128)(2,1)} %get-tuple-element.124.g1k.g1s, bf16[1024,3072]{1,0:T(8,128)(2,1)} %get-tuple-element.123.g2k.g2s, ...), custom_call_target="tpu_custom_call" | custom-call | flops 3000000000 | bytes 1500000 | tf_op jit(solution)/shard_map/wgrad_back/pallas_call | solution.py:576
  268.4 15.2 %wgrad_in.1 = (bf16[2,2,4,4,24,768]{5,4,3,2,1,0:T(8,128)(2,1)}, bf16[2,2,4,4,24,768]{5,4,3,2,1,0:T(8,128)(2,1)}) custom-call(s32[1]{0:T(128)} %bitcast.1.core_ref, bf16[1024,768]{1,0:T(8,128)(2,1)} %get-tuple-element.129.a_ref, bf16[1024,768]{1,0:T(8,128)(2,1)} %get-tuple-element.130.c_ref, bf16[1024,3072]{1,0:T(8,128)(2,1)} %get-tuple-element.131.b_ref, ...), custom_call_target="tpu_custom_call" | custom-call | flops 3000000000 | bytes 1500000 | tf_op jit(solution)/shard_map/wgrad_in/pallas_call | solution.py:475
  283.9 2.5 fusion
  287.0 1.4 collective-permute-done.20
  288.4 2.3 fusion.3
  290.7 1.6 collective-permute-start.22
  292.3 12.5 %attend_back.4 = (bf16[3,1024,384]{2,1,0:T(8,128)(2,1)}, f32[2,1,384]{2,1,0:T(1,128)}, f32[2,1,384]{2,1,0:T(1,128)}) custom-call(s32[2]{0:T(128)} %refs_0_.11, bf16[1024,2304]{1,0:T(8,128)(2,1)} %qkv.2.refs_1_.refs_2_.refs_3_, bf16[1024,2304]{1,0:T(8,128)(2,1)} %qkv.2.refs_1_.refs_2_.refs_3_, bf16[1024,2304]{1,0:T(8,128)(2,1)} %qkv.2.refs_1_.refs_2_.refs_3_, ...), custom_call_target="tpu_custom_call" | custom-call | flops 2400000000 | bytes 1200000 | tf_op jit(solution)/shard_map/attend_back/pallas_call | solution.py:395
  304.8 12.3 %attend_back.5 = (bf16[3,1024,384]{2,1,0:T(8,128)(2,1)}, f32[2,1,384]{2,1,0:T(1,128)}, f32[2,1,384]{2,1,0:T(1,128)}) custom-call(s32[2]{0:T(128)} %refs_0_.11, bf16[1024,2304]{1,0:T(8,128)(2,1)} %qkv.2.refs_1_.refs_2_.refs_3_, bf16[1024,2304]{1,0:T(8,128)(2,1)} %qkv.2.refs_1_.refs_2_.refs_3_, bf16[1024,2304]{1,0:T(8,128)(2,1)} %qkv.2.refs_1_.refs_2_.refs_3_, ...), custom_call_target="tpu_custom_call" | custom-call | flops 2400000000 | bytes 1200000 | tf_op jit(solution)/shard_map/attend_back/pallas_call | solution.py:395
  317.4 1.6 collective-permute-done.22
  319.9 1.5 collective-permute-start.24
  321.4 14.9 %wgrad_heads.2 = (bf16[2,2,4,5,24,384]{5,4,3,2,1,0:T(8,128)(2,1)}, bf16[2,2,4,5,24,384]{5,4,3,2,1,0:T(8,128)(2,1)}) custom-call(s32[1]{0:T(128)} %bitcast.1.core_ref, bf16[1024,768]{1,0:T(8,128)(2,1)} %get-tuple-element.152.x_ref.a_ref, bf16[1024,768]{1,0:T(8,128)(2,1)} %c_ref.3, bf16[3,1024,768]{2,1,0:T(8,128)(2,1)} %get-tuple-element.119.rest_0_.b_ref, ...), custom_call_target="tpu_custom_call" | custom-call | flops 2400000000 | bytes 1200000 | tf_op jit(solution)/shard_map/wgrad_heads/pallas_call | solution.py:540
  336.6 1.2 pad_maximum_fusion.2
  337.8 9.3 %wgrad_heads.3 = (bf16[2,2,4,4,24,384]{5,4,3,2,1,0:T(8,128)(2,1)}, bf16[2,2,4,4,24,384]{5,4,3,2,1,0:T(8,128)(2,1)}) custom-call(s32[1]{0:T(128)} %bitcast.1.core_ref, bf16[1024,768]{1,0:T(8,128)(2,1)} %get-tuple-element.152.x_ref.a_ref, bf16[1024,768]{1,0:T(8,128)(2,1)} %c_ref.3, bf16[3,1024,768]{2,1,0:T(8,128)(2,1)} %get-tuple-element.119.rest_0_.b_ref, ...), custom_call_target="tpu_custom_call" | custom-call | flops 2400000000 | bytes 1200000 | tf_op jit(solution)/shard_map/wgrad_heads/pallas_call | solution.py:540
  347.6 3.5 all-to-all-start.2
  351.1 2.0 fusion.11
  353.2 1.6 collective-permute-start.29
  355.7 9.3 %dx.3 = bf16[1024,768]{1,0:T(8,128)(2,1)} custom-call(f32[1024,768]{1,0:T(8,128)} %get-tuple-element.166.dz1_ref, bf16[3,1024,384]{2,1,0:T(8,128)(2,1)} %get-tuple-element.141.d_ref.rest_0_, bf16[3,1024,384]{2,1,0:T(8,128)(2,1)} %get-tuple-element.143.d_ref.rest_1_, bf16[2,768,768]{2,1,0:T(8,128)(2,1)} %bitcast.118, bf16[2,768,768]{2,1,0:T(8,128)(2,1)} %bitcast.106), custom_call_target="tpu_custom_call" | custom-call | flops 1800000000 | bytes 900000 | tf_op jit(solution)/shard_map/dx/pallas_call | solution.py:434
  365.0 3.5 collective-permute-done.29
  369.2 5.3 %collective-permute-done.27 = bf16[2,4,5,24,384]{4,3,2,1,0:T(8,128)(2,1)S(1)} collective-permute-done((bf16[2,4,5,24,384]{4,3,2,1,0:T(8,128)(2,1)S(1)}, bf16[2,4,5,24,384]{4,3,2,1,0:T(8,128)(2,1)S(1)}, u32[]{:S(2)}, u32[]{:S(2)}) %collective-permute-start.27) | collective-permute-done | bytes 737312 | tf_op jit(solution)/shard_map/ppermute | solution.py:622
  375.3 4.3 %collective-permute-done.30 = bf16[4,4,24,384]{3,2,1,0:T(8,128)(2,1)S(1)} collective-permute-done((bf16[4,4,24,384]{3,2,1,0:T(8,128)(2,1)S(1)}, bf16[4,4,24,384]{3,2,1,0:T(8,128)(2,1)S(1)}, u32[]{:S(2)}, u32[]{:S(2)}) %collective-permute-start.30) | collective-permute-done | bytes 294944 | tf_op jit(solution)/shard_map/ppermute | solution.py:622
  379.7 3.2 collective-permute-done.28
  383.0 1.0 pad_maximum_fusion.4
  384.0 4.5 %all-to-all-start.1 = ((bf16[4,9,24,384]{3,2,1,0:T(8,128)(2,1)}), bf16[4,9,24,384]{3,2,1,0:T(8,128)(2,1)S(1)}, u32[]{:S(2)}, u32[]{:S(2)}) async-start(bf16[4,9,24,384]{3,2,1,0:T(8,128)(2,1)} %pad_maximum_fusion.4), calls=%async_computation.1 | async-start | bytes 1327104 | tf_op jit(solution)/shard_map/all_to_all | solution.py:626
  388.6 0.8 fusion.18
  390.1 12.1 %all-to-all-done.1 = bf16[4,9,24,384]{3,2,1,0:T(8,128)(2,1)S(1)} async-done(((bf16[4,9,24,384]{3,2,1,0:T(8,128)(2,1)}), bf16[4,9,24,384]{3,2,1,0:T(8,128)(2,1)S(1)}, u32[]{:S(2)}, u32[]{:S(2)}) %all-to-all-start.1) | async-done | bytes 663584 | tf_op jit(solution)/shard_map/all_to_all | solution.py:626
  403.2 0.9 reshape.128
  (88 shorter events, 12.6 us)
Async XLA Ops:
  2.3 16.4 %copy-start.12 = (bf16[13,8,768]{2,1,0:T(8,128)(2,1)S(1)}, bf16[13,8,768]{2,1,0:T(8,128)(2,1)}, u32[]{:S(2)}) copy-start(bf16[13,8,768]{2,1,0:T(8,128)(2,1)} %pack_one.1) | copy-start | bytes 479236
  2.3 10.4 %collective-permute-start = (bf16[13,8,768]{2,1,0:T(8,128)(2,1)}, bf16[13,8,768]{2,1,0:T(8,128)(2,1)S(1)}, u32[]{:S(2)}, u32[]{:S(2)}) collective-permute-start(bf16[13,8,768]{2,1,0:T(8,128)(2,1)} %pack_one.1), channel_id=1, source_target_pairs={{0,2},{1,3},{2,4},{3,5},{4,6},{5,7},{6,0},{7,1},{8,10},{9,11},{10,... | collective-permute-start | bytes 479240 | tf_op jit(solution)/shard_map/ppermute | solution.py:622
  5.4 13.4 %collective-permute-start.1 = (bf16[13,8,768]{2,1,0:T(8,128)(2,1)}, bf16[13,8,768]{2,1,0:T(8,128)(2,1)S(1)}, u32[]{:S(2)}, u32[]{:S(2)}) collective-permute-start(bf16[13,8,768]{2,1,0:T(8,128)(2,1)} %pack_one.1), channel_id=1, source_target_pairs={{0,4},{1,5},{2,6},{3,7},{4,0},{5,1},{6,2},{7,3},{8,12},{9,13},{10,... | collective-permute-start | bytes 479240 | tf_op jit(solution)/shard_map/ppermute | solution.py:622
  7.9 10.8 %collective-permute-start.2 = (bf16[13,8,768]{2,1,0:T(8,128)(2,1)}, bf16[13,8,768]{2,1,0:T(8,128)(2,1)S(1)}, u32[]{:S(2)}, u32[]{:S(2)}) collective-permute-start(bf16[13,8,768]{2,1,0:T(8,128)(2,1)} %pack_one.1), channel_id=1, source_target_pairs={{0,6},{1,7},{2,0},{3,1},{4,2},{5,3},{6,4},{7,5},{8,14},{9,15},{10,... | collective-permute-start | bytes 479240 | tf_op jit(solution)/shard_map/ppermute | solution.py:622
  18.8 33.9 %all-to-all-start = ((bf16[4,8,24,768]{3,2,1,0:T(8,128)(2,1)}), bf16[4,8,24,768]{3,2,1,0:T(8,128)(2,1)S(1)}, u32[]{:S(2)}, u32[]{:S(2)}) async-start(bf16[4,8,24,768]{3,2,1,0:T(8,128)(2,1)} %pack_two.1), calls=%async_computation | async-start | bytes 2359296 | tf_op jit(solution)/shard_map/all_to_all | solution.py:626
  25.0 8.8 %collective-permute-start.6 = (bf16[4,7,8,768]{3,2,1,0:T(8,128)(2,1)S(1)}, bf16[4,7,8,768]{3,2,1,0:T(8,128)(2,1)S(1)}, u32[]{:S(2)}, u32[]{:S(2)}) collective-permute-start(bf16[4,7,8,768]{3,2,1,0:T(8,128)(2,1)S(1)} %slice.95), channel_id=1, source_target_pairs={{0,16},{1,17},{2,18},{3,19},{4,20},{5,21},{6,22},{7,23},{8,24},{9,... | collective-permute-start | bytes 1032200 | tf_op jit(solution)/shard_map/ppermute | solution.py:622
  26.6 8.9 %collective-permute-start.3 = (bf16[4,2,24,768]{3,2,1,0:T(8,128)(2,1)S(1)}, bf16[4,2,24,768]{3,2,1,0:T(8,128)(2,1)S(1)}, u32[]{:S(2)}, u32[]{:S(2)}) collective-permute-start(bf16[4,2,24,768]{3,2,1,0:T(8,128)(2,1)S(1)} %bitcast.121), channel_id=1, source_target_pairs={{0,1},{1,0},{2,3},{3,2},{4,5},{5,4},{6,7},{7,6},{8,9},{9,8},{10,11... | collective-permute-start | bytes 884744 | tf_op jit(solution)/shard_map/ppermute | solution.py:622
  33.8 19.8 %copy-start.2 = (bf16[2,4,7,8,768]{4,3,2,1,0:T(8,128)(2,1)}, bf16[2,4,7,8,768]{4,3,2,1,0:T(8,128)(2,1)S(1)}, u32[]{:S(2)}) copy-start(bf16[2,4,7,8,768]{4,3,2,1,0:T(8,128)(2,1)S(1)} %pad_maximum_fusion.3.refs_5_) | copy-start | bytes 2064388
  33.9 15.3 %collective-permute-start.7 = (bf16[2,4,7,8,768]{4,3,2,1,0:T(8,128)(2,1)S(1)}, bf16[2,4,7,8,768]{4,3,2,1,0:T(8,128)(2,1)}, u32[]{:S(2)}, u32[]{:S(2)}) collective-permute-start(bf16[2,4,7,8,768]{4,3,2,1,0:T(8,128)(2,1)S(1)} %pad_maximum_fusion.3.refs_5_), channel_id=1, source_target_pairs={{0,1},{1,0},{2,3},{3,2},{4,5},{5,4},{6,7},{7,6},{8,9},{9,8},{10,11... | collective-permute-start | bytes 2064392 | tf_op jit(solution)/shard_map/ppermute | solution.py:622
  35.5 18.1 %copy-start.3 = (bf16[2,4,2,24,768]{4,3,2,1,0:T(8,128)(2,1)}, bf16[2,4,2,24,768]{4,3,2,1,0:T(8,128)(2,1)S(1)}, u32[]{:S(2)}) copy-start(bf16[2,4,2,24,768]{4,3,2,1,0:T(8,128)(2,1)S(1)} %pad_maximum_fusion.6.refs_1_) | copy-start | bytes 1769476
  35.5 12.9 %collective-permute-start.5 = (bf16[2,4,2,24,768]{4,3,2,1,0:T(8,128)(2,1)S(1)}, bf16[2,4,2,24,768]{4,3,2,1,0:T(8,128)(2,1)}, u32[]{:S(2)}, u32[]{:S(2)}) collective-permute-start(bf16[2,4,2,24,768]{4,3,2,1,0:T(8,128)(2,1)S(1)} %pad_maximum_fusion.6.refs_1_), channel_id=1, source_target_pairs={{0,16},{1,17},{2,18},{3,19},{4,20},{5,21},{6,22},{7,23},{8,24},{9,... | collective-permute-start | bytes 1769480 | tf_op jit(solution)/shard_map/ppermute | solution.py:622
  37.1 18.0 %collective-permute-start.4 = (bf16[2,4,2,24,768]{4,3,2,1,0:T(8,128)(2,1)S(1)}, bf16[2,4,2,24,768]{4,3,2,1,0:T(8,128)(2,1)}, u32[]{:S(2)}, u32[]{:S(2)}) collective-permute-start(bf16[2,4,2,24,768]{4,3,2,1,0:T(8,128)(2,1)S(1)} %pad_maximum_fusion.6.refs_1_), channel_id=1, source_target_pairs={{0,8},{1,9},{2,10},{3,11},{4,12},{5,13},{6,14},{7,15},{8,0},{9,1},... | collective-permute-start | bytes 1769480 | tf_op jit(solution)/shard_map/ppermute | solution.py:622
  37.1 20.1 %collective-permute-start.9 = (bf16[2,4,7,8,768]{4,3,2,1,0:T(8,128)(2,1)S(1)}, bf16[2,4,7,8,768]{4,3,2,1,0:T(8,128)(2,1)}, u32[]{:S(2)}, u32[]{:S(2)}) collective-permute-start(bf16[2,4,7,8,768]{4,3,2,1,0:T(8,128)(2,1)S(1)} %pad_maximum_fusion.3.refs_5_), channel_id=1, source_target_pairs={{0,8},{1,9},{2,10},{3,11},{4,12},{5,13},{6,14},{7,15},{8,0},{9,1},... | collective-permute-start | bytes 2064392 | tf_op jit(solution)/shard_map/ppermute | solution.py:622
  49.2 8.0 %collective-permute-start.10 = (bf16[2,4,7,8,768]{4,3,2,1,0:T(8,128)(2,1)}, bf16[2,4,7,8,768]{4,3,2,1,0:T(8,128)(2,1)}, u32[]{:S(2)}, u32[]{:S(2)}) collective-permute-start(bf16[2,4,7,8,768]{4,3,2,1,0:T(8,128)(2,1)} %collective-permute-done.7.refs_7_), channel_id=1, source_target_pairs={{0,8},{1,9},{2,10},{3,11},{4,12},{5,13},{6,14},{7,15},{8,0},{9,1},... | collective-permute-start | bytes 2064392 | tf_op jit(solution)/shard_map/ppermute | solution.py:622
  49.2 8.0 %collective-permute-start.8 = (bf16[2,4,2,24,768]{4,3,2,1,0:T(8,128)(2,1)}, bf16[2,4,2,24,768]{4,3,2,1,0:T(8,128)(2,1)}, u32[]{:S(2)}, u32[]{:S(2)}) collective-permute-start(bf16[2,4,2,24,768]{4,3,2,1,0:T(8,128)(2,1)} %collective-permute-done.5.refs_3_), channel_id=1, source_target_pairs={{0,8},{1,9},{2,10},{3,11},{4,12},{5,13},{6,14},{7,15},{8,0},{9,1},... | collective-permute-start | bytes 1769480 | tf_op jit(solution)/shard_map/ppermute | solution.py:622
  53.6 14.5 %collective-permute-start.12 = (bf16[4,4,24,768]{3,2,1,0:T(8,128)(2,1)}, bf16[4,4,24,768]{3,2,1,0:T(8,128)(2,1)S(1)}, u32[]{:S(2)}, u32[]{:S(2)}) collective-permute-start(bf16[4,4,24,768]{3,2,1,0:T(8,128)(2,1)} %get-tuple-element.102), channel_id=1, source_target_pairs={{0,16},{1,17},{2,18},{3,19},{4,20},{5,21},{6,22},{7,23},{8,24},{9,... | collective-permute-start | bytes 1769480 | tf_op jit(solution)/shard_map/ppermute | solution.py:622
  55.1 15.8 %collective-permute-start.11 = (bf16[4,4,24,768]{3,2,1,0:T(8,128)(2,1)S(1)}, bf16[4,4,24,768]{3,2,1,0:T(8,128)(2,1)S(1)}, u32[]{:S(2)}, u32[]{:S(2)}) collective-permute-start(bf16[4,4,24,768]{3,2,1,0:T(8,128)(2,1)S(1)} %get-tuple-element.101), channel_id=1, source_target_pairs={{0,1},{1,0},{2,3},{3,2},{4,5},{5,4},{6,7},{7,6},{8,9},{9,8},{10,11... | collective-permute-start | bytes 1769480 | tf_op jit(solution)/shard_map/ppermute | solution.py:622
  69.3 10.9 %copy-start = (bf16[2,4,4,24,768]{4,3,2,1,0:T(8,128)(2,1)}, bf16[2,4,4,24,768]{4,3,2,1,0:T(8,128)(2,1)S(1)}, u32[]{:S(2)}) copy-start(bf16[2,4,4,24,768]{4,3,2,1,0:T(8,128)(2,1)S(1)} %pad_maximum_fusion.1.refs_5_) | copy-start | bytes 3538948
  69.3 26.1 %collective-permute-start.15 = (bf16[2,4,4,24,768]{4,3,2,1,0:T(8,128)(2,1)S(1)}, bf16[2,4,4,24,768]{4,3,2,1,0:T(8,128)(2,1)S(1)}, u32[]{:S(2)}, u32[]{:S(2)}) collective-permute-start(bf16[2,4,4,24,768]{4,3,2,1,0:T(8,128)(2,1)S(1)} %pad_maximum_fusion.1.refs_5_), channel_id=1, source_target_pairs={{0,1},{1,0},{2,3},{3,2},{4,5},{5,4},{6,7},{7,6},{8,9},{9,8},{10,11... | collective-permute-start | bytes 3538952 | tf_op jit(solution)/shard_map/ppermute | solution.py:622
  71.0 9.2 %copy-start.1 = (bf16[2,4,4,24,768]{4,3,2,1,0:T(8,128)(2,1)}, bf16[2,4,4,24,768]{4,3,2,1,0:T(8,128)(2,1)S(1)}, u32[]{:S(2)}) copy-start(bf16[2,4,4,24,768]{4,3,2,1,0:T(8,128)(2,1)S(1)} %pad_maximum_fusion.refs_1_) | copy-start | bytes 3538948
  71.0 25.8 %collective-permute-start.14 = (bf16[2,4,4,24,768]{4,3,2,1,0:T(8,128)(2,1)S(1)}, bf16[2,4,4,24,768]{4,3,2,1,0:T(8,128)(2,1)S(1)}, u32[]{:S(2)}, u32[]{:S(2)}) collective-permute-start(bf16[2,4,4,24,768]{4,3,2,1,0:T(8,128)(2,1)S(1)} %pad_maximum_fusion.refs_1_), channel_id=1, source_target_pairs={{0,16},{1,17},{2,18},{3,19},{4,20},{5,21},{6,22},{7,23},{8,24},{9,... | collective-permute-start | bytes 3538952 | tf_op jit(solution)/shard_map/ppermute | solution.py:622
  80.1 17.2 %collective-permute-start.17 = (bf16[2,4,4,24,768]{4,3,2,1,0:T(8,128)(2,1)S(1)}, bf16[2,4,4,24,768]{4,3,2,1,0:T(8,128)(2,1)S(1)}, u32[]{:S(2)}, u32[]{:S(2)}) collective-permute-start(bf16[2,4,4,24,768]{4,3,2,1,0:T(8,128)(2,1)S(1)} %pad_maximum_fusion.1.refs_5_), channel_id=1, source_target_pairs={{0,8},{1,9},{2,10},{3,11},{4,12},{5,13},{6,14},{7,15},{8,0},{9,1},... | collective-permute-start | bytes 3538952 | tf_op jit(solution)/shard_map/ppermute | solution.py:622
  80.2 17.1 %collective-permute-start.13 = (bf16[2,4,4,24,768]{4,3,2,1,0:T(8,128)(2,1)S(1)}, bf16[2,4,4,24,768]{4,3,2,1,0:T(8,128)(2,1)S(1)}, u32[]{:S(2)}, u32[]{:S(2)}) collective-permute-start(bf16[2,4,4,24,768]{4,3,2,1,0:T(8,128)(2,1)S(1)} %pad_maximum_fusion.refs_1_), channel_id=1, source_target_pairs={{0,8},{1,9},{2,10},{3,11},{4,12},{5,13},{6,14},{7,15},{8,0},{9,1},... | collective-permute-start | bytes 3538952 | tf_op jit(solution)/shard_map/ppermute | solution.py:622
  95.3 6.1 %copy-start.7 = (bf16[2,4,4,24,768]{4,3,2,1,0:T(8,128)(2,1)}, bf16[2,4,4,24,768]{4,3,2,1,0:T(8,128)(2,1)S(1)}, u32[]{:S(2)}) copy-start(bf16[2,4,4,24,768]{4,3,2,1,0:T(8,128)(2,1)S(1)} %collective-permute-done.15.refs_7_) | copy-start | bytes 3538948
  96.8 4.7 %copy-start.8 = (bf16[2,4,4,24,768]{4,3,2,1,0:T(8,128)(2,1)}, bf16[2,4,4,24,768]{4,3,2,1,0:T(8,128)(2,1)S(1)}, u32[]{:S(2)}) copy-start(bf16[2,4,4,24,768]{4,3,2,1,0:T(8,128)(2,1)S(1)} %collective-permute-done.14.refs_3_) | copy-start | bytes 3538948
  96.8 4.5 %collective-permute-start.16 = (bf16[2,4,4,24,768]{4,3,2,1,0:T(8,128)(2,1)S(1)}, bf16[2,4,4,24,768]{4,3,2,1,0:T(8,128)(2,1)S(1)}, u32[]{:S(2)}, u32[]{:S(2)}) collective-permute-start(bf16[2,4,4,24,768]{4,3,2,1,0:T(8,128)(2,1)S(1)} %collective-permute-done.14.refs_3_), channel_id=1, source_target_pairs={{0,8},{1,9},{2,10},{3,11},{4,12},{5,13},{6,14},{7,15},{8,0},{9,1},... | collective-permute-start | bytes 3538952 | tf_op jit(solution)/shard_map/ppermute | solution.py:622
  96.8 4.7 %collective-permute-start.18 = (bf16[2,4,4,24,768]{4,3,2,1,0:T(8,128)(2,1)S(1)}, bf16[2,4,4,24,768]{4,3,2,1,0:T(8,128)(2,1)}, u32[]{:S(2)}, u32[]{:S(2)}) collective-permute-start(bf16[2,4,4,24,768]{4,3,2,1,0:T(8,128)(2,1)S(1)} %collective-permute-done.15.refs_7_), channel_id=1, source_target_pairs={{0,8},{1,9},{2,10},{3,11},{4,12},{5,13},{6,14},{7,15},{8,0},{9,1},... | collective-permute-start | bytes 3538952 | tf_op jit(solution)/shard_map/ppermute | solution.py:622
  97.3 4.2 %copy-start.9 = (bf16[2,4,4,24,768]{4,3,2,1,0:T(8,128)(2,1)}, bf16[2,4,4,24,768]{4,3,2,1,0:T(8,128)(2,1)S(1)}, u32[]{:S(2)}) copy-start(bf16[2,4,4,24,768]{4,3,2,1,0:T(8,128)(2,1)S(1)} %collective-permute-done.17.refs_6_) | copy-start | bytes 3538948
  97.3 4.2 %copy-start.10 = (bf16[2,4,4,24,768]{4,3,2,1,0:T(8,128)(2,1)}, bf16[2,4,4,24,768]{4,3,2,1,0:T(8,128)(2,1)S(1)}, u32[]{:S(2)}) copy-start(bf16[2,4,4,24,768]{4,3,2,1,0:T(8,128)(2,1)S(1)} %collective-permute-done.13.refs_2_) | copy-start | bytes 3538948
  101.3 1.0 copy-start.11
  268.2 15.7 %collective-permute-start.19 = (bf16[2,2,4,4,24,768]{5,4,3,2,1,0:T(8,128)(2,1)}, bf16[2,2,4,4,24,768]{5,4,3,2,1,0:T(8,128)(2,1)}, u32[]{:S(2)}, u32[]{:S(2)}) collective-permute-start(bf16[2,2,4,4,24,768]{5,4,3,2,1,0:T(8,128)(2,1)} %get-tuple-element.135), channel_id=1, source_target_pairs={{0,8},{1,9},{2,10},{3,11},{4,12},{5,13},{6,14},{7,15},{8,0},{9,1},... | collective-permute-start | bytes 7077896 | tf_op jit(solution)/shard_map/ppermute | solution.py:622
  268.4 15.5 %copy-start.5 = (bf16[2,2,4,4,24,768]{5,4,3,2,1,0:T(8,128)(2,1)S(1)}, bf16[2,2,4,4,24,768]{5,4,3,2,1,0:T(8,128)(2,1)}, u32[]{:S(2)}) copy-start(bf16[2,2,4,4,24,768]{5,4,3,2,1,0:T(8,128)(2,1)} %get-tuple-element.134) | copy-start | bytes 7077892
  283.5 4.9 %collective-permute-start.20 = (bf16[2,2,4,4,24,768]{5,4,3,2,1,0:T(8,128)(2,1)}, bf16[2,2,4,4,24,768]{5,4,3,2,1,0:T(8,128)(2,1)}, u32[]{:S(2)}, u32[]{:S(2)}) collective-permute-start(bf16[2,2,4,4,24,768]{5,4,3,2,1,0:T(8,128)(2,1)} %get-tuple-element.138), channel_id=1, source_target_pairs={{0,8},{1,9},{2,10},{3,11},{4,12},{5,13},{6,14},{7,15},{8,0},{9,1},... | collective-permute-start | bytes 7077896 | tf_op jit(solution)/shard_map/ppermute | solution.py:622
  283.9 4.5 %copy-start.4 = (bf16[2,2,4,4,24,768]{5,4,3,2,1,0:T(8,128)(2,1)S(1)}, bf16[2,2,4,4,24,768]{5,4,3,2,1,0:T(8,128)(2,1)}, u32[]{:S(2)}) copy-start(bf16[2,2,4,4,24,768]{5,4,3,2,1,0:T(8,128)(2,1)} %get-tuple-element.137) | copy-start | bytes 7077892
  286.4 30.8 %collective-permute-start.21 = (bf16[2,4,4,24,768]{4,3,2,1,0:T(8,128)(2,1)S(1)}, bf16[2,4,4,24,768]{4,3,2,1,0:T(8,128)(2,1)S(1)}, u32[]{:S(2)}, u32[]{:S(2)}) collective-permute-start(bf16[2,4,4,24,768]{4,3,2,1,0:T(8,128)(2,1)S(1)} %get-tuple-element.172), channel_id=1, source_target_pairs={{0,1},{1,0},{2,3},{3,2},{4,5},{5,4},{6,7},{7,6},{8,9},{9,8},{10,11... | collective-permute-start | bytes 3538952 | tf_op jit(solution)/shard_map/ppermute | solution.py:622
  290.7 28.3 %collective-permute-start.22 = (bf16[2,4,4,24,768]{4,3,2,1,0:T(8,128)(2,1)S(1)}, bf16[2,4,4,24,768]{4,3,2,1,0:T(8,128)(2,1)S(1)}, u32[]{:S(2)}, u32[]{:S(2)}) collective-permute-start(bf16[2,4,4,24,768]{4,3,2,1,0:T(8,128)(2,1)S(1)} %get-tuple-element.170), channel_id=1, source_target_pairs={{0,16},{1,17},{2,18},{3,19},{4,20},{5,21},{6,22},{7,23},{8,24},{9,... | collective-permute-start | bytes 3538952 | tf_op jit(solution)/shard_map/ppermute | solution.py:622
  319.3 17.0 %collective-permute-start.23 = (bf16[4,4,24,768]{3,2,1,0:T(8,128)(2,1)S(1)}, bf16[4,4,24,768]{3,2,1,0:T(8,128)(2,1)S(1)}, u32[]{:S(2)}, u32[]{:S(2)}) collective-permute-start(bf16[4,4,24,768]{3,2,1,0:T(8,128)(2,1)S(1)} %get-tuple-element.178), channel_id=1, source_target_pairs={{0,1},{1,0},{2,3},{3,2},{4,5},{5,4},{6,7},{7,6},{8,9},{9,8},{10,11... | collective-permute-start | bytes 1769480 | tf_op jit(solution)/shard_map/ppermute | solution.py:622
  319.9 16.6 %collective-permute-start.24 = (bf16[4,4,24,768]{3,2,1,0:T(8,128)(2,1)S(1)}, bf16[4,4,24,768]{3,2,1,0:T(8,128)(2,1)S(1)}, u32[]{:S(2)}, u32[]{:S(2)}) collective-permute-start(bf16[4,4,24,768]{3,2,1,0:T(8,128)(2,1)S(1)} %get-tuple-element.180), channel_id=1, source_target_pairs={{0,16},{1,17},{2,18},{3,19},{4,20},{5,21},{6,22},{7,23},{8,24},{9,... | collective-permute-start | bytes 1769480 | tf_op jit(solution)/shard_map/ppermute | solution.py:622
  337.8 16.9 %collective-permute-start.25 = (bf16[2,2,4,5,24,384]{5,4,3,2,1,0:T(8,128)(2,1)}, bf16[2,2,4,5,24,384]{5,4,3,2,1,0:T(8,128)(2,1)S(1)}, u32[]{:S(2)}, u32[]{:S(2)}) collective-permute-start(bf16[2,2,4,5,24,384]{5,4,3,2,1,0:T(8,128)(2,1)} %get-tuple-element.164), channel_id=1, source_target_pairs={{0,8},{1,9},{2,10},{3,11},{4,12},{5,13},{6,14},{7,15},{8,0},{9,1},... | collective-permute-start | bytes 4423688 | tf_op jit(solution)/shard_map/ppermute | solution.py:622
  347.1 4.0 collective-permute-start.26
  347.6 36.4 %all-to-all-start.2 = ((bf16[4,8,24,768]{3,2,1,0:T(8,128)(2,1)}), bf16[4,8,24,768]{3,2,1,0:T(8,128)(2,1)S(1)}, u32[]{:S(2)}, u32[]{:S(2)}) async-start(bf16[4,8,24,768]{3,2,1,0:T(8,128)(2,1)} %pad_maximum_fusion.2), calls=%async_computation.2 | async-start | bytes 2359296 | tf_op jit(solution)/shard_map/all_to_all | solution.py:626
  351.1 3.6 copy-start.6
  353.2 15.3 %collective-permute-start.29 = (bf16[2,4,4,24,384]{4,3,2,1,0:T(8,128)(2,1)S(1)}, bf16[2,4,4,24,384]{4,3,2,1,0:T(8,128)(2,1)S(1)}, u32[]{:S(2)}, u32[]{:S(2)}) collective-permute-start(bf16[2,4,4,24,384]{4,3,2,1,0:T(8,128)(2,1)S(1)} %get-tuple-element.176), channel_id=1, source_target_pairs={{0,1},{1,0},{2,3},{3,2},{4,5},{5,4},{6,7},{7,6},{8,9},{9,8},{10,11... | collective-permute-start | bytes 1769480 | tf_op jit(solution)/shard_map/ppermute | solution.py:622
  355.1 19.5 %collective-permute-start.27 = (bf16[2,4,5,24,384]{4,3,2,1,0:T(8,128)(2,1)S(1)}, bf16[2,4,5,24,384]{4,3,2,1,0:T(8,128)(2,1)S(1)}, u32[]{:S(2)}, u32[]{:S(2)}) collective-permute-start(bf16[2,4,5,24,384]{4,3,2,1,0:T(8,128)(2,1)S(1)} %get-tuple-element.174), channel_id=1, source_target_pairs={{0,16},{1,17},{2,18},{3,19},{4,20},{5,21},{6,22},{7,23},{8,24},{9,... | collective-permute-start | bytes 2211848 | tf_op jit(solution)/shard_map/ppermute | solution.py:622
  368.6 11.0 %collective-permute-start.30 = (bf16[4,4,24,384]{3,2,1,0:T(8,128)(2,1)S(1)}, bf16[4,4,24,384]{3,2,1,0:T(8,128)(2,1)S(1)}, u32[]{:S(2)}, u32[]{:S(2)}) collective-permute-start(bf16[4,4,24,384]{3,2,1,0:T(8,128)(2,1)S(1)} %get-tuple-element.184), channel_id=1, source_target_pairs={{0,16},{1,17},{2,18},{3,19},{4,20},{5,21},{6,22},{7,23},{8,24},{9,... | collective-permute-start | bytes 884744 | tf_op jit(solution)/shard_map/ppermute | solution.py:622
  374.8 8.2 %collective-permute-start.28 = (bf16[4,5,24,384]{3,2,1,0:T(8,128)(2,1)S(1)}, bf16[4,5,24,384]{3,2,1,0:T(8,128)(2,1)S(1)}, u32[]{:S(2)}, u32[]{:S(2)}) collective-permute-start(bf16[4,5,24,384]{3,2,1,0:T(8,128)(2,1)S(1)} %get-tuple-element.182), channel_id=1, source_target_pairs={{0,1},{1,0},{2,3},{3,2},{4,5},{5,4},{6,7},{7,6},{8,9},{9,8},{10,11... | collective-permute-start | bytes 1105928 | tf_op jit(solution)/shard_map/ppermute | solution.py:622
  384.0 18.2 %all-to-all-start.1 = ((bf16[4,9,24,384]{3,2,1,0:T(8,128)(2,1)}), bf16[4,9,24,384]{3,2,1,0:T(8,128)(2,1)S(1)}, u32[]{:S(2)}, u32[]{:S(2)}) async-start(bf16[4,9,24,384]{3,2,1,0:T(8,128)(2,1)} %pad_maximum_fusion.4), calls=%async_computation.1 | async-start | bytes 1327104 | tf_op jit(solution)/shard_map/all_to_all | solution.py:626

commit v11 on v10

--- a/solution.py
+++ b/solution.py
@@ -763,6 +763,57 @@
     )(at, *parts)
 
 
+def place_half_body(far, at_ref, *refs):
+    parts, (outs, held, sems, out_sems) = refs[:4], (refs[-6:-4], refs[-4:-2], refs[-2], refs[-1])
+    x, core, y = at_ref[0], at_ref[1], at_ref[3]
+    copies = []
+    for i, part in enumerate(parts):
+        side, other = i >> 1, i & 1
+        pc = (core + other) % 2
+        for near in range(2):
+            if side == 0:
+                target = held[0].at[:, pc, :, (y + near) % 2]
+            else:
+                target = held[1].at[(x + near) % 2, pc]
+            for dz in range(4):
+                to = target.at[:, dz] if side == 0 else target.at[dz]
+                copies.append(pltpu.make_async_copy(part.at[near, dz], to, sems.at[len(copies)]))
+    for copy in copies:
+        copy.start()
+    for copy in copies:
+        copy.wait()
+    back = [
+        pltpu.make_async_copy(held[0], outs[0].at[:, (x + far) % 2], out_sems.at[0]),
+        pltpu.make_async_copy(held[1], outs[1].at[:, :, :, (y + far) % 2], out_sems.at[1]),
+    ]
+    for copy in back:
+        copy.start()
+    for copy in back:
+        copy.wait()
+
+
+def place_half(at, parts, far, begun=()):
+    rows = parts[0].shape[-2]
+    shapes = [(4, 2, 2, 4, 2, rows, D), (2, 2, 4, 2, 4, rows, D)]
+    held = [(4, 2, 4, 2, rows, D), (2, 2, 4, 4, rows, D)]
+    return pl.pallas_call(
+        lambda *refs: place_half_body(far, *refs),
+        grid_spec=pltpu.PrefetchScalarGridSpec(
+            num_scalar_prefetch=1,
+            grid=(1,),
+            in_specs=[ANY] * (4 + len(begun)),
+            out_specs=[ANY, ANY],
+            scratch_shapes=[pltpu.VMEM(shape, BF) for shape in held]
+            + [pltpu.SemaphoreType.DMA((32,)), pltpu.SemaphoreType.DMA((2,))],
+        ),
+        out_shape=[jax.ShapeDtypeStruct(shape, BF) for shape in shapes],
+        input_output_aliases={5: 0, 6: 1} if begun else {},
+        compiler_params=params(),
+        cost_estimate=cost(4),
+        name="place_half",
+    )(at, *parts, *begun)
+
+
 def after(value, *others):
     return lax.optimization_barrier((value, *others))[0]
 
@@ -853,7 +904,9 @@
     qkv = qkv_call(tokens, first, vec)
     two.two(vec)
     ctx, lse = attend_call(after(qkv, *two.near), lengths)
-    w_in, w_back = place(at, two.parts(ctx), True)
+    parts = two.parts(ctx)
+    begun = place_half(at, [parts[i] for i in (0, 1, 4, 5)], 0)
+    w_in, w_back = place_half(at, [parts[i] for i in (2, 3, 6, 7)], 1, begun)
     w_in = w_in.reshape(4, grid.count * rows, D)
     w_back = w_back.reshape(grid.count * span, D)
     z1, h1, g, slope, z2, low = ffn_call(tokens, ctx, first, vec, w_in, w_back, False)

time: 413 us -> 414 us (level)
    pallas_call x0 -> x2, Pallas kernels: none -> 11.1 us  [place_half(): pl.pallas_call(lambda *refs: place_half_body(far, *refs), grid_spec=pltpu...]
    pallas_call x2 -> x1, Pallas kernels: 14.7 us -> 6.41 us  [place(): pl.pallas_call(lambda *refs: place_body(split, *refs), grid_spec=pltpu.Pr...]
  transfers between devices with their start and end apart: 34 -> 34, of which waited for: 18 -> 16; matrix products, arithmetic and copies ran while one was open for 3% -> 3% of each run, Pallas kernels for 25% -> 26%
where the time goes in v11:
time: 414 us; the launch traced here: 407 us
  Pallas kernels  272 us (66%)
  waiting for transfers between devices  67.5 us (16%)
  starting transfers between devices  44 us (11%)
  other arithmetic  13.6 us (3%)
  local copies, waits for them, and re-layouts  7.74 us (2%)
    ppermute x31, waiting for transfers between devices, send(): return lax.ppermute(value, AXES, self.shift(dim, step))  52.4 us
    pallas_call x2, Pallas kernels, ffn_back_call(): pl.pallas_call(ffn_back_body, grid=(rows // block,), in_specs=[line, line...  47.6 us
    pallas_call x3, Pallas kernels, attend_back_call(): pl.pallas_call(body, grid_spec=pltpu.PrefetchScalarGridSpec(num_scalar_pr...  46.6 us
    pallas_call x2, Pallas kernels, ffn_call(): pl.pallas_call(lambda *refs: ffn_body(renorm, *refs), grid=(rows // block...  44.7 us
    ppermute x31, starting transfers between devices, send(): return lax.ppermute(value, AXES, self.shift(dim, step))  29.9 us
    pallas_call x2, Pallas kernels, attend_call(): pl.pallas_call(body, grid_spec=pltpu.PrefetchScalarGridSpec(num_scalar_pr...  24.8 us
    pallas_call x2, Pallas kernels, wgrad_heads_call(): pl.pallas_call(body, grid_spec=pltpu.PrefetchScalarGridSpec(num_scalar_pr...  24.2 us
    pallas_call x2, Pallas kernels, dx_call(): pl.pallas_call(dx_body, grid=(rows // block,), in_specs=[line, *specs, on...  17.7 us
  transfers between devices with their start and end apart: 34, of which 16 were waited for; matrix products, arithmetic and copies ran while one was open for 3% of the time, Pallas kernels for 26%

profile of v11, /device:TPU:0, one launch (start us, length us, event | category | flops | bytes accessed | tf_op | source)
XLA Modules:
  0.0 406.6 jit_solution(3547410105764392979)
XLA Ops:
  0.7 1.7 pack_one.1
  2.3 3.0 collective-permute-start
  5.4 2.6 collective-permute-start.1
  7.9 1.3 collective-permute-start.2
  9.3 2.1 pack_two.1
  11.4 1.3 collective-permute-done
  12.7 6.0 %collective-permute-done.1 = bf16[13,8,768]{2,1,0:T(8,128)(2,1)S(1)} collective-permute-done((bf16[13,8,768]{2,1,0:T(8,128)(2,1)}, bf16[13,8,768]{2,1,0:T(8,128)(2,1)S(1)}, u32[]{:S(2)}, u32[]{:S(2)}) %collective-permute-start.1) | collective-permute-done | bytes 159776 | tf_op jit(solution)/shard_map/ppermute | solution.py:622
  18.8 6.2 %all-to-all-start = ((bf16[4,8,24,768]{3,2,1,0:T(8,128)(2,1)}), bf16[4,8,24,768]{3,2,1,0:T(8,128)(2,1)S(1)}, u32[]{:S(2)}, u32[]{:S(2)}) async-start(bf16[4,8,24,768]{3,2,1,0:T(8,128)(2,1)} %pack_two.1), calls=%async_computation | async-start | bytes 2359296 | tf_op jit(solution)/shard_map/all_to_all | solution.py:626
  25.0 1.6 collective-permute-start.6
  26.6 1.6 collective-permute-start.3
  28.2 5.6 %collective-permute-done.6 = bf16[4,7,8,768]{3,2,1,0:T(8,128)(2,1)S(1)} collective-permute-done((bf16[4,7,8,768]{3,2,1,0:T(8,128)(2,1)S(1)}, bf16[4,7,8,768]{3,2,1,0:T(8,128)(2,1)S(1)}, u32[]{:S(2)}, u32[]{:S(2)}) %collective-permute-start.6) | collective-permute-done | bytes 344096 | tf_op jit(solution)/shard_map/ppermute | solution.py:622
  33.9 1.6 collective-permute-start.7
  35.5 1.6 collective-permute-start.5
  37.6 10.9 %collective-permute-done.5.refs_3_ = bf16[2,4,2,24,768]{4,3,2,1,0:T(8,128)(2,1)} collective-permute-done((bf16[2,4,2,24,768]{4,3,2,1,0:T(8,128)(2,1)S(1)}, bf16[2,4,2,24,768]{4,3,2,1,0:T(8,128)(2,1)}, u32[]{:S(2)}, u32[]{:S(2)}) %collective-permute-start.5) | collective-permute-done | bytes 589856 | tf_op jit(solution)/shard_map/ppermute | solution.py:622
  49.7 3.0 all-to-all-done
  52.7 0.9 fusion.17
  53.6 1.5 collective-permute-start.12
  55.1 1.5 collective-permute-start.11
  57.2 6.4 %place.1 = (bf16[2,2,2,4,2,24,768]{6,5,4,3,2,1,0:T(8,128)(2,1)}, bf16[2,2,2,4,2,3,8,768]{7,6,5,4,3,2,1,0:T(8,128)(2,1)}, f32[24,768]{1,0:T(8,128)}) custom-call(s32[4]{0:T(128)} %pad_add_fusion.refs_0_, bf16[2,4,2,24,768]{4,3,2,1,0:T(8,128)(2,1)} %copy-done.3, bf16[2,4,2,24,768]{4,3,2,1,0:T(8,128)(2,1)} %collective-permute-done.4.refs_2_, ...), custom_call_target="tpu_custom_call" | custom-call | flops 1200000000 | bytes 600000 | tf_op jit(solution)/shard_map/place/pallas_call | solution.py:750
  63.6 4.4 %collective-permute-done.12 = bf16[4,4,24,768]{3,2,1,0:T(8,128)(2,1)S(1)} collective-permute-done((bf16[4,4,24,768]{3,2,1,0:T(8,128)(2,1)}, bf16[4,4,24,768]{3,2,1,0:T(8,128)(2,1)S(1)}, u32[]{:S(2)}, u32[]{:S(2)}) %collective-permute-start.12) | collective-permute-done | bytes 589856 | tf_op jit(solution)/shard_map/ppermute | solution.py:622
  68.1 1.2 pad_maximum_fusion.1.refs_3_
  69.3 1.6 collective-permute-start.14
  71.0 1.6 collective-permute-start.13
  72.5 7.6 %qkv.2.refs_1_.refs_2_.refs_3_ = bf16[1024,2304]{1,0:T(8,128)(2,1)} custom-call(bf16[1024,768]{1,0:T(8,128)(2,1)} %c_ref.3, bf16[2,768,768]{2,1,0:T(8,128)(2,1)} %bitcast.115, bf16[2,768,768]{2,1,0:T(8,128)(2,1)} %bitcast.99, f32[24,768]{1,0:T(8,128)} %get-tuple-element.100.vec_ref.refs_2_), custom_call_target="tpu_custom_call" | custom-call | flops 1600000000 | bytes 800000 | tf_op jit(solution)/shard_map/qkv/pallas_call | solution.py:75
  80.6 12.2 %attend.2 = (bf16[1024,768]{1,0:T(8,128)(2,1)}, f32[2,6,2,512]{3,2,1,0:T(2,128)}) custom-call(s32[2]{0:T(128)} %refs_0_.11, bf16[1024,2304]{1,0:T(8,128)(2,1)} %qkv.2.refs_1_.refs_2_.refs_3_, bf16[1024,2304]{1,0:T(8,128)(2,1)} %qkv.2.refs_1_.refs_2_.refs_3_, bf16[1024,2304]{1,0:T(8,128)(2,1)} %qkv.2.refs_1_.refs_2_.refs_3_), custom_call_target="tpu_custom_call" | custom-call | flops 2600000000 | bytes 1300000 | tf_op jit(solution)/shard_map/attend/pallas_call | solution.py:137
  92.9 2.5 collective-permute-done.14.refs_3_
  95.3 1.4 collective-permute-done.13.refs_1_
  97.3 1.1 copy-done.7
  98.4 1.0 copy-done.8
  99.4 5.6 %place_half.2 = (bf16[4,2,2,4,2,24,768]{6,5,4,3,2,1,0:T(8,128)(2,1)}, bf16[2,2,4,2,4,24,768]{6,5,4,3,2,1,0:T(8,128)(2,1)}) custom-call(s32[4]{0:T(128)} %pad_add_fusion.refs_0_, bf16[2,4,4,24,768]{4,3,2,1,0:T(8,128)(2,1)} %copy-done.1, bf16[2,4,4,24,768]{4,3,2,1,0:T(8,128)(2,1)} %copy-done.8, bf16[2,4,4,24,768]{4,3,2,1,0:T(8,128)(2,1)} %copy-done, ...), custom_call_target="tpu_custom_call" | custom-call | flops 800000000 | bytes 400000 | tf_op jit(solution)/shard_map/place_half/pallas_call | solution.py:799
  105.0 1.0 copy-done.11
  106.0 5.5 %place_half.3 = (bf16[4,2,2,4,2,24,768]{6,5,4,3,2,1,0:T(8,128)(2,1)}, bf16[2,2,4,2,4,24,768]{6,5,4,3,2,1,0:T(8,128)(2,1)}) custom-call(s32[4]{0:T(128)} %pad_add_fusion.refs_0_, bf16[2,4,4,24,768]{4,3,2,1,0:T(8,128)(2,1)} %copy-done.10, bf16[2,4,4,24,768]{4,3,2,1,0:T(8,128)(2,1)} %copy-done.11, ...), custom_call_target="tpu_custom_call", output_to_operand_aliasing={{0}: (5, {}), {1}: (6, {})} | custom-call | flops 800000000 | bytes 400000 | tf_op jit(solution)/shard_map/place_half/pallas_call | solution.py:799
  111.5 22.2 %ffn.2 = (f32[1024,768]{1,0:T(8,128)}, bf16[1024,768]{1,0:T(8,128)(2,1)}, bf16[1024,3072]{1,0:T(8,128)(2,1)}, bf16[1024,3072]{1,0:T(8,128)(2,1)}, f32[1024,768]{1,0:T(8,128)}, /*index=5*/bf16[1024,768]{1,0:T(8,128)(2,1)}) custom-call(bf16[1024,768]{1,0:T(8,128)(2,1)} %c_ref.3, bf16[1024,768]{1,0:T(8,128)(2,1)} %get-tuple-element.106.refs_1_.rest_1_, ...), custom_call_target="tpu_custom_call" | custom-call | flops 4400000000 | bytes 2200000 | tf_op jit(solution)/shard_map/ffn/pallas_call | solution.py:237
  133.8 7.6 %qkv.3.refs_1_.refs_2_.refs_3_ = bf16[1024,2304]{1,0:T(8,128)(2,1)} custom-call(bf16[1024,768]{1,0:T(8,128)(2,1)} %get-tuple-element.156.x_ref.a_ref, bf16[2,768,768]{2,1,0:T(8,128)(2,1)} %bitcast.116, bf16[2,768,768]{2,1,0:T(8,128)(2,1)} %bitcast.101, f32[24,768]{1,0:T(8,128)} %get-tuple-element.100.vec_ref.refs_2_), custom_call_target="tpu_custom_call" | custom-call | flops 1600000000 | bytes 800000 | tf_op jit(solution)/shard_map/qkv/pallas_call | solution.py:75
  141.4 12.5 %attend.3 = (bf16[1024,768]{1,0:T(8,128)(2,1)}, f32[2,6,2,512]{3,2,1,0:T(2,128)}) custom-call(s32[2]{0:T(128)} %refs_0_.11, bf16[1024,2304]{1,0:T(8,128)(2,1)} %qkv.3.refs_1_.refs_2_.refs_3_, bf16[1024,2304]{1,0:T(8,128)(2,1)} %qkv.3.refs_1_.refs_2_.refs_3_, bf16[1024,2304]{1,0:T(8,128)(2,1)} %qkv.3.refs_1_.refs_2_.refs_3_), custom_call_target="tpu_custom_call" | custom-call | flops 2600000000 | bytes 1300000 | tf_op jit(solution)/shard_map/attend/pallas_call | solution.py:137
  153.9 22.5 %ffn.3 = (f32[1024,768]{1,0:T(8,128)}, bf16[1024,768]{1,0:T(8,128)(2,1)}, bf16[1024,3072]{1,0:T(8,128)(2,1)}, bf16[1024,3072]{1,0:T(8,128)(2,1)}, f32[1024,768]{1,0:T(8,128)}, /*index=5*/bf16[1024,768]{1,0:T(8,128)(2,1)}) custom-call(f32[1024,768]{1,0:T(8,128)} %get-tuple-element.113.refs_0_.z2_ref, bf16[1024,768]{1,0:T(8,128)(2,1)} %get-tuple-element.115.refs_1_.rest_0_, ...), custom_call_target="tpu_custom_call" | custom-call | flops 4400000000 | bytes 2200000 | tf_op jit(solution)/shard_map/ffn/pallas_call | solution.py:237
  176.4 23.8 %ffn_back.2 = (bf16[1024,768]{1,0:T(8,128)(2,1)}, bf16[1024,3072]{1,0:T(8,128)(2,1)}, f32[1024,768]{1,0:T(8,128)}, bf16[1024,768]{1,0:T(8,128)(2,1)}, bf16[1024,768]{1,0:T(8,128)(2,1)}, /*index=5*/f32[24,768]{1,0:T(8,128)}) custom-call(bf16[1024,768]{1,0:T(8,128)(2,1)} %dy_ref.1, f32[1024,768]{1,0:T(8,128)} %get-tuple-element.117.z2_ref, ...), custom_call_target="tpu_custom_call" | custom-call | flops 4800000000 | bytes 2400000 | tf_op jit(solution)/shard_map/ffn_back/pallas_call | solution.py:319
  200.2 21.8 %attend_back.3 = (bf16[3,1024,768]{2,1,0:T(8,128)(2,1)}, f32[2,1,768]{2,1,0:T(1,128)}, f32[2,1,768]{2,1,0:T(1,128)}) custom-call(s32[2]{0:T(128)} %refs_0_.11, bf16[1024,2304]{1,0:T(8,128)(2,1)} %qkv.3.refs_1_.refs_2_.refs_3_, bf16[1024,2304]{1,0:T(8,128)(2,1)} %qkv.3.refs_1_.refs_2_.refs_3_, bf16[1024,2304]{1,0:T(8,128)(2,1)} %qkv.3.refs_1_.refs_2_.refs_3_, ...), custom_call_target="tpu_custom_call" | custom-call | flops 4800000000 | bytes 2400000 | tf_op jit(solution)/shard_map/attend_back/pallas_call | solution.py:395
  222.0 8.4 %dx.2.dy_ref = f32[1024,768]{1,0:T(8,128)} custom-call(f32[1024,768]{1,0:T(8,128)} %get-tuple-element.120.dz1_ref, bf16[3,1024,768]{2,1,0:T(8,128)(2,1)} %get-tuple-element.123.rest_0_.b_ref, bf16[2,768,768]{2,1,0:T(8,128)(2,1)} %bitcast.117, bf16[2,768,768]{2,1,0:T(8,128)(2,1)} %bitcast.104), custom_call_target="tpu_custom_call" | custom-call | flops 1800000000 | bytes 900000 | tf_op jit(solution)/shard_map/dx/pallas_call | solution.py:434
  230.4 23.8 %ffn_back.3 = (bf16[1024,768]{1,0:T(8,128)(2,1)}, bf16[1024,3072]{1,0:T(8,128)(2,1)}, f32[1024,768]{1,0:T(8,128)}, bf16[1024,768]{1,0:T(8,128)(2,1)}, bf16[1024,768]{1,0:T(8,128)(2,1)}, /*index=5*/f32[24,768]{1,0:T(8,128)}) custom-call(f32[1024,768]{1,0:T(8,128)} %dx.2.dy_ref, f32[1024,768]{1,0:T(8,128)} %get-tuple-element.113.refs_0_.z2_ref, ...), custom_call_target="tpu_custom_call" | custom-call | flops 4800000000 | bytes 2400000 | tf_op jit(solution)/shard_map/ffn_back/pallas_call | solution.py:319
  254.2 15.0 %wgrad_back.1 = (bf16[2,2,4,4,24,768]{5,4,3,2,1,0:T(8,128)(2,1)}, bf16[2,2,4,4,24,768]{5,4,3,2,1,0:T(8,128)(2,1)}) custom-call(s32[1]{0:T(128)} %bitcast.1.core_ref, bf16[1024,3072]{1,0:T(8,128)(2,1)} %get-tuple-element.127.g2k.g2s, bf16[1024,3072]{1,0:T(8,128)(2,1)} %get-tuple-element.128.g1k.g1s, bf16[1024,3072]{1,0:T(8,128)(2,1)} %get-tuple-element.127.g2k.g2s, ...), custom_call_target="tpu_custom_call" | custom-call | flops 3000000000 | bytes 1500000 | tf_op jit(solution)/shard_map/wgrad_back/pallas_call | solution.py:576
  269.3 15.2 %wgrad_in.1 = (bf16[2,2,4,4,24,768]{5,4,3,2,1,0:T(8,128)(2,1)}, bf16[2,2,4,4,24,768]{5,4,3,2,1,0:T(8,128)(2,1)}) custom-call(s32[1]{0:T(128)} %bitcast.1.core_ref, bf16[1024,768]{1,0:T(8,128)(2,1)} %get-tuple-element.133.a_ref, bf16[1024,768]{1,0:T(8,128)(2,1)} %get-tuple-element.134.c_ref, bf16[1024,3072]{1,0:T(8,128)(2,1)} %get-tuple-element.135.b_ref, ...), custom_call_target="tpu_custom_call" | custom-call | flops 3000000000 | bytes 1500000 | tf_op jit(solution)/shard_map/wgrad_in/pallas_call | solution.py:475
  284.9 2.5 fusion
  288.0 1.5 collective-permute-done.20
  289.4 2.3 fusion.3
  291.8 1.5 collective-permute-start.22
  293.3 12.5 %attend_back.4 = (bf16[3,1024,384]{2,1,0:T(8,128)(2,1)}, f32[2,1,384]{2,1,0:T(1,128)}, f32[2,1,384]{2,1,0:T(1,128)}) custom-call(s32[2]{0:T(128)} %refs_0_.11, bf16[1024,2304]{1,0:T(8,128)(2,1)} %qkv.2.refs_1_.refs_2_.refs_3_, bf16[1024,2304]{1,0:T(8,128)(2,1)} %qkv.2.refs_1_.refs_2_.refs_3_, bf16[1024,2304]{1,0:T(8,128)(2,1)} %qkv.2.refs_1_.refs_2_.refs_3_, ...), custom_call_target="tpu_custom_call" | custom-call | flops 2400000000 | bytes 1200000 | tf_op jit(solution)/shard_map/attend_back/pallas_call | solution.py:395
  305.8 12.3 %attend_back.5 = (bf16[3,1024,384]{2,1,0:T(8,128)(2,1)}, f32[2,1,384]{2,1,0:T(1,128)}, f32[2,1,384]{2,1,0:T(1,128)}) custom-call(s32[2]{0:T(128)} %refs_0_.11, bf16[1024,2304]{1,0:T(8,128)(2,1)} %qkv.2.refs_1_.refs_2_.refs_3_, bf16[1024,2304]{1,0:T(8,128)(2,1)} %qkv.2.refs_1_.refs_2_.refs_3_, bf16[1024,2304]{1,0:T(8,128)(2,1)} %qkv.2.refs_1_.refs_2_.refs_3_, ...), custom_call_target="tpu_custom_call" | custom-call | flops 2400000000 | bytes 1200000 | tf_op jit(solution)/shard_map/attend_back/pallas_call | solution.py:395
  318.4 1.7 collective-permute-done.22
  320.9 1.5 collective-permute-start.24
  322.4 14.9 %wgrad_heads.2 = (bf16[2,2,4,5,24,384]{5,4,3,2,1,0:T(8,128)(2,1)}, bf16[2,2,4,5,24,384]{5,4,3,2,1,0:T(8,128)(2,1)}) custom-call(s32[1]{0:T(128)} %bitcast.1.core_ref, bf16[1024,768]{1,0:T(8,128)(2,1)} %get-tuple-element.156.x_ref.a_ref, bf16[1024,768]{1,0:T(8,128)(2,1)} %c_ref.3, bf16[3,1024,768]{2,1,0:T(8,128)(2,1)} %get-tuple-element.123.rest_0_.b_ref, ...), custom_call_target="tpu_custom_call" | custom-call | flops 2400000000 | bytes 1200000 | tf_op jit(solution)/shard_map/wgrad_heads/pallas_call | solution.py:540
  337.6 1.1 pad_maximum_fusion.2
  338.7 9.3 %wgrad_heads.3 = (bf16[2,2,4,4,24,384]{5,4,3,2,1,0:T(8,128)(2,1)}, bf16[2,2,4,4,24,384]{5,4,3,2,1,0:T(8,128)(2,1)}) custom-call(s32[1]{0:T(128)} %bitcast.1.core_ref, bf16[1024,768]{1,0:T(8,128)(2,1)} %get-tuple-element.156.x_ref.a_ref, bf16[1024,768]{1,0:T(8,128)(2,1)} %c_ref.3, bf16[3,1024,768]{2,1,0:T(8,128)(2,1)} %get-tuple-element.123.rest_0_.b_ref, ...), custom_call_target="tpu_custom_call" | custom-call | flops 2400000000 | bytes 1200000 | tf_op jit(solution)/shard_map/wgrad_heads/pallas_call | solution.py:540
  348.5 3.5 all-to-all-start.2
  352.1 2.0 fusion.11
  354.1 1.5 collective-permute-start.29
  356.6 9.3 %dx.3 = bf16[1024,768]{1,0:T(8,128)(2,1)} custom-call(f32[1024,768]{1,0:T(8,128)} %get-tuple-element.170.dz1_ref, bf16[3,1024,384]{2,1,0:T(8,128)(2,1)} %get-tuple-element.145.d_ref.rest_0_, bf16[3,1024,384]{2,1,0:T(8,128)(2,1)} %get-tuple-element.147.d_ref.rest_1_, bf16[2,768,768]{2,1,0:T(8,128)(2,1)} %bitcast.118, bf16[2,768,768]{2,1,0:T(8,128)(2,1)} %bitcast.106), custom_call_target="tpu_custom_call" | custom-call | flops 1800000000 | bytes 900000 | tf_op jit(solution)/shard_map/dx/pallas_call | solution.py:434
  365.9 3.5 collective-permute-done.29
  370.1 5.3 %collective-permute-done.27 = bf16[2,4,5,24,384]{4,3,2,1,0:T(8,128)(2,1)S(1)} collective-permute-done((bf16[2,4,5,24,384]{4,3,2,1,0:T(8,128)(2,1)S(1)}, bf16[2,4,5,24,384]{4,3,2,1,0:T(8,128)(2,1)S(1)}, u32[]{:S(2)}, u32[]{:S(2)}) %collective-permute-start.27) | collective-permute-done | bytes 737312 | tf_op jit(solution)/shard_map/ppermute | solution.py:622
  376.3 4.3 %collective-permute-done.30 = bf16[4,4,24,384]{3,2,1,0:T(8,128)(2,1)S(1)} collective-permute-done((bf16[4,4,24,384]{3,2,1,0:T(8,128)(2,1)S(1)}, bf16[4,4,24,384]{3,2,1,0:T(8,128)(2,1)S(1)}, u32[]{:S(2)}, u32[]{:S(2)}) %collective-permute-start.30) | collective-permute-done | bytes 294944 | tf_op jit(solution)/shard_map/ppermute | solution.py:622
  380.6 3.2 collective-permute-done.28
  383.9 1.0 pad_maximum_fusion.4
  384.9 4.5 %all-to-all-start.1 = ((bf16[4,9,24,384]{3,2,1,0:T(8,128)(2,1)}), bf16[4,9,24,384]{3,2,1,0:T(8,128)(2,1)S(1)}, u32[]{:S(2)}, u32[]{:S(2)}) async-start(bf16[4,9,24,384]{3,2,1,0:T(8,128)(2,1)} %pad_maximum_fusion.4), calls=%async_computation.1 | async-start | bytes 1327104 | tf_op jit(solution)/shard_map/all_to_all | solution.py:626
  391.0 12.1 %all-to-all-done.1 = bf16[4,9,24,384]{3,2,1,0:T(8,128)(2,1)S(1)} async-done(((bf16[4,9,24,384]{3,2,1,0:T(8,128)(2,1)}), bf16[4,9,24,384]{3,2,1,0:T(8,128)(2,1)S(1)}, u32[]{:S(2)}, u32[]{:S(2)}) %all-to-all-start.1) | async-done | bytes 663584 | tf_op jit(solution)/shard_map/all_to_all | solution.py:626
  (89 shorter events, 14.0 us)
Async XLA Ops:
  2.3 16.4 %copy-start.12 = (bf16[13,8,768]{2,1,0:T(8,128)(2,1)S(1)}, bf16[13,8,768]{2,1,0:T(8,128)(2,1)}, u32[]{:S(2)}) copy-start(bf16[13,8,768]{2,1,0:T(8,128)(2,1)} %pack_one.1) | copy-start | bytes 479236
  2.3 10.4 %collective-permute-start = (bf16[13,8,768]{2,1,0:T(8,128)(2,1)}, bf16[13,8,768]{2,1,0:T(8,128)(2,1)S(1)}, u32[]{:S(2)}, u32[]{:S(2)}) collective-permute-start(bf16[13,8,768]{2,1,0:T(8,128)(2,1)} %pack_one.1), channel_id=1, source_target_pairs={{0,2},{1,3},{2,4},{3,5},{4,6},{5,7},{6,0},{7,1},{8,10},{9,11},{10,... | collective-permute-start | bytes 479240 | tf_op jit(solution)/shard_map/ppermute | solution.py:622
  5.4 13.4 %collective-permute-start.1 = (bf16[13,8,768]{2,1,0:T(8,128)(2,1)}, bf16[13,8,768]{2,1,0:T(8,128)(2,1)S(1)}, u32[]{:S(2)}, u32[]{:S(2)}) collective-permute-start(bf16[13,8,768]{2,1,0:T(8,128)(2,1)} %pack_one.1), channel_id=1, source_target_pairs={{0,4},{1,5},{2,6},{3,7},{4,0},{5,1},{6,2},{7,3},{8,12},{9,13},{10,... | collective-permute-start | bytes 479240 | tf_op jit(solution)/shard_map/ppermute | solution.py:622
  7.9 10.8 %collective-permute-start.2 = (bf16[13,8,768]{2,1,0:T(8,128)(2,1)}, bf16[13,8,768]{2,1,0:T(8,128)(2,1)S(1)}, u32[]{:S(2)}, u32[]{:S(2)}) collective-permute-start(bf16[13,8,768]{2,1,0:T(8,128)(2,1)} %pack_one.1), channel_id=1, source_target_pairs={{0,6},{1,7},{2,0},{3,1},{4,2},{5,3},{6,4},{7,5},{8,14},{9,15},{10,... | collective-permute-start | bytes 479240 | tf_op jit(solution)/shard_map/ppermute | solution.py:622
  18.8 33.9 %all-to-all-start = ((bf16[4,8,24,768]{3,2,1,0:T(8,128)(2,1)}), bf16[4,8,24,768]{3,2,1,0:T(8,128)(2,1)S(1)}, u32[]{:S(2)}, u32[]{:S(2)}) async-start(bf16[4,8,24,768]{3,2,1,0:T(8,128)(2,1)} %pack_two.1), calls=%async_computation | async-start | bytes 2359296 | tf_op jit(solution)/shard_map/all_to_all | solution.py:626
  25.0 8.8 %collective-permute-start.6 = (bf16[4,7,8,768]{3,2,1,0:T(8,128)(2,1)S(1)}, bf16[4,7,8,768]{3,2,1,0:T(8,128)(2,1)S(1)}, u32[]{:S(2)}, u32[]{:S(2)}) collective-permute-start(bf16[4,7,8,768]{3,2,1,0:T(8,128)(2,1)S(1)} %slice.95), channel_id=1, source_target_pairs={{0,16},{1,17},{2,18},{3,19},{4,20},{5,21},{6,22},{7,23},{8,24},{9,... | collective-permute-start | bytes 1032200 | tf_op jit(solution)/shard_map/ppermute | solution.py:622
  26.6 8.9 %collective-permute-start.3 = (bf16[4,2,24,768]{3,2,1,0:T(8,128)(2,1)S(1)}, bf16[4,2,24,768]{3,2,1,0:T(8,128)(2,1)S(1)}, u32[]{:S(2)}, u32[]{:S(2)}) collective-permute-start(bf16[4,2,24,768]{3,2,1,0:T(8,128)(2,1)S(1)} %bitcast.121), channel_id=1, source_target_pairs={{0,1},{1,0},{2,3},{3,2},{4,5},{5,4},{6,7},{7,6},{8,9},{9,8},{10,11... | collective-permute-start | bytes 884744 | tf_op jit(solution)/shard_map/ppermute | solution.py:622
  33.8 19.8 %copy-start.2 = (bf16[2,4,7,8,768]{4,3,2,1,0:T(8,128)(2,1)}, bf16[2,4,7,8,768]{4,3,2,1,0:T(8,128)(2,1)S(1)}, u32[]{:S(2)}) copy-start(bf16[2,4,7,8,768]{4,3,2,1,0:T(8,128)(2,1)S(1)} %pad_maximum_fusion.3.refs_5_) | copy-start | bytes 2064388
  33.9 15.3 %collective-permute-start.7 = (bf16[2,4,7,8,768]{4,3,2,1,0:T(8,128)(2,1)S(1)}, bf16[2,4,7,8,768]{4,3,2,1,0:T(8,128)(2,1)}, u32[]{:S(2)}, u32[]{:S(2)}) collective-permute-start(bf16[2,4,7,8,768]{4,3,2,1,0:T(8,128)(2,1)S(1)} %pad_maximum_fusion.3.refs_5_), channel_id=1, source_target_pairs={{0,1},{1,0},{2,3},{3,2},{4,5},{5,4},{6,7},{7,6},{8,9},{9,8},{10,11... | collective-permute-start | bytes 2064392 | tf_op jit(solution)/shard_map/ppermute | solution.py:622
  35.5 21.7 %copy-start.3 = (bf16[2,4,2,24,768]{4,3,2,1,0:T(8,128)(2,1)}, bf16[2,4,2,24,768]{4,3,2,1,0:T(8,128)(2,1)S(1)}, u32[]{:S(2)}) copy-start(bf16[2,4,2,24,768]{4,3,2,1,0:T(8,128)(2,1)S(1)} %pad_maximum_fusion.6.refs_1_) | copy-start | bytes 1769476
  35.5 12.9 %collective-permute-start.5 = (bf16[2,4,2,24,768]{4,3,2,1,0:T(8,128)(2,1)S(1)}, bf16[2,4,2,24,768]{4,3,2,1,0:T(8,128)(2,1)}, u32[]{:S(2)}, u32[]{:S(2)}) collective-permute-start(bf16[2,4,2,24,768]{4,3,2,1,0:T(8,128)(2,1)S(1)} %pad_maximum_fusion.6.refs_1_), channel_id=1, source_target_pairs={{0,16},{1,17},{2,18},{3,19},{4,20},{5,21},{6,22},{7,23},{8,24},{9,... | collective-permute-start | bytes 1769480 | tf_op jit(solution)/shard_map/ppermute | solution.py:622
  37.1 18.0 %collective-permute-start.4 = (bf16[2,4,2,24,768]{4,3,2,1,0:T(8,128)(2,1)S(1)}, bf16[2,4,2,24,768]{4,3,2,1,0:T(8,128)(2,1)}, u32[]{:S(2)}, u32[]{:S(2)}) collective-permute-start(bf16[2,4,2,24,768]{4,3,2,1,0:T(8,128)(2,1)S(1)} %pad_maximum_fusion.6.refs_1_), channel_id=1, source_target_pairs={{0,8},{1,9},{2,10},{3,11},{4,12},{5,13},{6,14},{7,15},{8,0},{9,1},... | collective-permute-start | bytes 1769480 | tf_op jit(solution)/shard_map/ppermute | solution.py:622
  37.1 20.1 %collective-permute-start.9 = (bf16[2,4,7,8,768]{4,3,2,1,0:T(8,128)(2,1)S(1)}, bf16[2,4,7,8,768]{4,3,2,1,0:T(8,128)(2,1)}, u32[]{:S(2)}, u32[]{:S(2)}) collective-permute-start(bf16[2,4,7,8,768]{4,3,2,1,0:T(8,128)(2,1)S(1)} %pad_maximum_fusion.3.refs_5_), channel_id=1, source_target_pairs={{0,8},{1,9},{2,10},{3,11},{4,12},{5,13},{6,14},{7,15},{8,0},{9,1},... | collective-permute-start | bytes 2064392 | tf_op jit(solution)/shard_map/ppermute | solution.py:622
  49.2 8.0 %collective-permute-start.10 = (bf16[2,4,7,8,768]{4,3,2,1,0:T(8,128)(2,1)}, bf16[2,4,7,8,768]{4,3,2,1,0:T(8,128)(2,1)}, u32[]{:S(2)}, u32[]{:S(2)}) collective-permute-start(bf16[2,4,7,8,768]{4,3,2,1,0:T(8,128)(2,1)} %collective-permute-done.7.refs_7_), channel_id=1, source_target_pairs={{0,8},{1,9},{2,10},{3,11},{4,12},{5,13},{6,14},{7,15},{8,0},{9,1},... | collective-permute-start | bytes 2064392 | tf_op jit(solution)/shard_map/ppermute | solution.py:622
  49.2 8.0 %collective-permute-start.8 = (bf16[2,4,2,24,768]{4,3,2,1,0:T(8,128)(2,1)}, bf16[2,4,2,24,768]{4,3,2,1,0:T(8,128)(2,1)}, u32[]{:S(2)}, u32[]{:S(2)}) collective-permute-start(bf16[2,4,2,24,768]{4,3,2,1,0:T(8,128)(2,1)} %collective-permute-done.5.refs_3_), channel_id=1, source_target_pairs={{0,8},{1,9},{2,10},{3,11},{4,12},{5,13},{6,14},{7,15},{8,0},{9,1},... | collective-permute-start | bytes 1769480 | tf_op jit(solution)/shard_map/ppermute | solution.py:622
  53.6 14.5 %collective-permute-start.12 = (bf16[4,4,24,768]{3,2,1,0:T(8,128)(2,1)}, bf16[4,4,24,768]{3,2,1,0:T(8,128)(2,1)S(1)}, u32[]{:S(2)}, u32[]{:S(2)}) collective-permute-start(bf16[4,4,24,768]{3,2,1,0:T(8,128)(2,1)} %get-tuple-element.104), channel_id=1, source_target_pairs={{0,16},{1,17},{2,18},{3,19},{4,20},{5,21},{6,22},{7,23},{8,24},{9,... | collective-permute-start | bytes 1769480 | tf_op jit(solution)/shard_map/ppermute | solution.py:622
  55.1 15.8 %collective-permute-start.11 = (bf16[4,4,24,768]{3,2,1,0:T(8,128)(2,1)S(1)}, bf16[4,4,24,768]{3,2,1,0:T(8,128)(2,1)S(1)}, u32[]{:S(2)}, u32[]{:S(2)}) collective-permute-start(bf16[4,4,24,768]{3,2,1,0:T(8,128)(2,1)S(1)} %get-tuple-element.103), channel_id=1, source_target_pairs={{0,1},{1,0},{2,3},{3,2},{4,5},{5,4},{6,7},{7,6},{8,9},{9,8},{10,11... | collective-permute-start | bytes 1769480 | tf_op jit(solution)/shard_map/ppermute | solution.py:622
  69.3 10.9 %copy-start = (bf16[2,4,4,24,768]{4,3,2,1,0:T(8,128)(2,1)}, bf16[2,4,4,24,768]{4,3,2,1,0:T(8,128)(2,1)S(1)}, u32[]{:S(2)}) copy-start(bf16[2,4,4,24,768]{4,3,2,1,0:T(8,128)(2,1)S(1)} %pad_maximum_fusion.1.refs_3_) | copy-start | bytes 3538948
  69.3 26.1 %collective-permute-start.14 = (bf16[2,4,4,24,768]{4,3,2,1,0:T(8,128)(2,1)S(1)}, bf16[2,4,4,24,768]{4,3,2,1,0:T(8,128)(2,1)S(1)}, u32[]{:S(2)}, u32[]{:S(2)}) collective-permute-start(bf16[2,4,4,24,768]{4,3,2,1,0:T(8,128)(2,1)S(1)} %pad_maximum_fusion.1.refs_3_), channel_id=1, source_target_pairs={{0,1},{1,0},{2,3},{3,2},{4,5},{5,4},{6,7},{7,6},{8,9},{9,8},{10,11... | collective-permute-start | bytes 3538952 | tf_op jit(solution)/shard_map/ppermute | solution.py:622
  71.0 9.2 %copy-start.1 = (bf16[2,4,4,24,768]{4,3,2,1,0:T(8,128)(2,1)}, bf16[2,4,4,24,768]{4,3,2,1,0:T(8,128)(2,1)S(1)}, u32[]{:S(2)}) copy-start(bf16[2,4,4,24,768]{4,3,2,1,0:T(8,128)(2,1)S(1)} %pad_maximum_fusion.refs_1_) | copy-start | bytes 3538948
  71.0 25.8 %collective-permute-start.13 = (bf16[2,4,4,24,768]{4,3,2,1,0:T(8,128)(2,1)S(1)}, bf16[2,4,4,24,768]{4,3,2,1,0:T(8,128)(2,1)S(1)}, u32[]{:S(2)}, u32[]{:S(2)}) collective-permute-start(bf16[2,4,4,24,768]{4,3,2,1,0:T(8,128)(2,1)S(1)} %pad_maximum_fusion.refs_1_), channel_id=1, source_target_pairs={{0,16},{1,17},{2,18},{3,19},{4,20},{5,21},{6,22},{7,23},{8,24},{9,... | collective-permute-start | bytes 3538952 | tf_op jit(solution)/shard_map/ppermute | solution.py:622
  80.1 17.2 %collective-permute-start.18 = (bf16[2,4,4,24,768]{4,3,2,1,0:T(8,128)(2,1)S(1)}, bf16[2,4,4,24,768]{4,3,2,1,0:T(8,128)(2,1)S(1)}, u32[]{:S(2)}, u32[]{:S(2)}) collective-permute-start(bf16[2,4,4,24,768]{4,3,2,1,0:T(8,128)(2,1)S(1)} %pad_maximum_fusion.1.refs_3_), channel_id=1, source_target_pairs={{0,8},{1,9},{2,10},{3,11},{4,12},{5,13},{6,14},{7,15},{8,0},{9,1},... | collective-permute-start | bytes 3538952 | tf_op jit(solution)/shard_map/ppermute | solution.py:622
  80.1 17.2 %collective-permute-start.17 = (bf16[2,4,4,24,768]{4,3,2,1,0:T(8,128)(2,1)S(1)}, bf16[2,4,4,24,768]{4,3,2,1,0:T(8,128)(2,1)S(1)}, u32[]{:S(2)}, u32[]{:S(2)}) collective-permute-start(bf16[2,4,4,24,768]{4,3,2,1,0:T(8,128)(2,1)S(1)} %pad_maximum_fusion.refs_1_), channel_id=1, source_target_pairs={{0,8},{1,9},{2,10},{3,11},{4,12},{5,13},{6,14},{7,15},{8,0},{9,1},... | collective-permute-start | bytes 3538952 | tf_op jit(solution)/shard_map/ppermute | solution.py:622
  95.3 9.6 %copy-start.9 = (bf16[2,4,4,24,768]{4,3,2,1,0:T(8,128)(2,1)}, bf16[2,4,4,24,768]{4,3,2,1,0:T(8,128)(2,1)S(1)}, u32[]{:S(2)}) copy-start(bf16[2,4,4,24,768]{4,3,2,1,0:T(8,128)(2,1)S(1)} %collective-permute-done.14.refs_3_) | copy-start | bytes 3538948
  96.8 8.2 %copy-start.10 = (bf16[2,4,4,24,768]{4,3,2,1,0:T(8,128)(2,1)}, bf16[2,4,4,24,768]{4,3,2,1,0:T(8,128)(2,1)S(1)}, u32[]{:S(2)}) copy-start(bf16[2,4,4,24,768]{4,3,2,1,0:T(8,128)(2,1)S(1)} %collective-permute-done.13.refs_1_) | copy-start | bytes 3538948
  96.8 8.2 %collective-permute-start.15 = (bf16[2,4,4,24,768]{4,3,2,1,0:T(8,128)(2,1)S(1)}, bf16[2,4,4,24,768]{4,3,2,1,0:T(8,128)(2,1)S(1)}, u32[]{:S(2)}, u32[]{:S(2)}) collective-permute-start(bf16[2,4,4,24,768]{4,3,2,1,0:T(8,128)(2,1)S(1)} %collective-permute-done.13.refs_1_), channel_id=1, source_target_pairs={{0,8},{1,9},{2,10},{3,11},{4,12},{5,13},{6,14},{7,15},{8,0},{9,1},... | collective-permute-start | bytes 3538952 | tf_op jit(solution)/shard_map/ppermute | solution.py:622
  96.8 8.2 %collective-permute-start.16 = (bf16[2,4,4,24,768]{4,3,2,1,0:T(8,128)(2,1)S(1)}, bf16[2,4,4,24,768]{4,3,2,1,0:T(8,128)(2,1)}, u32[]{:S(2)}, u32[]{:S(2)}) collective-permute-start(bf16[2,4,4,24,768]{4,3,2,1,0:T(8,128)(2,1)S(1)} %collective-permute-done.14.refs_3_), channel_id=1, source_target_pairs={{0,8},{1,9},{2,10},{3,11},{4,12},{5,13},{6,14},{7,15},{8,0},{9,1},... | collective-permute-start | bytes 3538952 | tf_op jit(solution)/shard_map/ppermute | solution.py:622
  97.3 1.1 copy-start.7
  98.4 1.0 copy-start.8
  104.9 1.0 copy-start.11
  269.2 15.7 %collective-permute-start.19 = (bf16[2,2,4,4,24,768]{5,4,3,2,1,0:T(8,128)(2,1)}, bf16[2,2,4,4,24,768]{5,4,3,2,1,0:T(8,128)(2,1)}, u32[]{:S(2)}, u32[]{:S(2)}) collective-permute-start(bf16[2,2,4,4,24,768]{5,4,3,2,1,0:T(8,128)(2,1)} %get-tuple-element.139), channel_id=1, source_target_pairs={{0,8},{1,9},{2,10},{3,11},{4,12},{5,13},{6,14},{7,15},{8,0},{9,1},... | collective-permute-start | bytes 7077896 | tf_op jit(solution)/shard_map/ppermute | solution.py:622
  269.3 15.7 %copy-start.5 = (bf16[2,2,4,4,24,768]{5,4,3,2,1,0:T(8,128)(2,1)S(1)}, bf16[2,2,4,4,24,768]{5,4,3,2,1,0:T(8,128)(2,1)}, u32[]{:S(2)}) copy-start(bf16[2,2,4,4,24,768]{5,4,3,2,1,0:T(8,128)(2,1)} %get-tuple-element.138) | copy-start | bytes 7077892
  284.5 5.0 %collective-permute-start.20 = (bf16[2,2,4,4,24,768]{5,4,3,2,1,0:T(8,128)(2,1)}, bf16[2,2,4,4,24,768]{5,4,3,2,1,0:T(8,128)(2,1)}, u32[]{:S(2)}, u32[]{:S(2)}) collective-permute-start(bf16[2,2,4,4,24,768]{5,4,3,2,1,0:T(8,128)(2,1)} %get-tuple-element.142), channel_id=1, source_target_pairs={{0,8},{1,9},{2,10},{3,11},{4,12},{5,13},{6,14},{7,15},{8,0},{9,1},... | collective-permute-start | bytes 7077896 | tf_op jit(solution)/shard_map/ppermute | solution.py:622
  284.9 4.5 %copy-start.4 = (bf16[2,2,4,4,24,768]{5,4,3,2,1,0:T(8,128)(2,1)S(1)}, bf16[2,2,4,4,24,768]{5,4,3,2,1,0:T(8,128)(2,1)}, u32[]{:S(2)}) copy-start(bf16[2,2,4,4,24,768]{5,4,3,2,1,0:T(8,128)(2,1)} %get-tuple-element.141) | copy-start | bytes 7077892
  287.4 30.7 %collective-permute-start.21 = (bf16[2,4,4,24,768]{4,3,2,1,0:T(8,128)(2,1)S(1)}, bf16[2,4,4,24,768]{4,3,2,1,0:T(8,128)(2,1)S(1)}, u32[]{:S(2)}, u32[]{:S(2)}) collective-permute-start(bf16[2,4,4,24,768]{4,3,2,1,0:T(8,128)(2,1)S(1)} %get-tuple-element.176), channel_id=1, source_target_pairs={{0,1},{1,0},{2,3},{3,2},{4,5},{5,4},{6,7},{7,6},{8,9},{9,8},{10,11... | collective-permute-start | bytes 3538952 | tf_op jit(solution)/shard_map/ppermute | solution.py:622
  291.8 28.3 %collective-permute-start.22 = (bf16[2,4,4,24,768]{4,3,2,1,0:T(8,128)(2,1)S(1)}, bf16[2,4,4,24,768]{4,3,2,1,0:T(8,128)(2,1)S(1)}, u32[]{:S(2)}, u32[]{:S(2)}) collective-permute-start(bf16[2,4,4,24,768]{4,3,2,1,0:T(8,128)(2,1)S(1)} %get-tuple-element.174), channel_id=1, source_target_pairs={{0,16},{1,17},{2,18},{3,19},{4,20},{5,21},{6,22},{7,23},{8,24},{9,... | collective-permute-start | bytes 3538952 | tf_op jit(solution)/shard_map/ppermute | solution.py:622
  320.4 16.9 %collective-permute-start.23 = (bf16[4,4,24,768]{3,2,1,0:T(8,128)(2,1)S(1)}, bf16[4,4,24,768]{3,2,1,0:T(8,128)(2,1)S(1)}, u32[]{:S(2)}, u32[]{:S(2)}) collective-permute-start(bf16[4,4,24,768]{3,2,1,0:T(8,128)(2,1)S(1)} %get-tuple-element.182), channel_id=1, source_target_pairs={{0,1},{1,0},{2,3},{3,2},{4,5},{5,4},{6,7},{7,6},{8,9},{9,8},{10,11... | collective-permute-start | bytes 1769480 | tf_op jit(solution)/shard_map/ppermute | solution.py:622
  320.9 16.6 %collective-permute-start.24 = (bf16[4,4,24,768]{3,2,1,0:T(8,128)(2,1)S(1)}, bf16[4,4,24,768]{3,2,1,0:T(8,128)(2,1)S(1)}, u32[]{:S(2)}, u32[]{:S(2)}) collective-permute-start(bf16[4,4,24,768]{3,2,1,0:T(8,128)(2,1)S(1)} %get-tuple-element.184), channel_id=1, source_target_pairs={{0,16},{1,17},{2,18},{3,19},{4,20},{5,21},{6,22},{7,23},{8,24},{9,... | collective-permute-start | bytes 1769480 | tf_op jit(solution)/shard_map/ppermute | solution.py:622
  338.7 16.9 %collective-permute-start.25 = (bf16[2,2,4,5,24,384]{5,4,3,2,1,0:T(8,128)(2,1)}, bf16[2,2,4,5,24,384]{5,4,3,2,1,0:T(8,128)(2,1)S(1)}, u32[]{:S(2)}, u32[]{:S(2)}) collective-permute-start(bf16[2,2,4,5,24,384]{5,4,3,2,1,0:T(8,128)(2,1)} %get-tuple-element.168), channel_id=1, source_target_pairs={{0,8},{1,9},{2,10},{3,11},{4,12},{5,13},{6,14},{7,15},{8,0},{9,1},... | collective-permute-start | bytes 4423688 | tf_op jit(solution)/shard_map/ppermute | solution.py:622
  348.1 4.0 collective-permute-start.26
  348.5 36.4 %all-to-all-start.2 = ((bf16[4,8,24,768]{3,2,1,0:T(8,128)(2,1)}), bf16[4,8,24,768]{3,2,1,0:T(8,128)(2,1)S(1)}, u32[]{:S(2)}, u32[]{:S(2)}) async-start(bf16[4,8,24,768]{3,2,1,0:T(8,128)(2,1)} %pad_maximum_fusion.2), calls=%async_computation.2 | async-start | bytes 2359296 | tf_op jit(solution)/shard_map/all_to_all | solution.py:626
  352.1 3.6 copy-start.6
  354.1 15.3 %collective-permute-start.29 = (bf16[2,4,4,24,384]{4,3,2,1,0:T(8,128)(2,1)S(1)}, bf16[2,4,4,24,384]{4,3,2,1,0:T(8,128)(2,1)S(1)}, u32[]{:S(2)}, u32[]{:S(2)}) collective-permute-start(bf16[2,4,4,24,384]{4,3,2,1,0:T(8,128)(2,1)S(1)} %get-tuple-element.180), channel_id=1, source_target_pairs={{0,1},{1,0},{2,3},{3,2},{4,5},{5,4},{6,7},{7,6},{8,9},{9,8},{10,11... | collective-permute-start | bytes 1769480 | tf_op jit(solution)/shard_map/ppermute | solution.py:622
  356.0 19.5 %collective-permute-start.27 = (bf16[2,4,5,24,384]{4,3,2,1,0:T(8,128)(2,1)S(1)}, bf16[2,4,5,24,384]{4,3,2,1,0:T(8,128)(2,1)S(1)}, u32[]{:S(2)}, u32[]{:S(2)}) collective-permute-start(bf16[2,4,5,24,384]{4,3,2,1,0:T(8,128)(2,1)S(1)} %get-tuple-element.178), channel_id=1, source_target_pairs={{0,16},{1,17},{2,18},{3,19},{4,20},{5,21},{6,22},{7,23},{8,24},{9,... | collective-permute-start | bytes 2211848 | tf_op jit(solution)/shard_map/ppermute | solution.py:622
  369.6 10.9 %collective-permute-start.30 = (bf16[4,4,24,384]{3,2,1,0:T(8,128)(2,1)S(1)}, bf16[4,4,24,384]{3,2,1,0:T(8,128)(2,1)S(1)}, u32[]{:S(2)}, u32[]{:S(2)}) collective-permute-start(bf16[4,4,24,384]{3,2,1,0:T(8,128)(2,1)S(1)} %get-tuple-element.188), channel_id=1, source_target_pairs={{0,16},{1,17},{2,18},{3,19},{4,20},{5,21},{6,22},{7,23},{8,24},{9,... | collective-permute-start | bytes 884744 | tf_op jit(solution)/shard_map/ppermute | solution.py:622
  375.6 8.2 %collective-permute-start.28 = (bf16[4,5,24,384]{3,2,1,0:T(8,128)(2,1)S(1)}, bf16[4,5,24,384]{3,2,1,0:T(8,128)(2,1)S(1)}, u32[]{:S(2)}, u32[]{:S(2)}) collective-permute-start(bf16[4,5,24,384]{3,2,1,0:T(8,128)(2,1)S(1)} %get-tuple-element.186), channel_id=1, source_target_pairs={{0,1},{1,0},{2,3},{3,2},{4,5},{5,4},{6,7},{7,6},{8,9},{9,8},{10,11... | collective-permute-start | bytes 1105928 | tf_op jit(solution)/shard_map/ppermute | solution.py:622
  384.9 18.2 %all-to-all-start.1 = ((bf16[4,9,24,384]{3,2,1,0:T(8,128)(2,1)}), bf16[4,9,24,384]{3,2,1,0:T(8,128)(2,1)S(1)}, u32[]{:S(2)}, u32[]{:S(2)}) async-start(bf16[4,9,24,384]{3,2,1,0:T(8,128)(2,1)} %pad_maximum_fusion.4), calls=%async_computation.1 | async-start | bytes 1327104 | tf_op jit(solution)/shard_map/all_to_all | solution.py:626
